TPU v7x, 32 devices: a whole 2x2x4 slice. The times are simulated.
32 devices in a mesh: head: 4 (over x, core), gx: 8 (over z, y).
Axes of the slice: x: 2, y: 2, z: 4, core: 2. Of those that a mesh axis runs over, the one named last changes fastest.
Arguments:
- level_set: float32 [72, 48, 8, 128], P('gx', 'head'), may hold values from -6 to 6
- wind_field: float32 [2, 72, 128], P(None, 'gx'), may hold values from -3 to 3
- target_mask: int32 [72, 128], P('gx'), may hold values 0 or 1
- target_depth: float32 [72, 128], P('gx'), may hold values from 0.2 to 2
Outputs:
- level_next: float32 [72, 48, 8, 128], P('gx', 'head')
Inputs may be any that keep to these rules, and one draw needn't show every extreme that they name: `target_mask`: 1 marks a cell of the target set, 0 a cell outside it.
All inputs are finite; a program needn't handle non-finite values. No bound on the sum of `target_mask` on one device may be relied on, other than what follows from the above.
Results may differ from a plain program's by a relative error of at most 0.0003.
Values sent between devices are 32-bit elements; how exact they have to be, the bound alone decides.
No kernel may reach another device: no remote copies, remote signals or barrier semaphores. Data moves between devices by JAX's collectives and lax.ppermute only.
A program may use at most 64 MiB of HBM per device.

v0:
```python
import math

import jax
import jax.numpy as jnp
from jax import lax
from jax.sharding import PartitionSpec as P

epsilon = 1e-06
courant = 0.5
spacing = 0.05
turn_limit = 1.0
thrust_limit = 0.5
speed_low = 0.5
speed_high = 1.5


def with_halo(array, sides, width, wrap):
    for axis, dim in sides:
        size, length = (lax.axis_size(axis), array.shape[dim])
        up = [(i, (i + 1) % size) for i in range(size if wrap else size - 1)]
        down = [(j, i) for i, j in up]
        last = lax.slice_in_dim(array, length - width, length, axis=dim)
        leading = lax.slice_in_dim(array, 0, width, axis=dim)
        before = lax.ppermute(last, axis, up)
        after = lax.ppermute(leading, axis, down)
        array = jnp.concatenate([before, array, after], axis=dim)
    return array


def weno_side(slope_a, slope_b, slope_c, slope_d, slope_e):
    guess_a = slope_a / 3.0 - 7.0 * slope_b / 6.0 + 11.0 * slope_c / 6.0
    guess_b = -slope_b / 6.0 + 5.0 * slope_c / 6.0 + slope_d / 3.0
    guess_c = slope_c / 3.0 + 5.0 * slope_d / 6.0 - slope_e / 6.0
    bend_a = slope_a - 2.0 * slope_b + slope_c
    tilt_a = slope_a - 4.0 * slope_b + 3.0 * slope_c
    bend_b = slope_b - 2.0 * slope_c + slope_d
    tilt_b = slope_b - slope_d
    bend_c = slope_c - 2.0 * slope_d + slope_e
    tilt_c = 3.0 * slope_c - 4.0 * slope_d + slope_e
    smooth_a = 13.0 / 12.0 * bend_a * bend_a + 0.25 * tilt_a * tilt_a + epsilon
    smooth_b = 13.0 / 12.0 * bend_b * bend_b + 0.25 * tilt_b * tilt_b + epsilon
    smooth_c = 13.0 / 12.0 * bend_c * bend_c + 0.25 * tilt_c * tilt_c + epsilon
    weight_a = 0.1 / (smooth_a * smooth_a)
    weight_b = 0.6 / (smooth_b * smooth_b)
    weight_c = 0.3 / (smooth_c * smooth_c)
    return (weight_a * guess_a + weight_b * guess_b + weight_c * guess_c) / (
        weight_a + weight_b + weight_c
    )


def weno_pair(padded, along, step_size):
    inner_count = padded.shape[along] - 6
    differences = jnp.diff(padded, axis=along) / step_size

    def window(offset):
        return lax.slice_in_dim(differences, offset, offset + inner_count, axis=along)

    minus_side = weno_side(window(0), window(1), window(2), window(3), window(4))
    plus_side = weno_side(window(5), window(4), window(3), window(2), window(1))
    return (minus_side, plus_side)


def hamilton(
    padded, heading_step, speed_step, speeds, cosines, sines, wind_x, wind_y, peak_x, peak_y
):
    inner = padded[3:-3, 3:-3]
    minus_x, plus_x = weno_pair(padded[:, 3:-3], 0, spacing)
    minus_t, plus_t = weno_pair(padded[3:-3], 1, heading_step)
    minus_v, plus_v = weno_pair(
        jnp.pad(inner, ((0, 0), (0, 0), (3, 3), (0, 0)), mode="edge"), 2, speed_step
    )
    minus_y, plus_y = weno_pair(
        jnp.pad(inner, ((0, 0), (0, 0), (0, 0), (3, 3)), mode="edge"), 3, spacing
    )
    flow_x = speeds * cosines + wind_x
    flow_y = speeds * sines + wind_y
    slope_x = 0.5 * (minus_x + plus_x)
    slope_y = 0.5 * (minus_y + plus_y)
    slope_t = 0.5 * (minus_t + plus_t)
    slope_v = 0.5 * (minus_v + plus_v)
    drift = (
        slope_x * flow_x
        + slope_y * flow_y
        - turn_limit * jnp.abs(slope_t)
        - thrust_limit * jnp.abs(slope_v)
    )
    spread = (
        peak_x * (plus_x - minus_x)
        + peak_y * (plus_y - minus_y)
        + turn_limit * (plus_t - minus_t)
        + thrust_limit * (plus_v - minus_v)
    )
    return drift + 0.5 * spread


def clamp_ends(values, margin):
    position = lax.axis_index("gx")
    last_index = lax.axis_size("gx") - 1
    low_fill = jnp.broadcast_to(values[margin : margin + 1], (margin,) + values.shape[1:])
    high_fill = jnp.broadcast_to(values[-margin - 1 : -margin], (margin,) + values.shape[1:])
    low_part = jnp.where(position == 0, low_fill, values[:margin])
    high_part = jnp.where(position == last_index, high_fill, values[-margin:])
    return jnp.concatenate([low_part, values[margin:-margin], high_part], 0)


def heading_table(first_index, length, heading_total, heading_step):
    indices = jnp.mod(first_index + jnp.arange(length, dtype=jnp.int32), heading_total)
    angles = indices.astype(jnp.float32) * heading_step
    return (jnp.cos(angles).reshape(1, length, 1, 1), jnp.sin(angles).reshape(1, length, 1, 1))


def rimmed(values):
    beside_all = with_halo(values, (("head", 1),), 3, True)
    wide = with_halo(beside_all, (("gx", 0),), 3, False)
    return clamp_ends(wide, 3)


def local(level_set, wind_field, target_mask, target_depth):
    planes, headings, speed_count, cross_count = level_set.shape
    heading_total = headings * lax.axis_size("head")
    heading_step = 2.0 * math.pi / heading_total
    speed_step = (speed_high - speed_low) / (speed_count - 1)
    speed_row = (
        speed_low + jnp.arange(speed_count, dtype=jnp.int32).astype(jnp.float32) * speed_step
    )
    speeds = speed_row.reshape(1, 1, speed_count, 1)
    first_heading = lax.axis_index("head") * headings
    wind_x = wind_field[0]
    wind_y = wind_field[1]
    target_flat = jnp.where(target_mask == 1, -target_depth, target_depth)
    target = target_flat[:, None, None, :]
    all_angles = jnp.arange(heading_total, dtype=jnp.int32).astype(jnp.float32) * heading_step
    products_x = jnp.cos(all_angles)[:, None] * speed_row[None, :]
    products_y = jnp.sin(all_angles)[:, None] * speed_row[None, :]
    local_x = jnp.maximum(
        jnp.max(wind_x + jnp.max(products_x)), jnp.max(-(wind_x + jnp.min(products_x)))
    )
    local_y = jnp.maximum(
        jnp.max(wind_y + jnp.max(products_y)), jnp.max(-(wind_y + jnp.min(products_y)))
    )
    peak_x, peak_y = lax.pmax((local_x, local_y), "gx")
    time_step = courant / (
        peak_x / spacing + peak_y / spacing + turn_limit / heading_step + thrust_limit / speed_step
    )
    cosines, sines = heading_table(first_heading, headings, heading_total, heading_step)
    flow_wx = wind_x[:, None, None, :]
    flow_wy = wind_y[:, None, None, :]

    def rate_of(values):
        return hamilton(
            rimmed(values),
            heading_step,
            speed_step,
            speeds,
            cosines,
            sines,
            flow_wx,
            flow_wy,
            peak_x,
            peak_y,
        )

    section_one = jnp.minimum(level_set + time_step * rate_of(level_set), target)
    section_two = jnp.minimum(
        0.75 * level_set + 0.25 * (section_one + time_step * rate_of(section_one)), target
    )
    level_next = jnp.minimum(
        1.0 / 3.0 * level_set + 2.0 / 3.0 * (section_two + time_step * rate_of(section_two)), target
    )
    return level_next


def solution(mesh):
    return jax.shard_map(
        local,
        mesh=mesh,
        in_specs=(P("gx", "head", None, None), P(None, "gx", None), P("gx", None), P("gx", None)),
        out_specs=P("gx", "head", None, None),
        check_vma=False,
    )
```

profile of v0, /device:TPU:8, one launch (start us, length us, event | category | flops | bytes accessed | tf_op | source)
XLA Modules:
  0.0 119.7 jit_solution(9455544280892546364)
XLA Ops:
  0.0 1.0 fusion.341
  1.0 1.0 collective-permute-start.1
  2.1 1.3 %fusion.342 = (f32[9,12,1,128]{3,2,1,0:T(1,128)S(1)}, f32[9,12,1,128]{3,2,1,0:T(1,128)S(1)}) fusion(f32[9,12,8,128]{3,2,1,0:T(8,128)} %param.4), kind=kLoop, calls=%fused_computation.552 | loop fusion | bytes 221184 | tf_op jit(solution)/shard_map/jit(_pad)/slice | solution.py:70
  3.4 0.2 fusion.340
  3.8 0.2 pad_maximum_fusion.4
  4.0 0.1 fusion.4
  4.1 0.9 copy.164
  5.0 0.9 copy.165
  5.9 0.2 reshape.166
  6.1 0.2 reshape.165
  6.3 0.4 pad_maximum_fusion.3
  6.8 0.3 fusion.5
  7.1 0.4 copy-done.2
  7.5 0.7 multiply_reduce_fusion.2
  8.2 3.2 %negate_reduce_fusion = (f32[]{:T(128)}, f32[]{:T(128)}, f32[]{:T(128)}, f32[]{:T(128)}) fusion(f32[]{:T(128)} %get-tuple-element.14, f32[1,9,128]{2,0,1:T(1,128)S(1)} %get-tuple-element.48, f32[]{:T(128)} %get-tuple-element.13, f32[]{:T(128)} %get-tuple-element.10, f32[]{:T(128)} %get-tuple-element.9, f32[1,9,128]{2,0,1:T(1,128)S(1)} %get-tuple-element.47), kind=kLoop, calls=%fused_computation.522 | loop fusion | flops 11516 | bytes 9248 | tf_op jit(solution)/shard_map/reduce_max | solution.py:139
  14.0 0.1 broadcast_multiply_fusion.1
  14.1 19.4 %all-reduce = (f32[]{:T(128)}, f32[]{:T(128)}) all-reduce(f32[]{:T(128)S(6)} %max.11, f32[]{:T(128)S(6)} %max.10), channel_id=1, replica_groups=mesh['head'=4,'gx'=8] {'gx'}, use_global_device_ids=true, to_apply=%region_9.10 | all-reduce | flops 2 | bytes 16 | tf_op jit(solution)/shard_map/pmax | solution.py:141
  34.8 0.9 constant_dynamic-update-slice_fusion.2
  35.8 0.1 fusion.11
  35.9 1.9 %collective-permute-start.2 = (f32[3,18,8,128]{3,2,1,0:T(8,128)S(1)}, f32[3,18,8,128]{3,2,1,0:T(8,128)S(1)}, u32[]{:S(2)}, u32[]{:S(2)}) collective-permute-start(f32[3,18,8,128]{3,2,1,0:T(8,128)S(1)} %get-tuple-element.27), channel_id=1, source_target_pairs={{0,1},{1,2},{2,3},{3,4},{4,5},{5,6},{6,7},{8,9},{9,10},{10,11},{11... | collective-permute-start | bytes 663560 | tf_op jit(solution)/shard_map/ppermute | solution.py:24
  37.8 4.8 %collective-permute-start.3 = (f32[3,18,8,128]{3,2,1,0:T(8,128)S(1)}, f32[3,18,8,128]{3,2,1,0:T(8,128)S(1)}, u32[]{:S(2)}, u32[]{:S(2)}) collective-permute-start(f32[3,18,8,128]{3,2,1,0:T(8,128)S(1)} %get-tuple-element.28), channel_id=1, source_target_pairs={{1,0},{2,1},{3,2},{4,3},{5,4},{6,5},{7,6},{9,8},{10,9},{11,10},{12... | collective-permute-start | bytes 663560 | tf_op jit(solution)/shard_map/ppermute | solution.py:25
  42.7 2.3 %collective-permute-done.2 = f32[3,18,8,128]{3,2,1,0:T(8,128)S(1)} collective-permute-done((f32[3,18,8,128]{3,2,1,0:T(8,128)S(1)}, f32[3,18,8,128]{3,2,1,0:T(8,128)S(1)}, u32[]{:S(2)}, u32[]{:S(2)}) %collective-permute-start.2) | collective-permute-done | bytes 221216 | tf_op jit(solution)/shard_map/ppermute | solution.py:24
  45.0 3.0 %collective-permute-done.3 = f32[3,18,8,128]{3,2,1,0:T(8,128)S(1)} collective-permute-done((f32[3,18,8,128]{3,2,1,0:T(8,128)S(1)}, f32[3,18,8,128]{3,2,1,0:T(8,128)S(1)}, u32[]{:S(2)}, u32[]{:S(2)}) %collective-permute-start.3) | collective-permute-done | bytes 221216 | tf_op jit(solution)/shard_map/ppermute | solution.py:25
  48.0 0.1 pad_maximum_fusion
  48.1 0.1 fusion.8
  48.2 9.7 %fusion.306 = f32[9,12,8,128]{3,2,1,0:T(8,128)S(1)} fusion(f32[9,12,8,128]{3,2,1,0:T(8,128)S(1)} %copy-done, f32[9,12,13,128]{3,2,1,0:T(8,128)S(1)} %fusion.4, f32[9,17,8,128]{3,2,1,0:T(8,128)S(1)} %fusion.11, f32[9,12,8,133]{3,2,1,0:T(8,128)S(1)} %fusion.5, f32[14,12,8,128]{3,2,1,0:T(8,128)S(1)} %fusion.8, f32[9,128]{1,0:T(8,128)S(1)} %negate_select_fusion, ...), kind=kLoop, calls=%fused_computation.479 | loop fusion | flops 58503168 | bytes 11516172 | tf_op jit(solution)/shard_map/min | solution.py:163
  57.9 0.1 fusion.339
  58.0 0.2 fusion.337
  58.3 1.7 %collective-permute-start.5 = (f32[9,3,8,128]{3,2,1,0:T(8,128)S(1)}, f32[9,3,8,128]{3,2,1,0:T(8,128)S(1)}, u32[]{:S(2)}, u32[]{:S(2)}) collective-permute-start(f32[9,3,8,128]{3,2,1,0:T(8,128)S(1)} %get-tuple-element.38), channel_id=1, source_target_pairs={{8,0},{16,8},{24,16},{0,24},{9,1},{17,9},{25,17},{1,25},{10,2},{18... | collective-permute-start | bytes 331784 | tf_op jit(solution)/shard_map/ppermute | solution.py:25
  60.1 0.2 pad_maximum_fusion.6
  60.3 0.1 fusion.2
  60.4 0.9 copy.150
  61.3 0.9 copy.151
  62.2 0.2 reshape.170
  62.4 0.2 reshape.169
  62.6 0.4 pad_maximum_fusion.5
  63.0 0.3 fusion.3
  63.4 1.9 %collective-permute-start.6 = (f32[3,18,8,128]{3,2,1,0:T(8,128)S(1)}, f32[3,18,8,128]{3,2,1,0:T(8,128)S(1)}, u32[]{:S(2)}, u32[]{:S(2)}) collective-permute-start(f32[3,18,8,128]{3,2,1,0:T(8,128)S(1)} %get-tuple-element.23), channel_id=1, source_target_pairs={{0,1},{1,2},{2,3},{3,4},{4,5},{5,6},{6,7},{8,9},{9,10},{10,11},{11... | collective-permute-start | bytes 663560 | tf_op jit(solution)/shard_map/ppermute | solution.py:24
  65.4 4.8 %collective-permute-start.7 = (f32[3,18,8,128]{3,2,1,0:T(8,128)S(1)}, f32[3,18,8,128]{3,2,1,0:T(8,128)S(1)}, u32[]{:S(2)}, u32[]{:S(2)}) collective-permute-start(f32[3,18,8,128]{3,2,1,0:T(8,128)S(1)} %get-tuple-element.24), channel_id=1, source_target_pairs={{1,0},{2,1},{3,2},{4,3},{5,4},{6,5},{7,6},{9,8},{10,9},{11,10},{12... | collective-permute-start | bytes 663560 | tf_op jit(solution)/shard_map/ppermute | solution.py:25
  70.3 5.4 %collective-permute-done.6 = f32[3,18,8,128]{3,2,1,0:T(8,128)S(1)} collective-permute-done((f32[3,18,8,128]{3,2,1,0:T(8,128)S(1)}, f32[3,18,8,128]{3,2,1,0:T(8,128)S(1)}, u32[]{:S(2)}, u32[]{:S(2)}) %collective-permute-start.6) | collective-permute-done | bytes 221216 | tf_op jit(solution)/shard_map/ppermute | solution.py:24
  75.7 3.1 %collective-permute-done.7 = f32[3,18,8,128]{3,2,1,0:T(8,128)S(1)} collective-permute-done((f32[3,18,8,128]{3,2,1,0:T(8,128)S(1)}, f32[3,18,8,128]{3,2,1,0:T(8,128)S(1)}, u32[]{:S(2)}, u32[]{:S(2)}) %collective-permute-start.7) | collective-permute-done | bytes 221216 | tf_op jit(solution)/shard_map/ppermute | solution.py:25
  78.8 0.1 pad_maximum_fusion.1
  78.9 0.1 fusion.7
  79.0 9.7 %fusion.315 = f32[9,12,8,128]{3,2,1,0:T(8,128)S(1)} fusion(f32[9,12,8,128]{3,2,1,0:T(8,128)S(1)} %fusion.306, f32[9,12,13,128]{3,2,1,0:T(8,128)S(1)} %fusion.2, f32[9,17,8,128]{3,2,1,0:T(8,128)S(1)} %fusion.10, f32[9,12,8,133]{3,2,1,0:T(8,128)S(1)} %fusion.3, f32[14,12,8,128]{3,2,1,0:T(8,128)S(1)} %fusion.7, f32[9,12,8,128]{3,2,1,0:T(8,128)S(1)} %copy-done, ...), kind=kLoop, calls=%fused_computation.488 | loop fusion | flops 58834944 | bytes 11958540 | tf_op jit(solution)/shard_map/min | solution.py:164
  88.7 0.1 fusion.336
  88.8 0.2 fusion.334
  89.0 0.1 collective-permute-start.8
  89.1 1.7 %collective-permute-start.9 = (f32[9,3,8,128]{3,2,1,0:T(8,128)S(1)}, f32[9,3,8,128]{3,2,1,0:T(8,128)S(1)}, u32[]{:S(2)}, u32[]{:S(2)}) collective-permute-start(f32[9,3,8,128]{3,2,1,0:T(8,128)S(1)} %get-tuple-element.32), channel_id=1, source_target_pairs={{8,0},{16,8},{24,16},{0,24},{9,1},{17,9},{25,17},{1,25},{10,2},{18... | collective-permute-start | bytes 331784 | tf_op jit(solution)/shard_map/ppermute | solution.py:25
  90.9 0.2 pad_maximum_fusion.8
  91.0 0.1 fusion
  91.2 0.9 copy.152
  92.1 0.9 copy.153
  93.0 0.2 reshape.174
  93.2 0.2 reshape.173
  93.4 0.4 pad_maximum_fusion.7
  93.8 0.3 fusion.1
  94.2 1.9 %collective-permute-start.10 = (f32[3,18,8,128]{3,2,1,0:T(8,128)S(1)}, f32[3,18,8,128]{3,2,1,0:T(8,128)S(1)}, u32[]{:S(2)}, u32[]{:S(2)}) collective-permute-start(f32[3,18,8,128]{3,2,1,0:T(8,128)S(1)} %get-tuple-element.19), channel_id=1, source_target_pairs={{0,1},{1,2},{2,3},{3,4},{4,5},{5,6},{6,7},{8,9},{9,10},{10,11},{11... | collective-permute-start | bytes 663560 | tf_op jit(solution)/shard_map/ppermute | solution.py:24
  96.1 4.8 %collective-permute-start.11 = (f32[3,18,8,128]{3,2,1,0:T(8,128)S(1)}, f32[3,18,8,128]{3,2,1,0:T(8,128)S(1)}, u32[]{:S(2)}, u32[]{:S(2)}) collective-permute-start(f32[3,18,8,128]{3,2,1,0:T(8,128)S(1)} %get-tuple-element.20), channel_id=1, source_target_pairs={{1,0},{2,1},{3,2},{4,3},{5,4},{6,5},{7,6},{9,8},{10,9},{11,10},{12... | collective-permute-start | bytes 663560 | tf_op jit(solution)/shard_map/ppermute | solution.py:25
  101.0 0.1 fusion.9
  101.0 5.0 %collective-permute-done.10 = f32[3,18,8,128]{3,2,1,0:T(8,128)S(1)} collective-permute-done((f32[3,18,8,128]{3,2,1,0:T(8,128)S(1)}, f32[3,18,8,128]{3,2,1,0:T(8,128)S(1)}, u32[]{:S(2)}, u32[]{:S(2)}) %collective-permute-start.10) | collective-permute-done | bytes 221216 | tf_op jit(solution)/shard_map/ppermute | solution.py:24
  106.1 3.1 %collective-permute-done.11 = f32[3,18,8,128]{3,2,1,0:T(8,128)S(1)} collective-permute-done((f32[3,18,8,128]{3,2,1,0:T(8,128)S(1)}, f32[3,18,8,128]{3,2,1,0:T(8,128)S(1)}, u32[]{:S(2)}, u32[]{:S(2)}) %collective-permute-start.11) | collective-permute-done | bytes 221216 | tf_op jit(solution)/shard_map/ppermute | solution.py:25
  109.2 0.1 pad_maximum_fusion.2
  109.3 0.1 fusion.6
  109.3 10.4 %fusion.324 = f32[9,12,8,128]{3,2,1,0:T(8,128)} fusion(f32[9,12,8,128]{3,2,1,0:T(8,128)S(1)} %fusion.315, f32[9,12,13,128]{3,2,1,0:T(8,128)S(1)} %fusion, f32[9,17,8,128]{3,2,1,0:T(8,128)S(1)} %fusion.9, f32[9,12,8,133]{3,2,1,0:T(8,128)S(1)} %fusion.1, f32[14,12,8,128]{3,2,1,0:T(8,128)S(1)} %fusion.6, f32[9,12,8,128]{3,2,1,0:T(8,128)S(1)} %copy-done, ...), kind=kLoop, calls=%fused_computation.497 | loop fusion | flops 58834944 | bytes 11958540 | tf_op jit(solution)/shard_map/min | solution.py:167
  (52 shorter events, 1.0 us)
Async XLA Ops:
  0.0 3.4 %copy-start = (f32[9,12,8,128]{3,2,1,0:T(8,128)S(1)}, f32[9,12,8,128]{3,2,1,0:T(8,128)}, u32[]{:S(2)}) copy-start(f32[9,12,8,128]{3,2,1,0:T(8,128)} %param.4) | copy-start | bytes 1327108
  1.0 2.6 %copy-start.1 = (f32[2,9,128]{2,0,1:T(2,128)S(1)}, f32[2,9,128]{2,0,1:T(2,128)}, u32[]{:S(2)}) copy-start(f32[2,9,128]{2,0,1:T(2,128)} %param.5) | copy-start | bytes 27652
  1.0 34.7 %collective-permute-start.1 = (f32[9,3,8,128]{3,2,1,0:T(8,128)S(1)}, f32[9,3,8,128]{3,2,1,0:T(8,128)S(1)}, u32[]{:S(2)}, u32[]{:S(2)}) collective-permute-start(f32[9,3,8,128]{3,2,1,0:T(8,128)S(1)} %get-tuple-element.43), channel_id=1, source_target_pairs={{8,0},{16,8},{24,16},{0,24},{9,1},{17,9},{25,17},{1,25},{10,2},{18... | collective-permute-start | bytes 331784 | tf_op jit(solution)/shard_map/ppermute | solution.py:25
  2.0 32.8 %collective-permute-start = (f32[9,3,8,128]{3,2,1,0:T(8,128)S(1)}, f32[9,3,8,128]{3,2,1,0:T(8,128)}, u32[]{:S(2)}, u32[]{:S(2)}) collective-permute-start(f32[9,3,8,128]{3,2,1,0:T(8,128)S(1)} %get-tuple-element.44), channel_id=1, source_target_pairs={{0,8},{8,16},{16,24},{24,0},{1,9},{9,17},{17,25},{25,1},{2,10},{10... | collective-permute-start | bytes 331784 | tf_op jit(solution)/shard_map/ppermute | solution.py:24
  6.7 0.7 copy-start.2
  6.8 0.7 copy-start.3
  35.9 9.1 %collective-permute-start.2 = (f32[3,18,8,128]{3,2,1,0:T(8,128)S(1)}, f32[3,18,8,128]{3,2,1,0:T(8,128)S(1)}, u32[]{:S(2)}, u32[]{:S(2)}) collective-permute-start(f32[3,18,8,128]{3,2,1,0:T(8,128)S(1)} %get-tuple-element.27), channel_id=1, source_target_pairs={{0,1},{1,2},{2,3},{3,4},{4,5},{5,6},{6,7},{8,9},{9,10},{10,11},{11... | collective-permute-start | bytes 663560 | tf_op jit(solution)/shard_map/ppermute | solution.py:24
  37.8 10.2 %collective-permute-start.3 = (f32[3,18,8,128]{3,2,1,0:T(8,128)S(1)}, f32[3,18,8,128]{3,2,1,0:T(8,128)S(1)}, u32[]{:S(2)}, u32[]{:S(2)}) collective-permute-start(f32[3,18,8,128]{3,2,1,0:T(8,128)S(1)} %get-tuple-element.28), channel_id=1, source_target_pairs={{1,0},{2,1},{3,2},{4,3},{5,4},{6,5},{7,6},{9,8},{10,9},{11,10},{12... | collective-permute-start | bytes 663560 | tf_op jit(solution)/shard_map/ppermute | solution.py:25
  58.2 5.1 %collective-permute-start.4 = (f32[9,3,8,128]{3,2,1,0:T(8,128)S(1)}, f32[9,3,8,128]{3,2,1,0:T(8,128)S(1)}, u32[]{:S(2)}, u32[]{:S(2)}) collective-permute-start(f32[9,3,8,128]{3,2,1,0:T(8,128)S(1)} %get-tuple-element.37), channel_id=1, source_target_pairs={{0,8},{8,16},{16,24},{24,0},{1,9},{9,17},{17,25},{25,1},{2,10},{10... | collective-permute-start | bytes 331784 | tf_op jit(solution)/shard_map/ppermute | solution.py:24
  58.3 5.1 %collective-permute-start.5 = (f32[9,3,8,128]{3,2,1,0:T(8,128)S(1)}, f32[9,3,8,128]{3,2,1,0:T(8,128)S(1)}, u32[]{:S(2)}, u32[]{:S(2)}) collective-permute-start(f32[9,3,8,128]{3,2,1,0:T(8,128)S(1)} %get-tuple-element.38), channel_id=1, source_target_pairs={{8,0},{16,8},{24,16},{0,24},{9,1},{17,9},{25,17},{1,25},{10,2},{18... | collective-permute-start | bytes 331784 | tf_op jit(solution)/shard_map/ppermute | solution.py:25
  63.4 12.3 %collective-permute-start.6 = (f32[3,18,8,128]{3,2,1,0:T(8,128)S(1)}, f32[3,18,8,128]{3,2,1,0:T(8,128)S(1)}, u32[]{:S(2)}, u32[]{:S(2)}) collective-permute-start(f32[3,18,8,128]{3,2,1,0:T(8,128)S(1)} %get-tuple-element.23), channel_id=1, source_target_pairs={{0,1},{1,2},{2,3},{3,4},{4,5},{5,6},{6,7},{8,9},{9,10},{10,11},{11... | collective-permute-start | bytes 663560 | tf_op jit(solution)/shard_map/ppermute | solution.py:24
  65.4 13.4 %collective-permute-start.7 = (f32[3,18,8,128]{3,2,1,0:T(8,128)S(1)}, f32[3,18,8,128]{3,2,1,0:T(8,128)S(1)}, u32[]{:S(2)}, u32[]{:S(2)}) collective-permute-start(f32[3,18,8,128]{3,2,1,0:T(8,128)S(1)} %get-tuple-element.24), channel_id=1, source_target_pairs={{1,0},{2,1},{3,2},{4,3},{5,4},{6,5},{7,6},{9,8},{10,9},{11,10},{12... | collective-permute-start | bytes 663560 | tf_op jit(solution)/shard_map/ppermute | solution.py:25
  89.0 5.1 %collective-permute-start.8 = (f32[9,3,8,128]{3,2,1,0:T(8,128)S(1)}, f32[9,3,8,128]{3,2,1,0:T(8,128)S(1)}, u32[]{:S(2)}, u32[]{:S(2)}) collective-permute-start(f32[9,3,8,128]{3,2,1,0:T(8,128)S(1)} %get-tuple-element.31), channel_id=1, source_target_pairs={{0,8},{8,16},{16,24},{24,0},{1,9},{9,17},{17,25},{25,1},{2,10},{10... | collective-permute-start | bytes 331784 | tf_op jit(solution)/shard_map/ppermute | solution.py:24
  89.1 5.0 %collective-permute-start.9 = (f32[9,3,8,128]{3,2,1,0:T(8,128)S(1)}, f32[9,3,8,128]{3,2,1,0:T(8,128)S(1)}, u32[]{:S(2)}, u32[]{:S(2)}) collective-permute-start(f32[9,3,8,128]{3,2,1,0:T(8,128)S(1)} %get-tuple-element.32), channel_id=1, source_target_pairs={{8,0},{16,8},{24,16},{0,24},{9,1},{17,9},{25,17},{1,25},{10,2},{18... | collective-permute-start | bytes 331784 | tf_op jit(solution)/shard_map/ppermute | solution.py:25
  94.2 11.9 %collective-permute-start.10 = (f32[3,18,8,128]{3,2,1,0:T(8,128)S(1)}, f32[3,18,8,128]{3,2,1,0:T(8,128)S(1)}, u32[]{:S(2)}, u32[]{:S(2)}) collective-permute-start(f32[3,18,8,128]{3,2,1,0:T(8,128)S(1)} %get-tuple-element.19), channel_id=1, source_target_pairs={{0,1},{1,2},{2,3},{3,4},{4,5},{5,6},{6,7},{8,9},{9,10},{10,11},{11... | collective-permute-start | bytes 663560 | tf_op jit(solution)/shard_map/ppermute | solution.py:24
  96.1 13.0 %collective-permute-start.11 = (f32[3,18,8,128]{3,2,1,0:T(8,128)S(1)}, f32[3,18,8,128]{3,2,1,0:T(8,128)S(1)}, u32[]{:S(2)}, u32[]{:S(2)}) collective-permute-start(f32[3,18,8,128]{3,2,1,0:T(8,128)S(1)} %get-tuple-element.20), channel_id=1, source_target_pairs={{1,0},{2,1},{3,2},{4,3},{5,4},{6,5},{7,6},{9,8},{10,9},{11,10},{12... | collective-permute-start | bytes 663560 | tf_op jit(solution)/shard_map/ppermute | solution.py:25
where the time goes:
time: 120 us
  other arithmetic  37.8 us (31%)
  starting transfers between devices  24.8 us (21%)
  waiting for transfers between devices  21.9 us (18%)
  blocking collectives  19.4 us (16%)
  local copies, waits for them, and re-layouts  11.3 us (9%)
  between operations  4.43 us (4%)
    pmax x1, blocking collectives, local(): peak_x, peak_y = lax.pmax((local_x, local_y), 'gx')  19.4 us
    ppermute x6, starting transfers between devices, with_halo(): after = lax.ppermute(leading, axis, down)  18.9 us
    ppermute x6, waiting for transfers between devices, with_halo(): before = lax.ppermute(last, axis, up)  12.8 us
    min x1, other arithmetic, local(): jnp.minimum(1.0 / 3.0 * level_set + 2.0 / 3.0 * (section_two + time_step...  10.4 us
    min x1, other arithmetic, local(): jnp.minimum(level_set + time_step * rate_of(level_set), target)  9.68 us
    min x1, other arithmetic, local(): jnp.minimum(0.75 * level_set + 0.25 * (section_one + time_step * rate_of(...  9.66 us
    ppermute x6, waiting for transfers between devices, with_halo(): after = lax.ppermute(leading, axis, down)  9.17 us
    slice x9, local copies, waits for them, and re-layouts, hamilton(): jnp.pad(inner, ((0, 0), (0, 0), (0, 0), (3, 3)), mode='edge')  6.02 us
  transfers between devices with their start and end apart: 12, of which 6 were waited for; matrix products, arithmetic and copies ran while one was open for 14% of the time, Pallas kernels for 0%

commit v1 on v0

v1 whole, which is shorter than its diff:
```python
import functools
import math

import jax
import jax.numpy as jnp
import numpy as np
from jax import lax
from jax.experimental import pallas as pl
from jax.experimental.pallas import tpu as pltpu
from jax.sharding import PartitionSpec as P

epsilon = 1e-06
courant = 0.5
spacing = 0.05
turn_limit = 1.0
thrust_limit = 0.5
speed_low = 0.5
speed_high = 1.5
rim = 3


def inverse(value):
    return pl.reciprocal(value, approx=True)


def weights_of(e1, e2, turn, eps):
    level = turn * turn * (4.0 / 3.0) + eps
    ia = inverse(level + e2 * (e2 + turn))
    ib = inverse(level + e2 * e1)
    ic = inverse(level + e1 * (e1 - turn))
    return ia * ia, ib * ib * 6.0, ic * ic


def sides(fl, f0, fr, a2, a1, b1, b0, c0, c1):
    a3 = a1 * 3.0
    c3 = c0 * 3.0
    minus = ((fl + fl) * a2 + f0 * c3) * inverse(a2 + b1 + c3)
    plus = ((fr + fr) * c1 + f0 * a3) * inverse(c1 + b0 + a3)
    return minus, plus


def row_terms(cells, step):
    count = len(cells) - 2 * rim
    eps = epsilon * step * step
    slope = [cells[i + 1] - cells[i] for i in range(len(cells) - 1)]
    bend = {m: slope[m + 3] - slope[m + 2] for m in range(-2, count + 2)}
    turn = {m: bend[m + 1] - bend[m] for m in range(-2, count + 1)}
    jerk = {m: turn[m] - turn[m - 1] for m in range(-1, count + 1)}
    a, b, c = {}, {}, {}
    for m in turn:
        a[m], b[m], c[m] = weights_of(bend[m], bend[m + 1], turn[m], eps)
    out = []
    for i in range(count):
        base = (cells[i + 4] - cells[i + 2]) * 6.0 - (turn[i - 1] + turn[i])
        minus, plus = sides(
            jerk[i - 1], jerk[i], jerk[i + 1], a[i - 2], a[i - 1], b[i - 1], b[i], c[i], c[i + 1]
        )
        out.append((base + (plus - minus), (plus + minus) - jerk[i]))
    return out


def tile_terms(cell, axis, step):
    count = cell.shape[axis]
    eps = epsilon * step * step
    place = lax.broadcasted_iota(jnp.int32, cell.shape, axis)
    first = place == 0
    last = place == count - 1

    def after(value, by=1):
        return pltpu.roll(value, count - by, axis)

    def before(value):
        return pltpu.roll(value, 1, axis)

    ahead = jnp.where(last, 0.0, after(cell) - cell)
    behind = before(ahead)
    bend = ahead - behind
    wrapped = before(bend)
    turn_lo = bend - jnp.where(first, 0.0, wrapped)
    turn_hi = jnp.where(last, -bend, after(turn_lo))
    jerk = turn_hi - turn_lo
    jerk_l = jnp.where(first, bend, before(jerk))
    jerk_r = jnp.where(last, bend, after(jerk))
    bend_l = jnp.where(first, 0.0, wrapped)
    level = turn_lo * turn_lo * (4.0 / 3.0) + eps
    ia = inverse(level + bend * (bend + turn_lo))
    ib = inverse(level + bend * bend_l)
    turn_ring = jnp.where(first, -wrapped, turn_lo)
    level_ring = turn_ring * turn_ring * (4.0 / 3.0) + eps
    ic = inverse(level_ring + wrapped * (wrapped - turn_ring))
    ib_ring = jnp.where(first, inverse(level_ring), ib)
    a1 = ia * ia
    b1 = ib * ib * 6.0
    c_low = ic * ic
    b0 = after(ib_ring * ib_ring * 6.0)
    flat = 1.0 / (eps * eps)
    a2 = jnp.where(first, flat, before(a1))
    c0 = after(c_low)
    c1 = jnp.where(last, flat, after(c_low, 2))
    base = (ahead + behind) * 6.0 - (turn_lo + turn_hi)
    minus, plus = sides(jerk_l, jerk, jerk_r, a2, a1, b1, b0, c0, c1)
    return base + (plus - minus), (plus + minus) - jerk


def splat(row, like):
    return jnp.broadcast_to(row, like)


def inner_kernel(split, speed_step, s_ref, wind_ref, taby_ref, *rest):
    planes, headings = s_ref.shape[:2]
    tile = s_ref.shape[2:]
    gain = 1.0 / (12.0 * spacing)
    gain_v = thrust_limit / (12.0 * speed_step)
    if split:
        part_ref, extra_ref = rest
    else:
        pk_ref, part_ref = rest

    def plane(i, carry):
        wind = splat(wind_ref[1, pl.ds(i, 1), :] * gain, tile)

        def heading(j, inner):
            cell = s_ref[i, j]
            mean, gap = tile_terms(cell, 1, spacing)
            mean_v, gap_v = tile_terms(cell, 0, speed_step)
            part = mean * (taby_ref[j] + wind) + gain_v * (gap_v - jnp.abs(mean_v))
            if split:
                part_ref[i, j] = part
                extra_ref[i, j] = gap
            else:
                part_ref[i, j] = part + gap * splat(pk_ref[1:2, :] * gain, tile)
            return inner

        return lax.fori_loop(0, headings, heading, carry)

    lax.fori_loop(0, planes, plane, 0)


def peaks_into(pk_ref, gathered_ref, bounds, heading_step, speed_step):
    peaks = []
    for q in range(2):
        rows = [gathered_ref[g, q] for g in range(gathered_ref.shape[0])]
        top = jnp.max(functools.reduce(jnp.maximum, rows), axis=(0, 1), keepdims=True)
        low = jnp.min(functools.reduce(jnp.minimum, rows), axis=(0, 1), keepdims=True)
        peaks.append(jnp.maximum(top + bounds[q][1], -(low + bounds[q][0])))
    time_step = courant / (
        peaks[0] / spacing
        + peaks[1] / spacing
        + turn_limit / heading_step
        + thrust_limit / speed_step
    )
    width = pk_ref.shape[1]
    for row, value in enumerate(peaks + [time_step]):
        pk_ref[row : row + 1, :] = splat(value, (1, width))


def outer_kernel(
    section, bounds, heading_step, speed_step, ends_ref, *refs
):
    refs = list(refs)
    base_ref = None if section == 1 else refs.pop(0)
    s_ref, part_ref = refs.pop(0), refs.pop(0)
    extra_ref = refs.pop(0) if section == 1 else None
    xlo_ref, xhi_ref, tlo_ref, thi_ref = (refs.pop(0) for _ in range(4))
    wind_ref, tabx_ref, mask_ref, depth_ref = (refs.pop(0) for _ in range(4))
    if section == 1:
        gathered_ref = refs.pop(0)
    else:
        pk_ref = refs.pop(0)
    out_ref = refs.pop(0)
    if section < 3:
        edge_refs = [refs.pop(0) for _ in range(4)]
    if section == 1:
        pk_ref = refs.pop(0)
    acc_ref = refs.pop(0)
    planes, headings = s_ref.shape[:2]
    tile = s_ref.shape[2:]
    gain = 1.0 / (12.0 * spacing)
    gain_t = turn_limit / (12.0 * heading_step)
    if section == 1:
        peaks_into(pk_ref, gathered_ref, bounds, heading_step, speed_step)
    at_low = ends_ref[0] == 1
    at_high = ends_ref[1] == 1

    def along_x(j, carry):
        cells = [s_ref[i, j] for i in range(planes)]
        lows = [jnp.where(at_low, cells[0], xlo_ref[k, j]) for k in range(rim)]
        highs = [jnp.where(at_high, cells[-1], xhi_ref[k, j]) for k in range(rim)]
        peak = splat(pk_ref[0:1, :] * gain, tile)
        table = tabx_ref[j]
        for i, (mean, gap) in enumerate(row_terms(lows + cells + highs, spacing)):
            flow = table + splat(wind_ref[0, i : i + 1, :] * gain, tile)
            total = part_ref[i, j] + (mean * flow + gap * peak)
            if section == 1:
                total = total + extra_ref[i, j] * splat(pk_ref[1:2, :] * gain, tile)
            acc_ref[i, j] = total
        return carry

    lax.fori_loop(0, headings, along_x, 0)

    def along_t(i, carry):
        cells = (
            [tlo_ref[i, k] for k in range(rim)]
            + [s_ref[i, j] for j in range(headings)]
            + [thi_ref[i, k] for k in range(rim)]
        )
        step = splat(pk_ref[2:3, :], tile)
        depth = depth_ref[pl.ds(i, 1), :]
        target = splat(jnp.where(mask_ref[pl.ds(i, 1), :] == 1, -depth, depth), tile)
        for j, (mean, gap) in enumerate(row_terms(cells, heading_step)):
            rate = acc_ref[i, j] + gain_t * (gap - jnp.abs(mean))
            moved = cells[j + rim] + step * rate
            if section == 2:
                moved = 0.75 * base_ref[i, j] + 0.25 * moved
            if section == 3:
                moved = (1.0 / 3.0) * base_ref[i, j] + (2.0 / 3.0) * moved
            result = jnp.minimum(moved, target)
            out_ref[i, j] = result
            if section < 3 and j < rim:
                edge_refs[2][i, j] = result
            if section < 3 and j >= headings - rim:
                edge_refs[3][i, j - (headings - rim)] = result
        return carry

    lax.fori_loop(0, planes, along_t, 0)
    if section < 3:
        edge_refs[0][...] = out_ref[:rim]
        edge_refs[1][...] = out_ref[planes - rim :]


def swap(edges):
    size_x, size_t = lax.axis_size("gx"), lax.axis_size("head")
    x_up = [(i, i + 1) for i in range(size_x - 1)]
    x_down = [(j, i) for i, j in x_up]
    t_up = [(i, (i + 1) % size_t) for i in range(size_t)]
    t_down = [(j, i) for i, j in t_up]
    x_low, x_high, t_low, t_high = edges
    from_low = lax.ppermute(x_high, "gx", x_up)
    from_high = lax.ppermute(x_low, "gx", x_down)
    from_left = lax.ppermute(t_high, "head", t_up)
    from_right = lax.ppermute(t_low, "head", t_down)
    return from_low, from_high, from_left, from_right


def local(level_set, wind_field, target_mask, target_depth):
    planes, headings, speed_count, cross_count = level_set.shape
    heading_total = headings * lax.axis_size("head")
    heading_step = 2.0 * math.pi / heading_total
    speed_step = (speed_high - speed_low) / (speed_count - 1)
    gain = 1.0 / (12.0 * spacing)
    speed_row = np.float32(speed_low) + np.arange(speed_count, dtype=np.float32) * np.float32(
        speed_step
    )
    angles = np.arange(heading_total, dtype=np.float32) * np.float32(heading_step)
    bounds, tables = [], []
    for wave in (np.cos(angles), np.sin(angles)):
        product = wave[:, None] * speed_row[None, :]
        bounds.append((float(product.min()), float(product.max())))
        tables.append(product * np.float32(gain))
    first_heading = lax.axis_index("head") * headings
    position = lax.axis_index("gx")
    ends = jnp.stack([position == 0, position == lax.axis_size("gx") - 1]).astype(jnp.int32)
    tables = lax.dynamic_slice_in_dim(jnp.asarray(np.stack(tables)), first_heading, headings, 1)
    tables = jnp.broadcast_to(tables[..., None], (2, headings, speed_count, cross_count))
    gathered = lax.all_gather(wind_field, "gx")

    vmem = pl.BlockSpec(memory_space=pltpu.VMEM)
    smem = pl.BlockSpec(memory_space=pltpu.SMEM)
    field = jax.ShapeDtypeStruct(level_set.shape, jnp.float32)
    x_edge = jax.ShapeDtypeStruct((rim,) + level_set.shape[1:], jnp.float32)
    t_edge = jax.ShapeDtypeStruct((planes, rim, speed_count, cross_count), jnp.float32)
    pk_shape = jax.ShapeDtypeStruct((8, cross_count), jnp.float32)
    cells = math.prod(level_set.shape)

    def call(kernel, ins, outs, scratch, work, scalar_first):
        specs = [vmem] * len(ins)
        if scalar_first:
            specs[0] = smem
        return pl.pallas_call(
            kernel,
            out_shape=outs,
            in_specs=specs,
            out_specs=[vmem] * len(outs),
            scratch_shapes=scratch,
            compiler_params=pltpu.CompilerParams(vmem_limit_bytes=16 * 1024 * 1024),
            cost_estimate=pl.CostEstimate(
                flops=work * cells, bytes_accessed=12 * cells, transcendentals=0
            ),
        )(*ins)

    values, pk = level_set, None
    edges = (
        level_set[:rim],
        level_set[planes - rim :],
        level_set[:, :rim],
        level_set[:, headings - rim :],
    )
    for section in (1, 2, 3):
        ghosts = swap(edges)
        inner = functools.partial(inner_kernel, section == 1, speed_step)
        ins = [values, wind_field, tables[1]] + ([] if section == 1 else [pk])
        parts = call(inner, ins, [field] * (2 if section == 1 else 1), [], 120, False)
        outer = functools.partial(outer_kernel, section, bounds, heading_step, speed_step)
        ins = [ends] + ([] if section == 1 else [level_set]) + [values, *parts, *ghosts]
        ins += [wind_field, tables[0], target_mask, target_depth]
        ins += [gathered] if section == 1 else [pk]
        outs = [field]
        if section < 3:
            outs += [x_edge, x_edge, t_edge, t_edge]
        if section == 1:
            outs += [pk_shape]
        scratch = [pltpu.VMEM(level_set.shape, jnp.float32)]
        results = call(outer, ins, outs, scratch, 120, True)
        values = results[0]
        edges = results[1:5]
        if section == 1:
            pk = results[5]
    return values


def solution(mesh):
    return jax.shard_map(
        local,
        mesh=mesh,
        in_specs=(P("gx", "head", None, None), P(None, "gx", None), P("gx", None), P("gx", None)),
        out_specs=P("gx", "head", None, None),
        check_vma=False,
    )
```

time: 120 us -> 180 us (1.50)
  Pallas kernels: 0 us -> 124 us
  other arithmetic: 37.8 us -> 0.07 us
  waiting for transfers between devices: 21.9 us -> 0.03 us
  blocking collectives: 19.4 us -> 28.1 us
  local copies, waits for them, and re-layouts: 11.3 us -> 3.37 us
  between operations: 4.43 us -> 0.19 us
    pallas_call x0 -> x6, Pallas kernels: none -> 124 us  [call(): pl.pallas_call(kernel, out_shape=outs, in_specs=specs, out_specs=[vmem] *...]
    min x3 -> x0, other arithmetic: 29.7 us -> none  [the longest x1 10.4 us: local(): jnp.minimum(1.0 / 3.0 * level_set + 2.0 / 3.0 * (section_two + time_step...]
    all_gather x0 -> x1, blocking collectives: none -> 28.1 us  [local(): gathered = lax.all_gather(wind_field, 'gx')]
    ppermute x12, waiting for transfers between devices: 21.9 us -> 0.03 us  [the longest x3 0.01 us: swap(): from_right = lax.ppermute(t_low, 'head', t_down)]
    pmax x1 -> x0, blocking collectives: 19.4 us -> none  [local(): peak_x, peak_y = lax.pmax((local_x, local_y), 'gx')]
    slice x20 -> x2, local copies, waits for them, and re-layouts: 8.61 us -> 1.04 us  [the longest x1 1.02 us: local(): level_set[:, :rim]]
    reduce_max x1 -> x0, other arithmetic: 3.21 us -> none  [local(): jnp.max(-(wind_y + jnp.min(products_y)))]
    concatenate x11 -> x0, other arithmetic: 2.05 us -> none  [the longest x3 1.23 us: hamilton(): jnp.pad(inner, ((0, 0), (0, 0), (0, 0), (3, 3)), mode='edge')]
  transfers between devices with their start and end apart: 12 -> 12, of which waited for: 6 -> 0; matrix products, arithmetic and copies ran while one was open for 14% -> 0% of each run, Pallas kernels for 0% -> 64%
where the time goes in v1:
time: 180 us
  Pallas kernels  124 us (69%)
  blocking collectives  28.1 us (16%)
  starting transfers between devices  23.9 us (13%)
  local copies, waits for them, and re-layouts  3.37 us (2%)
    pallas_call x6, Pallas kernels, call(): pl.pallas_call(kernel, out_shape=outs, in_specs=specs, out_specs=[vmem] *...  124 us
    all_gather x1, blocking collectives, local(): gathered = lax.all_gather(wind_field, 'gx')  28.1 us
    ppermute x3, starting transfers between devices, swap(): from_high = lax.ppermute(x_low, 'gx', x_down)  13 us
    ppermute x3, starting transfers between devices, swap(): from_low = lax.ppermute(x_high, 'gx', x_up)  6.37 us
    ppermute x3, starting transfers between devices, swap(): from_right = lax.ppermute(t_low, 'head', t_down)  4.45 us
  transfers between devices with their start and end apart: 12, of which 0 were waited for; matrix products, arithmetic and copies ran while one was open for 0% of the time, Pallas kernels for 64%

profile of v1, /device:TPU:8, one launch (start us, length us, event | category | flops | bytes accessed | tf_op | source)
XLA Modules:
  0.0 179.7 jit_solution(14927778446760421438)
XLA Ops:
  0.0 0.0 copy-start
  0.0 1.0 fusion
  1.0 1.0 collective-permute-start.3
  2.0 0.0 collective-permute-start.2
  2.0 0.0 copy-done
  2.0 3.3 %collective-permute-start.1 = (f32[3,12,8,128]{3,2,1,0:T(8,128)S(1)}, f32[3,12,8,128]{3,2,1,0:T(8,128)S(1)}, u32[]{:S(2)}, u32[]{:S(2)}) collective-permute-start(f32[3,12,8,128]{3,2,1,0:T(8,128)S(1)} %get-tuple-element.33), channel_id=1, source_target_pairs={{1,0},{2,1},{3,2},{4,3},{5,4},{6,5},{7,6},{9,8},{10,9},{11,10},{12... | collective-permute-start | bytes 442376 | tf_op jit(solution)/shard_map/ppermute | solution.py:239
  5.4 2.5 %collective-permute-start = (f32[3,12,8,128]{3,2,1,0:T(8,128)S(1)}, f32[3,12,8,128]{3,2,1,0:T(8,128)S(1)}, u32[]{:S(2)}, u32[]{:S(2)}) collective-permute-start(f32[3,12,8,128]{3,2,1,0:T(8,128)S(1)} %get-tuple-element.34), channel_id=1, source_target_pairs={{0,1},{1,2},{2,3},{3,4},{4,5},{5,6},{6,7},{8,9},{9,10},{10,11},{11... | collective-permute-start | bytes 442376 | tf_op jit(solution)/shard_map/ppermute | solution.py:238
  7.9 0.0 copy-start.4
  7.9 0.7 copy-done.4
  8.6 0.1 dynamic-slice_bitcast_fusion
  8.7 0.1 copy.17
  8.8 0.0 copy-start.3
  8.8 0.1 copy.15
  8.8 0.6 copy-done.3
  9.5 0.1 broadcast_in_dim.13.taby_ref
  9.5 38.3 %shard_map.55 = (f32[9,12,8,128]{3,2,1,0:T(8,128)S(1)}, f32[9,12,8,128]{3,2,1,0:T(8,128)S(1)}) custom-call(f32[9,12,8,128]{3,2,1,0:T(8,128)S(1)} %copy-done, f32[2,9,128]{2,1,0:T(8,128)S(1)} %copy.16.wind_ref.refs_7_, f32[12,8,128]{2,1,0:T(8,128)S(1)} %broadcast_in_dim.13.taby_ref), custom_call_target="tpu_custom_call" | custom-call | flops 13271040 | bytes 1327104 | tf_op jit(solution)/shard_map/pallas_call | solution.py:279
  47.9 28.1 %all-gather = f32[16,9,128]{2,1,0:T(8,128)S(1)} all-gather(f32[2,9,128]{2,1,0:T(8,128)S(1)} %copy.16.wind_ref.refs_7_), channel_id=2, replica_groups=mesh['head'=4,'gx'=8] {'gx'}, dimensions={0}, use_global_device_ids=true | all-gather | bytes 82944 | tf_op jit(solution)/shard_map/all_gather | solution.py:265
  75.9 0.1 add_convert_fusion.ends_ref
  76.0 0.0 collective-permute-done.3.refs_6_
  76.0 0.0 collective-permute-done.2.refs_5_
  76.0 0.0 collective-permute-done.1.refs_4_
  76.0 0.0 collective-permute-done.refs_3_
  76.0 0.0 copy-start.1
  76.0 0.0 copy-start.2
  76.1 0.1 broadcast_in_dim.15.refs_8_
  76.1 0.6 copy-done.1
  76.7 0.0 copy-done.2
  76.7 2.8 %shard_map.56 = (f32[9,12,8,128]{3,2,1,0:T(8,128)S(1)}, f32[3,12,8,128]{3,2,1,0:T(8,128)S(1)}, f32[3,12,8,128]{3,2,1,0:T(8,128)S(1)}, f32[9,3,8,128]{3,2,1,0:T(8...) custom-call(s32[2]{0:T(128)S(1)} %add_convert_fusion.ends_ref, f32[9,12,8,128]{3,2,1,0:T(8,128)S(1)} %copy-done, ...), custom_call_target="tpu_custom_call" | custom-call | flops 13271040 | bytes 1327104 | tf_op jit(solution)/shard_map/pallas_call | solution.py:279
  79.5 1.9 %collective-permute-start.4 = (f32[3,12,8,128]{3,2,1,0:T(8,128)S(1)}, f32[3,12,8,128]{3,2,1,0:T(8,128)S(1)}, u32[]{:S(2)}, u32[]{:S(2)}) collective-permute-start(f32[3,12,8,128]{3,2,1,0:T(8,128)S(1)} %get-tuple-element.22), channel_id=1, source_target_pairs={{0,1},{1,2},{2,3},{3,4},{4,5},{5,6},{6,7},{8,9},{9,10},{10,11},{11... | collective-permute-start | bytes 442376 | tf_op jit(solution)/shard_map/ppermute | solution.py:238
  81.5 4.8 %collective-permute-start.5 = (f32[3,12,8,128]{3,2,1,0:T(8,128)S(1)}, f32[3,12,8,128]{3,2,1,0:T(8,128)S(1)}, u32[]{:S(2)}, u32[]{:S(2)}) collective-permute-start(f32[3,12,8,128]{3,2,1,0:T(8,128)S(1)} %get-tuple-element.23), channel_id=1, source_target_pairs={{1,0},{2,1},{3,2},{4,3},{5,4},{6,5},{7,6},{9,8},{10,9},{11,10},{12... | collective-permute-start | bytes 442376 | tf_op jit(solution)/shard_map/ppermute | solution.py:239
  86.3 0.1 collective-permute-start.6
  86.4 1.7 collective-permute-start.7
  88.1 38.4 %shard_map.57.refs_2_ = f32[9,12,8,128]{3,2,1,0:T(8,128)S(1)} custom-call(f32[9,12,8,128]{3,2,1,0:T(8,128)S(1)} %get-tuple-element.20.s_ref.refs_1_, f32[2,9,128]{2,1,0:T(8,128)S(1)} %copy.16.wind_ref.refs_7_, f32[12,8,128]{2,1,0:T(8,128)S(1)} %broadcast_in_dim.13.taby_ref, f32[8,128]{1,0:T(8,128)S(1)} %get-tuple-element.21.rest_0_.refs_11_), custom_call_target="tpu_custom_call" | custom-call | flops 13271040 | bytes 1327104 | tf_op jit(solution)/shard_map/pallas_call | solution.py:279
  126.5 0.0 collective-permute-done.6.refs_5_
  126.5 0.0 collective-permute-done.7.refs_6_
  126.5 0.0 collective-permute-done.4.refs_3_
  126.5 0.0 collective-permute-done.5.refs_4_
  126.6 2.7 %shard_map.58 = (f32[9,12,8,128]{3,2,1,0:T(8,128)S(1)}, f32[3,12,8,128]{3,2,1,0:T(8,128)S(1)}, f32[3,12,8,128]{3,2,1,0:T(8,128)S(1)}, f32[9,3,8,128]{3,2,1,0:T(8,128)S(1)}, f32[9,3,8,128]{3,2,1,0:T(8,128)S(1)}) custom-call(s32[2]{0:T(128)S(1)} %add_convert_fusion.ends_ref, f32[9,12,8,128]{3,2,1,0:T(8,128)S(1)} %copy-done, ...), custom_call_target="tpu_custom_call" | custom-call | flops 13271040 | bytes 1327104 | tf_op jit(solution)/shard_map/pallas_call | solution.py:279
  129.2 1.9 %collective-permute-start.8 = (f32[3,12,8,128]{3,2,1,0:T(8,128)S(1)}, f32[3,12,8,128]{3,2,1,0:T(8,128)S(1)}, u32[]{:S(2)}, u32[]{:S(2)}) collective-permute-start(f32[3,12,8,128]{3,2,1,0:T(8,128)S(1)} %get-tuple-element.27), channel_id=1, source_target_pairs={{0,1},{1,2},{2,3},{3,4},{4,5},{5,6},{6,7},{8,9},{9,10},{10,11},{11... | collective-permute-start | bytes 442376 | tf_op jit(solution)/shard_map/ppermute | solution.py:238
  131.2 4.8 %collective-permute-start.9 = (f32[3,12,8,128]{3,2,1,0:T(8,128)S(1)}, f32[3,12,8,128]{3,2,1,0:T(8,128)S(1)}, u32[]{:S(2)}, u32[]{:S(2)}) collective-permute-start(f32[3,12,8,128]{3,2,1,0:T(8,128)S(1)} %get-tuple-element.28), channel_id=1, source_target_pairs={{1,0},{2,1},{3,2},{4,3},{5,4},{6,5},{7,6},{9,8},{10,9},{11,10},{12... | collective-permute-start | bytes 442376 | tf_op jit(solution)/shard_map/ppermute | solution.py:239
  136.0 0.1 collective-permute-start.10
  136.1 1.7 collective-permute-start.11
  137.8 38.4 %shard_map.59.refs_2_ = f32[9,12,8,128]{3,2,1,0:T(8,128)S(1)} custom-call(f32[9,12,8,128]{3,2,1,0:T(8,128)S(1)} %get-tuple-element.26.s_ref.refs_1_, f32[2,9,128]{2,1,0:T(8,128)S(1)} %copy.16.wind_ref.refs_7_, f32[12,8,128]{2,1,0:T(8,128)S(1)} %broadcast_in_dim.13.taby_ref, f32[8,128]{1,0:T(8,128)S(1)} %get-tuple-element.21.rest_0_.refs_11_), custom_call_target="tpu_custom_call" | custom-call | flops 13271040 | bytes 1327104 | tf_op jit(solution)/shard_map/pallas_call | solution.py:279
  176.2 0.0 collective-permute-done.10.refs_5_
  176.2 0.0 collective-permute-done.11.refs_6_
  176.2 0.0 collective-permute-done.8.refs_3_
  176.3 0.0 collective-permute-done.9.refs_4_
  176.3 3.4 %shard_map.60 = f32[9,12,8,128]{3,2,1,0:T(8,128)} custom-call(s32[2]{0:T(128)S(1)} %add_convert_fusion.ends_ref, f32[9,12,8,128]{3,2,1,0:T(8,128)S(1)} %copy-done, f32[9,12,8,128]{3,2,1,0:T(8,128)S(1)} %get-tuple-element.26.s_ref.refs_1_, f32[9,12,8,128]{3,2,1,0:T(8,128)S(1)} %shard_map.59.refs_2_, f32[3,12,8,128]{3,2,1,0:T(8,128)S(1)} %collective-permute-done.8.refs_3_, ...), custom_call_target="tpu_custom_call" | custom-call | flops 13271040 | bytes 1327104 | tf_op jit(solution)/shard_map/pallas_call | solution.py:279
  (2 shorter events, 0.0 us)
Async XLA Ops:
  0.0 2.0 %copy-start = (f32[9,12,8,128]{3,2,1,0:T(8,128)S(1)}, f32[9,12,8,128]{3,2,1,0:T(8,128)}, u32[]{:S(2)}) copy-start(f32[9,12,8,128]{3,2,1,0:T(8,128)} %refs_0_.5) | copy-start | bytes 1327108
  1.0 75.0 %collective-permute-start.3 = (f32[9,3,8,128]{3,2,1,0:T(8,128)S(1)}, f32[9,3,8,128]{3,2,1,0:T(8,128)S(1)}, u32[]{:S(2)}, u32[]{:S(2)}) collective-permute-start(f32[9,3,8,128]{3,2,1,0:T(8,128)S(1)} %get-tuple-element.31), channel_id=1, source_target_pairs={{8,0},{16,8},{24,16},{0,24},{9,1},{17,9},{25,17},{1,25},{10,2},{18... | collective-permute-start | bytes 331784 | tf_op jit(solution)/shard_map/ppermute | solution.py:241
  2.0 74.0 %collective-permute-start.2 = (f32[9,3,8,128]{3,2,1,0:T(8,128)S(1)}, f32[9,3,8,128]{3,2,1,0:T(8,128)S(1)}, u32[]{:S(2)}, u32[]{:S(2)}) collective-permute-start(f32[9,3,8,128]{3,2,1,0:T(8,128)S(1)} %get-tuple-element.32), channel_id=1, source_target_pairs={{0,8},{8,16},{16,24},{24,0},{1,9},{9,17},{17,25},{25,1},{2,10},{10... | collective-permute-start | bytes 331784 | tf_op jit(solution)/shard_map/ppermute | solution.py:240
  2.0 74.0 %collective-permute-start.1 = (f32[3,12,8,128]{3,2,1,0:T(8,128)S(1)}, f32[3,12,8,128]{3,2,1,0:T(8,128)S(1)}, u32[]{:S(2)}, u32[]{:S(2)}) collective-permute-start(f32[3,12,8,128]{3,2,1,0:T(8,128)S(1)} %get-tuple-element.33), channel_id=1, source_target_pairs={{1,0},{2,1},{3,2},{4,3},{5,4},{6,5},{7,6},{9,8},{10,9},{11,10},{12... | collective-permute-start | bytes 442376 | tf_op jit(solution)/shard_map/ppermute | solution.py:239
  5.4 70.7 %collective-permute-start = (f32[3,12,8,128]{3,2,1,0:T(8,128)S(1)}, f32[3,12,8,128]{3,2,1,0:T(8,128)S(1)}, u32[]{:S(2)}, u32[]{:S(2)}) collective-permute-start(f32[3,12,8,128]{3,2,1,0:T(8,128)S(1)} %get-tuple-element.34), channel_id=1, source_target_pairs={{0,1},{1,2},{2,3},{3,4},{4,5},{5,6},{6,7},{8,9},{9,10},{10,11},{11... | collective-permute-start | bytes 442376 | tf_op jit(solution)/shard_map/ppermute | solution.py:238
  7.9 0.7 copy-start.4
  8.8 0.7 copy-start.3
  76.0 0.7 copy-start.1
  76.0 0.7 copy-start.2
  79.5 47.0 %collective-permute-start.4 = (f32[3,12,8,128]{3,2,1,0:T(8,128)S(1)}, f32[3,12,8,128]{3,2,1,0:T(8,128)S(1)}, u32[]{:S(2)}, u32[]{:S(2)}) collective-permute-start(f32[3,12,8,128]{3,2,1,0:T(8,128)S(1)} %get-tuple-element.22), channel_id=1, source_target_pairs={{0,1},{1,2},{2,3},{3,4},{4,5},{5,6},{6,7},{8,9},{9,10},{10,11},{11... | collective-permute-start | bytes 442376 | tf_op jit(solution)/shard_map/ppermute | solution.py:238
  81.5 45.1 %collective-permute-start.5 = (f32[3,12,8,128]{3,2,1,0:T(8,128)S(1)}, f32[3,12,8,128]{3,2,1,0:T(8,128)S(1)}, u32[]{:S(2)}, u32[]{:S(2)}) collective-permute-start(f32[3,12,8,128]{3,2,1,0:T(8,128)S(1)} %get-tuple-element.23), channel_id=1, source_target_pairs={{1,0},{2,1},{3,2},{4,3},{5,4},{6,5},{7,6},{9,8},{10,9},{11,10},{12... | collective-permute-start | bytes 442376 | tf_op jit(solution)/shard_map/ppermute | solution.py:239
  86.3 40.2 %collective-permute-start.6 = (f32[9,3,8,128]{3,2,1,0:T(8,128)S(1)}, f32[9,3,8,128]{3,2,1,0:T(8,128)S(1)}, u32[]{:S(2)}, u32[]{:S(2)}) collective-permute-start(f32[9,3,8,128]{3,2,1,0:T(8,128)S(1)} %get-tuple-element.24), channel_id=1, source_target_pairs={{0,8},{8,16},{16,24},{24,0},{1,9},{9,17},{17,25},{25,1},{2,10},{10... | collective-permute-start | bytes 331784 | tf_op jit(solution)/shard_map/ppermute | solution.py:240
  86.4 40.2 %collective-permute-start.7 = (f32[9,3,8,128]{3,2,1,0:T(8,128)S(1)}, f32[9,3,8,128]{3,2,1,0:T(8,128)S(1)}, u32[]{:S(2)}, u32[]{:S(2)}) collective-permute-start(f32[9,3,8,128]{3,2,1,0:T(8,128)S(1)} %get-tuple-element.25), channel_id=1, source_target_pairs={{8,0},{16,8},{24,16},{0,24},{9,1},{17,9},{25,17},{1,25},{10,2},{18... | collective-permute-start | bytes 331784 | tf_op jit(solution)/shard_map/ppermute | solution.py:241
  129.2 47.0 %collective-permute-start.8 = (f32[3,12,8,128]{3,2,1,0:T(8,128)S(1)}, f32[3,12,8,128]{3,2,1,0:T(8,128)S(1)}, u32[]{:S(2)}, u32[]{:S(2)}) collective-permute-start(f32[3,12,8,128]{3,2,1,0:T(8,128)S(1)} %get-tuple-element.27), channel_id=1, source_target_pairs={{0,1},{1,2},{2,3},{3,4},{4,5},{5,6},{6,7},{8,9},{9,10},{10,11},{11... | collective-permute-start | bytes 442376 | tf_op jit(solution)/shard_map/ppermute | solution.py:238
  131.2 45.1 %collective-permute-start.9 = (f32[3,12,8,128]{3,2,1,0:T(8,128)S(1)}, f32[3,12,8,128]{3,2,1,0:T(8,128)S(1)}, u32[]{:S(2)}, u32[]{:S(2)}) collective-permute-start(f32[3,12,8,128]{3,2,1,0:T(8,128)S(1)} %get-tuple-element.28), channel_id=1, source_target_pairs={{1,0},{2,1},{3,2},{4,3},{5,4},{6,5},{7,6},{9,8},{10,9},{11,10},{12... | collective-permute-start | bytes 442376 | tf_op jit(solution)/shard_map/ppermute | solution.py:239
  136.0 40.2 %collective-permute-start.10 = (f32[9,3,8,128]{3,2,1,0:T(8,128)S(1)}, f32[9,3,8,128]{3,2,1,0:T(8,128)S(1)}, u32[]{:S(2)}, u32[]{:S(2)}) collective-permute-start(f32[9,3,8,128]{3,2,1,0:T(8,128)S(1)} %get-tuple-element.29), channel_id=1, source_target_pairs={{0,8},{8,16},{16,24},{24,0},{1,9},{9,17},{17,25},{25,1},{2,10},{10... | collective-permute-start | bytes 331784 | tf_op jit(solution)/shard_map/ppermute | solution.py:240
  136.1 40.2 %collective-permute-start.11 = (f32[9,3,8,128]{3,2,1,0:T(8,128)S(1)}, f32[9,3,8,128]{3,2,1,0:T(8,128)S(1)}, u32[]{:S(2)}, u32[]{:S(2)}) collective-permute-start(f32[9,3,8,128]{3,2,1,0:T(8,128)S(1)} %get-tuple-element.30), channel_id=1, source_target_pairs={{8,0},{16,8},{24,16},{0,24},{9,1},{17,9},{25,17},{1,25},{10,2},{18... | collective-permute-start | bytes 331784 | tf_op jit(solution)/shard_map/ppermute | solution.py:241

commit v2 on v1

--- a/solution.py
+++ b/solution.py
@@ -59,46 +59,46 @@
     return out
 
 
-def tile_terms(cell, axis, step):
-    count = cell.shape[axis]
+def tile_terms(cell, step):
+    count = cell.shape[1]
     eps = epsilon * step * step
-    place = lax.broadcasted_iota(jnp.int32, cell.shape, axis)
-    first = place == 0
-    last = place == count - 1
+    flat = 1.0 / (eps * eps)
+    place = lax.broadcasted_iota(jnp.int32, cell.shape, 1)
 
     def after(value, by=1):
-        return pltpu.roll(value, count - by, axis)
-
-    def before(value):
-        return pltpu.roll(value, 1, axis)
-
-    ahead = jnp.where(last, 0.0, after(cell) - cell)
-    behind = before(ahead)
+        return pltpu.roll(value, count - by, 1)
+
+    def before(value, by=1):
+        return pltpu.roll(value, by, 1)
+
+    up1 = jnp.where(place == count - 1, cell, after(cell))
+    up2 = jnp.where(place >= count - 2, up1, after(cell, 2))
+    dn1 = jnp.where(place == 0, cell, before(cell))
+    dn2 = jnp.where(place <= 1, dn1, before(cell, 2))
+    ahead = up1 - cell
+    behind = cell - dn1
+    bend_l = behind - (dn1 - dn2)
     bend = ahead - behind
-    wrapped = before(bend)
-    turn_lo = bend - jnp.where(first, 0.0, wrapped)
-    turn_hi = jnp.where(last, -bend, after(turn_lo))
-    jerk = turn_hi - turn_lo
-    jerk_l = jnp.where(first, bend, before(jerk))
-    jerk_r = jnp.where(last, bend, after(jerk))
-    bend_l = jnp.where(first, 0.0, wrapped)
-    level = turn_lo * turn_lo * (4.0 / 3.0) + eps
-    ia = inverse(level + bend * (bend + turn_lo))
-    ib = inverse(level + bend * bend_l)
-    turn_ring = jnp.where(first, -wrapped, turn_lo)
-    level_ring = turn_ring * turn_ring * (4.0 / 3.0) + eps
-    ic = inverse(level_ring + wrapped * (wrapped - turn_ring))
-    ib_ring = jnp.where(first, inverse(level_ring), ib)
+    bend_r = (up2 - up1) - ahead
+    turn_l = bend - bend_l
+    turn_r = bend_r - bend
+    jerk = turn_r - turn_l
+    level_l = turn_l * turn_l * (4.0 / 3.0) + eps
+    level_r = turn_r * turn_r * (4.0 / 3.0) + eps
+    ia = inverse(level_l + bend * (bend + turn_l))
+    ib = inverse(level_l + bend * bend_l)
+    jb = inverse(level_r + bend * bend_r)
+    jc = inverse(level_r + bend * (bend - turn_r))
     a1 = ia * ia
-    b1 = ib * ib * 6.0
-    c_low = ic * ic
-    b0 = after(ib_ring * ib_ring * 6.0)
-    flat = 1.0 / (eps * eps)
-    a2 = jnp.where(first, flat, before(a1))
-    c0 = after(c_low)
-    c1 = jnp.where(last, flat, after(c_low, 2))
-    base = (ahead + behind) * 6.0 - (turn_lo + turn_hi)
-    minus, plus = sides(jerk_l, jerk, jerk_r, a2, a1, b1, b0, c0, c1)
+    c0 = jc * jc
+    a2 = jnp.where(place == 0, flat, before(a1))
+    c1 = jnp.where(place == count - 1, flat, after(c0))
+    jerk_l = jnp.where(place == 0, bend, before(jerk))
+    jerk_r = jnp.where(place == count - 1, bend, after(jerk))
+    base = (ahead + behind) * 6.0 - (turn_l + turn_r)
+    minus, plus = sides(
+        jerk_l, jerk, jerk_r, a2, a1, ib * ib * 6.0, jb * jb * 6.0, c0, c1
+    )
     return base + (plus - minus), (plus + minus) - jerk
 
 
@@ -106,43 +106,81 @@
     return jnp.broadcast_to(row, like)
 
 
-def inner_kernel(split, speed_step, s_ref, wind_ref, taby_ref, *rest):
-    planes, headings = s_ref.shape[:2]
-    tile = s_ref.shape[2:]
+def inner_kernel(split, speed_step, s_ref, wind_ref, tab_ref, *rest):
+    planes, headings, speeds, width = s_ref.shape
+    tile = (speeds, width)
     gain = 1.0 / (12.0 * spacing)
     gain_v = thrust_limit / (12.0 * speed_step)
     if split:
         part_ref, extra_ref = rest
     else:
         pk_ref, part_ref = rest
+    cells = planes * headings
+    group = 8
+    s_rows = s_ref.reshape(cells * speeds, width)
+    part_rows = part_ref.reshape(cells * speeds, width)
+
+    def speed_group(g, carry):
+        start = jnp.minimum(g * group, cells - group) * speeds
+        lines = [
+            s_rows[pl.ds(start + k, group, stride=speeds), :] for k in range(speeds)
+        ]
+        ends = [lines[0]] * rim + lines + [lines[-1]] * rim
+        for k, (mean, gap) in enumerate(row_terms(ends, speed_step)):
+            part_rows[pl.ds(start + k, group, stride=speeds), :] = gain_v * (
+                gap - jnp.abs(mean)
+            )
+        return carry
+
+    lax.fori_loop(0, -(-cells // group), speed_group, 0)
 
     def plane(i, carry):
-        wind = splat(wind_ref[1, pl.ds(i, 1), :] * gain, tile)
-
-        def heading(j, inner):
-            cell = s_ref[i, j]
-            mean, gap = tile_terms(cell, 1, spacing)
-            mean_v, gap_v = tile_terms(cell, 0, speed_step)
-            part = mean * (taby_ref[j] + wind) + gain_v * (gap_v - jnp.abs(mean_v))
+        wind = splat(wind_ref[i, 1:2, :] * gain, tile)
+        for j in range(headings):
+            mean, gap = tile_terms(s_ref[i, j], spacing)
+            part = part_ref[i, j] + mean * (tab_ref[1, j] + wind)
             if split:
                 part_ref[i, j] = part
                 extra_ref[i, j] = gap
             else:
                 part_ref[i, j] = part + gap * splat(pk_ref[1:2, :] * gain, tile)
-            return inner
-
-        return lax.fori_loop(0, headings, heading, carry)
+        return carry
 
     lax.fori_loop(0, planes, plane, 0)
 
 
-def peaks_into(pk_ref, gathered_ref, bounds, heading_step, speed_step):
-    peaks = []
-    for q in range(2):
-        rows = [gathered_ref[g, q] for g in range(gathered_ref.shape[0])]
-        top = jnp.max(functools.reduce(jnp.maximum, rows), axis=(0, 1), keepdims=True)
-        low = jnp.min(functools.reduce(jnp.minimum, rows), axis=(0, 1), keepdims=True)
-        peaks.append(jnp.maximum(top + bounds[q][1], -(low + bounds[q][0])))
+def opening_kernel(level_ref, wind_in, mask_in, depth_in, *refs):
+    edge_refs, (wind_ref, mask_ref, depth_ref, most_ref, sems) = refs[:4], refs[4:]
+    planes, headings = level_ref.shape[:2]
+    pairs = [
+        (wind_in, wind_ref),
+        (level_ref.at[:rim], edge_refs[0]),
+        (level_ref.at[planes - rim :], edge_refs[1]),
+        (level_ref.at[:, :rim], edge_refs[2]),
+        (level_ref.at[:, headings - rim :], edge_refs[3]),
+        (mask_in, mask_ref),
+        (depth_in, depth_ref),
+    ]
+    copies = [
+        pltpu.make_async_copy(src, dst, sems.at[k]) for k, (src, dst) in enumerate(pairs)
+    ]
+    for copy in copies:
+        copy.start()
+    copies[0].wait()
+    rows = [wind_ref[i] for i in range(planes)]
+    most_ref[...] = jnp.zeros_like(most_ref)
+    most_ref[0:2, :] = functools.reduce(jnp.maximum, rows)
+    most_ref[2:4, :] = -functools.reduce(jnp.minimum, rows)
+    for copy in copies[1:]:
+        copy.wait()
+
+
+def peaks_into(pk_ref, most_ref, bounds, heading_step, speed_step):
+    most = jnp.max(most_ref[...], axis=1, keepdims=True)
+    peaks = [
+        jnp.maximum(most[q : q + 1] + bounds[q][1], most[q + 2 : q + 3] - bounds[q][0])
+        for q in range(2)
+    ]
     time_step = courant / (
         peaks[0] / spacing
         + peaks[1] / spacing
@@ -162,9 +200,9 @@
     s_ref, part_ref = refs.pop(0), refs.pop(0)
     extra_ref = refs.pop(0) if section == 1 else None
     xlo_ref, xhi_ref, tlo_ref, thi_ref = (refs.pop(0) for _ in range(4))
-    wind_ref, tabx_ref, mask_ref, depth_ref = (refs.pop(0) for _ in range(4))
+    wind_ref, tab_ref, mask_ref, depth_ref = (refs.pop(0) for _ in range(4))
     if section == 1:
-        gathered_ref = refs.pop(0)
+        most_ref = refs.pop(0)
     else:
         pk_ref = refs.pop(0)
     out_ref = refs.pop(0)
@@ -178,7 +216,7 @@
     gain = 1.0 / (12.0 * spacing)
     gain_t = turn_limit / (12.0 * heading_step)
     if section == 1:
-        peaks_into(pk_ref, gathered_ref, bounds, heading_step, speed_step)
+        peaks_into(pk_ref, most_ref, bounds, heading_step, speed_step)
     at_low = ends_ref[0] == 1
     at_high = ends_ref[1] == 1
 
@@ -187,9 +225,9 @@
         lows = [jnp.where(at_low, cells[0], xlo_ref[k, j]) for k in range(rim)]
         highs = [jnp.where(at_high, cells[-1], xhi_ref[k, j]) for k in range(rim)]
         peak = splat(pk_ref[0:1, :] * gain, tile)
-        table = tabx_ref[j]
+        table = tab_ref[0, j]
         for i, (mean, gap) in enumerate(row_terms(lows + cells + highs, spacing)):
-            flow = table + splat(wind_ref[0, i : i + 1, :] * gain, tile)
+            flow = table + splat(wind_ref[i, 0:1, :] * gain, tile)
             total = part_ref[i, j] + (mean * flow + gap * peak)
             if section == 1:
                 total = total + extra_ref[i, j] * splat(pk_ref[1:2, :] * gain, tile)
@@ -242,6 +280,18 @@
     return from_low, from_high, from_left, from_right
 
 
+def most_of_all(most):
+    size, reach = lax.axis_size("gx"), 1
+    while reach < size:
+        if size & (size - 1):
+            pairs = [(i, (i + reach) % size) for i in range(size)]
+        else:
+            pairs = [(i, i ^ reach) for i in range(size)]
+        most = jnp.maximum(most, lax.ppermute(most, "gx", pairs))
+        reach *= 2
+    return most
+
+
 def local(level_set, wind_field, target_mask, target_depth):
     planes, headings, speed_count, cross_count = level_set.shape
     heading_total = headings * lax.axis_size("head")
@@ -260,9 +310,8 @@
     first_heading = lax.axis_index("head") * headings
     position = lax.axis_index("gx")
     ends = jnp.stack([position == 0, position == lax.axis_size("gx") - 1]).astype(jnp.int32)
-    tables = lax.dynamic_slice_in_dim(jnp.asarray(np.stack(tables)), first_heading, headings, 1)
-    tables = jnp.broadcast_to(tables[..., None], (2, headings, speed_count, cross_count))
-    gathered = lax.all_gather(wind_field, "gx")
+    tables = np.stack(tables)[..., None] * np.ones(cross_count, np.float32)
+    tables = lax.dynamic_slice_in_dim(jnp.asarray(tables), first_heading, headings, 1)
 
     vmem = pl.BlockSpec(memory_space=pltpu.VMEM)
     smem = pl.BlockSpec(memory_space=pltpu.SMEM)
@@ -288,22 +337,33 @@
             ),
         )(*ins)
 
+    hbm = pl.BlockSpec(memory_space=pltpu.HBM)
+    *edges, wind, mask, depth, most = pl.pallas_call(
+        opening_kernel,
+        out_shape=[x_edge, x_edge, t_edge, t_edge]
+        + [
+            jax.ShapeDtypeStruct((planes, 2, cross_count), jnp.float32),
+            jax.ShapeDtypeStruct(target_mask.shape, target_mask.dtype),
+            jax.ShapeDtypeStruct(target_depth.shape, jnp.float32),
+            pk_shape,
+        ],
+        in_specs=[hbm] * 4,
+        out_specs=[vmem] * 8,
+        scratch_shapes=[pltpu.SemaphoreType.DMA((7,))],
+        cost_estimate=pl.CostEstimate(flops=0, bytes_accessed=8 * cells, transcendentals=0),
+    )(level_set, jnp.transpose(wind_field, (1, 0, 2)), target_mask, target_depth)
     values, pk = level_set, None
-    edges = (
-        level_set[:rim],
-        level_set[planes - rim :],
-        level_set[:, :rim],
-        level_set[:, headings - rim :],
-    )
     for section in (1, 2, 3):
         ghosts = swap(edges)
+        if section == 1:
+            most = most_of_all(most)
         inner = functools.partial(inner_kernel, section == 1, speed_step)
-        ins = [values, wind_field, tables[1]] + ([] if section == 1 else [pk])
+        ins = [values, wind, tables] + ([] if section == 1 else [pk])
         parts = call(inner, ins, [field] * (2 if section == 1 else 1), [], 120, False)
         outer = functools.partial(outer_kernel, section, bounds, heading_step, speed_step)
         ins = [ends] + ([] if section == 1 else [level_set]) + [values, *parts, *ghosts]
-        ins += [wind_field, tables[0], target_mask, target_depth]
-        ins += [gathered] if section == 1 else [pk]
+        ins += [wind, tables, mask, depth]
+        ins += [most] if section == 1 else [pk]
         outs = [field]
         if section < 3:
             outs += [x_edge, x_edge, t_edge, t_edge]

time: 180 us -> 56.9 us (0.32)
  Pallas kernels: 124 us -> 20.4 us
  blocking collectives: 28.1 us -> 0 us
  starting transfers between devices: 23.9 us -> 29.7 us
  waiting for transfers between devices: 0.03 us -> 3.44 us
    pallas_call x6, Pallas kernels: 124 us -> 18.4 us  [call(): pl.pallas_call(kernel, out_shape=outs, in_specs=specs, out_specs=[vmem] *...]
    all_gather x1 -> x0, blocking collectives: 28.1 us -> none  [local(): gathered = lax.all_gather(wind_field, 'gx')]
    ppermute x0 -> x3, starting transfers between devices: none -> 4.18 us  [most_of_all(): most = jnp.maximum(most, lax.ppermute(most, 'gx', pairs))]
    ppermute x0 -> x3, waiting for transfers between devices: none -> 2.7 us  [most_of_all(): most = jnp.maximum(most, lax.ppermute(most, 'gx', pairs))]
    pallas_call x0 -> x1, Pallas kernels: none -> 2.02 us  [local(): pl.pallas_call(opening_kernel, out_shape=[x_edge, x_edge, t_edge, t_edge]...]
  transfers between devices with their start and end apart: 12 -> 15, of which waited for: 0 -> 2; matrix products, arithmetic and copies ran while one was open for 0% -> 2% of each run, Pallas kernels for 64% -> 17%
where the time goes in v2:
time: 56.9 us; the launch traced here: 56.1 us
  starting transfers between devices  29.7 us (52%)
  Pallas kernels  20.4 us (36%)
  waiting for transfers between devices  3.44 us (6%)
  local copies, waits for them, and re-layouts  2.2 us (4%)
    pallas_call x6, Pallas kernels, call(): pl.pallas_call(kernel, out_shape=outs, in_specs=specs, out_specs=[vmem] *...  18.4 us
    ppermute x3, starting transfers between devices, swap(): from_high = lax.ppermute(x_low, 'gx', x_down)  14 us
    ppermute x3, starting transfers between devices, swap(): from_low = lax.ppermute(x_high, 'gx', x_up)  6.24 us
    ppermute x3, starting transfers between devices, swap(): from_right = lax.ppermute(t_low, 'head', t_down)  4.99 us
    ppermute x3, starting transfers between devices, most_of_all(): most = jnp.maximum(most, lax.ppermute(most, 'gx', pairs))  4.18 us
    ppermute x3, waiting for transfers between devices, most_of_all(): most = jnp.maximum(most, lax.ppermute(most, 'gx', pairs))  2.7 us
    pallas_call x1, Pallas kernels, local(): pl.pallas_call(opening_kernel, out_shape=[x_edge, x_edge, t_edge, t_edge]...  2.02 us
    unnamed x10, local copies, waits for them, and re-layouts  1.3 us
  transfers between devices with their start and end apart: 15, of which 2 were waited for; matrix products, arithmetic and copies ran while one was open for 2% of the time, Pallas kernels for 17%

profile of v2, /device:TPU:8, one launch (start us, length us, event | category | flops | bytes accessed | tf_op | source)
XLA Modules:
  0.0 56.1 jit_solution(17320164685745344898)
XLA Ops:
  0.0 0.0 copy-start
  0.0 2.0 %shard_map.55 = (f32[3,12,8,128]{3,2,1,0:T(8,128)}, f32[3,12,8,128]{3,2,1,0:T(8,128)}, f32[9,3,8,128]{3,2,1,0:T(8,128)}, f32[9,3,8,128]{3,2,1,0:T(8,128)}, f32[9...) custom-call(f32[9,12,8,128]{3,2,1,0:T(8,128)} %refs_0_.5, f32[9,2,128]{2,1,0:T(2,128)} %bitcast.3, ...), custom_call_target="tpu_custom_call" | custom-call | bytes 884736 | tf_op jit(solution)/shard_map/pallas_call | solution.py:341
  2.0 1.6 %collective-permute-start.4 = (f32[8,128]{1,0:T(8,128)}, f32[8,128]{1,0:T(8,128)S(1)}, u32[]{:S(2)}, u32[]{:S(2)}) collective-permute-start(f32[8,128]{1,0:T(8,128)} %get-tuple-element.35), channel_id=1, source_target_pairs={{0,1},{1,0},{2,3},{3,2},{4,5},{5,4},{6,7},{7,6},{8,9},{9,8},{10,11... | collective-permute-start | bytes 12296 | tf_op jit(solution)/shard_map/ppermute | solution.py:290
  3.6 0.0 collective-permute-start.2
  3.6 1.7 %collective-permute-start.3 = (f32[9,3,8,128]{3,2,1,0:T(8,128)}, f32[9,3,8,128]{3,2,1,0:T(8,128)S(1)}, u32[]{:S(2)}, u32[]{:S(2)}) collective-permute-start(f32[9,3,8,128]{3,2,1,0:T(8,128)} %get-tuple-element.32), channel_id=1, source_target_pairs={{8,0},{16,8},{24,16},{0,24},{9,1},{17,9},{25,17},{1,25},{10,2},{18... | collective-permute-start | bytes 331784 | tf_op jit(solution)/shard_map/ppermute | solution.py:279
  5.4 2.4 %collective-permute-start = (f32[3,12,8,128]{3,2,1,0:T(8,128)}, f32[3,12,8,128]{3,2,1,0:T(8,128)S(1)}, u32[]{:S(2)}, u32[]{:S(2)}) collective-permute-start(f32[3,12,8,128]{3,2,1,0:T(8,128)} %get-tuple-element.29), channel_id=1, source_target_pairs={{0,1},{1,2},{2,3},{3,4},{4,5},{5,6},{6,7},{8,9},{9,10},{10,11},{11... | collective-permute-start | bytes 442376 | tf_op jit(solution)/shard_map/ppermute | solution.py:276
  7.8 4.3 %collective-permute-start.1 = (f32[3,12,8,128]{3,2,1,0:T(8,128)}, f32[3,12,8,128]{3,2,1,0:T(8,128)S(1)}, u32[]{:S(2)}, u32[]{:S(2)}) collective-permute-start(f32[3,12,8,128]{3,2,1,0:T(8,128)} %get-tuple-element.30), channel_id=1, source_target_pairs={{1,0},{2,1},{3,2},{4,3},{5,4},{6,5},{7,6},{9,8},{10,9},{11,10},{12... | collective-permute-start | bytes 442376 | tf_op jit(solution)/shard_map/ppermute | solution.py:277
  12.1 0.0 copy-start.4
  12.1 0.0 collective-permute-done.4
  12.1 0.7 %copy-done.4 = f32[8,128]{1,0:T(8,128)S(1)} copy-done((f32[8,128]{1,0:T(8,128)S(1)}, f32[8,128]{1,0:T(8,128)}, u32[]{:S(2)}) %copy-start.4) | copy-done | bytes 4120
  12.8 0.0 collective-permute-start.5
  12.8 0.9 %constant_dynamic-slice_fusion.tab_ref.refs_8_ = f32[2,12,8,128]{3,2,1,0:T(8,128)S(1)} fusion(f32[2,48,8,128]{3,2,1,0:T(8,128)} %constant.18.clone, s32[]{:T(128)S(6)} %select_n.3), kind=kLoop, calls=%fused_computation.1 | loop fusion | bytes 196612 | tf_op jit(solution)/shard_map/dynamic_slice | solution.py:314
  13.7 0.0 copy-start.1
  13.7 2.7 %collective-permute-done.5 = f32[8,128]{1,0:T(8,128)S(1)} collective-permute-done((f32[8,128]{1,0:T(8,128)S(1)}, f32[8,128]{1,0:T(8,128)S(1)}, u32[]{:S(2)}, u32[]{:S(2)}) %collective-permute-start.5) | collective-permute-done | bytes 4128 | tf_op jit(solution)/shard_map/ppermute | solution.py:290
  16.4 2.6 %collective-permute-start.6 = (f32[8,128]{1,0:T(8,128)S(1)}, f32[8,128]{1,0:T(8,128)S(1)}, u32[]{:S(2)}, u32[]{:S(2)}) collective-permute-start(f32[8,128]{1,0:T(8,128)S(1)} %max.10), channel_id=1, source_target_pairs={{0,4},{1,5},{2,6},{3,7},{4,0},{5,1},{6,2},{7,3},{8,12},{9,13},{10,... | collective-permute-start | bytes 12296 | tf_op jit(solution)/shard_map/ppermute | solution.py:290
  19.0 0.1 add_convert_fusion.ends_ref
  19.1 0.0 copy-done
  19.1 0.0 copy-done.1
  19.1 3.2 %shard_map.56 = (f32[9,12,8,128]{3,2,1,0:T(8,128)S(1)}, f32[9,12,8,128]{3,2,1,0:T(8,128)S(1)}) custom-call(f32[9,12,8,128]{3,2,1,0:T(8,128)S(1)} %copy-done, f32[9,2,128]{2,1,0:T(2,128)S(1)} %copy-done.1, f32[2,12,8,128]{3,2,1,0:T(8,128)S(1)} %constant_dynamic-slice_fusion.tab_ref.refs_8_), custom_call_target="tpu_custom_call" | custom-call | flops 13271040 | bytes 1327104 | tf_op jit(solution)/shard_map/pallas_call | solution.py:328
  22.2 0.0 copy-start.2
  22.3 0.0 copy-start.3
  22.3 0.0 collective-permute-done.6
  22.3 0.0 collective-permute-done.2.refs_5_
  22.3 0.0 collective-permute-done.3.refs_6_
  22.3 0.0 collective-permute-done.refs_3_
  22.3 0.0 collective-permute-done.1.refs_4_
  22.3 0.6 %copy-done.2 = s32[9,128]{1,0:T(8,128)S(1)} copy-done((s32[9,128]{1,0:T(8,128)S(1)}, s32[9,128]{1,0:T(8,128)}, u32[]{:S(2)}) %copy-start.2) | copy-done | bytes 4632
  22.9 0.0 copy-done.3
  23.0 2.8 %shard_map.57 = (f32[9,12,8,128]{3,2,1,0:T(8,128)S(1)}, f32[3,12,8,128]{3,2,1,0:T(8,128)S(1)}, f32[3,12,8,128]{3,2,1,0:T(8,128)S(1)}, f32[9,3,8,128]{3,2,1,0:T(8...) custom-call(s32[2]{0:T(128)S(1)} %add_convert_fusion.ends_ref, f32[9,12,8,128]{3,2,1,0:T(8,128)S(1)} %copy-done, ...), custom_call_target="tpu_custom_call" | custom-call | flops 13271040 | bytes 1327104 | tf_op jit(solution)/shard_map/pallas_call | solution.py:328
  25.8 1.9 %collective-permute-start.7 = (f32[3,12,8,128]{3,2,1,0:T(8,128)S(1)}, f32[3,12,8,128]{3,2,1,0:T(8,128)S(1)}, u32[]{:S(2)}, u32[]{:S(2)}) collective-permute-start(f32[3,12,8,128]{3,2,1,0:T(8,128)S(1)} %get-tuple-element.38), channel_id=1, source_target_pairs={{0,1},{1,2},{2,3},{3,4},{4,5},{5,6},{6,7},{8,9},{9,10},{10,11},{11... | collective-permute-start | bytes 442376 | tf_op jit(solution)/shard_map/ppermute | solution.py:276
  27.7 4.8 %collective-permute-start.8 = (f32[3,12,8,128]{3,2,1,0:T(8,128)S(1)}, f32[3,12,8,128]{3,2,1,0:T(8,128)S(1)}, u32[]{:S(2)}, u32[]{:S(2)}) collective-permute-start(f32[3,12,8,128]{3,2,1,0:T(8,128)S(1)} %get-tuple-element.39), channel_id=1, source_target_pairs={{1,0},{2,1},{3,2},{4,3},{5,4},{6,5},{7,6},{9,8},{10,9},{11,10},{12... | collective-permute-start | bytes 442376 | tf_op jit(solution)/shard_map/ppermute | solution.py:277
  32.5 0.1 collective-permute-start.9
  32.6 1.7 %collective-permute-start.10 = (f32[9,3,8,128]{3,2,1,0:T(8,128)S(1)}, f32[9,3,8,128]{3,2,1,0:T(8,128)S(1)}, u32[]{:S(2)}, u32[]{:S(2)}) collective-permute-start(f32[9,3,8,128]{3,2,1,0:T(8,128)S(1)} %get-tuple-element.41), channel_id=1, source_target_pairs={{8,0},{16,8},{24,16},{0,24},{9,1},{17,9},{25,17},{1,25},{10,2},{18... | collective-permute-start | bytes 331784 | tf_op jit(solution)/shard_map/ppermute | solution.py:279
  34.3 3.2 %shard_map.58.refs_2_ = f32[9,12,8,128]{3,2,1,0:T(8,128)S(1)} custom-call(f32[9,12,8,128]{3,2,1,0:T(8,128)S(1)} %get-tuple-element.36.s_ref.refs_1_, f32[9,2,128]{2,1,0:T(2,128)S(1)} %copy-done.1, f32[2,12,8,128]{3,2,1,0:T(8,128)S(1)} %constant_dynamic-slice_fusion.tab_ref.refs_8_, f32[8,128]{1,0:T(8,128)S(1)} %get-tuple-element.37.rest_0_.refs_11_), custom_call_target="tpu_custom_call" | custom-call | flops 13271040 | bytes 1327104 | tf_op jit(solution)/shard_map/pallas_call | solution.py:328
  37.5 0.0 collective-permute-done.9.refs_5_
  37.5 0.0 collective-permute-done.10.refs_6_
  37.5 0.0 collective-permute-done.7.refs_3_
  37.5 0.0 collective-permute-done.8.refs_4_
  37.5 2.7 %shard_map.59 = (f32[9,12,8,128]{3,2,1,0:T(8,128)S(1)}, f32[3,12,8,128]{3,2,1,0:T(8,128)S(1)}, f32[3,12,8,128]{3,2,1,0:T(8,128)S(1)}, f32[9,3,8,128]{3,2,1,0:T(8,128)S(1)}, f32[9,3,8,128]{3,2,1,0:T(8,128)S(1)}) custom-call(s32[2]{0:T(128)S(1)} %add_convert_fusion.ends_ref, f32[9,12,8,128]{3,2,1,0:T(8,128)S(1)} %copy-done, ...), custom_call_target="tpu_custom_call" | custom-call | flops 13271040 | bytes 1327104 | tf_op jit(solution)/shard_map/pallas_call | solution.py:328
  40.2 1.9 %collective-permute-start.11 = (f32[3,12,8,128]{3,2,1,0:T(8,128)S(1)}, f32[3,12,8,128]{3,2,1,0:T(8,128)S(1)}, u32[]{:S(2)}, u32[]{:S(2)}) collective-permute-start(f32[3,12,8,128]{3,2,1,0:T(8,128)S(1)} %get-tuple-element.43), channel_id=1, source_target_pairs={{0,1},{1,2},{2,3},{3,4},{4,5},{5,6},{6,7},{8,9},{9,10},{10,11},{11... | collective-permute-start | bytes 442376 | tf_op jit(solution)/shard_map/ppermute | solution.py:276
  42.2 4.8 %collective-permute-start.12 = (f32[3,12,8,128]{3,2,1,0:T(8,128)S(1)}, f32[3,12,8,128]{3,2,1,0:T(8,128)S(1)}, u32[]{:S(2)}, u32[]{:S(2)}) collective-permute-start(f32[3,12,8,128]{3,2,1,0:T(8,128)S(1)} %get-tuple-element.44), channel_id=1, source_target_pairs={{1,0},{2,1},{3,2},{4,3},{5,4},{6,5},{7,6},{9,8},{10,9},{11,10},{12... | collective-permute-start | bytes 442376 | tf_op jit(solution)/shard_map/ppermute | solution.py:277
  47.0 0.3 collective-permute-start.13
  47.3 1.5 %collective-permute-start.14 = (f32[9,3,8,128]{3,2,1,0:T(8,128)S(1)}, f32[9,3,8,128]{3,2,1,0:T(8,128)S(1)}, u32[]{:S(2)}, u32[]{:S(2)}) collective-permute-start(f32[9,3,8,128]{3,2,1,0:T(8,128)S(1)} %get-tuple-element.46), channel_id=1, source_target_pairs={{8,0},{16,8},{24,16},{0,24},{9,1},{17,9},{25,17},{1,25},{10,2},{18... | collective-permute-start | bytes 331784 | tf_op jit(solution)/shard_map/ppermute | solution.py:279
  48.8 3.2 %shard_map.60.refs_2_ = f32[9,12,8,128]{3,2,1,0:T(8,128)S(1)} custom-call(f32[9,12,8,128]{3,2,1,0:T(8,128)S(1)} %get-tuple-element.42.s_ref.refs_1_, f32[9,2,128]{2,1,0:T(2,128)S(1)} %copy-done.1, f32[2,12,8,128]{3,2,1,0:T(8,128)S(1)} %constant_dynamic-slice_fusion.tab_ref.refs_8_, f32[8,128]{1,0:T(8,128)S(1)} %get-tuple-element.37.rest_0_.refs_11_), custom_call_target="tpu_custom_call" | custom-call | flops 13271040 | bytes 1327104 | tf_op jit(solution)/shard_map/pallas_call | solution.py:328
  52.0 0.0 collective-permute-done.13.refs_5_
  52.0 0.0 collective-permute-done.14.refs_6_
  52.0 0.0 collective-permute-done.11.refs_3_
  52.0 0.7 %collective-permute-done.12.refs_4_ = f32[3,12,8,128]{3,2,1,0:T(8,128)S(1)} collective-permute-done((f32[3,12,8,128]{3,2,1,0:T(8,128)S(1)}, f32[3,12,8,128]{3,2,1,0:T(8,128)S(1)}, u32[]{:S(2)}, u32[]{:S(2)}) %collective-permute-start.12) | collective-permute-done | bytes 147488 | tf_op jit(solution)/shard_map/ppermute | solution.py:277
  52.7 3.4 %shard_map.61 = f32[9,12,8,128]{3,2,1,0:T(8,128)} custom-call(s32[2]{0:T(128)S(1)} %add_convert_fusion.ends_ref, f32[9,12,8,128]{3,2,1,0:T(8,128)S(1)} %copy-done, f32[9,12,8,128]{3,2,1,0:T(8,128)S(1)} %get-tuple-element.42.s_ref.refs_1_, f32[9,12,8,128]{3,2,1,0:T(8,128)S(1)} %shard_map.60.refs_2_, f32[3,12,8,128]{3,2,1,0:T(8,128)S(1)} %collective-permute-done.11.refs_3_, ...), custom_call_target="tpu_custom_call" | custom-call | flops 13271040 | bytes 1327104 | tf_op jit(solution)/shard_map/pallas_call | solution.py:328
  (3 shorter events, 0.0 us)
Async XLA Ops:
  0.0 19.1 %copy-start = (f32[9,12,8,128]{3,2,1,0:T(8,128)S(1)}, f32[9,12,8,128]{3,2,1,0:T(8,128)}, u32[]{:S(2)}) copy-start(f32[9,12,8,128]{3,2,1,0:T(8,128)} %refs_0_.5) | copy-start | bytes 1327108
  2.0 10.1 %collective-permute-start.4 = (f32[8,128]{1,0:T(8,128)}, f32[8,128]{1,0:T(8,128)S(1)}, u32[]{:S(2)}, u32[]{:S(2)}) collective-permute-start(f32[8,128]{1,0:T(8,128)} %get-tuple-element.35), channel_id=1, source_target_pairs={{0,1},{1,0},{2,3},{3,2},{4,5},{5,4},{6,7},{7,6},{8,9},{9,8},{10,11... | collective-permute-start | bytes 12296 | tf_op jit(solution)/shard_map/ppermute | solution.py:290
  3.6 18.7 %collective-permute-start.2 = (f32[9,3,8,128]{3,2,1,0:T(8,128)}, f32[9,3,8,128]{3,2,1,0:T(8,128)S(1)}, u32[]{:S(2)}, u32[]{:S(2)}) collective-permute-start(f32[9,3,8,128]{3,2,1,0:T(8,128)} %get-tuple-element.31), channel_id=1, source_target_pairs={{0,8},{8,16},{16,24},{24,0},{1,9},{9,17},{17,25},{25,1},{2,10},{10... | collective-permute-start | bytes 331784 | tf_op jit(solution)/shard_map/ppermute | solution.py:278
  3.6 18.7 %collective-permute-start.3 = (f32[9,3,8,128]{3,2,1,0:T(8,128)}, f32[9,3,8,128]{3,2,1,0:T(8,128)S(1)}, u32[]{:S(2)}, u32[]{:S(2)}) collective-permute-start(f32[9,3,8,128]{3,2,1,0:T(8,128)} %get-tuple-element.32), channel_id=1, source_target_pairs={{8,0},{16,8},{24,16},{0,24},{9,1},{17,9},{25,17},{1,25},{10,2},{18... | collective-permute-start | bytes 331784 | tf_op jit(solution)/shard_map/ppermute | solution.py:279
  5.4 16.9 %collective-permute-start = (f32[3,12,8,128]{3,2,1,0:T(8,128)}, f32[3,12,8,128]{3,2,1,0:T(8,128)S(1)}, u32[]{:S(2)}, u32[]{:S(2)}) collective-permute-start(f32[3,12,8,128]{3,2,1,0:T(8,128)} %get-tuple-element.29), channel_id=1, source_target_pairs={{0,1},{1,2},{2,3},{3,4},{4,5},{5,6},{6,7},{8,9},{9,10},{10,11},{11... | collective-permute-start | bytes 442376 | tf_op jit(solution)/shard_map/ppermute | solution.py:276
  7.8 14.5 %collective-permute-start.1 = (f32[3,12,8,128]{3,2,1,0:T(8,128)}, f32[3,12,8,128]{3,2,1,0:T(8,128)S(1)}, u32[]{:S(2)}, u32[]{:S(2)}) collective-permute-start(f32[3,12,8,128]{3,2,1,0:T(8,128)} %get-tuple-element.30), channel_id=1, source_target_pairs={{1,0},{2,1},{3,2},{4,3},{5,4},{6,5},{7,6},{9,8},{10,9},{11,10},{12... | collective-permute-start | bytes 442376 | tf_op jit(solution)/shard_map/ppermute | solution.py:277
  12.1 0.7 %copy-start.4 = (f32[8,128]{1,0:T(8,128)S(1)}, f32[8,128]{1,0:T(8,128)}, u32[]{:S(2)}) copy-start(f32[8,128]{1,0:T(8,128)} %get-tuple-element.35) | copy-start | bytes 12292
  12.8 3.6 %collective-permute-start.5 = (f32[8,128]{1,0:T(8,128)S(1)}, f32[8,128]{1,0:T(8,128)S(1)}, u32[]{:S(2)}, u32[]{:S(2)}) collective-permute-start(f32[8,128]{1,0:T(8,128)S(1)} %max.9), channel_id=1, source_target_pairs={{0,2},{1,3},{2,0},{3,1},{4,6},{5,7},{6,4},{7,5},{8,10},{9,11},{10,... | collective-permute-start | bytes 12296 | tf_op jit(solution)/shard_map/ppermute | solution.py:290
  13.7 5.4 %copy-start.1 = (f32[9,2,128]{2,1,0:T(2,128)S(1)}, f32[9,2,128]{2,1,0:T(2,128)}, u32[]{:S(2)}) copy-start(f32[9,2,128]{2,1,0:T(2,128)} %get-tuple-element.26.wind_ref.refs_7_) | copy-start | bytes 27652
  16.4 5.9 %collective-permute-start.6 = (f32[8,128]{1,0:T(8,128)S(1)}, f32[8,128]{1,0:T(8,128)S(1)}, u32[]{:S(2)}, u32[]{:S(2)}) collective-permute-start(f32[8,128]{1,0:T(8,128)S(1)} %max.10), channel_id=1, source_target_pairs={{0,4},{1,5},{2,6},{3,7},{4,0},{5,1},{6,2},{7,3},{8,12},{9,13},{10,... | collective-permute-start | bytes 12296 | tf_op jit(solution)/shard_map/ppermute | solution.py:290
  22.2 0.7 %copy-start.2 = (s32[9,128]{1,0:T(8,128)S(1)}, s32[9,128]{1,0:T(8,128)}, u32[]{:S(2)}) copy-start(s32[9,128]{1,0:T(8,128)} %get-tuple-element.33.refs_9_) | copy-start | bytes 13828
  22.3 0.7 %copy-start.3 = (f32[9,128]{1,0:T(8,128)S(1)}, f32[9,128]{1,0:T(8,128)}, u32[]{:S(2)}) copy-start(f32[9,128]{1,0:T(8,128)} %get-tuple-element.34.refs_10_) | copy-start | bytes 13828
  25.8 11.8 %collective-permute-start.7 = (f32[3,12,8,128]{3,2,1,0:T(8,128)S(1)}, f32[3,12,8,128]{3,2,1,0:T(8,128)S(1)}, u32[]{:S(2)}, u32[]{:S(2)}) collective-permute-start(f32[3,12,8,128]{3,2,1,0:T(8,128)S(1)} %get-tuple-element.38), channel_id=1, source_target_pairs={{0,1},{1,2},{2,3},{3,4},{4,5},{5,6},{6,7},{8,9},{9,10},{10,11},{11... | collective-permute-start | bytes 442376 | tf_op jit(solution)/shard_map/ppermute | solution.py:276
  27.7 9.9 %collective-permute-start.8 = (f32[3,12,8,128]{3,2,1,0:T(8,128)S(1)}, f32[3,12,8,128]{3,2,1,0:T(8,128)S(1)}, u32[]{:S(2)}, u32[]{:S(2)}) collective-permute-start(f32[3,12,8,128]{3,2,1,0:T(8,128)S(1)} %get-tuple-element.39), channel_id=1, source_target_pairs={{1,0},{2,1},{3,2},{4,3},{5,4},{6,5},{7,6},{9,8},{10,9},{11,10},{12... | collective-permute-start | bytes 442376 | tf_op jit(solution)/shard_map/ppermute | solution.py:277
  32.5 5.0 %collective-permute-start.9 = (f32[9,3,8,128]{3,2,1,0:T(8,128)S(1)}, f32[9,3,8,128]{3,2,1,0:T(8,128)S(1)}, u32[]{:S(2)}, u32[]{:S(2)}) collective-permute-start(f32[9,3,8,128]{3,2,1,0:T(8,128)S(1)} %get-tuple-element.40), channel_id=1, source_target_pairs={{0,8},{8,16},{16,24},{24,0},{1,9},{9,17},{17,25},{25,1},{2,10},{10... | collective-permute-start | bytes 331784 | tf_op jit(solution)/shard_map/ppermute | solution.py:278
  32.6 4.9 %collective-permute-start.10 = (f32[9,3,8,128]{3,2,1,0:T(8,128)S(1)}, f32[9,3,8,128]{3,2,1,0:T(8,128)S(1)}, u32[]{:S(2)}, u32[]{:S(2)}) collective-permute-start(f32[9,3,8,128]{3,2,1,0:T(8,128)S(1)} %get-tuple-element.41), channel_id=1, source_target_pairs={{8,0},{16,8},{24,16},{0,24},{9,1},{17,9},{25,17},{1,25},{10,2},{18... | collective-permute-start | bytes 331784 | tf_op jit(solution)/shard_map/ppermute | solution.py:279
  40.2 11.8 %collective-permute-start.11 = (f32[3,12,8,128]{3,2,1,0:T(8,128)S(1)}, f32[3,12,8,128]{3,2,1,0:T(8,128)S(1)}, u32[]{:S(2)}, u32[]{:S(2)}) collective-permute-start(f32[3,12,8,128]{3,2,1,0:T(8,128)S(1)} %get-tuple-element.43), channel_id=1, source_target_pairs={{0,1},{1,2},{2,3},{3,4},{4,5},{5,6},{6,7},{8,9},{9,10},{10,11},{11... | collective-permute-start | bytes 442376 | tf_op jit(solution)/shard_map/ppermute | solution.py:276
  42.2 10.6 %collective-permute-start.12 = (f32[3,12,8,128]{3,2,1,0:T(8,128)S(1)}, f32[3,12,8,128]{3,2,1,0:T(8,128)S(1)}, u32[]{:S(2)}, u32[]{:S(2)}) collective-permute-start(f32[3,12,8,128]{3,2,1,0:T(8,128)S(1)} %get-tuple-element.44), channel_id=1, source_target_pairs={{1,0},{2,1},{3,2},{4,3},{5,4},{6,5},{7,6},{9,8},{10,9},{11,10},{12... | collective-permute-start | bytes 442376 | tf_op jit(solution)/shard_map/ppermute | solution.py:277
  47.0 5.0 %collective-permute-start.13 = (f32[9,3,8,128]{3,2,1,0:T(8,128)S(1)}, f32[9,3,8,128]{3,2,1,0:T(8,128)S(1)}, u32[]{:S(2)}, u32[]{:S(2)}) collective-permute-start(f32[9,3,8,128]{3,2,1,0:T(8,128)S(1)} %get-tuple-element.45), channel_id=1, source_target_pairs={{0,8},{8,16},{16,24},{24,0},{1,9},{9,17},{17,25},{25,1},{2,10},{10... | collective-permute-start | bytes 331784 | tf_op jit(solution)/shard_map/ppermute | solution.py:278
  47.3 4.7 %collective-permute-start.14 = (f32[9,3,8,128]{3,2,1,0:T(8,128)S(1)}, f32[9,3,8,128]{3,2,1,0:T(8,128)S(1)}, u32[]{:S(2)}, u32[]{:S(2)}) collective-permute-start(f32[9,3,8,128]{3,2,1,0:T(8,128)S(1)} %get-tuple-element.46), channel_id=1, source_target_pairs={{8,0},{16,8},{24,16},{0,24},{9,1},{17,9},{25,17},{1,25},{10,2},{18... | collective-permute-start | bytes 331784 | tf_op jit(solution)/shard_map/ppermute | solution.py:279

commit v3 on v2

v3 whole, which is shorter than its diff:
```python
import functools
import math

import jax
import jax.numpy as jnp
import numpy as np
from jax import lax
from jax.experimental import pallas as pl
from jax.experimental.pallas import tpu as pltpu
from jax.sharding import PartitionSpec as P

epsilon = 1e-06
courant = 0.5
spacing = 0.05
turn_limit = 1.0
thrust_limit = 0.5
speed_low = 0.5
speed_high = 1.5
rim = 3
gain = 1.0 / (12.0 * spacing)


def inverse(value):
    return pltpu.reciprocal(value, approx=True)


def weights_of(e1, e2, turn, eps):
    level = turn * turn * (4.0 / 3.0) + eps
    ia = inverse(level + e2 * (e2 + turn))
    ib = inverse(level + e2 * e1)
    ic = inverse(level + e1 * (e1 - turn))
    return ia * ia, ib * ib * 6.0, ic * ic


def sides(fl, f0, fr, a2, a1, b1, b0, c0, c1):
    a3 = a1 * 3.0
    c3 = c0 * 3.0
    minus = ((fl + fl) * a2 + f0 * c3) * inverse(a2 + b1 + c3)
    plus = ((fr + fr) * c1 + f0 * a3) * inverse(c1 + b0 + a3)
    return minus, plus


def row_terms(cells, step):
    count = len(cells) - 2 * rim
    eps = epsilon * step * step
    slope = [cells[i + 1] - cells[i] for i in range(len(cells) - 1)]
    bend = {m: slope[m + 3] - slope[m + 2] for m in range(-2, count + 2)}
    turn = {m: bend[m + 1] - bend[m] for m in range(-2, count + 1)}
    jerk = {m: turn[m] - turn[m - 1] for m in range(-1, count + 1)}
    a, b, c = {}, {}, {}
    for m in turn:
        a[m], b[m], c[m] = weights_of(bend[m], bend[m + 1], turn[m], eps)
    out = []
    for i in range(count):
        base = (cells[i + 4] - cells[i + 2]) * 6.0 - (turn[i - 1] + turn[i])
        minus, plus = sides(
            jerk[i - 1], jerk[i], jerk[i + 1], a[i - 2], a[i - 1], b[i - 1], b[i], c[i], c[i + 1]
        )
        out.append((base + (plus - minus), (plus + minus) - jerk[i]))
    return out


def tile_terms(cell, step):
    count = cell.shape[1]
    eps = epsilon * step * step
    flat = 1.0 / (eps * eps)
    place = lax.broadcasted_iota(jnp.int32, cell.shape, 1)

    def after(value, by=1):
        return pltpu.roll(value, count - by, 1)

    def before(value, by=1):
        return pltpu.roll(value, by, 1)

    up1 = jnp.where(place == count - 1, cell, after(cell))
    up2 = jnp.where(place >= count - 2, up1, after(cell, 2))
    dn1 = jnp.where(place == 0, cell, before(cell))
    dn2 = jnp.where(place <= 1, dn1, before(cell, 2))
    ahead = up1 - cell
    behind = cell - dn1
    bend_l = behind - (dn1 - dn2)
    bend = ahead - behind
    bend_r = (up2 - up1) - ahead
    turn_l = bend - bend_l
    turn_r = bend_r - bend
    jerk = turn_r - turn_l
    level_l = turn_l * turn_l * (4.0 / 3.0) + eps
    level_r = turn_r * turn_r * (4.0 / 3.0) + eps
    ia = inverse(level_l + bend * (bend + turn_l))
    ib = inverse(level_l + bend * bend_l)
    jb = inverse(level_r + bend * bend_r)
    jc = inverse(level_r + bend * (bend - turn_r))
    a1 = ia * ia
    c0 = jc * jc
    a2 = jnp.where(place == 0, flat, before(a1))
    c1 = jnp.where(place == count - 1, flat, after(c0))
    jerk_l = jnp.where(place == 0, bend, before(jerk))
    jerk_r = jnp.where(place == count - 1, bend, after(jerk))
    base = (ahead + behind) * 6.0 - (turn_l + turn_r)
    minus, plus = sides(
        jerk_l, jerk, jerk_r, a2, a1, ib * ib * 6.0, jb * jb * 6.0, c0, c1
    )
    return base + (plus - minus), (plus + minus) - jerk


def batches(total, most):
    return max(k for k in range(1, most + 1) if total % k == 0)


def splat(row, tile):
    return jnp.broadcast_to(row, tile)


def speeds_of(tile, speed_step):
    place = lax.broadcasted_iota(jnp.int32, tile, 0).astype(jnp.float32)
    return speed_low + place * speed_step


def odd_place(axis):
    return lax.rem(lax.axis_index(axis), 2) == 1


def speed_kernel(speed_step, s_ref, part_ref):
    planes, headings, speeds, width = s_ref.shape
    gain_v = thrust_limit / (12.0 * speed_step)
    cells = planes * headings
    group = 8
    s_rows = s_ref.reshape(cells * speeds, width)
    part_rows = part_ref.reshape(cells * speeds, width)
    groups = -(-cells // group)
    wide = batches(groups, 2)

    def step(n, carry):
        for k in range(wide):
            start = jnp.minimum((n * wide + k) * group, cells - group) * speeds
            lines = [
                s_rows[pl.ds(start + v, group, stride=speeds), :] for v in range(speeds)
            ]
            ends = [lines[0]] * rim + lines + [lines[-1]] * rim
            for v, (mean, gap) in enumerate(row_terms(ends, speed_step)):
                part_rows[pl.ds(start + v, group, stride=speeds), :] = gain_v * (
                    gap - jnp.abs(mean)
                )
        return carry

    lax.fori_loop(0, groups // wide, step, 0)


def cross_kernel(split, speed_step, s_ref, part_ref, wind_ref, waves_ref, *rest):
    planes, headings, speeds, width = s_ref.shape
    tile = (speeds, width)
    if split:
        out_ref, extra_ref = rest
    else:
        pk_ref, out_ref = rest
        peak = splat(pk_ref[1:2, :] * gain, tile)
    pace = speeds_of(tile, speed_step) * gain
    first = lax.axis_index("head") * headings
    wide = batches(headings, 2)

    def step(n, carry):
        for k in range(wide):
            j = n * wide + k
            table = splat(waves_ref[1, pl.ds(first + j, 1), :], tile) * pace
            for i in range(planes):
                mean, gap = tile_terms(s_ref[i, j], spacing)
                flow = table + splat(wind_ref[i, 1:2, :] * gain, tile)
                part = part_ref[i, j] + mean * flow
                if split:
                    out_ref[i, j] = part
                    extra_ref[i, j] = gap
                else:
                    out_ref[i, j] = part + gap * peak
        return carry

    lax.fori_loop(0, headings // wide, step, 0)


def heading_kernel(heading_step, s_ref, part_ref, near_ref, far_ref, out_ref):
    planes, headings = s_ref.shape[:2]
    gain_t = turn_limit / (12.0 * heading_step)
    odd = odd_place("head")
    wide = batches(planes, 3)

    def step(n, carry):
        for w in range(wide):
            i = n * wide + w
            ghosts = [(near_ref[i, k], far_ref[i, k]) for k in range(rim)]
            lows = [jnp.where(odd, near, far) for near, far in ghosts]
            highs = [jnp.where(odd, far, near) for near, far in ghosts]
            cells = lows + [s_ref[i, j] for j in range(headings)] + highs
            for j, (mean, gap) in enumerate(row_terms(cells, heading_step)):
                out_ref[i, j] = part_ref[i, j] + gain_t * (gap - jnp.abs(mean))
        return carry

    lax.fori_loop(0, planes // wide, step, 0)


def peaks_into(pk_ref, most, bounds, heading_step, speed_step):
    most = jnp.max(most, axis=1, keepdims=True)
    peaks = [
        jnp.maximum(most[q : q + 1] + bounds[q][1], most[q + 2 : q + 3] - bounds[q][0])
        for q in range(2)
    ]
    time_step = courant / (
        peaks[0] / spacing
        + peaks[1] / spacing
        + turn_limit / heading_step
        + thrust_limit / speed_step
    )
    width = pk_ref.shape[1]
    for row, value in enumerate(peaks + [time_step]):
        pk_ref[row : row + 1, :] = splat(value, (1, width))


def cut_edges(field_ref, x_near, x_far, t_near, t_far):
    planes, headings = field_ref.shape[:2]
    x_low = jnp.where(odd_place("gx"), 0, planes - rim)
    t_low = jnp.where(odd_place("head"), 0, headings - rim)
    for k in range(rim):
        x_near[k * headings : (k + 1) * headings] = field_ref[x_low + k]
        x_far[k * headings : (k + 1) * headings] = field_ref[planes - rim - x_low + k]
        for i in range(planes):
            t_near[i, k] = field_ref[i, t_low + k]
            t_far[i, k] = field_ref[i, headings - rim - t_low + k]


def section_kernel(section, bounds, heading_step, speed_step, *refs):
    refs = list(refs)
    base_ref = None if section == 1 else refs.pop(0)
    s_ref, part_ref = refs.pop(0), refs.pop(0)
    extra_ref = refs.pop(0) if section == 1 else None
    near_ref, far_ref = refs.pop(0), refs.pop(0)
    wind_ref, waves_ref, mask_ref, depth_ref = (refs.pop(0) for _ in range(4))
    if section == 1:
        most_refs = [refs.pop(0), refs.pop(0)]
    else:
        pk_ref = refs.pop(0)
    out_ref = refs.pop(0)
    if section < 3:
        edge_refs = [refs.pop(0) for _ in range(4)]
    if section == 1:
        pk_ref = refs.pop(0)
    flow_ref, target_ref = refs
    planes, headings = s_ref.shape[:2]
    tile = s_ref.shape[2:]
    if section == 1:
        most = jnp.maximum(most_refs[0][...], most_refs[1][...])
        peaks_into(pk_ref, most, bounds, heading_step, speed_step)
    for i in range(planes):
        depth = depth_ref[i : i + 1, :]
        target_ref[i] = splat(jnp.where(mask_ref[i : i + 1, :] == 1, -depth, depth), tile)
        flow_ref[i] = splat(wind_ref[i, 0:1, :] * gain, tile)
    odd = odd_place("gx")
    at_low = lax.axis_index("gx") == 0
    at_high = lax.axis_index("gx") == lax.axis_size("gx") - 1
    peak_x = splat(pk_ref[0:1, :] * gain, tile)
    peak_y = splat(pk_ref[1:2, :] * gain, tile)
    time_step = splat(pk_ref[2:3, :], tile)
    pace = speeds_of(tile, speed_step) * gain
    first = lax.axis_index("head") * headings
    wide = batches(headings, 3)

    def step(n, carry):
        for w in range(wide):
            j = n * wide + w
            cells = [s_ref[i, j] for i in range(planes)]
            ghosts = [(near_ref[k * headings + j], far_ref[k * headings + j]) for k in range(rim)]
            lows = [jnp.where(at_low, cells[0], jnp.where(odd, near, far)) for near, far in ghosts]
            highs = [jnp.where(at_high, cells[-1], jnp.where(odd, far, near)) for near, far in ghosts]
            table = splat(waves_ref[0, pl.ds(first + j, 1), :], tile) * pace
            for i, (mean, gap) in enumerate(row_terms(lows + cells + highs, spacing)):
                rate = part_ref[i, j] + (mean * (table + flow_ref[i]) + gap * peak_x)
                if section == 1:
                    rate = rate + extra_ref[i, j] * peak_y
                moved = cells[i] + time_step * rate
                if section == 2:
                    moved = 0.75 * base_ref[i, j] + 0.25 * moved
                if section == 3:
                    moved = (1.0 / 3.0) * base_ref[i, j] + (2.0 / 3.0) * moved
                out_ref[i, j] = jnp.minimum(moved, target_ref[i])
        return carry

    lax.fori_loop(0, headings // wide, step, 0)
    if section < 3:
        cut_edges(out_ref, *edge_refs)


def opening_kernel(level_ref, wind_ref, *refs):
    edge_refs, (wind_in, sides_in, rims_in, sems) = refs[:4], refs[4:]
    planes, headings = level_ref.shape[:2]
    pairs = [
        (wind_ref, wind_in),
        (level_ref.at[:rim], sides_in.at[0]),
        (level_ref.at[planes - rim :], sides_in.at[1]),
        (level_ref.at[:, :rim], rims_in.at[0]),
        (level_ref.at[:, headings - rim :], rims_in.at[1]),
    ]
    copies = [
        pltpu.make_async_copy(src, dst, sems.at[k]) for k, (src, dst) in enumerate(pairs)
    ]
    for copy in copies:
        copy.start()
    x_near, x_far, t_near, t_far = edge_refs
    copies[0].wait()
    rows = [wind_in[i] for i in range(planes)]
    spot = rim * headings
    x_near[spot] = jnp.zeros_like(x_near[spot])
    x_near[spot, 0:2, :] = functools.reduce(jnp.maximum, rows)
    x_near[spot, 2:4, :] = -functools.reduce(jnp.minimum, rows)
    for copy in copies[1:]:
        copy.wait()
    x_side = jnp.where(odd_place("gx"), 0, 1)
    t_side = jnp.where(odd_place("head"), 0, 1)
    for k in range(rim):
        x_near[k * headings : (k + 1) * headings] = sides_in[x_side, k]
        x_far[k * headings : (k + 1) * headings] = sides_in[1 - x_side, k]
    t_near[...] = rims_in[t_side]
    t_far[...] = rims_in[1 - t_side]


def trade(value, axis, reach, wrap=False):
    size = lax.axis_size(axis)
    pairs = [(i, i + 1) for i in range(reach, size - 1, 2)]
    if wrap and reach and size % 2 == 0:
        pairs.append((size - 1, 0))
    return lax.ppermute(value, axis, pairs + [(j, i) for i, j in pairs])


def local(level_set, wind_field, target_mask, target_depth):
    planes, headings, speed_count, cross_count = level_set.shape
    heading_total = headings * lax.axis_size("head")
    heading_step = 2.0 * math.pi / heading_total
    speed_step = (speed_high - speed_low) / (speed_count - 1)
    speed_row = np.float32(speed_low) + np.arange(speed_count, dtype=np.float32) * np.float32(
        speed_step
    )
    angles = np.arange(heading_total, dtype=np.float32) * np.float32(heading_step)
    waves = [np.cos(angles), np.sin(angles)]
    bounds = []
    for wave in waves:
        product = wave[:, None] * speed_row[None, :]
        bounds.append((float(product.min()), float(product.max())))
    waves = jnp.asarray(np.stack(waves)[..., None] * np.ones(cross_count, np.float32))

    vmem = pl.BlockSpec(memory_space=pltpu.VMEM)
    hbm = pl.BlockSpec(memory_space=pltpu.HBM)
    tile = (speed_count, cross_count)

    def shape(*dims):
        return jax.ShapeDtypeStruct(dims + tile, jnp.float32)

    field = shape(planes, headings)
    t_edge = shape(planes, rim)
    cells = math.prod(level_set.shape)

    def call(kernel, ins, outs, scratch=(), work=50):
        return pl.pallas_call(
            kernel,
            out_shape=outs,
            in_specs=[vmem] * len(ins),
            out_specs=[vmem] * len(outs),
            scratch_shapes=list(scratch),
            compiler_params=pltpu.CompilerParams(vmem_limit_bytes=16 * 1024 * 1024),
            cost_estimate=pl.CostEstimate(
                flops=work * cells, bytes_accessed=12 * cells, transcendentals=0
            ),
        )(*ins)

    wind = jnp.transpose(wind_field, (1, 0, 2))
    edges = pl.pallas_call(
        opening_kernel,
        out_shape=[shape(rim * headings + 1), shape(rim * headings), t_edge, t_edge],
        in_specs=[hbm] * 2,
        out_specs=[vmem] * 4,
        scratch_shapes=[
            pltpu.VMEM(wind.shape, jnp.float32),
            pltpu.VMEM((2, rim, headings) + tile, jnp.float32),
            pltpu.VMEM((2, planes, rim) + tile, jnp.float32),
            pltpu.SemaphoreType.DMA((5,)),
        ],
        cost_estimate=pl.CostEstimate(flops=0, bytes_accessed=8 * cells, transcendentals=0),
    )(level_set, wind)

    values, pk = level_set, None
    for section in (1, 2, 3):
        x_out, x_last, t_out, t_last = edges
        x_near = trade(x_out, "gx", 0)
        t_near = trade(t_out, "head", 0)
        t_far = trade(t_last, "head", 1, True)
        (part,) = call(functools.partial(speed_kernel, speed_step), [values], [field])
        x_last, x_near, part = lax.optimization_barrier((x_last, x_near, part))
        if section == 1:
            most = [x_out[-1], x_near[-1]]
            reach = 2
            while reach < lax.axis_size("gx"):
                both = jnp.maximum(*most)
                size = lax.axis_size("gx")
                if size & (size - 1):
                    pairs = [(i, (i + reach) % size) for i in range(size)]
                else:
                    pairs = [(i, i ^ reach) for i in range(size)]
                most = [both, lax.ppermute(both, "gx", pairs)]
                reach *= 2
        x_far = trade(x_last, "gx", 1)
        split = section == 1
        turning = functools.partial(heading_kernel, heading_step)
        (part,) = call(turning, [values, part, t_near, t_far], [field])
        cross = functools.partial(cross_kernel, split, speed_step)
        ins = [values, part, wind, waves] + ([] if split else [pk])
        part, *extra = call(cross, ins, [field] * (2 if split else 1))
        last = functools.partial(section_kernel, section, bounds, heading_step, speed_step)
        ins = ([] if split else [level_set]) + [values, part, *extra, x_near, x_far]
        ins += [wind, waves, target_mask, target_depth]
        ins += most if split else [pk]
        outs = [field]
        if section < 3:
            outs += [shape(rim * headings)] * 2 + [t_edge] * 2
        if split:
            outs += [shape()]
        rows = pltpu.VMEM((planes,) + tile, jnp.float32)
        results = call(last, ins, outs, [rows, rows])
        values, edges = results[0], results[1:5]
        if split:
            pk = results[5]
    return values


def solution(mesh):
    return jax.shard_map(
        local,
        mesh=mesh,
        in_specs=(P("gx", "head", None, None), P(None, "gx", None), P("gx", None), P("gx", None)),
        out_specs=P("gx", "head", None, None),
        check_vma=False,
    )
```

time: 56.9 us -> 59.9 us (1.053)
  waiting for transfers between devices: 3.44 us -> 19.3 us
  starting transfers between devices: 29.7 us -> 21.3 us
  Pallas kernels: 20.4 us -> 17.5 us
  local copies, waits for them, and re-layouts: 2.2 us -> 0.03 us
  other arithmetic: 0.09 us -> 0.7 us
    ppermute x15 -> x14, waiting for transfers between devices: 3.44 us -> 19.3 us  [the longest x12 15.7 us: trade(): return lax.ppermute(value, axis, pairs + [(j, i) for i, j in pairs])]
    ppermute x15 -> x14, starting transfers between devices: 29.7 us -> 21.3 us  [the longest x12 18.6 us: trade(): return lax.ppermute(value, axis, pairs + [(j, i) for i, j in pairs])]
    pallas_call x7 -> x13, Pallas kernels: 20.4 us -> 17.5 us  [the longest x12 15.5 us: call(): pl.pallas_call(kernel, out_shape=outs, in_specs=[vmem] * len(ins), out_sp...]
    unnamed x10 -> x12, local copies, waits for them, and re-layouts: 1.3 us -> 0.03 us
    dynamic_slice x1 -> x0, local copies, waits for them, and re-layouts: 0.9 us -> none  [local(): lax.dynamic_slice_in_dim(jnp.asarray(tables), first_heading, headings, 1)]
    max x3 -> x2, other arithmetic: 0.01 us -> 0.7 us  [local(): both = jnp.maximum(*most)]
  transfers between devices with their start and end apart: 15 -> 14, of which waited for: 2 -> 6; matrix products, arithmetic and copies ran while one was open for 2% -> 1% of each run, Pallas kernels for 17% -> 19%
where the time goes in v3:
time: 59.9 us; the launch traced here: 59 us
  starting transfers between devices  21.3 us (36%)
  waiting for transfers between devices  19.3 us (32%)
  Pallas kernels  17.5 us (29%)
  other arithmetic  0.7 us (1%)
    ppermute x12, starting transfers between devices, trade(): return lax.ppermute(value, axis, pairs + [(j, i) for i, j in pairs])  18.6 us
    ppermute x12, waiting for transfers between devices, trade(): return lax.ppermute(value, axis, pairs + [(j, i) for i, j in pairs])  15.7 us
    pallas_call x12, Pallas kernels, call(): pl.pallas_call(kernel, out_shape=outs, in_specs=[vmem] * len(ins), out_sp...  15.5 us
    ppermute x2, waiting for transfers between devices, local(): most = [both, lax.ppermute(both, 'gx', pairs)]  3.61 us
    ppermute x2, starting transfers between devices, local(): most = [both, lax.ppermute(both, 'gx', pairs)]  2.65 us
    pallas_call x1, Pallas kernels, local(): pl.pallas_call(opening_kernel, out_shape=[shape(rim * headings + 1), shap...  2.01 us
  transfers between devices with their start and end apart: 14, of which 6 were waited for; matrix products, arithmetic and copies ran while one was open for 1% of the time, Pallas kernels for 19%

profile of v3, /device:TPU:8, one launch (start us, length us, event | category | flops | bytes accessed | tf_op | source)
XLA Modules:
  0.0 59.0 jit_solution(6344319922164097416)
XLA Ops:
  0.0 0.0 copy-start
  0.0 2.0 %shard_map.55 = (f32[37,8,128]{2,1,0:T(8,128)}, f32[36,8,128]{2,1,0:T(8,128)}, f32[9,3,8,128]{3,2,1,0:T(8,128)}, f32[9,3,8,128]{3,2,1,0:T(8,128)}) custom-call(f32[9,12,8,128]{3,2,1,0:T(8,128)} %refs_0_.5, f32[9,2,128]{2,1,0:T(2,128)} %bitcast.3), custom_call_target="tpu_custom_call" | custom-call | bytes 884736 | tf_op jit(solution)/shard_map/pallas_call | solution.py:371
  2.0 1.6 %collective-permute-start = (f32[37,8,128]{2,1,0:T(8,128)}, f32[37,8,128]{2,1,0:T(8,128)S(1)}, u32[]{:S(2)}, u32[]{:S(2)}) collective-permute-start(f32[37,8,128]{2,1,0:T(8,128)} %get-tuple-element.32), channel_id=1, source_target_pairs={{0,1},{2,3},{4,5},{6,7},{1,0},{3,2},{5,4},{7,6},{8,9},{10,11},{12,... | collective-permute-start | bytes 454664 | tf_op jit(solution)/shard_map/ppermute | solution.py:327
  3.6 0.0 collective-permute-start.1
  3.6 0.0 copy-start.5
  3.6 1.6 %collective-permute-start.2 = (f32[9,3,8,128]{3,2,1,0:T(8,128)}, f32[9,3,8,128]{3,2,1,0:T(8,128)S(1)}, u32[]{:S(2)}, u32[]{:S(2)}) collective-permute-start(f32[9,3,8,128]{3,2,1,0:T(8,128)} %get-tuple-element.35), channel_id=1, source_target_pairs={{8,16},{24,0},{16,8},{0,24},{9,17},{25,1},{17,9},{1,25},{10,18},{2... | collective-permute-start | bytes 331784 | tf_op jit(solution)/shard_map/ppermute | solution.py:327
  5.2 0.0 copy-done
  5.2 1.0 %shard_map.56.part_ref = f32[9,12,8,128]{3,2,1,0:T(8,128)S(1)} custom-call(f32[9,12,8,128]{3,2,1,0:T(8,128)S(1)} %copy-done), custom_call_target="tpu_custom_call" | custom-call | flops 5529600 | bytes 1327104 | tf_op jit(solution)/shard_map/pallas_call | solution.py:358
  6.2 1.8 %collective-permute-done.refs_3_ = f32[37,8,128]{2,1,0:T(8,128)S(1)} collective-permute-done((f32[37,8,128]{2,1,0:T(8,128)}, f32[37,8,128]{2,1,0:T(8,128)S(1)}, u32[]{:S(2)}, u32[]{:S(2)}) %collective-permute-start) | collective-permute-done | bytes 151584 | tf_op jit(solution)/shard_map/ppermute | solution.py:327
  8.0 0.0 copy-done.5
  8.0 3.3 %collective-permute-start.3 = (f32[36,8,128]{2,1,0:T(8,128)S(1)}, f32[36,8,128]{2,1,0:T(8,128)S(1)}, u32[]{:S(2)}, u32[]{:S(2)}) collective-permute-start(f32[36,8,128]{2,1,0:T(8,128)S(1)} %copy-done.5), channel_id=1, source_target_pairs={{1,2},{3,4},{5,6},{2,1},{4,3},{6,5},{9,10},{11,12},{13,14},{10,9},... | collective-permute-start | bytes 442376 | tf_op jit(solution)/shard_map/ppermute | solution.py:327
  11.3 0.7 %maximum_bitcast_fusion = f32[8,128]{1,0:T(8,128)S(1)} fusion(f32[37,8,128]{2,1,0:T(8,128)S(1)} %collective-permute-done.refs_3_, f32[37,8,128]{2,1,0:T(8,128)} %get-tuple-element.32), kind=kLoop, calls=%fused_computation | loop fusion | flops 1024 | bytes 12288 | tf_op jit(solution)/shard_map/max | solution.py:397
  12.0 0.0 collective-permute-start.4
  12.0 3.6 %collective-permute-done.4 = f32[8,128]{1,0:T(8,128)S(1)} collective-permute-done((f32[8,128]{1,0:T(8,128)S(1)}, f32[8,128]{1,0:T(8,128)S(1)}, u32[]{:S(2)}, u32[]{:S(2)}) %collective-permute-start.4) | collective-permute-done | bytes 4128 | tf_op jit(solution)/shard_map/ppermute | solution.py:403
  15.6 0.0 copy-start.1
  15.6 0.0 copy-start.2
  15.6 2.6 %collective-permute-start.5 = (f32[8,128]{1,0:T(8,128)S(1)}, f32[8,128]{1,0:T(8,128)S(1)}, u32[]{:S(2)}, u32[]{:S(2)}) collective-permute-start(f32[8,128]{1,0:T(8,128)S(1)} %max.11.refs_9_), channel_id=1, source_target_pairs={{0,4},{1,5},{2,6},{3,7},{4,0},{5,1},{6,2},{7,3},{8,12},{9,13},{10,... | collective-permute-start | bytes 12296 | tf_op jit(solution)/shard_map/ppermute | solution.py:403
  18.2 0.0 collective-permute-done.1.near_ref
  18.2 0.0 collective-permute-done.2.far_ref
  18.2 0.8 %shard_map.57.part_ref = f32[9,12,8,128]{3,2,1,0:T(8,128)S(1)} custom-call(f32[9,12,8,128]{3,2,1,0:T(8,128)S(1)} %copy-done, f32[9,12,8,128]{3,2,1,0:T(8,128)S(1)} %shard_map.56.part_ref, f32[9,3,8,128]{3,2,1,0:T(8,128)S(1)} %collective-permute-done.1.near_ref, f32[9,3,8,128]{3,2,1,0:T(8,128)S(1)} %collective-permute-done.2.far_ref), custom_call_target="tpu_custom_call" | custom-call | flops 5529600 | bytes 1327104 | tf_op jit(solution)/shard_map/pallas_call | solution.py:358
  19.1 0.0 copy-done.1
  19.1 0.0 copy-done.2
  19.1 0.0 copy-start.3
  19.1 0.0 copy-start.4
  19.1 2.0 %shard_map.58 = (f32[9,12,8,128]{3,2,1,0:T(8,128)S(1)}, f32[9,12,8,128]{3,2,1,0:T(8,128)S(1)}) custom-call(f32[9,12,8,128]{3,2,1,0:T(8,128)S(1)} %copy-done, f32[9,12,8,128]{3,2,1,0:T(8,128)S(1)} %shard_map.57.part_ref, f32[9,2,128]{2,1,0:T(2,128)S(1)} %bitcast.4, f32[2,48,128]{2,1,0:T(8,128)S(1)} %copy-done.1), custom_call_target="tpu_custom_call" | custom-call | flops 5529600 | bytes 1327104 | tf_op jit(solution)/shard_map/pallas_call | solution.py:358
  21.1 0.0 collective-permute-done.5.refs_10_
  21.2 0.0 collective-permute-done.3.refs_4_
  21.2 0.0 copy-done.3
  21.2 0.0 copy-done.4
  21.2 1.2 %shard_map.59 = (f32[9,12,8,128]{3,2,1,0:T(8,128)S(1)}, f32[36,8,128]{2,1,0:T(8,128)S(1)}, f32[36,8,128]{2,1,0:T(8,128)S(1)}, f32[9,3,8,128]{3,2,1,0:T(8,128)S(1...) custom-call(f32[9,12,8,128]{3,2,1,0:T(8,128)S(1)} %copy-done, f32[9,12,8,128]{3,2,1,0:T(8,128)S(1)} %get-tuple-element.36.refs_1_, ...), custom_call_target="tpu_custom_call" | custom-call | flops 5529600 | bytes 1327104 | tf_op jit(solution)/shard_map/pallas_call | solution.py:358
  22.4 1.0 %collective-permute-start.6 = (f32[36,8,128]{2,1,0:T(8,128)S(1)}, f32[36,8,128]{2,1,0:T(8,128)S(1)}, u32[]{:S(2)}, u32[]{:S(2)}) collective-permute-start(f32[36,8,128]{2,1,0:T(8,128)S(1)} %get-tuple-element.42), channel_id=1, source_target_pairs={{0,1},{2,3},{4,5},{6,7},{1,0},{3,2},{5,4},{7,6},{8,9},{10,11},{12,... | collective-permute-start | bytes 442376 | tf_op jit(solution)/shard_map/ppermute | solution.py:327
  23.4 1.0 %shard_map.60.part_ref = f32[9,12,8,128]{3,2,1,0:T(8,128)S(1)} custom-call(f32[9,12,8,128]{3,2,1,0:T(8,128)S(1)} %get-tuple-element.40.s_ref.refs_1_), custom_call_target="tpu_custom_call" | custom-call | flops 5529600 | bytes 1327104 | tf_op jit(solution)/shard_map/pallas_call | solution.py:358
  24.4 3.2 %collective-permute-done.6.refs_3_ = f32[36,8,128]{2,1,0:T(8,128)S(1)} collective-permute-done((f32[36,8,128]{2,1,0:T(8,128)S(1)}, f32[36,8,128]{2,1,0:T(8,128)S(1)}, u32[]{:S(2)}, u32[]{:S(2)}) %collective-permute-start.6) | collective-permute-done | bytes 147488 | tf_op jit(solution)/shard_map/ppermute | solution.py:327
  27.6 3.4 %collective-permute-start.9 = (f32[36,8,128]{2,1,0:T(8,128)S(1)}, f32[36,8,128]{2,1,0:T(8,128)S(1)}, u32[]{:S(2)}, u32[]{:S(2)}) collective-permute-start(f32[36,8,128]{2,1,0:T(8,128)S(1)} %get-tuple-element.48), channel_id=1, source_target_pairs={{1,2},{3,4},{5,6},{2,1},{4,3},{6,5},{9,10},{11,12},{13,14},{10,9},... | collective-permute-start | bytes 442376 | tf_op jit(solution)/shard_map/ppermute | solution.py:327
  31.0 0.1 collective-permute-start.7
  31.1 1.6 %collective-permute-start.8 = (f32[9,3,8,128]{3,2,1,0:T(8,128)S(1)}, f32[9,3,8,128]{3,2,1,0:T(8,128)S(1)}, u32[]{:S(2)}, u32[]{:S(2)}) collective-permute-start(f32[9,3,8,128]{3,2,1,0:T(8,128)S(1)} %get-tuple-element.45), channel_id=1, source_target_pairs={{8,16},{24,0},{16,8},{0,24},{9,17},{25,1},{17,9},{1,25},{10,18},{2... | collective-permute-start | bytes 331784 | tf_op jit(solution)/shard_map/ppermute | solution.py:327
  32.7 0.0 collective-permute-done.7.near_ref
  32.7 3.2 %collective-permute-done.8.far_ref = f32[9,3,8,128]{3,2,1,0:T(8,128)S(1)} collective-permute-done((f32[9,3,8,128]{3,2,1,0:T(8,128)S(1)}, f32[9,3,8,128]{3,2,1,0:T(8,128)S(1)}, u32[]{:S(2)}, u32[]{:S(2)}) %collective-permute-start.8) | collective-permute-done | bytes 110624 | tf_op jit(solution)/shard_map/ppermute | solution.py:327
  36.0 0.8 %shard_map.61.part_ref = f32[9,12,8,128]{3,2,1,0:T(8,128)S(1)} custom-call(f32[9,12,8,128]{3,2,1,0:T(8,128)S(1)} %get-tuple-element.40.s_ref.refs_1_, f32[9,12,8,128]{3,2,1,0:T(8,128)S(1)} %shard_map.60.part_ref, f32[9,3,8,128]{3,2,1,0:T(8,128)S(1)} %collective-permute-done.7.near_ref, f32[9,3,8,128]{3,2,1,0:T(8,128)S(1)} %collective-permute-done.8.far_ref), custom_call_target="tpu_custom_call" | custom-call | flops 5529600 | bytes 1327104 | tf_op jit(solution)/shard_map/pallas_call | solution.py:358
  36.8 2.0 %shard_map.62.refs_2_ = f32[9,12,8,128]{3,2,1,0:T(8,128)S(1)} custom-call(f32[9,12,8,128]{3,2,1,0:T(8,128)S(1)} %get-tuple-element.40.s_ref.refs_1_, f32[9,12,8,128]{3,2,1,0:T(8,128)S(1)} %shard_map.61.part_ref, f32[9,2,128]{2,1,0:T(2,128)S(1)} %bitcast.6, f32[2,48,128]{2,1,0:T(8,128)S(1)} %copy-done.1, f32[8,128]{1,0:T(8,128)S(1)} %get-tuple-element.46.rest_0_.refs_9_), custom_call_target="tpu_custom_call" | custom-call | flops 5529600 | bytes 1327104 | tf_op jit(solution)/shard_map/pallas_call | solution.py:358
  38.8 0.0 collective-permute-done.9.refs_4_
  38.8 1.1 %shard_map.63 = (f32[9,12,8,128]{3,2,1,0:T(8,128)S(1)}, f32[36,8,128]{2,1,0:T(8,128)S(1)}, f32[36,8,128]{2,1,0:T(8,128)S(1)}, f32[9,3,8,128]{3,2,1,0:T(8,128)S(1)}, f32[9,3,8,128]{3,2,1,0:T(8,128)S(1)}) custom-call(f32[9,12,8,128]{3,2,1,0:T(8,128)S(1)} %copy-done, f32[9,12,8,128]{3,2,1,0:T(8,128)S(1)} %get-tuple-element.40.s_ref.refs_1_, ...), custom_call_target="tpu_custom_call" | custom-call | flops 5529600 | bytes 1327104 | tf_op jit(solution)/shard_map/pallas_call | solution.py:358
  39.9 1.1 %collective-permute-start.10 = (f32[36,8,128]{2,1,0:T(8,128)S(1)}, f32[36,8,128]{2,1,0:T(8,128)S(1)}, u32[]{:S(2)}, u32[]{:S(2)}) collective-permute-start(f32[36,8,128]{2,1,0:T(8,128)S(1)} %get-tuple-element.51), channel_id=1, source_target_pairs={{0,1},{2,3},{4,5},{6,7},{1,0},{3,2},{5,4},{7,6},{8,9},{10,11},{12,... | collective-permute-start | bytes 442376 | tf_op jit(solution)/shard_map/ppermute | solution.py:327
  41.0 1.0 %shard_map.64.part_ref = f32[9,12,8,128]{3,2,1,0:T(8,128)S(1)} custom-call(f32[9,12,8,128]{3,2,1,0:T(8,128)S(1)} %get-tuple-element.49.s_ref.refs_1_), custom_call_target="tpu_custom_call" | custom-call | flops 5529600 | bytes 1327104 | tf_op jit(solution)/shard_map/pallas_call | solution.py:358
  41.9 4.2 %collective-permute-done.10.refs_3_ = f32[36,8,128]{2,1,0:T(8,128)S(1)} collective-permute-done((f32[36,8,128]{2,1,0:T(8,128)S(1)}, f32[36,8,128]{2,1,0:T(8,128)S(1)}, u32[]{:S(2)}, u32[]{:S(2)}) %collective-permute-start.10) | collective-permute-done | bytes 147488 | tf_op jit(solution)/shard_map/ppermute | solution.py:327
  46.1 3.3 %collective-permute-start.13 = (f32[36,8,128]{2,1,0:T(8,128)S(1)}, f32[36,8,128]{2,1,0:T(8,128)S(1)}, u32[]{:S(2)}, u32[]{:S(2)}) collective-permute-start(f32[36,8,128]{2,1,0:T(8,128)S(1)} %get-tuple-element.56), channel_id=1, source_target_pairs={{1,2},{3,4},{5,6},{2,1},{4,3},{6,5},{9,10},{11,12},{13,14},{10,9},... | collective-permute-start | bytes 442376 | tf_op jit(solution)/shard_map/ppermute | solution.py:327
  49.4 0.1 collective-permute-start.11
  49.5 1.6 %collective-permute-start.12 = (f32[9,3,8,128]{3,2,1,0:T(8,128)S(1)}, f32[9,3,8,128]{3,2,1,0:T(8,128)S(1)}, u32[]{:S(2)}, u32[]{:S(2)}) collective-permute-start(f32[9,3,8,128]{3,2,1,0:T(8,128)S(1)} %get-tuple-element.54), channel_id=1, source_target_pairs={{8,16},{24,0},{16,8},{0,24},{9,17},{25,1},{17,9},{1,25},{10,18},{2... | collective-permute-start | bytes 331784 | tf_op jit(solution)/shard_map/ppermute | solution.py:327
  51.1 0.0 collective-permute-done.11.near_ref
  51.1 3.2 %collective-permute-done.12.far_ref = f32[9,3,8,128]{3,2,1,0:T(8,128)S(1)} collective-permute-done((f32[9,3,8,128]{3,2,1,0:T(8,128)S(1)}, f32[9,3,8,128]{3,2,1,0:T(8,128)S(1)}, u32[]{:S(2)}, u32[]{:S(2)}) %collective-permute-start.12) | collective-permute-done | bytes 110624 | tf_op jit(solution)/shard_map/ppermute | solution.py:327
  54.4 0.8 %shard_map.65.part_ref = f32[9,12,8,128]{3,2,1,0:T(8,128)S(1)} custom-call(f32[9,12,8,128]{3,2,1,0:T(8,128)S(1)} %get-tuple-element.49.s_ref.refs_1_, f32[9,12,8,128]{3,2,1,0:T(8,128)S(1)} %shard_map.64.part_ref, f32[9,3,8,128]{3,2,1,0:T(8,128)S(1)} %collective-permute-done.11.near_ref, f32[9,3,8,128]{3,2,1,0:T(8,128)S(1)} %collective-permute-done.12.far_ref), custom_call_target="tpu_custom_call" | custom-call | flops 5529600 | bytes 1327104 | tf_op jit(solution)/shard_map/pallas_call | solution.py:358
  55.2 2.0 %shard_map.66.refs_2_ = f32[9,12,8,128]{3,2,1,0:T(8,128)S(1)} custom-call(f32[9,12,8,128]{3,2,1,0:T(8,128)S(1)} %get-tuple-element.49.s_ref.refs_1_, f32[9,12,8,128]{3,2,1,0:T(8,128)S(1)} %shard_map.65.part_ref, f32[9,2,128]{2,1,0:T(2,128)S(1)} %bitcast.8, f32[2,48,128]{2,1,0:T(8,128)S(1)} %copy-done.1, f32[8,128]{1,0:T(8,128)S(1)} %get-tuple-element.46.rest_0_.refs_9_), custom_call_target="tpu_custom_call" | custom-call | flops 5529600 | bytes 1327104 | tf_op jit(solution)/shard_map/pallas_call | solution.py:358
  57.2 0.0 collective-permute-done.13.refs_4_
  57.2 1.8 %shard_map.67 = f32[9,12,8,128]{3,2,1,0:T(8,128)} custom-call(f32[9,12,8,128]{3,2,1,0:T(8,128)S(1)} %copy-done, f32[9,12,8,128]{3,2,1,0:T(8,128)S(1)} %get-tuple-element.49.s_ref.refs_1_, f32[9,12,8,128]{3,2,1,0:T(8,128)S(1)} %shard_map.66.refs_2_, f32[36,8,128]{2,1,0:T(8,128)S(1)} %collective-permute-done.10.refs_3_, ...), custom_call_target="tpu_custom_call" | custom-call | flops 5529600 | bytes 1327104 | tf_op jit(solution)/shard_map/pallas_call | solution.py:358
  (1 shorter events, 0.0 us)
Async XLA Ops:
  0.0 5.2 %copy-start = (f32[9,12,8,128]{3,2,1,0:T(8,128)S(1)}, f32[9,12,8,128]{3,2,1,0:T(8,128)}, u32[]{:S(2)}) copy-start(f32[9,12,8,128]{3,2,1,0:T(8,128)} %refs_0_.5) | copy-start | bytes 1327108
  2.0 6.0 %collective-permute-start = (f32[37,8,128]{2,1,0:T(8,128)}, f32[37,8,128]{2,1,0:T(8,128)S(1)}, u32[]{:S(2)}, u32[]{:S(2)}) collective-permute-start(f32[37,8,128]{2,1,0:T(8,128)} %get-tuple-element.32), channel_id=1, source_target_pairs={{0,1},{2,3},{4,5},{6,7},{1,0},{3,2},{5,4},{7,6},{8,9},{10,11},{12,... | collective-permute-start | bytes 454664 | tf_op jit(solution)/shard_map/ppermute | solution.py:327
  3.6 14.6 %collective-permute-start.1 = (f32[9,3,8,128]{3,2,1,0:T(8,128)}, f32[9,3,8,128]{3,2,1,0:T(8,128)S(1)}, u32[]{:S(2)}, u32[]{:S(2)}) collective-permute-start(f32[9,3,8,128]{3,2,1,0:T(8,128)} %get-tuple-element.34), channel_id=1, source_target_pairs={{0,8},{16,24},{8,0},{24,16},{1,9},{17,25},{9,1},{25,17},{2,10},{18... | collective-permute-start | bytes 331784 | tf_op jit(solution)/shard_map/ppermute | solution.py:327
  3.6 4.4 %copy-start.5 = (f32[36,8,128]{2,1,0:T(8,128)S(1)}, f32[36,8,128]{2,1,0:T(8,128)}, u32[]{:S(2)}) copy-start(f32[36,8,128]{2,1,0:T(8,128)} %get-tuple-element.39) | copy-start | bytes 442372
  3.6 14.6 %collective-permute-start.2 = (f32[9,3,8,128]{3,2,1,0:T(8,128)}, f32[9,3,8,128]{3,2,1,0:T(8,128)S(1)}, u32[]{:S(2)}, u32[]{:S(2)}) collective-permute-start(f32[9,3,8,128]{3,2,1,0:T(8,128)} %get-tuple-element.35), channel_id=1, source_target_pairs={{8,16},{24,0},{16,8},{0,24},{9,17},{25,1},{17,9},{1,25},{10,18},{2... | collective-permute-start | bytes 331784 | tf_op jit(solution)/shard_map/ppermute | solution.py:327
  8.0 13.2 %collective-permute-start.3 = (f32[36,8,128]{2,1,0:T(8,128)S(1)}, f32[36,8,128]{2,1,0:T(8,128)S(1)}, u32[]{:S(2)}, u32[]{:S(2)}) collective-permute-start(f32[36,8,128]{2,1,0:T(8,128)S(1)} %copy-done.5), channel_id=1, source_target_pairs={{1,2},{3,4},{5,6},{2,1},{4,3},{6,5},{9,10},{11,12},{13,14},{10,9},... | collective-permute-start | bytes 442376 | tf_op jit(solution)/shard_map/ppermute | solution.py:327
  12.0 3.6 %collective-permute-start.4 = (f32[8,128]{1,0:T(8,128)S(1)}, f32[8,128]{1,0:T(8,128)S(1)}, u32[]{:S(2)}, u32[]{:S(2)}) collective-permute-start(f32[8,128]{1,0:T(8,128)S(1)} %maximum_bitcast_fusion), channel_id=1, source_target_pairs={{0,2},{1,3},{2,0},{3,1},{4,6},{5,7},{6,4},{7,5},{8,10},{9,11},{10,... | collective-permute-start | bytes 12296 | tf_op jit(solution)/shard_map/ppermute | solution.py:403
  15.6 3.5 %copy-start.1 = (f32[2,48,128]{2,1,0:T(8,128)S(1)}, f32[2,48,128]{2,1,0:T(8,128)}, u32[]{:S(2)}) copy-start(f32[2,48,128]{2,1,0:T(8,128)} %constant.2.clone.waves_ref.refs_6_) | copy-start | bytes 147460
  15.6 3.5 %copy-start.2 = (f32[2,9,128]{2,0,1:T(2,128)S(1)}, f32[2,9,128]{2,0,1:T(2,128)}, u32[]{:S(2)}) copy-start(f32[2,9,128]{2,0,1:T(2,128)} %param.6) | copy-start | bytes 27652
  15.6 5.6 %collective-permute-start.5 = (f32[8,128]{1,0:T(8,128)S(1)}, f32[8,128]{1,0:T(8,128)S(1)}, u32[]{:S(2)}, u32[]{:S(2)}) collective-permute-start(f32[8,128]{1,0:T(8,128)S(1)} %max.11.refs_9_), channel_id=1, source_target_pairs={{0,4},{1,5},{2,6},{3,7},{4,0},{5,1},{6,2},{7,3},{8,12},{9,13},{10,... | collective-permute-start | bytes 12296 | tf_op jit(solution)/shard_map/ppermute | solution.py:403
  19.1 2.1 %copy-start.3 = (s32[9,128]{1,0:T(8,128)S(1)}, s32[9,128]{1,0:T(8,128)}, u32[]{:S(2)}) copy-start(s32[9,128]{1,0:T(8,128)} %refs_7_.5) | copy-start | bytes 13828
  19.1 2.1 %copy-start.4 = (f32[9,128]{1,0:T(8,128)S(1)}, f32[9,128]{1,0:T(8,128)}, u32[]{:S(2)}) copy-start(f32[9,128]{1,0:T(8,128)} %refs_8_.5) | copy-start | bytes 13828
  22.4 5.2 %collective-permute-start.6 = (f32[36,8,128]{2,1,0:T(8,128)S(1)}, f32[36,8,128]{2,1,0:T(8,128)S(1)}, u32[]{:S(2)}, u32[]{:S(2)}) collective-permute-start(f32[36,8,128]{2,1,0:T(8,128)S(1)} %get-tuple-element.42), channel_id=1, source_target_pairs={{0,1},{2,3},{4,5},{6,7},{1,0},{3,2},{5,4},{7,6},{8,9},{10,11},{12,... | collective-permute-start | bytes 442376 | tf_op jit(solution)/shard_map/ppermute | solution.py:327
  27.6 11.2 %collective-permute-start.9 = (f32[36,8,128]{2,1,0:T(8,128)S(1)}, f32[36,8,128]{2,1,0:T(8,128)S(1)}, u32[]{:S(2)}, u32[]{:S(2)}) collective-permute-start(f32[36,8,128]{2,1,0:T(8,128)S(1)} %get-tuple-element.48), channel_id=1, source_target_pairs={{1,2},{3,4},{5,6},{2,1},{4,3},{6,5},{9,10},{11,12},{13,14},{10,9},... | collective-permute-start | bytes 442376 | tf_op jit(solution)/shard_map/ppermute | solution.py:327
  31.0 1.7 %collective-permute-start.7 = (f32[9,3,8,128]{3,2,1,0:T(8,128)S(1)}, f32[9,3,8,128]{3,2,1,0:T(8,128)S(1)}, u32[]{:S(2)}, u32[]{:S(2)}) collective-permute-start(f32[9,3,8,128]{3,2,1,0:T(8,128)S(1)} %get-tuple-element.44), channel_id=1, source_target_pairs={{0,8},{16,24},{8,0},{24,16},{1,9},{17,25},{9,1},{25,17},{2,10},{18... | collective-permute-start | bytes 331784 | tf_op jit(solution)/shard_map/ppermute | solution.py:327
  31.1 4.9 %collective-permute-start.8 = (f32[9,3,8,128]{3,2,1,0:T(8,128)S(1)}, f32[9,3,8,128]{3,2,1,0:T(8,128)S(1)}, u32[]{:S(2)}, u32[]{:S(2)}) collective-permute-start(f32[9,3,8,128]{3,2,1,0:T(8,128)S(1)} %get-tuple-element.45), channel_id=1, source_target_pairs={{8,16},{24,0},{16,8},{0,24},{9,17},{25,1},{17,9},{1,25},{10,18},{2... | collective-permute-start | bytes 331784 | tf_op jit(solution)/shard_map/ppermute | solution.py:327
  39.9 6.2 %collective-permute-start.10 = (f32[36,8,128]{2,1,0:T(8,128)S(1)}, f32[36,8,128]{2,1,0:T(8,128)S(1)}, u32[]{:S(2)}, u32[]{:S(2)}) collective-permute-start(f32[36,8,128]{2,1,0:T(8,128)S(1)} %get-tuple-element.51), channel_id=1, source_target_pairs={{0,1},{2,3},{4,5},{6,7},{1,0},{3,2},{5,4},{7,6},{8,9},{10,11},{12,... | collective-permute-start | bytes 442376 | tf_op jit(solution)/shard_map/ppermute | solution.py:327
  46.1 11.1 %collective-permute-start.13 = (f32[36,8,128]{2,1,0:T(8,128)S(1)}, f32[36,8,128]{2,1,0:T(8,128)S(1)}, u32[]{:S(2)}, u32[]{:S(2)}) collective-permute-start(f32[36,8,128]{2,1,0:T(8,128)S(1)} %get-tuple-element.56), channel_id=1, source_target_pairs={{1,2},{3,4},{5,6},{2,1},{4,3},{6,5},{9,10},{11,12},{13,14},{10,9},... | collective-permute-start | bytes 442376 | tf_op jit(solution)/shard_map/ppermute | solution.py:327
  49.4 1.7 %collective-permute-start.11 = (f32[9,3,8,128]{3,2,1,0:T(8,128)S(1)}, f32[9,3,8,128]{3,2,1,0:T(8,128)S(1)}, u32[]{:S(2)}, u32[]{:S(2)}) collective-permute-start(f32[9,3,8,128]{3,2,1,0:T(8,128)S(1)} %get-tuple-element.53), channel_id=1, source_target_pairs={{0,8},{16,24},{8,0},{24,16},{1,9},{17,25},{9,1},{25,17},{2,10},{18... | collective-permute-start | bytes 331784 | tf_op jit(solution)/shard_map/ppermute | solution.py:327
  49.5 4.9 %collective-permute-start.12 = (f32[9,3,8,128]{3,2,1,0:T(8,128)S(1)}, f32[9,3,8,128]{3,2,1,0:T(8,128)S(1)}, u32[]{:S(2)}, u32[]{:S(2)}) collective-permute-start(f32[9,3,8,128]{3,2,1,0:T(8,128)S(1)} %get-tuple-element.54), channel_id=1, source_target_pairs={{8,16},{24,0},{16,8},{0,24},{9,17},{25,1},{17,9},{1,25},{10,18},{2... | collective-permute-start | bytes 331784 | tf_op jit(solution)/shard_map/ppermute | solution.py:327

commit v4 on v3

--- a/solution.py
+++ b/solution.py
@@ -120,7 +120,29 @@
     return lax.rem(lax.axis_index(axis), 2) == 1
 
 
-def speed_kernel(speed_step, s_ref, part_ref):
+def extremes_of(wind_ref):
+    rows = [wind_ref[i] for i in range(wind_ref.shape[0])]
+    return functools.reduce(jnp.maximum, rows), -functools.reduce(jnp.minimum, rows)
+
+
+def opening_kernel(level_ref, wind_ref, *refs):
+    most_ref = refs[-1]
+    top, low = extremes_of(wind_ref)
+    most_ref[...] = jnp.zeros_like(most_ref)
+    most_ref[0:2, :] = top
+    most_ref[2:4, :] = low
+    cut_edges(level_ref, *refs[:-1])
+
+
+def speed_kernel(speed_step, s_ref, *refs):
+    if len(refs) == 1:
+        part_ref = refs[0]
+    else:
+        wind_ref, other_ref, part_ref, most_ref = refs
+        top, low = extremes_of(wind_ref)
+        most_ref[...] = other_ref[...]
+        most_ref[0:2, :] = jnp.maximum(top, other_ref[0:2, :])
+        most_ref[2:4, :] = jnp.maximum(low, other_ref[2:4, :])
     planes, headings, speeds, width = s_ref.shape
     gain_v = thrust_limit / (12.0 * speed_step)
     cells = planes * headings
@@ -185,7 +207,7 @@
     def step(n, carry):
         for w in range(wide):
             i = n * wide + w
-            ghosts = [(near_ref[i, k], far_ref[i, k]) for k in range(rim)]
+            ghosts = [(near_ref[i * rim + k], far_ref[i * rim + k]) for k in range(rim)]
             lows = [jnp.where(odd, near, far) for near, far in ghosts]
             highs = [jnp.where(odd, far, near) for near, far in ghosts]
             cells = lows + [s_ref[i, j] for j in range(headings)] + highs
@@ -221,8 +243,8 @@
         x_near[k * headings : (k + 1) * headings] = field_ref[x_low + k]
         x_far[k * headings : (k + 1) * headings] = field_ref[planes - rim - x_low + k]
         for i in range(planes):
-            t_near[i, k] = field_ref[i, t_low + k]
-            t_far[i, k] = field_ref[i, headings - rim - t_low + k]
+            t_near[i * rim + k] = field_ref[i, t_low + k]
+            t_far[i * rim + k] = field_ref[i, headings - rim - t_low + k]
 
 
 def section_kernel(section, bounds, heading_step, speed_step, *refs):
@@ -286,39 +308,6 @@
         cut_edges(out_ref, *edge_refs)
 
 
-def opening_kernel(level_ref, wind_ref, *refs):
-    edge_refs, (wind_in, sides_in, rims_in, sems) = refs[:4], refs[4:]
-    planes, headings = level_ref.shape[:2]
-    pairs = [
-        (wind_ref, wind_in),
-        (level_ref.at[:rim], sides_in.at[0]),
-        (level_ref.at[planes - rim :], sides_in.at[1]),
-        (level_ref.at[:, :rim], rims_in.at[0]),
-        (level_ref.at[:, headings - rim :], rims_in.at[1]),
-    ]
-    copies = [
-        pltpu.make_async_copy(src, dst, sems.at[k]) for k, (src, dst) in enumerate(pairs)
-    ]
-    for copy in copies:
-        copy.start()
-    x_near, x_far, t_near, t_far = edge_refs
-    copies[0].wait()
-    rows = [wind_in[i] for i in range(planes)]
-    spot = rim * headings
-    x_near[spot] = jnp.zeros_like(x_near[spot])
-    x_near[spot, 0:2, :] = functools.reduce(jnp.maximum, rows)
-    x_near[spot, 2:4, :] = -functools.reduce(jnp.minimum, rows)
-    for copy in copies[1:]:
-        copy.wait()
-    x_side = jnp.where(odd_place("gx"), 0, 1)
-    t_side = jnp.where(odd_place("head"), 0, 1)
-    for k in range(rim):
-        x_near[k * headings : (k + 1) * headings] = sides_in[x_side, k]
-        x_far[k * headings : (k + 1) * headings] = sides_in[1 - x_side, k]
-    t_near[...] = rims_in[t_side]
-    t_far[...] = rims_in[1 - t_side]
-
-
 def trade(value, axis, reach, wrap=False):
     size = lax.axis_size(axis)
     pairs = [(i, i + 1) for i in range(reach, size - 1, 2)]
@@ -344,17 +333,22 @@
     waves = jnp.asarray(np.stack(waves)[..., None] * np.ones(cross_count, np.float32))
 
     vmem = pl.BlockSpec(memory_space=pltpu.VMEM)
-    hbm = pl.BlockSpec(memory_space=pltpu.HBM)
     tile = (speed_count, cross_count)
 
     def shape(*dims):
         return jax.ShapeDtypeStruct(dims + tile, jnp.float32)
 
     field = shape(planes, headings)
-    t_edge = shape(planes, rim)
+    short = rim * headings
+    middle = max(short + 1, rim * planes)
+
+    def edge_shapes(far_first):
+        x_shapes = [shape(middle + 1), shape(short)]
+        return x_shapes[:: -1 if far_first else 1] + [shape(middle)] * 2
+
     cells = math.prod(level_set.shape)
 
-    def call(kernel, ins, outs, scratch=(), work=50):
+    def call(kernel, ins, outs, scratch=(), work=0):
         return pl.pallas_call(
             kernel,
             out_shape=outs,
@@ -363,65 +357,69 @@
             scratch_shapes=list(scratch),
             compiler_params=pltpu.CompilerParams(vmem_limit_bytes=16 * 1024 * 1024),
             cost_estimate=pl.CostEstimate(
-                flops=work * cells, bytes_accessed=12 * cells, transcendentals=0
+                flops=work * cells, bytes_accessed=work * cells, transcendentals=0
             ),
         )(*ins)
 
     wind = jnp.transpose(wind_field, (1, 0, 2))
-    edges = pl.pallas_call(
-        opening_kernel,
-        out_shape=[shape(rim * headings + 1), shape(rim * headings), t_edge, t_edge],
-        in_specs=[hbm] * 2,
-        out_specs=[vmem] * 4,
-        scratch_shapes=[
-            pltpu.VMEM(wind.shape, jnp.float32),
-            pltpu.VMEM((2, rim, headings) + tile, jnp.float32),
-            pltpu.VMEM((2, planes, rim) + tile, jnp.float32),
-            pltpu.SemaphoreType.DMA((5,)),
-        ],
-        cost_estimate=pl.CostEstimate(flops=0, bytes_accessed=8 * cells, transcendentals=0),
-    )(level_set, wind)
-
     values, pk = level_set, None
+    size = lax.axis_size("gx")
+
+    def spread(most, reach):
+        if size & (size - 1):
+            pairs = [(i, (i + reach) % size) for i in range(size)]
+        else:
+            pairs = [(i, i ^ reach) for i in range(size)]
+        return lax.ppermute(most, "gx", pairs)
+
     for section in (1, 2, 3):
+        opening = section == 1
+        speed = functools.partial(speed_kernel, speed_step)
+        if opening:
+            *edges, most = call(opening_kernel, [values, wind], edge_shapes(True) + [shape()])
+            other = spread(most, 1)
         x_out, x_last, t_out, t_last = edges
-        x_near = trade(x_out, "gx", 0)
+        if opening:
+            x_far = trade(x_last, "gx", 1)
+        else:
+            x_near = trade(x_out, "gx", 0)
         t_near = trade(t_out, "head", 0)
         t_far = trade(t_last, "head", 1, True)
-        (part,) = call(functools.partial(speed_kernel, speed_step), [values], [field])
-        x_last, x_near, part = lax.optimization_barrier((x_last, x_near, part))
-        if section == 1:
-            most = [x_out[-1], x_near[-1]]
-            reach = 2
-            while reach < lax.axis_size("gx"):
-                both = jnp.maximum(*most)
-                size = lax.axis_size("gx")
-                if size & (size - 1):
-                    pairs = [(i, (i + reach) % size) for i in range(size)]
-                else:
-                    pairs = [(i, i ^ reach) for i in range(size)]
-                most = [both, lax.ppermute(both, "gx", pairs)]
-                reach *= 2
-        x_far = trade(x_last, "gx", 1)
-        split = section == 1
+        if opening:
+            part, most = call(speed, [values, wind, other], [field, shape()])
+            other = spread(most, 2)
+            x_out, most = lax.optimization_barrier((x_out, most))
+            x_near = trade(x_out, "gx", 0)
+        else:
+            (part,) = call(speed, [values], [field])
+            x_far = trade(x_last, "gx", 1)
         turning = functools.partial(heading_kernel, heading_step)
         (part,) = call(turning, [values, part, t_near, t_far], [field])
-        cross = functools.partial(cross_kernel, split, speed_step)
-        ins = [values, part, wind, waves] + ([] if split else [pk])
-        part, *extra = call(cross, ins, [field] * (2 if split else 1))
+        if opening:
+            reach = 4
+            while reach < size:
+                most = jnp.maximum(most, other)
+                other = spread(most, reach)
+                reach *= 2
+            part, x_far = lax.optimization_barrier((part, x_far))
+        else:
+            part, x_near = lax.optimization_barrier((part, x_near))
+        cross = functools.partial(cross_kernel, opening, speed_step)
+        ins = [values, part, wind, waves] + ([] if opening else [pk])
+        part, *extra = call(cross, ins, [field] * (2 if opening else 1), work=1000)
         last = functools.partial(section_kernel, section, bounds, heading_step, speed_step)
-        ins = ([] if split else [level_set]) + [values, part, *extra, x_near, x_far]
+        ins = ([] if opening else [level_set]) + [values, part, *extra, x_near, x_far]
         ins += [wind, waves, target_mask, target_depth]
-        ins += most if split else [pk]
+        ins += [most, other] if opening else [pk]
         outs = [field]
         if section < 3:
-            outs += [shape(rim * headings)] * 2 + [t_edge] * 2
-        if split:
+            outs += edge_shapes(False)
+        if opening:
             outs += [shape()]
         rows = pltpu.VMEM((planes,) + tile, jnp.float32)
         results = call(last, ins, outs, [rows, rows])
         values, edges = results[0], results[1:5]
-        if split:
+        if opening:
             pk = results[5]
     return values
 

time: 59.9 us -> 48.2 us (0.80)
  the two profiles are of different devices: /device:TPU:8 before, /device:TPU:1 now
where the time goes in v4:
time: 48.2 us; the launch traced here: 48 us
  starting transfers between devices  21.3 us (44%)
  Pallas kernels  15.6 us (32%)
  waiting for transfers between devices  9.04 us (19%)
  local copies, waits for them, and re-layouts  1.74 us (4%)
    pallas_call x13, Pallas kernels, call(): pl.pallas_call(kernel, out_shape=outs, in_specs=[vmem] * len(ins), out_sp...  15.6 us
    ppermute x12, starting transfers between devices, trade(): return lax.ppermute(value, axis, pairs + [(j, i) for i, j in pairs])  14 us
    ppermute x3, starting transfers between devices, spread(): return lax.ppermute(most, 'gx', pairs)  7.31 us
    ppermute x12, waiting for transfers between devices, trade(): return lax.ppermute(value, axis, pairs + [(j, i) for i, j in pairs])  6.59 us
    ppermute x3, waiting for transfers between devices, spread(): return lax.ppermute(most, 'gx', pairs)  2.45 us
    unnamed x14, local copies, waits for them, and re-layouts  1.74 us
  transfers between devices with their start and end apart: 15, of which 4 were waited for; matrix products, arithmetic and copies ran while one was open for 0% of the time, Pallas kernels for 24%

profile of v4, /device:TPU:1, one launch (start us, length us, event | category | flops | bytes accessed | tf_op | source)
XLA Modules:
  0.0 48.0 jit_solution(15176808937347274876)
XLA Ops:
  0.0 0.0 copy-start
  0.0 1.0 %copy-done = f32[9,12,8,128]{3,2,1,0:T(8,128)S(1)} copy-done((f32[9,12,8,128]{3,2,1,0:T(8,128)S(1)}, f32[9,12,8,128]{3,2,1,0:T(8,128)}, u32[]{:S(2)}) %copy-start) | copy-done | bytes 442392
  1.0 0.0 copy-start.3
  1.0 0.7 %copy-done.3 = f32[2,9,128]{2,0,1:T(2,128)S(1)} copy-done((f32[2,9,128]{2,0,1:T(2,128)S(1)}, f32[2,9,128]{2,0,1:T(2,128)}, u32[]{:S(2)}) %copy-start.3) | copy-done | bytes 9240
  1.8 0.7 %collective-permute-start.3 = (f32[38,8,128]{2,1,0:T(8,128)S(1)}, f32[38,8,128]{2,1,0:T(8,128)S(1)}, u32[]{:S(2)}, u32[]{:S(2)}) collective-permute-start(f32[38,8,128]{2,1,0:T(8,128)S(1)} %get-tuple-element.37), channel_id=1, source_target_pairs={{1,2},{3,4},{5,6},{2,1},{4,3},{6,5},{9,10},{11,12},{13,14},{10,9},... | collective-permute-start | bytes 466952 | tf_op jit(solution)/shard_map/ppermute | solution.py:316
  2.4 0.1 collective-permute-start.1
  2.6 2.6 %collective-permute-start.2 = (f32[37,8,128]{2,1,0:T(8,128)S(1)}, f32[37,8,128]{2,1,0:T(8,128)S(1)}, u32[]{:S(2)}, u32[]{:S(2)}) collective-permute-start(f32[37,8,128]{2,1,0:T(8,128)S(1)} %get-tuple-element.36), channel_id=1, source_target_pairs={{8,16},{24,0},{16,8},{0,24},{9,17},{25,1},{17,9},{1,25},{10,18},{2... | collective-permute-start | bytes 454664 | tf_op jit(solution)/shard_map/ppermute | solution.py:316
  5.2 4.0 %collective-permute-start = (f32[8,128]{1,0:T(8,128)S(1)}, f32[8,128]{1,0:T(8,128)S(1)}, u32[]{:S(2)}, u32[]{:S(2)}) collective-permute-start(f32[8,128]{1,0:T(8,128)S(1)} %get-tuple-element.33), channel_id=1, source_target_pairs={{0,1},{1,0},{2,3},{3,2},{4,5},{5,4},{6,7},{7,6},{8,9},{9,8},{10,11... | collective-permute-start | bytes 12296 | tf_op jit(solution)/shard_map/ppermute | solution.py:373
  9.2 1.0 %collective-permute-done.refs_1_ = f32[8,128]{1,0:T(8,128)S(1)} collective-permute-done((f32[8,128]{1,0:T(8,128)S(1)}, f32[8,128]{1,0:T(8,128)S(1)}, u32[]{:S(2)}, u32[]{:S(2)}) %collective-permute-start) | collective-permute-done | bytes 4128 | tf_op jit(solution)/shard_map/ppermute | solution.py:373
  10.2 1.0 %shard_map.56 = (f32[9,12,8,128]{3,2,1,0:T(8,128)S(1)}, f32[8,128]{1,0:T(8,128)S(1)}) custom-call(f32[9,12,8,128]{3,2,1,0:T(8,128)S(1)} %copy-done, f32[9,2,128]{2,1,0:T(2,128)S(1)} %bitcast.2, f32[8,128]{1,0:T(8,128)S(1)} %collective-permute-done.refs_1_), custom_call_target="tpu_custom_call" | custom-call | tf_op jit(solution)/shard_map/pallas_call | solution.py:352
  11.2 2.2 %collective-permute-start.4 = (f32[36,8,128]{2,1,0:T(8,128)S(1)}, f32[36,8,128]{2,1,0:T(8,128)S(1)}, u32[]{:S(2)}, u32[]{:S(2)}) collective-permute-start(f32[36,8,128]{2,1,0:T(8,128)S(1)} %get-tuple-element.43), channel_id=1, source_target_pairs={{0,1},{2,3},{4,5},{6,7},{1,0},{3,2},{5,4},{7,6},{8,9},{10,11},{12,... | collective-permute-start | bytes 442376 | tf_op jit(solution)/shard_map/ppermute | solution.py:316
  13.4 1.3 %collective-permute-start.5 = (f32[8,128]{1,0:T(8,128)S(1)}, f32[8,128]{1,0:T(8,128)S(1)}, u32[]{:S(2)}, u32[]{:S(2)}) collective-permute-start(f32[8,128]{1,0:T(8,128)S(1)} %get-tuple-element.45), channel_id=1, source_target_pairs={{0,2},{1,3},{2,0},{3,1},{4,6},{5,7},{6,4},{7,5},{8,10},{9,11},{10,... | collective-permute-start | bytes 12296 | tf_op jit(solution)/shard_map/ppermute | solution.py:373
  14.7 1.5 %collective-permute-done.5 = f32[8,128]{1,0:T(8,128)S(1)} collective-permute-done((f32[8,128]{1,0:T(8,128)S(1)}, f32[8,128]{1,0:T(8,128)S(1)}, u32[]{:S(2)}, u32[]{:S(2)}) %collective-permute-start.5) | collective-permute-done | bytes 4128 | tf_op jit(solution)/shard_map/ppermute | solution.py:373
  16.2 2.0 %collective-permute-start.6 = (f32[8,128]{1,0:T(8,128)S(1)}, f32[8,128]{1,0:T(8,128)S(1)}, u32[]{:S(2)}, u32[]{:S(2)}) collective-permute-start(f32[8,128]{1,0:T(8,128)S(1)} %max.3.refs_9_), channel_id=1, source_target_pairs={{0,4},{1,5},{2,6},{3,7},{4,0},{5,1},{6,2},{7,3},{8,12},{9,13},{10,... | collective-permute-start | bytes 12296 | tf_op jit(solution)/shard_map/ppermute | solution.py:373
  18.2 0.0 collective-permute-done.1.near_ref
  18.2 0.0 collective-permute-done.2.far_ref
  18.2 0.0 copy-start.2
  18.2 0.0 copy-start.4
  18.2 0.8 %shard_map.57.part_ref = f32[9,12,8,128]{3,2,1,0:T(8,128)S(1)} custom-call(f32[9,12,8,128]{3,2,1,0:T(8,128)S(1)} %copy-done, f32[9,12,8,128]{3,2,1,0:T(8,128)S(1)} %get-tuple-element.34.part_ref, f32[37,8,128]{2,1,0:T(8,128)S(1)} %collective-permute-done.1.near_ref, f32[37,8,128]{2,1,0:T(8,128)S(1)} %collective-permute-done.2.far_ref), custom_call_target="tpu_custom_call" | custom-call | tf_op jit(solution)/shard_map/pallas_call | solution.py:352
  19.0 0.0 collective-permute-done.3.refs_4_
  19.0 0.0 copy-done.2
  19.1 0.0 copy-done.4
  19.1 0.0 copy-start.5
  19.1 0.0 copy-start.6
  19.1 2.0 %shard_map.58 = (f32[9,12,8,128]{3,2,1,0:T(8,128)S(1)}, f32[9,12,8,128]{3,2,1,0:T(8,128)S(1)}) custom-call(f32[9,12,8,128]{3,2,1,0:T(8,128)S(1)} %copy-done, f32[9,12,8,128]{3,2,1,0:T(8,128)S(1)} %shard_map.57.part_ref, f32[9,2,128]{2,1,0:T(2,128)S(1)} %bitcast.3, f32[2,48,128]{2,1,0:T(8,128)S(1)} %copy-done.2), custom_call_target="tpu_custom_call" | custom-call | flops 110592000 | bytes 110592000 | tf_op jit(solution)/shard_map/pallas_call | solution.py:352
  21.1 0.0 collective-permute-done.6.refs_10_
  21.1 0.0 collective-permute-done.4.refs_3_
  21.1 0.0 copy-done.5
  21.1 0.0 copy-done.6
  21.2 1.2 %shard_map.59 = (f32[9,12,8,128]{3,2,1,0:T(8,128)S(1)}, f32[38,8,128]{2,1,0:T(8,128)S(1)}, f32[36,8,128]{2,1,0:T(8,128)S(1)}, f32[37,8,128]{2,1,0:T(8,128)S(1)},...) custom-call(f32[9,12,8,128]{3,2,1,0:T(8,128)S(1)} %copy-done, f32[9,12,8,128]{3,2,1,0:T(8,128)S(1)} %get-tuple-element.39.refs_1_, ...), custom_call_target="tpu_custom_call" | custom-call | tf_op jit(solution)/shard_map/pallas_call | solution.py:352
  22.4 0.2 collective-permute-start.9
  22.6 2.9 %collective-permute-start.7 = (f32[37,8,128]{2,1,0:T(8,128)S(1)}, f32[37,8,128]{2,1,0:T(8,128)S(1)}, u32[]{:S(2)}, u32[]{:S(2)}) collective-permute-start(f32[37,8,128]{2,1,0:T(8,128)S(1)} %get-tuple-element.47), channel_id=1, source_target_pairs={{0,8},{16,24},{8,0},{24,16},{1,9},{17,25},{9,1},{25,17},{2,10},{18... | collective-permute-start | bytes 454664 | tf_op jit(solution)/shard_map/ppermute | solution.py:316
  25.5 0.5 collective-permute-start.8
  25.9 0.7 %collective-permute-start.10 = (f32[36,8,128]{2,1,0:T(8,128)S(1)}, f32[36,8,128]{2,1,0:T(8,128)S(1)}, u32[]{:S(2)}, u32[]{:S(2)}) collective-permute-start(f32[36,8,128]{2,1,0:T(8,128)S(1)} %get-tuple-element.53), channel_id=1, source_target_pairs={{1,2},{3,4},{5,6},{2,1},{4,3},{6,5},{9,10},{11,12},{13,14},{10,9},... | collective-permute-start | bytes 442376 | tf_op jit(solution)/shard_map/ppermute | solution.py:316
  26.6 1.0 %shard_map.60.part_ref = f32[9,12,8,128]{3,2,1,0:T(8,128)S(1)} custom-call(f32[9,12,8,128]{3,2,1,0:T(8,128)S(1)} %get-tuple-element.46.s_ref.refs_1_), custom_call_target="tpu_custom_call" | custom-call | tf_op jit(solution)/shard_map/pallas_call | solution.py:352
  27.6 0.0 collective-permute-done.7.near_ref
  27.6 3.4 %collective-permute-done.8.far_ref = f32[37,8,128]{2,1,0:T(8,128)S(1)} collective-permute-done((f32[37,8,128]{2,1,0:T(8,128)S(1)}, f32[37,8,128]{2,1,0:T(8,128)S(1)}, u32[]{:S(2)}, u32[]{:S(2)}) %collective-permute-start.8) | collective-permute-done | bytes 151584 | tf_op jit(solution)/shard_map/ppermute | solution.py:316
  31.0 0.8 %shard_map.61.part_ref = f32[9,12,8,128]{3,2,1,0:T(8,128)S(1)} custom-call(f32[9,12,8,128]{3,2,1,0:T(8,128)S(1)} %get-tuple-element.46.s_ref.refs_1_, f32[9,12,8,128]{3,2,1,0:T(8,128)S(1)} %shard_map.60.part_ref, f32[37,8,128]{2,1,0:T(8,128)S(1)} %collective-permute-done.7.near_ref, f32[37,8,128]{2,1,0:T(8,128)S(1)} %collective-permute-done.8.far_ref), custom_call_target="tpu_custom_call" | custom-call | tf_op jit(solution)/shard_map/pallas_call | solution.py:352
  31.8 0.0 collective-permute-done.9.refs_3_
  31.9 0.0 copy-start.1
  31.9 2.0 %shard_map.62.refs_2_ = f32[9,12,8,128]{3,2,1,0:T(8,128)S(1)} custom-call(f32[9,12,8,128]{3,2,1,0:T(8,128)S(1)} %get-tuple-element.46.s_ref.refs_1_, f32[9,12,8,128]{3,2,1,0:T(8,128)S(1)} %shard_map.61.part_ref, f32[9,2,128]{2,1,0:T(2,128)S(1)} %bitcast.5, f32[2,48,128]{2,1,0:T(8,128)S(1)} %copy-done.2, f32[8,128]{1,0:T(8,128)S(1)} %get-tuple-element.51.rest_0_.refs_9_), custom_call_target="tpu_custom_call" | custom-call | flops 110592000 | bytes 110592000 | tf_op jit(solution)/shard_map/pallas_call | solution.py:352
  33.9 0.0 collective-permute-done.10.refs_4_
  33.9 0.0 copy-done.1
  33.9 1.1 %shard_map.63 = (f32[9,12,8,128]{3,2,1,0:T(8,128)S(1)}, f32[38,8,128]{2,1,0:T(8,128)S(1)}, f32[36,8,128]{2,1,0:T(8,128)S(1)}, f32[37,8,128]{2,1,0:T(8,128)S(1)}, f32[37,8,128]{2,1,0:T(8,128)S(1)}) custom-call(f32[9,12,8,128]{3,2,1,0:T(8,128)S(1)} %copy-done.1, f32[9,12,8,128]{3,2,1,0:T(8,128)S(1)} %get-tuple-element.46.s_ref.refs_1_, ...), custom_call_target="tpu_custom_call" | custom-call | tf_op jit(solution)/shard_map/pallas_call | solution.py:352
  35.0 1.4 %collective-permute-start.13 = (f32[38,8,128]{2,1,0:T(8,128)S(1)}, f32[38,8,128]{2,1,0:T(8,128)S(1)}, u32[]{:S(2)}, u32[]{:S(2)}) collective-permute-start(f32[38,8,128]{2,1,0:T(8,128)S(1)} %get-tuple-element.57), channel_id=1, source_target_pairs={{0,1},{2,3},{4,5},{6,7},{1,0},{3,2},{5,4},{7,6},{8,9},{10,11},{12,... | collective-permute-start | bytes 466952 | tf_op jit(solution)/shard_map/ppermute | solution.py:316
  36.4 1.4 %collective-permute-start.11 = (f32[37,8,128]{2,1,0:T(8,128)S(1)}, f32[37,8,128]{2,1,0:T(8,128)S(1)}, u32[]{:S(2)}, u32[]{:S(2)}) collective-permute-start(f32[37,8,128]{2,1,0:T(8,128)S(1)} %get-tuple-element.55), channel_id=1, source_target_pairs={{0,8},{16,24},{8,0},{24,16},{1,9},{17,25},{9,1},{25,17},{2,10},{18... | collective-permute-start | bytes 454664 | tf_op jit(solution)/shard_map/ppermute | solution.py:316
  37.7 0.8 %collective-permute-start.12 = (f32[37,8,128]{2,1,0:T(8,128)S(1)}, f32[37,8,128]{2,1,0:T(8,128)S(1)}, u32[]{:S(2)}, u32[]{:S(2)}) collective-permute-start(f32[37,8,128]{2,1,0:T(8,128)S(1)} %get-tuple-element.56), channel_id=1, source_target_pairs={{8,16},{24,0},{16,8},{0,24},{9,17},{25,1},{17,9},{1,25},{10,18},{2... | collective-permute-start | bytes 454664 | tf_op jit(solution)/shard_map/ppermute | solution.py:316
  38.5 0.7 %collective-permute-start.14 = (f32[36,8,128]{2,1,0:T(8,128)S(1)}, f32[36,8,128]{2,1,0:T(8,128)S(1)}, u32[]{:S(2)}, u32[]{:S(2)}) collective-permute-start(f32[36,8,128]{2,1,0:T(8,128)S(1)} %get-tuple-element.60), channel_id=1, source_target_pairs={{1,2},{3,4},{5,6},{2,1},{4,3},{6,5},{9,10},{11,12},{13,14},{10,9},... | collective-permute-start | bytes 442376 | tf_op jit(solution)/shard_map/ppermute | solution.py:316
  39.2 1.0 %shard_map.64.part_ref = f32[9,12,8,128]{3,2,1,0:T(8,128)S(1)} custom-call(f32[9,12,8,128]{3,2,1,0:T(8,128)S(1)} %get-tuple-element.54.s_ref.refs_1_), custom_call_target="tpu_custom_call" | custom-call | tf_op jit(solution)/shard_map/pallas_call | solution.py:352
  40.1 0.0 collective-permute-done.11.near_ref
  40.2 3.1 %collective-permute-done.12.far_ref = f32[37,8,128]{2,1,0:T(8,128)S(1)} collective-permute-done((f32[37,8,128]{2,1,0:T(8,128)S(1)}, f32[37,8,128]{2,1,0:T(8,128)S(1)}, u32[]{:S(2)}, u32[]{:S(2)}) %collective-permute-start.12) | collective-permute-done | bytes 151584 | tf_op jit(solution)/shard_map/ppermute | solution.py:316
  43.3 0.8 %shard_map.65.part_ref = f32[9,12,8,128]{3,2,1,0:T(8,128)S(1)} custom-call(f32[9,12,8,128]{3,2,1,0:T(8,128)S(1)} %get-tuple-element.54.s_ref.refs_1_, f32[9,12,8,128]{3,2,1,0:T(8,128)S(1)} %shard_map.64.part_ref, f32[37,8,128]{2,1,0:T(8,128)S(1)} %collective-permute-done.11.near_ref, f32[37,8,128]{2,1,0:T(8,128)S(1)} %collective-permute-done.12.far_ref), custom_call_target="tpu_custom_call" | custom-call | tf_op jit(solution)/shard_map/pallas_call | solution.py:352
  44.1 0.0 collective-permute-done.13.refs_3_
  44.1 2.0 %shard_map.66.refs_2_ = f32[9,12,8,128]{3,2,1,0:T(8,128)S(1)} custom-call(f32[9,12,8,128]{3,2,1,0:T(8,128)S(1)} %get-tuple-element.54.s_ref.refs_1_, f32[9,12,8,128]{3,2,1,0:T(8,128)S(1)} %shard_map.65.part_ref, f32[9,2,128]{2,1,0:T(2,128)S(1)} %bitcast.7, f32[2,48,128]{2,1,0:T(8,128)S(1)} %copy-done.2, f32[8,128]{1,0:T(8,128)S(1)} %get-tuple-element.51.rest_0_.refs_9_), custom_call_target="tpu_custom_call" | custom-call | flops 110592000 | bytes 110592000 | tf_op jit(solution)/shard_map/pallas_call | solution.py:352
  46.2 0.0 collective-permute-done.14.refs_4_
  46.2 1.8 %shard_map.67 = f32[9,12,8,128]{3,2,1,0:T(8,128)} custom-call(f32[9,12,8,128]{3,2,1,0:T(8,128)S(1)} %copy-done.1, f32[9,12,8,128]{3,2,1,0:T(8,128)S(1)} %get-tuple-element.54.s_ref.refs_1_, f32[9,12,8,128]{3,2,1,0:T(8,128)S(1)} %shard_map.66.refs_2_, f32[38,8,128]{2,1,0:T(8,128)S(1)} %collective-permute-done.13.refs_3_, ...), custom_call_target="tpu_custom_call" | custom-call | tf_op jit(solution)/shard_map/pallas_call | solution.py:352
  (2 shorter events, 0.1 us)
Async XLA Ops:
  0.0 1.0 %copy-start = (f32[9,12,8,128]{3,2,1,0:T(8,128)S(1)}, f32[9,12,8,128]{3,2,1,0:T(8,128)}, u32[]{:S(2)}) copy-start(f32[9,12,8,128]{3,2,1,0:T(8,128)} %refs_0_.5) | copy-start | bytes 1327108
  1.0 0.7 %copy-start.3 = (f32[2,9,128]{2,0,1:T(2,128)S(1)}, f32[2,9,128]{2,0,1:T(2,128)}, u32[]{:S(2)}) copy-start(f32[2,9,128]{2,0,1:T(2,128)} %param.6) | copy-start | bytes 27652
  1.8 17.3 %collective-permute-start.3 = (f32[38,8,128]{2,1,0:T(8,128)S(1)}, f32[38,8,128]{2,1,0:T(8,128)S(1)}, u32[]{:S(2)}, u32[]{:S(2)}) collective-permute-start(f32[38,8,128]{2,1,0:T(8,128)S(1)} %get-tuple-element.37), channel_id=1, source_target_pairs={{1,2},{3,4},{5,6},{2,1},{4,3},{6,5},{9,10},{11,12},{13,14},{10,9},... | collective-permute-start | bytes 466952 | tf_op jit(solution)/shard_map/ppermute | solution.py:316
  2.4 15.7 %collective-permute-start.1 = (f32[37,8,128]{2,1,0:T(8,128)S(1)}, f32[37,8,128]{2,1,0:T(8,128)S(1)}, u32[]{:S(2)}, u32[]{:S(2)}) collective-permute-start(f32[37,8,128]{2,1,0:T(8,128)S(1)} %get-tuple-element.35), channel_id=1, source_target_pairs={{0,8},{16,24},{8,0},{24,16},{1,9},{17,25},{9,1},{25,17},{2,10},{18... | collective-permute-start | bytes 454664 | tf_op jit(solution)/shard_map/ppermute | solution.py:316
  2.6 15.6 %collective-permute-start.2 = (f32[37,8,128]{2,1,0:T(8,128)S(1)}, f32[37,8,128]{2,1,0:T(8,128)S(1)}, u32[]{:S(2)}, u32[]{:S(2)}) collective-permute-start(f32[37,8,128]{2,1,0:T(8,128)S(1)} %get-tuple-element.36), channel_id=1, source_target_pairs={{8,16},{24,0},{16,8},{0,24},{9,17},{25,1},{17,9},{1,25},{10,18},{2... | collective-permute-start | bytes 454664 | tf_op jit(solution)/shard_map/ppermute | solution.py:316
  5.2 5.0 %collective-permute-start = (f32[8,128]{1,0:T(8,128)S(1)}, f32[8,128]{1,0:T(8,128)S(1)}, u32[]{:S(2)}, u32[]{:S(2)}) collective-permute-start(f32[8,128]{1,0:T(8,128)S(1)} %get-tuple-element.33), channel_id=1, source_target_pairs={{0,1},{1,0},{2,3},{3,2},{4,5},{5,4},{6,7},{7,6},{8,9},{9,8},{10,11... | collective-permute-start | bytes 12296 | tf_op jit(solution)/shard_map/ppermute | solution.py:373
  11.2 10.0 %collective-permute-start.4 = (f32[36,8,128]{2,1,0:T(8,128)S(1)}, f32[36,8,128]{2,1,0:T(8,128)S(1)}, u32[]{:S(2)}, u32[]{:S(2)}) collective-permute-start(f32[36,8,128]{2,1,0:T(8,128)S(1)} %get-tuple-element.43), channel_id=1, source_target_pairs={{0,1},{2,3},{4,5},{6,7},{1,0},{3,2},{5,4},{7,6},{8,9},{10,11},{12,... | collective-permute-start | bytes 442376 | tf_op jit(solution)/shard_map/ppermute | solution.py:316
  13.4 2.8 %collective-permute-start.5 = (f32[8,128]{1,0:T(8,128)S(1)}, f32[8,128]{1,0:T(8,128)S(1)}, u32[]{:S(2)}, u32[]{:S(2)}) collective-permute-start(f32[8,128]{1,0:T(8,128)S(1)} %get-tuple-element.45), channel_id=1, source_target_pairs={{0,2},{1,3},{2,0},{3,1},{4,6},{5,7},{6,4},{7,5},{8,10},{9,11},{10,... | collective-permute-start | bytes 12296 | tf_op jit(solution)/shard_map/ppermute | solution.py:373
  16.2 5.0 %collective-permute-start.6 = (f32[8,128]{1,0:T(8,128)S(1)}, f32[8,128]{1,0:T(8,128)S(1)}, u32[]{:S(2)}, u32[]{:S(2)}) collective-permute-start(f32[8,128]{1,0:T(8,128)S(1)} %max.3.refs_9_), channel_id=1, source_target_pairs={{0,4},{1,5},{2,6},{3,7},{4,0},{5,1},{6,2},{7,3},{8,12},{9,13},{10,... | collective-permute-start | bytes 12296 | tf_op jit(solution)/shard_map/ppermute | solution.py:373
  18.2 0.9 %copy-start.2 = (f32[2,48,128]{2,1,0:T(8,128)S(1)}, f32[2,48,128]{2,1,0:T(8,128)}, u32[]{:S(2)}) copy-start(f32[2,48,128]{2,1,0:T(8,128)} %constant.2.clone.waves_ref.refs_6_) | copy-start | bytes 147460
  18.2 0.9 %copy-start.4 = (f32[2,9,128]{2,0,1:T(2,128)S(1)}, f32[2,9,128]{2,0,1:T(2,128)}, u32[]{:S(2)}) copy-start(f32[2,9,128]{2,0,1:T(2,128)} %param.6) | copy-start | bytes 27652
  19.1 2.1 %copy-start.5 = (s32[9,128]{1,0:T(8,128)S(1)}, s32[9,128]{1,0:T(8,128)}, u32[]{:S(2)}) copy-start(s32[9,128]{1,0:T(8,128)} %refs_7_.5) | copy-start | bytes 13828
  19.1 2.1 %copy-start.6 = (f32[9,128]{1,0:T(8,128)S(1)}, f32[9,128]{1,0:T(8,128)}, u32[]{:S(2)}) copy-start(f32[9,128]{1,0:T(8,128)} %refs_8_.5) | copy-start | bytes 13828
  22.4 9.5 %collective-permute-start.9 = (f32[38,8,128]{2,1,0:T(8,128)S(1)}, f32[38,8,128]{2,1,0:T(8,128)S(1)}, u32[]{:S(2)}, u32[]{:S(2)}) collective-permute-start(f32[38,8,128]{2,1,0:T(8,128)S(1)} %get-tuple-element.49), channel_id=1, source_target_pairs={{0,1},{2,3},{4,5},{6,7},{1,0},{3,2},{5,4},{7,6},{8,9},{10,11},{12,... | collective-permute-start | bytes 466952 | tf_op jit(solution)/shard_map/ppermute | solution.py:316
  22.6 5.0 %collective-permute-start.7 = (f32[37,8,128]{2,1,0:T(8,128)S(1)}, f32[37,8,128]{2,1,0:T(8,128)S(1)}, u32[]{:S(2)}, u32[]{:S(2)}) collective-permute-start(f32[37,8,128]{2,1,0:T(8,128)S(1)} %get-tuple-element.47), channel_id=1, source_target_pairs={{0,8},{16,24},{8,0},{24,16},{1,9},{17,25},{9,1},{25,17},{2,10},{18... | collective-permute-start | bytes 454664 | tf_op jit(solution)/shard_map/ppermute | solution.py:316
  25.5 5.5 %collective-permute-start.8 = (f32[37,8,128]{2,1,0:T(8,128)S(1)}, f32[37,8,128]{2,1,0:T(8,128)S(1)}, u32[]{:S(2)}, u32[]{:S(2)}) collective-permute-start(f32[37,8,128]{2,1,0:T(8,128)S(1)} %get-tuple-element.48), channel_id=1, source_target_pairs={{8,16},{24,0},{16,8},{0,24},{9,17},{25,1},{17,9},{1,25},{10,18},{2... | collective-permute-start | bytes 454664 | tf_op jit(solution)/shard_map/ppermute | solution.py:316
  25.9 8.0 %collective-permute-start.10 = (f32[36,8,128]{2,1,0:T(8,128)S(1)}, f32[36,8,128]{2,1,0:T(8,128)S(1)}, u32[]{:S(2)}, u32[]{:S(2)}) collective-permute-start(f32[36,8,128]{2,1,0:T(8,128)S(1)} %get-tuple-element.53), channel_id=1, source_target_pairs={{1,2},{3,4},{5,6},{2,1},{4,3},{6,5},{9,10},{11,12},{13,14},{10,9},... | collective-permute-start | bytes 442376 | tf_op jit(solution)/shard_map/ppermute | solution.py:316
  31.9 2.1 %copy-start.1 = (f32[9,12,8,128]{3,2,1,0:T(8,128)S(1)}, f32[9,12,8,128]{3,2,1,0:T(8,128)}, u32[]{:S(2)}) copy-start(f32[9,12,8,128]{3,2,1,0:T(8,128)} %refs_0_.5) | copy-start | bytes 1327108
  35.0 9.1 %collective-permute-start.13 = (f32[38,8,128]{2,1,0:T(8,128)S(1)}, f32[38,8,128]{2,1,0:T(8,128)S(1)}, u32[]{:S(2)}, u32[]{:S(2)}) collective-permute-start(f32[38,8,128]{2,1,0:T(8,128)S(1)} %get-tuple-element.57), channel_id=1, source_target_pairs={{0,1},{2,3},{4,5},{6,7},{1,0},{3,2},{5,4},{7,6},{8,9},{10,11},{12,... | collective-permute-start | bytes 466952 | tf_op jit(solution)/shard_map/ppermute | solution.py:316
  36.4 3.8 %collective-permute-start.11 = (f32[37,8,128]{2,1,0:T(8,128)S(1)}, f32[37,8,128]{2,1,0:T(8,128)S(1)}, u32[]{:S(2)}, u32[]{:S(2)}) collective-permute-start(f32[37,8,128]{2,1,0:T(8,128)S(1)} %get-tuple-element.55), channel_id=1, source_target_pairs={{0,8},{16,24},{8,0},{24,16},{1,9},{17,25},{9,1},{25,17},{2,10},{18... | collective-permute-start | bytes 454664 | tf_op jit(solution)/shard_map/ppermute | solution.py:316
  37.7 5.5 %collective-permute-start.12 = (f32[37,8,128]{2,1,0:T(8,128)S(1)}, f32[37,8,128]{2,1,0:T(8,128)S(1)}, u32[]{:S(2)}, u32[]{:S(2)}) collective-permute-start(f32[37,8,128]{2,1,0:T(8,128)S(1)} %get-tuple-element.56), channel_id=1, source_target_pairs={{8,16},{24,0},{16,8},{0,24},{9,17},{25,1},{17,9},{1,25},{10,18},{2... | collective-permute-start | bytes 454664 | tf_op jit(solution)/shard_map/ppermute | solution.py:316
  38.5 7.7 %collective-permute-start.14 = (f32[36,8,128]{2,1,0:T(8,128)S(1)}, f32[36,8,128]{2,1,0:T(8,128)S(1)}, u32[]{:S(2)}, u32[]{:S(2)}) collective-permute-start(f32[36,8,128]{2,1,0:T(8,128)S(1)} %get-tuple-element.60), channel_id=1, source_target_pairs={{1,2},{3,4},{5,6},{2,1},{4,3},{6,5},{9,10},{11,12},{13,14},{10,9},... | collective-permute-start | bytes 442376 | tf_op jit(solution)/shard_map/ppermute | solution.py:316

commit v5 on v4

--- a/solution.py
+++ b/solution.py
@@ -125,24 +125,38 @@
     return functools.reduce(jnp.maximum, rows), -functools.reduce(jnp.minimum, rows)
 
 
-def opening_kernel(level_ref, wind_ref, *refs):
-    most_ref = refs[-1]
+def put_extremes(wind_ref, most_ref):
     top, low = extremes_of(wind_ref)
     most_ref[...] = jnp.zeros_like(most_ref)
     most_ref[0:2, :] = top
     most_ref[2:4, :] = low
-    cut_edges(level_ref, *refs[:-1])
-
-
-def speed_kernel(speed_step, s_ref, *refs):
-    if len(refs) == 1:
-        part_ref = refs[0]
-    else:
-        wind_ref, other_ref, part_ref, most_ref = refs
-        top, low = extremes_of(wind_ref)
-        most_ref[...] = other_ref[...]
-        most_ref[0:2, :] = jnp.maximum(top, other_ref[0:2, :])
-        most_ref[2:4, :] = jnp.maximum(low, other_ref[2:4, :])
+
+
+def opening_kernel(level_in, wind_in, level_ref, x_near, x_far, t_near, t_far, wind_ref, sems):
+    planes, headings = level_ref.shape[:2]
+    step = planes // batches(planes, 3)
+    pairs = [(wind_in, wind_ref)] + [
+        (level_in.at[pl.ds(i, step)], level_ref.at[pl.ds(i, step)])
+        for i in range(0, planes, step)
+    ]
+    copies = [
+        pltpu.make_async_copy(src, dst, sems.at[k]) for k, (src, dst) in enumerate(pairs)
+    ]
+    for copy in copies:
+        copy.start()
+    copies[0].wait()
+    put_extremes(wind_ref, x_near.at[x_near.shape[0] - 2])
+    for copy in copies[1:]:
+        copy.wait()
+    cut_edges(level_ref, x_near, x_far, t_near, t_far)
+
+
+def meeting_kernel(wind_ref, x_near, most_ref):
+    put_extremes(wind_ref, most_ref)
+    most_ref[...] = jnp.maximum(most_ref[...], x_near[x_near.shape[0] - 2])
+
+
+def speed_kernel(speed_step, s_ref, part_ref):
     planes, headings, speeds, width = s_ref.shape
     gain_v = thrust_limit / (12.0 * speed_step)
     cells = planes * headings
@@ -150,7 +164,7 @@
     s_rows = s_ref.reshape(cells * speeds, width)
     part_rows = part_ref.reshape(cells * speeds, width)
     groups = -(-cells // group)
-    wide = batches(groups, 2)
+    wide = batches(groups, 7)
 
     def step(n, carry):
         for k in range(wide):
@@ -178,7 +192,7 @@
         peak = splat(pk_ref[1:2, :] * gain, tile)
     pace = speeds_of(tile, speed_step) * gain
     first = lax.axis_index("head") * headings
-    wide = batches(headings, 2)
+    wide = batches(headings, 4)
 
     def step(n, carry):
         for k in range(wide):
@@ -263,7 +277,7 @@
         edge_refs = [refs.pop(0) for _ in range(4)]
     if section == 1:
         pk_ref = refs.pop(0)
-    flow_ref, target_ref = refs
+    flow_ref, target_ref = refs[:2]
     planes, headings = s_ref.shape[:2]
     tile = s_ref.shape[2:]
     if section == 1:
@@ -281,7 +295,12 @@
     time_step = splat(pk_ref[2:3, :], tile)
     pace = speeds_of(tile, speed_step) * gain
     first = lax.axis_index("head") * headings
-    wide = batches(headings, 3)
+    wide = batches(headings, 6 if section < 3 else 3)
+    result_ref = out_ref if section < 3 else refs[2]
+
+    def leaving(n):
+        part = (slice(None), pl.ds(n * wide, wide))
+        return pltpu.make_async_copy(result_ref.at[part], out_ref.at[part], refs[3].at[n])
 
     def step(n, carry):
         for w in range(wide):
@@ -300,12 +319,17 @@
                     moved = 0.75 * base_ref[i, j] + 0.25 * moved
                 if section == 3:
                     moved = (1.0 / 3.0) * base_ref[i, j] + (2.0 / 3.0) * moved
-                out_ref[i, j] = jnp.minimum(moved, target_ref[i])
+                result_ref[i, j] = jnp.minimum(moved, target_ref[i])
+        if section == 3:
+            leaving(n).start()
         return carry
 
     lax.fori_loop(0, headings // wide, step, 0)
     if section < 3:
         cut_edges(out_ref, *edge_refs)
+    else:
+        for n in range(headings // wide):
+            leaving(n).wait()
 
 
 def trade(value, axis, reach, wrap=False):
@@ -339,21 +363,19 @@
         return jax.ShapeDtypeStruct(dims + tile, jnp.float32)
 
     field = shape(planes, headings)
-    short = rim * headings
-    middle = max(short + 1, rim * planes)
-
-    def edge_shapes(far_first):
-        x_shapes = [shape(middle + 1), shape(short)]
-        return x_shapes[:: -1 if far_first else 1] + [shape(middle)] * 2
+    short = rim * max(planes, headings)
+
+    def edge_shapes():
+        return [shape(short + 2), shape(short + 1)] + [shape(rim * planes)] * 2
 
     cells = math.prod(level_set.shape)
 
-    def call(kernel, ins, outs, scratch=(), work=0):
+    def call(kernel, ins, outs, scratch=(), work=0, place=vmem):
         return pl.pallas_call(
             kernel,
             out_shape=outs,
             in_specs=[vmem] * len(ins),
-            out_specs=[vmem] * len(outs),
+            out_specs=[place] * len(outs),
             scratch_shapes=list(scratch),
             compiler_params=pltpu.CompilerParams(vmem_limit_bytes=16 * 1024 * 1024),
             cost_estimate=pl.CostEstimate(
@@ -362,7 +384,6 @@
         )(*ins)
 
     wind = jnp.transpose(wind_field, (1, 0, 2))
-    values, pk = level_set, None
     size = lax.axis_size("gx")
 
     def spread(most, reach):
@@ -372,52 +393,56 @@
             pairs = [(i, i ^ reach) for i in range(size)]
         return lax.ppermute(most, "gx", pairs)
 
+    hbm = pl.BlockSpec(memory_space=pltpu.HBM)
+    level, *edges = pl.pallas_call(
+        opening_kernel,
+        out_shape=[field] + edge_shapes(),
+        in_specs=[hbm] * 2,
+        out_specs=[vmem] * 5,
+        scratch_shapes=[pltpu.VMEM(wind.shape, jnp.float32), pltpu.SemaphoreType.DMA((planes + 1,))],
+        cost_estimate=pl.CostEstimate(flops=0, bytes_accessed=0, transcendentals=0),
+    )(level_set, wind)
+    values, pk = level, None
     for section in (1, 2, 3):
         opening = section == 1
-        speed = functools.partial(speed_kernel, speed_step)
-        if opening:
-            *edges, most = call(opening_kernel, [values, wind], edge_shapes(True) + [shape()])
-            other = spread(most, 1)
         x_out, x_last, t_out, t_last = edges
-        if opening:
-            x_far = trade(x_last, "gx", 1)
-        else:
-            x_near = trade(x_out, "gx", 0)
+        x_near = trade(x_out, "gx", 0)
+        x_far = trade(x_last, "gx", 1)
         t_near = trade(t_out, "head", 0)
         t_far = trade(t_last, "head", 1, True)
+        (part,) = call(functools.partial(speed_kernel, speed_step), [values], [field])
         if opening:
-            part, most = call(speed, [values, wind, other], [field, shape()])
+            (most,) = call(meeting_kernel, [wind, x_near], [shape()])
             other = spread(most, 2)
-            x_out, most = lax.optimization_barrier((x_out, most))
-            x_near = trade(x_out, "gx", 0)
-        else:
-            (part,) = call(speed, [values], [field])
-            x_far = trade(x_last, "gx", 1)
-        turning = functools.partial(heading_kernel, heading_step)
-        (part,) = call(turning, [values, part, t_near, t_far], [field])
+        cross = functools.partial(cross_kernel, opening, speed_step)
+        ins = [values, part, wind, waves] + ([] if opening else [pk])
+        part, *extra = call(cross, ins, [field] * (2 if opening else 1), work=100)
         if opening:
             reach = 4
             while reach < size:
                 most = jnp.maximum(most, other)
+                most, part = lax.optimization_barrier((most, part))
                 other = spread(most, reach)
                 reach *= 2
-            part, x_far = lax.optimization_barrier((part, x_far))
-        else:
-            part, x_near = lax.optimization_barrier((part, x_near))
-        cross = functools.partial(cross_kernel, opening, speed_step)
-        ins = [values, part, wind, waves] + ([] if opening else [pk])
-        part, *extra = call(cross, ins, [field] * (2 if opening else 1), work=1000)
+        turning = functools.partial(heading_kernel, heading_step)
+        (part,) = call(turning, [values, part, t_near, t_far], [field])
         last = functools.partial(section_kernel, section, bounds, heading_step, speed_step)
-        ins = ([] if opening else [level_set]) + [values, part, *extra, x_near, x_far]
+        ins = ([] if opening else [level]) + [values, part, *extra, x_near, x_far]
         ins += [wind, waves, target_mask, target_depth]
         ins += [most, other] if opening else [pk]
         outs = [field]
         if section < 3:
-            outs += edge_shapes(False)
+            outs += edge_shapes()
         if opening:
             outs += [shape()]
         rows = pltpu.VMEM((planes,) + tile, jnp.float32)
-        results = call(last, ins, outs, [rows, rows])
+        scratch = [rows, rows]
+        if section == 3:
+            scratch += [
+                pltpu.VMEM(level_set.shape, jnp.float32),
+                pltpu.SemaphoreType.DMA((headings,)),
+            ]
+        results = call(last, ins, outs, scratch, place=vmem if section < 3 else hbm)
         values, edges = results[0], results[1:5]
         if opening:
             pk = results[5]

time: 48.2 us -> 53.8 us (1.12)
  the two profiles are of different devices: /device:TPU:1 before, /device:TPU:13 now
where the time goes in v5:
time: 53.8 us; the launch traced here: 53.6 us
  Pallas kernels  26.1 us (49%)
  starting transfers between devices  25.9 us (48%)
  local copies, waits for them, and re-layouts  1.14 us (2%)
    pallas_call x13, Pallas kernels, call(): pl.pallas_call(kernel, out_shape=outs, in_specs=[vmem] * len(ins), out_sp...  24 us
    ppermute x12, starting transfers between devices, trade(): return lax.ppermute(value, axis, pairs + [(j, i) for i, j in pairs])  23.3 us
    ppermute x2, starting transfers between devices, spread(): return lax.ppermute(most, 'gx', pairs)  2.6 us
    pallas_call x1, Pallas kernels, local(): pl.pallas_call(opening_kernel, out_shape=[field] + edge_shapes(), in_spec...  2.1 us
    unnamed x12, local copies, waits for them, and re-layouts  1.14 us
  transfers between devices with their start and end apart: 14, of which 1 were waited for; matrix products, arithmetic and copies ran while one was open for 0% of the time, Pallas kernels for 37%

profile of v5, /device:TPU:13, one launch (start us, length us, event | category | flops | bytes accessed | tf_op | source)
XLA Modules:
  0.0 53.6 jit_solution(8576580636560720293)
XLA Ops:
  0.0 0.0 copy-start.3
  0.0 2.1 %shard_map.55 = (f32[9,12,8,128]{3,2,1,0:T(8,128)}, f32[38,8,128]{2,1,0:T(8,128)}, f32[37,8,128]{2,1,0:T(8,128)}, f32[27,8,128]{2,1,0:T(8,128)}, f32[27,8,128]{2,1,0:T(8,128)}) custom-call(f32[9,12,8,128]{3,2,1,0:T(8,128)} %level_in.1, f32[9,2,128]{2,1,0:T(2,128)} %bitcast.1), custom_call_target="tpu_custom_call" | custom-call | tf_op jit(solution)/shard_map/pallas_call | solution.py:397
  2.1 0.3 collective-permute-start
  2.4 4.1 %collective-permute-start.4 = (f32[37,8,128]{2,1,0:T(8,128)}, f32[37,8,128]{2,1,0:T(8,128)S(1)}, u32[]{:S(2)}, u32[]{:S(2)}) collective-permute-start(f32[37,8,128]{2,1,0:T(8,128)} %get-tuple-element.32), channel_id=1, source_target_pairs={{1,2},{3,4},{5,6},{2,1},{4,3},{6,5},{9,10},{11,12},{13,14},{10,9},... | collective-permute-start | bytes 454664 | tf_op jit(solution)/shard_map/ppermute | solution.py:340
  6.6 1.3 %collective-permute-start.2 = (f32[27,8,128]{2,1,0:T(8,128)}, f32[27,8,128]{2,1,0:T(8,128)S(1)}, u32[]{:S(2)}, u32[]{:S(2)}) collective-permute-start(f32[27,8,128]{2,1,0:T(8,128)} %get-tuple-element.29), channel_id=1, source_target_pairs={{0,8},{16,24},{8,0},{24,16},{1,9},{17,25},{9,1},{25,17},{2,10},{18... | collective-permute-start | bytes 331784 | tf_op jit(solution)/shard_map/ppermute | solution.py:340
  7.9 1.2 %collective-permute-start.3 = (f32[27,8,128]{2,1,0:T(8,128)}, f32[27,8,128]{2,1,0:T(8,128)S(1)}, u32[]{:S(2)}, u32[]{:S(2)}) collective-permute-start(f32[27,8,128]{2,1,0:T(8,128)} %get-tuple-element.30), channel_id=1, source_target_pairs={{8,16},{24,0},{16,8},{0,24},{9,17},{25,1},{17,9},{1,25},{10,18},{2... | collective-permute-start | bytes 331784 | tf_op jit(solution)/shard_map/ppermute | solution.py:340
  9.0 0.0 collective-permute-done.x_near.refs_3_
  9.0 0.0 copy-done.3
  9.1 0.2 collective-permute-start.1
  9.3 0.0 copy-start
  9.3 1.0 %copy-done = f32[9,12,8,128]{3,2,1,0:T(8,128)S(1)} copy-done((f32[9,12,8,128]{3,2,1,0:T(8,128)S(1)}, f32[9,12,8,128]{3,2,1,0:T(8,128)}, u32[]{:S(2)}) %copy-start) | copy-done | bytes 442392
  10.3 0.0 copy-start.1
  10.3 0.0 copy-start.2
  10.3 0.9 %shard_map.57.part_ref = f32[9,12,8,128]{3,2,1,0:T(8,128)S(1)} custom-call(f32[9,12,8,128]{3,2,1,0:T(8,128)S(1)} %copy-done), custom_call_target="tpu_custom_call" | custom-call | tf_op jit(solution)/shard_map/pallas_call | solution.py:374
  11.2 0.1 copy-done.1
  11.3 0.0 copy-done.2
  11.3 4.9 %shard_map.58 = (f32[9,12,8,128]{3,2,1,0:T(8,128)S(1)}, f32[9,12,8,128]{3,2,1,0:T(8,128)S(1)}) custom-call(f32[9,12,8,128]{3,2,1,0:T(8,128)S(1)} %copy-done.1, f32[9,12,8,128]{3,2,1,0:T(8,128)S(1)} %shard_map.57.part_ref, f32[9,2,128]{2,1,0:T(2,128)S(1)} %bitcast.3, f32[2,48,128]{2,1,0:T(8,128)S(1)} %copy-done.2), custom_call_target="tpu_custom_call" | custom-call | flops 11059200 | bytes 11059200 | tf_op jit(solution)/shard_map/pallas_call | solution.py:374
  16.2 0.0 collective-permute-done.1
  16.3 0.0 copy-start.4
  16.3 0.0 copy-start.5
  16.3 2.4 %collective-permute-start.5 = (f32[8,128]{1,0:T(8,128)S(1)}, f32[8,128]{1,0:T(8,128)S(1)}, u32[]{:S(2)}, u32[]{:S(2)}) collective-permute-start(f32[8,128]{1,0:T(8,128)S(1)} %max.3.refs_9_), channel_id=1, source_target_pairs={{0,4},{1,5},{2,6},{3,7},{4,0},{5,1},{6,2},{7,3},{8,12},{9,13},{10,... | collective-permute-start | bytes 12296 | tf_op jit(solution)/shard_map/ppermute | solution.py:394
  18.7 0.0 collective-permute-done.2.near_ref
  18.7 0.0 collective-permute-done.3.far_ref
  18.7 0.8 %shard_map.59.refs_1_ = f32[9,12,8,128]{3,2,1,0:T(8,128)S(1)} custom-call(f32[9,12,8,128]{3,2,1,0:T(8,128)S(1)} %copy-done.1, f32[9,12,8,128]{3,2,1,0:T(8,128)S(1)} %get-tuple-element.28.part_ref, f32[27,8,128]{2,1,0:T(8,128)S(1)} %collective-permute-done.2.near_ref, f32[27,8,128]{2,1,0:T(8,128)S(1)} %collective-permute-done.3.far_ref), custom_call_target="tpu_custom_call" | custom-call | tf_op jit(solution)/shard_map/pallas_call | solution.py:374
  19.5 0.0 collective-permute-done.4.refs_4_
  19.5 0.2 collective-permute-done.5.refs_10_
  19.7 0.0 copy-done.4
  19.7 0.0 copy-done.5
  19.7 1.2 %shard_map.60 = (f32[9,12,8,128]{3,2,1,0:T(8,128)S(1)}, f32[38,8,128]{2,1,0:T(8,128)S(1)}, f32[37,8,128]{2,1,0:T(8,128)S(1)}, f32[27,8,128]{2,1,0:T(8,128)S(1)},...) custom-call(f32[9,12,8,128]{3,2,1,0:T(8,128)S(1)} %copy-done.1, f32[9,12,8,128]{3,2,1,0:T(8,128)S(1)} %shard_map.59.refs_1_, ...), custom_call_target="tpu_custom_call" | custom-call | tf_op jit(solution)/shard_map/pallas_call | solution.py:374
  20.9 0.1 collective-permute-start.8
  21.0 4.2 %collective-permute-start.9 = (f32[37,8,128]{2,1,0:T(8,128)S(1)}, f32[37,8,128]{2,1,0:T(8,128)S(1)}, u32[]{:S(2)}, u32[]{:S(2)}) collective-permute-start(f32[37,8,128]{2,1,0:T(8,128)S(1)} %get-tuple-element.39), channel_id=1, source_target_pairs={{1,2},{3,4},{5,6},{2,1},{4,3},{6,5},{9,10},{11,12},{13,14},{10,9},... | collective-permute-start | bytes 454664 | tf_op jit(solution)/shard_map/ppermute | solution.py:340
  25.2 4.8 %collective-permute-start.6 = (f32[27,8,128]{2,1,0:T(8,128)S(1)}, f32[27,8,128]{2,1,0:T(8,128)S(1)}, u32[]{:S(2)}, u32[]{:S(2)}) collective-permute-start(f32[27,8,128]{2,1,0:T(8,128)S(1)} %get-tuple-element.36), channel_id=1, source_target_pairs={{0,8},{16,24},{8,0},{24,16},{1,9},{17,25},{9,1},{25,17},{2,10},{18... | collective-permute-start | bytes 331784 | tf_op jit(solution)/shard_map/ppermute | solution.py:340
  30.0 1.2 %collective-permute-start.7 = (f32[27,8,128]{2,1,0:T(8,128)S(1)}, f32[27,8,128]{2,1,0:T(8,128)S(1)}, u32[]{:S(2)}, u32[]{:S(2)}) collective-permute-start(f32[27,8,128]{2,1,0:T(8,128)S(1)} %get-tuple-element.37), channel_id=1, source_target_pairs={{8,16},{24,0},{16,8},{0,24},{9,17},{25,1},{17,9},{1,25},{10,18},{2... | collective-permute-start | bytes 331784 | tf_op jit(solution)/shard_map/ppermute | solution.py:340
  31.2 0.9 %shard_map.61.part_ref = f32[9,12,8,128]{3,2,1,0:T(8,128)S(1)} custom-call(f32[9,12,8,128]{3,2,1,0:T(8,128)S(1)} %get-tuple-element.34.s_ref.refs_1_), custom_call_target="tpu_custom_call" | custom-call | tf_op jit(solution)/shard_map/pallas_call | solution.py:374
  32.1 4.9 %shard_map.62.part_ref = f32[9,12,8,128]{3,2,1,0:T(8,128)S(1)} custom-call(f32[9,12,8,128]{3,2,1,0:T(8,128)S(1)} %get-tuple-element.34.s_ref.refs_1_, f32[9,12,8,128]{3,2,1,0:T(8,128)S(1)} %shard_map.61.part_ref, f32[9,2,128]{2,1,0:T(2,128)S(1)} %bitcast.5, f32[2,48,128]{2,1,0:T(8,128)S(1)} %copy-done.2, f32[8,128]{1,0:T(8,128)S(1)} %get-tuple-element.35.rest_0_.refs_9_), custom_call_target="tpu_custom_call" | custom-call | flops 11059200 | bytes 11059200 | tf_op jit(solution)/shard_map/pallas_call | solution.py:374
  37.0 0.0 collective-permute-done.6.near_ref
  37.0 0.0 collective-permute-done.7.far_ref
  37.0 0.8 %shard_map.63.refs_2_ = f32[9,12,8,128]{3,2,1,0:T(8,128)S(1)} custom-call(f32[9,12,8,128]{3,2,1,0:T(8,128)S(1)} %get-tuple-element.34.s_ref.refs_1_, f32[9,12,8,128]{3,2,1,0:T(8,128)S(1)} %shard_map.62.part_ref, f32[27,8,128]{2,1,0:T(8,128)S(1)} %collective-permute-done.6.near_ref, f32[27,8,128]{2,1,0:T(8,128)S(1)} %collective-permute-done.7.far_ref), custom_call_target="tpu_custom_call" | custom-call | tf_op jit(solution)/shard_map/pallas_call | solution.py:374
  37.9 0.0 collective-permute-done.9.refs_4_
  37.9 0.0 collective-permute-done.8.refs_3_
  37.9 1.0 %shard_map.64 = (f32[9,12,8,128]{3,2,1,0:T(8,128)S(1)}, f32[38,8,128]{2,1,0:T(8,128)S(1)}, f32[37,8,128]{2,1,0:T(8,128)S(1)}, f32[27,8,128]{2,1,0:T(8,128)S(1)}, f32[27,8,128]{2,1,0:T(8,128)S(1)}) custom-call(f32[9,12,8,128]{3,2,1,0:T(8,128)S(1)} %copy-done.1, f32[9,12,8,128]{3,2,1,0:T(8,128)S(1)} %get-tuple-element.34.s_ref.refs_1_, ...), custom_call_target="tpu_custom_call" | custom-call | tf_op jit(solution)/shard_map/pallas_call | solution.py:374
  38.9 0.2 collective-permute-start.12
  39.2 4.6 %collective-permute-start.13 = (f32[37,8,128]{2,1,0:T(8,128)S(1)}, f32[37,8,128]{2,1,0:T(8,128)S(1)}, u32[]{:S(2)}, u32[]{:S(2)}) collective-permute-start(f32[37,8,128]{2,1,0:T(8,128)S(1)} %get-tuple-element.44), channel_id=1, source_target_pairs={{1,2},{3,4},{5,6},{2,1},{4,3},{6,5},{9,10},{11,12},{13,14},{10,9},... | collective-permute-start | bytes 454664 | tf_op jit(solution)/shard_map/ppermute | solution.py:340
  43.8 1.1 %collective-permute-start.10 = (f32[27,8,128]{2,1,0:T(8,128)S(1)}, f32[27,8,128]{2,1,0:T(8,128)S(1)}, u32[]{:S(2)}, u32[]{:S(2)}) collective-permute-start(f32[27,8,128]{2,1,0:T(8,128)S(1)} %get-tuple-element.41), channel_id=1, source_target_pairs={{0,8},{16,24},{8,0},{24,16},{1,9},{17,25},{9,1},{25,17},{2,10},{18... | collective-permute-start | bytes 331784 | tf_op jit(solution)/shard_map/ppermute | solution.py:340
  44.9 0.2 collective-permute-start.11
  45.1 0.9 %shard_map.65.part_ref = f32[9,12,8,128]{3,2,1,0:T(8,128)S(1)} custom-call(f32[9,12,8,128]{3,2,1,0:T(8,128)S(1)} %get-tuple-element.40.s_ref.refs_1_), custom_call_target="tpu_custom_call" | custom-call | tf_op jit(solution)/shard_map/pallas_call | solution.py:374
  46.0 4.9 %shard_map.66.part_ref = f32[9,12,8,128]{3,2,1,0:T(8,128)S(1)} custom-call(f32[9,12,8,128]{3,2,1,0:T(8,128)S(1)} %get-tuple-element.40.s_ref.refs_1_, f32[9,12,8,128]{3,2,1,0:T(8,128)S(1)} %shard_map.65.part_ref, f32[9,2,128]{2,1,0:T(2,128)S(1)} %bitcast.7, f32[2,48,128]{2,1,0:T(8,128)S(1)} %copy-done.2, f32[8,128]{1,0:T(8,128)S(1)} %get-tuple-element.35.rest_0_.refs_9_), custom_call_target="tpu_custom_call" | custom-call | flops 11059200 | bytes 11059200 | tf_op jit(solution)/shard_map/pallas_call | solution.py:374
  50.9 0.0 collective-permute-done.10.near_ref
  50.9 0.0 collective-permute-done.11.far_ref
  51.0 0.8 %shard_map.67.refs_2_ = f32[9,12,8,128]{3,2,1,0:T(8,128)S(1)} custom-call(f32[9,12,8,128]{3,2,1,0:T(8,128)S(1)} %get-tuple-element.40.s_ref.refs_1_, f32[9,12,8,128]{3,2,1,0:T(8,128)S(1)} %shard_map.66.part_ref, f32[27,8,128]{2,1,0:T(8,128)S(1)} %collective-permute-done.10.near_ref, f32[27,8,128]{2,1,0:T(8,128)S(1)} %collective-permute-done.11.far_ref), custom_call_target="tpu_custom_call" | custom-call | tf_op jit(solution)/shard_map/pallas_call | solution.py:374
  51.8 0.0 collective-permute-done.13.refs_4_
  51.8 0.0 collective-permute-done.12.refs_3_
  51.8 1.8 %shard_map.68 = f32[9,12,8,128]{3,2,1,0:T(8,128)} custom-call(f32[9,12,8,128]{3,2,1,0:T(8,128)S(1)} %copy-done.1, f32[9,12,8,128]{3,2,1,0:T(8,128)S(1)} %get-tuple-element.40.s_ref.refs_1_, f32[9,12,8,128]{3,2,1,0:T(8,128)S(1)} %shard_map.67.refs_2_, f32[38,8,128]{2,1,0:T(8,128)S(1)} %collective-permute-done.12.refs_3_, ...), custom_call_target="tpu_custom_call" | custom-call | tf_op jit(solution)/shard_map/pallas_call | solution.py:374
  (2 shorter events, 0.0 us)
Async XLA Ops:
  0.0 9.0 %copy-start.3 = (f32[2,9,128]{2,0,1:T(2,128)S(1)}, f32[2,9,128]{2,0,1:T(2,128)}, u32[]{:S(2)}) copy-start(f32[2,9,128]{2,0,1:T(2,128)} %param.6) | copy-start | bytes 27652
  2.1 6.9 %collective-permute-start = (f32[38,8,128]{2,1,0:T(8,128)}, f32[38,8,128]{2,1,0:T(8,128)S(1)}, u32[]{:S(2)}, u32[]{:S(2)}) collective-permute-start(f32[38,8,128]{2,1,0:T(8,128)} %get-tuple-element.26), channel_id=1, source_target_pairs={{0,1},{2,3},{4,5},{6,7},{1,0},{3,2},{5,4},{7,6},{8,9},{10,11},{12,... | collective-permute-start | bytes 466952 | tf_op jit(solution)/shard_map/ppermute | solution.py:340
  2.4 17.1 %collective-permute-start.4 = (f32[37,8,128]{2,1,0:T(8,128)}, f32[37,8,128]{2,1,0:T(8,128)S(1)}, u32[]{:S(2)}, u32[]{:S(2)}) collective-permute-start(f32[37,8,128]{2,1,0:T(8,128)} %get-tuple-element.32), channel_id=1, source_target_pairs={{1,2},{3,4},{5,6},{2,1},{4,3},{6,5},{9,10},{11,12},{13,14},{10,9},... | collective-permute-start | bytes 454664 | tf_op jit(solution)/shard_map/ppermute | solution.py:340
  6.6 12.1 %collective-permute-start.2 = (f32[27,8,128]{2,1,0:T(8,128)}, f32[27,8,128]{2,1,0:T(8,128)S(1)}, u32[]{:S(2)}, u32[]{:S(2)}) collective-permute-start(f32[27,8,128]{2,1,0:T(8,128)} %get-tuple-element.29), channel_id=1, source_target_pairs={{0,8},{16,24},{8,0},{24,16},{1,9},{17,25},{9,1},{25,17},{2,10},{18... | collective-permute-start | bytes 331784 | tf_op jit(solution)/shard_map/ppermute | solution.py:340
  7.9 10.8 %collective-permute-start.3 = (f32[27,8,128]{2,1,0:T(8,128)}, f32[27,8,128]{2,1,0:T(8,128)S(1)}, u32[]{:S(2)}, u32[]{:S(2)}) collective-permute-start(f32[27,8,128]{2,1,0:T(8,128)} %get-tuple-element.30), channel_id=1, source_target_pairs={{8,16},{24,0},{16,8},{0,24},{9,17},{25,1},{17,9},{1,25},{10,18},{2... | collective-permute-start | bytes 331784 | tf_op jit(solution)/shard_map/ppermute | solution.py:340
  9.1 7.2 %collective-permute-start.1 = (f32[8,128]{1,0:T(8,128)S(1)}, f32[8,128]{1,0:T(8,128)S(1)}, u32[]{:S(2)}, u32[]{:S(2)}) collective-permute-start(f32[8,128]{1,0:T(8,128)S(1)} %shard_map.56), channel_id=1, source_target_pairs={{0,2},{1,3},{2,0},{3,1},{4,6},{5,7},{6,4},{7,5},{8,10},{9,11},{10,... | collective-permute-start | bytes 12296 | tf_op jit(solution)/shard_map/ppermute | solution.py:394
  9.3 1.0 %copy-start = (f32[9,12,8,128]{3,2,1,0:T(8,128)S(1)}, f32[9,12,8,128]{3,2,1,0:T(8,128)}, u32[]{:S(2)}) copy-start(f32[9,12,8,128]{3,2,1,0:T(8,128)} %get-tuple-element.25.s_ref.refs_0_) | copy-start | bytes 1327108
  10.3 1.0 %copy-start.1 = (f32[9,12,8,128]{3,2,1,0:T(8,128)S(1)}, f32[9,12,8,128]{3,2,1,0:T(8,128)}, u32[]{:S(2)}) copy-start(f32[9,12,8,128]{3,2,1,0:T(8,128)} %get-tuple-element.25.s_ref.refs_0_) | copy-start | bytes 1327108
  10.3 1.0 %copy-start.2 = (f32[2,48,128]{2,1,0:T(8,128)S(1)}, f32[2,48,128]{2,1,0:T(8,128)}, u32[]{:S(2)}) copy-start(f32[2,48,128]{2,1,0:T(8,128)} %constant.2.clone.waves_ref.refs_6_) | copy-start | bytes 147460
  16.3 3.4 %copy-start.4 = (s32[9,128]{1,0:T(8,128)S(1)}, s32[9,128]{1,0:T(8,128)}, u32[]{:S(2)}) copy-start(s32[9,128]{1,0:T(8,128)} %refs_7_.5) | copy-start | bytes 13828
  16.3 3.4 %copy-start.5 = (f32[9,128]{1,0:T(8,128)S(1)}, f32[9,128]{1,0:T(8,128)}, u32[]{:S(2)}) copy-start(f32[9,128]{1,0:T(8,128)} %refs_8_.5) | copy-start | bytes 13828
  16.3 3.4 %collective-permute-start.5 = (f32[8,128]{1,0:T(8,128)S(1)}, f32[8,128]{1,0:T(8,128)S(1)}, u32[]{:S(2)}, u32[]{:S(2)}) collective-permute-start(f32[8,128]{1,0:T(8,128)S(1)} %max.3.refs_9_), channel_id=1, source_target_pairs={{0,4},{1,5},{2,6},{3,7},{4,0},{5,1},{6,2},{7,3},{8,12},{9,13},{10,... | collective-permute-start | bytes 12296 | tf_op jit(solution)/shard_map/ppermute | solution.py:394
  20.9 17.0 %collective-permute-start.8 = (f32[38,8,128]{2,1,0:T(8,128)S(1)}, f32[38,8,128]{2,1,0:T(8,128)S(1)}, u32[]{:S(2)}, u32[]{:S(2)}) collective-permute-start(f32[38,8,128]{2,1,0:T(8,128)S(1)} %get-tuple-element.38), channel_id=1, source_target_pairs={{0,1},{2,3},{4,5},{6,7},{1,0},{3,2},{5,4},{7,6},{8,9},{10,11},{12,... | collective-permute-start | bytes 466952 | tf_op jit(solution)/shard_map/ppermute | solution.py:340
  21.0 16.9 %collective-permute-start.9 = (f32[37,8,128]{2,1,0:T(8,128)S(1)}, f32[37,8,128]{2,1,0:T(8,128)S(1)}, u32[]{:S(2)}, u32[]{:S(2)}) collective-permute-start(f32[37,8,128]{2,1,0:T(8,128)S(1)} %get-tuple-element.39), channel_id=1, source_target_pairs={{1,2},{3,4},{5,6},{2,1},{4,3},{6,5},{9,10},{11,12},{13,14},{10,9},... | collective-permute-start | bytes 454664 | tf_op jit(solution)/shard_map/ppermute | solution.py:340
  25.2 11.8 %collective-permute-start.6 = (f32[27,8,128]{2,1,0:T(8,128)S(1)}, f32[27,8,128]{2,1,0:T(8,128)S(1)}, u32[]{:S(2)}, u32[]{:S(2)}) collective-permute-start(f32[27,8,128]{2,1,0:T(8,128)S(1)} %get-tuple-element.36), channel_id=1, source_target_pairs={{0,8},{16,24},{8,0},{24,16},{1,9},{17,25},{9,1},{25,17},{2,10},{18... | collective-permute-start | bytes 331784 | tf_op jit(solution)/shard_map/ppermute | solution.py:340
  30.0 7.0 %collective-permute-start.7 = (f32[27,8,128]{2,1,0:T(8,128)S(1)}, f32[27,8,128]{2,1,0:T(8,128)S(1)}, u32[]{:S(2)}, u32[]{:S(2)}) collective-permute-start(f32[27,8,128]{2,1,0:T(8,128)S(1)} %get-tuple-element.37), channel_id=1, source_target_pairs={{8,16},{24,0},{16,8},{0,24},{9,17},{25,1},{17,9},{1,25},{10,18},{2... | collective-permute-start | bytes 331784 | tf_op jit(solution)/shard_map/ppermute | solution.py:340
  38.9 12.9 %collective-permute-start.12 = (f32[38,8,128]{2,1,0:T(8,128)S(1)}, f32[38,8,128]{2,1,0:T(8,128)S(1)}, u32[]{:S(2)}, u32[]{:S(2)}) collective-permute-start(f32[38,8,128]{2,1,0:T(8,128)S(1)} %get-tuple-element.43), channel_id=1, source_target_pairs={{0,1},{2,3},{4,5},{6,7},{1,0},{3,2},{5,4},{7,6},{8,9},{10,11},{12,... | collective-permute-start | bytes 466952 | tf_op jit(solution)/shard_map/ppermute | solution.py:340
  39.2 12.6 %collective-permute-start.13 = (f32[37,8,128]{2,1,0:T(8,128)S(1)}, f32[37,8,128]{2,1,0:T(8,128)S(1)}, u32[]{:S(2)}, u32[]{:S(2)}) collective-permute-start(f32[37,8,128]{2,1,0:T(8,128)S(1)} %get-tuple-element.44), channel_id=1, source_target_pairs={{1,2},{3,4},{5,6},{2,1},{4,3},{6,5},{9,10},{11,12},{13,14},{10,9},... | collective-permute-start | bytes 454664 | tf_op jit(solution)/shard_map/ppermute | solution.py:340
  43.8 7.1 %collective-permute-start.10 = (f32[27,8,128]{2,1,0:T(8,128)S(1)}, f32[27,8,128]{2,1,0:T(8,128)S(1)}, u32[]{:S(2)}, u32[]{:S(2)}) collective-permute-start(f32[27,8,128]{2,1,0:T(8,128)S(1)} %get-tuple-element.41), channel_id=1, source_target_pairs={{0,8},{16,24},{8,0},{24,16},{1,9},{17,25},{9,1},{25,17},{2,10},{18... | collective-permute-start | bytes 331784 | tf_op jit(solution)/shard_map/ppermute | solution.py:340
  44.9 6.1 %collective-permute-start.11 = (f32[27,8,128]{2,1,0:T(8,128)S(1)}, f32[27,8,128]{2,1,0:T(8,128)S(1)}, u32[]{:S(2)}, u32[]{:S(2)}) collective-permute-start(f32[27,8,128]{2,1,0:T(8,128)S(1)} %get-tuple-element.42), channel_id=1, source_target_pairs={{8,16},{24,0},{16,8},{0,24},{9,17},{25,1},{17,9},{1,25},{10,18},{2... | collective-permute-start | bytes 331784 | tf_op jit(solution)/shard_map/ppermute | solution.py:340

commit v6 on v4

--- a/solution.py
+++ b/solution.py
@@ -125,60 +125,46 @@
     return functools.reduce(jnp.maximum, rows), -functools.reduce(jnp.minimum, rows)
 
 
-def opening_kernel(level_ref, wind_ref, *refs):
-    most_ref = refs[-1]
+def put_extremes(wind_ref, most_ref):
     top, low = extremes_of(wind_ref)
     most_ref[...] = jnp.zeros_like(most_ref)
     most_ref[0:2, :] = top
     most_ref[2:4, :] = low
-    cut_edges(level_ref, *refs[:-1])
-
-
-def speed_kernel(speed_step, s_ref, *refs):
-    if len(refs) == 1:
-        part_ref = refs[0]
-    else:
-        wind_ref, other_ref, part_ref, most_ref = refs
-        top, low = extremes_of(wind_ref)
-        most_ref[...] = other_ref[...]
-        most_ref[0:2, :] = jnp.maximum(top, other_ref[0:2, :])
-        most_ref[2:4, :] = jnp.maximum(low, other_ref[2:4, :])
-    planes, headings, speeds, width = s_ref.shape
-    gain_v = thrust_limit / (12.0 * speed_step)
-    cells = planes * headings
-    group = 8
-    s_rows = s_ref.reshape(cells * speeds, width)
-    part_rows = part_ref.reshape(cells * speeds, width)
-    groups = -(-cells // group)
-    wide = batches(groups, 2)
-
-    def step(n, carry):
-        for k in range(wide):
-            start = jnp.minimum((n * wide + k) * group, cells - group) * speeds
-            lines = [
-                s_rows[pl.ds(start + v, group, stride=speeds), :] for v in range(speeds)
-            ]
-            ends = [lines[0]] * rim + lines + [lines[-1]] * rim
-            for v, (mean, gap) in enumerate(row_terms(ends, speed_step)):
-                part_rows[pl.ds(start + v, group, stride=speeds), :] = gain_v * (
-                    gap - jnp.abs(mean)
-                )
-        return carry
-
-    lax.fori_loop(0, groups // wide, step, 0)
-
-
-def cross_kernel(split, speed_step, s_ref, part_ref, wind_ref, waves_ref, *rest):
+
+
+def opening_kernel(level_ref, wind_ref, x_near, *others):
+    put_extremes(wind_ref, x_near.at[x_near.shape[0] - 1])
+    cut_edges(level_ref, x_near, *others)
+
+
+def meeting_kernel(wind_ref, x_near, most_ref):
+    put_extremes(wind_ref, most_ref)
+    most_ref[...] = jnp.maximum(most_ref[...], x_near[x_near.shape[0] - 1])
+
+
+def free_kernel(split, speed_step, s_ref, wind_ref, waves_ref, *rest):
     planes, headings, speeds, width = s_ref.shape
     tile = (speeds, width)
     if split:
-        out_ref, extra_ref = rest
+        speed_ref, out_ref, extra_ref = rest
     else:
-        pk_ref, out_ref = rest
+        pk_ref, speed_ref, out_ref = rest
         peak = splat(pk_ref[1:2, :] * gain, tile)
     pace = speeds_of(tile, speed_step) * gain
+    gain_v = thrust_limit / (12.0 * speed_step)
     first = lax.axis_index("head") * headings
+    cells = planes * headings
+    s_rows = s_ref.reshape(cells * speeds, width)
+    speed_rows = speed_ref.reshape(cells * speeds, width)
     wide = batches(headings, 2)
+    group = 8
+
+    def along_speed(start, count, stride):
+        spots = [pl.ds(start * speeds + v, count, stride=stride * speeds) for v in range(speeds)]
+        lines = [s_rows[spot, :] for spot in spots]
+        ends = [lines[0]] * rim + lines + [lines[-1]] * rim
+        for spot, (mean, gap) in zip(spots, row_terms(ends, speed_step)):
+            speed_rows[spot, :] = gain_v * (gap - jnp.abs(mean))
 
     def step(n, carry):
         for k in range(wide):
@@ -187,18 +173,23 @@
             for i in range(planes):
                 mean, gap = tile_terms(s_ref[i, j], spacing)
                 flow = table + splat(wind_ref[i, 1:2, :] * gain, tile)
-                part = part_ref[i, j] + mean * flow
                 if split:
-                    out_ref[i, j] = part
+                    out_ref[i, j] = mean * flow
                     extra_ref[i, j] = gap
                 else:
-                    out_ref[i, j] = part + gap * peak
+                    out_ref[i, j] = mean * flow + gap * peak
+            for i in range(0, planes - group + 1, group):
+                along_speed(i * headings + j, group, headings)
         return carry
 
     lax.fori_loop(0, headings // wide, step, 0)
-
-
-def heading_kernel(heading_step, s_ref, part_ref, near_ref, far_ref, out_ref):
+    count = min(group, headings)
+    for i in range(planes // group * group, planes):
+        for j in range(0, headings, count):
+            along_speed(i * headings + min(j, headings - count), count, 1)
+
+
+def heading_kernel(heading_step, s_ref, speed_ref, part_ref, near_ref, far_ref, out_ref):
     planes, headings = s_ref.shape[:2]
     gain_t = turn_limit / (12.0 * heading_step)
     odd = odd_place("head")
@@ -212,7 +203,8 @@
             highs = [jnp.where(odd, far, near) for near, far in ghosts]
             cells = lows + [s_ref[i, j] for j in range(headings)] + highs
             for j, (mean, gap) in enumerate(row_terms(cells, heading_step)):
-                out_ref[i, j] = part_ref[i, j] + gain_t * (gap - jnp.abs(mean))
+                own = speed_ref[i, j] + part_ref[i, j]
+                out_ref[i, j] = own + gain_t * (gap - jnp.abs(mean))
         return carry
 
     lax.fori_loop(0, planes // wide, step, 0)
@@ -281,7 +273,7 @@
     time_step = splat(pk_ref[2:3, :], tile)
     pace = speeds_of(tile, speed_step) * gain
     first = lax.axis_index("head") * headings
-    wide = batches(headings, 3)
+    wide = batches(headings, 6)
 
     def step(n, carry):
         for w in range(wide):
@@ -342,10 +334,7 @@
     short = rim * headings
     middle = max(short + 1, rim * planes)
 
-    def edge_shapes(far_first):
-        x_shapes = [shape(middle + 1), shape(short)]
-        return x_shapes[:: -1 if far_first else 1] + [shape(middle)] * 2
-
+    edge_shapes = [shape(middle + 1), shape(short)] + [shape(middle)] * 2
     cells = math.prod(level_set.shape)
 
     def call(kernel, ins, outs, scratch=(), work=0):
@@ -372,48 +361,38 @@
             pairs = [(i, i ^ reach) for i in range(size)]
         return lax.ppermute(most, "gx", pairs)
 
+    edges = call(opening_kernel, [values, wind], edge_shapes)
     for section in (1, 2, 3):
         opening = section == 1
-        speed = functools.partial(speed_kernel, speed_step)
-        if opening:
-            *edges, most = call(opening_kernel, [values, wind], edge_shapes(True) + [shape()])
-            other = spread(most, 1)
         x_out, x_last, t_out, t_last = edges
-        if opening:
-            x_far = trade(x_last, "gx", 1)
-        else:
-            x_near = trade(x_out, "gx", 0)
+        x_near = trade(x_out, "gx", 0)
         t_near = trade(t_out, "head", 0)
         t_far = trade(t_last, "head", 1, True)
+        x_far = trade(x_last, "gx", 1)
+        free = functools.partial(free_kernel, opening, speed_step)
+        turning = functools.partial(heading_kernel, heading_step)
         if opening:
-            part, most = call(speed, [values, wind, other], [field, shape()])
+            (most,) = call(meeting_kernel, [wind, x_near], [shape()])
             other = spread(most, 2)
-            x_out, most = lax.optimization_barrier((x_out, most))
-            x_near = trade(x_out, "gx", 0)
-        else:
-            (part,) = call(speed, [values], [field])
-            x_far = trade(x_last, "gx", 1)
-        turning = functools.partial(heading_kernel, heading_step)
-        (part,) = call(turning, [values, part, t_near, t_far], [field])
-        if opening:
+            spun, part, extra = call(free, [values, wind, waves], [field] * 3, work=300)
             reach = 4
             while reach < size:
                 most = jnp.maximum(most, other)
+                most, part = lax.optimization_barrier((most, part))
                 other = spread(most, reach)
                 reach *= 2
-            part, x_far = lax.optimization_barrier((part, x_far))
         else:
+            spun, part = call(free, [values, wind, waves, pk], [field] * 2)
             part, x_near = lax.optimization_barrier((part, x_near))
-        cross = functools.partial(cross_kernel, opening, speed_step)
-        ins = [values, part, wind, waves] + ([] if opening else [pk])
-        part, *extra = call(cross, ins, [field] * (2 if opening else 1), work=1000)
+        (part,) = call(turning, [values, spun, part, t_near, t_far], [field], work=1000)
         last = functools.partial(section_kernel, section, bounds, heading_step, speed_step)
-        ins = ([] if opening else [level_set]) + [values, part, *extra, x_near, x_far]
+        ins = [values, part, extra] if opening else [level_set, values, part]
+        ins += [x_near, x_far]
         ins += [wind, waves, target_mask, target_depth]
         ins += [most, other] if opening else [pk]
         outs = [field]
         if section < 3:
-            outs += edge_shapes(False)
+            outs += edge_shapes
         if opening:
             outs += [shape()]
         rows = pltpu.VMEM((planes,) + tile, jnp.float32)

time: 48.2 us -> 43 us (0.89)
  the two profiles are of different devices: /device:TPU:1 before, /device:TPU:8 now
where the time goes in v6:
time: 43 us; the launch traced here: 42.4 us
  starting transfers between devices  18.8 us (44%)
  Pallas kernels  14.7 us (34%)
  waiting for transfers between devices  6.94 us (16%)
  local copies, waits for them, and re-layouts  1.74 us (4%)
    ppermute x12, starting transfers between devices, trade(): return lax.ppermute(value, axis, pairs + [(j, i) for i, j in pairs])  15.9 us
    pallas_call x11, Pallas kernels, call(): pl.pallas_call(kernel, out_shape=outs, in_specs=[vmem] * len(ins), out_sp...  14.7 us
    ppermute x12, waiting for transfers between devices, trade(): return lax.ppermute(value, axis, pairs + [(j, i) for i, j in pairs])  5.28 us
    ppermute x2, starting transfers between devices, spread(): return lax.ppermute(most, 'gx', pairs)  2.88 us
    unnamed x14, local copies, waits for them, and re-layouts  1.74 us
    ppermute x2, waiting for transfers between devices, spread(): return lax.ppermute(most, 'gx', pairs)  1.66 us
  transfers between devices with their start and end apart: 14, of which 5 were waited for; matrix products, arithmetic and copies ran while one was open for 0% of the time, Pallas kernels for 25%

profile of v6, /device:TPU:8, one launch (start us, length us, event | category | flops | bytes accessed | tf_op | source)
XLA Modules:
  0.0 42.4 jit_solution(10809358156503217698)
XLA Ops:
  0.0 0.0 copy-start
  0.0 1.0 %copy-done = f32[9,12,8,128]{3,2,1,0:T(8,128)S(1)} copy-done((f32[9,12,8,128]{3,2,1,0:T(8,128)S(1)}, f32[9,12,8,128]{3,2,1,0:T(8,128)}, u32[]{:S(2)}) %copy-start) | copy-done | bytes 442392
  1.0 0.0 copy-start.3
  1.0 0.7 %copy-done.3 = f32[2,9,128]{2,0,1:T(2,128)S(1)} copy-done((f32[2,9,128]{2,0,1:T(2,128)S(1)}, f32[2,9,128]{2,0,1:T(2,128)}, u32[]{:S(2)}) %copy-start.3) | copy-done | bytes 9240
  1.7 0.0 copy-start.1
  1.8 1.6 %collective-permute-start = (f32[38,8,128]{2,1,0:T(8,128)S(1)}, f32[38,8,128]{2,1,0:T(8,128)S(1)}, u32[]{:S(2)}, u32[]{:S(2)}) collective-permute-start(f32[38,8,128]{2,1,0:T(8,128)S(1)} %get-tuple-element.34), channel_id=1, source_target_pairs={{0,1},{2,3},{4,5},{6,7},{1,0},{3,2},{5,4},{7,6},{8,9},{10,11},{12,... | collective-permute-start | bytes 466952 | tf_op jit(solution)/shard_map/ppermute | solution.py:308
  3.4 0.0 collective-permute-start.2
  3.4 1.6 %collective-permute-start.3 = (f32[37,8,128]{2,1,0:T(8,128)S(1)}, f32[37,8,128]{2,1,0:T(8,128)S(1)}, u32[]{:S(2)}, u32[]{:S(2)}) collective-permute-start(f32[37,8,128]{2,1,0:T(8,128)S(1)} %get-tuple-element.38), channel_id=1, source_target_pairs={{8,16},{24,0},{16,8},{0,24},{9,17},{25,1},{17,9},{1,25},{10,18},{2... | collective-permute-start | bytes 454664 | tf_op jit(solution)/shard_map/ppermute | solution.py:308
  5.0 0.0 copy-start.2
  5.0 2.4 %collective-permute-start.4 = (f32[36,8,128]{2,1,0:T(8,128)S(1)}, f32[36,8,128]{2,1,0:T(8,128)S(1)}, u32[]{:S(2)}, u32[]{:S(2)}) collective-permute-start(f32[36,8,128]{2,1,0:T(8,128)S(1)} %get-tuple-element.40), channel_id=1, source_target_pairs={{1,2},{3,4},{5,6},{2,1},{4,3},{6,5},{9,10},{11,12},{13,14},{10,9},... | collective-permute-start | bytes 442376 | tf_op jit(solution)/shard_map/ppermute | solution.py:308
  7.4 0.2 collective-permute-done.x_near.refs_3_
  7.6 0.3 collective-permute-start.1
  7.9 0.0 copy-done.1
  7.9 0.0 copy-done.2
  7.9 2.7 %shard_map.55 = (f32[9,12,8,128]{3,2,1,0:T(8,128)S(1)}, f32[9,12,8,128]{3,2,1,0:T(8,128)S(1)}, f32[9,12,8,128]{3,2,1,0:T(8,128)S(1)}) custom-call(f32[9,12,8,128]{3,2,1,0:T(8,128)S(1)} %copy-done.1, f32[9,2,128]{2,1,0:T(2,128)S(1)} %bitcast.3, f32[2,48,128]{2,1,0:T(8,128)S(1)} %copy-done.2), custom_call_target="tpu_custom_call" | custom-call | flops 33177600 | bytes 33177600 | tf_op jit(solution)/shard_map/pallas_call | solution.py:341
  10.6 0.6 %collective-permute-done.1 = f32[8,128]{1,0:T(8,128)S(1)} collective-permute-done((f32[8,128]{1,0:T(8,128)S(1)}, f32[8,128]{1,0:T(8,128)S(1)}, u32[]{:S(2)}, u32[]{:S(2)}) %collective-permute-start.1) | collective-permute-done | bytes 4128 | tf_op jit(solution)/shard_map/ppermute | solution.py:362
  11.3 2.6 %collective-permute-start.5 = (f32[8,128]{1,0:T(8,128)S(1)}, f32[8,128]{1,0:T(8,128)S(1)}, u32[]{:S(2)}, u32[]{:S(2)}) collective-permute-start(f32[8,128]{1,0:T(8,128)S(1)} %max.3.refs_9_), channel_id=1, source_target_pairs={{0,4},{1,5},{2,6},{3,7},{4,0},{5,1},{6,2},{7,3},{8,12},{9,13},{10,... | collective-permute-start | bytes 12296 | tf_op jit(solution)/shard_map/ppermute | solution.py:362
  13.9 0.0 collective-permute-done.2.near_ref
  13.9 0.0 collective-permute-done.3.far_ref
  13.9 0.0 copy-start.4
  13.9 0.0 copy-start.5
  13.9 0.0 copy-start.6
  13.9 0.9 %shard_map.58.refs_1_ = f32[9,12,8,128]{3,2,1,0:T(8,128)S(1)} custom-call(f32[9,12,8,128]{3,2,1,0:T(8,128)S(1)} %copy-done.1, f32[9,12,8,128]{3,2,1,0:T(8,128)S(1)} %get-tuple-element.33.speed_ref, f32[9,12,8,128]{3,2,1,0:T(8,128)S(1)} %get-tuple-element.36.part_ref, f32[37,8,128]{2,1,0:T(8,128)S(1)} %collective-permute-done.2.near_ref, ...), custom_call_target="tpu_custom_call" | custom-call | flops 110592000 | bytes 110592000 | tf_op jit(solution)/shard_map/pallas_call | solution.py:341
  14.8 0.0 collective-permute-done.4.refs_4_
  14.8 1.0 %collective-permute-done.5.refs_10_ = f32[8,128]{1,0:T(8,128)S(1)} collective-permute-done((f32[8,128]{1,0:T(8,128)S(1)}, f32[8,128]{1,0:T(8,128)S(1)}, u32[]{:S(2)}, u32[]{:S(2)}) %collective-permute-start.5) | collective-permute-done | bytes 4128 | tf_op jit(solution)/shard_map/ppermute | solution.py:362
  15.8 0.0 copy-done.4
  15.8 0.0 copy-done.5
  15.8 0.0 copy-done.6
  15.8 1.2 %shard_map.59 = (f32[9,12,8,128]{3,2,1,0:T(8,128)S(1)}, f32[38,8,128]{2,1,0:T(8,128)S(1)}, f32[36,8,128]{2,1,0:T(8,128)S(1)}, f32[37,8,128]{2,1,0:T(8,128)S(1)},...) custom-call(f32[9,12,8,128]{3,2,1,0:T(8,128)S(1)} %copy-done.1, f32[9,12,8,128]{3,2,1,0:T(8,128)S(1)} %shard_map.58.refs_1_, ...), custom_call_target="tpu_custom_call" | custom-call | tf_op jit(solution)/shard_map/pallas_call | solution.py:341
  17.0 3.1 %collective-permute-start.6 = (f32[38,8,128]{2,1,0:T(8,128)S(1)}, f32[38,8,128]{2,1,0:T(8,128)S(1)}, u32[]{:S(2)}, u32[]{:S(2)}) collective-permute-start(f32[38,8,128]{2,1,0:T(8,128)S(1)} %get-tuple-element.46), channel_id=1, source_target_pairs={{0,1},{2,3},{4,5},{6,7},{1,0},{3,2},{5,4},{7,6},{8,9},{10,11},{12,... | collective-permute-start | bytes 466952 | tf_op jit(solution)/shard_map/ppermute | solution.py:308
  20.0 0.0 collective-permute-start.7
  20.0 0.6 %collective-permute-start.8 = (f32[37,8,128]{2,1,0:T(8,128)S(1)}, f32[37,8,128]{2,1,0:T(8,128)S(1)}, u32[]{:S(2)}, u32[]{:S(2)}) collective-permute-start(f32[37,8,128]{2,1,0:T(8,128)S(1)} %get-tuple-element.49), channel_id=1, source_target_pairs={{8,16},{24,0},{16,8},{0,24},{9,17},{25,1},{17,9},{1,25},{10,18},{2... | collective-permute-start | bytes 454664 | tf_op jit(solution)/shard_map/ppermute | solution.py:308
  20.7 2.6 %collective-permute-start.9 = (f32[36,8,128]{2,1,0:T(8,128)S(1)}, f32[36,8,128]{2,1,0:T(8,128)S(1)}, u32[]{:S(2)}, u32[]{:S(2)}) collective-permute-start(f32[36,8,128]{2,1,0:T(8,128)S(1)} %get-tuple-element.51), channel_id=1, source_target_pairs={{1,2},{3,4},{5,6},{2,1},{4,3},{6,5},{9,10},{11,12},{13,14},{10,9},... | collective-permute-start | bytes 442376 | tf_op jit(solution)/shard_map/ppermute | solution.py:308
  23.3 2.7 %shard_map.60 = (f32[9,12,8,128]{3,2,1,0:T(8,128)S(1)}, f32[9,12,8,128]{3,2,1,0:T(8,128)S(1)}) custom-call(f32[9,12,8,128]{3,2,1,0:T(8,128)S(1)} %get-tuple-element.42.s_ref.refs_1_, f32[9,2,128]{2,1,0:T(2,128)S(1)} %bitcast.5, f32[2,48,128]{2,1,0:T(8,128)S(1)} %copy-done.2, f32[8,128]{1,0:T(8,128)S(1)} %get-tuple-element.43.rest_0_.refs_9_), custom_call_target="tpu_custom_call" | custom-call | tf_op jit(solution)/shard_map/pallas_call | solution.py:341
  26.0 0.0 collective-permute-done.6.refs_3_
  26.0 0.0 collective-permute-done.7.near_ref
  26.0 0.0 collective-permute-done.8.far_ref
  26.0 0.9 %shard_map.61.refs_2_ = f32[9,12,8,128]{3,2,1,0:T(8,128)S(1)} custom-call(f32[9,12,8,128]{3,2,1,0:T(8,128)S(1)} %get-tuple-element.42.s_ref.refs_1_, f32[9,12,8,128]{3,2,1,0:T(8,128)S(1)} %get-tuple-element.44.speed_ref, f32[9,12,8,128]{3,2,1,0:T(8,128)S(1)} %get-tuple-element.47.part_ref, f32[37,8,128]{2,1,0:T(8,128)S(1)} %collective-permute-done.7.near_ref, ...), custom_call_target="tpu_custom_call" | custom-call | flops 110592000 | bytes 110592000 | tf_op jit(solution)/shard_map/pallas_call | solution.py:341
  26.9 2.4 %collective-permute-done.9.refs_4_ = f32[36,8,128]{2,1,0:T(8,128)S(1)} collective-permute-done((f32[36,8,128]{2,1,0:T(8,128)S(1)}, f32[36,8,128]{2,1,0:T(8,128)S(1)}, u32[]{:S(2)}, u32[]{:S(2)}) %collective-permute-start.9) | collective-permute-done | bytes 147488 | tf_op jit(solution)/shard_map/ppermute | solution.py:308
  29.2 1.0 %shard_map.62 = (f32[9,12,8,128]{3,2,1,0:T(8,128)S(1)}, f32[38,8,128]{2,1,0:T(8,128)S(1)}, f32[36,8,128]{2,1,0:T(8,128)S(1)}, f32[37,8,128]{2,1,0:T(8,128)S(1)}, f32[37,8,128]{2,1,0:T(8,128)S(1)}) custom-call(f32[9,12,8,128]{3,2,1,0:T(8,128)S(1)} %copy-done.1, f32[9,12,8,128]{3,2,1,0:T(8,128)S(1)} %get-tuple-element.42.s_ref.refs_1_, ...), custom_call_target="tpu_custom_call" | custom-call | tf_op jit(solution)/shard_map/pallas_call | solution.py:341
  30.3 0.7 %collective-permute-start.10 = (f32[38,8,128]{2,1,0:T(8,128)S(1)}, f32[38,8,128]{2,1,0:T(8,128)S(1)}, u32[]{:S(2)}, u32[]{:S(2)}) collective-permute-start(f32[38,8,128]{2,1,0:T(8,128)S(1)} %get-tuple-element.55), channel_id=1, source_target_pairs={{0,1},{2,3},{4,5},{6,7},{1,0},{3,2},{5,4},{7,6},{8,9},{10,11},{12,... | collective-permute-start | bytes 466952 | tf_op jit(solution)/shard_map/ppermute | solution.py:308
  31.0 0.0 collective-permute-start.11
  31.0 1.1 %collective-permute-start.12 = (f32[37,8,128]{2,1,0:T(8,128)S(1)}, f32[37,8,128]{2,1,0:T(8,128)S(1)}, u32[]{:S(2)}, u32[]{:S(2)}) collective-permute-start(f32[37,8,128]{2,1,0:T(8,128)S(1)} %get-tuple-element.58), channel_id=1, source_target_pairs={{8,16},{24,0},{16,8},{0,24},{9,17},{25,1},{17,9},{1,25},{10,18},{2... | collective-permute-start | bytes 454664 | tf_op jit(solution)/shard_map/ppermute | solution.py:308
  32.1 2.2 %collective-permute-start.13 = (f32[36,8,128]{2,1,0:T(8,128)S(1)}, f32[36,8,128]{2,1,0:T(8,128)S(1)}, u32[]{:S(2)}, u32[]{:S(2)}) collective-permute-start(f32[36,8,128]{2,1,0:T(8,128)S(1)} %get-tuple-element.60), channel_id=1, source_target_pairs={{1,2},{3,4},{5,6},{2,1},{4,3},{6,5},{9,10},{11,12},{13,14},{10,9},... | collective-permute-start | bytes 442376 | tf_op jit(solution)/shard_map/ppermute | solution.py:308
  34.3 2.7 %shard_map.63 = (f32[9,12,8,128]{3,2,1,0:T(8,128)S(1)}, f32[9,12,8,128]{3,2,1,0:T(8,128)S(1)}) custom-call(f32[9,12,8,128]{3,2,1,0:T(8,128)S(1)} %get-tuple-element.52.s_ref.refs_1_, f32[9,2,128]{2,1,0:T(2,128)S(1)} %bitcast.7, f32[2,48,128]{2,1,0:T(8,128)S(1)} %copy-done.2, f32[8,128]{1,0:T(8,128)S(1)} %get-tuple-element.43.rest_0_.refs_9_), custom_call_target="tpu_custom_call" | custom-call | tf_op jit(solution)/shard_map/pallas_call | solution.py:341
  37.0 0.0 collective-permute-done.10.refs_3_
  37.1 0.0 collective-permute-done.11.near_ref
  37.1 0.0 collective-permute-done.12.far_ref
  37.1 0.9 %shard_map.64.refs_2_ = f32[9,12,8,128]{3,2,1,0:T(8,128)S(1)} custom-call(f32[9,12,8,128]{3,2,1,0:T(8,128)S(1)} %get-tuple-element.52.s_ref.refs_1_, f32[9,12,8,128]{3,2,1,0:T(8,128)S(1)} %get-tuple-element.53.speed_ref, f32[9,12,8,128]{3,2,1,0:T(8,128)S(1)} %get-tuple-element.56.part_ref, f32[37,8,128]{2,1,0:T(8,128)S(1)} %collective-permute-done.11.near_ref, ...), custom_call_target="tpu_custom_call" | custom-call | flops 110592000 | bytes 110592000 | tf_op jit(solution)/shard_map/pallas_call | solution.py:341
  37.9 2.7 %collective-permute-done.13.refs_4_ = f32[36,8,128]{2,1,0:T(8,128)S(1)} collective-permute-done((f32[36,8,128]{2,1,0:T(8,128)S(1)}, f32[36,8,128]{2,1,0:T(8,128)S(1)}, u32[]{:S(2)}, u32[]{:S(2)}) %collective-permute-start.13) | collective-permute-done | bytes 147488 | tf_op jit(solution)/shard_map/ppermute | solution.py:308
  40.6 1.7 %shard_map.65 = f32[9,12,8,128]{3,2,1,0:T(8,128)} custom-call(f32[9,12,8,128]{3,2,1,0:T(8,128)S(1)} %copy-done.1, f32[9,12,8,128]{3,2,1,0:T(8,128)S(1)} %get-tuple-element.52.s_ref.refs_1_, f32[9,12,8,128]{3,2,1,0:T(8,128)S(1)} %shard_map.64.refs_2_, f32[38,8,128]{2,1,0:T(8,128)S(1)} %collective-permute-done.10.refs_3_, ...), custom_call_target="tpu_custom_call" | custom-call | tf_op jit(solution)/shard_map/pallas_call | solution.py:341
  (3 shorter events, 0.1 us)
Async XLA Ops:
  0.0 1.0 %copy-start = (f32[9,12,8,128]{3,2,1,0:T(8,128)S(1)}, f32[9,12,8,128]{3,2,1,0:T(8,128)}, u32[]{:S(2)}) copy-start(f32[9,12,8,128]{3,2,1,0:T(8,128)} %refs_0_.5) | copy-start | bytes 1327108
  1.0 0.7 %copy-start.3 = (f32[2,9,128]{2,0,1:T(2,128)S(1)}, f32[2,9,128]{2,0,1:T(2,128)}, u32[]{:S(2)}) copy-start(f32[2,9,128]{2,0,1:T(2,128)} %param.6) | copy-start | bytes 27652
  1.7 6.2 %copy-start.1 = (f32[9,12,8,128]{3,2,1,0:T(8,128)S(1)}, f32[9,12,8,128]{3,2,1,0:T(8,128)}, u32[]{:S(2)}) copy-start(f32[9,12,8,128]{3,2,1,0:T(8,128)} %refs_0_.5) | copy-start | bytes 1327108
  1.8 5.8 %collective-permute-start = (f32[38,8,128]{2,1,0:T(8,128)S(1)}, f32[38,8,128]{2,1,0:T(8,128)S(1)}, u32[]{:S(2)}, u32[]{:S(2)}) collective-permute-start(f32[38,8,128]{2,1,0:T(8,128)S(1)} %get-tuple-element.34), channel_id=1, source_target_pairs={{0,1},{2,3},{4,5},{6,7},{1,0},{3,2},{5,4},{7,6},{8,9},{10,11},{12,... | collective-permute-start | bytes 466952 | tf_op jit(solution)/shard_map/ppermute | solution.py:308
  3.4 10.5 %collective-permute-start.2 = (f32[37,8,128]{2,1,0:T(8,128)S(1)}, f32[37,8,128]{2,1,0:T(8,128)S(1)}, u32[]{:S(2)}, u32[]{:S(2)}) collective-permute-start(f32[37,8,128]{2,1,0:T(8,128)S(1)} %get-tuple-element.37), channel_id=1, source_target_pairs={{0,8},{16,24},{8,0},{24,16},{1,9},{17,25},{9,1},{25,17},{2,10},{18... | collective-permute-start | bytes 454664 | tf_op jit(solution)/shard_map/ppermute | solution.py:308
  3.4 10.5 %collective-permute-start.3 = (f32[37,8,128]{2,1,0:T(8,128)S(1)}, f32[37,8,128]{2,1,0:T(8,128)S(1)}, u32[]{:S(2)}, u32[]{:S(2)}) collective-permute-start(f32[37,8,128]{2,1,0:T(8,128)S(1)} %get-tuple-element.38), channel_id=1, source_target_pairs={{8,16},{24,0},{16,8},{0,24},{9,17},{25,1},{17,9},{1,25},{10,18},{2... | collective-permute-start | bytes 454664 | tf_op jit(solution)/shard_map/ppermute | solution.py:308
  5.0 3.0 %copy-start.2 = (f32[2,48,128]{2,1,0:T(8,128)S(1)}, f32[2,48,128]{2,1,0:T(8,128)}, u32[]{:S(2)}) copy-start(f32[2,48,128]{2,1,0:T(8,128)} %constant.2.clone.waves_ref.refs_6_) | copy-start | bytes 147460
  5.0 9.8 %collective-permute-start.4 = (f32[36,8,128]{2,1,0:T(8,128)S(1)}, f32[36,8,128]{2,1,0:T(8,128)S(1)}, u32[]{:S(2)}, u32[]{:S(2)}) collective-permute-start(f32[36,8,128]{2,1,0:T(8,128)S(1)} %get-tuple-element.40), channel_id=1, source_target_pairs={{1,2},{3,4},{5,6},{2,1},{4,3},{6,5},{9,10},{11,12},{13,14},{10,9},... | collective-permute-start | bytes 442376 | tf_op jit(solution)/shard_map/ppermute | solution.py:308
  7.6 3.7 %collective-permute-start.1 = (f32[8,128]{1,0:T(8,128)S(1)}, f32[8,128]{1,0:T(8,128)S(1)}, u32[]{:S(2)}, u32[]{:S(2)}) collective-permute-start(f32[8,128]{1,0:T(8,128)S(1)} %shard_map.57), channel_id=1, source_target_pairs={{0,2},{1,3},{2,0},{3,1},{4,6},{5,7},{6,4},{7,5},{8,10},{9,11},{10,... | collective-permute-start | bytes 12296 | tf_op jit(solution)/shard_map/ppermute | solution.py:362
  11.3 4.5 %collective-permute-start.5 = (f32[8,128]{1,0:T(8,128)S(1)}, f32[8,128]{1,0:T(8,128)S(1)}, u32[]{:S(2)}, u32[]{:S(2)}) collective-permute-start(f32[8,128]{1,0:T(8,128)S(1)} %max.3.refs_9_), channel_id=1, source_target_pairs={{0,4},{1,5},{2,6},{3,7},{4,0},{5,1},{6,2},{7,3},{8,12},{9,13},{10,... | collective-permute-start | bytes 12296 | tf_op jit(solution)/shard_map/ppermute | solution.py:362
  13.9 1.9 %copy-start.4 = (f32[2,9,128]{2,0,1:T(2,128)S(1)}, f32[2,9,128]{2,0,1:T(2,128)}, u32[]{:S(2)}) copy-start(f32[2,9,128]{2,0,1:T(2,128)} %param.6) | copy-start | bytes 27652
  13.9 1.9 %copy-start.5 = (s32[9,128]{1,0:T(8,128)S(1)}, s32[9,128]{1,0:T(8,128)}, u32[]{:S(2)}) copy-start(s32[9,128]{1,0:T(8,128)} %refs_7_.5) | copy-start | bytes 13828
  13.9 1.9 %copy-start.6 = (f32[9,128]{1,0:T(8,128)S(1)}, f32[9,128]{1,0:T(8,128)}, u32[]{:S(2)}) copy-start(f32[9,128]{1,0:T(8,128)} %refs_8_.5) | copy-start | bytes 13828
  17.0 9.0 %collective-permute-start.6 = (f32[38,8,128]{2,1,0:T(8,128)S(1)}, f32[38,8,128]{2,1,0:T(8,128)S(1)}, u32[]{:S(2)}, u32[]{:S(2)}) collective-permute-start(f32[38,8,128]{2,1,0:T(8,128)S(1)} %get-tuple-element.46), channel_id=1, source_target_pairs={{0,1},{2,3},{4,5},{6,7},{1,0},{3,2},{5,4},{7,6},{8,9},{10,11},{12,... | collective-permute-start | bytes 466952 | tf_op jit(solution)/shard_map/ppermute | solution.py:308
  20.0 5.9 %collective-permute-start.7 = (f32[37,8,128]{2,1,0:T(8,128)S(1)}, f32[37,8,128]{2,1,0:T(8,128)S(1)}, u32[]{:S(2)}, u32[]{:S(2)}) collective-permute-start(f32[37,8,128]{2,1,0:T(8,128)S(1)} %get-tuple-element.48), channel_id=1, source_target_pairs={{0,8},{16,24},{8,0},{24,16},{1,9},{17,25},{9,1},{25,17},{2,10},{18... | collective-permute-start | bytes 454664 | tf_op jit(solution)/shard_map/ppermute | solution.py:308
  20.0 6.0 %collective-permute-start.8 = (f32[37,8,128]{2,1,0:T(8,128)S(1)}, f32[37,8,128]{2,1,0:T(8,128)S(1)}, u32[]{:S(2)}, u32[]{:S(2)}) collective-permute-start(f32[37,8,128]{2,1,0:T(8,128)S(1)} %get-tuple-element.49), channel_id=1, source_target_pairs={{8,16},{24,0},{16,8},{0,24},{9,17},{25,1},{17,9},{1,25},{10,18},{2... | collective-permute-start | bytes 454664 | tf_op jit(solution)/shard_map/ppermute | solution.py:308
  20.7 8.5 %collective-permute-start.9 = (f32[36,8,128]{2,1,0:T(8,128)S(1)}, f32[36,8,128]{2,1,0:T(8,128)S(1)}, u32[]{:S(2)}, u32[]{:S(2)}) collective-permute-start(f32[36,8,128]{2,1,0:T(8,128)S(1)} %get-tuple-element.51), channel_id=1, source_target_pairs={{1,2},{3,4},{5,6},{2,1},{4,3},{6,5},{9,10},{11,12},{13,14},{10,9},... | collective-permute-start | bytes 442376 | tf_op jit(solution)/shard_map/ppermute | solution.py:308
  30.3 6.8 %collective-permute-start.10 = (f32[38,8,128]{2,1,0:T(8,128)S(1)}, f32[38,8,128]{2,1,0:T(8,128)S(1)}, u32[]{:S(2)}, u32[]{:S(2)}) collective-permute-start(f32[38,8,128]{2,1,0:T(8,128)S(1)} %get-tuple-element.55), channel_id=1, source_target_pairs={{0,1},{2,3},{4,5},{6,7},{1,0},{3,2},{5,4},{7,6},{8,9},{10,11},{12,... | collective-permute-start | bytes 466952 | tf_op jit(solution)/shard_map/ppermute | solution.py:308
  31.0 6.1 %collective-permute-start.11 = (f32[37,8,128]{2,1,0:T(8,128)S(1)}, f32[37,8,128]{2,1,0:T(8,128)S(1)}, u32[]{:S(2)}, u32[]{:S(2)}) collective-permute-start(f32[37,8,128]{2,1,0:T(8,128)S(1)} %get-tuple-element.57), channel_id=1, source_target_pairs={{0,8},{16,24},{8,0},{24,16},{1,9},{17,25},{9,1},{25,17},{2,10},{18... | collective-permute-start | bytes 454664 | tf_op jit(solution)/shard_map/ppermute | solution.py:308
  31.0 6.1 %collective-permute-start.12 = (f32[37,8,128]{2,1,0:T(8,128)S(1)}, f32[37,8,128]{2,1,0:T(8,128)S(1)}, u32[]{:S(2)}, u32[]{:S(2)}) collective-permute-start(f32[37,8,128]{2,1,0:T(8,128)S(1)} %get-tuple-element.58), channel_id=1, source_target_pairs={{8,16},{24,0},{16,8},{0,24},{9,17},{25,1},{17,9},{1,25},{10,18},{2... | collective-permute-start | bytes 454664 | tf_op jit(solution)/shard_map/ppermute | solution.py:308
  32.1 8.5 %collective-permute-start.13 = (f32[36,8,128]{2,1,0:T(8,128)S(1)}, f32[36,8,128]{2,1,0:T(8,128)S(1)}, u32[]{:S(2)}, u32[]{:S(2)}) collective-permute-start(f32[36,8,128]{2,1,0:T(8,128)S(1)} %get-tuple-element.60), channel_id=1, source_target_pairs={{1,2},{3,4},{5,6},{2,1},{4,3},{6,5},{9,10},{11,12},{13,14},{10,9},... | collective-permute-start | bytes 442376 | tf_op jit(solution)/shard_map/ppermute | solution.py:308

commit v7 on v6

--- a/solution.py
+++ b/solution.py
@@ -120,16 +120,11 @@
     return lax.rem(lax.axis_index(axis), 2) == 1
 
 
-def extremes_of(wind_ref):
+def put_extremes(wind_ref, most_ref):
     rows = [wind_ref[i] for i in range(wind_ref.shape[0])]
-    return functools.reduce(jnp.maximum, rows), -functools.reduce(jnp.minimum, rows)
-
-
-def put_extremes(wind_ref, most_ref):
-    top, low = extremes_of(wind_ref)
     most_ref[...] = jnp.zeros_like(most_ref)
-    most_ref[0:2, :] = top
-    most_ref[2:4, :] = low
+    most_ref[0:2, :] = functools.reduce(jnp.maximum, rows)
+    most_ref[2:4, :] = -functools.reduce(jnp.minimum, rows)
 
 
 def opening_kernel(level_ref, wind_ref, x_near, *others):
@@ -239,41 +234,23 @@
             t_far[i * rim + k] = field_ref[i, headings - rim - t_low + k]
 
 
-def section_kernel(section, bounds, heading_step, speed_step, *refs):
-    refs = list(refs)
-    base_ref = None if section == 1 else refs.pop(0)
-    s_ref, part_ref = refs.pop(0), refs.pop(0)
-    extra_ref = refs.pop(0) if section == 1 else None
-    near_ref, far_ref = refs.pop(0), refs.pop(0)
-    wind_ref, waves_ref, mask_ref, depth_ref = (refs.pop(0) for _ in range(4))
-    if section == 1:
-        most_refs = [refs.pop(0), refs.pop(0)]
-    else:
-        pk_ref = refs.pop(0)
-    out_ref = refs.pop(0)
-    if section < 3:
-        edge_refs = [refs.pop(0) for _ in range(4)]
-    if section == 1:
-        pk_ref = refs.pop(0)
-    flow_ref, target_ref = refs
+def splat_targets(mask_ref, depth_ref, target_ref):
+    for i in range(target_ref.shape[0]):
+        depth = depth_ref[i : i + 1, :]
+        target = jnp.where(mask_ref[i : i + 1, :] == 1, -depth, depth)
+        target_ref[i] = splat(target, target_ref.shape[1:])
+
+
+def across_planes(wide, speed_step, s_ref, near_ref, far_ref, wind_ref, waves_ref, flow_ref, use):
     planes, headings = s_ref.shape[:2]
     tile = s_ref.shape[2:]
-    if section == 1:
-        most = jnp.maximum(most_refs[0][...], most_refs[1][...])
-        peaks_into(pk_ref, most, bounds, heading_step, speed_step)
     for i in range(planes):
-        depth = depth_ref[i : i + 1, :]
-        target_ref[i] = splat(jnp.where(mask_ref[i : i + 1, :] == 1, -depth, depth), tile)
         flow_ref[i] = splat(wind_ref[i, 0:1, :] * gain, tile)
     odd = odd_place("gx")
     at_low = lax.axis_index("gx") == 0
     at_high = lax.axis_index("gx") == lax.axis_size("gx") - 1
-    peak_x = splat(pk_ref[0:1, :] * gain, tile)
-    peak_y = splat(pk_ref[1:2, :] * gain, tile)
-    time_step = splat(pk_ref[2:3, :], tile)
     pace = speeds_of(tile, speed_step) * gain
     first = lax.axis_index("head") * headings
-    wide = batches(headings, 6)
 
     def step(n, carry):
         for w in range(wide):
@@ -284,19 +261,70 @@
             highs = [jnp.where(at_high, cells[-1], jnp.where(odd, far, near)) for near, far in ghosts]
             table = splat(waves_ref[0, pl.ds(first + j, 1), :], tile) * pace
             for i, (mean, gap) in enumerate(row_terms(lows + cells + highs, spacing)):
-                rate = part_ref[i, j] + (mean * (table + flow_ref[i]) + gap * peak_x)
-                if section == 1:
-                    rate = rate + extra_ref[i, j] * peak_y
-                moved = cells[i] + time_step * rate
-                if section == 2:
-                    moved = 0.75 * base_ref[i, j] + 0.25 * moved
-                if section == 3:
-                    moved = (1.0 / 3.0) * base_ref[i, j] + (2.0 / 3.0) * moved
-                out_ref[i, j] = jnp.minimum(moved, target_ref[i])
+                use(i, j, mean * (table + flow_ref[i]), gap, cells[i])
         return carry
 
     lax.fori_loop(0, headings // wide, step, 0)
-    if section < 3:
+
+
+def first_kernel(
+    speed_step, s_ref, part_ref, near_ref, far_ref, wind_ref, waves_ref, out_ref, gap_ref, flow_ref
+):
+    def use(i, j, drift, gap, cell):
+        out_ref[i, j] = part_ref[i, j] + drift
+        gap_ref[i, j] = gap
+
+    wide = batches(s_ref.shape[1], 6)
+    across_planes(
+        wide, speed_step, s_ref, near_ref, far_ref, wind_ref, waves_ref, flow_ref, use
+    )
+
+
+def closing_kernel(
+    bounds, heading_step, speed_step, s_ref, part_ref, gap_x_ref, gap_y_ref, mask_ref, depth_ref,
+    most_ref, other_ref, out_ref, x_near, x_far, t_near, t_far, pk_ref, target_ref
+):
+    planes, headings = s_ref.shape[:2]
+    tile = s_ref.shape[2:]
+    most = jnp.maximum(most_ref[...], other_ref[...])
+    peaks_into(pk_ref, most, bounds, heading_step, speed_step)
+    splat_targets(mask_ref, depth_ref, target_ref)
+    peak_x = splat(pk_ref[0:1, :] * gain, tile)
+    peak_y = splat(pk_ref[1:2, :] * gain, tile)
+    time_step = splat(pk_ref[2:3, :], tile)
+
+    def plane(i, carry):
+        for j in range(headings):
+            rate = part_ref[i, j] + (gap_x_ref[i, j] * peak_x + gap_y_ref[i, j] * peak_y)
+            out_ref[i, j] = jnp.minimum(s_ref[i, j] + time_step * rate, target_ref[i])
+        return carry
+
+    lax.fori_loop(0, planes, plane, 0)
+    cut_edges(out_ref, x_near, x_far, t_near, t_far)
+
+
+def section_kernel(
+    section, speed_step, base_ref, s_ref, part_ref, near_ref, far_ref, wind_ref, waves_ref,
+    mask_ref, depth_ref, pk_ref, out_ref, *refs
+):
+    edge_refs, (flow_ref, target_ref) = refs[:-2], refs[-2:]
+    tile = s_ref.shape[2:]
+    splat_targets(mask_ref, depth_ref, target_ref)
+    peak_x = splat(pk_ref[0:1, :] * gain, tile)
+    time_step = splat(pk_ref[2:3, :], tile)
+    base_share = 0.75 if section == 2 else 1.0 / 3.0
+    own_share = 0.25 if section == 2 else 2.0 / 3.0
+
+    def use(i, j, drift, gap, cell):
+        rate = part_ref[i, j] + (drift + gap * peak_x)
+        moved = base_share * base_ref[i, j] + own_share * (cell + time_step * rate)
+        out_ref[i, j] = jnp.minimum(moved, target_ref[i])
+
+    wide = batches(s_ref.shape[1], 6)
+    across_planes(
+        wide, speed_step, s_ref, near_ref, far_ref, wind_ref, waves_ref, flow_ref, use
+    )
+    if section == 2:
         cut_edges(out_ref, *edge_refs)
 
 
@@ -305,7 +333,9 @@
     pairs = [(i, i + 1) for i in range(reach, size - 1, 2)]
     if wrap and reach and size % 2 == 0:
         pairs.append((size - 1, 0))
-    return lax.ppermute(value, axis, pairs + [(j, i) for i, j in pairs])
+    pairs += [(j, i) for i, j in pairs]
+    pairs += [(i, i) for i in range(size) if i not in dict(pairs)]
+    return lax.ppermute(value, axis, pairs)
 
 
 def local(level_set, wind_field, target_mask, target_depth):
@@ -335,6 +365,7 @@
     middle = max(short + 1, rim * planes)
 
     edge_shapes = [shape(middle + 1), shape(short)] + [shape(middle)] * 2
+    rows = pltpu.VMEM((planes,) + tile, jnp.float32)
     cells = math.prod(level_set.shape)
 
     def call(kernel, ins, outs, scratch=(), work=0):
@@ -385,21 +416,19 @@
             spun, part = call(free, [values, wind, waves, pk], [field] * 2)
             part, x_near = lax.optimization_barrier((part, x_near))
         (part,) = call(turning, [values, spun, part, t_near, t_far], [field], work=1000)
-        last = functools.partial(section_kernel, section, bounds, heading_step, speed_step)
-        ins = [values, part, extra] if opening else [level_set, values, part]
-        ins += [x_near, x_far]
-        ins += [wind, waves, target_mask, target_depth]
-        ins += [most, other] if opening else [pk]
-        outs = [field]
-        if section < 3:
-            outs += edge_shapes
         if opening:
-            outs += [shape()]
-        rows = pltpu.VMEM((planes,) + tile, jnp.float32)
-        results = call(last, ins, outs, [rows, rows])
-        values, edges = results[0], results[1:5]
-        if opening:
-            pk = results[5]
+            ins = [values, part, x_near, x_far, wind, waves]
+            first = functools.partial(first_kernel, speed_step)
+            part, gap = call(first, ins, [field] * 2, [rows])
+            closing = functools.partial(closing_kernel, bounds, heading_step, speed_step)
+            ins = [values, part, gap, extra, target_mask, target_depth, most, other]
+            values, *edges, pk = call(closing, ins, [field, *edge_shapes, shape()], [rows])
+        else:
+            ins = [level_set, values, part, x_near, x_far, wind, waves]
+            ins += [target_mask, target_depth, pk]
+            outs = [field] + (edge_shapes if section == 2 else [])
+            last = functools.partial(section_kernel, section, speed_step)
+            values, *edges = call(last, ins, outs, [rows, rows])
     return values
 
 

time: 43 us -> 42.3 us (0.984)
  waiting for transfers between devices: 6.94 us -> 6.05 us
    ppermute x2, waiting for transfers between devices: 1.66 us -> 0.79 us  [spread(): return lax.ppermute(most, 'gx', pairs)]
    pallas_call x11 -> x12, Pallas kernels: 14.7 us -> 14.9 us  [call(): pl.pallas_call(kernel, out_shape=outs, in_specs=[vmem] * len(ins), out_sp...]
  transfers between devices with their start and end apart: 14 -> 14, of which waited for: 5 -> 5; matrix products, arithmetic and copies ran while one was open for 0% -> 0% of each run, Pallas kernels for 25% -> 28%
where the time goes in v7:
time: 42.3 us; the launch traced here: 41.6 us
  starting transfers between devices  18.8 us (44%)
  Pallas kernels  14.9 us (35%)
  waiting for transfers between devices  6.05 us (14%)
  local copies, waits for them, and re-layouts  1.74 us (4%)
    ppermute x12, starting transfers between devices, trade(): return lax.ppermute(value, axis, pairs)  15.9 us
    pallas_call x12, Pallas kernels, call(): pl.pallas_call(kernel, out_shape=outs, in_specs=[vmem] * len(ins), out_sp...  14.9 us
    ppermute x12, waiting for transfers between devices, trade(): return lax.ppermute(value, axis, pairs)  5.26 us
    ppermute x2, starting transfers between devices, spread(): return lax.ppermute(most, 'gx', pairs)  2.88 us
    unnamed x14, local copies, waits for them, and re-layouts  1.74 us
  transfers between devices with their start and end apart: 14, of which 5 were waited for; matrix products, arithmetic and copies ran while one was open for 0% of the time, Pallas kernels for 28%

profile of v7, /device:TPU:8, one launch (start us, length us, event | category | flops | bytes accessed | tf_op | source)
XLA Modules:
  0.0 41.6 jit_solution(17302756379251859082)
XLA Ops:
  0.0 0.0 copy-start
  0.0 1.0 %copy-done = f32[9,12,8,128]{3,2,1,0:T(8,128)S(1)} copy-done((f32[9,12,8,128]{3,2,1,0:T(8,128)S(1)}, f32[9,12,8,128]{3,2,1,0:T(8,128)}, u32[]{:S(2)}) %copy-start) | copy-done | bytes 442392
  1.0 0.0 copy-start.3
  1.0 0.7 %copy-done.3 = f32[2,9,128]{2,0,1:T(2,128)S(1)} copy-done((f32[2,9,128]{2,0,1:T(2,128)S(1)}, f32[2,9,128]{2,0,1:T(2,128)}, u32[]{:S(2)}) %copy-start.3) | copy-done | bytes 9240
  1.7 0.0 copy-start.1
  1.8 1.6 %collective-permute-start = (f32[38,8,128]{2,1,0:T(8,128)S(1)}, f32[38,8,128]{2,1,0:T(8,128)S(1)}, u32[]{:S(2)}, u32[]{:S(2)}) collective-permute-start(f32[38,8,128]{2,1,0:T(8,128)S(1)} %get-tuple-element.36), channel_id=1, source_target_pairs={{0,1},{2,3},{4,5},{6,7},{1,0},{3,2},{5,4},{7,6},{8,9},{10,11},{12,... | collective-permute-start | bytes 466952 | tf_op jit(solution)/shard_map/ppermute | solution.py:338
  3.4 0.0 collective-permute-start.2
  3.4 1.6 %collective-permute-start.3 = (f32[37,8,128]{2,1,0:T(8,128)S(1)}, f32[37,8,128]{2,1,0:T(8,128)S(1)}, u32[]{:S(2)}, u32[]{:S(2)}) collective-permute-start(f32[37,8,128]{2,1,0:T(8,128)S(1)} %get-tuple-element.40), channel_id=1, source_target_pairs={{8,16},{24,0},{16,8},{0,24},{9,17},{25,1},{17,9},{1,25},{10,18},{2... | collective-permute-start | bytes 454664 | tf_op jit(solution)/shard_map/ppermute | solution.py:338
  5.0 0.0 copy-start.2
  5.0 2.4 %collective-permute-start.4 = (f32[36,8,128]{2,1,0:T(8,128)S(1)}, f32[36,8,128]{2,1,0:T(8,128)S(1)}, u32[]{:S(2)}, u32[]{:S(2)}) collective-permute-start(f32[36,8,128]{2,1,0:T(8,128)S(1)} %get-tuple-element.41), channel_id=1, source_target_pairs={{1,2},{3,4},{5,6},{2,1},{4,3},{6,5},{0,0},{7,7},{9,10},{11,12},{13... | collective-permute-start | bytes 442376 | tf_op jit(solution)/shard_map/ppermute | solution.py:338
  7.4 0.2 collective-permute-done.x_near.near_ref
  7.6 0.3 collective-permute-start.1
  7.9 0.0 copy-done.1
  7.9 0.0 copy-done.2
  7.9 2.7 %shard_map.55 = (f32[9,12,8,128]{3,2,1,0:T(8,128)S(1)}, f32[9,12,8,128]{3,2,1,0:T(8,128)S(1)}, f32[9,12,8,128]{3,2,1,0:T(8,128)S(1)}) custom-call(f32[9,12,8,128]{3,2,1,0:T(8,128)S(1)} %copy-done.1, f32[9,2,128]{2,1,0:T(2,128)S(1)} %bitcast.3, f32[2,48,128]{2,1,0:T(8,128)S(1)} %copy-done.2), custom_call_target="tpu_custom_call" | custom-call | flops 33177600 | bytes 33177600 | tf_op jit(solution)/shard_map/pallas_call | solution.py:372
  10.6 0.6 %collective-permute-done.1 = f32[8,128]{1,0:T(8,128)S(1)} collective-permute-done((f32[8,128]{1,0:T(8,128)S(1)}, f32[8,128]{1,0:T(8,128)S(1)}, u32[]{:S(2)}, u32[]{:S(2)}) %collective-permute-start.1) | collective-permute-done | bytes 4128 | tf_op jit(solution)/shard_map/ppermute | solution.py:393
  11.3 2.6 %collective-permute-start.5 = (f32[8,128]{1,0:T(8,128)S(1)}, f32[8,128]{1,0:T(8,128)S(1)}, u32[]{:S(2)}, u32[]{:S(2)}) collective-permute-start(f32[8,128]{1,0:T(8,128)S(1)} %max.3.most_ref), channel_id=1, source_target_pairs={{0,4},{1,5},{2,6},{3,7},{4,0},{5,1},{6,2},{7,3},{8,12},{9,13},{10,... | collective-permute-start | bytes 12296 | tf_op jit(solution)/shard_map/ppermute | solution.py:393
  13.9 0.0 collective-permute-done.2.near_ref
  13.9 0.0 collective-permute-done.3.far_ref
  13.9 0.0 copy-start.4
  13.9 0.9 %shard_map.58.part_ref = f32[9,12,8,128]{3,2,1,0:T(8,128)S(1)} custom-call(f32[9,12,8,128]{3,2,1,0:T(8,128)S(1)} %copy-done.1, f32[9,12,8,128]{3,2,1,0:T(8,128)S(1)} %get-tuple-element.35.speed_ref, f32[9,12,8,128]{3,2,1,0:T(8,128)S(1)} %get-tuple-element.38.part_ref, f32[37,8,128]{2,1,0:T(8,128)S(1)} %collective-permute-done.2.near_ref, ...), custom_call_target="tpu_custom_call" | custom-call | flops 110592000 | bytes 110592000 | tf_op jit(solution)/shard_map/pallas_call | solution.py:372
  14.7 0.0 collective-permute-done.4.far_ref
  14.8 0.0 copy-done.4
  14.8 0.0 copy-start.5
  14.8 0.0 copy-start.6
  14.8 0.8 %shard_map.59 = (f32[9,12,8,128]{3,2,1,0:T(8,128)S(1)}, f32[9,12,8,128]{3,2,1,0:T(8,128)S(1)}) custom-call(f32[9,12,8,128]{3,2,1,0:T(8,128)S(1)} %copy-done.1, f32[9,12,8,128]{3,2,1,0:T(8,128)S(1)} %shard_map.58.part_ref, f32[38,8,128]{2,1,0:T(8,128)S(1)} %collective-permute-done.x_near.near_ref, f32[36,8,128]{2,1,0:T(8,128)S(1)} %collective-permute-done.4.far_ref, ...), custom_call_target="tpu_custom_call" | custom-call | tf_op jit(solution)/shard_map/pallas_call | solution.py:372
  15.6 0.2 collective-permute-done.5.other_ref
  15.8 0.0 copy-done.5
  15.8 0.0 copy-done.6
  15.8 0.4 %shard_map.60 = (f32[9,12,8,128]{3,2,1,0:T(8,128)S(1)}, f32[38,8,128]{2,1,0:T(8,128)S(1)}, f32[36,8,128]{2,1,0:T(8,128)S(1)}, f32[37,8,128]{2,1,0:T(8,128)S(1)},...) custom-call(f32[9,12,8,128]{3,2,1,0:T(8,128)S(1)} %copy-done.1, f32[9,12,8,128]{3,2,1,0:T(8,128)S(1)} %get-tuple-element.42.part_ref, ...), custom_call_target="tpu_custom_call" | custom-call | tf_op jit(solution)/shard_map/pallas_call | solution.py:372
  16.2 3.1 %collective-permute-start.6 = (f32[38,8,128]{2,1,0:T(8,128)S(1)}, f32[38,8,128]{2,1,0:T(8,128)S(1)}, u32[]{:S(2)}, u32[]{:S(2)}) collective-permute-start(f32[38,8,128]{2,1,0:T(8,128)S(1)} %get-tuple-element.50), channel_id=1, source_target_pairs={{0,1},{2,3},{4,5},{6,7},{1,0},{3,2},{5,4},{7,6},{8,9},{10,11},{12,... | collective-permute-start | bytes 466952 | tf_op jit(solution)/shard_map/ppermute | solution.py:338
  19.3 0.0 collective-permute-start.7
  19.3 0.6 %collective-permute-start.8 = (f32[37,8,128]{2,1,0:T(8,128)S(1)}, f32[37,8,128]{2,1,0:T(8,128)S(1)}, u32[]{:S(2)}, u32[]{:S(2)}) collective-permute-start(f32[37,8,128]{2,1,0:T(8,128)S(1)} %get-tuple-element.53), channel_id=1, source_target_pairs={{8,16},{24,0},{16,8},{0,24},{9,17},{25,1},{17,9},{1,25},{10,18},{2... | collective-permute-start | bytes 454664 | tf_op jit(solution)/shard_map/ppermute | solution.py:338
  19.9 2.6 %collective-permute-start.9 = (f32[36,8,128]{2,1,0:T(8,128)S(1)}, f32[36,8,128]{2,1,0:T(8,128)S(1)}, u32[]{:S(2)}, u32[]{:S(2)}) collective-permute-start(f32[36,8,128]{2,1,0:T(8,128)S(1)} %get-tuple-element.55), channel_id=1, source_target_pairs={{1,2},{3,4},{5,6},{2,1},{4,3},{6,5},{0,0},{7,7},{9,10},{11,12},{13... | collective-permute-start | bytes 442376 | tf_op jit(solution)/shard_map/ppermute | solution.py:338
  22.5 2.7 %shard_map.61 = (f32[9,12,8,128]{3,2,1,0:T(8,128)S(1)}, f32[9,12,8,128]{3,2,1,0:T(8,128)S(1)}) custom-call(f32[9,12,8,128]{3,2,1,0:T(8,128)S(1)} %get-tuple-element.46.s_ref, f32[9,2,128]{2,1,0:T(2,128)S(1)} %bitcast.5, f32[2,48,128]{2,1,0:T(8,128)S(1)} %copy-done.2, f32[8,128]{1,0:T(8,128)S(1)} %get-tuple-element.47.rest_0_.pk_ref), custom_call_target="tpu_custom_call" | custom-call | tf_op jit(solution)/shard_map/pallas_call | solution.py:372
  25.2 0.0 collective-permute-done.6.near_ref
  25.3 0.0 collective-permute-done.7.near_ref
  25.3 0.0 collective-permute-done.8.far_ref
  25.3 0.9 %shard_map.62.part_ref = f32[9,12,8,128]{3,2,1,0:T(8,128)S(1)} custom-call(f32[9,12,8,128]{3,2,1,0:T(8,128)S(1)} %get-tuple-element.46.s_ref, f32[9,12,8,128]{3,2,1,0:T(8,128)S(1)} %get-tuple-element.48.speed_ref, f32[9,12,8,128]{3,2,1,0:T(8,128)S(1)} %get-tuple-element.51.part_ref, f32[37,8,128]{2,1,0:T(8,128)S(1)} %collective-permute-done.7.near_ref, ...), custom_call_target="tpu_custom_call" | custom-call | flops 110592000 | bytes 110592000 | tf_op jit(solution)/shard_map/pallas_call | solution.py:372
  26.1 2.3 %collective-permute-done.9.far_ref = f32[36,8,128]{2,1,0:T(8,128)S(1)} collective-permute-done((f32[36,8,128]{2,1,0:T(8,128)S(1)}, f32[36,8,128]{2,1,0:T(8,128)S(1)}, u32[]{:S(2)}, u32[]{:S(2)}) %collective-permute-start.9) | collective-permute-done | bytes 147488 | tf_op jit(solution)/shard_map/ppermute | solution.py:338
  28.5 1.0 %shard_map.63 = (f32[9,12,8,128]{3,2,1,0:T(8,128)S(1)}, f32[38,8,128]{2,1,0:T(8,128)S(1)}, f32[36,8,128]{2,1,0:T(8,128)S(1)}, f32[37,8,128]{2,1,0:T(8,128)S(1)}, f32[37,8,128]{2,1,0:T(8,128)S(1)}) custom-call(f32[9,12,8,128]{3,2,1,0:T(8,128)S(1)} %copy-done.1, f32[9,12,8,128]{3,2,1,0:T(8,128)S(1)} %get-tuple-element.46.s_ref, ...), custom_call_target="tpu_custom_call" | custom-call | tf_op jit(solution)/shard_map/pallas_call | solution.py:372
  29.5 0.7 %collective-permute-start.10 = (f32[38,8,128]{2,1,0:T(8,128)S(1)}, f32[38,8,128]{2,1,0:T(8,128)S(1)}, u32[]{:S(2)}, u32[]{:S(2)}) collective-permute-start(f32[38,8,128]{2,1,0:T(8,128)S(1)} %get-tuple-element.59), channel_id=1, source_target_pairs={{0,1},{2,3},{4,5},{6,7},{1,0},{3,2},{5,4},{7,6},{8,9},{10,11},{12,... | collective-permute-start | bytes 466952 | tf_op jit(solution)/shard_map/ppermute | solution.py:338
  30.2 0.0 collective-permute-start.11
  30.2 1.1 %collective-permute-start.12 = (f32[37,8,128]{2,1,0:T(8,128)S(1)}, f32[37,8,128]{2,1,0:T(8,128)S(1)}, u32[]{:S(2)}, u32[]{:S(2)}) collective-permute-start(f32[37,8,128]{2,1,0:T(8,128)S(1)} %get-tuple-element.62), channel_id=1, source_target_pairs={{8,16},{24,0},{16,8},{0,24},{9,17},{25,1},{17,9},{1,25},{10,18},{2... | collective-permute-start | bytes 454664 | tf_op jit(solution)/shard_map/ppermute | solution.py:338
  31.3 2.2 %collective-permute-start.13 = (f32[36,8,128]{2,1,0:T(8,128)S(1)}, f32[36,8,128]{2,1,0:T(8,128)S(1)}, u32[]{:S(2)}, u32[]{:S(2)}) collective-permute-start(f32[36,8,128]{2,1,0:T(8,128)S(1)} %get-tuple-element.64), channel_id=1, source_target_pairs={{1,2},{3,4},{5,6},{2,1},{4,3},{6,5},{0,0},{7,7},{9,10},{11,12},{13... | collective-permute-start | bytes 442376 | tf_op jit(solution)/shard_map/ppermute | solution.py:338
  33.6 2.7 %shard_map.64 = (f32[9,12,8,128]{3,2,1,0:T(8,128)S(1)}, f32[9,12,8,128]{3,2,1,0:T(8,128)S(1)}) custom-call(f32[9,12,8,128]{3,2,1,0:T(8,128)S(1)} %get-tuple-element.56.s_ref, f32[9,2,128]{2,1,0:T(2,128)S(1)} %bitcast.7, f32[2,48,128]{2,1,0:T(8,128)S(1)} %copy-done.2, f32[8,128]{1,0:T(8,128)S(1)} %get-tuple-element.47.rest_0_.pk_ref), custom_call_target="tpu_custom_call" | custom-call | tf_op jit(solution)/shard_map/pallas_call | solution.py:372
  36.3 0.0 collective-permute-done.10.near_ref
  36.3 0.0 collective-permute-done.11.near_ref
  36.3 0.0 collective-permute-done.12.far_ref
  36.3 0.9 %shard_map.65.part_ref = f32[9,12,8,128]{3,2,1,0:T(8,128)S(1)} custom-call(f32[9,12,8,128]{3,2,1,0:T(8,128)S(1)} %get-tuple-element.56.s_ref, f32[9,12,8,128]{3,2,1,0:T(8,128)S(1)} %get-tuple-element.57.speed_ref, f32[9,12,8,128]{3,2,1,0:T(8,128)S(1)} %get-tuple-element.60.part_ref, f32[37,8,128]{2,1,0:T(8,128)S(1)} %collective-permute-done.11.near_ref, ...), custom_call_target="tpu_custom_call" | custom-call | flops 110592000 | bytes 110592000 | tf_op jit(solution)/shard_map/pallas_call | solution.py:372
  37.2 2.7 %collective-permute-done.13.far_ref = f32[36,8,128]{2,1,0:T(8,128)S(1)} collective-permute-done((f32[36,8,128]{2,1,0:T(8,128)S(1)}, f32[36,8,128]{2,1,0:T(8,128)S(1)}, u32[]{:S(2)}, u32[]{:S(2)}) %collective-permute-start.13) | collective-permute-done | bytes 147488 | tf_op jit(solution)/shard_map/ppermute | solution.py:338
  39.9 1.7 %shard_map.66 = f32[9,12,8,128]{3,2,1,0:T(8,128)} custom-call(f32[9,12,8,128]{3,2,1,0:T(8,128)S(1)} %copy-done.1, f32[9,12,8,128]{3,2,1,0:T(8,128)S(1)} %get-tuple-element.56.s_ref, f32[9,12,8,128]{3,2,1,0:T(8,128)S(1)} %shard_map.65.part_ref, f32[38,8,128]{2,1,0:T(8,128)S(1)} %collective-permute-done.10.near_ref, ...), custom_call_target="tpu_custom_call" | custom-call | tf_op jit(solution)/shard_map/pallas_call | solution.py:372
  (3 shorter events, 0.1 us)
Async XLA Ops:
  0.0 1.0 %copy-start = (f32[9,12,8,128]{3,2,1,0:T(8,128)S(1)}, f32[9,12,8,128]{3,2,1,0:T(8,128)}, u32[]{:S(2)}) copy-start(f32[9,12,8,128]{3,2,1,0:T(8,128)} %base_ref.3) | copy-start | bytes 1327108
  1.0 0.7 %copy-start.3 = (f32[2,9,128]{2,0,1:T(2,128)S(1)}, f32[2,9,128]{2,0,1:T(2,128)}, u32[]{:S(2)}) copy-start(f32[2,9,128]{2,0,1:T(2,128)} %param.6) | copy-start | bytes 27652
  1.7 6.2 %copy-start.1 = (f32[9,12,8,128]{3,2,1,0:T(8,128)S(1)}, f32[9,12,8,128]{3,2,1,0:T(8,128)}, u32[]{:S(2)}) copy-start(f32[9,12,8,128]{3,2,1,0:T(8,128)} %base_ref.3) | copy-start | bytes 1327108
  1.8 5.8 %collective-permute-start = (f32[38,8,128]{2,1,0:T(8,128)S(1)}, f32[38,8,128]{2,1,0:T(8,128)S(1)}, u32[]{:S(2)}, u32[]{:S(2)}) collective-permute-start(f32[38,8,128]{2,1,0:T(8,128)S(1)} %get-tuple-element.36), channel_id=1, source_target_pairs={{0,1},{2,3},{4,5},{6,7},{1,0},{3,2},{5,4},{7,6},{8,9},{10,11},{12,... | collective-permute-start | bytes 466952 | tf_op jit(solution)/shard_map/ppermute | solution.py:338
  3.4 10.5 %collective-permute-start.2 = (f32[37,8,128]{2,1,0:T(8,128)S(1)}, f32[37,8,128]{2,1,0:T(8,128)S(1)}, u32[]{:S(2)}, u32[]{:S(2)}) collective-permute-start(f32[37,8,128]{2,1,0:T(8,128)S(1)} %get-tuple-element.39), channel_id=1, source_target_pairs={{0,8},{16,24},{8,0},{24,16},{1,9},{17,25},{9,1},{25,17},{2,10},{18... | collective-permute-start | bytes 454664 | tf_op jit(solution)/shard_map/ppermute | solution.py:338
  3.4 10.5 %collective-permute-start.3 = (f32[37,8,128]{2,1,0:T(8,128)S(1)}, f32[37,8,128]{2,1,0:T(8,128)S(1)}, u32[]{:S(2)}, u32[]{:S(2)}) collective-permute-start(f32[37,8,128]{2,1,0:T(8,128)S(1)} %get-tuple-element.40), channel_id=1, source_target_pairs={{8,16},{24,0},{16,8},{0,24},{9,17},{25,1},{17,9},{1,25},{10,18},{2... | collective-permute-start | bytes 454664 | tf_op jit(solution)/shard_map/ppermute | solution.py:338
  5.0 3.0 %copy-start.2 = (f32[2,48,128]{2,1,0:T(8,128)S(1)}, f32[2,48,128]{2,1,0:T(8,128)}, u32[]{:S(2)}) copy-start(f32[2,48,128]{2,1,0:T(8,128)} %constant.2.clone.waves_ref) | copy-start | bytes 147460
  5.0 9.8 %collective-permute-start.4 = (f32[36,8,128]{2,1,0:T(8,128)S(1)}, f32[36,8,128]{2,1,0:T(8,128)S(1)}, u32[]{:S(2)}, u32[]{:S(2)}) collective-permute-start(f32[36,8,128]{2,1,0:T(8,128)S(1)} %get-tuple-element.41), channel_id=1, source_target_pairs={{1,2},{3,4},{5,6},{2,1},{4,3},{6,5},{0,0},{7,7},{9,10},{11,12},{13... | collective-permute-start | bytes 442376 | tf_op jit(solution)/shard_map/ppermute | solution.py:338
  7.6 3.7 %collective-permute-start.1 = (f32[8,128]{1,0:T(8,128)S(1)}, f32[8,128]{1,0:T(8,128)S(1)}, u32[]{:S(2)}, u32[]{:S(2)}) collective-permute-start(f32[8,128]{1,0:T(8,128)S(1)} %shard_map.57), channel_id=1, source_target_pairs={{0,2},{1,3},{2,0},{3,1},{4,6},{5,7},{6,4},{7,5},{8,10},{9,11},{10,... | collective-permute-start | bytes 12296 | tf_op jit(solution)/shard_map/ppermute | solution.py:393
  11.3 4.5 %collective-permute-start.5 = (f32[8,128]{1,0:T(8,128)S(1)}, f32[8,128]{1,0:T(8,128)S(1)}, u32[]{:S(2)}, u32[]{:S(2)}) collective-permute-start(f32[8,128]{1,0:T(8,128)S(1)} %max.3.most_ref), channel_id=1, source_target_pairs={{0,4},{1,5},{2,6},{3,7},{4,0},{5,1},{6,2},{7,3},{8,12},{9,13},{10,... | collective-permute-start | bytes 12296 | tf_op jit(solution)/shard_map/ppermute | solution.py:393
  13.9 0.9 %copy-start.4 = (f32[2,9,128]{2,0,1:T(2,128)S(1)}, f32[2,9,128]{2,0,1:T(2,128)}, u32[]{:S(2)}) copy-start(f32[2,9,128]{2,0,1:T(2,128)} %param.6) | copy-start | bytes 27652
  14.8 1.0 %copy-start.5 = (s32[9,128]{1,0:T(8,128)S(1)}, s32[9,128]{1,0:T(8,128)}, u32[]{:S(2)}) copy-start(s32[9,128]{1,0:T(8,128)} %mask_ref.5) | copy-start | bytes 13828
  14.8 1.0 %copy-start.6 = (f32[9,128]{1,0:T(8,128)S(1)}, f32[9,128]{1,0:T(8,128)}, u32[]{:S(2)}) copy-start(f32[9,128]{1,0:T(8,128)} %depth_ref.5) | copy-start | bytes 13828
  16.2 9.0 %collective-permute-start.6 = (f32[38,8,128]{2,1,0:T(8,128)S(1)}, f32[38,8,128]{2,1,0:T(8,128)S(1)}, u32[]{:S(2)}, u32[]{:S(2)}) collective-permute-start(f32[38,8,128]{2,1,0:T(8,128)S(1)} %get-tuple-element.50), channel_id=1, source_target_pairs={{0,1},{2,3},{4,5},{6,7},{1,0},{3,2},{5,4},{7,6},{8,9},{10,11},{12,... | collective-permute-start | bytes 466952 | tf_op jit(solution)/shard_map/ppermute | solution.py:338
  19.3 6.0 %collective-permute-start.7 = (f32[37,8,128]{2,1,0:T(8,128)S(1)}, f32[37,8,128]{2,1,0:T(8,128)S(1)}, u32[]{:S(2)}, u32[]{:S(2)}) collective-permute-start(f32[37,8,128]{2,1,0:T(8,128)S(1)} %get-tuple-element.52), channel_id=1, source_target_pairs={{0,8},{16,24},{8,0},{24,16},{1,9},{17,25},{9,1},{25,17},{2,10},{18... | collective-permute-start | bytes 454664 | tf_op jit(solution)/shard_map/ppermute | solution.py:338
  19.3 6.0 %collective-permute-start.8 = (f32[37,8,128]{2,1,0:T(8,128)S(1)}, f32[37,8,128]{2,1,0:T(8,128)S(1)}, u32[]{:S(2)}, u32[]{:S(2)}) collective-permute-start(f32[37,8,128]{2,1,0:T(8,128)S(1)} %get-tuple-element.53), channel_id=1, source_target_pairs={{8,16},{24,0},{16,8},{0,24},{9,17},{25,1},{17,9},{1,25},{10,18},{2... | collective-permute-start | bytes 454664 | tf_op jit(solution)/shard_map/ppermute | solution.py:338
  19.9 8.5 %collective-permute-start.9 = (f32[36,8,128]{2,1,0:T(8,128)S(1)}, f32[36,8,128]{2,1,0:T(8,128)S(1)}, u32[]{:S(2)}, u32[]{:S(2)}) collective-permute-start(f32[36,8,128]{2,1,0:T(8,128)S(1)} %get-tuple-element.55), channel_id=1, source_target_pairs={{1,2},{3,4},{5,6},{2,1},{4,3},{6,5},{0,0},{7,7},{9,10},{11,12},{13... | collective-permute-start | bytes 442376 | tf_op jit(solution)/shard_map/ppermute | solution.py:338
  29.5 6.8 %collective-permute-start.10 = (f32[38,8,128]{2,1,0:T(8,128)S(1)}, f32[38,8,128]{2,1,0:T(8,128)S(1)}, u32[]{:S(2)}, u32[]{:S(2)}) collective-permute-start(f32[38,8,128]{2,1,0:T(8,128)S(1)} %get-tuple-element.59), channel_id=1, source_target_pairs={{0,1},{2,3},{4,5},{6,7},{1,0},{3,2},{5,4},{7,6},{8,9},{10,11},{12,... | collective-permute-start | bytes 466952 | tf_op jit(solution)/shard_map/ppermute | solution.py:338
  30.2 6.1 %collective-permute-start.11 = (f32[37,8,128]{2,1,0:T(8,128)S(1)}, f32[37,8,128]{2,1,0:T(8,128)S(1)}, u32[]{:S(2)}, u32[]{:S(2)}) collective-permute-start(f32[37,8,128]{2,1,0:T(8,128)S(1)} %get-tuple-element.61), channel_id=1, source_target_pairs={{0,8},{16,24},{8,0},{24,16},{1,9},{17,25},{9,1},{25,17},{2,10},{18... | collective-permute-start | bytes 454664 | tf_op jit(solution)/shard_map/ppermute | solution.py:338
  30.2 6.1 %collective-permute-start.12 = (f32[37,8,128]{2,1,0:T(8,128)S(1)}, f32[37,8,128]{2,1,0:T(8,128)S(1)}, u32[]{:S(2)}, u32[]{:S(2)}) collective-permute-start(f32[37,8,128]{2,1,0:T(8,128)S(1)} %get-tuple-element.62), channel_id=1, source_target_pairs={{8,16},{24,0},{16,8},{0,24},{9,17},{25,1},{17,9},{1,25},{10,18},{2... | collective-permute-start | bytes 454664 | tf_op jit(solution)/shard_map/ppermute | solution.py:338
  31.3 8.5 %collective-permute-start.13 = (f32[36,8,128]{2,1,0:T(8,128)S(1)}, f32[36,8,128]{2,1,0:T(8,128)S(1)}, u32[]{:S(2)}, u32[]{:S(2)}) collective-permute-start(f32[36,8,128]{2,1,0:T(8,128)S(1)} %get-tuple-element.64), channel_id=1, source_target_pairs={{1,2},{3,4},{5,6},{2,1},{4,3},{6,5},{0,0},{7,7},{9,10},{11,12},{13... | collective-permute-start | bytes 442376 | tf_op jit(solution)/shard_map/ppermute | solution.py:338

commit v8 on v7

--- a/solution.py
+++ b/solution.py
@@ -60,49 +60,6 @@
     return out
 
 
-def tile_terms(cell, step):
-    count = cell.shape[1]
-    eps = epsilon * step * step
-    flat = 1.0 / (eps * eps)
-    place = lax.broadcasted_iota(jnp.int32, cell.shape, 1)
-
-    def after(value, by=1):
-        return pltpu.roll(value, count - by, 1)
-
-    def before(value, by=1):
-        return pltpu.roll(value, by, 1)
-
-    up1 = jnp.where(place == count - 1, cell, after(cell))
-    up2 = jnp.where(place >= count - 2, up1, after(cell, 2))
-    dn1 = jnp.where(place == 0, cell, before(cell))
-    dn2 = jnp.where(place <= 1, dn1, before(cell, 2))
-    ahead = up1 - cell
-    behind = cell - dn1
-    bend_l = behind - (dn1 - dn2)
-    bend = ahead - behind
-    bend_r = (up2 - up1) - ahead
-    turn_l = bend - bend_l
-    turn_r = bend_r - bend
-    jerk = turn_r - turn_l
-    level_l = turn_l * turn_l * (4.0 / 3.0) + eps
-    level_r = turn_r * turn_r * (4.0 / 3.0) + eps
-    ia = inverse(level_l + bend * (bend + turn_l))
-    ib = inverse(level_l + bend * bend_l)
-    jb = inverse(level_r + bend * bend_r)
-    jc = inverse(level_r + bend * (bend - turn_r))
-    a1 = ia * ia
-    c0 = jc * jc
-    a2 = jnp.where(place == 0, flat, before(a1))
-    c1 = jnp.where(place == count - 1, flat, after(c0))
-    jerk_l = jnp.where(place == 0, bend, before(jerk))
-    jerk_r = jnp.where(place == count - 1, bend, after(jerk))
-    base = (ahead + behind) * 6.0 - (turn_l + turn_r)
-    minus, plus = sides(
-        jerk_l, jerk, jerk_r, a2, a1, ib * ib * 6.0, jb * jb * 6.0, c0, c1
-    )
-    return base + (plus - minus), (plus + minus) - jerk
-
-
 def batches(total, most):
     return max(k for k in range(1, most + 1) if total % k == 0)
 
@@ -141,47 +98,73 @@
     planes, headings, speeds, width = s_ref.shape
     tile = (speeds, width)
     if split:
-        speed_ref, out_ref, extra_ref = rest
+        speed_ref, out_ref, extra_ref, turned_ref, mean_ref, gap_ref, flow_ref = rest
     else:
-        pk_ref, speed_ref, out_ref = rest
+        pk_ref, speed_ref, out_ref, turned_ref, mean_ref, gap_ref, flow_ref = rest
         peak = splat(pk_ref[1:2, :] * gain, tile)
-    pace = speeds_of(tile, speed_step) * gain
     gain_v = thrust_limit / (12.0 * speed_step)
     first = lax.axis_index("head") * headings
     cells = planes * headings
     s_rows = s_ref.reshape(cells * speeds, width)
     speed_rows = speed_ref.reshape(cells * speeds, width)
-    wide = batches(headings, 2)
-    group = 8
-
-    def along_speed(start, count, stride):
-        spots = [pl.ds(start * speeds + v, count, stride=stride * speeds) for v in range(speeds)]
-        lines = [s_rows[spot, :] for spot in spots]
-        ends = [lines[0]] * rim + lines + [lines[-1]] * rim
+    out_rows = out_ref.reshape(cells * speeds, width)
+    flow_rows = flow_ref.reshape(cells * speeds, width)
+    few, many = 8, turned_ref.shape[2] // speeds
+    groups = turned_ref.shape[0]
+    lanes = many * speeds
+    high = 8
+    lines = width // high
+
+    def along_speed(n):
+        start = jnp.minimum(n * few, cells - few) * speeds
+        spots = [pl.ds(start + v, few, stride=speeds) for v in range(speeds)]
+        rows = [s_rows[spot, :] for spot in spots]
+        ends = [rows[0]] * rim + rows + [rows[-1]] * rim
         for spot, (mean, gap) in zip(spots, row_terms(ends, speed_step)):
             speed_rows[spot, :] = gain_v * (gap - jnp.abs(mean))
 
-    def step(n, carry):
-        for k in range(wide):
-            j = n * wide + k
-            table = splat(waves_ref[1, pl.ds(first + j, 1), :], tile) * pace
-            for i in range(planes):
-                mean, gap = tile_terms(s_ref[i, j], spacing)
-                flow = table + splat(wind_ref[i, 1:2, :] * gain, tile)
-                if split:
-                    out_ref[i, j] = mean * flow
-                    extra_ref[i, j] = gap
-                else:
-                    out_ref[i, j] = mean * flow + gap * peak
-            for i in range(0, planes - group + 1, group):
-                along_speed(i * headings + j, group, headings)
-        return carry
-
-    lax.fori_loop(0, headings // wide, step, 0)
-    count = min(group, headings)
-    for i in range(planes // group * group, planes):
-        for j in range(0, headings, count):
-            along_speed(i * headings + min(j, headings - count), count, 1)
+    def span(n):
+        return pl.ds(pl.multiple_of(jnp.minimum(n * many, cells - many) * speeds, speeds), lanes)
+
+    def turn_in(n, carry):
+        along_speed(n)
+        turned = s_rows[span(n), :].T
+        turned_ref[n, rim : rim + width, :] = turned
+        for k in range(rim):
+            turned_ref[n, k : k + 1, :] = turned[:1]
+            turned_ref[n, rim + width + k : rim + width + k + 1, :] = turned[-1:]
+        return carry
+
+    def along_y(n, carry):
+        ends = [turned_ref[n, pl.ds(k, high, stride=lines), :] for k in range(lines + 2 * rim)]
+        for k, (mean, gap) in enumerate(row_terms(ends, spacing)):
+            mean_ref[n, pl.ds(k, high, stride=lines), :] = mean
+            gap_ref[n, pl.ds(k, high, stride=lines), :] = gap
+        return carry
+
+    def turn_out(n, carry):
+        along_speed(groups + n)
+        mean = mean_ref[n].T
+        gap = gap_ref[n].T
+        drift = mean * flow_rows[span(n), :]
+        if split:
+            out_rows[span(n), :] = drift
+            extra_ref.reshape(cells * speeds, width)[span(n), :] = gap
+        else:
+            out_rows[span(n), :] = drift + gap * splat(peak[:1], gap.shape)
+        return carry
+
+    pace = speeds_of(tile, speed_step) * gain
+    tables = [
+        splat(waves_ref[1, pl.ds(first + j, 1), :], tile) * pace for j in range(headings)
+    ]
+    for i in range(planes):
+        wind = splat(wind_ref[i, 1:2, :] * gain, tile)
+        for j in range(headings):
+            flow_ref[i, j] = tables[j] + wind
+    lax.fori_loop(0, groups, turn_in, 0)
+    lax.fori_loop(0, groups, along_y, 0)
+    lax.fori_loop(0, groups, turn_out, 0)
 
 
 def heading_kernel(heading_step, s_ref, speed_ref, part_ref, near_ref, far_ref, out_ref):
@@ -364,7 +347,9 @@
     short = rim * headings
     middle = max(short + 1, rim * planes)
 
-    edge_shapes = [shape(middle + 1), shape(short)] + [shape(middle)] * 2
+    longest, t_shapes = middle + 1, [shape(middle)] * 2
+    first_edges = [shape(longest), shape(short)] + t_shapes
+    later_edges = [shape(short), shape(longest)] + t_shapes
     rows = pltpu.VMEM((planes,) + tile, jnp.float32)
     cells = math.prod(level_set.shape)
 
@@ -382,6 +367,14 @@
         )(*ins)
 
     wind = jnp.transpose(wind_field, (1, 0, 2))
+    many = 16
+    groups, lanes = -(-planes * headings // many), many * speed_count
+    room = [
+        pltpu.VMEM((groups, cross_count + 8, lanes), jnp.float32),
+        pltpu.VMEM((groups, cross_count, lanes), jnp.float32),
+        pltpu.VMEM((groups, cross_count, lanes), jnp.float32),
+        pltpu.VMEM(level_set.shape, jnp.float32),
+    ]
     values, pk = level_set, None
     size = lax.axis_size("gx")
 
@@ -392,7 +385,7 @@
             pairs = [(i, i ^ reach) for i in range(size)]
         return lax.ppermute(most, "gx", pairs)
 
-    edges = call(opening_kernel, [values, wind], edge_shapes)
+    edges = call(opening_kernel, [values, wind], first_edges)
     for section in (1, 2, 3):
         opening = section == 1
         x_out, x_last, t_out, t_last = edges
@@ -405,7 +398,8 @@
         if opening:
             (most,) = call(meeting_kernel, [wind, x_near], [shape()])
             other = spread(most, 2)
-            spun, part, extra = call(free, [values, wind, waves], [field] * 3, work=300)
+            ins = [values, wind, waves]
+            spun, part, extra = call(free, ins, [field] * 3, room, work=300)
             reach = 4
             while reach < size:
                 most = jnp.maximum(most, other)
@@ -413,8 +407,8 @@
                 other = spread(most, reach)
                 reach *= 2
         else:
-            spun, part = call(free, [values, wind, waves, pk], [field] * 2)
-            part, x_near = lax.optimization_barrier((part, x_near))
+            spun, part = call(free, [values, wind, waves, pk], [field] * 2, room)
+            part, x_far = lax.optimization_barrier((part, x_far))
         (part,) = call(turning, [values, spun, part, t_near, t_far], [field], work=1000)
         if opening:
             ins = [values, part, x_near, x_far, wind, waves]
@@ -422,11 +416,11 @@
             part, gap = call(first, ins, [field] * 2, [rows])
             closing = functools.partial(closing_kernel, bounds, heading_step, speed_step)
             ins = [values, part, gap, extra, target_mask, target_depth, most, other]
-            values, *edges, pk = call(closing, ins, [field, *edge_shapes, shape()], [rows])
+            values, *edges, pk = call(closing, ins, [field, *later_edges, shape()], [rows])
         else:
             ins = [level_set, values, part, x_near, x_far, wind, waves]
             ins += [target_mask, target_depth, pk]
-            outs = [field] + (edge_shapes if section == 2 else [])
+            outs = [field] + (later_edges if section == 2 else [])
             last = functools.partial(section_kernel, section, speed_step)
             values, *edges = call(last, ins, outs, [rows, rows])
     return values

time: 42.3 us -> 44.2 us (1.045)
  the two profiles are of different devices: /device:TPU:8 before, /device:TPU:0 now
where the time goes in v8:
time: 44.2 us; the launch traced here: 44 us
  starting transfers between devices  21.4 us (48%)
  Pallas kernels  14.1 us (32%)
  waiting for transfers between devices  6.61 us (15%)
  local copies, waits for them, and re-layouts  1.74 us (4%)
    ppermute x12, starting transfers between devices, trade(): return lax.ppermute(value, axis, pairs)  16.9 us
    pallas_call x12, Pallas kernels, call(): pl.pallas_call(kernel, out_shape=outs, in_specs=[vmem] * len(ins), out_sp...  14.1 us
    ppermute x12, waiting for transfers between devices, trade(): return lax.ppermute(value, axis, pairs)  5.46 us
    ppermute x2, starting transfers between devices, spread(): return lax.ppermute(most, 'gx', pairs)  4.49 us
    unnamed x14, local copies, waits for them, and re-layouts  1.74 us
    ppermute x2, waiting for transfers between devices, spread(): return lax.ppermute(most, 'gx', pairs)  1.15 us
  transfers between devices with their start and end apart: 14, of which 5 were waited for; matrix products, arithmetic and copies ran while one was open for 0% of the time, Pallas kernels for 25%

profile of v8, /device:TPU:0, one launch (start us, length us, event | category | flops | bytes accessed | tf_op | source)
XLA Modules:
  0.0 44.0 jit_solution(1754745400702088119)
XLA Ops:
  0.0 0.0 copy-start
  0.0 1.0 %copy-done = f32[9,12,8,128]{3,2,1,0:T(8,128)S(1)} copy-done((f32[9,12,8,128]{3,2,1,0:T(8,128)S(1)}, f32[9,12,8,128]{3,2,1,0:T(8,128)}, u32[]{:S(2)}) %copy-start) | copy-done | bytes 442392
  1.0 0.0 copy-start.3
  1.0 0.7 %copy-done.3 = f32[2,9,128]{2,0,1:T(2,128)S(1)} copy-done((f32[2,9,128]{2,0,1:T(2,128)S(1)}, f32[2,9,128]{2,0,1:T(2,128)}, u32[]{:S(2)}) %copy-start.3) | copy-done | bytes 9240
  1.7 0.0 copy-start.1
  1.8 3.0 %collective-permute-start = (f32[38,8,128]{2,1,0:T(8,128)S(1)}, f32[38,8,128]{2,1,0:T(8,128)S(1)}, u32[]{:S(2)}, u32[]{:S(2)}) collective-permute-start(f32[38,8,128]{2,1,0:T(8,128)S(1)} %get-tuple-element.36), channel_id=1, source_target_pairs={{0,1},{2,3},{4,5},{6,7},{1,0},{3,2},{5,4},{7,6},{8,9},{10,11},{12,... | collective-permute-start | bytes 466952 | tf_op jit(solution)/shard_map/ppermute | solution.py:321
  4.8 0.0 collective-permute-start.2
  4.8 1.6 %collective-permute-start.3 = (f32[37,8,128]{2,1,0:T(8,128)S(1)}, f32[37,8,128]{2,1,0:T(8,128)S(1)}, u32[]{:S(2)}, u32[]{:S(2)}) collective-permute-start(f32[37,8,128]{2,1,0:T(8,128)S(1)} %get-tuple-element.40), channel_id=1, source_target_pairs={{8,16},{24,0},{16,8},{0,24},{9,17},{25,1},{17,9},{1,25},{10,18},{2... | collective-permute-start | bytes 454664 | tf_op jit(solution)/shard_map/ppermute | solution.py:321
  6.4 0.0 copy-start.2
  6.4 0.8 %collective-permute-start.4 = (f32[36,8,128]{2,1,0:T(8,128)S(1)}, f32[36,8,128]{2,1,0:T(8,128)S(1)}, u32[]{:S(2)}, u32[]{:S(2)}) collective-permute-start(f32[36,8,128]{2,1,0:T(8,128)S(1)} %get-tuple-element.41), channel_id=1, source_target_pairs={{1,2},{3,4},{5,6},{2,1},{4,3},{6,5},{0,0},{7,7},{9,10},{11,12},{13... | collective-permute-start | bytes 442376 | tf_op jit(solution)/shard_map/ppermute | solution.py:321
  7.2 1.6 %collective-permute-done.x_near.near_ref = f32[38,8,128]{2,1,0:T(8,128)S(1)} collective-permute-done((f32[38,8,128]{2,1,0:T(8,128)S(1)}, f32[38,8,128]{2,1,0:T(8,128)S(1)}, u32[]{:S(2)}, u32[]{:S(2)}) %collective-permute-start) | collective-permute-done | bytes 155680 | tf_op jit(solution)/shard_map/ppermute | solution.py:321
  8.8 1.9 %collective-permute-start.1 = (f32[8,128]{1,0:T(8,128)S(1)}, f32[8,128]{1,0:T(8,128)S(1)}, u32[]{:S(2)}, u32[]{:S(2)}) collective-permute-start(f32[8,128]{1,0:T(8,128)S(1)} %shard_map.57), channel_id=1, source_target_pairs={{0,2},{1,3},{2,0},{3,1},{4,6},{5,7},{6,4},{7,5},{8,10},{9,11},{10,... | collective-permute-start | bytes 12296 | tf_op jit(solution)/shard_map/ppermute | solution.py:386
  10.7 0.0 copy-done.1
  10.7 0.0 copy-done.2
  10.7 2.5 %shard_map.55 = (f32[9,12,8,128]{3,2,1,0:T(8,128)S(1)}, f32[9,12,8,128]{3,2,1,0:T(8,128)S(1)}, f32[9,12,8,128]{3,2,1,0:T(8,128)S(1)}) custom-call(f32[9,12,8,128]{3,2,1,0:T(8,128)S(1)} %copy-done.1, f32[9,2,128]{2,1,0:T(2,128)S(1)} %bitcast.3, f32[2,48,128]{2,1,0:T(8,128)S(1)} %copy-done.2), custom_call_target="tpu_custom_call" | custom-call | flops 33177600 | bytes 33177600 | tf_op jit(solution)/shard_map/pallas_call | solution.py:357
  13.2 1.0 %collective-permute-done.1 = f32[8,128]{1,0:T(8,128)S(1)} collective-permute-done((f32[8,128]{1,0:T(8,128)S(1)}, f32[8,128]{1,0:T(8,128)S(1)}, u32[]{:S(2)}, u32[]{:S(2)}) %collective-permute-start.1) | collective-permute-done | bytes 4128 | tf_op jit(solution)/shard_map/ppermute | solution.py:386
  14.2 2.6 %collective-permute-start.5 = (f32[8,128]{1,0:T(8,128)S(1)}, f32[8,128]{1,0:T(8,128)S(1)}, u32[]{:S(2)}, u32[]{:S(2)}) collective-permute-start(f32[8,128]{1,0:T(8,128)S(1)} %max.3.most_ref), channel_id=1, source_target_pairs={{0,4},{1,5},{2,6},{3,7},{4,0},{5,1},{6,2},{7,3},{8,12},{9,13},{10,... | collective-permute-start | bytes 12296 | tf_op jit(solution)/shard_map/ppermute | solution.py:386
  16.8 0.0 collective-permute-done.2.near_ref
  16.9 0.0 collective-permute-done.3.far_ref
  16.9 0.0 copy-start.4
  16.9 0.9 %shard_map.58.part_ref = f32[9,12,8,128]{3,2,1,0:T(8,128)S(1)} custom-call(f32[9,12,8,128]{3,2,1,0:T(8,128)S(1)} %copy-done.1, f32[9,12,8,128]{3,2,1,0:T(8,128)S(1)} %get-tuple-element.35.speed_ref, f32[9,12,8,128]{3,2,1,0:T(8,128)S(1)} %get-tuple-element.38.part_ref, f32[37,8,128]{2,1,0:T(8,128)S(1)} %collective-permute-done.2.near_ref, ...), custom_call_target="tpu_custom_call" | custom-call | flops 110592000 | bytes 110592000 | tf_op jit(solution)/shard_map/pallas_call | solution.py:357
  17.7 0.0 collective-permute-done.4.far_ref
  17.7 0.0 copy-done.4
  17.7 0.0 copy-start.5
  17.7 0.0 copy-start.6
  17.8 0.8 %shard_map.59 = (f32[9,12,8,128]{3,2,1,0:T(8,128)S(1)}, f32[9,12,8,128]{3,2,1,0:T(8,128)S(1)}) custom-call(f32[9,12,8,128]{3,2,1,0:T(8,128)S(1)} %copy-done.1, f32[9,12,8,128]{3,2,1,0:T(8,128)S(1)} %shard_map.58.part_ref, f32[38,8,128]{2,1,0:T(8,128)S(1)} %collective-permute-done.x_near.near_ref, f32[36,8,128]{2,1,0:T(8,128)S(1)} %collective-permute-done.4.far_ref, ...), custom_call_target="tpu_custom_call" | custom-call | tf_op jit(solution)/shard_map/pallas_call | solution.py:357
  18.6 0.1 collective-permute-done.5.other_ref
  18.7 0.0 copy-done.5
  18.7 0.0 copy-done.6
  18.7 0.4 shard_map.60
  19.2 0.7 %collective-permute-start.6 = (f32[38,8,128]{2,1,0:T(8,128)S(1)}, f32[38,8,128]{2,1,0:T(8,128)S(1)}, u32[]{:S(2)}, u32[]{:S(2)}) collective-permute-start(f32[38,8,128]{2,1,0:T(8,128)S(1)} %get-tuple-element.50), channel_id=1, source_target_pairs={{1,2},{3,4},{5,6},{2,1},{4,3},{6,5},{0,0},{7,7},{9,10},{11,12},{13... | collective-permute-start | bytes 466952 | tf_op jit(solution)/shard_map/ppermute | solution.py:321
  19.8 0.1 collective-permute-start.7
  19.9 0.6 %collective-permute-start.8 = (f32[37,8,128]{2,1,0:T(8,128)S(1)}, f32[37,8,128]{2,1,0:T(8,128)S(1)}, u32[]{:S(2)}, u32[]{:S(2)}) collective-permute-start(f32[37,8,128]{2,1,0:T(8,128)S(1)} %get-tuple-element.53), channel_id=1, source_target_pairs={{8,16},{24,0},{16,8},{0,24},{9,17},{25,1},{17,9},{1,25},{10,18},{2... | collective-permute-start | bytes 454664 | tf_op jit(solution)/shard_map/ppermute | solution.py:321
  20.6 3.8 %collective-permute-start.9 = (f32[36,8,128]{2,1,0:T(8,128)S(1)}, f32[36,8,128]{2,1,0:T(8,128)S(1)}, u32[]{:S(2)}, u32[]{:S(2)}) collective-permute-start(f32[36,8,128]{2,1,0:T(8,128)S(1)} %get-tuple-element.54), channel_id=1, source_target_pairs={{0,1},{2,3},{4,5},{6,7},{1,0},{3,2},{5,4},{7,6},{8,9},{10,11},{12,... | collective-permute-start | bytes 442376 | tf_op jit(solution)/shard_map/ppermute | solution.py:321
  24.3 2.5 %shard_map.61 = (f32[9,12,8,128]{3,2,1,0:T(8,128)S(1)}, f32[9,12,8,128]{3,2,1,0:T(8,128)S(1)}) custom-call(f32[9,12,8,128]{3,2,1,0:T(8,128)S(1)} %get-tuple-element.46.s_ref, f32[9,2,128]{2,1,0:T(2,128)S(1)} %bitcast.5, f32[2,48,128]{2,1,0:T(8,128)S(1)} %copy-done.2, f32[8,128]{1,0:T(8,128)S(1)} %get-tuple-element.47.rest_0_.pk_ref), custom_call_target="tpu_custom_call" | custom-call | tf_op jit(solution)/shard_map/pallas_call | solution.py:357
  26.8 0.0 collective-permute-done.6.far_ref
  26.8 0.0 collective-permute-done.7.near_ref
  26.8 0.0 collective-permute-done.8.far_ref
  26.8 0.9 %shard_map.62.part_ref = f32[9,12,8,128]{3,2,1,0:T(8,128)S(1)} custom-call(f32[9,12,8,128]{3,2,1,0:T(8,128)S(1)} %get-tuple-element.46.s_ref, f32[9,12,8,128]{3,2,1,0:T(8,128)S(1)} %get-tuple-element.48.speed_ref, f32[9,12,8,128]{3,2,1,0:T(8,128)S(1)} %get-tuple-element.51.part_ref, f32[37,8,128]{2,1,0:T(8,128)S(1)} %collective-permute-done.7.near_ref, ...), custom_call_target="tpu_custom_call" | custom-call | flops 110592000 | bytes 110592000 | tf_op jit(solution)/shard_map/pallas_call | solution.py:357
  27.7 1.6 %collective-permute-done.9.near_ref = f32[36,8,128]{2,1,0:T(8,128)S(1)} collective-permute-done((f32[36,8,128]{2,1,0:T(8,128)S(1)}, f32[36,8,128]{2,1,0:T(8,128)S(1)}, u32[]{:S(2)}, u32[]{:S(2)}) %collective-permute-start.9) | collective-permute-done | bytes 147488 | tf_op jit(solution)/shard_map/ppermute | solution.py:321
  29.3 1.0 %shard_map.63 = (f32[9,12,8,128]{3,2,1,0:T(8,128)S(1)}, f32[36,8,128]{2,1,0:T(8,128)S(1)}, f32[38,8,128]{2,1,0:T(8,128)S(1)}, f32[37,8,128]{2,1,0:T(8,128)S(1)}, f32[37,8,128]{2,1,0:T(8,128)S(1)}) custom-call(f32[9,12,8,128]{3,2,1,0:T(8,128)S(1)} %copy-done.1, f32[9,12,8,128]{3,2,1,0:T(8,128)S(1)} %get-tuple-element.46.s_ref, ...), custom_call_target="tpu_custom_call" | custom-call | tf_op jit(solution)/shard_map/pallas_call | solution.py:357
  30.3 0.7 %collective-permute-start.10 = (f32[38,8,128]{2,1,0:T(8,128)S(1)}, f32[38,8,128]{2,1,0:T(8,128)S(1)}, u32[]{:S(2)}, u32[]{:S(2)}) collective-permute-start(f32[38,8,128]{2,1,0:T(8,128)S(1)} %get-tuple-element.59), channel_id=1, source_target_pairs={{1,2},{3,4},{5,6},{2,1},{4,3},{6,5},{0,0},{7,7},{9,10},{11,12},{13... | collective-permute-start | bytes 466952 | tf_op jit(solution)/shard_map/ppermute | solution.py:321
  31.0 0.1 collective-permute-start.11
  31.1 0.7 %collective-permute-start.12 = (f32[37,8,128]{2,1,0:T(8,128)S(1)}, f32[37,8,128]{2,1,0:T(8,128)S(1)}, u32[]{:S(2)}, u32[]{:S(2)}) collective-permute-start(f32[37,8,128]{2,1,0:T(8,128)S(1)} %get-tuple-element.62), channel_id=1, source_target_pairs={{8,16},{24,0},{16,8},{0,24},{9,17},{25,1},{17,9},{1,25},{10,18},{2... | collective-permute-start | bytes 454664 | tf_op jit(solution)/shard_map/ppermute | solution.py:321
  31.8 4.9 %collective-permute-start.13 = (f32[36,8,128]{2,1,0:T(8,128)S(1)}, f32[36,8,128]{2,1,0:T(8,128)S(1)}, u32[]{:S(2)}, u32[]{:S(2)}) collective-permute-start(f32[36,8,128]{2,1,0:T(8,128)S(1)} %get-tuple-element.63), channel_id=1, source_target_pairs={{0,1},{2,3},{4,5},{6,7},{1,0},{3,2},{5,4},{7,6},{8,9},{10,11},{12,... | collective-permute-start | bytes 442376 | tf_op jit(solution)/shard_map/ppermute | solution.py:321
  36.7 2.5 %shard_map.64 = (f32[9,12,8,128]{3,2,1,0:T(8,128)S(1)}, f32[9,12,8,128]{3,2,1,0:T(8,128)S(1)}) custom-call(f32[9,12,8,128]{3,2,1,0:T(8,128)S(1)} %get-tuple-element.56.s_ref, f32[9,2,128]{2,1,0:T(2,128)S(1)} %bitcast.7, f32[2,48,128]{2,1,0:T(8,128)S(1)} %copy-done.2, f32[8,128]{1,0:T(8,128)S(1)} %get-tuple-element.47.rest_0_.pk_ref), custom_call_target="tpu_custom_call" | custom-call | tf_op jit(solution)/shard_map/pallas_call | solution.py:357
  39.1 0.0 collective-permute-done.10.far_ref
  39.2 0.0 collective-permute-done.11.near_ref
  39.2 0.0 collective-permute-done.12.far_ref
  39.2 0.9 %shard_map.65.part_ref = f32[9,12,8,128]{3,2,1,0:T(8,128)S(1)} custom-call(f32[9,12,8,128]{3,2,1,0:T(8,128)S(1)} %get-tuple-element.56.s_ref, f32[9,12,8,128]{3,2,1,0:T(8,128)S(1)} %get-tuple-element.57.speed_ref, f32[9,12,8,128]{3,2,1,0:T(8,128)S(1)} %get-tuple-element.60.part_ref, f32[37,8,128]{2,1,0:T(8,128)S(1)} %collective-permute-done.11.near_ref, ...), custom_call_target="tpu_custom_call" | custom-call | flops 110592000 | bytes 110592000 | tf_op jit(solution)/shard_map/pallas_call | solution.py:357
  40.0 2.2 %collective-permute-done.13.near_ref = f32[36,8,128]{2,1,0:T(8,128)S(1)} collective-permute-done((f32[36,8,128]{2,1,0:T(8,128)S(1)}, f32[36,8,128]{2,1,0:T(8,128)S(1)}, u32[]{:S(2)}, u32[]{:S(2)}) %collective-permute-start.13) | collective-permute-done | bytes 147488 | tf_op jit(solution)/shard_map/ppermute | solution.py:321
  42.2 1.7 %shard_map.66 = f32[9,12,8,128]{3,2,1,0:T(8,128)} custom-call(f32[9,12,8,128]{3,2,1,0:T(8,128)S(1)} %copy-done.1, f32[9,12,8,128]{3,2,1,0:T(8,128)S(1)} %get-tuple-element.56.s_ref, f32[9,12,8,128]{3,2,1,0:T(8,128)S(1)} %shard_map.65.part_ref, f32[36,8,128]{2,1,0:T(8,128)S(1)} %collective-permute-done.13.near_ref, ...), custom_call_target="tpu_custom_call" | custom-call | tf_op jit(solution)/shard_map/pallas_call | solution.py:357
  (3 shorter events, 0.1 us)
Async XLA Ops:
  0.0 1.0 %copy-start = (f32[9,12,8,128]{3,2,1,0:T(8,128)S(1)}, f32[9,12,8,128]{3,2,1,0:T(8,128)}, u32[]{:S(2)}) copy-start(f32[9,12,8,128]{3,2,1,0:T(8,128)} %base_ref.3) | copy-start | bytes 1327108
  1.0 0.7 %copy-start.3 = (f32[2,9,128]{2,0,1:T(2,128)S(1)}, f32[2,9,128]{2,0,1:T(2,128)}, u32[]{:S(2)}) copy-start(f32[2,9,128]{2,0,1:T(2,128)} %param.6) | copy-start | bytes 27652
  1.7 9.0 %copy-start.1 = (f32[9,12,8,128]{3,2,1,0:T(8,128)S(1)}, f32[9,12,8,128]{3,2,1,0:T(8,128)}, u32[]{:S(2)}) copy-start(f32[9,12,8,128]{3,2,1,0:T(8,128)} %base_ref.3) | copy-start | bytes 1327108
  1.8 7.1 %collective-permute-start = (f32[38,8,128]{2,1,0:T(8,128)S(1)}, f32[38,8,128]{2,1,0:T(8,128)S(1)}, u32[]{:S(2)}, u32[]{:S(2)}) collective-permute-start(f32[38,8,128]{2,1,0:T(8,128)S(1)} %get-tuple-element.36), channel_id=1, source_target_pairs={{0,1},{2,3},{4,5},{6,7},{1,0},{3,2},{5,4},{7,6},{8,9},{10,11},{12,... | collective-permute-start | bytes 466952 | tf_op jit(solution)/shard_map/ppermute | solution.py:321
  4.8 12.0 %collective-permute-start.2 = (f32[37,8,128]{2,1,0:T(8,128)S(1)}, f32[37,8,128]{2,1,0:T(8,128)S(1)}, u32[]{:S(2)}, u32[]{:S(2)}) collective-permute-start(f32[37,8,128]{2,1,0:T(8,128)S(1)} %get-tuple-element.39), channel_id=1, source_target_pairs={{0,8},{16,24},{8,0},{24,16},{1,9},{17,25},{9,1},{25,17},{2,10},{18... | collective-permute-start | bytes 454664 | tf_op jit(solution)/shard_map/ppermute | solution.py:321
  4.8 12.0 %collective-permute-start.3 = (f32[37,8,128]{2,1,0:T(8,128)S(1)}, f32[37,8,128]{2,1,0:T(8,128)S(1)}, u32[]{:S(2)}, u32[]{:S(2)}) collective-permute-start(f32[37,8,128]{2,1,0:T(8,128)S(1)} %get-tuple-element.40), channel_id=1, source_target_pairs={{8,16},{24,0},{16,8},{0,24},{9,17},{25,1},{17,9},{1,25},{10,18},{2... | collective-permute-start | bytes 454664 | tf_op jit(solution)/shard_map/ppermute | solution.py:321
  6.4 4.3 %copy-start.2 = (f32[2,48,128]{2,1,0:T(8,128)S(1)}, f32[2,48,128]{2,1,0:T(8,128)}, u32[]{:S(2)}) copy-start(f32[2,48,128]{2,1,0:T(8,128)} %constant.2.clone.waves_ref) | copy-start | bytes 147460
  6.4 11.3 %collective-permute-start.4 = (f32[36,8,128]{2,1,0:T(8,128)S(1)}, f32[36,8,128]{2,1,0:T(8,128)S(1)}, u32[]{:S(2)}, u32[]{:S(2)}) collective-permute-start(f32[36,8,128]{2,1,0:T(8,128)S(1)} %get-tuple-element.41), channel_id=1, source_target_pairs={{1,2},{3,4},{5,6},{2,1},{4,3},{6,5},{0,0},{7,7},{9,10},{11,12},{13... | collective-permute-start | bytes 442376 | tf_op jit(solution)/shard_map/ppermute | solution.py:321
  8.8 5.4 %collective-permute-start.1 = (f32[8,128]{1,0:T(8,128)S(1)}, f32[8,128]{1,0:T(8,128)S(1)}, u32[]{:S(2)}, u32[]{:S(2)}) collective-permute-start(f32[8,128]{1,0:T(8,128)S(1)} %shard_map.57), channel_id=1, source_target_pairs={{0,2},{1,3},{2,0},{3,1},{4,6},{5,7},{6,4},{7,5},{8,10},{9,11},{10,... | collective-permute-start | bytes 12296 | tf_op jit(solution)/shard_map/ppermute | solution.py:386
  14.2 4.5 %collective-permute-start.5 = (f32[8,128]{1,0:T(8,128)S(1)}, f32[8,128]{1,0:T(8,128)S(1)}, u32[]{:S(2)}, u32[]{:S(2)}) collective-permute-start(f32[8,128]{1,0:T(8,128)S(1)} %max.3.most_ref), channel_id=1, source_target_pairs={{0,4},{1,5},{2,6},{3,7},{4,0},{5,1},{6,2},{7,3},{8,12},{9,13},{10,... | collective-permute-start | bytes 12296 | tf_op jit(solution)/shard_map/ppermute | solution.py:386
  16.9 0.9 %copy-start.4 = (f32[2,9,128]{2,0,1:T(2,128)S(1)}, f32[2,9,128]{2,0,1:T(2,128)}, u32[]{:S(2)}) copy-start(f32[2,9,128]{2,0,1:T(2,128)} %param.6) | copy-start | bytes 27652
  17.7 1.0 %copy-start.5 = (s32[9,128]{1,0:T(8,128)S(1)}, s32[9,128]{1,0:T(8,128)}, u32[]{:S(2)}) copy-start(s32[9,128]{1,0:T(8,128)} %mask_ref.5) | copy-start | bytes 13828
  17.7 1.0 %copy-start.6 = (f32[9,128]{1,0:T(8,128)S(1)}, f32[9,128]{1,0:T(8,128)}, u32[]{:S(2)}) copy-start(f32[9,128]{1,0:T(8,128)} %depth_ref.5) | copy-start | bytes 13828
  19.2 7.6 %collective-permute-start.6 = (f32[38,8,128]{2,1,0:T(8,128)S(1)}, f32[38,8,128]{2,1,0:T(8,128)S(1)}, u32[]{:S(2)}, u32[]{:S(2)}) collective-permute-start(f32[38,8,128]{2,1,0:T(8,128)S(1)} %get-tuple-element.50), channel_id=1, source_target_pairs={{1,2},{3,4},{5,6},{2,1},{4,3},{6,5},{0,0},{7,7},{9,10},{11,12},{13... | collective-permute-start | bytes 466952 | tf_op jit(solution)/shard_map/ppermute | solution.py:321
  19.8 7.0 %collective-permute-start.7 = (f32[37,8,128]{2,1,0:T(8,128)S(1)}, f32[37,8,128]{2,1,0:T(8,128)S(1)}, u32[]{:S(2)}, u32[]{:S(2)}) collective-permute-start(f32[37,8,128]{2,1,0:T(8,128)S(1)} %get-tuple-element.52), channel_id=1, source_target_pairs={{0,8},{16,24},{8,0},{24,16},{1,9},{17,25},{9,1},{25,17},{2,10},{18... | collective-permute-start | bytes 454664 | tf_op jit(solution)/shard_map/ppermute | solution.py:321
  19.9 6.9 %collective-permute-start.8 = (f32[37,8,128]{2,1,0:T(8,128)S(1)}, f32[37,8,128]{2,1,0:T(8,128)S(1)}, u32[]{:S(2)}, u32[]{:S(2)}) collective-permute-start(f32[37,8,128]{2,1,0:T(8,128)S(1)} %get-tuple-element.53), channel_id=1, source_target_pairs={{8,16},{24,0},{16,8},{0,24},{9,17},{25,1},{17,9},{1,25},{10,18},{2... | collective-permute-start | bytes 454664 | tf_op jit(solution)/shard_map/ppermute | solution.py:321
  20.6 8.8 %collective-permute-start.9 = (f32[36,8,128]{2,1,0:T(8,128)S(1)}, f32[36,8,128]{2,1,0:T(8,128)S(1)}, u32[]{:S(2)}, u32[]{:S(2)}) collective-permute-start(f32[36,8,128]{2,1,0:T(8,128)S(1)} %get-tuple-element.54), channel_id=1, source_target_pairs={{0,1},{2,3},{4,5},{6,7},{1,0},{3,2},{5,4},{7,6},{8,9},{10,11},{12,... | collective-permute-start | bytes 442376 | tf_op jit(solution)/shard_map/ppermute | solution.py:321
  30.3 8.8 %collective-permute-start.10 = (f32[38,8,128]{2,1,0:T(8,128)S(1)}, f32[38,8,128]{2,1,0:T(8,128)S(1)}, u32[]{:S(2)}, u32[]{:S(2)}) collective-permute-start(f32[38,8,128]{2,1,0:T(8,128)S(1)} %get-tuple-element.59), channel_id=1, source_target_pairs={{1,2},{3,4},{5,6},{2,1},{4,3},{6,5},{0,0},{7,7},{9,10},{11,12},{13... | collective-permute-start | bytes 466952 | tf_op jit(solution)/shard_map/ppermute | solution.py:321
  31.0 8.1 %collective-permute-start.11 = (f32[37,8,128]{2,1,0:T(8,128)S(1)}, f32[37,8,128]{2,1,0:T(8,128)S(1)}, u32[]{:S(2)}, u32[]{:S(2)}) collective-permute-start(f32[37,8,128]{2,1,0:T(8,128)S(1)} %get-tuple-element.61), channel_id=1, source_target_pairs={{0,8},{16,24},{8,0},{24,16},{1,9},{17,25},{9,1},{25,17},{2,10},{18... | collective-permute-start | bytes 454664 | tf_op jit(solution)/shard_map/ppermute | solution.py:321
  31.1 8.1 %collective-permute-start.12 = (f32[37,8,128]{2,1,0:T(8,128)S(1)}, f32[37,8,128]{2,1,0:T(8,128)S(1)}, u32[]{:S(2)}, u32[]{:S(2)}) collective-permute-start(f32[37,8,128]{2,1,0:T(8,128)S(1)} %get-tuple-element.62), channel_id=1, source_target_pairs={{8,16},{24,0},{16,8},{0,24},{9,17},{25,1},{17,9},{1,25},{10,18},{2... | collective-permute-start | bytes 454664 | tf_op jit(solution)/shard_map/ppermute | solution.py:321
  31.8 10.5 %collective-permute-start.13 = (f32[36,8,128]{2,1,0:T(8,128)S(1)}, f32[36,8,128]{2,1,0:T(8,128)S(1)}, u32[]{:S(2)}, u32[]{:S(2)}) collective-permute-start(f32[36,8,128]{2,1,0:T(8,128)S(1)} %get-tuple-element.63), channel_id=1, source_target_pairs={{0,1},{2,3},{4,5},{6,7},{1,0},{3,2},{5,4},{7,6},{8,9},{10,11},{12,... | collective-permute-start | bytes 442376 | tf_op jit(solution)/shard_map/ppermute | solution.py:321

commit v9 on v8

--- a/solution.py
+++ b/solution.py
@@ -84,9 +84,14 @@
     most_ref[2:4, :] = -functools.reduce(jnp.minimum, rows)
 
 
-def opening_kernel(level_ref, wind_ref, x_near, *others):
+def near_kernel(level_ref, wind_ref, x_near):
     put_extremes(wind_ref, x_near.at[x_near.shape[0] - 1])
-    cut_edges(level_ref, x_near, *others)
+    cut_near(level_ref, x_near)
+
+
+def far_kernel(level_ref, x_far, t_near, t_far):
+    cut_far(level_ref, x_far)
+    cut_headings(level_ref, t_near, t_far)
 
 
 def meeting_kernel(wind_ref, x_near, most_ref):
@@ -205,13 +210,35 @@
         pk_ref[row : row + 1, :] = splat(value, (1, width))
 
 
-def cut_edges(field_ref, x_near, x_far, t_near, t_far):
+def plane_at(i, planes):
+    return jnp.where(odd_place("gx"), i, planes - 1 - i)
+
+
+def alone(reach):
+    place, size = lax.axis_index("gx"), lax.axis_size("gx")
+    if reach == 0:
+        return (place == size - 1) if size % 2 else place < 0
+    return (place == 0) | (place == size - 1) if size % 2 == 0 else place == 0
+
+
+def cut_near(field_ref, x_near):
     planes, headings = field_ref.shape[:2]
-    x_low = jnp.where(odd_place("gx"), 0, planes - rim)
+    for k in range(rim):
+        i = jnp.where(alone(0), 0, k)
+        x_near[k * headings : (k + 1) * headings] = field_ref[plane_at(i, planes)]
+
+
+def cut_far(field_ref, x_far):
+    planes, headings = field_ref.shape[:2]
+    for k in range(rim):
+        i = planes - 1 - jnp.where(alone(1), 0, k)
+        x_far[k * headings : (k + 1) * headings] = field_ref[plane_at(i, planes)]
+
+
+def cut_headings(field_ref, t_near, t_far):
+    planes, headings = field_ref.shape[:2]
     t_low = jnp.where(odd_place("head"), 0, headings - rim)
     for k in range(rim):
-        x_near[k * headings : (k + 1) * headings] = field_ref[x_low + k]
-        x_far[k * headings : (k + 1) * headings] = field_ref[planes - rim - x_low + k]
         for i in range(planes):
             t_near[i * rim + k] = field_ref[i, t_low + k]
             t_far[i * rim + k] = field_ref[i, headings - rim - t_low + k]
@@ -224,27 +251,35 @@
         target_ref[i] = splat(target, target_ref.shape[1:])
 
 
-def across_planes(wide, speed_step, s_ref, near_ref, far_ref, wind_ref, waves_ref, flow_ref, use):
+def across_planes(
+    span, speed_step, s_ref, near_ref, far_ref, wind_ref, waves_ref, flow_ref, use
+):
     planes, headings = s_ref.shape[:2]
     tile = s_ref.shape[2:]
+    side = jnp.where(odd_place("gx"), gain, -gain).astype(jnp.float32)
+    spots = [plane_at(i, planes) for i in range(planes)]
     for i in range(planes):
-        flow_ref[i] = splat(wind_ref[i, 0:1, :] * gain, tile)
-    odd = odd_place("gx")
-    at_low = lax.axis_index("gx") == 0
-    at_high = lax.axis_index("gx") == lax.axis_size("gx") - 1
-    pace = speeds_of(tile, speed_step) * gain
+        flow_ref[i] = splat(wind_ref[i, 0:1, :] * side, tile)
+    pace = speeds_of(tile, speed_step) * side
     first = lax.axis_index("head") * headings
+    low, high = span
+    wide = batches(headings, max(1, 54 // (high - low)))
+
+    def line(i, j):
+        if i < 0:
+            return near_ref[(-1 - i) * headings + j]
+        if i >= planes:
+            return far_ref[(i - planes) * headings + j]
+        return s_ref[spots[i], j]
 
     def step(n, carry):
         for w in range(wide):
             j = n * wide + w
-            cells = [s_ref[i, j] for i in range(planes)]
-            ghosts = [(near_ref[k * headings + j], far_ref[k * headings + j]) for k in range(rim)]
-            lows = [jnp.where(at_low, cells[0], jnp.where(odd, near, far)) for near, far in ghosts]
-            highs = [jnp.where(at_high, cells[-1], jnp.where(odd, far, near)) for near, far in ghosts]
+            cells = [line(i, j) for i in range(low - rim, high + rim)]
             table = splat(waves_ref[0, pl.ds(first + j, 1), :], tile) * pace
-            for i, (mean, gap) in enumerate(row_terms(lows + cells + highs, spacing)):
-                use(i, j, mean * (table + flow_ref[i]), gap, cells[i])
+            for k, (mean, gap) in enumerate(row_terms(cells, spacing)):
+                spot = spots[low + k]
+                use(spot, j, mean * (table + flow_ref[spot]), gap, cells[k + rim])
         return carry
 
     lax.fori_loop(0, headings // wide, step, 0)
@@ -257,9 +292,8 @@
         out_ref[i, j] = part_ref[i, j] + drift
         gap_ref[i, j] = gap
 
-    wide = batches(s_ref.shape[1], 6)
     across_planes(
-        wide, speed_step, s_ref, near_ref, far_ref, wind_ref, waves_ref, flow_ref, use
+        (0, s_ref.shape[0]), speed_step, s_ref, near_ref, far_ref, wind_ref, waves_ref, flow_ref, use
     )
 
 
@@ -283,14 +317,19 @@
         return carry
 
     lax.fori_loop(0, planes, plane, 0)
-    cut_edges(out_ref, x_near, x_far, t_near, t_far)
+    cut_near(out_ref, x_near)
+    cut_far(out_ref, x_far)
+    cut_headings(out_ref, t_near, t_far)
 
 
 def section_kernel(
-    section, speed_step, base_ref, s_ref, part_ref, near_ref, far_ref, wind_ref, waves_ref,
-    mask_ref, depth_ref, pk_ref, out_ref, *refs
+    section, span, speed_step, base_ref, s_ref, part_ref, ghosts_ref, wind_ref, waves_ref,
+    mask_ref, depth_ref, pk_ref, *refs
 ):
-    edge_refs, (flow_ref, target_ref) = refs[:-2], refs[-2:]
+    planes = s_ref.shape[0]
+    refs, (flow_ref, target_ref) = list(refs[:-2]), refs[-2:]
+    early_ref = refs.pop(0) if span[0] > 0 else None
+    out_ref = refs.pop(0)
     tile = s_ref.shape[2:]
     splat_targets(mask_ref, depth_ref, target_ref)
     peak_x = splat(pk_ref[0:1, :] * gain, tile)
@@ -303,12 +342,18 @@
         moved = base_share * base_ref[i, j] + own_share * (cell + time_step * rate)
         out_ref[i, j] = jnp.minimum(moved, target_ref[i])
 
-    wide = batches(s_ref.shape[1], 6)
+    near_ref, far_ref = (None, ghosts_ref) if span[0] > 0 else (ghosts_ref, None)
     across_planes(
-        wide, speed_step, s_ref, near_ref, far_ref, wind_ref, waves_ref, flow_ref, use
+        span, speed_step, s_ref, near_ref, far_ref, wind_ref, waves_ref, flow_ref, use
     )
-    if section == 2:
-        cut_edges(out_ref, *edge_refs)
+    for i in range(span[0]):
+        spot = plane_at(i, planes)
+        out_ref[spot] = early_ref[spot]
+    if section == 2 and span[0] == 0:
+        cut_near(out_ref, *refs)
+    elif section == 2:
+        cut_far(out_ref, refs[0])
+        cut_headings(out_ref, *refs[1:])
 
 
 def trade(value, axis, reach, wrap=False):
@@ -347,9 +392,7 @@
     short = rim * headings
     middle = max(short + 1, rim * planes)
 
-    longest, t_shapes = middle + 1, [shape(middle)] * 2
-    first_edges = [shape(longest), shape(short)] + t_shapes
-    later_edges = [shape(short), shape(longest)] + t_shapes
+    longest = middle + 1
     rows = pltpu.VMEM((planes,) + tile, jnp.float32)
     cells = math.prod(level_set.shape)
 
@@ -375,6 +418,68 @@
         pltpu.VMEM((groups, cross_count, lanes), jnp.float32),
         pltpu.VMEM(level_set.shape, jnp.float32),
     ]
+    values = level_set
+    size = lax.axis_size(axis)
+    pairs = [(i, i + 1) for i in range(reach, size - 1, 2)]
+    if wrap and reach and size % 2 == 0:
+        pairs.append((size - 1, 0))
+    pairs += [(j, i) for i, j in pairs]
+    pairs += [(i, i) for i in range(size) if i not in dict(pairs)]
+    return lax.ppermute(value, axis, pairs)
+
+
+def local(level_set, wind_field, target_mask, target_depth):
+    planes, headings, speed_count, cross_count = level_set.shape
+    heading_total = headings * lax.axis_size("head")
+    heading_step = 2.0 * math.pi / heading_total
+    speed_step = (speed_high - speed_low) / (speed_count - 1)
+    speed_row = np.float32(speed_low) + np.arange(speed_count, dtype=np.float32) * np.float32(
+        speed_step
+    )
+    angles = np.arange(heading_total, dtype=np.float32) * np.float32(heading_step)
+    waves = [np.cos(angles), np.sin(angles)]
+    bounds = []
+    for wave in waves:
+        product = wave[:, None] * speed_row[None, :]
+        bounds.append((float(product.min()), float(product.max())))
+    waves = jnp.asarray(np.stack(waves)[..., None] * np.ones(cross_count, np.float32))
+
+    vmem = pl.BlockSpec(memory_space=pltpu.VMEM)
+    tile = (speed_count, cross_count)
+
+    def shape(*dims):
+        return jax.ShapeDtypeStruct(dims + tile, jnp.float32)
+
+    field = shape(planes, headings)
+    short = rim * headings
+    middle = max(short + 1, rim * planes)
+
+    longest = middle + 1
+    rows = pltpu.VMEM((planes,) + tile, jnp.float32)
+    cells = math.prod(level_set.shape)
+
+    def call(kernel, ins, outs, scratch=(), work=0):
+        return pl.pallas_call(
+            kernel,
+            out_shape=outs,
+            in_specs=[vmem] * len(ins),
+            out_specs=[vmem] * len(outs),
+            scratch_shapes=list(scratch),
+            compiler_params=pltpu.CompilerParams(vmem_limit_bytes=16 * 1024 * 1024),
+            cost_estimate=pl.CostEstimate(
+                flops=work * cells, bytes_accessed=work * cells, transcendentals=0
+            ),
+        )(*ins)
+
+    wind = jnp.transpose(wind_field, (1, 0, 2))
+    many = 16
+    groups, lanes = -(-planes * headings // many), many * speed_count
+    room = [
+        pltpu.VMEM((groups, cross_count + 8, lanes), jnp.float32),
+        pltpu.VMEM((groups, cross_count, lanes), jnp.float32),
+        pltpu.VMEM((groups, cross_count, lanes), jnp.float32),
+        pltpu.VMEM(level_set.shape, jnp.float32),
+    ]
     values, pk = level_set, None
     size = lax.axis_size("gx")
 
@@ -385,10 +490,12 @@
             pairs = [(i, i ^ reach) for i in range(size)]
         return lax.ppermute(most, "gx", pairs)
 
-    edges = call(opening_kernel, [values, wind], first_edges)
+    far_shapes = [shape(short), shape(longest + 1), shape(longest + 1)]
+    x_last, t_out, t_last = call(far_kernel, [values], far_shapes)
+    (x_out,) = call(near_kernel, [values, wind], [shape(longest)])
+    far_shapes = [shape(short), shape(middle), shape(middle)]
     for section in (1, 2, 3):
         opening = section == 1
-        x_out, x_last, t_out, t_last = edges
         x_near = trade(x_out, "gx", 0)
         t_near = trade(t_out, "head", 0)
         t_far = trade(t_last, "head", 1, True)
@@ -407,8 +514,8 @@
                 other = spread(most, reach)
                 reach *= 2
         else:
+            values, x_near = lax.optimization_barrier((values, x_near))
             spun, part = call(free, [values, wind, waves, pk], [field] * 2, room)
-            part, x_far = lax.optimization_barrier((part, x_far))
         (part,) = call(turning, [values, spun, part, t_near, t_far], [field], work=1000)
         if opening:
             ins = [values, part, x_near, x_far, wind, waves]
@@ -416,13 +523,20 @@
             part, gap = call(first, ins, [field] * 2, [rows])
             closing = functools.partial(closing_kernel, bounds, heading_step, speed_step)
             ins = [values, part, gap, extra, target_mask, target_depth, most, other]
-            values, *edges, pk = call(closing, ins, [field, *later_edges, shape()], [rows])
+            outs = [field, shape(longest), *far_shapes, shape()]
+            values, x_out, x_last, t_out, t_last, pk = call(closing, ins, outs, [rows])
         else:
-            ins = [level_set, values, part, x_near, x_far, wind, waves]
-            ins += [target_mask, target_depth, pk]
-            outs = [field] + (later_edges if section == 2 else [])
-            last = functools.partial(section_kernel, section, speed_step)
-            values, *edges = call(last, ins, outs, [rows, rows])
+            more = section == 2
+            ins = [level_set, values, part, x_near, wind, waves, target_mask, target_depth, pk]
+            outs = [field] + ([shape(longest)] if more else [])
+            last = functools.partial(section_kernel, section, (0, planes - rim), speed_step)
+            early, *x_next = call(last, ins, outs, [rows, rows])
+            ins = ins[:3] + [x_far] + ins[4:] + [early]
+            outs = [field] + (far_shapes if more else [])
+            last = functools.partial(section_kernel, section, (planes - rim, planes), speed_step)
+            values, *far_next = call(last, ins, outs, [rows, rows])
+            if more:
+                (x_out,), (x_last, t_out, t_last) = x_next, far_next
     return values
 
 

time: 44.2 us -> 41.3 us (0.934)
  the two profiles are of different devices: /device:TPU:0 before, /device:TPU:16 now
where the time goes in v9:
time: 41.3 us; the launch traced here: 41.1 us
  starting transfers between devices  17.2 us (42%)
  Pallas kernels  14.3 us (35%)
  waiting for transfers between devices  7.62 us (18%)
  local copies, waits for them, and re-layouts  1.74 us (4%)
    ppermute x12, starting transfers between devices, trade(): return lax.ppermute(value, axis, pairs)  15.3 us
    pallas_call x15, Pallas kernels, call(): pl.pallas_call(kernel, out_shape=outs, in_specs=[vmem] * len(ins), out_sp...  14.3 us
    ppermute x12, waiting for transfers between devices, trade(): return lax.ppermute(value, axis, pairs)  3.93 us
    ppermute x2, waiting for transfers between devices, spread(): return lax.ppermute(most, 'gx', pairs)  3.69 us
    ppermute x2, starting transfers between devices, spread(): return lax.ppermute(most, 'gx', pairs)  1.93 us
    unnamed x14, local copies, waits for them, and re-layouts  1.74 us
  transfers between devices with their start and end apart: 14, of which 5 were waited for; matrix products, arithmetic and copies ran while one was open for 0% of the time, Pallas kernels for 31%

profile of v9, /device:TPU:16, one launch (start us, length us, event | category | flops | bytes accessed | tf_op | source)
XLA Modules:
  0.0 41.1 jit_solution(14132321550057319362)
XLA Ops:
  0.0 0.0 copy-start
  0.0 1.0 %copy-done = f32[9,12,8,128]{3,2,1,0:T(8,128)S(1)} copy-done((f32[9,12,8,128]{3,2,1,0:T(8,128)S(1)}, f32[9,12,8,128]{3,2,1,0:T(8,128)}, u32[]{:S(2)}) %copy-start) | copy-done | bytes 442392
  1.0 0.0 copy-start.3
  1.0 0.7 %copy-done.3 = f32[2,9,128]{2,0,1:T(2,128)S(1)} copy-done((f32[2,9,128]{2,0,1:T(2,128)S(1)}, f32[2,9,128]{2,0,1:T(2,128)}, u32[]{:S(2)}) %copy-start.3) | copy-done | bytes 9240
  1.7 0.0 copy-start.4
  1.7 0.0 copy-start.1
  1.8 1.6 %collective-permute-start = (f32[38,8,128]{2,1,0:T(8,128)S(1)}, f32[38,8,128]{2,1,0:T(8,128)S(1)}, u32[]{:S(2)}, u32[]{:S(2)}) collective-permute-start(f32[38,8,128]{2,1,0:T(8,128)S(1)} %shard_map.56), channel_id=1, source_target_pairs={{0,1},{2,3},{4,5},{6,7},{1,0},{3,2},{5,4},{7,6},{8,9},{10,11},{12,... | collective-permute-start | bytes 466952 | tf_op jit(solution)/shard_map/ppermute | solution.py:366
  3.4 0.1 collective-permute-start.2
  3.4 1.6 %collective-permute-start.3 = (f32[39,8,128]{2,1,0:T(8,128)S(1)}, f32[39,8,128]{2,1,0:T(8,128)S(1)}, u32[]{:S(2)}, u32[]{:S(2)}) collective-permute-start(f32[39,8,128]{2,1,0:T(8,128)S(1)} %get-tuple-element.39), channel_id=1, source_target_pairs={{8,16},{24,0},{16,8},{0,24},{9,17},{25,1},{17,9},{1,25},{10,18},{2... | collective-permute-start | bytes 479240 | tf_op jit(solution)/shard_map/ppermute | solution.py:366
  5.1 0.0 copy-start.2
  5.1 2.4 %collective-permute-start.4 = (f32[36,8,128]{2,1,0:T(8,128)S(1)}, f32[36,8,128]{2,1,0:T(8,128)S(1)}, u32[]{:S(2)}, u32[]{:S(2)}) collective-permute-start(f32[36,8,128]{2,1,0:T(8,128)S(1)} %get-tuple-element.40), channel_id=1, source_target_pairs={{1,2},{3,4},{5,6},{2,1},{4,3},{6,5},{0,0},{7,7},{9,10},{11,12},{13... | collective-permute-start | bytes 442376 | tf_op jit(solution)/shard_map/ppermute | solution.py:366
  7.5 0.1 collective-permute-done.x_near.near_ref
  7.6 0.0 copy-done.4
  7.6 1.6 %collective-permute-start.1 = (f32[8,128]{1,0:T(8,128)S(1)}, f32[8,128]{1,0:T(8,128)S(1)}, u32[]{:S(2)}, u32[]{:S(2)}) collective-permute-start(f32[8,128]{1,0:T(8,128)S(1)} %shard_map.57), channel_id=1, source_target_pairs={{0,2},{1,3},{2,0},{3,1},{4,6},{5,7},{6,4},{7,5},{8,10},{9,11},{10,... | collective-permute-start | bytes 12296 | tf_op jit(solution)/shard_map/ppermute | solution.py:491
  9.2 0.0 copy-done.1
  9.2 0.0 copy-done.2
  9.2 2.5 %shard_map.55 = (f32[9,12,8,128]{3,2,1,0:T(8,128)S(1)}, f32[9,12,8,128]{3,2,1,0:T(8,128)S(1)}, f32[9,12,8,128]{3,2,1,0:T(8,128)S(1)}) custom-call(f32[9,12,8,128]{3,2,1,0:T(8,128)S(1)} %copy-done.1, f32[9,2,128]{2,1,0:T(2,128)S(1)} %bitcast.3, f32[2,48,128]{2,1,0:T(8,128)S(1)} %copy-done.2), custom_call_target="tpu_custom_call" | custom-call | flops 33177600 | bytes 33177600 | tf_op jit(solution)/shard_map/pallas_call | solution.py:462
  11.7 1.3 %collective-permute-done.1 = f32[8,128]{1,0:T(8,128)S(1)} collective-permute-done((f32[8,128]{1,0:T(8,128)S(1)}, f32[8,128]{1,0:T(8,128)S(1)}, u32[]{:S(2)}, u32[]{:S(2)}) %collective-permute-start.1) | collective-permute-done | bytes 4128 | tf_op jit(solution)/shard_map/ppermute | solution.py:491
  13.0 0.3 collective-permute-start.5
  13.3 0.0 collective-permute-done.2.near_ref
  13.3 0.0 collective-permute-done.3.far_ref
  13.3 0.8 %shard_map.59.part_ref = f32[9,12,8,128]{3,2,1,0:T(8,128)S(1)} custom-call(f32[9,12,8,128]{3,2,1,0:T(8,128)S(1)} %copy-done.1, f32[9,12,8,128]{3,2,1,0:T(8,128)S(1)} %get-tuple-element.35.speed_ref, f32[9,12,8,128]{3,2,1,0:T(8,128)S(1)} %get-tuple-element.37.part_ref, f32[39,8,128]{2,1,0:T(8,128)S(1)} %collective-permute-done.2.near_ref, ...), custom_call_target="tpu_custom_call" | custom-call | flops 110592000 | bytes 110592000 | tf_op jit(solution)/shard_map/pallas_call | solution.py:462
  14.1 0.0 collective-permute-done.4.far_ref
  14.1 0.0 copy-start.5
  14.1 0.0 copy-start.6
  14.1 0.9 %shard_map.60 = (f32[9,12,8,128]{3,2,1,0:T(8,128)S(1)}, f32[9,12,8,128]{3,2,1,0:T(8,128)S(1)}) custom-call(f32[9,12,8,128]{3,2,1,0:T(8,128)S(1)} %copy-done.1, f32[9,12,8,128]{3,2,1,0:T(8,128)S(1)} %shard_map.59.part_ref, f32[38,8,128]{2,1,0:T(8,128)S(1)} %collective-permute-done.x_near.near_ref, f32[36,8,128]{2,1,0:T(8,128)S(1)} %collective-permute-done.4.far_ref, ...), custom_call_target="tpu_custom_call" | custom-call | tf_op jit(solution)/shard_map/pallas_call | solution.py:462
  15.0 2.4 %collective-permute-done.5.other_ref = f32[8,128]{1,0:T(8,128)S(1)} collective-permute-done((f32[8,128]{1,0:T(8,128)S(1)}, f32[8,128]{1,0:T(8,128)S(1)}, u32[]{:S(2)}, u32[]{:S(2)}) %collective-permute-start.5) | collective-permute-done | bytes 4128 | tf_op jit(solution)/shard_map/ppermute | solution.py:491
  17.5 0.0 copy-done.5
  17.5 0.0 copy-done.6
  17.5 0.4 %shard_map.61 = (f32[9,12,8,128]{3,2,1,0:T(8,128)S(1)}, f32[38,8,128]{2,1,0:T(8,128)S(1)}, f32[36,8,128]{2,1,0:T(8,128)S(1)}, f32[37,8,128]{2,1,0:T(8,128)S(1)},...) custom-call(f32[9,12,8,128]{3,2,1,0:T(8,128)S(1)} %copy-done.1, f32[9,12,8,128]{3,2,1,0:T(8,128)S(1)} %get-tuple-element.41.part_ref, ...), custom_call_target="tpu_custom_call" | custom-call | tf_op jit(solution)/shard_map/pallas_call | solution.py:462
  17.9 0.9 %collective-permute-start.6 = (f32[38,8,128]{2,1,0:T(8,128)S(1)}, f32[38,8,128]{2,1,0:T(8,128)S(1)}, u32[]{:S(2)}, u32[]{:S(2)}) collective-permute-start(f32[38,8,128]{2,1,0:T(8,128)S(1)} %get-tuple-element.46), channel_id=1, source_target_pairs={{0,1},{2,3},{4,5},{6,7},{1,0},{3,2},{5,4},{7,6},{8,9},{10,11},{12,... | collective-permute-start | bytes 466952 | tf_op jit(solution)/shard_map/ppermute | solution.py:366
  18.9 0.0 collective-permute-start.7
  18.9 1.1 %collective-permute-start.8 = (f32[37,8,128]{2,1,0:T(8,128)S(1)}, f32[37,8,128]{2,1,0:T(8,128)S(1)}, u32[]{:S(2)}, u32[]{:S(2)}) collective-permute-start(f32[37,8,128]{2,1,0:T(8,128)S(1)} %get-tuple-element.52), channel_id=1, source_target_pairs={{8,16},{24,0},{16,8},{0,24},{9,17},{25,1},{17,9},{1,25},{10,18},{2... | collective-permute-start | bytes 454664 | tf_op jit(solution)/shard_map/ppermute | solution.py:366
  19.9 2.0 %collective-permute-start.9 = (f32[36,8,128]{2,1,0:T(8,128)S(1)}, f32[36,8,128]{2,1,0:T(8,128)S(1)}, u32[]{:S(2)}, u32[]{:S(2)}) collective-permute-start(f32[36,8,128]{2,1,0:T(8,128)S(1)} %get-tuple-element.53), channel_id=1, source_target_pairs={{1,2},{3,4},{5,6},{2,1},{4,3},{6,5},{0,0},{7,7},{9,10},{11,12},{13... | collective-permute-start | bytes 442376 | tf_op jit(solution)/shard_map/ppermute | solution.py:366
  22.0 1.2 %collective-permute-done.6.ghosts_ref = f32[38,8,128]{2,1,0:T(8,128)S(1)} collective-permute-done((f32[38,8,128]{2,1,0:T(8,128)S(1)}, f32[38,8,128]{2,1,0:T(8,128)S(1)}, u32[]{:S(2)}, u32[]{:S(2)}) %collective-permute-start.6) | collective-permute-done | bytes 155680 | tf_op jit(solution)/shard_map/ppermute | solution.py:366
  23.2 2.5 %shard_map.62 = (f32[9,12,8,128]{3,2,1,0:T(8,128)S(1)}, f32[9,12,8,128]{3,2,1,0:T(8,128)S(1)}) custom-call(f32[9,12,8,128]{3,2,1,0:T(8,128)S(1)} %get-tuple-element.47.s_ref, f32[9,2,128]{2,1,0:T(2,128)S(1)} %bitcast.5, f32[2,48,128]{2,1,0:T(8,128)S(1)} %copy-done.2, f32[8,128]{1,0:T(8,128)S(1)} %get-tuple-element.48.rest_0_.pk_ref), custom_call_target="tpu_custom_call" | custom-call | tf_op jit(solution)/shard_map/pallas_call | solution.py:462
  25.7 0.0 collective-permute-done.7.near_ref
  25.7 0.0 collective-permute-done.8.far_ref
  25.7 0.9 %shard_map.63.part_ref = f32[9,12,8,128]{3,2,1,0:T(8,128)S(1)} custom-call(f32[9,12,8,128]{3,2,1,0:T(8,128)S(1)} %get-tuple-element.47.s_ref, f32[9,12,8,128]{3,2,1,0:T(8,128)S(1)} %get-tuple-element.49.speed_ref, f32[9,12,8,128]{3,2,1,0:T(8,128)S(1)} %get-tuple-element.50.part_ref, f32[37,8,128]{2,1,0:T(8,128)S(1)} %collective-permute-done.7.near_ref, ...), custom_call_target="tpu_custom_call" | custom-call | flops 110592000 | bytes 110592000 | tf_op jit(solution)/shard_map/pallas_call | solution.py:462
  26.6 0.7 %shard_map.64 = (f32[9,12,8,128]{3,2,1,0:T(8,128)S(1)}, f32[38,8,128]{2,1,0:T(8,128)S(1)}) custom-call(f32[9,12,8,128]{3,2,1,0:T(8,128)S(1)} %copy-done.1, f32[9,12,8,128]{3,2,1,0:T(8,128)S(1)} %get-tuple-element.47.s_ref, f32[9,12,8,128]{3,2,1,0:T(8,128)S(1)} %shard_map.63.part_ref, f32[38,8,128]{2,1,0:T(8,128)S(1)} %collective-permute-done.6.ghosts_ref, ...), custom_call_target="tpu_custom_call" | custom-call | tf_op jit(solution)/shard_map/pallas_call | solution.py:462
  27.3 1.9 %collective-permute-start.10 = (f32[38,8,128]{2,1,0:T(8,128)S(1)}, f32[38,8,128]{2,1,0:T(8,128)S(1)}, u32[]{:S(2)}, u32[]{:S(2)}) collective-permute-start(f32[38,8,128]{2,1,0:T(8,128)S(1)} %get-tuple-element.57), channel_id=1, source_target_pairs={{0,1},{2,3},{4,5},{6,7},{1,0},{3,2},{5,4},{7,6},{8,9},{10,11},{12,... | collective-permute-start | bytes 466952 | tf_op jit(solution)/shard_map/ppermute | solution.py:366
  29.2 0.0 collective-permute-done.9.ghosts_ref
  29.2 0.4 %shard_map.65 = (f32[9,12,8,128]{3,2,1,0:T(8,128)S(1)}, f32[36,8,128]{2,1,0:T(8,128)S(1)}, f32[37,8,128]{2,1,0:T(8,128)S(1)}, f32[37,8,128]{2,1,0:T(8,128)S(1)}) custom-call(f32[9,12,8,128]{3,2,1,0:T(8,128)S(1)} %copy-done.1, f32[9,12,8,128]{3,2,1,0:T(8,128)S(1)} %get-tuple-element.47.s_ref, f32[9,12,8,128]{3,2,1,0:T(8,128)S(1)} %shard_map.63.part_ref, ...), custom_call_target="tpu_custom_call" | custom-call | tf_op jit(solution)/shard_map/pallas_call | solution.py:462
  29.6 0.1 collective-permute-start.11
  29.7 1.6 %collective-permute-start.12 = (f32[37,8,128]{2,1,0:T(8,128)S(1)}, f32[37,8,128]{2,1,0:T(8,128)S(1)}, u32[]{:S(2)}, u32[]{:S(2)}) collective-permute-start(f32[37,8,128]{2,1,0:T(8,128)S(1)} %get-tuple-element.62), channel_id=1, source_target_pairs={{8,16},{24,0},{16,8},{0,24},{9,17},{25,1},{17,9},{1,25},{10,18},{2... | collective-permute-start | bytes 454664 | tf_op jit(solution)/shard_map/ppermute | solution.py:366
  31.3 1.9 %collective-permute-start.13 = (f32[36,8,128]{2,1,0:T(8,128)S(1)}, f32[36,8,128]{2,1,0:T(8,128)S(1)}, u32[]{:S(2)}, u32[]{:S(2)}) collective-permute-start(f32[36,8,128]{2,1,0:T(8,128)S(1)} %get-tuple-element.63), channel_id=1, source_target_pairs={{1,2},{3,4},{5,6},{2,1},{4,3},{6,5},{0,0},{7,7},{9,10},{11,12},{13... | collective-permute-start | bytes 442376 | tf_op jit(solution)/shard_map/ppermute | solution.py:366
  33.2 0.0 collective-permute-done.10.ghosts_ref
  33.2 2.5 %shard_map.66 = (f32[9,12,8,128]{3,2,1,0:T(8,128)S(1)}, f32[9,12,8,128]{3,2,1,0:T(8,128)S(1)}) custom-call(f32[9,12,8,128]{3,2,1,0:T(8,128)S(1)} %get-tuple-element.58.s_ref, f32[9,2,128]{2,1,0:T(2,128)S(1)} %bitcast.8, f32[2,48,128]{2,1,0:T(8,128)S(1)} %copy-done.2, f32[8,128]{1,0:T(8,128)S(1)} %get-tuple-element.48.rest_0_.pk_ref), custom_call_target="tpu_custom_call" | custom-call | tf_op jit(solution)/shard_map/pallas_call | solution.py:462
  35.7 0.0 collective-permute-done.11.near_ref
  35.7 0.0 collective-permute-done.12.far_ref
  35.7 0.9 %shard_map.67.part_ref = f32[9,12,8,128]{3,2,1,0:T(8,128)S(1)} custom-call(f32[9,12,8,128]{3,2,1,0:T(8,128)S(1)} %get-tuple-element.58.s_ref, f32[9,12,8,128]{3,2,1,0:T(8,128)S(1)} %get-tuple-element.59.speed_ref, f32[9,12,8,128]{3,2,1,0:T(8,128)S(1)} %get-tuple-element.60.part_ref, f32[37,8,128]{2,1,0:T(8,128)S(1)} %collective-permute-done.11.near_ref, ...), custom_call_target="tpu_custom_call" | custom-call | flops 110592000 | bytes 110592000 | tf_op jit(solution)/shard_map/pallas_call | solution.py:462
  36.6 0.7 %shard_map.68.refs_0_ = f32[9,12,8,128]{3,2,1,0:T(8,128)S(1)} custom-call(f32[9,12,8,128]{3,2,1,0:T(8,128)S(1)} %copy-done.1, f32[9,12,8,128]{3,2,1,0:T(8,128)S(1)} %get-tuple-element.58.s_ref, f32[9,12,8,128]{3,2,1,0:T(8,128)S(1)} %shard_map.67.part_ref, f32[38,8,128]{2,1,0:T(8,128)S(1)} %collective-permute-done.10.ghosts_ref, f32[9,2,128]{2,1,0:T(2,128)S(1)} %bitcast.9, ...), custom_call_target="tpu_custom_call" | custom-call | tf_op jit(solution)/shard_map/pallas_call | solution.py:462
  37.3 2.6 %collective-permute-done.13.ghosts_ref = f32[36,8,128]{2,1,0:T(8,128)S(1)} collective-permute-done((f32[36,8,128]{2,1,0:T(8,128)S(1)}, f32[36,8,128]{2,1,0:T(8,128)S(1)}, u32[]{:S(2)}, u32[]{:S(2)}) %collective-permute-start.13) | collective-permute-done | bytes 147488 | tf_op jit(solution)/shard_map/ppermute | solution.py:366
  39.9 1.1 %shard_map.69 = f32[9,12,8,128]{3,2,1,0:T(8,128)} custom-call(f32[9,12,8,128]{3,2,1,0:T(8,128)S(1)} %copy-done.1, f32[9,12,8,128]{3,2,1,0:T(8,128)S(1)} %get-tuple-element.58.s_ref, f32[9,12,8,128]{3,2,1,0:T(8,128)S(1)} %shard_map.67.part_ref, f32[36,8,128]{2,1,0:T(8,128)S(1)} %collective-permute-done.13.ghosts_ref, f32[9,2,128]{2,1,0:T(2,128)S(1)} %bitcast.10, ...), custom_call_target="tpu_custom_call" | custom-call | tf_op jit(solution)/shard_map/pallas_call | solution.py:462
  (4 shorter events, 0.1 us)
Async XLA Ops:
  0.0 1.0 %copy-start = (f32[9,12,8,128]{3,2,1,0:T(8,128)S(1)}, f32[9,12,8,128]{3,2,1,0:T(8,128)}, u32[]{:S(2)}) copy-start(f32[9,12,8,128]{3,2,1,0:T(8,128)} %base_ref.7) | copy-start | bytes 1327108
  1.0 0.7 %copy-start.3 = (f32[2,9,128]{2,0,1:T(2,128)S(1)}, f32[2,9,128]{2,0,1:T(2,128)}, u32[]{:S(2)}) copy-start(f32[2,9,128]{2,0,1:T(2,128)} %param.6) | copy-start | bytes 27652
  1.7 5.9 %copy-start.4 = (f32[2,9,128]{2,0,1:T(2,128)S(1)}, f32[2,9,128]{2,0,1:T(2,128)}, u32[]{:S(2)}) copy-start(f32[2,9,128]{2,0,1:T(2,128)} %param.6) | copy-start | bytes 27652
  1.7 7.5 %copy-start.1 = (f32[9,12,8,128]{3,2,1,0:T(8,128)S(1)}, f32[9,12,8,128]{3,2,1,0:T(8,128)}, u32[]{:S(2)}) copy-start(f32[9,12,8,128]{3,2,1,0:T(8,128)} %base_ref.7) | copy-start | bytes 1327108
  1.8 5.8 %collective-permute-start = (f32[38,8,128]{2,1,0:T(8,128)S(1)}, f32[38,8,128]{2,1,0:T(8,128)S(1)}, u32[]{:S(2)}, u32[]{:S(2)}) collective-permute-start(f32[38,8,128]{2,1,0:T(8,128)S(1)} %shard_map.56), channel_id=1, source_target_pairs={{0,1},{2,3},{4,5},{6,7},{1,0},{3,2},{5,4},{7,6},{8,9},{10,11},{12,... | collective-permute-start | bytes 466952 | tf_op jit(solution)/shard_map/ppermute | solution.py:366
  3.4 9.9 %collective-permute-start.2 = (f32[39,8,128]{2,1,0:T(8,128)S(1)}, f32[39,8,128]{2,1,0:T(8,128)S(1)}, u32[]{:S(2)}, u32[]{:S(2)}) collective-permute-start(f32[39,8,128]{2,1,0:T(8,128)S(1)} %get-tuple-element.38), channel_id=1, source_target_pairs={{0,8},{16,24},{8,0},{24,16},{1,9},{17,25},{9,1},{25,17},{2,10},{18... | collective-permute-start | bytes 479240 | tf_op jit(solution)/shard_map/ppermute | solution.py:366
  3.4 9.8 %collective-permute-start.3 = (f32[39,8,128]{2,1,0:T(8,128)S(1)}, f32[39,8,128]{2,1,0:T(8,128)S(1)}, u32[]{:S(2)}, u32[]{:S(2)}) collective-permute-start(f32[39,8,128]{2,1,0:T(8,128)S(1)} %get-tuple-element.39), channel_id=1, source_target_pairs={{8,16},{24,0},{16,8},{0,24},{9,17},{25,1},{17,9},{1,25},{10,18},{2... | collective-permute-start | bytes 479240 | tf_op jit(solution)/shard_map/ppermute | solution.py:366
  5.1 4.2 %copy-start.2 = (f32[2,48,128]{2,1,0:T(8,128)S(1)}, f32[2,48,128]{2,1,0:T(8,128)}, u32[]{:S(2)}) copy-start(f32[2,48,128]{2,1,0:T(8,128)} %constant.2.clone.waves_ref) | copy-start | bytes 147460
  5.1 9.1 %collective-permute-start.4 = (f32[36,8,128]{2,1,0:T(8,128)S(1)}, f32[36,8,128]{2,1,0:T(8,128)S(1)}, u32[]{:S(2)}, u32[]{:S(2)}) collective-permute-start(f32[36,8,128]{2,1,0:T(8,128)S(1)} %get-tuple-element.40), channel_id=1, source_target_pairs={{1,2},{3,4},{5,6},{2,1},{4,3},{6,5},{0,0},{7,7},{9,10},{11,12},{13... | collective-permute-start | bytes 442376 | tf_op jit(solution)/shard_map/ppermute | solution.py:366
  7.6 5.4 %collective-permute-start.1 = (f32[8,128]{1,0:T(8,128)S(1)}, f32[8,128]{1,0:T(8,128)S(1)}, u32[]{:S(2)}, u32[]{:S(2)}) collective-permute-start(f32[8,128]{1,0:T(8,128)S(1)} %shard_map.57), channel_id=1, source_target_pairs={{0,2},{1,3},{2,0},{3,1},{4,6},{5,7},{6,4},{7,5},{8,10},{9,11},{10,... | collective-permute-start | bytes 12296 | tf_op jit(solution)/shard_map/ppermute | solution.py:491
  13.0 4.5 %collective-permute-start.5 = (f32[8,128]{1,0:T(8,128)S(1)}, f32[8,128]{1,0:T(8,128)S(1)}, u32[]{:S(2)}, u32[]{:S(2)}) collective-permute-start(f32[8,128]{1,0:T(8,128)S(1)} %max.3.most_ref), channel_id=1, source_target_pairs={{0,4},{1,5},{2,6},{3,7},{4,0},{5,1},{6,2},{7,3},{8,12},{9,13},{10,... | collective-permute-start | bytes 12296 | tf_op jit(solution)/shard_map/ppermute | solution.py:491
  14.1 3.4 %copy-start.5 = (s32[9,128]{1,0:T(8,128)S(1)}, s32[9,128]{1,0:T(8,128)}, u32[]{:S(2)}) copy-start(s32[9,128]{1,0:T(8,128)} %mask_ref.9) | copy-start | bytes 13828
  14.1 3.4 %copy-start.6 = (f32[9,128]{1,0:T(8,128)S(1)}, f32[9,128]{1,0:T(8,128)}, u32[]{:S(2)}) copy-start(f32[9,128]{1,0:T(8,128)} %depth_ref.9) | copy-start | bytes 13828
  17.9 5.3 %collective-permute-start.6 = (f32[38,8,128]{2,1,0:T(8,128)S(1)}, f32[38,8,128]{2,1,0:T(8,128)S(1)}, u32[]{:S(2)}, u32[]{:S(2)}) collective-permute-start(f32[38,8,128]{2,1,0:T(8,128)S(1)} %get-tuple-element.46), channel_id=1, source_target_pairs={{0,1},{2,3},{4,5},{6,7},{1,0},{3,2},{5,4},{7,6},{8,9},{10,11},{12,... | collective-permute-start | bytes 466952 | tf_op jit(solution)/shard_map/ppermute | solution.py:366
  18.9 6.8 %collective-permute-start.7 = (f32[37,8,128]{2,1,0:T(8,128)S(1)}, f32[37,8,128]{2,1,0:T(8,128)S(1)}, u32[]{:S(2)}, u32[]{:S(2)}) collective-permute-start(f32[37,8,128]{2,1,0:T(8,128)S(1)} %get-tuple-element.51), channel_id=1, source_target_pairs={{0,8},{16,24},{8,0},{24,16},{1,9},{17,25},{9,1},{25,17},{2,10},{18... | collective-permute-start | bytes 454664 | tf_op jit(solution)/shard_map/ppermute | solution.py:366
  18.9 6.8 %collective-permute-start.8 = (f32[37,8,128]{2,1,0:T(8,128)S(1)}, f32[37,8,128]{2,1,0:T(8,128)S(1)}, u32[]{:S(2)}, u32[]{:S(2)}) collective-permute-start(f32[37,8,128]{2,1,0:T(8,128)S(1)} %get-tuple-element.52), channel_id=1, source_target_pairs={{8,16},{24,0},{16,8},{0,24},{9,17},{25,1},{17,9},{1,25},{10,18},{2... | collective-permute-start | bytes 454664 | tf_op jit(solution)/shard_map/ppermute | solution.py:366
  19.9 9.3 %collective-permute-start.9 = (f32[36,8,128]{2,1,0:T(8,128)S(1)}, f32[36,8,128]{2,1,0:T(8,128)S(1)}, u32[]{:S(2)}, u32[]{:S(2)}) collective-permute-start(f32[36,8,128]{2,1,0:T(8,128)S(1)} %get-tuple-element.53), channel_id=1, source_target_pairs={{1,2},{3,4},{5,6},{2,1},{4,3},{6,5},{0,0},{7,7},{9,10},{11,12},{13... | collective-permute-start | bytes 442376 | tf_op jit(solution)/shard_map/ppermute | solution.py:366
  27.3 5.9 %collective-permute-start.10 = (f32[38,8,128]{2,1,0:T(8,128)S(1)}, f32[38,8,128]{2,1,0:T(8,128)S(1)}, u32[]{:S(2)}, u32[]{:S(2)}) collective-permute-start(f32[38,8,128]{2,1,0:T(8,128)S(1)} %get-tuple-element.57), channel_id=1, source_target_pairs={{0,1},{2,3},{4,5},{6,7},{1,0},{3,2},{5,4},{7,6},{8,9},{10,11},{12,... | collective-permute-start | bytes 466952 | tf_op jit(solution)/shard_map/ppermute | solution.py:366
  29.6 6.1 %collective-permute-start.11 = (f32[37,8,128]{2,1,0:T(8,128)S(1)}, f32[37,8,128]{2,1,0:T(8,128)S(1)}, u32[]{:S(2)}, u32[]{:S(2)}) collective-permute-start(f32[37,8,128]{2,1,0:T(8,128)S(1)} %get-tuple-element.61), channel_id=1, source_target_pairs={{0,8},{16,24},{8,0},{24,16},{1,9},{17,25},{9,1},{25,17},{2,10},{18... | collective-permute-start | bytes 454664 | tf_op jit(solution)/shard_map/ppermute | solution.py:366
  29.7 6.0 %collective-permute-start.12 = (f32[37,8,128]{2,1,0:T(8,128)S(1)}, f32[37,8,128]{2,1,0:T(8,128)S(1)}, u32[]{:S(2)}, u32[]{:S(2)}) collective-permute-start(f32[37,8,128]{2,1,0:T(8,128)S(1)} %get-tuple-element.62), channel_id=1, source_target_pairs={{8,16},{24,0},{16,8},{0,24},{9,17},{25,1},{17,9},{1,25},{10,18},{2... | collective-permute-start | bytes 454664 | tf_op jit(solution)/shard_map/ppermute | solution.py:366
  31.3 8.6 %collective-permute-start.13 = (f32[36,8,128]{2,1,0:T(8,128)S(1)}, f32[36,8,128]{2,1,0:T(8,128)S(1)}, u32[]{:S(2)}, u32[]{:S(2)}) collective-permute-start(f32[36,8,128]{2,1,0:T(8,128)S(1)} %get-tuple-element.63), channel_id=1, source_target_pairs={{1,2},{3,4},{5,6},{2,1},{4,3},{6,5},{0,0},{7,7},{9,10},{11,12},{13... | collective-permute-start | bytes 442376 | tf_op jit(solution)/shard_map/ppermute | solution.py:366

commit v10 on v9

--- a/solution.py
+++ b/solution.py
@@ -84,81 +84,24 @@
     most_ref[2:4, :] = -functools.reduce(jnp.minimum, rows)
 
 
-def near_kernel(level_ref, wind_ref, x_near):
-    put_extremes(wind_ref, x_near.at[x_near.shape[0] - 1])
+def extremes_kernel(wind_ref, most_ref):
+    put_extremes(wind_ref, most_ref.at[0])
+
+
+def opening_kernel(level_ref, x_near, x_far, t_near, t_far):
     cut_near(level_ref, x_near)
-
-
-def far_kernel(level_ref, x_far, t_near, t_far):
     cut_far(level_ref, x_far)
     cut_headings(level_ref, t_near, t_far)
 
 
-def meeting_kernel(wind_ref, x_near, most_ref):
-    put_extremes(wind_ref, most_ref)
-    most_ref[...] = jnp.maximum(most_ref[...], x_near[x_near.shape[0] - 1])
-
-
-def free_kernel(split, speed_step, s_ref, wind_ref, waves_ref, *rest):
-    planes, headings, speeds, width = s_ref.shape
-    tile = (speeds, width)
-    if split:
-        speed_ref, out_ref, extra_ref, turned_ref, mean_ref, gap_ref, flow_ref = rest
-    else:
-        pk_ref, speed_ref, out_ref, turned_ref, mean_ref, gap_ref, flow_ref = rest
-        peak = splat(pk_ref[1:2, :] * gain, tile)
-    gain_v = thrust_limit / (12.0 * speed_step)
+def meeting_kernel(own_ref, other_ref, most_ref):
+    most_ref[...] = jnp.maximum(own_ref[0], other_ref[0])
+
+
+def flows_into(flow_ref, speed_step, wind_ref, waves_ref):
+    planes, headings = flow_ref.shape[:2]
+    tile = flow_ref.shape[2:]
     first = lax.axis_index("head") * headings
-    cells = planes * headings
-    s_rows = s_ref.reshape(cells * speeds, width)
-    speed_rows = speed_ref.reshape(cells * speeds, width)
-    out_rows = out_ref.reshape(cells * speeds, width)
-    flow_rows = flow_ref.reshape(cells * speeds, width)
-    few, many = 8, turned_ref.shape[2] // speeds
-    groups = turned_ref.shape[0]
-    lanes = many * speeds
-    high = 8
-    lines = width // high
-
-    def along_speed(n):
-        start = jnp.minimum(n * few, cells - few) * speeds
-        spots = [pl.ds(start + v, few, stride=speeds) for v in range(speeds)]
-        rows = [s_rows[spot, :] for spot in spots]
-        ends = [rows[0]] * rim + rows + [rows[-1]] * rim
-        for spot, (mean, gap) in zip(spots, row_terms(ends, speed_step)):
-            speed_rows[spot, :] = gain_v * (gap - jnp.abs(mean))
-
-    def span(n):
-        return pl.ds(pl.multiple_of(jnp.minimum(n * many, cells - many) * speeds, speeds), lanes)
-
-    def turn_in(n, carry):
-        along_speed(n)
-        turned = s_rows[span(n), :].T
-        turned_ref[n, rim : rim + width, :] = turned
-        for k in range(rim):
-            turned_ref[n, k : k + 1, :] = turned[:1]
-            turned_ref[n, rim + width + k : rim + width + k + 1, :] = turned[-1:]
-        return carry
-
-    def along_y(n, carry):
-        ends = [turned_ref[n, pl.ds(k, high, stride=lines), :] for k in range(lines + 2 * rim)]
-        for k, (mean, gap) in enumerate(row_terms(ends, spacing)):
-            mean_ref[n, pl.ds(k, high, stride=lines), :] = mean
-            gap_ref[n, pl.ds(k, high, stride=lines), :] = gap
-        return carry
-
-    def turn_out(n, carry):
-        along_speed(groups + n)
-        mean = mean_ref[n].T
-        gap = gap_ref[n].T
-        drift = mean * flow_rows[span(n), :]
-        if split:
-            out_rows[span(n), :] = drift
-            extra_ref.reshape(cells * speeds, width)[span(n), :] = gap
-        else:
-            out_rows[span(n), :] = drift + gap * splat(peak[:1], gap.shape)
-        return carry
-
     pace = speeds_of(tile, speed_step) * gain
     tables = [
         splat(waves_ref[1, pl.ds(first + j, 1), :], tile) * pace for j in range(headings)
@@ -167,9 +110,77 @@
         wind = splat(wind_ref[i, 1:2, :] * gain, tile)
         for j in range(headings):
             flow_ref[i, j] = tables[j] + wind
-    lax.fori_loop(0, groups, turn_in, 0)
-    lax.fori_loop(0, groups, along_y, 0)
-    lax.fori_loop(0, groups, turn_out, 0)
+
+
+def free_kernel(split, speed_step, s_ref, *rest):
+    planes, headings, speeds, width = s_ref.shape
+    cells = planes * headings
+
+    def rows_of(ref):
+        return ref.reshape(cells * speeds, width)
+
+    if split:
+        wind_ref, waves_ref, speed_ref, out_ref, extra_ref, flow_ref = rest[:-3]
+        flows_into(flow_ref, speed_step, wind_ref, waves_ref)
+        extra_rows = rows_of(extra_ref)
+    else:
+        flow_ref, pk_ref, speed_ref, out_ref = rest[:-3]
+        peak = splat(pk_ref[1:2, :] * gain, (16 * speeds, width))
+    turned_ref, mean_ref, gap_ref = rest[-3:]
+    gain_v = thrust_limit / (12.0 * speed_step)
+    s_rows, speed_rows = rows_of(s_ref), rows_of(speed_ref)
+    out_rows, flow_rows = rows_of(out_ref), rows_of(flow_ref)
+    few, many = 8, turned_ref.shape[2] // speeds
+    groups = turned_ref.shape[0]
+    lanes = many * speeds
+    high = 8
+    lines = width // high
+
+    def along_speed(n):
+        start = jnp.minimum(n * few, cells - few) * speeds
+        spots = [pl.ds(start + v, few, stride=speeds) for v in range(speeds)]
+        rows = [s_rows[spot, :] for spot in spots]
+        ends = [rows[0]] * rim + rows + [rows[-1]] * rim
+        for spot, (mean, gap) in zip(spots, row_terms(ends, speed_step)):
+            speed_rows[spot, :] = gain_v * (gap - jnp.abs(mean))
+
+    def span(n):
+        return pl.ds(pl.multiple_of(jnp.minimum(n * many, cells - many) * speeds, speeds), lanes)
+
+    def turn_in(n):
+        turned = s_rows[span(n), :].T
+        turned_ref[n, rim : rim + width, :] = turned
+        for k in range(rim):
+            turned_ref[n, k : k + 1, :] = turned[:1]
+            turned_ref[n, rim + width + k : rim + width + k + 1, :] = turned[-1:]
+
+    def along_y(n):
+        ends = [turned_ref[n, pl.ds(k, high, stride=lines), :] for k in range(lines + 2 * rim)]
+        for k, (mean, gap) in enumerate(row_terms(ends, spacing)):
+            mean_ref[n, pl.ds(k, high, stride=lines), :] = mean
+            gap_ref[n, pl.ds(k, high, stride=lines), :] = gap
+
+    def turn_out(n):
+        mean = mean_ref[n].T
+        gap = gap_ref[n].T
+        drift = mean * flow_rows[span(n), :]
+        if split:
+            out_rows[span(n), :] = drift
+            extra_rows[span(n), :] = gap
+        else:
+            out_rows[span(n), :] = drift + gap * peak
+
+    def step(n, carry):
+        turn_out(jnp.maximum(n - 1, 0))
+        along_y(n)
+        turn_in(jnp.minimum(n + 1, groups - 1))
+        along_speed(2 * n)
+        along_speed(2 * n + 1)
+        return carry
+
+    turn_in(0)
+    lax.fori_loop(0, groups, step, 0)
+    turn_out(groups - 1)
 
 
 def heading_kernel(heading_step, s_ref, speed_ref, part_ref, near_ref, far_ref, out_ref):
@@ -416,7 +427,6 @@
         pltpu.VMEM((groups, cross_count + 8, lanes), jnp.float32),
         pltpu.VMEM((groups, cross_count, lanes), jnp.float32),
         pltpu.VMEM((groups, cross_count, lanes), jnp.float32),
-        pltpu.VMEM(level_set.shape, jnp.float32),
     ]
     values = level_set
     size = lax.axis_size(axis)
@@ -478,7 +488,6 @@
         pltpu.VMEM((groups, cross_count + 8, lanes), jnp.float32),
         pltpu.VMEM((groups, cross_count, lanes), jnp.float32),
         pltpu.VMEM((groups, cross_count, lanes), jnp.float32),
-        pltpu.VMEM(level_set.shape, jnp.float32),
     ]
     values, pk = level_set, None
     size = lax.axis_size("gx")
@@ -490,9 +499,10 @@
             pairs = [(i, i ^ reach) for i in range(size)]
         return lax.ppermute(most, "gx", pairs)
 
-    far_shapes = [shape(short), shape(longest + 1), shape(longest + 1)]
-    x_last, t_out, t_last = call(far_kernel, [values], far_shapes)
-    (x_out,) = call(near_kernel, [values, wind], [shape(longest)])
+    (most,) = call(extremes_kernel, [wind], [shape(longest + 2)])
+    other = spread(most, 1)
+    x_shapes = [shape(longest), shape(longest + 1)]
+    x_out, x_last, t_out, t_last = call(opening_kernel, [values], x_shapes + [shape(middle)] * 2)
     far_shapes = [shape(short), shape(middle), shape(middle)]
     for section in (1, 2, 3):
         opening = section == 1
@@ -503,19 +513,23 @@
         free = functools.partial(free_kernel, opening, speed_step)
         turning = functools.partial(heading_kernel, heading_step)
         if opening:
-            (most,) = call(meeting_kernel, [wind, x_near], [shape()])
+            (most,) = call(meeting_kernel, [most, other], [shape()])
             other = spread(most, 2)
             ins = [values, wind, waves]
-            spun, part, extra = call(free, ins, [field] * 3, room, work=300)
+            spun, part, extra, flow = call(free, ins, [field] * 4, room, work=300)
             reach = 4
             while reach < size:
                 most = jnp.maximum(most, other)
                 most, part = lax.optimization_barrier((most, part))
                 other = spread(most, reach)
                 reach *= 2
+            part, x_far = lax.optimization_barrier((part, x_far))
         else:
-            values, x_near = lax.optimization_barrier((values, x_near))
-            spun, part = call(free, [values, wind, waves, pk], [field] * 2, room)
+            if section == 3:
+                values, x_near = lax.optimization_barrier((values, x_near))
+            spun, part = call(free, [values, flow, pk], [field] * 2, room)
+            if section == 2:
+                part, x_near = lax.optimization_barrier((part, x_near))
         (part,) = call(turning, [values, spun, part, t_near, t_far], [field], work=1000)
         if opening:
             ins = [values, part, x_near, x_far, wind, waves]

time: 41.3 us -> 40.8 us (0.988)
  the two profiles are of different devices: /device:TPU:16 before, /device:TPU:8 now
where the time goes in v10:
time: 40.8 us; the launch traced here: 40.1 us
  starting transfers between devices  21.7 us (53%)
  Pallas kernels  13.3 us (33%)
  waiting for transfers between devices  3.12 us (8%)
  local copies, waits for them, and re-layouts  1.74 us (4%)
    ppermute x12, starting transfers between devices, trade(): return lax.ppermute(value, axis, pairs)  18 us
    pallas_call x15, Pallas kernels, call(): pl.pallas_call(kernel, out_shape=outs, in_specs=[vmem] * len(ins), out_sp...  13.3 us
    ppermute x3, starting transfers between devices, spread(): return lax.ppermute(most, 'gx', pairs)  3.74 us
    ppermute x3, waiting for transfers between devices, spread(): return lax.ppermute(most, 'gx', pairs)  1.98 us
    unnamed x14, local copies, waits for them, and re-layouts  1.74 us
    ppermute x12, waiting for transfers between devices, trade(): return lax.ppermute(value, axis, pairs)  1.14 us
  transfers between devices with their start and end apart: 15, of which 3 were waited for; matrix products, arithmetic and copies ran while one was open for 0% of the time, Pallas kernels for 29%

profile of v10, /device:TPU:8, one launch (start us, length us, event | category | flops | bytes accessed | tf_op | source)
XLA Modules:
  0.0 40.1 jit_solution(17355894145032430319)
XLA Ops:
  0.0 0.0 copy-start.3
  0.0 0.7 %copy-done.3 = f32[2,9,128]{2,0,1:T(2,128)S(1)} copy-done((f32[2,9,128]{2,0,1:T(2,128)S(1)}, f32[2,9,128]{2,0,1:T(2,128)}, u32[]{:S(2)}) %copy-start.3) | copy-done | bytes 9240
  0.7 1.6 %collective-permute-start = (f32[40,8,128]{2,1,0:T(8,128)S(1)}, f32[40,8,128]{2,1,0:T(8,128)S(1)}, u32[]{:S(2)}, u32[]{:S(2)}) collective-permute-start(f32[40,8,128]{2,1,0:T(8,128)S(1)} %shard_map.56.own_ref), channel_id=1, source_target_pairs={{0,1},{1,0},{2,3},{3,2},{4,5},{5,4},{6,7},{7,6},{8,9},{9,8},{10,11... | collective-permute-start | bytes 491528 | tf_op jit(solution)/shard_map/ppermute | solution.py:500
  2.3 0.0 copy-start
  2.3 1.0 %copy-done = f32[9,12,8,128]{3,2,1,0:T(8,128)S(1)} copy-done((f32[9,12,8,128]{3,2,1,0:T(8,128)S(1)}, f32[9,12,8,128]{3,2,1,0:T(8,128)}, u32[]{:S(2)}) %copy-start) | copy-done | bytes 442392
  3.3 0.0 copy-start.1
  3.3 2.1 %collective-permute-start.2 = (f32[39,8,128]{2,1,0:T(8,128)S(1)}, f32[39,8,128]{2,1,0:T(8,128)S(1)}, u32[]{:S(2)}, u32[]{:S(2)}) collective-permute-start(f32[39,8,128]{2,1,0:T(8,128)S(1)} %get-tuple-element.42), channel_id=1, source_target_pairs={{1,2},{3,4},{5,6},{2,1},{4,3},{6,5},{0,0},{7,7},{9,10},{11,12},{13... | collective-permute-start | bytes 479240 | tf_op jit(solution)/shard_map/ppermute | solution.py:377
  5.4 0.1 collective-permute-start.3
  5.5 2.0 %collective-permute-start.4 = (f32[37,8,128]{2,1,0:T(8,128)S(1)}, f32[37,8,128]{2,1,0:T(8,128)S(1)}, u32[]{:S(2)}, u32[]{:S(2)}) collective-permute-start(f32[37,8,128]{2,1,0:T(8,128)S(1)} %get-tuple-element.45), channel_id=1, source_target_pairs={{8,16},{24,0},{16,8},{0,24},{9,17},{25,1},{17,9},{1,25},{10,18},{2... | collective-permute-start | bytes 454664 | tf_op jit(solution)/shard_map/ppermute | solution.py:377
  7.5 0.0 copy-start.2
  7.5 0.0 copy-start.4
  7.5 2.6 %collective-permute-start.5 = (f32[38,8,128]{2,1,0:T(8,128)S(1)}, f32[38,8,128]{2,1,0:T(8,128)S(1)}, u32[]{:S(2)}, u32[]{:S(2)}) collective-permute-start(f32[38,8,128]{2,1,0:T(8,128)S(1)} %get-tuple-element.46), channel_id=1, source_target_pairs={{0,1},{2,3},{4,5},{6,7},{1,0},{3,2},{5,4},{7,6},{8,9},{10,11},{12,... | collective-permute-start | bytes 466952 | tf_op jit(solution)/shard_map/ppermute | solution.py:377
  10.1 0.0 collective-permute-done.other_ref
  10.1 0.5 %collective-permute-start.1 = (f32[8,128]{1,0:T(8,128)S(1)}, f32[8,128]{1,0:T(8,128)S(1)}, u32[]{:S(2)}, u32[]{:S(2)}) collective-permute-start(f32[8,128]{1,0:T(8,128)S(1)} %shard_map.57), channel_id=1, source_target_pairs={{0,2},{1,3},{2,0},{3,1},{4,6},{5,7},{6,4},{7,5},{8,10},{9,11},{10,... | collective-permute-start | bytes 12296 | tf_op jit(solution)/shard_map/ppermute | solution.py:500
  10.6 0.0 copy-done.1
  10.6 0.0 copy-done.2
  10.6 0.0 copy-done.4
  10.6 2.2 %shard_map.55 = (f32[9,12,8,128]{3,2,1,0:T(8,128)S(1)}, f32[9,12,8,128]{3,2,1,0:T(8,128)S(1)}, f32[9,12,8,128]{3,2,1,0:T(8,128)S(1)}, f32[9,12,8,128]{3,2,1,0:T(8,128)S(1)}) custom-call(f32[9,12,8,128]{3,2,1,0:T(8,128)S(1)} %copy-done.1, f32[9,2,128]{2,1,0:T(2,128)S(1)} %bitcast.2, f32[2,48,128]{2,1,0:T(8,128)S(1)} %copy-done.2), custom_call_target="tpu_custom_call" | custom-call | flops 33177600 | bytes 33177600 | tf_op jit(solution)/shard_map/pallas_call | solution.py:472
  12.8 1.0 %collective-permute-done.1 = f32[8,128]{1,0:T(8,128)S(1)} collective-permute-done((f32[8,128]{1,0:T(8,128)S(1)}, f32[8,128]{1,0:T(8,128)S(1)}, u32[]{:S(2)}, u32[]{:S(2)}) %collective-permute-start.1) | collective-permute-done | bytes 4128 | tf_op jit(solution)/shard_map/ppermute | solution.py:500
  13.7 0.0 collective-permute-done.2.far_ref
  13.7 1.7 %collective-permute-start.6 = (f32[8,128]{1,0:T(8,128)S(1)}, f32[8,128]{1,0:T(8,128)S(1)}, u32[]{:S(2)}, u32[]{:S(2)}) collective-permute-start(f32[8,128]{1,0:T(8,128)S(1)} %max.3.most_ref), channel_id=1, source_target_pairs={{0,4},{1,5},{2,6},{3,7},{4,0},{5,1},{6,2},{7,3},{8,12},{9,13},{10,... | collective-permute-start | bytes 12296 | tf_op jit(solution)/shard_map/ppermute | solution.py:500
  15.5 0.0 collective-permute-done.3.near_ref
  15.5 0.0 collective-permute-done.4.far_ref
  15.5 0.8 %shard_map.59.part_ref = f32[9,12,8,128]{3,2,1,0:T(8,128)S(1)} custom-call(f32[9,12,8,128]{3,2,1,0:T(8,128)S(1)} %copy-done.1, f32[9,12,8,128]{3,2,1,0:T(8,128)S(1)} %get-tuple-element.39.speed_ref, f32[9,12,8,128]{3,2,1,0:T(8,128)S(1)} %get-tuple-element.43.part_ref, f32[37,8,128]{2,1,0:T(8,128)S(1)} %collective-permute-done.3.near_ref, ...), custom_call_target="tpu_custom_call" | custom-call | flops 110592000 | bytes 110592000 | tf_op jit(solution)/shard_map/pallas_call | solution.py:472
  16.3 0.0 collective-permute-done.5.near_ref
  16.3 0.0 copy-start.5
  16.3 0.0 copy-start.6
  16.3 0.9 %shard_map.60 = (f32[9,12,8,128]{3,2,1,0:T(8,128)S(1)}, f32[9,12,8,128]{3,2,1,0:T(8,128)S(1)}) custom-call(f32[9,12,8,128]{3,2,1,0:T(8,128)S(1)} %copy-done.1, f32[9,12,8,128]{3,2,1,0:T(8,128)S(1)} %shard_map.59.part_ref, f32[38,8,128]{2,1,0:T(8,128)S(1)} %collective-permute-done.5.near_ref, f32[39,8,128]{2,1,0:T(8,128)S(1)} %collective-permute-done.2.far_ref, ...), custom_call_target="tpu_custom_call" | custom-call | tf_op jit(solution)/shard_map/pallas_call | solution.py:472
  17.2 1.0 %collective-permute-done.6.other_ref = f32[8,128]{1,0:T(8,128)S(1)} collective-permute-done((f32[8,128]{1,0:T(8,128)S(1)}, f32[8,128]{1,0:T(8,128)S(1)}, u32[]{:S(2)}, u32[]{:S(2)}) %collective-permute-start.6) | collective-permute-done | bytes 4128 | tf_op jit(solution)/shard_map/ppermute | solution.py:500
  18.3 0.0 copy-done.5
  18.3 0.0 copy-done.6
  18.3 0.4 shard_map.61
  18.7 0.1 collective-permute-start.7
  18.8 0.0 collective-permute-start.8
  18.8 0.7 %collective-permute-start.9 = (f32[37,8,128]{2,1,0:T(8,128)S(1)}, f32[37,8,128]{2,1,0:T(8,128)S(1)}, u32[]{:S(2)}, u32[]{:S(2)}) collective-permute-start(f32[37,8,128]{2,1,0:T(8,128)S(1)} %get-tuple-element.60), channel_id=1, source_target_pairs={{8,16},{24,0},{16,8},{0,24},{9,17},{25,1},{17,9},{1,25},{10,18},{2... | collective-permute-start | bytes 454664 | tf_op jit(solution)/shard_map/ppermute | solution.py:377
  19.5 4.0 %collective-permute-start.10 = (f32[36,8,128]{2,1,0:T(8,128)S(1)}, f32[36,8,128]{2,1,0:T(8,128)S(1)}, u32[]{:S(2)}, u32[]{:S(2)}) collective-permute-start(f32[36,8,128]{2,1,0:T(8,128)S(1)} %get-tuple-element.61), channel_id=1, source_target_pairs={{1,2},{3,4},{5,6},{2,1},{4,3},{6,5},{0,0},{7,7},{9,10},{11,12},{13... | collective-permute-start | bytes 442376 | tf_op jit(solution)/shard_map/ppermute | solution.py:377
  23.4 2.1 %shard_map.62 = (f32[9,12,8,128]{3,2,1,0:T(8,128)S(1)}, f32[9,12,8,128]{3,2,1,0:T(8,128)S(1)}) custom-call(f32[9,12,8,128]{3,2,1,0:T(8,128)S(1)} %get-tuple-element.52.s_ref, f32[9,12,8,128]{3,2,1,0:T(8,128)S(1)} %get-tuple-element.53.rest_0_, f32[8,128]{1,0:T(8,128)S(1)} %get-tuple-element.54.rest_1_.pk_ref), custom_call_target="tpu_custom_call" | custom-call | tf_op jit(solution)/shard_map/pallas_call | solution.py:472
  25.6 0.0 collective-permute-done.7.ghosts_ref
  25.6 0.0 collective-permute-done.8.near_ref
  25.6 0.0 collective-permute-done.9.far_ref
  25.6 0.9 %shard_map.63.part_ref = f32[9,12,8,128]{3,2,1,0:T(8,128)S(1)} custom-call(f32[9,12,8,128]{3,2,1,0:T(8,128)S(1)} %get-tuple-element.52.s_ref, f32[9,12,8,128]{3,2,1,0:T(8,128)S(1)} %get-tuple-element.55.speed_ref, f32[9,12,8,128]{3,2,1,0:T(8,128)S(1)} %get-tuple-element.58.part_ref, f32[37,8,128]{2,1,0:T(8,128)S(1)} %collective-permute-done.8.near_ref, ...), custom_call_target="tpu_custom_call" | custom-call | flops 110592000 | bytes 110592000 | tf_op jit(solution)/shard_map/pallas_call | solution.py:472
  26.4 0.7 %shard_map.64 = (f32[9,12,8,128]{3,2,1,0:T(8,128)S(1)}, f32[38,8,128]{2,1,0:T(8,128)S(1)}) custom-call(f32[9,12,8,128]{3,2,1,0:T(8,128)S(1)} %copy-done.1, f32[9,12,8,128]{3,2,1,0:T(8,128)S(1)} %get-tuple-element.52.s_ref, f32[9,12,8,128]{3,2,1,0:T(8,128)S(1)} %shard_map.63.part_ref, f32[38,8,128]{2,1,0:T(8,128)S(1)} %collective-permute-done.7.ghosts_ref, ...), custom_call_target="tpu_custom_call" | custom-call | tf_op jit(solution)/shard_map/pallas_call | solution.py:472
  27.2 1.0 %collective-permute-start.11 = (f32[38,8,128]{2,1,0:T(8,128)S(1)}, f32[38,8,128]{2,1,0:T(8,128)S(1)}, u32[]{:S(2)}, u32[]{:S(2)}) collective-permute-start(f32[38,8,128]{2,1,0:T(8,128)S(1)} %get-tuple-element.65), channel_id=1, source_target_pairs={{0,1},{2,3},{4,5},{6,7},{1,0},{3,2},{5,4},{7,6},{8,9},{10,11},{12,... | collective-permute-start | bytes 466952 | tf_op jit(solution)/shard_map/ppermute | solution.py:377
  28.2 0.0 collective-permute-done.10.ghosts_ref
  28.2 0.4 %shard_map.65 = (f32[9,12,8,128]{3,2,1,0:T(8,128)S(1)}, f32[36,8,128]{2,1,0:T(8,128)S(1)}, f32[37,8,128]{2,1,0:T(8,128)S(1)}, f32[37,8,128]{2,1,0:T(8,128)S(1)}) custom-call(f32[9,12,8,128]{3,2,1,0:T(8,128)S(1)} %copy-done.1, f32[9,12,8,128]{3,2,1,0:T(8,128)S(1)} %get-tuple-element.52.s_ref, f32[9,12,8,128]{3,2,1,0:T(8,128)S(1)} %shard_map.63.part_ref, ...), custom_call_target="tpu_custom_call" | custom-call | tf_op jit(solution)/shard_map/pallas_call | solution.py:472
  28.6 0.1 collective-permute-start.12
  28.7 1.6 %collective-permute-start.13 = (f32[37,8,128]{2,1,0:T(8,128)S(1)}, f32[37,8,128]{2,1,0:T(8,128)S(1)}, u32[]{:S(2)}, u32[]{:S(2)}) collective-permute-start(f32[37,8,128]{2,1,0:T(8,128)S(1)} %get-tuple-element.70), channel_id=1, source_target_pairs={{8,16},{24,0},{16,8},{0,24},{9,17},{25,1},{17,9},{1,25},{10,18},{2... | collective-permute-start | bytes 454664 | tf_op jit(solution)/shard_map/ppermute | solution.py:377
  30.3 3.7 %collective-permute-start.14 = (f32[36,8,128]{2,1,0:T(8,128)S(1)}, f32[36,8,128]{2,1,0:T(8,128)S(1)}, u32[]{:S(2)}, u32[]{:S(2)}) collective-permute-start(f32[36,8,128]{2,1,0:T(8,128)S(1)} %get-tuple-element.71), channel_id=1, source_target_pairs={{1,2},{3,4},{5,6},{2,1},{4,3},{6,5},{0,0},{7,7},{9,10},{11,12},{13... | collective-permute-start | bytes 442376 | tf_op jit(solution)/shard_map/ppermute | solution.py:377
  34.1 0.0 collective-permute-done.11.ghosts_ref
  34.1 2.1 %shard_map.66 = (f32[9,12,8,128]{3,2,1,0:T(8,128)S(1)}, f32[9,12,8,128]{3,2,1,0:T(8,128)S(1)}) custom-call(f32[9,12,8,128]{3,2,1,0:T(8,128)S(1)} %get-tuple-element.66.s_ref, f32[9,12,8,128]{3,2,1,0:T(8,128)S(1)} %get-tuple-element.53.rest_0_, f32[8,128]{1,0:T(8,128)S(1)} %get-tuple-element.54.rest_1_.pk_ref), custom_call_target="tpu_custom_call" | custom-call | tf_op jit(solution)/shard_map/pallas_call | solution.py:472
  36.2 0.0 collective-permute-done.12.near_ref
  36.2 0.0 collective-permute-done.13.far_ref
  36.2 0.9 %shard_map.67.part_ref = f32[9,12,8,128]{3,2,1,0:T(8,128)S(1)} custom-call(f32[9,12,8,128]{3,2,1,0:T(8,128)S(1)} %get-tuple-element.66.s_ref, f32[9,12,8,128]{3,2,1,0:T(8,128)S(1)} %get-tuple-element.67.speed_ref, f32[9,12,8,128]{3,2,1,0:T(8,128)S(1)} %get-tuple-element.68.part_ref, f32[37,8,128]{2,1,0:T(8,128)S(1)} %collective-permute-done.12.near_ref, ...), custom_call_target="tpu_custom_call" | custom-call | flops 110592000 | bytes 110592000 | tf_op jit(solution)/shard_map/pallas_call | solution.py:472
  37.1 0.7 %shard_map.68.refs_0_ = f32[9,12,8,128]{3,2,1,0:T(8,128)S(1)} custom-call(f32[9,12,8,128]{3,2,1,0:T(8,128)S(1)} %copy-done.1, f32[9,12,8,128]{3,2,1,0:T(8,128)S(1)} %get-tuple-element.66.s_ref, f32[9,12,8,128]{3,2,1,0:T(8,128)S(1)} %shard_map.67.part_ref, f32[38,8,128]{2,1,0:T(8,128)S(1)} %collective-permute-done.11.ghosts_ref, f32[9,2,128]{2,1,0:T(2,128)S(1)} %bitcast.6, ...), custom_call_target="tpu_custom_call" | custom-call | tf_op jit(solution)/shard_map/pallas_call | solution.py:472
  37.8 1.1 %collective-permute-done.14.ghosts_ref = f32[36,8,128]{2,1,0:T(8,128)S(1)} collective-permute-done((f32[36,8,128]{2,1,0:T(8,128)S(1)}, f32[36,8,128]{2,1,0:T(8,128)S(1)}, u32[]{:S(2)}, u32[]{:S(2)}) %collective-permute-start.14) | collective-permute-done | bytes 147488 | tf_op jit(solution)/shard_map/ppermute | solution.py:377
  38.9 1.1 %shard_map.69 = f32[9,12,8,128]{3,2,1,0:T(8,128)} custom-call(f32[9,12,8,128]{3,2,1,0:T(8,128)S(1)} %copy-done.1, f32[9,12,8,128]{3,2,1,0:T(8,128)S(1)} %get-tuple-element.66.s_ref, f32[9,12,8,128]{3,2,1,0:T(8,128)S(1)} %shard_map.67.part_ref, f32[36,8,128]{2,1,0:T(8,128)S(1)} %collective-permute-done.14.ghosts_ref, f32[9,2,128]{2,1,0:T(2,128)S(1)} %bitcast.7, ...), custom_call_target="tpu_custom_call" | custom-call | tf_op jit(solution)/shard_map/pallas_call | solution.py:472
  (4 shorter events, 0.1 us)
Async XLA Ops:
  0.0 0.7 %copy-start.3 = (f32[2,9,128]{2,0,1:T(2,128)S(1)}, f32[2,9,128]{2,0,1:T(2,128)}, u32[]{:S(2)}) copy-start(f32[2,9,128]{2,0,1:T(2,128)} %param.6) | copy-start | bytes 27652
  0.7 9.4 %collective-permute-start = (f32[40,8,128]{2,1,0:T(8,128)S(1)}, f32[40,8,128]{2,1,0:T(8,128)S(1)}, u32[]{:S(2)}, u32[]{:S(2)}) collective-permute-start(f32[40,8,128]{2,1,0:T(8,128)S(1)} %shard_map.56.own_ref), channel_id=1, source_target_pairs={{0,1},{1,0},{2,3},{3,2},{4,5},{5,4},{6,7},{7,6},{8,9},{9,8},{10,11... | collective-permute-start | bytes 491528 | tf_op jit(solution)/shard_map/ppermute | solution.py:500
  2.3 1.0 %copy-start = (f32[9,12,8,128]{3,2,1,0:T(8,128)S(1)}, f32[9,12,8,128]{3,2,1,0:T(8,128)}, u32[]{:S(2)}) copy-start(f32[9,12,8,128]{3,2,1,0:T(8,128)} %base_ref.7) | copy-start | bytes 1327108
  3.3 7.3 %copy-start.1 = (f32[9,12,8,128]{3,2,1,0:T(8,128)S(1)}, f32[9,12,8,128]{3,2,1,0:T(8,128)}, u32[]{:S(2)}) copy-start(f32[9,12,8,128]{3,2,1,0:T(8,128)} %base_ref.7) | copy-start | bytes 1327108
  3.3 10.4 %collective-permute-start.2 = (f32[39,8,128]{2,1,0:T(8,128)S(1)}, f32[39,8,128]{2,1,0:T(8,128)S(1)}, u32[]{:S(2)}, u32[]{:S(2)}) collective-permute-start(f32[39,8,128]{2,1,0:T(8,128)S(1)} %get-tuple-element.42), channel_id=1, source_target_pairs={{1,2},{3,4},{5,6},{2,1},{4,3},{6,5},{0,0},{7,7},{9,10},{11,12},{13... | collective-permute-start | bytes 479240 | tf_op jit(solution)/shard_map/ppermute | solution.py:377
  5.4 10.1 %collective-permute-start.3 = (f32[37,8,128]{2,1,0:T(8,128)S(1)}, f32[37,8,128]{2,1,0:T(8,128)S(1)}, u32[]{:S(2)}, u32[]{:S(2)}) collective-permute-start(f32[37,8,128]{2,1,0:T(8,128)S(1)} %get-tuple-element.44), channel_id=1, source_target_pairs={{0,8},{16,24},{8,0},{24,16},{1,9},{17,25},{9,1},{25,17},{2,10},{18... | collective-permute-start | bytes 454664 | tf_op jit(solution)/shard_map/ppermute | solution.py:377
  5.5 10.0 %collective-permute-start.4 = (f32[37,8,128]{2,1,0:T(8,128)S(1)}, f32[37,8,128]{2,1,0:T(8,128)S(1)}, u32[]{:S(2)}, u32[]{:S(2)}) collective-permute-start(f32[37,8,128]{2,1,0:T(8,128)S(1)} %get-tuple-element.45), channel_id=1, source_target_pairs={{8,16},{24,0},{16,8},{0,24},{9,17},{25,1},{17,9},{1,25},{10,18},{2... | collective-permute-start | bytes 454664 | tf_op jit(solution)/shard_map/ppermute | solution.py:377
  7.5 3.1 %copy-start.2 = (f32[2,48,128]{2,1,0:T(8,128)S(1)}, f32[2,48,128]{2,1,0:T(8,128)}, u32[]{:S(2)}) copy-start(f32[2,48,128]{2,1,0:T(8,128)} %constant.2.clone.rest_1_.waves_ref) | copy-start | bytes 147460
  7.5 3.1 %copy-start.4 = (f32[2,9,128]{2,0,1:T(2,128)S(1)}, f32[2,9,128]{2,0,1:T(2,128)}, u32[]{:S(2)}) copy-start(f32[2,9,128]{2,0,1:T(2,128)} %param.6) | copy-start | bytes 27652
  7.5 8.8 %collective-permute-start.5 = (f32[38,8,128]{2,1,0:T(8,128)S(1)}, f32[38,8,128]{2,1,0:T(8,128)S(1)}, u32[]{:S(2)}, u32[]{:S(2)}) collective-permute-start(f32[38,8,128]{2,1,0:T(8,128)S(1)} %get-tuple-element.46), channel_id=1, source_target_pairs={{0,1},{2,3},{4,5},{6,7},{1,0},{3,2},{5,4},{7,6},{8,9},{10,11},{12,... | collective-permute-start | bytes 466952 | tf_op jit(solution)/shard_map/ppermute | solution.py:377
  10.1 3.6 %collective-permute-start.1 = (f32[8,128]{1,0:T(8,128)S(1)}, f32[8,128]{1,0:T(8,128)S(1)}, u32[]{:S(2)}, u32[]{:S(2)}) collective-permute-start(f32[8,128]{1,0:T(8,128)S(1)} %shard_map.57), channel_id=1, source_target_pairs={{0,2},{1,3},{2,0},{3,1},{4,6},{5,7},{6,4},{7,5},{8,10},{9,11},{10,... | collective-permute-start | bytes 12296 | tf_op jit(solution)/shard_map/ppermute | solution.py:500
  13.7 4.5 %collective-permute-start.6 = (f32[8,128]{1,0:T(8,128)S(1)}, f32[8,128]{1,0:T(8,128)S(1)}, u32[]{:S(2)}, u32[]{:S(2)}) collective-permute-start(f32[8,128]{1,0:T(8,128)S(1)} %max.3.most_ref), channel_id=1, source_target_pairs={{0,4},{1,5},{2,6},{3,7},{4,0},{5,1},{6,2},{7,3},{8,12},{9,13},{10,... | collective-permute-start | bytes 12296 | tf_op jit(solution)/shard_map/ppermute | solution.py:500
  16.3 1.9 %copy-start.5 = (s32[9,128]{1,0:T(8,128)S(1)}, s32[9,128]{1,0:T(8,128)}, u32[]{:S(2)}) copy-start(s32[9,128]{1,0:T(8,128)} %mask_ref.9) | copy-start | bytes 13828
  16.3 1.9 %copy-start.6 = (f32[9,128]{1,0:T(8,128)S(1)}, f32[9,128]{1,0:T(8,128)}, u32[]{:S(2)}) copy-start(f32[9,128]{1,0:T(8,128)} %depth_ref.9) | copy-start | bytes 13828
  18.7 6.9 %collective-permute-start.7 = (f32[38,8,128]{2,1,0:T(8,128)S(1)}, f32[38,8,128]{2,1,0:T(8,128)S(1)}, u32[]{:S(2)}, u32[]{:S(2)}) collective-permute-start(f32[38,8,128]{2,1,0:T(8,128)S(1)} %get-tuple-element.57), channel_id=1, source_target_pairs={{0,1},{2,3},{4,5},{6,7},{1,0},{3,2},{5,4},{7,6},{8,9},{10,11},{12,... | collective-permute-start | bytes 466952 | tf_op jit(solution)/shard_map/ppermute | solution.py:377
  18.8 6.8 %collective-permute-start.8 = (f32[37,8,128]{2,1,0:T(8,128)S(1)}, f32[37,8,128]{2,1,0:T(8,128)S(1)}, u32[]{:S(2)}, u32[]{:S(2)}) collective-permute-start(f32[37,8,128]{2,1,0:T(8,128)S(1)} %get-tuple-element.59), channel_id=1, source_target_pairs={{0,8},{16,24},{8,0},{24,16},{1,9},{17,25},{9,1},{25,17},{2,10},{18... | collective-permute-start | bytes 454664 | tf_op jit(solution)/shard_map/ppermute | solution.py:377
  18.8 6.8 %collective-permute-start.9 = (f32[37,8,128]{2,1,0:T(8,128)S(1)}, f32[37,8,128]{2,1,0:T(8,128)S(1)}, u32[]{:S(2)}, u32[]{:S(2)}) collective-permute-start(f32[37,8,128]{2,1,0:T(8,128)S(1)} %get-tuple-element.60), channel_id=1, source_target_pairs={{8,16},{24,0},{16,8},{0,24},{9,17},{25,1},{17,9},{1,25},{10,18},{2... | collective-permute-start | bytes 454664 | tf_op jit(solution)/shard_map/ppermute | solution.py:377
  19.5 8.8 %collective-permute-start.10 = (f32[36,8,128]{2,1,0:T(8,128)S(1)}, f32[36,8,128]{2,1,0:T(8,128)S(1)}, u32[]{:S(2)}, u32[]{:S(2)}) collective-permute-start(f32[36,8,128]{2,1,0:T(8,128)S(1)} %get-tuple-element.61), channel_id=1, source_target_pairs={{1,2},{3,4},{5,6},{2,1},{4,3},{6,5},{0,0},{7,7},{9,10},{11,12},{13... | collective-permute-start | bytes 442376 | tf_op jit(solution)/shard_map/ppermute | solution.py:377
  27.2 6.9 %collective-permute-start.11 = (f32[38,8,128]{2,1,0:T(8,128)S(1)}, f32[38,8,128]{2,1,0:T(8,128)S(1)}, u32[]{:S(2)}, u32[]{:S(2)}) collective-permute-start(f32[38,8,128]{2,1,0:T(8,128)S(1)} %get-tuple-element.65), channel_id=1, source_target_pairs={{0,1},{2,3},{4,5},{6,7},{1,0},{3,2},{5,4},{7,6},{8,9},{10,11},{12,... | collective-permute-start | bytes 466952 | tf_op jit(solution)/shard_map/ppermute | solution.py:377
  28.6 7.6 %collective-permute-start.12 = (f32[37,8,128]{2,1,0:T(8,128)S(1)}, f32[37,8,128]{2,1,0:T(8,128)S(1)}, u32[]{:S(2)}, u32[]{:S(2)}) collective-permute-start(f32[37,8,128]{2,1,0:T(8,128)S(1)} %get-tuple-element.69), channel_id=1, source_target_pairs={{0,8},{16,24},{8,0},{24,16},{1,9},{17,25},{9,1},{25,17},{2,10},{18... | collective-permute-start | bytes 454664 | tf_op jit(solution)/shard_map/ppermute | solution.py:377
  28.7 7.5 %collective-permute-start.13 = (f32[37,8,128]{2,1,0:T(8,128)S(1)}, f32[37,8,128]{2,1,0:T(8,128)S(1)}, u32[]{:S(2)}, u32[]{:S(2)}) collective-permute-start(f32[37,8,128]{2,1,0:T(8,128)S(1)} %get-tuple-element.70), channel_id=1, source_target_pairs={{8,16},{24,0},{16,8},{0,24},{9,17},{25,1},{17,9},{1,25},{10,18},{2... | collective-permute-start | bytes 454664 | tf_op jit(solution)/shard_map/ppermute | solution.py:377
  30.3 8.6 %collective-permute-start.14 = (f32[36,8,128]{2,1,0:T(8,128)S(1)}, f32[36,8,128]{2,1,0:T(8,128)S(1)}, u32[]{:S(2)}, u32[]{:S(2)}) collective-permute-start(f32[36,8,128]{2,1,0:T(8,128)S(1)} %get-tuple-element.71), channel_id=1, source_target_pairs={{1,2},{3,4},{5,6},{2,1},{4,3},{6,5},{0,0},{7,7},{9,10},{11,12},{13... | collective-permute-start | bytes 442376 | tf_op jit(solution)/shard_map/ppermute | solution.py:377

commit v11 on v10

--- a/solution.py
+++ b/solution.py
@@ -40,19 +40,40 @@
     return minus, plus
 
 
-def row_terms(cells, step):
-    count = len(cells) - 2 * rim
+def row_terms(cells, step, closed=False):
     eps = epsilon * step * step
-    slope = [cells[i + 1] - cells[i] for i in range(len(cells) - 1)]
-    bend = {m: slope[m + 3] - slope[m + 2] for m in range(-2, count + 2)}
-    turn = {m: bend[m + 1] - bend[m] for m in range(-2, count + 1)}
-    jerk = {m: turn[m] - turn[m - 1] for m in range(-1, count + 1)}
+    count = len(cells) if closed else len(cells) - 2 * rim
+    shift = 0 if closed else rim
+    slope = {m: cells[m + 1 + shift] - cells[m + shift] for m in range(-shift, count + shift - 1)}
     a, b, c = {}, {}, {}
-    for m in turn:
+    if closed:
+        bend = {m: slope[m] - slope[m - 1] for m in range(1, count - 1)}
+        bend[0], bend[count - 1] = slope[0], -slope[count - 2]
+        turn = {m: bend[m + 1] - bend[m] for m in range(count - 1)}
+        turn[-1], turn[count - 1] = bend[0], -bend[count - 1]
+        jerk = {m: turn[m] - turn[m - 1] for m in range(count)}
+        jerk[-1], jerk[count] = bend[0], bend[count - 1]
+        rise = {m: slope[m] + slope[m - 1] for m in range(1, count - 1)}
+        rise[0], rise[count - 1] = slope[0], slope[count - 2]
+        a[-2] = c[count] = 1.0 / (eps * eps)
+        for m, (e1, e2) in ((-1, (None, bend[0])), (count - 1, (bend[count - 1], None))):
+            square = turn[m] * turn[m]
+            level = square * (4.0 / 3.0) + eps
+            ib, outer = inverse(level), inverse(level + (square + square))
+            b[m] = ib * ib * 6.0
+            (c if e2 is None else a)[m] = outer * outer
+        inner = range(count - 1)
+    else:
+        bend = {m: slope[m] - slope[m - 1] for m in range(-2, count + 2)}
+        turn = {m: bend[m + 1] - bend[m] for m in range(-2, count + 1)}
+        jerk = {m: turn[m] - turn[m - 1] for m in range(-1, count + 1)}
+        rise = {m: cells[m + 1 + rim] - cells[m - 1 + rim] for m in range(count)}
+        inner = range(-2, count + 1)
+    for m in inner:
         a[m], b[m], c[m] = weights_of(bend[m], bend[m + 1], turn[m], eps)
     out = []
     for i in range(count):
-        base = (cells[i + 4] - cells[i + 2]) * 6.0 - (turn[i - 1] + turn[i])
+        base = rise[i] * 6.0 - (turn[i - 1] + turn[i])
         minus, plus = sides(
             jerk[i - 1], jerk[i], jerk[i + 1], a[i - 2], a[i - 1], b[i - 1], b[i], c[i], c[i + 1]
         )
@@ -140,8 +161,7 @@
         start = jnp.minimum(n * few, cells - few) * speeds
         spots = [pl.ds(start + v, few, stride=speeds) for v in range(speeds)]
         rows = [s_rows[spot, :] for spot in spots]
-        ends = [rows[0]] * rim + rows + [rows[-1]] * rim
-        for spot, (mean, gap) in zip(spots, row_terms(ends, speed_step)):
+        for spot, (mean, gap) in zip(spots, row_terms(rows, speed_step, True)):
             speed_rows[spot, :] = gain_v * (gap - jnp.abs(mean))
 
     def span(n):
@@ -503,10 +523,11 @@
     other = spread(most, 1)
     x_shapes = [shape(longest), shape(longest + 1)]
     x_out, x_last, t_out, t_last = call(opening_kernel, [values], x_shapes + [shape(middle)] * 2)
-    far_shapes = [shape(short), shape(middle), shape(middle)]
+    far_shapes = [shape(short), shape(rim * planes), shape(middle)]
     for section in (1, 2, 3):
         opening = section == 1
-        x_near = trade(x_out, "gx", 0)
+        if not opening:
+            x_near = trade(x_out, "gx", 0)
         t_near = trade(t_out, "head", 0)
         t_far = trade(t_last, "head", 1, True)
         x_far = trade(x_last, "gx", 1)
@@ -515,14 +536,11 @@
         if opening:
             (most,) = call(meeting_kernel, [most, other], [shape()])
             other = spread(most, 2)
+            values, most = lax.optimization_barrier((values, most))
             ins = [values, wind, waves]
             spun, part, extra, flow = call(free, ins, [field] * 4, room, work=300)
-            reach = 4
-            while reach < size:
-                most = jnp.maximum(most, other)
-                most, part = lax.optimization_barrier((most, part))
-                other = spread(most, reach)
-                reach *= 2
+            x_out, part = lax.optimization_barrier((x_out, part))
+            x_near = trade(x_out, "gx", 0)
             part, x_far = lax.optimization_barrier((part, x_far))
         else:
             if section == 3:
@@ -532,6 +550,12 @@
                 part, x_near = lax.optimization_barrier((part, x_near))
         (part,) = call(turning, [values, spun, part, t_near, t_far], [field], work=1000)
         if opening:
+            reach = 4
+            while reach < size:
+                most = jnp.maximum(most, other)
+                most, part = lax.optimization_barrier((most, part))
+                other = spread(most, reach)
+                reach *= 2
             ins = [values, part, x_near, x_far, wind, waves]
             first = functools.partial(first_kernel, speed_step)
             part, gap = call(first, ins, [field] * 2, [rows])

time: 40.8 us -> 42.3 us (1.037)
  waiting for transfers between devices: 3.12 us -> 7.14 us
  starting transfers between devices: 21.7 us -> 19.7 us
    ppermute x3, waiting for transfers between devices: 1.98 us -> 4.87 us  [spread(): return lax.ppermute(most, 'gx', pairs)]
    ppermute x12, starting transfers between devices: 18 us -> 16.6 us  [trade(): return lax.ppermute(value, axis, pairs)]
    ppermute x12, waiting for transfers between devices: 1.14 us -> 2.27 us  [trade(): return lax.ppermute(value, axis, pairs)]
    ppermute x3, starting transfers between devices: 3.74 us -> 3.04 us  [spread(): return lax.ppermute(most, 'gx', pairs)]
  transfers between devices with their start and end apart: 15 -> 15, of which waited for: 3 -> 4; matrix products, arithmetic and copies ran while one was open for 0% -> 0% of each run, Pallas kernels for 29% -> 28%
where the time goes in v11:
time: 42.3 us; the launch traced here: 41.9 us
  starting transfers between devices  19.7 us (47%)
  Pallas kernels  13.2 us (31%)
  waiting for transfers between devices  7.14 us (17%)
  local copies, waits for them, and re-layouts  1.74 us (4%)
    ppermute x12, starting transfers between devices, trade(): return lax.ppermute(value, axis, pairs)  16.6 us
    pallas_call x15, Pallas kernels, call(): pl.pallas_call(kernel, out_shape=outs, in_specs=[vmem] * len(ins), out_sp...  13.2 us
    ppermute x3, waiting for transfers between devices, spread(): return lax.ppermute(most, 'gx', pairs)  4.87 us
    ppermute x3, starting transfers between devices, spread(): return lax.ppermute(most, 'gx', pairs)  3.04 us
    ppermute x12, waiting for transfers between devices, trade(): return lax.ppermute(value, axis, pairs)  2.27 us
    unnamed x14, local copies, waits for them, and re-layouts  1.74 us
  transfers between devices with their start and end apart: 15, of which 4 were waited for; matrix products, arithmetic and copies ran while one was open for 0% of the time, Pallas kernels for 28%

profile of v11, /device:TPU:8, one launch (start us, length us, event | category | flops | bytes accessed | tf_op | source)
XLA Modules:
  0.0 41.9 jit_solution(3650770905155767936)
XLA Ops:
  0.0 0.0 copy-start.3
  0.0 0.7 %copy-done.3 = f32[2,9,128]{2,0,1:T(2,128)S(1)} copy-done((f32[2,9,128]{2,0,1:T(2,128)S(1)}, f32[2,9,128]{2,0,1:T(2,128)}, u32[]{:S(2)}) %copy-start.3) | copy-done | bytes 9240
  0.7 1.6 %collective-permute-start = (f32[40,8,128]{2,1,0:T(8,128)S(1)}, f32[40,8,128]{2,1,0:T(8,128)S(1)}, u32[]{:S(2)}, u32[]{:S(2)}) collective-permute-start(f32[40,8,128]{2,1,0:T(8,128)S(1)} %shard_map.55.own_ref), channel_id=1, source_target_pairs={{0,1},{1,0},{2,3},{3,2},{4,5},{5,4},{6,7},{7,6},{8,9},{9,8},{10,11... | collective-permute-start | bytes 491528 | tf_op jit(solution)/shard_map/ppermute | solution.py:520
  2.3 0.0 copy-start
  2.3 1.0 %copy-done = f32[9,12,8,128]{3,2,1,0:T(8,128)S(1)} copy-done((f32[9,12,8,128]{3,2,1,0:T(8,128)S(1)}, f32[9,12,8,128]{3,2,1,0:T(8,128)}, u32[]{:S(2)}) %copy-start) | copy-done | bytes 442392
  3.3 0.0 copy-start.1
  3.3 2.1 %collective-permute-start.2 = (f32[39,8,128]{2,1,0:T(8,128)S(1)}, f32[39,8,128]{2,1,0:T(8,128)S(1)}, u32[]{:S(2)}, u32[]{:S(2)}) collective-permute-start(f32[39,8,128]{2,1,0:T(8,128)S(1)} %get-tuple-element.49), channel_id=1, source_target_pairs={{1,2},{3,4},{5,6},{2,1},{4,3},{6,5},{0,0},{7,7},{9,10},{11,12},{13... | collective-permute-start | bytes 479240 | tf_op jit(solution)/shard_map/ppermute | solution.py:397
  5.4 0.1 collective-permute-start.3
  5.5 0.0 copy-start.2
  5.5 0.0 copy-start.4
  5.5 2.0 %collective-permute-start.4 = (f32[37,8,128]{2,1,0:T(8,128)S(1)}, f32[37,8,128]{2,1,0:T(8,128)S(1)}, u32[]{:S(2)}, u32[]{:S(2)}) collective-permute-start(f32[37,8,128]{2,1,0:T(8,128)S(1)} %get-tuple-element.52), channel_id=1, source_target_pairs={{8,16},{24,0},{16,8},{0,24},{9,17},{25,1},{17,9},{1,25},{10,18},{2... | collective-permute-start | bytes 454664 | tf_op jit(solution)/shard_map/ppermute | solution.py:397
  7.5 0.0 collective-permute-done.other_ref
  7.5 0.0 copy-done.1
  7.5 0.0 copy-done.2
  7.5 0.0 copy-done.4
  7.5 2.1 %shard_map.57 = (f32[9,12,8,128]{3,2,1,0:T(8,128)S(1)}, f32[9,12,8,128]{3,2,1,0:T(8,128)S(1)}, f32[9,12,8,128]{3,2,1,0:T(8,128)S(1)}, f32[9,12,8,128]{3,2,1,0:T(8,128)S(1)}) custom-call(f32[9,12,8,128]{3,2,1,0:T(8,128)S(1)} %copy-done.1, f32[9,2,128]{2,1,0:T(2,128)S(1)} %bitcast.2, f32[2,48,128]{2,1,0:T(8,128)S(1)} %copy-done.2), custom_call_target="tpu_custom_call" | custom-call | flops 33177600 | bytes 33177600 | tf_op jit(solution)/shard_map/pallas_call | solution.py:492
  9.6 2.7 %collective-permute-start.5 = (f32[38,8,128]{2,1,0:T(8,128)S(1)}, f32[38,8,128]{2,1,0:T(8,128)S(1)}, u32[]{:S(2)}, u32[]{:S(2)}) collective-permute-start(f32[38,8,128]{2,1,0:T(8,128)S(1)} %get-tuple-element.54), channel_id=1, source_target_pairs={{0,1},{2,3},{4,5},{6,7},{1,0},{3,2},{5,4},{7,6},{8,9},{10,11},{12,... | collective-permute-start | bytes 466952 | tf_op jit(solution)/shard_map/ppermute | solution.py:397
  12.4 0.4 %collective-permute-start.1 = (f32[8,128]{1,0:T(8,128)S(1)}, f32[8,128]{1,0:T(8,128)S(1)}, u32[]{:S(2)}, u32[]{:S(2)}) collective-permute-start(f32[8,128]{1,0:T(8,128)S(1)} %shard_map.56), channel_id=1, source_target_pairs={{0,2},{1,3},{2,0},{3,1},{4,6},{5,7},{6,4},{7,5},{8,10},{9,11},{10,... | collective-permute-start | bytes 12296 | tf_op jit(solution)/shard_map/ppermute | solution.py:520
  12.8 0.0 collective-permute-done.2.far_ref
  12.8 0.0 collective-permute-done.3.near_ref
  12.8 0.0 collective-permute-done.4.far_ref
  12.8 0.9 %shard_map.59.part_ref = f32[9,12,8,128]{3,2,1,0:T(8,128)S(1)} custom-call(f32[9,12,8,128]{3,2,1,0:T(8,128)S(1)} %copy-done.1, f32[9,12,8,128]{3,2,1,0:T(8,128)S(1)} %get-tuple-element.45.speed_ref, f32[9,12,8,128]{3,2,1,0:T(8,128)S(1)} %get-tuple-element.50.part_ref, f32[37,8,128]{2,1,0:T(8,128)S(1)} %collective-permute-done.3.near_ref, ...), custom_call_target="tpu_custom_call" | custom-call | flops 110592000 | bytes 110592000 | tf_op jit(solution)/shard_map/pallas_call | solution.py:492
  13.7 2.3 %collective-permute-done.1 = f32[8,128]{1,0:T(8,128)S(1)} collective-permute-done((f32[8,128]{1,0:T(8,128)S(1)}, f32[8,128]{1,0:T(8,128)S(1)}, u32[]{:S(2)}, u32[]{:S(2)}) %collective-permute-start.1) | collective-permute-done | bytes 4128 | tf_op jit(solution)/shard_map/ppermute | solution.py:520
  16.0 1.0 %collective-permute-start.6 = (f32[8,128]{1,0:T(8,128)S(1)}, f32[8,128]{1,0:T(8,128)S(1)}, u32[]{:S(2)}, u32[]{:S(2)}) collective-permute-start(f32[8,128]{1,0:T(8,128)S(1)} %max.3.most_ref), channel_id=1, source_target_pairs={{0,4},{1,5},{2,6},{3,7},{4,0},{5,1},{6,2},{7,3},{8,12},{9,13},{10,... | collective-permute-start | bytes 12296 | tf_op jit(solution)/shard_map/ppermute | solution.py:520
  17.0 0.0 collective-permute-done.5.near_ref
  17.0 0.0 copy-start.5
  17.0 0.0 copy-start.6
  17.0 0.9 %shard_map.60 = (f32[9,12,8,128]{3,2,1,0:T(8,128)S(1)}, f32[9,12,8,128]{3,2,1,0:T(8,128)S(1)}) custom-call(f32[9,12,8,128]{3,2,1,0:T(8,128)S(1)} %copy-done.1, f32[9,12,8,128]{3,2,1,0:T(8,128)S(1)} %shard_map.59.part_ref, f32[38,8,128]{2,1,0:T(8,128)S(1)} %collective-permute-done.5.near_ref, f32[39,8,128]{2,1,0:T(8,128)S(1)} %collective-permute-done.2.far_ref, ...), custom_call_target="tpu_custom_call" | custom-call | tf_op jit(solution)/shard_map/pallas_call | solution.py:492
  17.9 2.6 %collective-permute-done.6.other_ref = f32[8,128]{1,0:T(8,128)S(1)} collective-permute-done((f32[8,128]{1,0:T(8,128)S(1)}, f32[8,128]{1,0:T(8,128)S(1)}, u32[]{:S(2)}, u32[]{:S(2)}) %collective-permute-start.6) | collective-permute-done | bytes 4128 | tf_op jit(solution)/shard_map/ppermute | solution.py:520
  20.5 0.0 copy-done.5
  20.5 0.0 copy-done.6
  20.5 0.4 shard_map.61
  20.9 0.1 collective-permute-start.7
  21.0 0.0 collective-permute-start.9
  21.0 3.7 %collective-permute-start.10 = (f32[36,8,128]{2,1,0:T(8,128)S(1)}, f32[36,8,128]{2,1,0:T(8,128)S(1)}, u32[]{:S(2)}, u32[]{:S(2)}) collective-permute-start(f32[36,8,128]{2,1,0:T(8,128)S(1)} %get-tuple-element.69), channel_id=1, source_target_pairs={{1,2},{3,4},{5,6},{2,1},{4,3},{6,5},{0,0},{7,7},{9,10},{11,12},{13... | collective-permute-start | bytes 442376 | tf_op jit(solution)/shard_map/ppermute | solution.py:397
  24.8 0.5 %collective-permute-start.8 = (f32[27,8,128]{2,1,0:T(8,128)S(1)}, f32[27,8,128]{2,1,0:T(8,128)S(1)}, u32[]{:S(2)}, u32[]{:S(2)}) collective-permute-start(f32[27,8,128]{2,1,0:T(8,128)S(1)} %get-tuple-element.67), channel_id=1, source_target_pairs={{0,8},{16,24},{8,0},{24,16},{1,9},{17,25},{9,1},{25,17},{2,10},{18... | collective-permute-start | bytes 331784 | tf_op jit(solution)/shard_map/ppermute | solution.py:397
  25.3 2.1 %shard_map.62 = (f32[9,12,8,128]{3,2,1,0:T(8,128)S(1)}, f32[9,12,8,128]{3,2,1,0:T(8,128)S(1)}) custom-call(f32[9,12,8,128]{3,2,1,0:T(8,128)S(1)} %get-tuple-element.60.s_ref, f32[9,12,8,128]{3,2,1,0:T(8,128)S(1)} %get-tuple-element.61.rest_0_, f32[8,128]{1,0:T(8,128)S(1)} %get-tuple-element.62.rest_1_.pk_ref), custom_call_target="tpu_custom_call" | custom-call | tf_op jit(solution)/shard_map/pallas_call | solution.py:492
  27.4 0.0 collective-permute-done.7.ghosts_ref
  27.4 0.0 collective-permute-done.8.near_ref
  27.4 0.0 collective-permute-done.9.far_ref
  27.4 0.9 %shard_map.63.part_ref = f32[9,12,8,128]{3,2,1,0:T(8,128)S(1)} custom-call(f32[9,12,8,128]{3,2,1,0:T(8,128)S(1)} %get-tuple-element.60.s_ref, f32[9,12,8,128]{3,2,1,0:T(8,128)S(1)} %get-tuple-element.63.speed_ref, f32[9,12,8,128]{3,2,1,0:T(8,128)S(1)} %get-tuple-element.66.part_ref, f32[27,8,128]{2,1,0:T(8,128)S(1)} %collective-permute-done.8.near_ref, ...), custom_call_target="tpu_custom_call" | custom-call | flops 110592000 | bytes 110592000 | tf_op jit(solution)/shard_map/pallas_call | solution.py:492
  28.3 0.7 %shard_map.64 = (f32[9,12,8,128]{3,2,1,0:T(8,128)S(1)}, f32[38,8,128]{2,1,0:T(8,128)S(1)}) custom-call(f32[9,12,8,128]{3,2,1,0:T(8,128)S(1)} %copy-done.1, f32[9,12,8,128]{3,2,1,0:T(8,128)S(1)} %get-tuple-element.60.s_ref, f32[9,12,8,128]{3,2,1,0:T(8,128)S(1)} %shard_map.63.part_ref, f32[38,8,128]{2,1,0:T(8,128)S(1)} %collective-permute-done.7.ghosts_ref, ...), custom_call_target="tpu_custom_call" | custom-call | tf_op jit(solution)/shard_map/pallas_call | solution.py:492
  29.0 1.3 %collective-permute-start.11 = (f32[38,8,128]{2,1,0:T(8,128)S(1)}, f32[38,8,128]{2,1,0:T(8,128)S(1)}, u32[]{:S(2)}, u32[]{:S(2)}) collective-permute-start(f32[38,8,128]{2,1,0:T(8,128)S(1)} %get-tuple-element.73), channel_id=1, source_target_pairs={{0,1},{2,3},{4,5},{6,7},{1,0},{3,2},{5,4},{7,6},{8,9},{10,11},{12,... | collective-permute-start | bytes 466952 | tf_op jit(solution)/shard_map/ppermute | solution.py:397
  30.3 0.0 collective-permute-done.10.ghosts_ref
  30.3 0.4 shard_map.65
  30.8 0.7 %collective-permute-start.13 = (f32[37,8,128]{2,1,0:T(8,128)S(1)}, f32[37,8,128]{2,1,0:T(8,128)S(1)}, u32[]{:S(2)}, u32[]{:S(2)}) collective-permute-start(f32[37,8,128]{2,1,0:T(8,128)S(1)} %get-tuple-element.78), channel_id=1, source_target_pairs={{8,16},{24,0},{16,8},{0,24},{9,17},{25,1},{17,9},{1,25},{10,18},{2... | collective-permute-start | bytes 454664 | tf_op jit(solution)/shard_map/ppermute | solution.py:397
  31.5 3.3 %collective-permute-start.14 = (f32[36,8,128]{2,1,0:T(8,128)S(1)}, f32[36,8,128]{2,1,0:T(8,128)S(1)}, u32[]{:S(2)}, u32[]{:S(2)}) collective-permute-start(f32[36,8,128]{2,1,0:T(8,128)S(1)} %get-tuple-element.79), channel_id=1, source_target_pairs={{1,2},{3,4},{5,6},{2,1},{4,3},{6,5},{0,0},{7,7},{9,10},{11,12},{13... | collective-permute-start | bytes 442376 | tf_op jit(solution)/shard_map/ppermute | solution.py:397
  34.8 0.1 collective-permute-start.12
  34.9 0.1 collective-permute-done.11.ghosts_ref
  35.0 2.1 %shard_map.66 = (f32[9,12,8,128]{3,2,1,0:T(8,128)S(1)}, f32[9,12,8,128]{3,2,1,0:T(8,128)S(1)}) custom-call(f32[9,12,8,128]{3,2,1,0:T(8,128)S(1)} %get-tuple-element.74.s_ref, f32[9,12,8,128]{3,2,1,0:T(8,128)S(1)} %get-tuple-element.61.rest_0_, f32[8,128]{1,0:T(8,128)S(1)} %get-tuple-element.62.rest_1_.pk_ref), custom_call_target="tpu_custom_call" | custom-call | tf_op jit(solution)/shard_map/pallas_call | solution.py:492
  37.1 0.0 collective-permute-done.12.near_ref
  37.1 0.0 collective-permute-done.13.far_ref
  37.1 0.9 %shard_map.67.part_ref = f32[9,12,8,128]{3,2,1,0:T(8,128)S(1)} custom-call(f32[9,12,8,128]{3,2,1,0:T(8,128)S(1)} %get-tuple-element.74.s_ref, f32[9,12,8,128]{3,2,1,0:T(8,128)S(1)} %get-tuple-element.75.speed_ref, f32[9,12,8,128]{3,2,1,0:T(8,128)S(1)} %get-tuple-element.76.part_ref, f32[27,8,128]{2,1,0:T(8,128)S(1)} %collective-permute-done.12.near_ref, ...), custom_call_target="tpu_custom_call" | custom-call | flops 110592000 | bytes 110592000 | tf_op jit(solution)/shard_map/pallas_call | solution.py:492
  38.0 0.7 %shard_map.68.refs_0_ = f32[9,12,8,128]{3,2,1,0:T(8,128)S(1)} custom-call(f32[9,12,8,128]{3,2,1,0:T(8,128)S(1)} %copy-done.1, f32[9,12,8,128]{3,2,1,0:T(8,128)S(1)} %get-tuple-element.74.s_ref, f32[9,12,8,128]{3,2,1,0:T(8,128)S(1)} %shard_map.67.part_ref, f32[38,8,128]{2,1,0:T(8,128)S(1)} %collective-permute-done.11.ghosts_ref, f32[9,2,128]{2,1,0:T(2,128)S(1)} %bitcast.6, ...), custom_call_target="tpu_custom_call" | custom-call | tf_op jit(solution)/shard_map/pallas_call | solution.py:492
  38.7 2.1 %collective-permute-done.14.ghosts_ref = f32[36,8,128]{2,1,0:T(8,128)S(1)} collective-permute-done((f32[36,8,128]{2,1,0:T(8,128)S(1)}, f32[36,8,128]{2,1,0:T(8,128)S(1)}, u32[]{:S(2)}, u32[]{:S(2)}) %collective-permute-start.14) | collective-permute-done | bytes 147488 | tf_op jit(solution)/shard_map/ppermute | solution.py:397
  40.8 1.1 %shard_map.69 = f32[9,12,8,128]{3,2,1,0:T(8,128)} custom-call(f32[9,12,8,128]{3,2,1,0:T(8,128)S(1)} %copy-done.1, f32[9,12,8,128]{3,2,1,0:T(8,128)S(1)} %get-tuple-element.74.s_ref, f32[9,12,8,128]{3,2,1,0:T(8,128)S(1)} %shard_map.67.part_ref, f32[36,8,128]{2,1,0:T(8,128)S(1)} %collective-permute-done.14.ghosts_ref, f32[9,2,128]{2,1,0:T(2,128)S(1)} %bitcast.7, ...), custom_call_target="tpu_custom_call" | custom-call | tf_op jit(solution)/shard_map/pallas_call | solution.py:492
  (4 shorter events, 0.1 us)
Async XLA Ops:
  0.0 0.7 %copy-start.3 = (f32[2,9,128]{2,0,1:T(2,128)S(1)}, f32[2,9,128]{2,0,1:T(2,128)}, u32[]{:S(2)}) copy-start(f32[2,9,128]{2,0,1:T(2,128)} %param.6) | copy-start | bytes 27652
  0.7 6.8 %collective-permute-start = (f32[40,8,128]{2,1,0:T(8,128)S(1)}, f32[40,8,128]{2,1,0:T(8,128)S(1)}, u32[]{:S(2)}, u32[]{:S(2)}) collective-permute-start(f32[40,8,128]{2,1,0:T(8,128)S(1)} %shard_map.55.own_ref), channel_id=1, source_target_pairs={{0,1},{1,0},{2,3},{3,2},{4,5},{5,4},{6,7},{7,6},{8,9},{9,8},{10,11... | collective-permute-start | bytes 491528 | tf_op jit(solution)/shard_map/ppermute | solution.py:520
  2.3 1.0 %copy-start = (f32[9,12,8,128]{3,2,1,0:T(8,128)S(1)}, f32[9,12,8,128]{3,2,1,0:T(8,128)}, u32[]{:S(2)}) copy-start(f32[9,12,8,128]{3,2,1,0:T(8,128)} %base_ref.7) | copy-start | bytes 1327108
  3.3 4.2 %copy-start.1 = (f32[9,12,8,128]{3,2,1,0:T(8,128)S(1)}, f32[9,12,8,128]{3,2,1,0:T(8,128)}, u32[]{:S(2)}) copy-start(f32[9,12,8,128]{3,2,1,0:T(8,128)} %base_ref.7) | copy-start | bytes 1327108
  3.3 9.5 %collective-permute-start.2 = (f32[39,8,128]{2,1,0:T(8,128)S(1)}, f32[39,8,128]{2,1,0:T(8,128)S(1)}, u32[]{:S(2)}, u32[]{:S(2)}) collective-permute-start(f32[39,8,128]{2,1,0:T(8,128)S(1)} %get-tuple-element.49), channel_id=1, source_target_pairs={{1,2},{3,4},{5,6},{2,1},{4,3},{6,5},{0,0},{7,7},{9,10},{11,12},{13... | collective-permute-start | bytes 479240 | tf_op jit(solution)/shard_map/ppermute | solution.py:397
  5.4 7.4 %collective-permute-start.3 = (f32[37,8,128]{2,1,0:T(8,128)S(1)}, f32[37,8,128]{2,1,0:T(8,128)S(1)}, u32[]{:S(2)}, u32[]{:S(2)}) collective-permute-start(f32[37,8,128]{2,1,0:T(8,128)S(1)} %get-tuple-element.51), channel_id=1, source_target_pairs={{0,8},{16,24},{8,0},{24,16},{1,9},{17,25},{9,1},{25,17},{2,10},{18... | collective-permute-start | bytes 454664 | tf_op jit(solution)/shard_map/ppermute | solution.py:397
  5.5 2.0 %copy-start.2 = (f32[2,48,128]{2,1,0:T(8,128)S(1)}, f32[2,48,128]{2,1,0:T(8,128)}, u32[]{:S(2)}) copy-start(f32[2,48,128]{2,1,0:T(8,128)} %constant.2.clone.rest_1_.waves_ref) | copy-start | bytes 147460
  5.5 2.0 %copy-start.4 = (f32[2,9,128]{2,0,1:T(2,128)S(1)}, f32[2,9,128]{2,0,1:T(2,128)}, u32[]{:S(2)}) copy-start(f32[2,9,128]{2,0,1:T(2,128)} %param.6) | copy-start | bytes 27652
  5.5 7.3 %collective-permute-start.4 = (f32[37,8,128]{2,1,0:T(8,128)S(1)}, f32[37,8,128]{2,1,0:T(8,128)S(1)}, u32[]{:S(2)}, u32[]{:S(2)}) collective-permute-start(f32[37,8,128]{2,1,0:T(8,128)S(1)} %get-tuple-element.52), channel_id=1, source_target_pairs={{8,16},{24,0},{16,8},{0,24},{9,17},{25,1},{17,9},{1,25},{10,18},{2... | collective-permute-start | bytes 454664 | tf_op jit(solution)/shard_map/ppermute | solution.py:397
  9.6 7.3 %collective-permute-start.5 = (f32[38,8,128]{2,1,0:T(8,128)S(1)}, f32[38,8,128]{2,1,0:T(8,128)S(1)}, u32[]{:S(2)}, u32[]{:S(2)}) collective-permute-start(f32[38,8,128]{2,1,0:T(8,128)S(1)} %get-tuple-element.54), channel_id=1, source_target_pairs={{0,1},{2,3},{4,5},{6,7},{1,0},{3,2},{5,4},{7,6},{8,9},{10,11},{12,... | collective-permute-start | bytes 466952 | tf_op jit(solution)/shard_map/ppermute | solution.py:397
  12.4 3.6 %collective-permute-start.1 = (f32[8,128]{1,0:T(8,128)S(1)}, f32[8,128]{1,0:T(8,128)S(1)}, u32[]{:S(2)}, u32[]{:S(2)}) collective-permute-start(f32[8,128]{1,0:T(8,128)S(1)} %shard_map.56), channel_id=1, source_target_pairs={{0,2},{1,3},{2,0},{3,1},{4,6},{5,7},{6,4},{7,5},{8,10},{9,11},{10,... | collective-permute-start | bytes 12296 | tf_op jit(solution)/shard_map/ppermute | solution.py:520
  16.0 4.5 %collective-permute-start.6 = (f32[8,128]{1,0:T(8,128)S(1)}, f32[8,128]{1,0:T(8,128)S(1)}, u32[]{:S(2)}, u32[]{:S(2)}) collective-permute-start(f32[8,128]{1,0:T(8,128)S(1)} %max.3.most_ref), channel_id=1, source_target_pairs={{0,4},{1,5},{2,6},{3,7},{4,0},{5,1},{6,2},{7,3},{8,12},{9,13},{10,... | collective-permute-start | bytes 12296 | tf_op jit(solution)/shard_map/ppermute | solution.py:520
  17.0 3.5 %copy-start.5 = (s32[9,128]{1,0:T(8,128)S(1)}, s32[9,128]{1,0:T(8,128)}, u32[]{:S(2)}) copy-start(s32[9,128]{1,0:T(8,128)} %mask_ref.9) | copy-start | bytes 13828
  17.0 3.5 %copy-start.6 = (f32[9,128]{1,0:T(8,128)S(1)}, f32[9,128]{1,0:T(8,128)}, u32[]{:S(2)}) copy-start(f32[9,128]{1,0:T(8,128)} %depth_ref.9) | copy-start | bytes 13828
  20.9 6.5 %collective-permute-start.7 = (f32[38,8,128]{2,1,0:T(8,128)S(1)}, f32[38,8,128]{2,1,0:T(8,128)S(1)}, u32[]{:S(2)}, u32[]{:S(2)}) collective-permute-start(f32[38,8,128]{2,1,0:T(8,128)S(1)} %get-tuple-element.65), channel_id=1, source_target_pairs={{0,1},{2,3},{4,5},{6,7},{1,0},{3,2},{5,4},{7,6},{8,9},{10,11},{12,... | collective-permute-start | bytes 466952 | tf_op jit(solution)/shard_map/ppermute | solution.py:397
  21.0 6.4 %collective-permute-start.9 = (f32[37,8,128]{2,1,0:T(8,128)S(1)}, f32[37,8,128]{2,1,0:T(8,128)S(1)}, u32[]{:S(2)}, u32[]{:S(2)}) collective-permute-start(f32[37,8,128]{2,1,0:T(8,128)S(1)} %get-tuple-element.68), channel_id=1, source_target_pairs={{8,16},{24,0},{16,8},{0,24},{9,17},{25,1},{17,9},{1,25},{10,18},{2... | collective-permute-start | bytes 454664 | tf_op jit(solution)/shard_map/ppermute | solution.py:397
  21.0 9.3 %collective-permute-start.10 = (f32[36,8,128]{2,1,0:T(8,128)S(1)}, f32[36,8,128]{2,1,0:T(8,128)S(1)}, u32[]{:S(2)}, u32[]{:S(2)}) collective-permute-start(f32[36,8,128]{2,1,0:T(8,128)S(1)} %get-tuple-element.69), channel_id=1, source_target_pairs={{1,2},{3,4},{5,6},{2,1},{4,3},{6,5},{0,0},{7,7},{9,10},{11,12},{13... | collective-permute-start | bytes 442376 | tf_op jit(solution)/shard_map/ppermute | solution.py:397
  24.8 2.6 %collective-permute-start.8 = (f32[27,8,128]{2,1,0:T(8,128)S(1)}, f32[27,8,128]{2,1,0:T(8,128)S(1)}, u32[]{:S(2)}, u32[]{:S(2)}) collective-permute-start(f32[27,8,128]{2,1,0:T(8,128)S(1)} %get-tuple-element.67), channel_id=1, source_target_pairs={{0,8},{16,24},{8,0},{24,16},{1,9},{17,25},{9,1},{25,17},{2,10},{18... | collective-permute-start | bytes 331784 | tf_op jit(solution)/shard_map/ppermute | solution.py:397
  29.0 6.0 %collective-permute-start.11 = (f32[38,8,128]{2,1,0:T(8,128)S(1)}, f32[38,8,128]{2,1,0:T(8,128)S(1)}, u32[]{:S(2)}, u32[]{:S(2)}) collective-permute-start(f32[38,8,128]{2,1,0:T(8,128)S(1)} %get-tuple-element.73), channel_id=1, source_target_pairs={{0,1},{2,3},{4,5},{6,7},{1,0},{3,2},{5,4},{7,6},{8,9},{10,11},{12,... | collective-permute-start | bytes 466952 | tf_op jit(solution)/shard_map/ppermute | solution.py:397
  30.8 6.4 %collective-permute-start.13 = (f32[37,8,128]{2,1,0:T(8,128)S(1)}, f32[37,8,128]{2,1,0:T(8,128)S(1)}, u32[]{:S(2)}, u32[]{:S(2)}) collective-permute-start(f32[37,8,128]{2,1,0:T(8,128)S(1)} %get-tuple-element.78), channel_id=1, source_target_pairs={{8,16},{24,0},{16,8},{0,24},{9,17},{25,1},{17,9},{1,25},{10,18},{2... | collective-permute-start | bytes 454664 | tf_op jit(solution)/shard_map/ppermute | solution.py:397
  31.5 9.3 %collective-permute-start.14 = (f32[36,8,128]{2,1,0:T(8,128)S(1)}, f32[36,8,128]{2,1,0:T(8,128)S(1)}, u32[]{:S(2)}, u32[]{:S(2)}) collective-permute-start(f32[36,8,128]{2,1,0:T(8,128)S(1)} %get-tuple-element.79), channel_id=1, source_target_pairs={{1,2},{3,4},{5,6},{2,1},{4,3},{6,5},{0,0},{7,7},{9,10},{11,12},{13... | collective-permute-start | bytes 442376 | tf_op jit(solution)/shard_map/ppermute | solution.py:397
  34.8 2.3 %collective-permute-start.12 = (f32[27,8,128]{2,1,0:T(8,128)S(1)}, f32[27,8,128]{2,1,0:T(8,128)S(1)}, u32[]{:S(2)}, u32[]{:S(2)}) collective-permute-start(f32[27,8,128]{2,1,0:T(8,128)S(1)} %get-tuple-element.77), channel_id=1, source_target_pairs={{0,8},{16,24},{8,0},{24,16},{1,9},{17,25},{9,1},{25,17},{2,10},{18... | collective-permute-start | bytes 331784 | tf_op jit(solution)/shard_map/ppermute | solution.py:397

commit v12 on v11

--- a/solution.py
+++ b/solution.py
@@ -521,13 +521,12 @@
 
     (most,) = call(extremes_kernel, [wind], [shape(longest + 2)])
     other = spread(most, 1)
-    x_shapes = [shape(longest), shape(longest + 1)]
+    x_shapes = [shape(longest + 1), shape(longest)]
     x_out, x_last, t_out, t_last = call(opening_kernel, [values], x_shapes + [shape(middle)] * 2)
     far_shapes = [shape(short), shape(rim * planes), shape(middle)]
     for section in (1, 2, 3):
         opening = section == 1
-        if not opening:
-            x_near = trade(x_out, "gx", 0)
+        x_near = trade(x_out, "gx", 0)
         t_near = trade(t_out, "head", 0)
         t_far = trade(t_last, "head", 1, True)
         x_far = trade(x_last, "gx", 1)
@@ -536,12 +535,15 @@
         if opening:
             (most,) = call(meeting_kernel, [most, other], [shape()])
             other = spread(most, 2)
-            values, most = lax.optimization_barrier((values, most))
             ins = [values, wind, waves]
             spun, part, extra, flow = call(free, ins, [field] * 4, room, work=300)
-            x_out, part = lax.optimization_barrier((x_out, part))
-            x_near = trade(x_out, "gx", 0)
-            part, x_far = lax.optimization_barrier((part, x_far))
+            reach = 4
+            while reach < size:
+                most = jnp.maximum(most, other)
+                most, part = lax.optimization_barrier((most, part))
+                other = spread(most, reach)
+                reach *= 2
+            part, x_near, x_far = lax.optimization_barrier((part, x_near, x_far))
         else:
             if section == 3:
                 values, x_near = lax.optimization_barrier((values, x_near))
@@ -550,12 +552,6 @@
                 part, x_near = lax.optimization_barrier((part, x_near))
         (part,) = call(turning, [values, spun, part, t_near, t_far], [field], work=1000)
         if opening:
-            reach = 4
-            while reach < size:
-                most = jnp.maximum(most, other)
-                most, part = lax.optimization_barrier((most, part))
-                other = spread(most, reach)
-                reach *= 2
             ins = [values, part, x_near, x_far, wind, waves]
             first = functools.partial(first_kernel, speed_step)
             part, gap = call(first, ins, [field] * 2, [rows])

time: 42.3 us -> 41.2 us (0.974)
  waiting for transfers between devices: 7.14 us -> 5.92 us
    ppermute x3, waiting for transfers between devices: 4.87 us -> 1.58 us  [spread(): return lax.ppermute(most, 'gx', pairs)]
    ppermute x12, waiting for transfers between devices: 2.27 us -> 4.34 us  [trade(): return lax.ppermute(value, axis, pairs)]
    ppermute x3, starting transfers between devices: 3.04 us -> 4.17 us  [spread(): return lax.ppermute(most, 'gx', pairs)]
    ppermute x12, starting transfers between devices: 16.6 us -> 15.8 us  [trade(): return lax.ppermute(value, axis, pairs)]
  transfers between devices with their start and end apart: 15 -> 15, of which waited for: 4 -> 7; matrix products, arithmetic and copies ran while one was open for 0% -> 0% of each run, Pallas kernels for 28% -> 28%
where the time goes in v12:
time: 41.2 us; the launch traced here: 40.9 us
  starting transfers between devices  19.9 us (48%)
  Pallas kernels  13.1 us (32%)
  waiting for transfers between devices  5.92 us (14%)
  local copies, waits for them, and re-layouts  1.74 us (4%)
    ppermute x12, starting transfers between devices, trade(): return lax.ppermute(value, axis, pairs)  15.8 us
    pallas_call x15, Pallas kernels, call(): pl.pallas_call(kernel, out_shape=outs, in_specs=[vmem] * len(ins), out_sp...  13.1 us
    ppermute x12, waiting for transfers between devices, trade(): return lax.ppermute(value, axis, pairs)  4.34 us
    ppermute x3, starting transfers between devices, spread(): return lax.ppermute(most, 'gx', pairs)  4.17 us
    unnamed x14, local copies, waits for them, and re-layouts  1.74 us
    ppermute x3, waiting for transfers between devices, spread(): return lax.ppermute(most, 'gx', pairs)  1.58 us
  transfers between devices with their start and end apart: 15, of which 7 were waited for; matrix products, arithmetic and copies ran while one was open for 0% of the time, Pallas kernels for 28%

profile of v12, /device:TPU:8, one launch (start us, length us, event | category | flops | bytes accessed | tf_op | source)
XLA Modules:
  0.0 40.9 jit_solution(12270844762938049758)
XLA Ops:
  0.0 0.0 copy-start.3
  0.0 0.7 %copy-done.3 = f32[2,9,128]{2,0,1:T(2,128)S(1)} copy-done((f32[2,9,128]{2,0,1:T(2,128)S(1)}, f32[2,9,128]{2,0,1:T(2,128)}, u32[]{:S(2)}) %copy-start.3) | copy-done | bytes 9240
  0.7 1.6 %collective-permute-start = (f32[40,8,128]{2,1,0:T(8,128)S(1)}, f32[40,8,128]{2,1,0:T(8,128)S(1)}, u32[]{:S(2)}, u32[]{:S(2)}) collective-permute-start(f32[40,8,128]{2,1,0:T(8,128)S(1)} %shard_map.56.own_ref), channel_id=1, source_target_pairs={{0,1},{1,0},{2,3},{3,2},{4,5},{5,4},{6,7},{7,6},{8,9},{9,8},{10,11... | collective-permute-start | bytes 491528 | tf_op jit(solution)/shard_map/ppermute | solution.py:520
  2.3 0.0 copy-start
  2.3 1.0 %copy-done = f32[9,12,8,128]{3,2,1,0:T(8,128)S(1)} copy-done((f32[9,12,8,128]{3,2,1,0:T(8,128)S(1)}, f32[9,12,8,128]{3,2,1,0:T(8,128)}, u32[]{:S(2)}) %copy-start) | copy-done | bytes 442392
  3.3 0.0 copy-start.1
  3.3 0.6 %collective-permute-start.2 = (f32[39,8,128]{2,1,0:T(8,128)S(1)}, f32[39,8,128]{2,1,0:T(8,128)S(1)}, u32[]{:S(2)}, u32[]{:S(2)}) collective-permute-start(f32[39,8,128]{2,1,0:T(8,128)S(1)} %get-tuple-element.43), channel_id=1, source_target_pairs={{0,1},{2,3},{4,5},{6,7},{1,0},{3,2},{5,4},{7,6},{8,9},{10,11},{12,... | collective-permute-start | bytes 479240 | tf_op jit(solution)/shard_map/ppermute | solution.py:397
  3.9 3.3 %collective-permute-start.3 = (f32[38,8,128]{2,1,0:T(8,128)S(1)}, f32[38,8,128]{2,1,0:T(8,128)S(1)}, u32[]{:S(2)}, u32[]{:S(2)}) collective-permute-start(f32[38,8,128]{2,1,0:T(8,128)S(1)} %get-tuple-element.44), channel_id=1, source_target_pairs={{1,2},{3,4},{5,6},{2,1},{4,3},{6,5},{0,0},{7,7},{9,10},{11,12},{13... | collective-permute-start | bytes 466952 | tf_op jit(solution)/shard_map/ppermute | solution.py:397
  7.2 0.1 collective-permute-start.4
  7.3 0.0 copy-start.2
  7.3 0.0 copy-start.4
  7.3 1.6 %collective-permute-start.5 = (f32[37,8,128]{2,1,0:T(8,128)S(1)}, f32[37,8,128]{2,1,0:T(8,128)S(1)}, u32[]{:S(2)}, u32[]{:S(2)}) collective-permute-start(f32[37,8,128]{2,1,0:T(8,128)S(1)} %get-tuple-element.47), channel_id=1, source_target_pairs={{8,16},{24,0},{16,8},{0,24},{9,17},{25,1},{17,9},{1,25},{10,18},{2... | collective-permute-start | bytes 454664 | tf_op jit(solution)/shard_map/ppermute | solution.py:397
  8.9 0.0 collective-permute-done.other_ref
  8.9 0.0 collective-permute-start.1
  8.9 0.0 copy-done.1
  8.9 0.0 copy-done.2
  9.0 0.0 copy-done.4
  9.0 2.1 %shard_map.55 = (f32[9,12,8,128]{3,2,1,0:T(8,128)S(1)}, f32[9,12,8,128]{3,2,1,0:T(8,128)S(1)}, f32[9,12,8,128]{3,2,1,0:T(8,128)S(1)}, f32[9,12,8,128]{3,2,1,0:T(8,128)S(1)}) custom-call(f32[9,12,8,128]{3,2,1,0:T(8,128)S(1)} %copy-done.1, f32[9,2,128]{2,1,0:T(2,128)S(1)} %bitcast.2, f32[2,48,128]{2,1,0:T(8,128)S(1)} %copy-done.2), custom_call_target="tpu_custom_call" | custom-call | flops 33177600 | bytes 33177600 | tf_op jit(solution)/shard_map/pallas_call | solution.py:492
  11.1 1.4 %collective-permute-done.1 = f32[8,128]{1,0:T(8,128)S(1)} collective-permute-done((f32[8,128]{1,0:T(8,128)S(1)}, f32[8,128]{1,0:T(8,128)S(1)}, u32[]{:S(2)}, u32[]{:S(2)}) %collective-permute-start.1) | collective-permute-done | bytes 4128 | tf_op jit(solution)/shard_map/ppermute | solution.py:520
  12.5 0.0 collective-permute-done.3.far_ref
  12.5 0.9 %collective-permute-done.2.near_ref = f32[39,8,128]{2,1,0:T(8,128)S(1)} collective-permute-done((f32[39,8,128]{2,1,0:T(8,128)S(1)}, f32[39,8,128]{2,1,0:T(8,128)S(1)}, u32[]{:S(2)}, u32[]{:S(2)}) %collective-permute-start.2) | collective-permute-done | bytes 159776 | tf_op jit(solution)/shard_map/ppermute | solution.py:397
  13.5 2.6 %collective-permute-start.6 = (f32[8,128]{1,0:T(8,128)S(1)}, f32[8,128]{1,0:T(8,128)S(1)}, u32[]{:S(2)}, u32[]{:S(2)}) collective-permute-start(f32[8,128]{1,0:T(8,128)S(1)} %max.3.most_ref), channel_id=1, source_target_pairs={{0,4},{1,5},{2,6},{3,7},{4,0},{5,1},{6,2},{7,3},{8,12},{9,13},{10,... | collective-permute-start | bytes 12296 | tf_op jit(solution)/shard_map/ppermute | solution.py:520
  16.1 0.0 collective-permute-done.4.near_ref
  16.1 0.0 collective-permute-done.5.far_ref
  16.1 0.8 %shard_map.59.part_ref = f32[9,12,8,128]{3,2,1,0:T(8,128)S(1)} custom-call(f32[9,12,8,128]{3,2,1,0:T(8,128)S(1)} %copy-done.1, f32[9,12,8,128]{3,2,1,0:T(8,128)S(1)} %get-tuple-element.40.speed_ref, f32[9,12,8,128]{3,2,1,0:T(8,128)S(1)} %get-tuple-element.45.part_ref, f32[37,8,128]{2,1,0:T(8,128)S(1)} %collective-permute-done.4.near_ref, ...), custom_call_target="tpu_custom_call" | custom-call | flops 110592000 | bytes 110592000 | tf_op jit(solution)/shard_map/pallas_call | solution.py:492
  16.9 0.0 copy-start.5
  16.9 0.0 copy-start.6
  16.9 0.9 %shard_map.60 = (f32[9,12,8,128]{3,2,1,0:T(8,128)S(1)}, f32[9,12,8,128]{3,2,1,0:T(8,128)S(1)}) custom-call(f32[9,12,8,128]{3,2,1,0:T(8,128)S(1)} %copy-done.1, f32[9,12,8,128]{3,2,1,0:T(8,128)S(1)} %shard_map.59.part_ref, f32[39,8,128]{2,1,0:T(8,128)S(1)} %collective-permute-done.2.near_ref, f32[38,8,128]{2,1,0:T(8,128)S(1)} %collective-permute-done.3.far_ref, ...), custom_call_target="tpu_custom_call" | custom-call | tf_op jit(solution)/shard_map/pallas_call | solution.py:492
  17.8 0.1 collective-permute-done.6.other_ref
  18.0 0.0 copy-done.5
  18.0 0.0 copy-done.6
  18.0 0.4 shard_map.61
  18.4 1.6 %collective-permute-start.7 = (f32[38,8,128]{2,1,0:T(8,128)S(1)}, f32[38,8,128]{2,1,0:T(8,128)S(1)}, u32[]{:S(2)}, u32[]{:S(2)}) collective-permute-start(f32[38,8,128]{2,1,0:T(8,128)S(1)} %get-tuple-element.59), channel_id=1, source_target_pairs={{0,1},{2,3},{4,5},{6,7},{1,0},{3,2},{5,4},{7,6},{8,9},{10,11},{12,... | collective-permute-start | bytes 466952 | tf_op jit(solution)/shard_map/ppermute | solution.py:397
  20.0 0.0 collective-permute-start.9
  20.0 2.2 %collective-permute-start.10 = (f32[36,8,128]{2,1,0:T(8,128)S(1)}, f32[36,8,128]{2,1,0:T(8,128)S(1)}, u32[]{:S(2)}, u32[]{:S(2)}) collective-permute-start(f32[36,8,128]{2,1,0:T(8,128)S(1)} %get-tuple-element.63), channel_id=1, source_target_pairs={{1,2},{3,4},{5,6},{2,1},{4,3},{6,5},{0,0},{7,7},{9,10},{11,12},{13... | collective-permute-start | bytes 442376 | tf_op jit(solution)/shard_map/ppermute | solution.py:397
  22.2 1.4 %collective-permute-start.8 = (f32[27,8,128]{2,1,0:T(8,128)S(1)}, f32[27,8,128]{2,1,0:T(8,128)S(1)}, u32[]{:S(2)}, u32[]{:S(2)}) collective-permute-start(f32[27,8,128]{2,1,0:T(8,128)S(1)} %get-tuple-element.61), channel_id=1, source_target_pairs={{0,8},{16,24},{8,0},{24,16},{1,9},{17,25},{9,1},{25,17},{2,10},{18... | collective-permute-start | bytes 331784 | tf_op jit(solution)/shard_map/ppermute | solution.py:397
  23.5 2.1 %shard_map.62 = (f32[9,12,8,128]{3,2,1,0:T(8,128)S(1)}, f32[9,12,8,128]{3,2,1,0:T(8,128)S(1)}) custom-call(f32[9,12,8,128]{3,2,1,0:T(8,128)S(1)} %get-tuple-element.54.s_ref, f32[9,12,8,128]{3,2,1,0:T(8,128)S(1)} %get-tuple-element.55.rest_0_, f32[8,128]{1,0:T(8,128)S(1)} %get-tuple-element.56.rest_1_.pk_ref), custom_call_target="tpu_custom_call" | custom-call | tf_op jit(solution)/shard_map/pallas_call | solution.py:492
  25.6 0.0 collective-permute-done.7.ghosts_ref
  25.6 0.0 collective-permute-done.8.near_ref
  25.7 0.5 %collective-permute-done.9.far_ref = f32[37,8,128]{2,1,0:T(8,128)S(1)} collective-permute-done((f32[37,8,128]{2,1,0:T(8,128)S(1)}, f32[37,8,128]{2,1,0:T(8,128)S(1)}, u32[]{:S(2)}, u32[]{:S(2)}) %collective-permute-start.9) | collective-permute-done | bytes 151584 | tf_op jit(solution)/shard_map/ppermute | solution.py:397
  26.2 0.8 %shard_map.63.part_ref = f32[9,12,8,128]{3,2,1,0:T(8,128)S(1)} custom-call(f32[9,12,8,128]{3,2,1,0:T(8,128)S(1)} %get-tuple-element.54.s_ref, f32[9,12,8,128]{3,2,1,0:T(8,128)S(1)} %get-tuple-element.57.speed_ref, f32[9,12,8,128]{3,2,1,0:T(8,128)S(1)} %get-tuple-element.60.part_ref, f32[27,8,128]{2,1,0:T(8,128)S(1)} %collective-permute-done.8.near_ref, ...), custom_call_target="tpu_custom_call" | custom-call | flops 110592000 | bytes 110592000 | tf_op jit(solution)/shard_map/pallas_call | solution.py:492
  27.0 0.7 %shard_map.64 = (f32[9,12,8,128]{3,2,1,0:T(8,128)S(1)}, f32[38,8,128]{2,1,0:T(8,128)S(1)}) custom-call(f32[9,12,8,128]{3,2,1,0:T(8,128)S(1)} %copy-done.1, f32[9,12,8,128]{3,2,1,0:T(8,128)S(1)} %get-tuple-element.54.s_ref, f32[9,12,8,128]{3,2,1,0:T(8,128)S(1)} %shard_map.63.part_ref, f32[38,8,128]{2,1,0:T(8,128)S(1)} %collective-permute-done.7.ghosts_ref, ...), custom_call_target="tpu_custom_call" | custom-call | tf_op jit(solution)/shard_map/pallas_call | solution.py:492
  27.7 2.3 %collective-permute-start.11 = (f32[38,8,128]{2,1,0:T(8,128)S(1)}, f32[38,8,128]{2,1,0:T(8,128)S(1)}, u32[]{:S(2)}, u32[]{:S(2)}) collective-permute-start(f32[38,8,128]{2,1,0:T(8,128)S(1)} %get-tuple-element.67), channel_id=1, source_target_pairs={{0,1},{2,3},{4,5},{6,7},{1,0},{3,2},{5,4},{7,6},{8,9},{10,11},{12,... | collective-permute-start | bytes 466952 | tf_op jit(solution)/shard_map/ppermute | solution.py:397
  30.1 0.0 collective-permute-done.10.ghosts_ref
  30.1 0.4 %shard_map.65 = (f32[9,12,8,128]{3,2,1,0:T(8,128)S(1)}, f32[36,8,128]{2,1,0:T(8,128)S(1)}, f32[27,8,128]{2,1,0:T(8,128)S(1)}, f32[37,8,128]{2,1,0:T(8,128)S(1)}) custom-call(f32[9,12,8,128]{3,2,1,0:T(8,128)S(1)} %copy-done.1, f32[9,12,8,128]{3,2,1,0:T(8,128)S(1)} %get-tuple-element.54.s_ref, f32[9,12,8,128]{3,2,1,0:T(8,128)S(1)} %shard_map.63.part_ref, ...), custom_call_target="tpu_custom_call" | custom-call | tf_op jit(solution)/shard_map/pallas_call | solution.py:492
  30.5 0.1 collective-permute-start.13
  30.6 2.1 %collective-permute-start.14 = (f32[36,8,128]{2,1,0:T(8,128)S(1)}, f32[36,8,128]{2,1,0:T(8,128)S(1)}, u32[]{:S(2)}, u32[]{:S(2)}) collective-permute-start(f32[36,8,128]{2,1,0:T(8,128)S(1)} %get-tuple-element.73), channel_id=1, source_target_pairs={{1,2},{3,4},{5,6},{2,1},{4,3},{6,5},{0,0},{7,7},{9,10},{11,12},{13... | collective-permute-start | bytes 442376 | tf_op jit(solution)/shard_map/ppermute | solution.py:397
  32.7 0.5 %collective-permute-start.12 = (f32[27,8,128]{2,1,0:T(8,128)S(1)}, f32[27,8,128]{2,1,0:T(8,128)S(1)}, u32[]{:S(2)}, u32[]{:S(2)}) collective-permute-start(f32[27,8,128]{2,1,0:T(8,128)S(1)} %get-tuple-element.71), channel_id=1, source_target_pairs={{0,8},{16,24},{8,0},{24,16},{1,9},{17,25},{9,1},{25,17},{2,10},{18... | collective-permute-start | bytes 331784 | tf_op jit(solution)/shard_map/ppermute | solution.py:397
  33.2 1.1 %collective-permute-done.11.ghosts_ref = f32[38,8,128]{2,1,0:T(8,128)S(1)} collective-permute-done((f32[38,8,128]{2,1,0:T(8,128)S(1)}, f32[38,8,128]{2,1,0:T(8,128)S(1)}, u32[]{:S(2)}, u32[]{:S(2)}) %collective-permute-start.11) | collective-permute-done | bytes 155680 | tf_op jit(solution)/shard_map/ppermute | solution.py:397
  34.3 2.1 %shard_map.66 = (f32[9,12,8,128]{3,2,1,0:T(8,128)S(1)}, f32[9,12,8,128]{3,2,1,0:T(8,128)S(1)}) custom-call(f32[9,12,8,128]{3,2,1,0:T(8,128)S(1)} %get-tuple-element.68.s_ref, f32[9,12,8,128]{3,2,1,0:T(8,128)S(1)} %get-tuple-element.55.rest_0_, f32[8,128]{1,0:T(8,128)S(1)} %get-tuple-element.56.rest_1_.pk_ref), custom_call_target="tpu_custom_call" | custom-call | tf_op jit(solution)/shard_map/pallas_call | solution.py:492
  36.3 0.0 collective-permute-done.12.near_ref
  36.4 0.3 collective-permute-done.13.far_ref
  36.7 0.8 %shard_map.67.part_ref = f32[9,12,8,128]{3,2,1,0:T(8,128)S(1)} custom-call(f32[9,12,8,128]{3,2,1,0:T(8,128)S(1)} %get-tuple-element.68.s_ref, f32[9,12,8,128]{3,2,1,0:T(8,128)S(1)} %get-tuple-element.69.speed_ref, f32[9,12,8,128]{3,2,1,0:T(8,128)S(1)} %get-tuple-element.70.part_ref, f32[27,8,128]{2,1,0:T(8,128)S(1)} %collective-permute-done.12.near_ref, ...), custom_call_target="tpu_custom_call" | custom-call | flops 110592000 | bytes 110592000 | tf_op jit(solution)/shard_map/pallas_call | solution.py:492
  37.5 0.7 %shard_map.68.refs_0_ = f32[9,12,8,128]{3,2,1,0:T(8,128)S(1)} custom-call(f32[9,12,8,128]{3,2,1,0:T(8,128)S(1)} %copy-done.1, f32[9,12,8,128]{3,2,1,0:T(8,128)S(1)} %get-tuple-element.68.s_ref, f32[9,12,8,128]{3,2,1,0:T(8,128)S(1)} %shard_map.67.part_ref, f32[38,8,128]{2,1,0:T(8,128)S(1)} %collective-permute-done.11.ghosts_ref, f32[9,2,128]{2,1,0:T(2,128)S(1)} %bitcast.6, ...), custom_call_target="tpu_custom_call" | custom-call | tf_op jit(solution)/shard_map/pallas_call | solution.py:492
  38.2 1.5 %collective-permute-done.14.ghosts_ref = f32[36,8,128]{2,1,0:T(8,128)S(1)} collective-permute-done((f32[36,8,128]{2,1,0:T(8,128)S(1)}, f32[36,8,128]{2,1,0:T(8,128)S(1)}, u32[]{:S(2)}, u32[]{:S(2)}) %collective-permute-start.14) | collective-permute-done | bytes 147488 | tf_op jit(solution)/shard_map/ppermute | solution.py:397
  39.8 1.1 %shard_map.69 = f32[9,12,8,128]{3,2,1,0:T(8,128)} custom-call(f32[9,12,8,128]{3,2,1,0:T(8,128)S(1)} %copy-done.1, f32[9,12,8,128]{3,2,1,0:T(8,128)S(1)} %get-tuple-element.68.s_ref, f32[9,12,8,128]{3,2,1,0:T(8,128)S(1)} %shard_map.67.part_ref, f32[36,8,128]{2,1,0:T(8,128)S(1)} %collective-permute-done.14.ghosts_ref, f32[9,2,128]{2,1,0:T(2,128)S(1)} %bitcast.7, ...), custom_call_target="tpu_custom_call" | custom-call | tf_op jit(solution)/shard_map/pallas_call | solution.py:492
  (4 shorter events, 0.1 us)
Async XLA Ops:
  0.0 0.7 %copy-start.3 = (f32[2,9,128]{2,0,1:T(2,128)S(1)}, f32[2,9,128]{2,0,1:T(2,128)}, u32[]{:S(2)}) copy-start(f32[2,9,128]{2,0,1:T(2,128)} %param.6) | copy-start | bytes 27652
  0.7 8.2 %collective-permute-start = (f32[40,8,128]{2,1,0:T(8,128)S(1)}, f32[40,8,128]{2,1,0:T(8,128)S(1)}, u32[]{:S(2)}, u32[]{:S(2)}) collective-permute-start(f32[40,8,128]{2,1,0:T(8,128)S(1)} %shard_map.56.own_ref), channel_id=1, source_target_pairs={{0,1},{1,0},{2,3},{3,2},{4,5},{5,4},{6,7},{7,6},{8,9},{9,8},{10,11... | collective-permute-start | bytes 491528 | tf_op jit(solution)/shard_map/ppermute | solution.py:520
  2.3 1.0 %copy-start = (f32[9,12,8,128]{3,2,1,0:T(8,128)S(1)}, f32[9,12,8,128]{3,2,1,0:T(8,128)}, u32[]{:S(2)}) copy-start(f32[9,12,8,128]{3,2,1,0:T(8,128)} %base_ref.7) | copy-start | bytes 1327108
  3.3 5.6 %copy-start.1 = (f32[9,12,8,128]{3,2,1,0:T(8,128)S(1)}, f32[9,12,8,128]{3,2,1,0:T(8,128)}, u32[]{:S(2)}) copy-start(f32[9,12,8,128]{3,2,1,0:T(8,128)} %base_ref.7) | copy-start | bytes 1327108
  3.3 10.1 %collective-permute-start.2 = (f32[39,8,128]{2,1,0:T(8,128)S(1)}, f32[39,8,128]{2,1,0:T(8,128)S(1)}, u32[]{:S(2)}, u32[]{:S(2)}) collective-permute-start(f32[39,8,128]{2,1,0:T(8,128)S(1)} %get-tuple-element.43), channel_id=1, source_target_pairs={{0,1},{2,3},{4,5},{6,7},{1,0},{3,2},{5,4},{7,6},{8,9},{10,11},{12,... | collective-permute-start | bytes 479240 | tf_op jit(solution)/shard_map/ppermute | solution.py:397
  3.9 8.6 %collective-permute-start.3 = (f32[38,8,128]{2,1,0:T(8,128)S(1)}, f32[38,8,128]{2,1,0:T(8,128)S(1)}, u32[]{:S(2)}, u32[]{:S(2)}) collective-permute-start(f32[38,8,128]{2,1,0:T(8,128)S(1)} %get-tuple-element.44), channel_id=1, source_target_pairs={{1,2},{3,4},{5,6},{2,1},{4,3},{6,5},{0,0},{7,7},{9,10},{11,12},{13... | collective-permute-start | bytes 466952 | tf_op jit(solution)/shard_map/ppermute | solution.py:397
  7.2 8.8 %collective-permute-start.4 = (f32[37,8,128]{2,1,0:T(8,128)S(1)}, f32[37,8,128]{2,1,0:T(8,128)S(1)}, u32[]{:S(2)}, u32[]{:S(2)}) collective-permute-start(f32[37,8,128]{2,1,0:T(8,128)S(1)} %get-tuple-element.46), channel_id=1, source_target_pairs={{0,8},{16,24},{8,0},{24,16},{1,9},{17,25},{9,1},{25,17},{2,10},{18... | collective-permute-start | bytes 454664 | tf_op jit(solution)/shard_map/ppermute | solution.py:397
  7.3 1.6 %copy-start.2 = (f32[2,48,128]{2,1,0:T(8,128)S(1)}, f32[2,48,128]{2,1,0:T(8,128)}, u32[]{:S(2)}) copy-start(f32[2,48,128]{2,1,0:T(8,128)} %constant.2.clone.rest_1_.waves_ref) | copy-start | bytes 147460
  7.3 1.6 %copy-start.4 = (f32[2,9,128]{2,0,1:T(2,128)S(1)}, f32[2,9,128]{2,0,1:T(2,128)}, u32[]{:S(2)}) copy-start(f32[2,9,128]{2,0,1:T(2,128)} %param.6) | copy-start | bytes 27652
  7.3 8.7 %collective-permute-start.5 = (f32[37,8,128]{2,1,0:T(8,128)S(1)}, f32[37,8,128]{2,1,0:T(8,128)S(1)}, u32[]{:S(2)}, u32[]{:S(2)}) collective-permute-start(f32[37,8,128]{2,1,0:T(8,128)S(1)} %get-tuple-element.47), channel_id=1, source_target_pairs={{8,16},{24,0},{16,8},{0,24},{9,17},{25,1},{17,9},{1,25},{10,18},{2... | collective-permute-start | bytes 454664 | tf_op jit(solution)/shard_map/ppermute | solution.py:397
  8.9 3.6 %collective-permute-start.1 = (f32[8,128]{1,0:T(8,128)S(1)}, f32[8,128]{1,0:T(8,128)S(1)}, u32[]{:S(2)}, u32[]{:S(2)}) collective-permute-start(f32[8,128]{1,0:T(8,128)S(1)} %shard_map.57), channel_id=1, source_target_pairs={{0,2},{1,3},{2,0},{3,1},{4,6},{5,7},{6,4},{7,5},{8,10},{9,11},{10,... | collective-permute-start | bytes 12296 | tf_op jit(solution)/shard_map/ppermute | solution.py:520
  13.5 4.5 %collective-permute-start.6 = (f32[8,128]{1,0:T(8,128)S(1)}, f32[8,128]{1,0:T(8,128)S(1)}, u32[]{:S(2)}, u32[]{:S(2)}) collective-permute-start(f32[8,128]{1,0:T(8,128)S(1)} %max.3.most_ref), channel_id=1, source_target_pairs={{0,4},{1,5},{2,6},{3,7},{4,0},{5,1},{6,2},{7,3},{8,12},{9,13},{10,... | collective-permute-start | bytes 12296 | tf_op jit(solution)/shard_map/ppermute | solution.py:520
  16.9 1.1 %copy-start.5 = (s32[9,128]{1,0:T(8,128)S(1)}, s32[9,128]{1,0:T(8,128)}, u32[]{:S(2)}) copy-start(s32[9,128]{1,0:T(8,128)} %mask_ref.9) | copy-start | bytes 13828
  16.9 1.1 %copy-start.6 = (f32[9,128]{1,0:T(8,128)S(1)}, f32[9,128]{1,0:T(8,128)}, u32[]{:S(2)}) copy-start(f32[9,128]{1,0:T(8,128)} %depth_ref.9) | copy-start | bytes 13828
  18.4 7.3 %collective-permute-start.7 = (f32[38,8,128]{2,1,0:T(8,128)S(1)}, f32[38,8,128]{2,1,0:T(8,128)S(1)}, u32[]{:S(2)}, u32[]{:S(2)}) collective-permute-start(f32[38,8,128]{2,1,0:T(8,128)S(1)} %get-tuple-element.59), channel_id=1, source_target_pairs={{0,1},{2,3},{4,5},{6,7},{1,0},{3,2},{5,4},{7,6},{8,9},{10,11},{12,... | collective-permute-start | bytes 466952 | tf_op jit(solution)/shard_map/ppermute | solution.py:397
  20.0 6.2 %collective-permute-start.9 = (f32[37,8,128]{2,1,0:T(8,128)S(1)}, f32[37,8,128]{2,1,0:T(8,128)S(1)}, u32[]{:S(2)}, u32[]{:S(2)}) collective-permute-start(f32[37,8,128]{2,1,0:T(8,128)S(1)} %get-tuple-element.62), channel_id=1, source_target_pairs={{8,16},{24,0},{16,8},{0,24},{9,17},{25,1},{17,9},{1,25},{10,18},{2... | collective-permute-start | bytes 454664 | tf_op jit(solution)/shard_map/ppermute | solution.py:397
  20.0 10.1 %collective-permute-start.10 = (f32[36,8,128]{2,1,0:T(8,128)S(1)}, f32[36,8,128]{2,1,0:T(8,128)S(1)}, u32[]{:S(2)}, u32[]{:S(2)}) collective-permute-start(f32[36,8,128]{2,1,0:T(8,128)S(1)} %get-tuple-element.63), channel_id=1, source_target_pairs={{1,2},{3,4},{5,6},{2,1},{4,3},{6,5},{0,0},{7,7},{9,10},{11,12},{13... | collective-permute-start | bytes 442376 | tf_op jit(solution)/shard_map/ppermute | solution.py:397
  22.2 3.5 %collective-permute-start.8 = (f32[27,8,128]{2,1,0:T(8,128)S(1)}, f32[27,8,128]{2,1,0:T(8,128)S(1)}, u32[]{:S(2)}, u32[]{:S(2)}) collective-permute-start(f32[27,8,128]{2,1,0:T(8,128)S(1)} %get-tuple-element.61), channel_id=1, source_target_pairs={{0,8},{16,24},{8,0},{24,16},{1,9},{17,25},{9,1},{25,17},{2,10},{18... | collective-permute-start | bytes 331784 | tf_op jit(solution)/shard_map/ppermute | solution.py:397
  27.7 6.5 %collective-permute-start.11 = (f32[38,8,128]{2,1,0:T(8,128)S(1)}, f32[38,8,128]{2,1,0:T(8,128)S(1)}, u32[]{:S(2)}, u32[]{:S(2)}) collective-permute-start(f32[38,8,128]{2,1,0:T(8,128)S(1)} %get-tuple-element.67), channel_id=1, source_target_pairs={{0,1},{2,3},{4,5},{6,7},{1,0},{3,2},{5,4},{7,6},{8,9},{10,11},{12,... | collective-permute-start | bytes 466952 | tf_op jit(solution)/shard_map/ppermute | solution.py:397
  30.5 6.2 %collective-permute-start.13 = (f32[37,8,128]{2,1,0:T(8,128)S(1)}, f32[37,8,128]{2,1,0:T(8,128)S(1)}, u32[]{:S(2)}, u32[]{:S(2)}) collective-permute-start(f32[37,8,128]{2,1,0:T(8,128)S(1)} %get-tuple-element.72), channel_id=1, source_target_pairs={{8,16},{24,0},{16,8},{0,24},{9,17},{25,1},{17,9},{1,25},{10,18},{2... | collective-permute-start | bytes 454664 | tf_op jit(solution)/shard_map/ppermute | solution.py:397
  30.6 9.2 %collective-permute-start.14 = (f32[36,8,128]{2,1,0:T(8,128)S(1)}, f32[36,8,128]{2,1,0:T(8,128)S(1)}, u32[]{:S(2)}, u32[]{:S(2)}) collective-permute-start(f32[36,8,128]{2,1,0:T(8,128)S(1)} %get-tuple-element.73), channel_id=1, source_target_pairs={{1,2},{3,4},{5,6},{2,1},{4,3},{6,5},{0,0},{7,7},{9,10},{11,12},{13... | collective-permute-start | bytes 442376 | tf_op jit(solution)/shard_map/ppermute | solution.py:397
  32.7 3.6 %collective-permute-start.12 = (f32[27,8,128]{2,1,0:T(8,128)S(1)}, f32[27,8,128]{2,1,0:T(8,128)S(1)}, u32[]{:S(2)}, u32[]{:S(2)}) collective-permute-start(f32[27,8,128]{2,1,0:T(8,128)S(1)} %get-tuple-element.71), channel_id=1, source_target_pairs={{0,8},{16,24},{8,0},{24,16},{1,9},{17,25},{9,1},{25,17},{2,10},{18... | collective-permute-start | bytes 331784 | tf_op jit(solution)/shard_map/ppermute | solution.py:397

commit v13 on v12

--- a/solution.py
+++ b/solution.py
@@ -106,17 +106,13 @@
 
 
 def extremes_kernel(wind_ref, most_ref):
-    put_extremes(wind_ref, most_ref.at[0])
+    put_extremes(wind_ref, most_ref.at[0:8])
 
 
 def opening_kernel(level_ref, x_near, x_far, t_near, t_far):
     cut_near(level_ref, x_near)
     cut_far(level_ref, x_far)
     cut_headings(level_ref, t_near, t_far)
-
-
-def meeting_kernel(own_ref, other_ref, most_ref):
-    most_ref[...] = jnp.maximum(own_ref[0], other_ref[0])
 
 
 def flows_into(flow_ref, speed_step, wind_ref, waves_ref):
@@ -330,11 +326,11 @@
 
 def closing_kernel(
     bounds, heading_step, speed_step, s_ref, part_ref, gap_x_ref, gap_y_ref, mask_ref, depth_ref,
-    most_ref, other_ref, out_ref, x_near, x_far, t_near, t_far, pk_ref, target_ref
+    most_ref, out_ref, x_near, x_far, t_near, t_far, pk_ref, target_ref
 ):
     planes, headings = s_ref.shape[:2]
     tile = s_ref.shape[2:]
-    most = jnp.maximum(most_ref[...], other_ref[...])
+    most = functools.reduce(jnp.maximum, [most_ref[g, 0:8, :] for g in range(most_ref.shape[0])])
     peaks_into(pk_ref, most, bounds, heading_step, speed_step)
     splat_targets(mask_ref, depth_ref, target_ref)
     peak_x = splat(pk_ref[0:1, :] * gain, tile)
@@ -510,17 +506,9 @@
         pltpu.VMEM((groups, cross_count, lanes), jnp.float32),
     ]
     values, pk = level_set, None
-    size = lax.axis_size("gx")
-
-    def spread(most, reach):
-        if size & (size - 1):
-            pairs = [(i, (i + reach) % size) for i in range(size)]
-        else:
-            pairs = [(i, i ^ reach) for i in range(size)]
-        return lax.ppermute(most, "gx", pairs)
-
-    (most,) = call(extremes_kernel, [wind], [shape(longest + 2)])
-    other = spread(most, 1)
+    most_shape = jax.ShapeDtypeStruct((64, cross_count), jnp.float32)
+    (most,) = call(extremes_kernel, [wind], [most_shape])
+    most = lax.all_gather(most, "gx")
     x_shapes = [shape(longest + 1), shape(longest)]
     x_out, x_last, t_out, t_last = call(opening_kernel, [values], x_shapes + [shape(middle)] * 2)
     far_shapes = [shape(short), shape(rim * planes), shape(middle)]
@@ -533,16 +521,8 @@
         free = functools.partial(free_kernel, opening, speed_step)
         turning = functools.partial(heading_kernel, heading_step)
         if opening:
-            (most,) = call(meeting_kernel, [most, other], [shape()])
-            other = spread(most, 2)
             ins = [values, wind, waves]
             spun, part, extra, flow = call(free, ins, [field] * 4, room, work=300)
-            reach = 4
-            while reach < size:
-                most = jnp.maximum(most, other)
-                most, part = lax.optimization_barrier((most, part))
-                other = spread(most, reach)
-                reach *= 2
             part, x_near, x_far = lax.optimization_barrier((part, x_near, x_far))
         else:
             if section == 3:
@@ -556,7 +536,7 @@
             first = functools.partial(first_kernel, speed_step)
             part, gap = call(first, ins, [field] * 2, [rows])
             closing = functools.partial(closing_kernel, bounds, heading_step, speed_step)
-            ins = [values, part, gap, extra, target_mask, target_depth, most, other]
+            ins = [values, part, gap, extra, target_mask, target_depth, most]
             outs = [field, shape(longest), *far_shapes, shape()]
             values, x_out, x_last, t_out, t_last, pk = call(closing, ins, outs, [rows])
         else:

time: 41.2 us -> 63.8 us (1.55); the launches traced: 40.9 us -> 62.9 us
  blocking collectives: 0 us -> 28.4 us
  waiting for transfers between devices: 5.92 us -> 1.56 us
  starting transfers between devices: 19.9 us -> 17.7 us
    all_gather x0 -> x1, blocking collectives: none -> 28.4 us  [local(): most = lax.all_gather(most, 'gx')]
    ppermute x3 -> x0, starting transfers between devices: 4.17 us -> none  [spread(): return lax.ppermute(most, 'gx', pairs)]
    ppermute x12, waiting for transfers between devices: 4.34 us -> 1.56 us  [trade(): return lax.ppermute(value, axis, pairs)]
    ppermute x12, starting transfers between devices: 15.8 us -> 17.7 us  [trade(): return lax.ppermute(value, axis, pairs)]
    ppermute x3 -> x0, waiting for transfers between devices: 1.58 us -> none  [spread(): return lax.ppermute(most, 'gx', pairs)]
    pallas_call x15 -> x14, Pallas kernels: 13.1 us -> 13.3 us  [call(): pl.pallas_call(kernel, out_shape=outs, in_specs=[vmem] * len(ins), out_sp...]
  transfers between devices with their start and end apart: 15 -> 12, of which waited for: 7 -> 3; matrix products, arithmetic and copies ran while one was open for 0% -> 0% of each run, Pallas kernels for 28% -> 16%
where the time goes in v13:
time: 63.8 us; the launch traced here: 62.9 us
  blocking collectives  28.4 us (45%)
  starting transfers between devices  17.7 us (28%)
  Pallas kernels  13.3 us (21%)
  local copies, waits for them, and re-layouts  1.74 us (3%)
  waiting for transfers between devices  1.56 us (2%)
    all_gather x1, blocking collectives, local(): most = lax.all_gather(most, 'gx')  28.4 us
    ppermute x12, starting transfers between devices, trade(): return lax.ppermute(value, axis, pairs)  17.7 us
    pallas_call x14, Pallas kernels, call(): pl.pallas_call(kernel, out_shape=outs, in_specs=[vmem] * len(ins), out_sp...  13.3 us
    unnamed x14, local copies, waits for them, and re-layouts  1.74 us
    ppermute x12, waiting for transfers between devices, trade(): return lax.ppermute(value, axis, pairs)  1.56 us
  transfers between devices with their start and end apart: 12, of which 3 were waited for; matrix products, arithmetic and copies ran while one was open for 0% of the time, Pallas kernels for 16%

profile of v13, /device:TPU:8, one launch (start us, length us, event | category | flops | bytes accessed | tf_op | source)
XLA Modules:
  0.0 62.9 jit_solution(1584207589427393574)
XLA Ops:
  0.0 0.0 copy-start
  0.0 1.0 %copy-done = f32[9,12,8,128]{3,2,1,0:T(8,128)S(1)} copy-done((f32[9,12,8,128]{3,2,1,0:T(8,128)S(1)}, f32[9,12,8,128]{3,2,1,0:T(8,128)}, u32[]{:S(2)}) %copy-start) | copy-done | bytes 442392
  1.0 0.0 copy-start.1
  1.1 0.0 copy-start.2
  1.1 1.6 %collective-permute-start = (f32[39,8,128]{2,1,0:T(8,128)S(1)}, f32[39,8,128]{2,1,0:T(8,128)S(1)}, u32[]{:S(2)}, u32[]{:S(2)}) collective-permute-start(f32[39,8,128]{2,1,0:T(8,128)S(1)} %get-tuple-element.40), channel_id=1, source_target_pairs={{0,1},{2,3},{4,5},{6,7},{1,0},{3,2},{5,4},{7,6},{8,9},{10,11},{12,... | collective-permute-start | bytes 479240 | tf_op jit(solution)/shard_map/ppermute | solution.py:393
  2.7 1.9 %collective-permute-start.1 = (f32[38,8,128]{2,1,0:T(8,128)S(1)}, f32[38,8,128]{2,1,0:T(8,128)S(1)}, u32[]{:S(2)}, u32[]{:S(2)}) collective-permute-start(f32[38,8,128]{2,1,0:T(8,128)S(1)} %get-tuple-element.41), channel_id=1, source_target_pairs={{1,2},{3,4},{5,6},{2,1},{4,3},{6,5},{0,0},{7,7},{9,10},{11,12},{13... | collective-permute-start | bytes 466952 | tf_op jit(solution)/shard_map/ppermute | solution.py:393
  4.6 0.1 collective-permute-start.2
  4.7 2.0 %collective-permute-start.3 = (f32[37,8,128]{2,1,0:T(8,128)S(1)}, f32[37,8,128]{2,1,0:T(8,128)S(1)}, u32[]{:S(2)}, u32[]{:S(2)}) collective-permute-start(f32[37,8,128]{2,1,0:T(8,128)S(1)} %get-tuple-element.44), channel_id=1, source_target_pairs={{8,16},{24,0},{16,8},{0,24},{9,17},{25,1},{17,9},{1,25},{10,18},{2... | collective-permute-start | bytes 454664 | tf_op jit(solution)/shard_map/ppermute | solution.py:393
  6.6 0.0 copy-start.3
  6.6 0.7 %copy-done.3 = f32[2,9,128]{2,0,1:T(2,128)S(1)} copy-done((f32[2,9,128]{2,0,1:T(2,128)S(1)}, f32[2,9,128]{2,0,1:T(2,128)}, u32[]{:S(2)}) %copy-start.3) | copy-done | bytes 9240
  7.3 0.0 copy-done.1
  7.4 0.0 copy-done.2
  7.4 2.1 %shard_map.55 = (f32[9,12,8,128]{3,2,1,0:T(8,128)S(1)}, f32[9,12,8,128]{3,2,1,0:T(8,128)S(1)}, f32[9,12,8,128]{3,2,1,0:T(8,128)S(1)}, f32[9,12,8,128]{3,2,1,0:T(8,128)S(1)}) custom-call(f32[9,12,8,128]{3,2,1,0:T(8,128)S(1)} %copy-done.1, f32[9,2,128]{2,1,0:T(2,128)S(1)} %bitcast.4, f32[2,48,128]{2,1,0:T(8,128)S(1)} %copy-done.2), custom_call_target="tpu_custom_call" | custom-call | flops 33177600 | bytes 33177600 | tf_op jit(solution)/shard_map/pallas_call | solution.py:488
  9.5 28.4 %all-gather = f32[512,128]{1,0:T(8,128)S(1)} all-gather(f32[64,128]{1,0:T(8,128)S(1)} %shard_map.59), channel_id=2, replica_groups=mesh['head'=4,'gx'=8] {'gx'}, dimensions={0}, use_global_device_ids=true | all-gather | bytes 294912 | tf_op jit(solution)/shard_map/all_gather | solution.py:511
  37.9 0.0 collective-permute-done.1.far_ref
  37.9 0.0 collective-permute-done.near_ref
  37.9 0.0 collective-permute-done.2.near_ref
  37.9 0.0 collective-permute-done.3.far_ref
  37.9 0.0 copy-start.4
  37.9 0.9 %shard_map.57.part_ref = f32[9,12,8,128]{3,2,1,0:T(8,128)S(1)} custom-call(f32[9,12,8,128]{3,2,1,0:T(8,128)S(1)} %copy-done.1, f32[9,12,8,128]{3,2,1,0:T(8,128)S(1)} %get-tuple-element.38.speed_ref, f32[9,12,8,128]{3,2,1,0:T(8,128)S(1)} %get-tuple-element.42.part_ref, f32[37,8,128]{2,1,0:T(8,128)S(1)} %collective-permute-done.2.near_ref, ...), custom_call_target="tpu_custom_call" | custom-call | flops 110592000 | bytes 110592000 | tf_op jit(solution)/shard_map/pallas_call | solution.py:488
  38.8 0.0 copy-done.4
  38.8 0.0 copy-start.5
  38.8 0.0 copy-start.6
  38.8 0.9 %shard_map.58 = (f32[9,12,8,128]{3,2,1,0:T(8,128)S(1)}, f32[9,12,8,128]{3,2,1,0:T(8,128)S(1)}) custom-call(f32[9,12,8,128]{3,2,1,0:T(8,128)S(1)} %copy-done.1, f32[9,12,8,128]{3,2,1,0:T(8,128)S(1)} %shard_map.57.part_ref, f32[39,8,128]{2,1,0:T(8,128)S(1)} %collective-permute-done.near_ref, f32[38,8,128]{2,1,0:T(8,128)S(1)} %collective-permute-done.1.far_ref, ...), custom_call_target="tpu_custom_call" | custom-call | tf_op jit(solution)/shard_map/pallas_call | solution.py:488
  39.7 0.0 copy-done.5
  39.7 0.0 copy-done.6
  39.7 0.4 shard_map.60
  40.2 0.1 collective-permute-start.4
  40.2 0.1 collective-permute-start.6
  40.3 6.5 %collective-permute-start.7 = (f32[36,8,128]{2,1,0:T(8,128)S(1)}, f32[36,8,128]{2,1,0:T(8,128)S(1)}, u32[]{:S(2)}, u32[]{:S(2)}) collective-permute-start(f32[36,8,128]{2,1,0:T(8,128)S(1)} %get-tuple-element.59), channel_id=1, source_target_pairs={{1,2},{3,4},{5,6},{2,1},{4,3},{6,5},{0,0},{7,7},{9,10},{11,12},{13... | collective-permute-start | bytes 442376 | tf_op jit(solution)/shard_map/ppermute | solution.py:393
  46.9 0.4 collective-permute-start.5
  47.3 2.1 %shard_map.61 = (f32[9,12,8,128]{3,2,1,0:T(8,128)S(1)}, f32[9,12,8,128]{3,2,1,0:T(8,128)S(1)}) custom-call(f32[9,12,8,128]{3,2,1,0:T(8,128)S(1)} %get-tuple-element.50.s_ref, f32[9,12,8,128]{3,2,1,0:T(8,128)S(1)} %get-tuple-element.51.rest_0_, f32[8,128]{1,0:T(8,128)S(1)} %get-tuple-element.52.rest_1_.pk_ref), custom_call_target="tpu_custom_call" | custom-call | tf_op jit(solution)/shard_map/pallas_call | solution.py:488
  49.4 0.0 collective-permute-done.4.ghosts_ref
  49.4 0.0 collective-permute-done.5.near_ref
  49.4 0.0 collective-permute-done.6.far_ref
  49.4 0.9 %shard_map.62.part_ref = f32[9,12,8,128]{3,2,1,0:T(8,128)S(1)} custom-call(f32[9,12,8,128]{3,2,1,0:T(8,128)S(1)} %get-tuple-element.50.s_ref, f32[9,12,8,128]{3,2,1,0:T(8,128)S(1)} %get-tuple-element.53.speed_ref, f32[9,12,8,128]{3,2,1,0:T(8,128)S(1)} %get-tuple-element.56.part_ref, f32[27,8,128]{2,1,0:T(8,128)S(1)} %collective-permute-done.5.near_ref, ...), custom_call_target="tpu_custom_call" | custom-call | flops 110592000 | bytes 110592000 | tf_op jit(solution)/shard_map/pallas_call | solution.py:488
  50.3 0.7 %shard_map.63 = (f32[9,12,8,128]{3,2,1,0:T(8,128)S(1)}, f32[38,8,128]{2,1,0:T(8,128)S(1)}) custom-call(f32[9,12,8,128]{3,2,1,0:T(8,128)S(1)} %copy-done.1, f32[9,12,8,128]{3,2,1,0:T(8,128)S(1)} %get-tuple-element.50.s_ref, f32[9,12,8,128]{3,2,1,0:T(8,128)S(1)} %shard_map.62.part_ref, f32[38,8,128]{2,1,0:T(8,128)S(1)} %collective-permute-done.4.ghosts_ref, ...), custom_call_target="tpu_custom_call" | custom-call | tf_op jit(solution)/shard_map/pallas_call | solution.py:488
  51.0 0.1 collective-permute-start.8
  51.1 0.4 collective-permute-done.7.ghosts_ref
  51.5 0.4 shard_map.64
  51.9 0.8 %collective-permute-start.10 = (f32[37,8,128]{2,1,0:T(8,128)S(1)}, f32[37,8,128]{2,1,0:T(8,128)S(1)}, u32[]{:S(2)}, u32[]{:S(2)}) collective-permute-start(f32[37,8,128]{2,1,0:T(8,128)S(1)} %get-tuple-element.68), channel_id=1, source_target_pairs={{8,16},{24,0},{16,8},{0,24},{9,17},{25,1},{17,9},{1,25},{10,18},{2... | collective-permute-start | bytes 454664 | tf_op jit(solution)/shard_map/ppermute | solution.py:393
  52.7 4.1 %collective-permute-start.11 = (f32[36,8,128]{2,1,0:T(8,128)S(1)}, f32[36,8,128]{2,1,0:T(8,128)S(1)}, u32[]{:S(2)}, u32[]{:S(2)}) collective-permute-start(f32[36,8,128]{2,1,0:T(8,128)S(1)} %get-tuple-element.69), channel_id=1, source_target_pairs={{1,2},{3,4},{5,6},{2,1},{4,3},{6,5},{0,0},{7,7},{9,10},{11,12},{13... | collective-permute-start | bytes 442376 | tf_op jit(solution)/shard_map/ppermute | solution.py:393
  56.8 0.1 collective-permute-start.9
  56.9 0.2 collective-permute-done.8.ghosts_ref
  57.1 2.1 %shard_map.65 = (f32[9,12,8,128]{3,2,1,0:T(8,128)S(1)}, f32[9,12,8,128]{3,2,1,0:T(8,128)S(1)}) custom-call(f32[9,12,8,128]{3,2,1,0:T(8,128)S(1)} %get-tuple-element.64.s_ref, f32[9,12,8,128]{3,2,1,0:T(8,128)S(1)} %get-tuple-element.51.rest_0_, f32[8,128]{1,0:T(8,128)S(1)} %get-tuple-element.52.rest_1_.pk_ref), custom_call_target="tpu_custom_call" | custom-call | tf_op jit(solution)/shard_map/pallas_call | solution.py:488
  59.2 0.0 collective-permute-done.9.near_ref
  59.2 0.0 collective-permute-done.10.far_ref
  59.3 0.9 %shard_map.66.part_ref = f32[9,12,8,128]{3,2,1,0:T(8,128)S(1)} custom-call(f32[9,12,8,128]{3,2,1,0:T(8,128)S(1)} %get-tuple-element.64.s_ref, f32[9,12,8,128]{3,2,1,0:T(8,128)S(1)} %get-tuple-element.65.speed_ref, f32[9,12,8,128]{3,2,1,0:T(8,128)S(1)} %get-tuple-element.66.part_ref, f32[27,8,128]{2,1,0:T(8,128)S(1)} %collective-permute-done.9.near_ref, ...), custom_call_target="tpu_custom_call" | custom-call | flops 110592000 | bytes 110592000 | tf_op jit(solution)/shard_map/pallas_call | solution.py:488
  60.1 0.7 %shard_map.67.refs_0_ = f32[9,12,8,128]{3,2,1,0:T(8,128)S(1)} custom-call(f32[9,12,8,128]{3,2,1,0:T(8,128)S(1)} %copy-done.1, f32[9,12,8,128]{3,2,1,0:T(8,128)S(1)} %get-tuple-element.64.s_ref, f32[9,12,8,128]{3,2,1,0:T(8,128)S(1)} %shard_map.66.part_ref, f32[38,8,128]{2,1,0:T(8,128)S(1)} %collective-permute-done.8.ghosts_ref, f32[9,2,128]{2,1,0:T(2,128)S(1)} %bitcast.8, ...), custom_call_target="tpu_custom_call" | custom-call | tf_op jit(solution)/shard_map/pallas_call | solution.py:488
  60.8 0.9 %collective-permute-done.11.ghosts_ref = f32[36,8,128]{2,1,0:T(8,128)S(1)} collective-permute-done((f32[36,8,128]{2,1,0:T(8,128)S(1)}, f32[36,8,128]{2,1,0:T(8,128)S(1)}, u32[]{:S(2)}, u32[]{:S(2)}) %collective-permute-start.11) | collective-permute-done | bytes 147488 | tf_op jit(solution)/shard_map/ppermute | solution.py:393
  61.7 1.1 %shard_map.68 = f32[9,12,8,128]{3,2,1,0:T(8,128)} custom-call(f32[9,12,8,128]{3,2,1,0:T(8,128)S(1)} %copy-done.1, f32[9,12,8,128]{3,2,1,0:T(8,128)S(1)} %get-tuple-element.64.s_ref, f32[9,12,8,128]{3,2,1,0:T(8,128)S(1)} %shard_map.66.part_ref, f32[36,8,128]{2,1,0:T(8,128)S(1)} %collective-permute-done.11.ghosts_ref, f32[9,2,128]{2,1,0:T(2,128)S(1)} %bitcast.9, ...), custom_call_target="tpu_custom_call" | custom-call | tf_op jit(solution)/shard_map/pallas_call | solution.py:488
  (2 shorter events, 0.0 us)
Async XLA Ops:
  0.0 1.0 %copy-start = (f32[9,12,8,128]{3,2,1,0:T(8,128)S(1)}, f32[9,12,8,128]{3,2,1,0:T(8,128)}, u32[]{:S(2)}) copy-start(f32[9,12,8,128]{3,2,1,0:T(8,128)} %base_ref.7) | copy-start | bytes 1327108
  1.0 6.3 %copy-start.1 = (f32[9,12,8,128]{3,2,1,0:T(8,128)S(1)}, f32[9,12,8,128]{3,2,1,0:T(8,128)}, u32[]{:S(2)}) copy-start(f32[9,12,8,128]{3,2,1,0:T(8,128)} %base_ref.7) | copy-start | bytes 1327108
  1.1 6.3 %copy-start.2 = (f32[2,48,128]{2,1,0:T(8,128)S(1)}, f32[2,48,128]{2,1,0:T(8,128)}, u32[]{:S(2)}) copy-start(f32[2,48,128]{2,1,0:T(8,128)} %constant.2.clone.rest_1_.waves_ref) | copy-start | bytes 147460
  1.1 36.8 %collective-permute-start = (f32[39,8,128]{2,1,0:T(8,128)S(1)}, f32[39,8,128]{2,1,0:T(8,128)S(1)}, u32[]{:S(2)}, u32[]{:S(2)}) collective-permute-start(f32[39,8,128]{2,1,0:T(8,128)S(1)} %get-tuple-element.40), channel_id=1, source_target_pairs={{0,1},{2,3},{4,5},{6,7},{1,0},{3,2},{5,4},{7,6},{8,9},{10,11},{12,... | collective-permute-start | bytes 479240 | tf_op jit(solution)/shard_map/ppermute | solution.py:393
  2.7 35.2 %collective-permute-start.1 = (f32[38,8,128]{2,1,0:T(8,128)S(1)}, f32[38,8,128]{2,1,0:T(8,128)S(1)}, u32[]{:S(2)}, u32[]{:S(2)}) collective-permute-start(f32[38,8,128]{2,1,0:T(8,128)S(1)} %get-tuple-element.41), channel_id=1, source_target_pairs={{1,2},{3,4},{5,6},{2,1},{4,3},{6,5},{0,0},{7,7},{9,10},{11,12},{13... | collective-permute-start | bytes 466952 | tf_op jit(solution)/shard_map/ppermute | solution.py:393
  4.6 33.3 %collective-permute-start.2 = (f32[37,8,128]{2,1,0:T(8,128)S(1)}, f32[37,8,128]{2,1,0:T(8,128)S(1)}, u32[]{:S(2)}, u32[]{:S(2)}) collective-permute-start(f32[37,8,128]{2,1,0:T(8,128)S(1)} %get-tuple-element.43), channel_id=1, source_target_pairs={{0,8},{16,24},{8,0},{24,16},{1,9},{17,25},{9,1},{25,17},{2,10},{18... | collective-permute-start | bytes 454664 | tf_op jit(solution)/shard_map/ppermute | solution.py:393
  4.7 33.2 %collective-permute-start.3 = (f32[37,8,128]{2,1,0:T(8,128)S(1)}, f32[37,8,128]{2,1,0:T(8,128)S(1)}, u32[]{:S(2)}, u32[]{:S(2)}) collective-permute-start(f32[37,8,128]{2,1,0:T(8,128)S(1)} %get-tuple-element.44), channel_id=1, source_target_pairs={{8,16},{24,0},{16,8},{0,24},{9,17},{25,1},{17,9},{1,25},{10,18},{2... | collective-permute-start | bytes 454664 | tf_op jit(solution)/shard_map/ppermute | solution.py:393
  6.6 0.7 %copy-start.3 = (f32[2,9,128]{2,0,1:T(2,128)S(1)}, f32[2,9,128]{2,0,1:T(2,128)}, u32[]{:S(2)}) copy-start(f32[2,9,128]{2,0,1:T(2,128)} %param.6) | copy-start | bytes 27652
  37.9 0.9 %copy-start.4 = (f32[2,9,128]{2,0,1:T(2,128)S(1)}, f32[2,9,128]{2,0,1:T(2,128)}, u32[]{:S(2)}) copy-start(f32[2,9,128]{2,0,1:T(2,128)} %param.6) | copy-start | bytes 27652
  38.8 0.9 %copy-start.5 = (s32[9,128]{1,0:T(8,128)S(1)}, s32[9,128]{1,0:T(8,128)}, u32[]{:S(2)}) copy-start(s32[9,128]{1,0:T(8,128)} %mask_ref.9) | copy-start | bytes 13828
  38.8 0.9 %copy-start.6 = (f32[9,128]{1,0:T(8,128)S(1)}, f32[9,128]{1,0:T(8,128)}, u32[]{:S(2)}) copy-start(f32[9,128]{1,0:T(8,128)} %depth_ref.9) | copy-start | bytes 13828
  40.2 9.2 %collective-permute-start.4 = (f32[38,8,128]{2,1,0:T(8,128)S(1)}, f32[38,8,128]{2,1,0:T(8,128)S(1)}, u32[]{:S(2)}, u32[]{:S(2)}) collective-permute-start(f32[38,8,128]{2,1,0:T(8,128)S(1)} %get-tuple-element.55), channel_id=1, source_target_pairs={{0,1},{2,3},{4,5},{6,7},{1,0},{3,2},{5,4},{7,6},{8,9},{10,11},{12,... | collective-permute-start | bytes 466952 | tf_op jit(solution)/shard_map/ppermute | solution.py:393
  40.2 9.2 %collective-permute-start.6 = (f32[37,8,128]{2,1,0:T(8,128)S(1)}, f32[37,8,128]{2,1,0:T(8,128)S(1)}, u32[]{:S(2)}, u32[]{:S(2)}) collective-permute-start(f32[37,8,128]{2,1,0:T(8,128)S(1)} %get-tuple-element.58), channel_id=1, source_target_pairs={{8,16},{24,0},{16,8},{0,24},{9,17},{25,1},{17,9},{1,25},{10,18},{2... | collective-permute-start | bytes 454664 | tf_op jit(solution)/shard_map/ppermute | solution.py:393
  40.3 11.2 %collective-permute-start.7 = (f32[36,8,128]{2,1,0:T(8,128)S(1)}, f32[36,8,128]{2,1,0:T(8,128)S(1)}, u32[]{:S(2)}, u32[]{:S(2)}) collective-permute-start(f32[36,8,128]{2,1,0:T(8,128)S(1)} %get-tuple-element.59), channel_id=1, source_target_pairs={{1,2},{3,4},{5,6},{2,1},{4,3},{6,5},{0,0},{7,7},{9,10},{11,12},{13... | collective-permute-start | bytes 442376 | tf_op jit(solution)/shard_map/ppermute | solution.py:393
  46.9 2.5 %collective-permute-start.5 = (f32[27,8,128]{2,1,0:T(8,128)S(1)}, f32[27,8,128]{2,1,0:T(8,128)S(1)}, u32[]{:S(2)}, u32[]{:S(2)}) collective-permute-start(f32[27,8,128]{2,1,0:T(8,128)S(1)} %get-tuple-element.57), channel_id=1, source_target_pairs={{0,8},{16,24},{8,0},{24,16},{1,9},{17,25},{9,1},{25,17},{2,10},{18... | collective-permute-start | bytes 331784 | tf_op jit(solution)/shard_map/ppermute | solution.py:393
  51.0 6.1 %collective-permute-start.8 = (f32[38,8,128]{2,1,0:T(8,128)S(1)}, f32[38,8,128]{2,1,0:T(8,128)S(1)}, u32[]{:S(2)}, u32[]{:S(2)}) collective-permute-start(f32[38,8,128]{2,1,0:T(8,128)S(1)} %get-tuple-element.63), channel_id=1, source_target_pairs={{0,1},{2,3},{4,5},{6,7},{1,0},{3,2},{5,4},{7,6},{8,9},{10,11},{12,... | collective-permute-start | bytes 466952 | tf_op jit(solution)/shard_map/ppermute | solution.py:393
  51.9 7.3 %collective-permute-start.10 = (f32[37,8,128]{2,1,0:T(8,128)S(1)}, f32[37,8,128]{2,1,0:T(8,128)S(1)}, u32[]{:S(2)}, u32[]{:S(2)}) collective-permute-start(f32[37,8,128]{2,1,0:T(8,128)S(1)} %get-tuple-element.68), channel_id=1, source_target_pairs={{8,16},{24,0},{16,8},{0,24},{9,17},{25,1},{17,9},{1,25},{10,18},{2... | collective-permute-start | bytes 454664 | tf_op jit(solution)/shard_map/ppermute | solution.py:393
  52.7 9.0 %collective-permute-start.11 = (f32[36,8,128]{2,1,0:T(8,128)S(1)}, f32[36,8,128]{2,1,0:T(8,128)S(1)}, u32[]{:S(2)}, u32[]{:S(2)}) collective-permute-start(f32[36,8,128]{2,1,0:T(8,128)S(1)} %get-tuple-element.69), channel_id=1, source_target_pairs={{1,2},{3,4},{5,6},{2,1},{4,3},{6,5},{0,0},{7,7},{9,10},{11,12},{13... | collective-permute-start | bytes 442376 | tf_op jit(solution)/shard_map/ppermute | solution.py:393
  56.8 2.4 %collective-permute-start.9 = (f32[27,8,128]{2,1,0:T(8,128)S(1)}, f32[27,8,128]{2,1,0:T(8,128)S(1)}, u32[]{:S(2)}, u32[]{:S(2)}) collective-permute-start(f32[27,8,128]{2,1,0:T(8,128)S(1)} %get-tuple-element.67), channel_id=1, source_target_pairs={{0,8},{16,24},{8,0},{24,16},{1,9},{17,25},{9,1},{25,17},{2,10},{18... | collective-permute-start | bytes 331784 | tf_op jit(solution)/shard_map/ppermute | solution.py:393

commit v14 on v12

--- a/solution.py
+++ b/solution.py
@@ -105,18 +105,30 @@
     most_ref[2:4, :] = -functools.reduce(jnp.minimum, rows)
 
 
-def extremes_kernel(wind_ref, most_ref):
-    put_extremes(wind_ref, most_ref.at[0])
-
-
-def opening_kernel(level_ref, x_near, x_far, t_near, t_far):
+def opening_kernel(level_in, wind_in, level_ref, x_near, x_far, t_near, t_far, wind_ref, sems):
+    planes = level_ref.shape[0]
+    step = batches(planes, 3)
+    pairs = [(wind_in, wind_ref)] + [
+        (level_in.at[pl.ds(i, step)], level_ref.at[pl.ds(i, step)])
+        for i in range(0, planes, step)
+    ]
+    copies = [
+        pltpu.make_async_copy(src, dst, sems.at[k]) for k, (src, dst) in enumerate(pairs)
+    ]
+    for copy in copies:
+        copy.start()
+    copies[0].wait()
+    put_extremes(wind_ref, x_near.at[x_near.shape[0] - 1])
+    for copy in copies[1:]:
+        copy.wait()
     cut_near(level_ref, x_near)
     cut_far(level_ref, x_far)
     cut_headings(level_ref, t_near, t_far)
 
 
-def meeting_kernel(own_ref, other_ref, most_ref):
-    most_ref[...] = jnp.maximum(own_ref[0], other_ref[0])
+def meeting_kernel(x_out, x_near, most_ref):
+    spot = x_near.shape[0] - 1
+    most_ref[...] = jnp.maximum(x_out[spot], x_near[spot])
 
 
 def flows_into(flow_ref, speed_step, wind_ref, waves_ref):
@@ -448,7 +460,6 @@
         pltpu.VMEM((groups, cross_count, lanes), jnp.float32),
         pltpu.VMEM((groups, cross_count, lanes), jnp.float32),
     ]
-    values = level_set
     size = lax.axis_size(axis)
     pairs = [(i, i + 1) for i in range(reach, size - 1, 2)]
     if wrap and reach and size % 2 == 0:
@@ -519,10 +530,16 @@
             pairs = [(i, i ^ reach) for i in range(size)]
         return lax.ppermute(most, "gx", pairs)
 
-    (most,) = call(extremes_kernel, [wind], [shape(longest + 2)])
-    other = spread(most, 1)
-    x_shapes = [shape(longest + 1), shape(longest)]
-    x_out, x_last, t_out, t_last = call(opening_kernel, [values], x_shapes + [shape(middle)] * 2)
+    level, x_out, x_last, t_out, t_last = pl.pallas_call(
+        opening_kernel,
+        out_shape=[field, shape(longest + 1), shape(longest), shape(middle), shape(middle)],
+        in_specs=[pl.BlockSpec(memory_space=pltpu.HBM)] * 2,
+        out_specs=[vmem] * 5,
+        scratch_shapes=[pltpu.VMEM(wind.shape, jnp.float32), pltpu.SemaphoreType.DMA((planes + 1,))],
+        compiler_params=pltpu.CompilerParams(vmem_limit_bytes=16 * 1024 * 1024),
+        cost_estimate=pl.CostEstimate(flops=0, bytes_accessed=0, transcendentals=0),
+    )(level_set, wind)
+    values = level
     far_shapes = [shape(short), shape(rim * planes), shape(middle)]
     for section in (1, 2, 3):
         opening = section == 1
@@ -533,7 +550,7 @@
         free = functools.partial(free_kernel, opening, speed_step)
         turning = functools.partial(heading_kernel, heading_step)
         if opening:
-            (most,) = call(meeting_kernel, [most, other], [shape()])
+            (most,) = call(meeting_kernel, [x_out, x_near], [shape()])
             other = spread(most, 2)
             ins = [values, wind, waves]
             spun, part, extra, flow = call(free, ins, [field] * 4, room, work=300)
@@ -543,7 +560,7 @@
                 most, part = lax.optimization_barrier((most, part))
                 other = spread(most, reach)
                 reach *= 2
-            part, x_near, x_far = lax.optimization_barrier((part, x_near, x_far))
+            part, x_far = lax.optimization_barrier((part, x_far))
         else:
             if section == 3:
                 values, x_near = lax.optimization_barrier((values, x_near))
@@ -561,7 +578,7 @@
             values, x_out, x_last, t_out, t_last, pk = call(closing, ins, outs, [rows])
         else:
             more = section == 2
-            ins = [level_set, values, part, x_near, wind, waves, target_mask, target_depth, pk]
+            ins = [level, values, part, x_near, wind, waves, target_mask, target_depth, pk]
             outs = [field] + ([shape(longest)] if more else [])
             last = functools.partial(section_kernel, section, (0, planes - rim), speed_step)
             early, *x_next = call(last, ins, outs, [rows, rows])

time: 41.2 us -> 43.1 us (1.046)
  waiting for transfers between devices: 5.92 us -> 8.24 us
  starting transfers between devices: 19.9 us -> 18.8 us
  Pallas kernels: 13.1 us -> 13.8 us
    ppermute x3 -> x2, starting transfers between devices: 4.17 us -> 2.1 us  [spread(): return lax.ppermute(most, 'gx', pairs)]
    ppermute x12, waiting for transfers between devices: 4.34 us -> 6.17 us  [trade(): return lax.ppermute(value, axis, pairs)]
    ppermute x12, starting transfers between devices: 15.8 us -> 16.7 us  [trade(): return lax.ppermute(value, axis, pairs)]
    pallas_call x0 -> x1, Pallas kernels: none -> 0.71 us  [local(): pl.pallas_call(opening_kernel, out_shape=[field, shape(longest + 1), shap...]
    ppermute x3 -> x2, waiting for transfers between devices: 1.58 us -> 2.07 us  [spread(): return lax.ppermute(most, 'gx', pairs)]
    pallas_call x15 -> x13, Pallas kernels: 13.1 us -> 13.1 us  [call(): pl.pallas_call(kernel, out_shape=outs, in_specs=[vmem] * len(ins), out_sp...]
    unnamed x14 -> x12, local copies, waits for them, and re-layouts: 1.74 us -> 1.73 us
  transfers between devices with their start and end apart: 15 -> 14, of which waited for: 7 -> 7; matrix products, arithmetic and copies ran while one was open for 0% -> 0% of each run, Pallas kernels for 28% -> 27%
where the time goes in v14:
time: 43.1 us; the launch traced here: 42.7 us
  starting transfers between devices  18.8 us (44%)
  Pallas kernels  13.8 us (32%)
  waiting for transfers between devices  8.24 us (19%)
  local copies, waits for them, and re-layouts  1.73 us (4%)
    ppermute x12, starting transfers between devices, trade(): return lax.ppermute(value, axis, pairs)  16.7 us
    pallas_call x13, Pallas kernels, call(): pl.pallas_call(kernel, out_shape=outs, in_specs=[vmem] * len(ins), out_sp...  13.1 us
    ppermute x12, waiting for transfers between devices, trade(): return lax.ppermute(value, axis, pairs)  6.17 us
    ppermute x2, starting transfers between devices, spread(): return lax.ppermute(most, 'gx', pairs)  2.1 us
    ppermute x2, waiting for transfers between devices, spread(): return lax.ppermute(most, 'gx', pairs)  2.07 us
    unnamed x12, local copies, waits for them, and re-layouts  1.73 us
  transfers between devices with their start and end apart: 14, of which 7 were waited for; matrix products, arithmetic and copies ran while one was open for 0% of the time, Pallas kernels for 27%

profile of v14, /device:TPU:8, one launch (start us, length us, event | category | flops | bytes accessed | tf_op | source)
XLA Modules:
  0.0 42.7 jit_solution(15270675032551832239)
XLA Ops:
  0.0 0.0 copy-start.1
  0.0 0.7 %copy-done.1 = f32[2,9,128]{2,0,1:T(2,128)S(1)} copy-done((f32[2,9,128]{2,0,1:T(2,128)S(1)}, f32[2,9,128]{2,0,1:T(2,128)}, u32[]{:S(2)}) %copy-start.1) | copy-done | bytes 9240
  0.7 0.0 copy-start.3
  0.7 1.0 %copy-done.3 = f32[9,12,8,128]{3,2,1,0:T(8,128)S(1)} copy-done((f32[9,12,8,128]{3,2,1,0:T(8,128)S(1)}, f32[9,12,8,128]{3,2,1,0:T(8,128)}, u32[]{:S(2)}) %copy-start.3) | copy-done | bytes 442392
  1.7 0.7 %shard_map.55 = (f32[9,12,8,128]{3,2,1,0:T(8,128)S(1)}, f32[39,8,128]{2,1,0:T(8,128)S(1)}, f32[38,8,128]{2,1,0:T(8,128)S(1)}, f32[37,8,128]{2,1,0:T(8,128)S(1)}, f32[37,8,128]{2,1,0:T(8,128)S(1)}) custom-call(f32[9,12,8,128]{3,2,1,0:T(8,128)S(1)} %copy-done.3, f32[9,2,128]{2,1,0:T(2,128)S(1)} %bitcast.1), custom_call_target="tpu_custom_call" | custom-call | tf_op jit(solution)/shard_map/pallas_call | solution.py:533
  2.4 1.6 %collective-permute-start = (f32[39,8,128]{2,1,0:T(8,128)S(1)}, f32[39,8,128]{2,1,0:T(8,128)S(1)}, u32[]{:S(2)}, u32[]{:S(2)}) collective-permute-start(f32[39,8,128]{2,1,0:T(8,128)S(1)} %get-tuple-element.42.x_out), channel_id=1, source_target_pairs={{0,1},{2,3},{4,5},{6,7},{1,0},{3,2},{5,4},{7,6},{8,9},{10,11},{12,... | collective-permute-start | bytes 479240 | tf_op jit(solution)/shard_map/ppermute | solution.py:409
  4.0 1.9 %collective-permute-start.2 = (f32[38,8,128]{2,1,0:T(8,128)S(1)}, f32[38,8,128]{2,1,0:T(8,128)S(1)}, u32[]{:S(2)}, u32[]{:S(2)}) collective-permute-start(f32[38,8,128]{2,1,0:T(8,128)S(1)} %get-tuple-element.45), channel_id=1, source_target_pairs={{1,2},{3,4},{5,6},{2,1},{4,3},{6,5},{0,0},{7,7},{9,10},{11,12},{13... | collective-permute-start | bytes 466952 | tf_op jit(solution)/shard_map/ppermute | solution.py:409
  5.9 0.1 collective-permute-start.3
  6.0 0.0 copy-start
  6.0 2.0 %collective-permute-start.4 = (f32[37,8,128]{2,1,0:T(8,128)S(1)}, f32[37,8,128]{2,1,0:T(8,128)S(1)}, u32[]{:S(2)}, u32[]{:S(2)}) collective-permute-start(f32[37,8,128]{2,1,0:T(8,128)S(1)} %get-tuple-element.48), channel_id=1, source_target_pairs={{8,16},{24,0},{16,8},{0,24},{9,17},{25,1},{17,9},{1,25},{10,18},{2... | collective-permute-start | bytes 454664 | tf_op jit(solution)/shard_map/ppermute | solution.py:409
  8.0 2.8 %collective-permute-done.x_near.near_ref = f32[39,8,128]{2,1,0:T(8,128)S(1)} collective-permute-done((f32[39,8,128]{2,1,0:T(8,128)S(1)}, f32[39,8,128]{2,1,0:T(8,128)S(1)}, u32[]{:S(2)}, u32[]{:S(2)}) %collective-permute-start) | collective-permute-done | bytes 159776 | tf_op jit(solution)/shard_map/ppermute | solution.py:409
  10.8 0.4 %collective-permute-start.1 = (f32[8,128]{1,0:T(8,128)S(1)}, f32[8,128]{1,0:T(8,128)S(1)}, u32[]{:S(2)}, u32[]{:S(2)}) collective-permute-start(f32[8,128]{1,0:T(8,128)S(1)} %shard_map.57), channel_id=1, source_target_pairs={{0,2},{1,3},{2,0},{3,1},{4,6},{5,7},{6,4},{7,5},{8,10},{9,11},{10,... | collective-permute-start | bytes 12296 | tf_op jit(solution)/shard_map/ppermute | solution.py:531
  11.2 0.0 copy-done
  11.2 2.1 %shard_map.56 = (f32[9,12,8,128]{3,2,1,0:T(8,128)S(1)}, f32[9,12,8,128]{3,2,1,0:T(8,128)S(1)}, f32[9,12,8,128]{3,2,1,0:T(8,128)S(1)}, f32[9,12,8,128]{3,2,1,0:T(8,128)S(1)}) custom-call(f32[9,12,8,128]{3,2,1,0:T(8,128)S(1)} %get-tuple-element.40.s_ref.base_ref, f32[9,2,128]{2,1,0:T(2,128)S(1)} %bitcast.2, f32[2,48,128]{2,1,0:T(8,128)S(1)} %copy-done), custom_call_target="tpu_custom_call" | custom-call | flops 33177600 | bytes 33177600 | tf_op jit(solution)/shard_map/pallas_call | solution.py:503
  13.3 1.0 %collective-permute-done.1 = f32[8,128]{1,0:T(8,128)S(1)} collective-permute-done((f32[8,128]{1,0:T(8,128)S(1)}, f32[8,128]{1,0:T(8,128)S(1)}, u32[]{:S(2)}, u32[]{:S(2)}) %collective-permute-start.1) | collective-permute-done | bytes 4128 | tf_op jit(solution)/shard_map/ppermute | solution.py:531
  14.4 0.0 collective-permute-done.2.far_ref
  14.4 1.7 %collective-permute-start.5 = (f32[8,128]{1,0:T(8,128)S(1)}, f32[8,128]{1,0:T(8,128)S(1)}, u32[]{:S(2)}, u32[]{:S(2)}) collective-permute-start(f32[8,128]{1,0:T(8,128)S(1)} %max.3.most_ref), channel_id=1, source_target_pairs={{0,4},{1,5},{2,6},{3,7},{4,0},{5,1},{6,2},{7,3},{8,12},{9,13},{10,... | collective-permute-start | bytes 12296 | tf_op jit(solution)/shard_map/ppermute | solution.py:531
  16.0 0.0 collective-permute-done.3.near_ref
  16.0 0.0 collective-permute-done.4.far_ref
  16.0 0.0 copy-start.2
  16.0 0.9 %shard_map.58.part_ref = f32[9,12,8,128]{3,2,1,0:T(8,128)S(1)} custom-call(f32[9,12,8,128]{3,2,1,0:T(8,128)S(1)} %get-tuple-element.40.s_ref.base_ref, f32[9,12,8,128]{3,2,1,0:T(8,128)S(1)} %get-tuple-element.41.speed_ref, f32[9,12,8,128]{3,2,1,0:T(8,128)S(1)} %get-tuple-element.46.part_ref, f32[37,8,128]{2,1,0:T(8,128)S(1)} %collective-permute-done.3.near_ref, ...), custom_call_target="tpu_custom_call" | custom-call | flops 110592000 | bytes 110592000 | tf_op jit(solution)/shard_map/pallas_call | solution.py:503
  16.9 0.0 copy-done.2
  16.9 0.0 copy-start.4
  16.9 0.0 copy-start.5
  16.9 0.9 %shard_map.59 = (f32[9,12,8,128]{3,2,1,0:T(8,128)S(1)}, f32[9,12,8,128]{3,2,1,0:T(8,128)S(1)}) custom-call(f32[9,12,8,128]{3,2,1,0:T(8,128)S(1)} %get-tuple-element.40.s_ref.base_ref, f32[9,12,8,128]{3,2,1,0:T(8,128)S(1)} %shard_map.58.part_ref, f32[39,8,128]{2,1,0:T(8,128)S(1)} %collective-permute-done.x_near.near_ref, ...), custom_call_target="tpu_custom_call" | custom-call | tf_op jit(solution)/shard_map/pallas_call | solution.py:503
  17.8 1.0 %collective-permute-done.5.other_ref = f32[8,128]{1,0:T(8,128)S(1)} collective-permute-done((f32[8,128]{1,0:T(8,128)S(1)}, f32[8,128]{1,0:T(8,128)S(1)}, u32[]{:S(2)}, u32[]{:S(2)}) %collective-permute-start.5) | collective-permute-done | bytes 4128 | tf_op jit(solution)/shard_map/ppermute | solution.py:531
  18.9 0.0 copy-done.4
  18.9 0.0 copy-done.5
  18.9 0.4 shard_map.60
  19.3 2.5 %collective-permute-start.6 = (f32[38,8,128]{2,1,0:T(8,128)S(1)}, f32[38,8,128]{2,1,0:T(8,128)S(1)}, u32[]{:S(2)}, u32[]{:S(2)}) collective-permute-start(f32[38,8,128]{2,1,0:T(8,128)S(1)} %get-tuple-element.59), channel_id=1, source_target_pairs={{0,1},{2,3},{4,5},{6,7},{1,0},{3,2},{5,4},{7,6},{8,9},{10,11},{12,... | collective-permute-start | bytes 466952 | tf_op jit(solution)/shard_map/ppermute | solution.py:409
  21.8 0.0 collective-permute-start.8
  21.8 2.1 %collective-permute-start.9 = (f32[36,8,128]{2,1,0:T(8,128)S(1)}, f32[36,8,128]{2,1,0:T(8,128)S(1)}, u32[]{:S(2)}, u32[]{:S(2)}) collective-permute-start(f32[36,8,128]{2,1,0:T(8,128)S(1)} %get-tuple-element.63), channel_id=1, source_target_pairs={{1,2},{3,4},{5,6},{2,1},{4,3},{6,5},{0,0},{7,7},{9,10},{11,12},{13... | collective-permute-start | bytes 442376 | tf_op jit(solution)/shard_map/ppermute | solution.py:409
  23.9 1.5 %collective-permute-start.7 = (f32[27,8,128]{2,1,0:T(8,128)S(1)}, f32[27,8,128]{2,1,0:T(8,128)S(1)}, u32[]{:S(2)}, u32[]{:S(2)}) collective-permute-start(f32[27,8,128]{2,1,0:T(8,128)S(1)} %get-tuple-element.61), channel_id=1, source_target_pairs={{0,8},{16,24},{8,0},{24,16},{1,9},{17,25},{9,1},{25,17},{2,10},{18... | collective-permute-start | bytes 331784 | tf_op jit(solution)/shard_map/ppermute | solution.py:409
  25.4 2.1 %shard_map.61 = (f32[9,12,8,128]{3,2,1,0:T(8,128)S(1)}, f32[9,12,8,128]{3,2,1,0:T(8,128)S(1)}) custom-call(f32[9,12,8,128]{3,2,1,0:T(8,128)S(1)} %get-tuple-element.54.s_ref, f32[9,12,8,128]{3,2,1,0:T(8,128)S(1)} %get-tuple-element.55.rest_0_, f32[8,128]{1,0:T(8,128)S(1)} %get-tuple-element.56.rest_1_.pk_ref), custom_call_target="tpu_custom_call" | custom-call | tf_op jit(solution)/shard_map/pallas_call | solution.py:503
  27.5 0.0 collective-permute-done.6.ghosts_ref
  27.5 0.0 collective-permute-done.7.near_ref
  27.5 0.5 %collective-permute-done.8.far_ref = f32[37,8,128]{2,1,0:T(8,128)S(1)} collective-permute-done((f32[37,8,128]{2,1,0:T(8,128)S(1)}, f32[37,8,128]{2,1,0:T(8,128)S(1)}, u32[]{:S(2)}, u32[]{:S(2)}) %collective-permute-start.8) | collective-permute-done | bytes 151584 | tf_op jit(solution)/shard_map/ppermute | solution.py:409
  28.0 0.8 %shard_map.62.part_ref = f32[9,12,8,128]{3,2,1,0:T(8,128)S(1)} custom-call(f32[9,12,8,128]{3,2,1,0:T(8,128)S(1)} %get-tuple-element.54.s_ref, f32[9,12,8,128]{3,2,1,0:T(8,128)S(1)} %get-tuple-element.57.speed_ref, f32[9,12,8,128]{3,2,1,0:T(8,128)S(1)} %get-tuple-element.60.part_ref, f32[27,8,128]{2,1,0:T(8,128)S(1)} %collective-permute-done.7.near_ref, ...), custom_call_target="tpu_custom_call" | custom-call | flops 110592000 | bytes 110592000 | tf_op jit(solution)/shard_map/pallas_call | solution.py:503
  28.8 0.7 %shard_map.63 = (f32[9,12,8,128]{3,2,1,0:T(8,128)S(1)}, f32[38,8,128]{2,1,0:T(8,128)S(1)}) custom-call(f32[9,12,8,128]{3,2,1,0:T(8,128)S(1)} %get-tuple-element.40.s_ref.base_ref, f32[9,12,8,128]{3,2,1,0:T(8,128)S(1)} %get-tuple-element.54.s_ref, f32[9,12,8,128]{3,2,1,0:T(8,128)S(1)} %shard_map.62.part_ref, ...), custom_call_target="tpu_custom_call" | custom-call | tf_op jit(solution)/shard_map/pallas_call | solution.py:503
  29.6 2.3 %collective-permute-start.10 = (f32[38,8,128]{2,1,0:T(8,128)S(1)}, f32[38,8,128]{2,1,0:T(8,128)S(1)}, u32[]{:S(2)}, u32[]{:S(2)}) collective-permute-start(f32[38,8,128]{2,1,0:T(8,128)S(1)} %get-tuple-element.67), channel_id=1, source_target_pairs={{0,1},{2,3},{4,5},{6,7},{1,0},{3,2},{5,4},{7,6},{8,9},{10,11},{12,... | collective-permute-start | bytes 466952 | tf_op jit(solution)/shard_map/ppermute | solution.py:409
  31.9 0.0 collective-permute-done.9.ghosts_ref
  31.9 0.4 shard_map.64
  32.3 0.1 collective-permute-start.12
  32.4 2.3 %collective-permute-start.13 = (f32[36,8,128]{2,1,0:T(8,128)S(1)}, f32[36,8,128]{2,1,0:T(8,128)S(1)}, u32[]{:S(2)}, u32[]{:S(2)}) collective-permute-start(f32[36,8,128]{2,1,0:T(8,128)S(1)} %get-tuple-element.73), channel_id=1, source_target_pairs={{1,2},{3,4},{5,6},{2,1},{4,3},{6,5},{0,0},{7,7},{9,10},{11,12},{13... | collective-permute-start | bytes 442376 | tf_op jit(solution)/shard_map/ppermute | solution.py:409
  34.7 0.4 collective-permute-start.11
  35.0 1.1 %collective-permute-done.10.ghosts_ref = f32[38,8,128]{2,1,0:T(8,128)S(1)} collective-permute-done((f32[38,8,128]{2,1,0:T(8,128)S(1)}, f32[38,8,128]{2,1,0:T(8,128)S(1)}, u32[]{:S(2)}, u32[]{:S(2)}) %collective-permute-start.10) | collective-permute-done | bytes 155680 | tf_op jit(solution)/shard_map/ppermute | solution.py:409
  36.1 2.1 %shard_map.65 = (f32[9,12,8,128]{3,2,1,0:T(8,128)S(1)}, f32[9,12,8,128]{3,2,1,0:T(8,128)S(1)}) custom-call(f32[9,12,8,128]{3,2,1,0:T(8,128)S(1)} %get-tuple-element.68.s_ref, f32[9,12,8,128]{3,2,1,0:T(8,128)S(1)} %get-tuple-element.55.rest_0_, f32[8,128]{1,0:T(8,128)S(1)} %get-tuple-element.56.rest_1_.pk_ref), custom_call_target="tpu_custom_call" | custom-call | tf_op jit(solution)/shard_map/pallas_call | solution.py:503
  38.2 0.0 collective-permute-done.11.near_ref
  38.2 0.3 collective-permute-done.12.far_ref
  38.5 0.8 %shard_map.66.part_ref = f32[9,12,8,128]{3,2,1,0:T(8,128)S(1)} custom-call(f32[9,12,8,128]{3,2,1,0:T(8,128)S(1)} %get-tuple-element.68.s_ref, f32[9,12,8,128]{3,2,1,0:T(8,128)S(1)} %get-tuple-element.69.speed_ref, f32[9,12,8,128]{3,2,1,0:T(8,128)S(1)} %get-tuple-element.70.part_ref, f32[27,8,128]{2,1,0:T(8,128)S(1)} %collective-permute-done.11.near_ref, ...), custom_call_target="tpu_custom_call" | custom-call | flops 110592000 | bytes 110592000 | tf_op jit(solution)/shard_map/pallas_call | solution.py:503
  39.4 0.7 %shard_map.67.refs_0_ = f32[9,12,8,128]{3,2,1,0:T(8,128)S(1)} custom-call(f32[9,12,8,128]{3,2,1,0:T(8,128)S(1)} %get-tuple-element.40.s_ref.base_ref, f32[9,12,8,128]{3,2,1,0:T(8,128)S(1)} %get-tuple-element.68.s_ref, f32[9,12,8,128]{3,2,1,0:T(8,128)S(1)} %shard_map.66.part_ref, f32[38,8,128]{2,1,0:T(8,128)S(1)} %collective-permute-done.10.ghosts_ref, ...), custom_call_target="tpu_custom_call" | custom-call | tf_op jit(solution)/shard_map/pallas_call | solution.py:503
  40.1 1.5 %collective-permute-done.13.ghosts_ref = f32[36,8,128]{2,1,0:T(8,128)S(1)} collective-permute-done((f32[36,8,128]{2,1,0:T(8,128)S(1)}, f32[36,8,128]{2,1,0:T(8,128)S(1)}, u32[]{:S(2)}, u32[]{:S(2)}) %collective-permute-start.13) | collective-permute-done | bytes 147488 | tf_op jit(solution)/shard_map/ppermute | solution.py:409
  41.6 1.1 %shard_map.68 = f32[9,12,8,128]{3,2,1,0:T(8,128)} custom-call(f32[9,12,8,128]{3,2,1,0:T(8,128)S(1)} %get-tuple-element.40.s_ref.base_ref, f32[9,12,8,128]{3,2,1,0:T(8,128)S(1)} %get-tuple-element.68.s_ref, f32[9,12,8,128]{3,2,1,0:T(8,128)S(1)} %shard_map.66.part_ref, f32[36,8,128]{2,1,0:T(8,128)S(1)} %collective-permute-done.13.ghosts_ref, ...), custom_call_target="tpu_custom_call" | custom-call | tf_op jit(solution)/shard_map/pallas_call | solution.py:503
  (2 shorter events, 0.0 us)
Async XLA Ops:
  0.0 0.7 %copy-start.1 = (f32[2,9,128]{2,0,1:T(2,128)S(1)}, f32[2,9,128]{2,0,1:T(2,128)}, u32[]{:S(2)}) copy-start(f32[2,9,128]{2,0,1:T(2,128)} %param.6) | copy-start | bytes 27652
  0.7 1.0 %copy-start.3 = (f32[9,12,8,128]{3,2,1,0:T(8,128)S(1)}, f32[9,12,8,128]{3,2,1,0:T(8,128)}, u32[]{:S(2)}) copy-start(f32[9,12,8,128]{3,2,1,0:T(8,128)} %level_in.1) | copy-start | bytes 1327108
  2.4 8.3 %collective-permute-start = (f32[39,8,128]{2,1,0:T(8,128)S(1)}, f32[39,8,128]{2,1,0:T(8,128)S(1)}, u32[]{:S(2)}, u32[]{:S(2)}) collective-permute-start(f32[39,8,128]{2,1,0:T(8,128)S(1)} %get-tuple-element.42.x_out), channel_id=1, source_target_pairs={{0,1},{2,3},{4,5},{6,7},{1,0},{3,2},{5,4},{7,6},{8,9},{10,11},{12,... | collective-permute-start | bytes 479240 | tf_op jit(solution)/shard_map/ppermute | solution.py:409
  4.0 10.4 %collective-permute-start.2 = (f32[38,8,128]{2,1,0:T(8,128)S(1)}, f32[38,8,128]{2,1,0:T(8,128)S(1)}, u32[]{:S(2)}, u32[]{:S(2)}) collective-permute-start(f32[38,8,128]{2,1,0:T(8,128)S(1)} %get-tuple-element.45), channel_id=1, source_target_pairs={{1,2},{3,4},{5,6},{2,1},{4,3},{6,5},{0,0},{7,7},{9,10},{11,12},{13... | collective-permute-start | bytes 466952 | tf_op jit(solution)/shard_map/ppermute | solution.py:409
  5.9 10.1 %collective-permute-start.3 = (f32[37,8,128]{2,1,0:T(8,128)S(1)}, f32[37,8,128]{2,1,0:T(8,128)S(1)}, u32[]{:S(2)}, u32[]{:S(2)}) collective-permute-start(f32[37,8,128]{2,1,0:T(8,128)S(1)} %get-tuple-element.47), channel_id=1, source_target_pairs={{0,8},{16,24},{8,0},{24,16},{1,9},{17,25},{9,1},{25,17},{2,10},{18... | collective-permute-start | bytes 454664 | tf_op jit(solution)/shard_map/ppermute | solution.py:409
  6.0 5.2 %copy-start = (f32[2,48,128]{2,1,0:T(8,128)S(1)}, f32[2,48,128]{2,1,0:T(8,128)}, u32[]{:S(2)}) copy-start(f32[2,48,128]{2,1,0:T(8,128)} %constant.2.clone.rest_1_.waves_ref) | copy-start | bytes 147460
  6.0 10.0 %collective-permute-start.4 = (f32[37,8,128]{2,1,0:T(8,128)S(1)}, f32[37,8,128]{2,1,0:T(8,128)S(1)}, u32[]{:S(2)}, u32[]{:S(2)}) collective-permute-start(f32[37,8,128]{2,1,0:T(8,128)S(1)} %get-tuple-element.48), channel_id=1, source_target_pairs={{8,16},{24,0},{16,8},{0,24},{9,17},{25,1},{17,9},{1,25},{10,18},{2... | collective-permute-start | bytes 454664 | tf_op jit(solution)/shard_map/ppermute | solution.py:409
  10.8 3.6 %collective-permute-start.1 = (f32[8,128]{1,0:T(8,128)S(1)}, f32[8,128]{1,0:T(8,128)S(1)}, u32[]{:S(2)}, u32[]{:S(2)}) collective-permute-start(f32[8,128]{1,0:T(8,128)S(1)} %shard_map.57), channel_id=1, source_target_pairs={{0,2},{1,3},{2,0},{3,1},{4,6},{5,7},{6,4},{7,5},{8,10},{9,11},{10,... | collective-permute-start | bytes 12296 | tf_op jit(solution)/shard_map/ppermute | solution.py:531
  14.4 4.5 %collective-permute-start.5 = (f32[8,128]{1,0:T(8,128)S(1)}, f32[8,128]{1,0:T(8,128)S(1)}, u32[]{:S(2)}, u32[]{:S(2)}) collective-permute-start(f32[8,128]{1,0:T(8,128)S(1)} %max.3.most_ref), channel_id=1, source_target_pairs={{0,4},{1,5},{2,6},{3,7},{4,0},{5,1},{6,2},{7,3},{8,12},{9,13},{10,... | collective-permute-start | bytes 12296 | tf_op jit(solution)/shard_map/ppermute | solution.py:531
  16.0 0.9 %copy-start.2 = (f32[2,9,128]{2,0,1:T(2,128)S(1)}, f32[2,9,128]{2,0,1:T(2,128)}, u32[]{:S(2)}) copy-start(f32[2,9,128]{2,0,1:T(2,128)} %param.6) | copy-start | bytes 27652
  16.9 2.0 %copy-start.4 = (s32[9,128]{1,0:T(8,128)S(1)}, s32[9,128]{1,0:T(8,128)}, u32[]{:S(2)}) copy-start(s32[9,128]{1,0:T(8,128)} %mask_ref.9) | copy-start | bytes 13828
  16.9 2.0 %copy-start.5 = (f32[9,128]{1,0:T(8,128)S(1)}, f32[9,128]{1,0:T(8,128)}, u32[]{:S(2)}) copy-start(f32[9,128]{1,0:T(8,128)} %depth_ref.9) | copy-start | bytes 13828
  19.3 8.2 %collective-permute-start.6 = (f32[38,8,128]{2,1,0:T(8,128)S(1)}, f32[38,8,128]{2,1,0:T(8,128)S(1)}, u32[]{:S(2)}, u32[]{:S(2)}) collective-permute-start(f32[38,8,128]{2,1,0:T(8,128)S(1)} %get-tuple-element.59), channel_id=1, source_target_pairs={{0,1},{2,3},{4,5},{6,7},{1,0},{3,2},{5,4},{7,6},{8,9},{10,11},{12,... | collective-permute-start | bytes 466952 | tf_op jit(solution)/shard_map/ppermute | solution.py:409
  21.8 6.2 %collective-permute-start.8 = (f32[37,8,128]{2,1,0:T(8,128)S(1)}, f32[37,8,128]{2,1,0:T(8,128)S(1)}, u32[]{:S(2)}, u32[]{:S(2)}) collective-permute-start(f32[37,8,128]{2,1,0:T(8,128)S(1)} %get-tuple-element.62), channel_id=1, source_target_pairs={{8,16},{24,0},{16,8},{0,24},{9,17},{25,1},{17,9},{1,25},{10,18},{2... | collective-permute-start | bytes 454664 | tf_op jit(solution)/shard_map/ppermute | solution.py:409
  21.8 10.1 %collective-permute-start.9 = (f32[36,8,128]{2,1,0:T(8,128)S(1)}, f32[36,8,128]{2,1,0:T(8,128)S(1)}, u32[]{:S(2)}, u32[]{:S(2)}) collective-permute-start(f32[36,8,128]{2,1,0:T(8,128)S(1)} %get-tuple-element.63), channel_id=1, source_target_pairs={{1,2},{3,4},{5,6},{2,1},{4,3},{6,5},{0,0},{7,7},{9,10},{11,12},{13... | collective-permute-start | bytes 442376 | tf_op jit(solution)/shard_map/ppermute | solution.py:409
  23.9 3.6 %collective-permute-start.7 = (f32[27,8,128]{2,1,0:T(8,128)S(1)}, f32[27,8,128]{2,1,0:T(8,128)S(1)}, u32[]{:S(2)}, u32[]{:S(2)}) collective-permute-start(f32[27,8,128]{2,1,0:T(8,128)S(1)} %get-tuple-element.61), channel_id=1, source_target_pairs={{0,8},{16,24},{8,0},{24,16},{1,9},{17,25},{9,1},{25,17},{2,10},{18... | collective-permute-start | bytes 331784 | tf_op jit(solution)/shard_map/ppermute | solution.py:409
  29.6 6.5 %collective-permute-start.10 = (f32[38,8,128]{2,1,0:T(8,128)S(1)}, f32[38,8,128]{2,1,0:T(8,128)S(1)}, u32[]{:S(2)}, u32[]{:S(2)}) collective-permute-start(f32[38,8,128]{2,1,0:T(8,128)S(1)} %get-tuple-element.67), channel_id=1, source_target_pairs={{0,1},{2,3},{4,5},{6,7},{1,0},{3,2},{5,4},{7,6},{8,9},{10,11},{12,... | collective-permute-start | bytes 466952 | tf_op jit(solution)/shard_map/ppermute | solution.py:409
  32.3 6.2 %collective-permute-start.12 = (f32[37,8,128]{2,1,0:T(8,128)S(1)}, f32[37,8,128]{2,1,0:T(8,128)S(1)}, u32[]{:S(2)}, u32[]{:S(2)}) collective-permute-start(f32[37,8,128]{2,1,0:T(8,128)S(1)} %get-tuple-element.72), channel_id=1, source_target_pairs={{8,16},{24,0},{16,8},{0,24},{9,17},{25,1},{17,9},{1,25},{10,18},{2... | collective-permute-start | bytes 454664 | tf_op jit(solution)/shard_map/ppermute | solution.py:409
  32.4 9.2 %collective-permute-start.13 = (f32[36,8,128]{2,1,0:T(8,128)S(1)}, f32[36,8,128]{2,1,0:T(8,128)S(1)}, u32[]{:S(2)}, u32[]{:S(2)}) collective-permute-start(f32[36,8,128]{2,1,0:T(8,128)S(1)} %get-tuple-element.73), channel_id=1, source_target_pairs={{1,2},{3,4},{5,6},{2,1},{4,3},{6,5},{0,0},{7,7},{9,10},{11,12},{13... | collective-permute-start | bytes 442376 | tf_op jit(solution)/shard_map/ppermute | solution.py:409
  34.7 3.5 %collective-permute-start.11 = (f32[27,8,128]{2,1,0:T(8,128)S(1)}, f32[27,8,128]{2,1,0:T(8,128)S(1)}, u32[]{:S(2)}, u32[]{:S(2)}) collective-permute-start(f32[27,8,128]{2,1,0:T(8,128)S(1)} %get-tuple-element.71), channel_id=1, source_target_pairs={{0,8},{16,24},{8,0},{24,16},{1,9},{17,25},{9,1},{25,17},{2,10},{18... | collective-permute-start | bytes 331784 | tf_op jit(solution)/shard_map/ppermute | solution.py:409

commit v15 on v12

--- a/solution.py
+++ b/solution.py
@@ -141,16 +141,15 @@
         return ref.reshape(cells * speeds, width)
 
     if split:
-        wind_ref, waves_ref, speed_ref, out_ref, extra_ref, flow_ref = rest[:-3]
+        wind_ref, waves_ref, speed_ref, out_ref, extra_ref, flow_t_ref = rest[:6]
+        turned_ref, drift_ref, gap_ref, flow_ref = rest[6:]
         flows_into(flow_ref, speed_step, wind_ref, waves_ref)
-        extra_rows = rows_of(extra_ref)
+        extra_rows, flow_rows = rows_of(extra_ref), rows_of(flow_ref)
     else:
-        flow_ref, pk_ref, speed_ref, out_ref = rest[:-3]
-        peak = splat(pk_ref[1:2, :] * gain, (16 * speeds, width))
-    turned_ref, mean_ref, gap_ref = rest[-3:]
+        flow_t_ref, pk_ref, speed_ref, out_ref, turned_ref, drift_ref = rest
+        peak = splat(pk_ref[1:2, :] * gain, (speeds, width))
     gain_v = thrust_limit / (12.0 * speed_step)
-    s_rows, speed_rows = rows_of(s_ref), rows_of(speed_ref)
-    out_rows, flow_rows = rows_of(out_ref), rows_of(flow_ref)
+    s_rows, speed_rows, out_rows = rows_of(s_ref), rows_of(speed_ref), rows_of(out_ref)
     few, many = 8, turned_ref.shape[2] // speeds
     groups = turned_ref.shape[0]
     lanes = many * speeds
@@ -173,22 +172,24 @@
         for k in range(rim):
             turned_ref[n, k : k + 1, :] = turned[:1]
             turned_ref[n, rim + width + k : rim + width + k + 1, :] = turned[-1:]
+        if split:
+            flow_t_ref[n] = flow_rows[span(n), :].T
 
     def along_y(n):
         ends = [turned_ref[n, pl.ds(k, high, stride=lines), :] for k in range(lines + 2 * rim)]
         for k, (mean, gap) in enumerate(row_terms(ends, spacing)):
-            mean_ref[n, pl.ds(k, high, stride=lines), :] = mean
-            gap_ref[n, pl.ds(k, high, stride=lines), :] = gap
+            spot = pl.ds(k, high, stride=lines)
+            drift = mean * flow_t_ref[n, spot, :]
+            if split:
+                drift_ref[n, spot, :] = drift
+                gap_ref[n, spot, :] = gap
+            else:
+                drift_ref[n, spot, :] = drift + gap * peak
 
     def turn_out(n):
-        mean = mean_ref[n].T
-        gap = gap_ref[n].T
-        drift = mean * flow_rows[span(n), :]
+        out_rows[span(n), :] = drift_ref[n].T
         if split:
-            out_rows[span(n), :] = drift
-            extra_rows[span(n), :] = gap
-        else:
-            out_rows[span(n), :] = drift + gap * peak
+            extra_rows[span(n), :] = gap_ref[n].T
 
     def step(n, carry):
         turn_out(jnp.maximum(n - 1, 0))
@@ -207,7 +208,7 @@
     planes, headings = s_ref.shape[:2]
     gain_t = turn_limit / (12.0 * heading_step)
     odd = odd_place("head")
-    wide = batches(planes, 3)
+    wide = batches(planes, 9)
 
     def step(n, carry):
         for w in range(wide):
@@ -443,73 +444,13 @@
     wind = jnp.transpose(wind_field, (1, 0, 2))
     many = 16
     groups, lanes = -(-planes * headings // many), many * speed_count
+    turned = (groups, cross_count, lanes)
     room = [
         pltpu.VMEM((groups, cross_count + 8, lanes), jnp.float32),
-        pltpu.VMEM((groups, cross_count, lanes), jnp.float32),
-        pltpu.VMEM((groups, cross_count, lanes), jnp.float32),
+        pltpu.VMEM(turned, jnp.float32),
     ]
+    wide_room = room + [pltpu.VMEM(turned, jnp.float32), pltpu.VMEM(level_set.shape, jnp.float32)]
     values = level_set
-    size = lax.axis_size(axis)
-    pairs = [(i, i + 1) for i in range(reach, size - 1, 2)]
-    if wrap and reach and size % 2 == 0:
-        pairs.append((size - 1, 0))
-    pairs += [(j, i) for i, j in pairs]
-    pairs += [(i, i) for i in range(size) if i not in dict(pairs)]
-    return lax.ppermute(value, axis, pairs)
-
-
-def local(level_set, wind_field, target_mask, target_depth):
-    planes, headings, speed_count, cross_count = level_set.shape
-    heading_total = headings * lax.axis_size("head")
-    heading_step = 2.0 * math.pi / heading_total
-    speed_step = (speed_high - speed_low) / (speed_count - 1)
-    speed_row = np.float32(speed_low) + np.arange(speed_count, dtype=np.float32) * np.float32(
-        speed_step
-    )
-    angles = np.arange(heading_total, dtype=np.float32) * np.float32(heading_step)
-    waves = [np.cos(angles), np.sin(angles)]
-    bounds = []
-    for wave in waves:
-        product = wave[:, None] * speed_row[None, :]
-        bounds.append((float(product.min()), float(product.max())))
-    waves = jnp.asarray(np.stack(waves)[..., None] * np.ones(cross_count, np.float32))
-
-    vmem = pl.BlockSpec(memory_space=pltpu.VMEM)
-    tile = (speed_count, cross_count)
-
-    def shape(*dims):
-        return jax.ShapeDtypeStruct(dims + tile, jnp.float32)
-
-    field = shape(planes, headings)
-    short = rim * headings
-    middle = max(short + 1, rim * planes)
-
-    longest = middle + 1
-    rows = pltpu.VMEM((planes,) + tile, jnp.float32)
-    cells = math.prod(level_set.shape)
-
-    def call(kernel, ins, outs, scratch=(), work=0):
-        return pl.pallas_call(
-            kernel,
-            out_shape=outs,
-            in_specs=[vmem] * len(ins),
-            out_specs=[vmem] * len(outs),
-            scratch_shapes=list(scratch),
-            compiler_params=pltpu.CompilerParams(vmem_limit_bytes=16 * 1024 * 1024),
-            cost_estimate=pl.CostEstimate(
-                flops=work * cells, bytes_accessed=work * cells, transcendentals=0
-            ),
-        )(*ins)
-
-    wind = jnp.transpose(wind_field, (1, 0, 2))
-    many = 16
-    groups, lanes = -(-planes * headings // many), many * speed_count
-    room = [
-        pltpu.VMEM((groups, cross_count + 8, lanes), jnp.float32),
-        pltpu.VMEM((groups, cross_count, lanes), jnp.float32),
-        pltpu.VMEM((groups, cross_count, lanes), jnp.float32),
-    ]
-    values, pk = level_set, None
     size = lax.axis_size("gx")
 
     def spread(most, reach):
@@ -521,7 +462,7 @@
 
     (most,) = call(extremes_kernel, [wind], [shape(longest + 2)])
     other = spread(most, 1)
-    x_shapes = [shape(longest + 1), shape(longest)]
+    x_shapes = [shape(longest), shape(longest + 1)]
     x_out, x_last, t_out, t_last = call(opening_kernel, [values], x_shapes + [shape(middle)] * 2)
     far_shapes = [shape(short), shape(rim * planes), shape(middle)]
     for section in (1, 2, 3):
@@ -536,14 +477,16 @@
             (most,) = call(meeting_kernel, [most, other], [shape()])
             other = spread(most, 2)
             ins = [values, wind, waves]
-            spun, part, extra, flow = call(free, ins, [field] * 4, room, work=300)
+            spun, part, extra, flow = call(
+                free, ins, [field] * 3 + [jax.ShapeDtypeStruct(turned, jnp.float32)], wide_room, work=300
+            )
             reach = 4
             while reach < size:
                 most = jnp.maximum(most, other)
                 most, part = lax.optimization_barrier((most, part))
                 other = spread(most, reach)
                 reach *= 2
-            part, x_near, x_far = lax.optimization_barrier((part, x_near, x_far))
+            part, x_far = lax.optimization_barrier((part, x_far))
         else:
             if section == 3:
                 values, x_near = lax.optimization_barrier((values, x_near))

time: 41.2 us -> 40.1 us (0.973)
  waiting for transfers between devices: 5.92 us -> 3.63 us
  starting transfers between devices: 19.9 us -> 20.8 us
    ppermute x12, waiting for transfers between devices: 4.34 us -> 1.94 us  [trade(): return lax.ppermute(value, axis, pairs)]
    ppermute x12, starting transfers between devices: 15.8 us -> 16.9 us  [trade(): return lax.ppermute(value, axis, pairs)]
  transfers between devices with their start and end apart: 15 -> 15, of which waited for: 7 -> 4; matrix products, arithmetic and copies ran while one was open for 0% -> 0% of each run, Pallas kernels for 28% -> 30%
where the time goes in v15:
time: 40.1 us; the launch traced here: 39.7 us
  starting transfers between devices  20.8 us (52%)
  Pallas kernels  13.4 us (33%)
  waiting for transfers between devices  3.63 us (9%)
  local copies, waits for them, and re-layouts  1.74 us (4%)
    ppermute x12, starting transfers between devices, trade(): return lax.ppermute(value, axis, pairs)  16.9 us
    pallas_call x15, Pallas kernels, call(): pl.pallas_call(kernel, out_shape=outs, in_specs=[vmem] * len(ins), out_sp...  13.4 us
    ppermute x3, starting transfers between devices, spread(): return lax.ppermute(most, 'gx', pairs)  3.9 us
    ppermute x12, waiting for transfers between devices, trade(): return lax.ppermute(value, axis, pairs)  1.94 us
    unnamed x14, local copies, waits for them, and re-layouts  1.74 us
    ppermute x3, waiting for transfers between devices, spread(): return lax.ppermute(most, 'gx', pairs)  1.68 us
  transfers between devices with their start and end apart: 15, of which 4 were waited for; matrix products, arithmetic and copies ran while one was open for 0% of the time, Pallas kernels for 30%

profile of v15, /device:TPU:8, one launch (start us, length us, event | category | flops | bytes accessed | tf_op | source)
XLA Modules:
  0.0 39.7 jit_solution(15975071854570851673)
XLA Ops:
  0.0 0.0 copy-start.3
  0.0 0.7 %copy-done.3 = f32[2,9,128]{2,0,1:T(2,128)S(1)} copy-done((f32[2,9,128]{2,0,1:T(2,128)S(1)}, f32[2,9,128]{2,0,1:T(2,128)}, u32[]{:S(2)}) %copy-start.3) | copy-done | bytes 9240
  0.7 1.6 %collective-permute-start = (f32[40,8,128]{2,1,0:T(8,128)S(1)}, f32[40,8,128]{2,1,0:T(8,128)S(1)}, u32[]{:S(2)}, u32[]{:S(2)}) collective-permute-start(f32[40,8,128]{2,1,0:T(8,128)S(1)} %shard_map.56.own_ref), channel_id=1, source_target_pairs={{0,1},{1,0},{2,3},{3,2},{4,5},{5,4},{6,7},{7,6},{8,9},{9,8},{10,11... | collective-permute-start | bytes 491528 | tf_op jit(solution)/shard_map/ppermute | solution.py:461
  2.3 0.0 copy-start
  2.3 1.0 %copy-done = f32[9,12,8,128]{3,2,1,0:T(8,128)S(1)} copy-done((f32[9,12,8,128]{3,2,1,0:T(8,128)S(1)}, f32[9,12,8,128]{3,2,1,0:T(8,128)}, u32[]{:S(2)}) %copy-start) | copy-done | bytes 442392
  3.3 0.0 copy-start.1
  3.3 2.1 %collective-permute-start.2 = (f32[39,8,128]{2,1,0:T(8,128)S(1)}, f32[39,8,128]{2,1,0:T(8,128)S(1)}, u32[]{:S(2)}, u32[]{:S(2)}) collective-permute-start(f32[39,8,128]{2,1,0:T(8,128)S(1)} %get-tuple-element.42), channel_id=1, source_target_pairs={{1,2},{3,4},{5,6},{2,1},{4,3},{6,5},{0,0},{7,7},{9,10},{11,12},{13... | collective-permute-start | bytes 479240 | tf_op jit(solution)/shard_map/ppermute | solution.py:398
  5.4 0.1 collective-permute-start.3
  5.5 2.0 %collective-permute-start.4 = (f32[37,8,128]{2,1,0:T(8,128)S(1)}, f32[37,8,128]{2,1,0:T(8,128)S(1)}, u32[]{:S(2)}, u32[]{:S(2)}) collective-permute-start(f32[37,8,128]{2,1,0:T(8,128)S(1)} %get-tuple-element.45), channel_id=1, source_target_pairs={{8,16},{24,0},{16,8},{0,24},{9,17},{25,1},{17,9},{1,25},{10,18},{2... | collective-permute-start | bytes 454664 | tf_op jit(solution)/shard_map/ppermute | solution.py:398
  7.5 0.0 copy-start.2
  7.5 0.0 copy-start.4
  7.5 2.6 %collective-permute-start.5 = (f32[38,8,128]{2,1,0:T(8,128)S(1)}, f32[38,8,128]{2,1,0:T(8,128)S(1)}, u32[]{:S(2)}, u32[]{:S(2)}) collective-permute-start(f32[38,8,128]{2,1,0:T(8,128)S(1)} %get-tuple-element.46), channel_id=1, source_target_pairs={{0,1},{2,3},{4,5},{6,7},{1,0},{3,2},{5,4},{7,6},{8,9},{10,11},{12,... | collective-permute-start | bytes 466952 | tf_op jit(solution)/shard_map/ppermute | solution.py:398
  10.1 0.0 collective-permute-done.other_ref
  10.1 0.5 %collective-permute-start.1 = (f32[8,128]{1,0:T(8,128)S(1)}, f32[8,128]{1,0:T(8,128)S(1)}, u32[]{:S(2)}, u32[]{:S(2)}) collective-permute-start(f32[8,128]{1,0:T(8,128)S(1)} %shard_map.57), channel_id=1, source_target_pairs={{0,2},{1,3},{2,0},{3,1},{4,6},{5,7},{6,4},{7,5},{8,10},{9,11},{10,... | collective-permute-start | bytes 12296 | tf_op jit(solution)/shard_map/ppermute | solution.py:461
  10.6 0.0 copy-done.1
  10.6 0.0 copy-done.2
  10.6 0.0 copy-done.4
  10.6 2.3 %shard_map.55 = (f32[9,12,8,128]{3,2,1,0:T(8,128)S(1)}, f32[9,12,8,128]{3,2,1,0:T(8,128)S(1)}, f32[9,12,8,128]{3,2,1,0:T(8,128)S(1)}, f32[7,128,128]{2,1,0:T(8,128)S(1)}) custom-call(f32[9,12,8,128]{3,2,1,0:T(8,128)S(1)} %copy-done.1, f32[9,2,128]{2,1,0:T(2,128)S(1)} %bitcast.2, f32[2,48,128]{2,1,0:T(8,128)S(1)} %copy-done.2), custom_call_target="tpu_custom_call" | custom-call | flops 33177600 | bytes 33177600 | tf_op jit(solution)/shard_map/pallas_call | solution.py:432
  12.9 0.8 %collective-permute-done.1 = f32[8,128]{1,0:T(8,128)S(1)} collective-permute-done((f32[8,128]{1,0:T(8,128)S(1)}, f32[8,128]{1,0:T(8,128)S(1)}, u32[]{:S(2)}, u32[]{:S(2)}) %collective-permute-start.1) | collective-permute-done | bytes 4128 | tf_op jit(solution)/shard_map/ppermute | solution.py:461
  13.7 0.0 collective-permute-done.2.far_ref
  13.7 1.9 %collective-permute-start.6 = (f32[8,128]{1,0:T(8,128)S(1)}, f32[8,128]{1,0:T(8,128)S(1)}, u32[]{:S(2)}, u32[]{:S(2)}) collective-permute-start(f32[8,128]{1,0:T(8,128)S(1)} %max.3.most_ref), channel_id=1, source_target_pairs={{0,4},{1,5},{2,6},{3,7},{4,0},{5,1},{6,2},{7,3},{8,12},{9,13},{10,... | collective-permute-start | bytes 12296 | tf_op jit(solution)/shard_map/ppermute | solution.py:461
  15.6 0.0 collective-permute-done.3.near_ref
  15.6 0.0 collective-permute-done.4.far_ref
  15.6 0.8 %shard_map.59.part_ref = f32[9,12,8,128]{3,2,1,0:T(8,128)S(1)} custom-call(f32[9,12,8,128]{3,2,1,0:T(8,128)S(1)} %copy-done.1, f32[9,12,8,128]{3,2,1,0:T(8,128)S(1)} %get-tuple-element.39.speed_ref, f32[9,12,8,128]{3,2,1,0:T(8,128)S(1)} %get-tuple-element.43.part_ref, f32[37,8,128]{2,1,0:T(8,128)S(1)} %collective-permute-done.3.near_ref, ...), custom_call_target="tpu_custom_call" | custom-call | flops 110592000 | bytes 110592000 | tf_op jit(solution)/shard_map/pallas_call | solution.py:432
  16.4 0.0 collective-permute-done.5.near_ref
  16.4 0.0 copy-start.5
  16.5 0.0 copy-start.6
  16.5 0.9 %shard_map.60 = (f32[9,12,8,128]{3,2,1,0:T(8,128)S(1)}, f32[9,12,8,128]{3,2,1,0:T(8,128)S(1)}) custom-call(f32[9,12,8,128]{3,2,1,0:T(8,128)S(1)} %copy-done.1, f32[9,12,8,128]{3,2,1,0:T(8,128)S(1)} %shard_map.59.part_ref, f32[38,8,128]{2,1,0:T(8,128)S(1)} %collective-permute-done.5.near_ref, f32[39,8,128]{2,1,0:T(8,128)S(1)} %collective-permute-done.2.far_ref, ...), custom_call_target="tpu_custom_call" | custom-call | tf_op jit(solution)/shard_map/pallas_call | solution.py:432
  17.4 0.9 %collective-permute-done.6.other_ref = f32[8,128]{1,0:T(8,128)S(1)} collective-permute-done((f32[8,128]{1,0:T(8,128)S(1)}, f32[8,128]{1,0:T(8,128)S(1)}, u32[]{:S(2)}, u32[]{:S(2)}) %collective-permute-start.6) | collective-permute-done | bytes 4128 | tf_op jit(solution)/shard_map/ppermute | solution.py:461
  18.3 0.0 copy-done.5
  18.3 0.0 copy-done.6
  18.3 0.4 shard_map.61
  18.7 0.1 collective-permute-start.7
  18.8 0.0 collective-permute-start.9
  18.8 4.1 %collective-permute-start.10 = (f32[36,8,128]{2,1,0:T(8,128)S(1)}, f32[36,8,128]{2,1,0:T(8,128)S(1)}, u32[]{:S(2)}, u32[]{:S(2)}) collective-permute-start(f32[36,8,128]{2,1,0:T(8,128)S(1)} %get-tuple-element.61), channel_id=1, source_target_pairs={{1,2},{3,4},{5,6},{2,1},{4,3},{6,5},{0,0},{7,7},{9,10},{11,12},{13... | collective-permute-start | bytes 442376 | tf_op jit(solution)/shard_map/ppermute | solution.py:398
  22.9 0.4 %collective-permute-start.8 = (f32[27,8,128]{2,1,0:T(8,128)S(1)}, f32[27,8,128]{2,1,0:T(8,128)S(1)}, u32[]{:S(2)}, u32[]{:S(2)}) collective-permute-start(f32[27,8,128]{2,1,0:T(8,128)S(1)} %get-tuple-element.59), channel_id=1, source_target_pairs={{0,8},{16,24},{8,0},{24,16},{1,9},{17,25},{9,1},{25,17},{2,10},{18... | collective-permute-start | bytes 331784 | tf_op jit(solution)/shard_map/ppermute | solution.py:398
  23.4 2.1 %shard_map.62 = (f32[9,12,8,128]{3,2,1,0:T(8,128)S(1)}, f32[9,12,8,128]{3,2,1,0:T(8,128)S(1)}) custom-call(f32[9,12,8,128]{3,2,1,0:T(8,128)S(1)} %get-tuple-element.52.s_ref, f32[7,128,128]{2,1,0:T(8,128)S(1)} %get-tuple-element.53.rest_0_, f32[8,128]{1,0:T(8,128)S(1)} %get-tuple-element.54.rest_1_.pk_ref), custom_call_target="tpu_custom_call" | custom-call | tf_op jit(solution)/shard_map/pallas_call | solution.py:432
  25.5 0.0 collective-permute-done.7.ghosts_ref
  25.5 0.0 collective-permute-done.8.near_ref
  25.5 0.0 collective-permute-done.9.far_ref
  25.5 0.8 %shard_map.63.part_ref = f32[9,12,8,128]{3,2,1,0:T(8,128)S(1)} custom-call(f32[9,12,8,128]{3,2,1,0:T(8,128)S(1)} %get-tuple-element.52.s_ref, f32[9,12,8,128]{3,2,1,0:T(8,128)S(1)} %get-tuple-element.55.speed_ref, f32[9,12,8,128]{3,2,1,0:T(8,128)S(1)} %get-tuple-element.58.part_ref, f32[27,8,128]{2,1,0:T(8,128)S(1)} %collective-permute-done.8.near_ref, ...), custom_call_target="tpu_custom_call" | custom-call | flops 110592000 | bytes 110592000 | tf_op jit(solution)/shard_map/pallas_call | solution.py:432
  26.4 0.7 %shard_map.64 = (f32[9,12,8,128]{3,2,1,0:T(8,128)S(1)}, f32[38,8,128]{2,1,0:T(8,128)S(1)}) custom-call(f32[9,12,8,128]{3,2,1,0:T(8,128)S(1)} %copy-done.1, f32[9,12,8,128]{3,2,1,0:T(8,128)S(1)} %get-tuple-element.52.s_ref, f32[9,12,8,128]{3,2,1,0:T(8,128)S(1)} %shard_map.63.part_ref, f32[38,8,128]{2,1,0:T(8,128)S(1)} %collective-permute-done.7.ghosts_ref, ...), custom_call_target="tpu_custom_call" | custom-call | tf_op jit(solution)/shard_map/pallas_call | solution.py:432
  27.1 0.9 %collective-permute-start.11 = (f32[38,8,128]{2,1,0:T(8,128)S(1)}, f32[38,8,128]{2,1,0:T(8,128)S(1)}, u32[]{:S(2)}, u32[]{:S(2)}) collective-permute-start(f32[38,8,128]{2,1,0:T(8,128)S(1)} %get-tuple-element.65), channel_id=1, source_target_pairs={{0,1},{2,3},{4,5},{6,7},{1,0},{3,2},{5,4},{7,6},{8,9},{10,11},{12,... | collective-permute-start | bytes 466952 | tf_op jit(solution)/shard_map/ppermute | solution.py:398
  28.0 0.0 collective-permute-done.10.ghosts_ref
  28.0 0.4 %shard_map.65 = (f32[9,12,8,128]{3,2,1,0:T(8,128)S(1)}, f32[36,8,128]{2,1,0:T(8,128)S(1)}, f32[27,8,128]{2,1,0:T(8,128)S(1)}, f32[37,8,128]{2,1,0:T(8,128)S(1)}) custom-call(f32[9,12,8,128]{3,2,1,0:T(8,128)S(1)} %copy-done.1, f32[9,12,8,128]{3,2,1,0:T(8,128)S(1)} %get-tuple-element.52.s_ref, f32[9,12,8,128]{3,2,1,0:T(8,128)S(1)} %shard_map.63.part_ref, ...), custom_call_target="tpu_custom_call" | custom-call | tf_op jit(solution)/shard_map/pallas_call | solution.py:432
  28.4 0.9 %collective-permute-start.13 = (f32[37,8,128]{2,1,0:T(8,128)S(1)}, f32[37,8,128]{2,1,0:T(8,128)S(1)}, u32[]{:S(2)}, u32[]{:S(2)}) collective-permute-start(f32[37,8,128]{2,1,0:T(8,128)S(1)} %get-tuple-element.70), channel_id=1, source_target_pairs={{8,16},{24,0},{16,8},{0,24},{9,17},{25,1},{17,9},{1,25},{10,18},{2... | collective-permute-start | bytes 454664 | tf_op jit(solution)/shard_map/ppermute | solution.py:398
  29.3 3.6 %collective-permute-start.14 = (f32[36,8,128]{2,1,0:T(8,128)S(1)}, f32[36,8,128]{2,1,0:T(8,128)S(1)}, u32[]{:S(2)}, u32[]{:S(2)}) collective-permute-start(f32[36,8,128]{2,1,0:T(8,128)S(1)} %get-tuple-element.71), channel_id=1, source_target_pairs={{1,2},{3,4},{5,6},{2,1},{4,3},{6,5},{0,0},{7,7},{9,10},{11,12},{13... | collective-permute-start | bytes 442376 | tf_op jit(solution)/shard_map/ppermute | solution.py:398
  32.9 0.1 collective-permute-start.12
  33.0 0.2 collective-permute-done.11.ghosts_ref
  33.2 2.1 %shard_map.66 = (f32[9,12,8,128]{3,2,1,0:T(8,128)S(1)}, f32[9,12,8,128]{3,2,1,0:T(8,128)S(1)}) custom-call(f32[9,12,8,128]{3,2,1,0:T(8,128)S(1)} %get-tuple-element.66.s_ref, f32[7,128,128]{2,1,0:T(8,128)S(1)} %get-tuple-element.53.rest_0_, f32[8,128]{1,0:T(8,128)S(1)} %get-tuple-element.54.rest_1_.pk_ref), custom_call_target="tpu_custom_call" | custom-call | tf_op jit(solution)/shard_map/pallas_call | solution.py:432
  35.4 0.0 collective-permute-done.12.near_ref
  35.4 0.0 collective-permute-done.13.far_ref
  35.4 0.8 %shard_map.67.part_ref = f32[9,12,8,128]{3,2,1,0:T(8,128)S(1)} custom-call(f32[9,12,8,128]{3,2,1,0:T(8,128)S(1)} %get-tuple-element.66.s_ref, f32[9,12,8,128]{3,2,1,0:T(8,128)S(1)} %get-tuple-element.67.speed_ref, f32[9,12,8,128]{3,2,1,0:T(8,128)S(1)} %get-tuple-element.68.part_ref, f32[27,8,128]{2,1,0:T(8,128)S(1)} %collective-permute-done.12.near_ref, ...), custom_call_target="tpu_custom_call" | custom-call | flops 110592000 | bytes 110592000 | tf_op jit(solution)/shard_map/pallas_call | solution.py:432
  36.2 0.7 %shard_map.68.refs_0_ = f32[9,12,8,128]{3,2,1,0:T(8,128)S(1)} custom-call(f32[9,12,8,128]{3,2,1,0:T(8,128)S(1)} %copy-done.1, f32[9,12,8,128]{3,2,1,0:T(8,128)S(1)} %get-tuple-element.66.s_ref, f32[9,12,8,128]{3,2,1,0:T(8,128)S(1)} %shard_map.67.part_ref, f32[38,8,128]{2,1,0:T(8,128)S(1)} %collective-permute-done.11.ghosts_ref, f32[9,2,128]{2,1,0:T(2,128)S(1)} %bitcast.6, ...), custom_call_target="tpu_custom_call" | custom-call | tf_op jit(solution)/shard_map/pallas_call | solution.py:432
  36.9 1.7 %collective-permute-done.14.ghosts_ref = f32[36,8,128]{2,1,0:T(8,128)S(1)} collective-permute-done((f32[36,8,128]{2,1,0:T(8,128)S(1)}, f32[36,8,128]{2,1,0:T(8,128)S(1)}, u32[]{:S(2)}, u32[]{:S(2)}) %collective-permute-start.14) | collective-permute-done | bytes 147488 | tf_op jit(solution)/shard_map/ppermute | solution.py:398
  38.6 1.1 %shard_map.69 = f32[9,12,8,128]{3,2,1,0:T(8,128)} custom-call(f32[9,12,8,128]{3,2,1,0:T(8,128)S(1)} %copy-done.1, f32[9,12,8,128]{3,2,1,0:T(8,128)S(1)} %get-tuple-element.66.s_ref, f32[9,12,8,128]{3,2,1,0:T(8,128)S(1)} %shard_map.67.part_ref, f32[36,8,128]{2,1,0:T(8,128)S(1)} %collective-permute-done.14.ghosts_ref, f32[9,2,128]{2,1,0:T(2,128)S(1)} %bitcast.7, ...), custom_call_target="tpu_custom_call" | custom-call | tf_op jit(solution)/shard_map/pallas_call | solution.py:432
  (4 shorter events, 0.1 us)
Async XLA Ops:
  0.0 0.7 %copy-start.3 = (f32[2,9,128]{2,0,1:T(2,128)S(1)}, f32[2,9,128]{2,0,1:T(2,128)}, u32[]{:S(2)}) copy-start(f32[2,9,128]{2,0,1:T(2,128)} %param.6) | copy-start | bytes 27652
  0.7 9.4 %collective-permute-start = (f32[40,8,128]{2,1,0:T(8,128)S(1)}, f32[40,8,128]{2,1,0:T(8,128)S(1)}, u32[]{:S(2)}, u32[]{:S(2)}) collective-permute-start(f32[40,8,128]{2,1,0:T(8,128)S(1)} %shard_map.56.own_ref), channel_id=1, source_target_pairs={{0,1},{1,0},{2,3},{3,2},{4,5},{5,4},{6,7},{7,6},{8,9},{9,8},{10,11... | collective-permute-start | bytes 491528 | tf_op jit(solution)/shard_map/ppermute | solution.py:461
  2.3 1.0 %copy-start = (f32[9,12,8,128]{3,2,1,0:T(8,128)S(1)}, f32[9,12,8,128]{3,2,1,0:T(8,128)}, u32[]{:S(2)}) copy-start(f32[9,12,8,128]{3,2,1,0:T(8,128)} %base_ref.7) | copy-start | bytes 1327108
  3.3 7.3 %copy-start.1 = (f32[9,12,8,128]{3,2,1,0:T(8,128)S(1)}, f32[9,12,8,128]{3,2,1,0:T(8,128)}, u32[]{:S(2)}) copy-start(f32[9,12,8,128]{3,2,1,0:T(8,128)} %base_ref.7) | copy-start | bytes 1327108
  3.3 10.4 %collective-permute-start.2 = (f32[39,8,128]{2,1,0:T(8,128)S(1)}, f32[39,8,128]{2,1,0:T(8,128)S(1)}, u32[]{:S(2)}, u32[]{:S(2)}) collective-permute-start(f32[39,8,128]{2,1,0:T(8,128)S(1)} %get-tuple-element.42), channel_id=1, source_target_pairs={{1,2},{3,4},{5,6},{2,1},{4,3},{6,5},{0,0},{7,7},{9,10},{11,12},{13... | collective-permute-start | bytes 479240 | tf_op jit(solution)/shard_map/ppermute | solution.py:398
  5.4 10.2 %collective-permute-start.3 = (f32[37,8,128]{2,1,0:T(8,128)S(1)}, f32[37,8,128]{2,1,0:T(8,128)S(1)}, u32[]{:S(2)}, u32[]{:S(2)}) collective-permute-start(f32[37,8,128]{2,1,0:T(8,128)S(1)} %get-tuple-element.44), channel_id=1, source_target_pairs={{0,8},{16,24},{8,0},{24,16},{1,9},{17,25},{9,1},{25,17},{2,10},{18... | collective-permute-start | bytes 454664 | tf_op jit(solution)/shard_map/ppermute | solution.py:398
  5.5 10.1 %collective-permute-start.4 = (f32[37,8,128]{2,1,0:T(8,128)S(1)}, f32[37,8,128]{2,1,0:T(8,128)S(1)}, u32[]{:S(2)}, u32[]{:S(2)}) collective-permute-start(f32[37,8,128]{2,1,0:T(8,128)S(1)} %get-tuple-element.45), channel_id=1, source_target_pairs={{8,16},{24,0},{16,8},{0,24},{9,17},{25,1},{17,9},{1,25},{10,18},{2... | collective-permute-start | bytes 454664 | tf_op jit(solution)/shard_map/ppermute | solution.py:398
  7.5 3.1 %copy-start.2 = (f32[2,48,128]{2,1,0:T(8,128)S(1)}, f32[2,48,128]{2,1,0:T(8,128)}, u32[]{:S(2)}) copy-start(f32[2,48,128]{2,1,0:T(8,128)} %constant.2.clone.rest_1_.waves_ref) | copy-start | bytes 147460
  7.5 3.1 %copy-start.4 = (f32[2,9,128]{2,0,1:T(2,128)S(1)}, f32[2,9,128]{2,0,1:T(2,128)}, u32[]{:S(2)}) copy-start(f32[2,9,128]{2,0,1:T(2,128)} %param.6) | copy-start | bytes 27652
  7.5 9.0 %collective-permute-start.5 = (f32[38,8,128]{2,1,0:T(8,128)S(1)}, f32[38,8,128]{2,1,0:T(8,128)S(1)}, u32[]{:S(2)}, u32[]{:S(2)}) collective-permute-start(f32[38,8,128]{2,1,0:T(8,128)S(1)} %get-tuple-element.46), channel_id=1, source_target_pairs={{0,1},{2,3},{4,5},{6,7},{1,0},{3,2},{5,4},{7,6},{8,9},{10,11},{12,... | collective-permute-start | bytes 466952 | tf_op jit(solution)/shard_map/ppermute | solution.py:398
  10.1 3.6 %collective-permute-start.1 = (f32[8,128]{1,0:T(8,128)S(1)}, f32[8,128]{1,0:T(8,128)S(1)}, u32[]{:S(2)}, u32[]{:S(2)}) collective-permute-start(f32[8,128]{1,0:T(8,128)S(1)} %shard_map.57), channel_id=1, source_target_pairs={{0,2},{1,3},{2,0},{3,1},{4,6},{5,7},{6,4},{7,5},{8,10},{9,11},{10,... | collective-permute-start | bytes 12296 | tf_op jit(solution)/shard_map/ppermute | solution.py:461
  13.7 4.5 %collective-permute-start.6 = (f32[8,128]{1,0:T(8,128)S(1)}, f32[8,128]{1,0:T(8,128)S(1)}, u32[]{:S(2)}, u32[]{:S(2)}) collective-permute-start(f32[8,128]{1,0:T(8,128)S(1)} %max.3.most_ref), channel_id=1, source_target_pairs={{0,4},{1,5},{2,6},{3,7},{4,0},{5,1},{6,2},{7,3},{8,12},{9,13},{10,... | collective-permute-start | bytes 12296 | tf_op jit(solution)/shard_map/ppermute | solution.py:461
  16.4 1.8 %copy-start.5 = (s32[9,128]{1,0:T(8,128)S(1)}, s32[9,128]{1,0:T(8,128)}, u32[]{:S(2)}) copy-start(s32[9,128]{1,0:T(8,128)} %mask_ref.9) | copy-start | bytes 13828
  16.5 1.8 %copy-start.6 = (f32[9,128]{1,0:T(8,128)S(1)}, f32[9,128]{1,0:T(8,128)}, u32[]{:S(2)}) copy-start(f32[9,128]{1,0:T(8,128)} %depth_ref.9) | copy-start | bytes 13828
  18.7 6.9 %collective-permute-start.7 = (f32[38,8,128]{2,1,0:T(8,128)S(1)}, f32[38,8,128]{2,1,0:T(8,128)S(1)}, u32[]{:S(2)}, u32[]{:S(2)}) collective-permute-start(f32[38,8,128]{2,1,0:T(8,128)S(1)} %get-tuple-element.57), channel_id=1, source_target_pairs={{0,1},{2,3},{4,5},{6,7},{1,0},{3,2},{5,4},{7,6},{8,9},{10,11},{12,... | collective-permute-start | bytes 466952 | tf_op jit(solution)/shard_map/ppermute | solution.py:398
  18.8 6.7 %collective-permute-start.9 = (f32[37,8,128]{2,1,0:T(8,128)S(1)}, f32[37,8,128]{2,1,0:T(8,128)S(1)}, u32[]{:S(2)}, u32[]{:S(2)}) collective-permute-start(f32[37,8,128]{2,1,0:T(8,128)S(1)} %get-tuple-element.60), channel_id=1, source_target_pairs={{8,16},{24,0},{16,8},{0,24},{9,17},{25,1},{17,9},{1,25},{10,18},{2... | collective-permute-start | bytes 454664 | tf_op jit(solution)/shard_map/ppermute | solution.py:398
  18.8 9.2 %collective-permute-start.10 = (f32[36,8,128]{2,1,0:T(8,128)S(1)}, f32[36,8,128]{2,1,0:T(8,128)S(1)}, u32[]{:S(2)}, u32[]{:S(2)}) collective-permute-start(f32[36,8,128]{2,1,0:T(8,128)S(1)} %get-tuple-element.61), channel_id=1, source_target_pairs={{1,2},{3,4},{5,6},{2,1},{4,3},{6,5},{0,0},{7,7},{9,10},{11,12},{13... | collective-permute-start | bytes 442376 | tf_op jit(solution)/shard_map/ppermute | solution.py:398
  22.9 2.6 %collective-permute-start.8 = (f32[27,8,128]{2,1,0:T(8,128)S(1)}, f32[27,8,128]{2,1,0:T(8,128)S(1)}, u32[]{:S(2)}, u32[]{:S(2)}) collective-permute-start(f32[27,8,128]{2,1,0:T(8,128)S(1)} %get-tuple-element.59), channel_id=1, source_target_pairs={{0,8},{16,24},{8,0},{24,16},{1,9},{17,25},{9,1},{25,17},{2,10},{18... | collective-permute-start | bytes 331784 | tf_op jit(solution)/shard_map/ppermute | solution.py:398
  27.1 6.1 %collective-permute-start.11 = (f32[38,8,128]{2,1,0:T(8,128)S(1)}, f32[38,8,128]{2,1,0:T(8,128)S(1)}, u32[]{:S(2)}, u32[]{:S(2)}) collective-permute-start(f32[38,8,128]{2,1,0:T(8,128)S(1)} %get-tuple-element.65), channel_id=1, source_target_pairs={{0,1},{2,3},{4,5},{6,7},{1,0},{3,2},{5,4},{7,6},{8,9},{10,11},{12,... | collective-permute-start | bytes 466952 | tf_op jit(solution)/shard_map/ppermute | solution.py:398
  28.4 7.0 %collective-permute-start.13 = (f32[37,8,128]{2,1,0:T(8,128)S(1)}, f32[37,8,128]{2,1,0:T(8,128)S(1)}, u32[]{:S(2)}, u32[]{:S(2)}) collective-permute-start(f32[37,8,128]{2,1,0:T(8,128)S(1)} %get-tuple-element.70), channel_id=1, source_target_pairs={{8,16},{24,0},{16,8},{0,24},{9,17},{25,1},{17,9},{1,25},{10,18},{2... | collective-permute-start | bytes 454664 | tf_op jit(solution)/shard_map/ppermute | solution.py:398
  29.3 9.3 %collective-permute-start.14 = (f32[36,8,128]{2,1,0:T(8,128)S(1)}, f32[36,8,128]{2,1,0:T(8,128)S(1)}, u32[]{:S(2)}, u32[]{:S(2)}) collective-permute-start(f32[36,8,128]{2,1,0:T(8,128)S(1)} %get-tuple-element.71), channel_id=1, source_target_pairs={{1,2},{3,4},{5,6},{2,1},{4,3},{6,5},{0,0},{7,7},{9,10},{11,12},{13... | collective-permute-start | bytes 442376 | tf_op jit(solution)/shard_map/ppermute | solution.py:398
  32.9 2.5 %collective-permute-start.12 = (f32[27,8,128]{2,1,0:T(8,128)S(1)}, f32[27,8,128]{2,1,0:T(8,128)S(1)}, u32[]{:S(2)}, u32[]{:S(2)}) collective-permute-start(f32[27,8,128]{2,1,0:T(8,128)S(1)} %get-tuple-element.69), channel_id=1, source_target_pairs={{0,8},{16,24},{8,0},{24,16},{1,9},{17,25},{9,1},{25,17},{2,10},{18... | collective-permute-start | bytes 331784 | tf_op jit(solution)/shard_map/ppermute | solution.py:398

commit v16 on v15

--- a/solution.py
+++ b/solution.py
@@ -157,14 +157,14 @@
     lines = width // high
 
     def along_speed(n):
-        start = jnp.minimum(n * few, cells - few) * speeds
+        start = min(n * few, cells - few) * speeds
         spots = [pl.ds(start + v, few, stride=speeds) for v in range(speeds)]
         rows = [s_rows[spot, :] for spot in spots]
         for spot, (mean, gap) in zip(spots, row_terms(rows, speed_step, True)):
             speed_rows[spot, :] = gain_v * (gap - jnp.abs(mean))
 
     def span(n):
-        return pl.ds(pl.multiple_of(jnp.minimum(n * many, cells - many) * speeds, speeds), lanes)
+        return pl.ds(min(n * many, cells - many) * speeds, lanes)
 
     def turn_in(n):
         turned = s_rows[span(n), :].T
@@ -191,16 +191,16 @@
         if split:
             extra_rows[span(n), :] = gap_ref[n].T
 
-    def step(n, carry):
-        turn_out(jnp.maximum(n - 1, 0))
+    turn_in(0)
+    for n in range(groups):
+        if n > 0:
+            turn_out(n - 1)
         along_y(n)
-        turn_in(jnp.minimum(n + 1, groups - 1))
-        along_speed(2 * n)
-        along_speed(2 * n + 1)
-        return carry
-
-    turn_in(0)
-    lax.fori_loop(0, groups, step, 0)
+        if n + 1 < groups:
+            turn_in(n + 1)
+        for k in (2 * n, 2 * n + 1):
+            if k * few < cells:
+                along_speed(k)
     turn_out(groups - 1)
 
 
@@ -295,7 +295,7 @@
     pace = speeds_of(tile, speed_step) * side
     first = lax.axis_index("head") * headings
     low, high = span
-    wide = batches(headings, max(1, 54 // (high - low)))
+    wide = batches(headings, max(1, 72 // (high - low)))
 
     def line(i, j):
         if i < 0:
@@ -462,7 +462,7 @@
 
     (most,) = call(extremes_kernel, [wind], [shape(longest + 2)])
     other = spread(most, 1)
-    x_shapes = [shape(longest), shape(longest + 1)]
+    x_shapes = [shape(longest + 1), shape(longest)]
     x_out, x_last, t_out, t_last = call(opening_kernel, [values], x_shapes + [shape(middle)] * 2)
     far_shapes = [shape(short), shape(rim * planes), shape(middle)]
     for section in (1, 2, 3):
@@ -486,14 +486,14 @@
                 most, part = lax.optimization_barrier((most, part))
                 other = spread(most, reach)
                 reach *= 2
-            part, x_far = lax.optimization_barrier((part, x_far))
         else:
             if section == 3:
                 values, x_near = lax.optimization_barrier((values, x_near))
             spun, part = call(free, [values, flow, pk], [field] * 2, room)
             if section == 2:
                 part, x_near = lax.optimization_barrier((part, x_near))
-        (part,) = call(turning, [values, spun, part, t_near, t_far], [field], work=1000)
+        weight = 0 if opening else 1000
+        (part,) = call(turning, [values, spun, part, t_near, t_far], [field], work=weight)
         if opening:
             ins = [values, part, x_near, x_far, wind, waves]
             first = functools.partial(first_kernel, speed_step)

time: 40.1 us -> 40.2 us (level)
  waiting for transfers between devices: 3.63 us -> 4.91 us
  starting transfers between devices: 20.8 us -> 20.2 us
  Pallas kernels: 13.4 us -> 12.8 us
    ppermute x12, waiting for transfers between devices: 1.94 us -> 3.36 us  [trade(): return lax.ppermute(value, axis, pairs)]
    ppermute x12, starting transfers between devices: 16.9 us -> 16.1 us  [trade(): return lax.ppermute(value, axis, pairs)]
    pallas_call x15, Pallas kernels: 13.4 us -> 12.8 us  [call(): pl.pallas_call(kernel, out_shape=outs, in_specs=[vmem] * len(ins), out_sp...]
  transfers between devices with their start and end apart: 15 -> 15, of which waited for: 4 -> 7; matrix products, arithmetic and copies ran while one was open for 0% -> 0% of each run, Pallas kernels for 30% -> 28%
where the time goes in v16:
time: 40.2 us; the launch traced here: 39.9 us
  starting transfers between devices  20.2 us (50%)
  Pallas kernels  12.8 us (32%)
  waiting for transfers between devices  4.91 us (12%)
  local copies, waits for them, and re-layouts  1.74 us (4%)
    ppermute x12, starting transfers between devices, trade(): return lax.ppermute(value, axis, pairs)  16.1 us
    pallas_call x15, Pallas kernels, call(): pl.pallas_call(kernel, out_shape=outs, in_specs=[vmem] * len(ins), out_sp...  12.8 us
    ppermute x3, starting transfers between devices, spread(): return lax.ppermute(most, 'gx', pairs)  4.17 us
    ppermute x12, waiting for transfers between devices, trade(): return lax.ppermute(value, axis, pairs)  3.36 us
    unnamed x14, local copies, waits for them, and re-layouts  1.74 us
    ppermute x3, waiting for transfers between devices, spread(): return lax.ppermute(most, 'gx', pairs)  1.55 us
  transfers between devices with their start and end apart: 15, of which 7 were waited for; matrix products, arithmetic and copies ran while one was open for 0% of the time, Pallas kernels for 28%

profile of v16, /device:TPU:8, one launch (start us, length us, event | category | flops | bytes accessed | tf_op | source)
XLA Modules:
  0.0 39.9 jit_solution(11500447809795533364)
XLA Ops:
  0.0 0.0 copy-start.3
  0.0 0.7 %copy-done.3 = f32[2,9,128]{2,0,1:T(2,128)S(1)} copy-done((f32[2,9,128]{2,0,1:T(2,128)S(1)}, f32[2,9,128]{2,0,1:T(2,128)}, u32[]{:S(2)}) %copy-start.3) | copy-done | bytes 9240
  0.7 1.6 %collective-permute-start = (f32[40,8,128]{2,1,0:T(8,128)S(1)}, f32[40,8,128]{2,1,0:T(8,128)S(1)}, u32[]{:S(2)}, u32[]{:S(2)}) collective-permute-start(f32[40,8,128]{2,1,0:T(8,128)S(1)} %shard_map.56.own_ref), channel_id=1, source_target_pairs={{0,1},{1,0},{2,3},{3,2},{4,5},{5,4},{6,7},{7,6},{8,9},{9,8},{10,11... | collective-permute-start | bytes 491528 | tf_op jit(solution)/shard_map/ppermute | solution.py:461
  2.3 0.0 copy-start
  2.3 1.0 %copy-done = f32[9,12,8,128]{3,2,1,0:T(8,128)S(1)} copy-done((f32[9,12,8,128]{3,2,1,0:T(8,128)S(1)}, f32[9,12,8,128]{3,2,1,0:T(8,128)}, u32[]{:S(2)}) %copy-start) | copy-done | bytes 442392
  3.3 0.0 copy-start.1
  3.3 0.6 %collective-permute-start.4 = (f32[39,8,128]{2,1,0:T(8,128)S(1)}, f32[39,8,128]{2,1,0:T(8,128)S(1)}, u32[]{:S(2)}, u32[]{:S(2)}) collective-permute-start(f32[39,8,128]{2,1,0:T(8,128)S(1)} %get-tuple-element.42), channel_id=1, source_target_pairs={{0,1},{2,3},{4,5},{6,7},{1,0},{3,2},{5,4},{7,6},{8,9},{10,11},{12,... | collective-permute-start | bytes 479240 | tf_op jit(solution)/shard_map/ppermute | solution.py:398
  3.9 3.3 %collective-permute-start.5 = (f32[38,8,128]{2,1,0:T(8,128)S(1)}, f32[38,8,128]{2,1,0:T(8,128)S(1)}, u32[]{:S(2)}, u32[]{:S(2)}) collective-permute-start(f32[38,8,128]{2,1,0:T(8,128)S(1)} %get-tuple-element.43), channel_id=1, source_target_pairs={{1,2},{3,4},{5,6},{2,1},{4,3},{6,5},{0,0},{7,7},{9,10},{11,12},{13... | collective-permute-start | bytes 466952 | tf_op jit(solution)/shard_map/ppermute | solution.py:398
  7.2 0.1 collective-permute-start.2
  7.3 0.0 copy-start.2
  7.3 0.0 copy-start.4
  7.3 1.6 %collective-permute-start.3 = (f32[37,8,128]{2,1,0:T(8,128)S(1)}, f32[37,8,128]{2,1,0:T(8,128)S(1)}, u32[]{:S(2)}, u32[]{:S(2)}) collective-permute-start(f32[37,8,128]{2,1,0:T(8,128)S(1)} %get-tuple-element.41), channel_id=1, source_target_pairs={{8,16},{24,0},{16,8},{0,24},{9,17},{25,1},{17,9},{1,25},{10,18},{2... | collective-permute-start | bytes 454664 | tf_op jit(solution)/shard_map/ppermute | solution.py:398
  8.9 0.0 collective-permute-done.other_ref
  8.9 0.0 collective-permute-start.1
  8.9 0.0 copy-done.1
  8.9 0.0 copy-done.2
  9.0 0.0 copy-done.4
  9.0 2.2 %shard_map.55 = (f32[9,12,8,128]{3,2,1,0:T(8,128)S(1)}, f32[9,12,8,128]{3,2,1,0:T(8,128)S(1)}, f32[9,12,8,128]{3,2,1,0:T(8,128)S(1)}, f32[7,128,128]{2,1,0:T(8,128)S(1)}) custom-call(f32[9,12,8,128]{3,2,1,0:T(8,128)S(1)} %copy-done.1, f32[9,2,128]{2,1,0:T(2,128)S(1)} %bitcast.2, f32[2,48,128]{2,1,0:T(8,128)S(1)} %copy-done.2), custom_call_target="tpu_custom_call" | custom-call | flops 33177600 | bytes 33177600 | tf_op jit(solution)/shard_map/pallas_call | solution.py:432
  11.1 1.4 %collective-permute-done.1 = f32[8,128]{1,0:T(8,128)S(1)} collective-permute-done((f32[8,128]{1,0:T(8,128)S(1)}, f32[8,128]{1,0:T(8,128)S(1)}, u32[]{:S(2)}, u32[]{:S(2)}) %collective-permute-start.1) | collective-permute-done | bytes 4128 | tf_op jit(solution)/shard_map/ppermute | solution.py:461
  12.5 2.6 %collective-permute-start.6 = (f32[8,128]{1,0:T(8,128)S(1)}, f32[8,128]{1,0:T(8,128)S(1)}, u32[]{:S(2)}, u32[]{:S(2)}) collective-permute-start(f32[8,128]{1,0:T(8,128)S(1)} %max.3.most_ref), channel_id=1, source_target_pairs={{0,4},{1,5},{2,6},{3,7},{4,0},{5,1},{6,2},{7,3},{8,12},{9,13},{10,... | collective-permute-start | bytes 12296 | tf_op jit(solution)/shard_map/ppermute | solution.py:461
  15.1 0.0 collective-permute-done.2.near_ref
  15.1 0.0 collective-permute-done.3.far_ref
  15.1 0.8 %shard_map.59.part_ref = f32[9,12,8,128]{3,2,1,0:T(8,128)S(1)} custom-call(f32[9,12,8,128]{3,2,1,0:T(8,128)S(1)} %copy-done.1, f32[9,12,8,128]{3,2,1,0:T(8,128)S(1)} %get-tuple-element.37.speed_ref, f32[9,12,8,128]{3,2,1,0:T(8,128)S(1)} %get-tuple-element.39.part_ref, f32[37,8,128]{2,1,0:T(8,128)S(1)} %collective-permute-done.2.near_ref, ...), custom_call_target="tpu_custom_call" | custom-call | tf_op jit(solution)/shard_map/pallas_call | solution.py:432
  15.9 0.0 collective-permute-done.5.far_ref
  16.0 0.0 collective-permute-done.4.near_ref
  16.0 0.0 copy-start.5
  16.0 0.0 copy-start.6
  16.0 0.9 %shard_map.60 = (f32[9,12,8,128]{3,2,1,0:T(8,128)S(1)}, f32[9,12,8,128]{3,2,1,0:T(8,128)S(1)}) custom-call(f32[9,12,8,128]{3,2,1,0:T(8,128)S(1)} %copy-done.1, f32[9,12,8,128]{3,2,1,0:T(8,128)S(1)} %shard_map.59.part_ref, f32[39,8,128]{2,1,0:T(8,128)S(1)} %collective-permute-done.4.near_ref, f32[38,8,128]{2,1,0:T(8,128)S(1)} %collective-permute-done.5.far_ref, ...), custom_call_target="tpu_custom_call" | custom-call | tf_op jit(solution)/shard_map/pallas_call | solution.py:432
  16.9 0.1 collective-permute-done.6.other_ref
  17.0 0.0 copy-done.5
  17.0 0.0 copy-done.6
  17.1 0.4 shard_map.61
  17.4 1.7 %collective-permute-start.7 = (f32[38,8,128]{2,1,0:T(8,128)S(1)}, f32[38,8,128]{2,1,0:T(8,128)S(1)}, u32[]{:S(2)}, u32[]{:S(2)}) collective-permute-start(f32[38,8,128]{2,1,0:T(8,128)S(1)} %get-tuple-element.53), channel_id=1, source_target_pairs={{0,1},{2,3},{4,5},{6,7},{1,0},{3,2},{5,4},{7,6},{8,9},{10,11},{12,... | collective-permute-start | bytes 466952 | tf_op jit(solution)/shard_map/ppermute | solution.py:398
  19.1 0.0 collective-permute-start.9
  19.1 2.4 %collective-permute-start.10 = (f32[36,8,128]{2,1,0:T(8,128)S(1)}, f32[36,8,128]{2,1,0:T(8,128)S(1)}, u32[]{:S(2)}, u32[]{:S(2)}) collective-permute-start(f32[36,8,128]{2,1,0:T(8,128)S(1)} %get-tuple-element.57), channel_id=1, source_target_pairs={{1,2},{3,4},{5,6},{2,1},{4,3},{6,5},{0,0},{7,7},{9,10},{11,12},{13... | collective-permute-start | bytes 442376 | tf_op jit(solution)/shard_map/ppermute | solution.py:398
  21.6 0.7 %collective-permute-start.8 = (f32[27,8,128]{2,1,0:T(8,128)S(1)}, f32[27,8,128]{2,1,0:T(8,128)S(1)}, u32[]{:S(2)}, u32[]{:S(2)}) collective-permute-start(f32[27,8,128]{2,1,0:T(8,128)S(1)} %get-tuple-element.55), channel_id=1, source_target_pairs={{0,8},{16,24},{8,0},{24,16},{1,9},{17,25},{9,1},{25,17},{2,10},{18... | collective-permute-start | bytes 331784 | tf_op jit(solution)/shard_map/ppermute | solution.py:398
  22.3 2.0 %shard_map.62 = (f32[9,12,8,128]{3,2,1,0:T(8,128)S(1)}, f32[9,12,8,128]{3,2,1,0:T(8,128)S(1)}) custom-call(f32[9,12,8,128]{3,2,1,0:T(8,128)S(1)} %get-tuple-element.48.s_ref, f32[7,128,128]{2,1,0:T(8,128)S(1)} %get-tuple-element.49.rest_0_, f32[8,128]{1,0:T(8,128)S(1)} %get-tuple-element.50.rest_1_.pk_ref), custom_call_target="tpu_custom_call" | custom-call | tf_op jit(solution)/shard_map/pallas_call | solution.py:432
  24.3 0.0 collective-permute-done.7.ghosts_ref
  24.3 0.0 collective-permute-done.8.near_ref
  24.3 0.2 collective-permute-done.9.far_ref
  24.5 0.8 %shard_map.63.part_ref = f32[9,12,8,128]{3,2,1,0:T(8,128)S(1)} custom-call(f32[9,12,8,128]{3,2,1,0:T(8,128)S(1)} %get-tuple-element.48.s_ref, f32[9,12,8,128]{3,2,1,0:T(8,128)S(1)} %get-tuple-element.51.speed_ref, f32[9,12,8,128]{3,2,1,0:T(8,128)S(1)} %get-tuple-element.54.part_ref, f32[27,8,128]{2,1,0:T(8,128)S(1)} %collective-permute-done.8.near_ref, ...), custom_call_target="tpu_custom_call" | custom-call | flops 110592000 | bytes 110592000 | tf_op jit(solution)/shard_map/pallas_call | solution.py:432
  25.3 0.7 %shard_map.64 = (f32[9,12,8,128]{3,2,1,0:T(8,128)S(1)}, f32[38,8,128]{2,1,0:T(8,128)S(1)}) custom-call(f32[9,12,8,128]{3,2,1,0:T(8,128)S(1)} %copy-done.1, f32[9,12,8,128]{3,2,1,0:T(8,128)S(1)} %get-tuple-element.48.s_ref, f32[9,12,8,128]{3,2,1,0:T(8,128)S(1)} %shard_map.63.part_ref, f32[38,8,128]{2,1,0:T(8,128)S(1)} %collective-permute-done.7.ghosts_ref, ...), custom_call_target="tpu_custom_call" | custom-call | tf_op jit(solution)/shard_map/pallas_call | solution.py:432
  25.9 2.1 %collective-permute-start.11 = (f32[38,8,128]{2,1,0:T(8,128)S(1)}, f32[38,8,128]{2,1,0:T(8,128)S(1)}, u32[]{:S(2)}, u32[]{:S(2)}) collective-permute-start(f32[38,8,128]{2,1,0:T(8,128)S(1)} %get-tuple-element.61), channel_id=1, source_target_pairs={{0,1},{2,3},{4,5},{6,7},{1,0},{3,2},{5,4},{7,6},{8,9},{10,11},{12,... | collective-permute-start | bytes 466952 | tf_op jit(solution)/shard_map/ppermute | solution.py:398
  28.1 0.2 collective-permute-done.10.ghosts_ref
  28.3 0.4 %shard_map.65 = (f32[9,12,8,128]{3,2,1,0:T(8,128)S(1)}, f32[36,8,128]{2,1,0:T(8,128)S(1)}, f32[27,8,128]{2,1,0:T(8,128)S(1)}, f32[37,8,128]{2,1,0:T(8,128)S(1)}) custom-call(f32[9,12,8,128]{3,2,1,0:T(8,128)S(1)} %copy-done.1, f32[9,12,8,128]{3,2,1,0:T(8,128)S(1)} %get-tuple-element.48.s_ref, f32[9,12,8,128]{3,2,1,0:T(8,128)S(1)} %shard_map.63.part_ref, ...), custom_call_target="tpu_custom_call" | custom-call | tf_op jit(solution)/shard_map/pallas_call | solution.py:432
  28.7 0.7 %collective-permute-start.13 = (f32[37,8,128]{2,1,0:T(8,128)S(1)}, f32[37,8,128]{2,1,0:T(8,128)S(1)}, u32[]{:S(2)}, u32[]{:S(2)}) collective-permute-start(f32[37,8,128]{2,1,0:T(8,128)S(1)} %get-tuple-element.66), channel_id=1, source_target_pairs={{8,16},{24,0},{16,8},{0,24},{9,17},{25,1},{17,9},{1,25},{10,18},{2... | collective-permute-start | bytes 454664 | tf_op jit(solution)/shard_map/ppermute | solution.py:398
  29.4 2.6 %collective-permute-start.14 = (f32[36,8,128]{2,1,0:T(8,128)S(1)}, f32[36,8,128]{2,1,0:T(8,128)S(1)}, u32[]{:S(2)}, u32[]{:S(2)}) collective-permute-start(f32[36,8,128]{2,1,0:T(8,128)S(1)} %get-tuple-element.67), channel_id=1, source_target_pairs={{1,2},{3,4},{5,6},{2,1},{4,3},{6,5},{0,0},{7,7},{9,10},{11,12},{13... | collective-permute-start | bytes 442376 | tf_op jit(solution)/shard_map/ppermute | solution.py:398
  32.0 0.4 collective-permute-start.12
  32.3 0.1 collective-permute-done.11.ghosts_ref
  32.4 2.0 %shard_map.66 = (f32[9,12,8,128]{3,2,1,0:T(8,128)S(1)}, f32[9,12,8,128]{3,2,1,0:T(8,128)S(1)}) custom-call(f32[9,12,8,128]{3,2,1,0:T(8,128)S(1)} %get-tuple-element.62.s_ref, f32[7,128,128]{2,1,0:T(8,128)S(1)} %get-tuple-element.49.rest_0_, f32[8,128]{1,0:T(8,128)S(1)} %get-tuple-element.50.rest_1_.pk_ref), custom_call_target="tpu_custom_call" | custom-call | tf_op jit(solution)/shard_map/pallas_call | solution.py:432
  34.4 0.0 collective-permute-done.12.near_ref
  34.4 0.6 %collective-permute-done.13.far_ref = f32[37,8,128]{2,1,0:T(8,128)S(1)} collective-permute-done((f32[37,8,128]{2,1,0:T(8,128)S(1)}, f32[37,8,128]{2,1,0:T(8,128)S(1)}, u32[]{:S(2)}, u32[]{:S(2)}) %collective-permute-start.13) | collective-permute-done | bytes 151584 | tf_op jit(solution)/shard_map/ppermute | solution.py:398
  35.0 0.8 %shard_map.67.part_ref = f32[9,12,8,128]{3,2,1,0:T(8,128)S(1)} custom-call(f32[9,12,8,128]{3,2,1,0:T(8,128)S(1)} %get-tuple-element.62.s_ref, f32[9,12,8,128]{3,2,1,0:T(8,128)S(1)} %get-tuple-element.63.speed_ref, f32[9,12,8,128]{3,2,1,0:T(8,128)S(1)} %get-tuple-element.64.part_ref, f32[27,8,128]{2,1,0:T(8,128)S(1)} %collective-permute-done.12.near_ref, ...), custom_call_target="tpu_custom_call" | custom-call | flops 110592000 | bytes 110592000 | tf_op jit(solution)/shard_map/pallas_call | solution.py:432
  35.8 0.7 %shard_map.68.refs_0_ = f32[9,12,8,128]{3,2,1,0:T(8,128)S(1)} custom-call(f32[9,12,8,128]{3,2,1,0:T(8,128)S(1)} %copy-done.1, f32[9,12,8,128]{3,2,1,0:T(8,128)S(1)} %get-tuple-element.62.s_ref, f32[9,12,8,128]{3,2,1,0:T(8,128)S(1)} %shard_map.67.part_ref, f32[38,8,128]{2,1,0:T(8,128)S(1)} %collective-permute-done.11.ghosts_ref, f32[9,2,128]{2,1,0:T(2,128)S(1)} %bitcast.6, ...), custom_call_target="tpu_custom_call" | custom-call | tf_op jit(solution)/shard_map/pallas_call | solution.py:432
  36.5 2.2 %collective-permute-done.14.ghosts_ref = f32[36,8,128]{2,1,0:T(8,128)S(1)} collective-permute-done((f32[36,8,128]{2,1,0:T(8,128)S(1)}, f32[36,8,128]{2,1,0:T(8,128)S(1)}, u32[]{:S(2)}, u32[]{:S(2)}) %collective-permute-start.14) | collective-permute-done | bytes 147488 | tf_op jit(solution)/shard_map/ppermute | solution.py:398
  38.7 1.1 %shard_map.69 = f32[9,12,8,128]{3,2,1,0:T(8,128)} custom-call(f32[9,12,8,128]{3,2,1,0:T(8,128)S(1)} %copy-done.1, f32[9,12,8,128]{3,2,1,0:T(8,128)S(1)} %get-tuple-element.62.s_ref, f32[9,12,8,128]{3,2,1,0:T(8,128)S(1)} %shard_map.67.part_ref, f32[36,8,128]{2,1,0:T(8,128)S(1)} %collective-permute-done.14.ghosts_ref, f32[9,2,128]{2,1,0:T(2,128)S(1)} %bitcast.7, ...), custom_call_target="tpu_custom_call" | custom-call | tf_op jit(solution)/shard_map/pallas_call | solution.py:432
  (4 shorter events, 0.1 us)
Async XLA Ops:
  0.0 0.7 %copy-start.3 = (f32[2,9,128]{2,0,1:T(2,128)S(1)}, f32[2,9,128]{2,0,1:T(2,128)}, u32[]{:S(2)}) copy-start(f32[2,9,128]{2,0,1:T(2,128)} %param.6) | copy-start | bytes 27652
  0.7 8.2 %collective-permute-start = (f32[40,8,128]{2,1,0:T(8,128)S(1)}, f32[40,8,128]{2,1,0:T(8,128)S(1)}, u32[]{:S(2)}, u32[]{:S(2)}) collective-permute-start(f32[40,8,128]{2,1,0:T(8,128)S(1)} %shard_map.56.own_ref), channel_id=1, source_target_pairs={{0,1},{1,0},{2,3},{3,2},{4,5},{5,4},{6,7},{7,6},{8,9},{9,8},{10,11... | collective-permute-start | bytes 491528 | tf_op jit(solution)/shard_map/ppermute | solution.py:461
  2.3 1.0 %copy-start = (f32[9,12,8,128]{3,2,1,0:T(8,128)S(1)}, f32[9,12,8,128]{3,2,1,0:T(8,128)}, u32[]{:S(2)}) copy-start(f32[9,12,8,128]{3,2,1,0:T(8,128)} %base_ref.7) | copy-start | bytes 1327108
  3.3 5.6 %copy-start.1 = (f32[9,12,8,128]{3,2,1,0:T(8,128)S(1)}, f32[9,12,8,128]{3,2,1,0:T(8,128)}, u32[]{:S(2)}) copy-start(f32[9,12,8,128]{3,2,1,0:T(8,128)} %base_ref.7) | copy-start | bytes 1327108
  3.3 12.6 %collective-permute-start.4 = (f32[39,8,128]{2,1,0:T(8,128)S(1)}, f32[39,8,128]{2,1,0:T(8,128)S(1)}, u32[]{:S(2)}, u32[]{:S(2)}) collective-permute-start(f32[39,8,128]{2,1,0:T(8,128)S(1)} %get-tuple-element.42), channel_id=1, source_target_pairs={{0,1},{2,3},{4,5},{6,7},{1,0},{3,2},{5,4},{7,6},{8,9},{10,11},{12,... | collective-permute-start | bytes 479240 | tf_op jit(solution)/shard_map/ppermute | solution.py:398
  3.9 12.0 %collective-permute-start.5 = (f32[38,8,128]{2,1,0:T(8,128)S(1)}, f32[38,8,128]{2,1,0:T(8,128)S(1)}, u32[]{:S(2)}, u32[]{:S(2)}) collective-permute-start(f32[38,8,128]{2,1,0:T(8,128)S(1)} %get-tuple-element.43), channel_id=1, source_target_pairs={{1,2},{3,4},{5,6},{2,1},{4,3},{6,5},{0,0},{7,7},{9,10},{11,12},{13... | collective-permute-start | bytes 466952 | tf_op jit(solution)/shard_map/ppermute | solution.py:398
  7.2 7.9 %collective-permute-start.2 = (f32[37,8,128]{2,1,0:T(8,128)S(1)}, f32[37,8,128]{2,1,0:T(8,128)S(1)}, u32[]{:S(2)}, u32[]{:S(2)}) collective-permute-start(f32[37,8,128]{2,1,0:T(8,128)S(1)} %get-tuple-element.40), channel_id=1, source_target_pairs={{0,8},{16,24},{8,0},{24,16},{1,9},{17,25},{9,1},{25,17},{2,10},{18... | collective-permute-start | bytes 454664 | tf_op jit(solution)/shard_map/ppermute | solution.py:398
  7.3 1.6 %copy-start.2 = (f32[2,48,128]{2,1,0:T(8,128)S(1)}, f32[2,48,128]{2,1,0:T(8,128)}, u32[]{:S(2)}) copy-start(f32[2,48,128]{2,1,0:T(8,128)} %constant.2.clone.rest_1_.waves_ref) | copy-start | bytes 147460
  7.3 1.6 %copy-start.4 = (f32[2,9,128]{2,0,1:T(2,128)S(1)}, f32[2,9,128]{2,0,1:T(2,128)}, u32[]{:S(2)}) copy-start(f32[2,9,128]{2,0,1:T(2,128)} %param.6) | copy-start | bytes 27652
  7.3 7.8 %collective-permute-start.3 = (f32[37,8,128]{2,1,0:T(8,128)S(1)}, f32[37,8,128]{2,1,0:T(8,128)S(1)}, u32[]{:S(2)}, u32[]{:S(2)}) collective-permute-start(f32[37,8,128]{2,1,0:T(8,128)S(1)} %get-tuple-element.41), channel_id=1, source_target_pairs={{8,16},{24,0},{16,8},{0,24},{9,17},{25,1},{17,9},{1,25},{10,18},{2... | collective-permute-start | bytes 454664 | tf_op jit(solution)/shard_map/ppermute | solution.py:398
  8.9 3.6 %collective-permute-start.1 = (f32[8,128]{1,0:T(8,128)S(1)}, f32[8,128]{1,0:T(8,128)S(1)}, u32[]{:S(2)}, u32[]{:S(2)}) collective-permute-start(f32[8,128]{1,0:T(8,128)S(1)} %shard_map.57), channel_id=1, source_target_pairs={{0,2},{1,3},{2,0},{3,1},{4,6},{5,7},{6,4},{7,5},{8,10},{9,11},{10,... | collective-permute-start | bytes 12296 | tf_op jit(solution)/shard_map/ppermute | solution.py:461
  12.5 4.5 %collective-permute-start.6 = (f32[8,128]{1,0:T(8,128)S(1)}, f32[8,128]{1,0:T(8,128)S(1)}, u32[]{:S(2)}, u32[]{:S(2)}) collective-permute-start(f32[8,128]{1,0:T(8,128)S(1)} %max.3.most_ref), channel_id=1, source_target_pairs={{0,4},{1,5},{2,6},{3,7},{4,0},{5,1},{6,2},{7,3},{8,12},{9,13},{10,... | collective-permute-start | bytes 12296 | tf_op jit(solution)/shard_map/ppermute | solution.py:461
  16.0 1.1 %copy-start.5 = (s32[9,128]{1,0:T(8,128)S(1)}, s32[9,128]{1,0:T(8,128)}, u32[]{:S(2)}) copy-start(s32[9,128]{1,0:T(8,128)} %mask_ref.9) | copy-start | bytes 13828
  16.0 1.1 %copy-start.6 = (f32[9,128]{1,0:T(8,128)S(1)}, f32[9,128]{1,0:T(8,128)}, u32[]{:S(2)}) copy-start(f32[9,128]{1,0:T(8,128)} %depth_ref.9) | copy-start | bytes 13828
  17.4 6.8 %collective-permute-start.7 = (f32[38,8,128]{2,1,0:T(8,128)S(1)}, f32[38,8,128]{2,1,0:T(8,128)S(1)}, u32[]{:S(2)}, u32[]{:S(2)}) collective-permute-start(f32[38,8,128]{2,1,0:T(8,128)S(1)} %get-tuple-element.53), channel_id=1, source_target_pairs={{0,1},{2,3},{4,5},{6,7},{1,0},{3,2},{5,4},{7,6},{8,9},{10,11},{12,... | collective-permute-start | bytes 466952 | tf_op jit(solution)/shard_map/ppermute | solution.py:398
  19.1 5.3 %collective-permute-start.9 = (f32[37,8,128]{2,1,0:T(8,128)S(1)}, f32[37,8,128]{2,1,0:T(8,128)S(1)}, u32[]{:S(2)}, u32[]{:S(2)}) collective-permute-start(f32[37,8,128]{2,1,0:T(8,128)S(1)} %get-tuple-element.56), channel_id=1, source_target_pairs={{8,16},{24,0},{16,8},{0,24},{9,17},{25,1},{17,9},{1,25},{10,18},{2... | collective-permute-start | bytes 454664 | tf_op jit(solution)/shard_map/ppermute | solution.py:398
  19.1 9.2 %collective-permute-start.10 = (f32[36,8,128]{2,1,0:T(8,128)S(1)}, f32[36,8,128]{2,1,0:T(8,128)S(1)}, u32[]{:S(2)}, u32[]{:S(2)}) collective-permute-start(f32[36,8,128]{2,1,0:T(8,128)S(1)} %get-tuple-element.57), channel_id=1, source_target_pairs={{1,2},{3,4},{5,6},{2,1},{4,3},{6,5},{0,0},{7,7},{9,10},{11,12},{13... | collective-permute-start | bytes 442376 | tf_op jit(solution)/shard_map/ppermute | solution.py:398
  21.6 2.7 %collective-permute-start.8 = (f32[27,8,128]{2,1,0:T(8,128)S(1)}, f32[27,8,128]{2,1,0:T(8,128)S(1)}, u32[]{:S(2)}, u32[]{:S(2)}) collective-permute-start(f32[27,8,128]{2,1,0:T(8,128)S(1)} %get-tuple-element.55), channel_id=1, source_target_pairs={{0,8},{16,24},{8,0},{24,16},{1,9},{17,25},{9,1},{25,17},{2,10},{18... | collective-permute-start | bytes 331784 | tf_op jit(solution)/shard_map/ppermute | solution.py:398
  25.9 6.5 %collective-permute-start.11 = (f32[38,8,128]{2,1,0:T(8,128)S(1)}, f32[38,8,128]{2,1,0:T(8,128)S(1)}, u32[]{:S(2)}, u32[]{:S(2)}) collective-permute-start(f32[38,8,128]{2,1,0:T(8,128)S(1)} %get-tuple-element.61), channel_id=1, source_target_pairs={{0,1},{2,3},{4,5},{6,7},{1,0},{3,2},{5,4},{7,6},{8,9},{10,11},{12,... | collective-permute-start | bytes 466952 | tf_op jit(solution)/shard_map/ppermute | solution.py:398
  28.7 6.3 %collective-permute-start.13 = (f32[37,8,128]{2,1,0:T(8,128)S(1)}, f32[37,8,128]{2,1,0:T(8,128)S(1)}, u32[]{:S(2)}, u32[]{:S(2)}) collective-permute-start(f32[37,8,128]{2,1,0:T(8,128)S(1)} %get-tuple-element.66), channel_id=1, source_target_pairs={{8,16},{24,0},{16,8},{0,24},{9,17},{25,1},{17,9},{1,25},{10,18},{2... | collective-permute-start | bytes 454664 | tf_op jit(solution)/shard_map/ppermute | solution.py:398
  29.4 9.3 %collective-permute-start.14 = (f32[36,8,128]{2,1,0:T(8,128)S(1)}, f32[36,8,128]{2,1,0:T(8,128)S(1)}, u32[]{:S(2)}, u32[]{:S(2)}) collective-permute-start(f32[36,8,128]{2,1,0:T(8,128)S(1)} %get-tuple-element.67), channel_id=1, source_target_pairs={{1,2},{3,4},{5,6},{2,1},{4,3},{6,5},{0,0},{7,7},{9,10},{11,12},{13... | collective-permute-start | bytes 442376 | tf_op jit(solution)/shard_map/ppermute | solution.py:398
  32.0 2.4 %collective-permute-start.12 = (f32[27,8,128]{2,1,0:T(8,128)S(1)}, f32[27,8,128]{2,1,0:T(8,128)S(1)}, u32[]{:S(2)}, u32[]{:S(2)}) collective-permute-start(f32[27,8,128]{2,1,0:T(8,128)S(1)} %get-tuple-element.65), channel_id=1, source_target_pairs={{0,8},{16,24},{8,0},{24,16},{1,9},{17,25},{9,1},{25,17},{2,10},{18... | collective-permute-start | bytes 331784 | tf_op jit(solution)/shard_map/ppermute | solution.py:398

commit v17 on v16

--- a/solution.py
+++ b/solution.py
@@ -107,16 +107,14 @@
 
 def extremes_kernel(wind_ref, most_ref):
     put_extremes(wind_ref, most_ref.at[0])
+    for g in range(1, most_ref.shape[0]):
+        most_ref[g] = most_ref[0]
 
 
 def opening_kernel(level_ref, x_near, x_far, t_near, t_far):
     cut_near(level_ref, x_near)
     cut_far(level_ref, x_far)
     cut_headings(level_ref, t_near, t_far)
-
-
-def meeting_kernel(own_ref, other_ref, most_ref):
-    most_ref[...] = jnp.maximum(own_ref[0], other_ref[0])
 
 
 def flows_into(flow_ref, speed_step, wind_ref, waves_ref):
@@ -331,11 +329,11 @@
 
 def closing_kernel(
     bounds, heading_step, speed_step, s_ref, part_ref, gap_x_ref, gap_y_ref, mask_ref, depth_ref,
-    most_ref, other_ref, out_ref, x_near, x_far, t_near, t_far, pk_ref, target_ref
+    most_ref, out_ref, x_near, x_far, t_near, t_far, pk_ref, target_ref
 ):
     planes, headings = s_ref.shape[:2]
     tile = s_ref.shape[2:]
-    most = jnp.maximum(most_ref[...], other_ref[...])
+    most = functools.reduce(jnp.maximum, [most_ref[g] for g in range(most_ref.shape[0])])
     peaks_into(pk_ref, most, bounds, heading_step, speed_step)
     splat_targets(mask_ref, depth_ref, target_ref)
     peak_x = splat(pk_ref[0:1, :] * gain, tile)
@@ -451,17 +449,8 @@
     ]
     wide_room = room + [pltpu.VMEM(turned, jnp.float32), pltpu.VMEM(level_set.shape, jnp.float32)]
     values = level_set
-    size = lax.axis_size("gx")
-
-    def spread(most, reach):
-        if size & (size - 1):
-            pairs = [(i, (i + reach) % size) for i in range(size)]
-        else:
-            pairs = [(i, i ^ reach) for i in range(size)]
-        return lax.ppermute(most, "gx", pairs)
-
-    (most,) = call(extremes_kernel, [wind], [shape(longest + 2)])
-    other = spread(most, 1)
+    (most,) = call(extremes_kernel, [wind], [shape(lax.axis_size("gx"))])
+    most = lax.all_to_all(most, "gx", 0, 0)
     x_shapes = [shape(longest + 1), shape(longest)]
     x_out, x_last, t_out, t_last = call(opening_kernel, [values], x_shapes + [shape(middle)] * 2)
     far_shapes = [shape(short), shape(rim * planes), shape(middle)]
@@ -474,18 +463,10 @@
         free = functools.partial(free_kernel, opening, speed_step)
         turning = functools.partial(heading_kernel, heading_step)
         if opening:
-            (most,) = call(meeting_kernel, [most, other], [shape()])
-            other = spread(most, 2)
             ins = [values, wind, waves]
             spun, part, extra, flow = call(
                 free, ins, [field] * 3 + [jax.ShapeDtypeStruct(turned, jnp.float32)], wide_room, work=300
             )
-            reach = 4
-            while reach < size:
-                most = jnp.maximum(most, other)
-                most, part = lax.optimization_barrier((most, part))
-                other = spread(most, reach)
-                reach *= 2
         else:
             if section == 3:
                 values, x_near = lax.optimization_barrier((values, x_near))
@@ -499,7 +480,7 @@
             first = functools.partial(first_kernel, speed_step)
             part, gap = call(first, ins, [field] * 2, [rows])
             closing = functools.partial(closing_kernel, bounds, heading_step, speed_step)
-            ins = [values, part, gap, extra, target_mask, target_depth, most, other]
+            ins = [values, part, gap, extra, target_mask, target_depth, most]
             outs = [field, shape(longest), *far_shapes, shape()]
             values, x_out, x_last, t_out, t_last, pk = call(closing, ins, outs, [rows])
         else:

time: 40.2 us -> 41.2 us (1.025)
  the two profiles are of different devices: /device:TPU:8 before, /device:TPU:7 now
where the time goes in v17:
time: 41.2 us; the launch traced here: 40.9 us
  starting transfers between devices  21.9 us (53%)
  Pallas kernels  13.4 us (33%)
  waiting for transfers between devices  4.36 us (11%)
  local copies, waits for them, and re-layouts  1.04 us (3%)
    ppermute x12, starting transfers between devices, trade(): return lax.ppermute(value, axis, pairs)  17.2 us
    pallas_call x14, Pallas kernels, call(): pl.pallas_call(kernel, out_shape=outs, in_specs=[vmem] * len(ins), out_sp...  13.4 us
    all_to_all x1, starting transfers between devices, local(): most = lax.all_to_all(most, 'gx', 0, 0)  4.76 us
    ppermute x12, waiting for transfers between devices, trade(): return lax.ppermute(value, axis, pairs)  4.05 us
    unnamed x12, local copies, waits for them, and re-layouts  1.04 us
  transfers between devices with their start and end apart: 13, of which 4 were waited for; matrix products, arithmetic and copies ran while one was open for 0% of the time, Pallas kernels for 29%

profile of v17, /device:TPU:7, one launch (start us, length us, event | category | flops | bytes accessed | tf_op | source)
XLA Modules:
  0.0 40.9 jit_solution(12019426815295392899)
XLA Ops:
  0.0 0.0 copy-start
  0.0 1.0 %copy-done = f32[9,12,8,128]{3,2,1,0:T(8,128)S(1)} copy-done((f32[9,12,8,128]{3,2,1,0:T(8,128)S(1)}, f32[9,12,8,128]{3,2,1,0:T(8,128)}, u32[]{:S(2)}) %copy-start) | copy-done | bytes 442392
  1.0 0.0 copy-start.1
  1.1 0.0 copy-start.3
  1.1 0.3 collective-permute-start.2
  1.4 4.1 %collective-permute-start.3 = (f32[38,8,128]{2,1,0:T(8,128)S(1)}, f32[38,8,128]{2,1,0:T(8,128)S(1)}, u32[]{:S(2)}, u32[]{:S(2)}) collective-permute-start(f32[38,8,128]{2,1,0:T(8,128)S(1)} %get-tuple-element.40), channel_id=1, source_target_pairs={{1,2},{3,4},{5,6},{2,1},{4,3},{6,5},{0,0},{7,7},{9,10},{11,12},{13... | collective-permute-start | bytes 466952 | tf_op jit(solution)/shard_map/ppermute | solution.py:396
  5.5 1.3 %collective-permute-start = (f32[37,8,128]{2,1,0:T(8,128)S(1)}, f32[37,8,128]{2,1,0:T(8,128)S(1)}, u32[]{:S(2)}, u32[]{:S(2)}) collective-permute-start(f32[37,8,128]{2,1,0:T(8,128)S(1)} %get-tuple-element.37), channel_id=1, source_target_pairs={{0,8},{16,24},{8,0},{24,16},{1,9},{17,25},{9,1},{25,17},{2,10},{18... | collective-permute-start | bytes 454664 | tf_op jit(solution)/shard_map/ppermute | solution.py:396
  6.8 0.2 collective-permute-start.1
  7.0 0.0 copy-done.3
  7.0 0.0 copy-start.2
  7.0 0.6 %shard_map.59 = f32[8,8,128]{2,1,0:T(8,128)} custom-call(f32[9,2,128]{2,1,0:T(2,128)S(1)} %bitcast.1), custom_call_target="tpu_custom_call" | custom-call | tf_op jit(solution)/shard_map/pallas_call | solution.py:430
  7.7 4.8 %all-to-all-start = ((f32[8,8,128]{2,1,0:T(8,128)}), f32[8,8,128]{2,1,0:T(8,128)S(1)}, u32[]{:S(2)}, u32[]{:S(2)}) async-start(f32[8,8,128]{2,1,0:T(8,128)} %shard_map.59), calls=%async_computation | async-start | bytes 65536 | tf_op jit(solution)/shard_map/all_to_all | solution.py:453
  12.4 0.0 copy-done.1
  12.4 0.0 copy-done.2
  12.4 2.2 %shard_map.55 = (f32[9,12,8,128]{3,2,1,0:T(8,128)S(1)}, f32[9,12,8,128]{3,2,1,0:T(8,128)S(1)}, f32[9,12,8,128]{3,2,1,0:T(8,128)S(1)}, f32[7,128,128]{2,1,0:T(8,128)S(1)}) custom-call(f32[9,12,8,128]{3,2,1,0:T(8,128)S(1)} %copy-done.1, f32[9,2,128]{2,1,0:T(2,128)S(1)} %bitcast.2, f32[2,48,128]{2,1,0:T(8,128)S(1)} %copy-done.2), custom_call_target="tpu_custom_call" | custom-call | flops 33177600 | bytes 33177600 | tf_op jit(solution)/shard_map/pallas_call | solution.py:430
  14.6 0.0 collective-permute-done.near_ref
  14.6 0.0 collective-permute-done.1.far_ref
  14.6 0.8 %shard_map.57.part_ref = f32[9,12,8,128]{3,2,1,0:T(8,128)S(1)} custom-call(f32[9,12,8,128]{3,2,1,0:T(8,128)S(1)} %copy-done.1, f32[9,12,8,128]{3,2,1,0:T(8,128)S(1)} %get-tuple-element.35.speed_ref, f32[9,12,8,128]{3,2,1,0:T(8,128)S(1)} %get-tuple-element.36.part_ref, f32[37,8,128]{2,1,0:T(8,128)S(1)} %collective-permute-done.near_ref, ...), custom_call_target="tpu_custom_call" | custom-call | tf_op jit(solution)/shard_map/pallas_call | solution.py:430
  15.4 0.0 collective-permute-done.3.far_ref
  15.5 0.0 collective-permute-done.2.near_ref
  15.5 0.0 copy-start.4
  15.5 0.0 copy-start.5
  15.5 0.9 %shard_map.58 = (f32[9,12,8,128]{3,2,1,0:T(8,128)S(1)}, f32[9,12,8,128]{3,2,1,0:T(8,128)S(1)}) custom-call(f32[9,12,8,128]{3,2,1,0:T(8,128)S(1)} %copy-done.1, f32[9,12,8,128]{3,2,1,0:T(8,128)S(1)} %shard_map.57.part_ref, f32[39,8,128]{2,1,0:T(8,128)S(1)} %collective-permute-done.2.near_ref, f32[38,8,128]{2,1,0:T(8,128)S(1)} %collective-permute-done.3.far_ref, ...), custom_call_target="tpu_custom_call" | custom-call | tf_op jit(solution)/shard_map/pallas_call | solution.py:430
  16.4 0.3 all-to-all-done.most_ref
  16.7 0.0 copy-done.4
  16.7 0.0 copy-done.5
  16.7 0.4 shard_map.60
  17.1 1.3 %collective-permute-start.4 = (f32[38,8,128]{2,1,0:T(8,128)S(1)}, f32[38,8,128]{2,1,0:T(8,128)S(1)}, u32[]{:S(2)}, u32[]{:S(2)}) collective-permute-start(f32[38,8,128]{2,1,0:T(8,128)S(1)} %get-tuple-element.49), channel_id=1, source_target_pairs={{0,1},{2,3},{4,5},{6,7},{1,0},{3,2},{5,4},{7,6},{8,9},{10,11},{12,... | collective-permute-start | bytes 466952 | tf_op jit(solution)/shard_map/ppermute | solution.py:396
  18.4 3.3 %collective-permute-start.6 = (f32[37,8,128]{2,1,0:T(8,128)S(1)}, f32[37,8,128]{2,1,0:T(8,128)S(1)}, u32[]{:S(2)}, u32[]{:S(2)}) collective-permute-start(f32[37,8,128]{2,1,0:T(8,128)S(1)} %get-tuple-element.52), channel_id=1, source_target_pairs={{8,16},{24,0},{16,8},{0,24},{9,17},{25,1},{17,9},{1,25},{10,18},{2... | collective-permute-start | bytes 454664 | tf_op jit(solution)/shard_map/ppermute | solution.py:396
  21.7 2.2 %collective-permute-start.7 = (f32[36,8,128]{2,1,0:T(8,128)S(1)}, f32[36,8,128]{2,1,0:T(8,128)S(1)}, u32[]{:S(2)}, u32[]{:S(2)}) collective-permute-start(f32[36,8,128]{2,1,0:T(8,128)S(1)} %get-tuple-element.53), channel_id=1, source_target_pairs={{1,2},{3,4},{5,6},{2,1},{4,3},{6,5},{0,0},{7,7},{9,10},{11,12},{13... | collective-permute-start | bytes 442376 | tf_op jit(solution)/shard_map/ppermute | solution.py:396
  23.9 0.1 collective-permute-start.5
  24.0 2.0 %shard_map.61 = (f32[9,12,8,128]{3,2,1,0:T(8,128)S(1)}, f32[9,12,8,128]{3,2,1,0:T(8,128)S(1)}) custom-call(f32[9,12,8,128]{3,2,1,0:T(8,128)S(1)} %get-tuple-element.44.s_ref, f32[7,128,128]{2,1,0:T(8,128)S(1)} %get-tuple-element.45.rest_0_, f32[8,128]{1,0:T(8,128)S(1)} %get-tuple-element.46.rest_1_.pk_ref), custom_call_target="tpu_custom_call" | custom-call | tf_op jit(solution)/shard_map/pallas_call | solution.py:430
  26.0 0.0 collective-permute-done.4.ghosts_ref
  26.0 0.0 collective-permute-done.5.near_ref
  26.0 0.4 collective-permute-done.6.far_ref
  26.4 0.8 %shard_map.62.part_ref = f32[9,12,8,128]{3,2,1,0:T(8,128)S(1)} custom-call(f32[9,12,8,128]{3,2,1,0:T(8,128)S(1)} %get-tuple-element.44.s_ref, f32[9,12,8,128]{3,2,1,0:T(8,128)S(1)} %get-tuple-element.47.speed_ref, f32[9,12,8,128]{3,2,1,0:T(8,128)S(1)} %get-tuple-element.50.part_ref, f32[27,8,128]{2,1,0:T(8,128)S(1)} %collective-permute-done.5.near_ref, ...), custom_call_target="tpu_custom_call" | custom-call | flops 110592000 | bytes 110592000 | tf_op jit(solution)/shard_map/pallas_call | solution.py:430
  27.2 0.7 %shard_map.63 = (f32[9,12,8,128]{3,2,1,0:T(8,128)S(1)}, f32[38,8,128]{2,1,0:T(8,128)S(1)}) custom-call(f32[9,12,8,128]{3,2,1,0:T(8,128)S(1)} %copy-done.1, f32[9,12,8,128]{3,2,1,0:T(8,128)S(1)} %get-tuple-element.44.s_ref, f32[9,12,8,128]{3,2,1,0:T(8,128)S(1)} %shard_map.62.part_ref, f32[38,8,128]{2,1,0:T(8,128)S(1)} %collective-permute-done.4.ghosts_ref, ...), custom_call_target="tpu_custom_call" | custom-call | tf_op jit(solution)/shard_map/pallas_call | solution.py:430
  27.9 0.3 collective-permute-start.8
  28.1 1.3 %collective-permute-done.7.ghosts_ref = f32[36,8,128]{2,1,0:T(8,128)S(1)} collective-permute-done((f32[36,8,128]{2,1,0:T(8,128)S(1)}, f32[36,8,128]{2,1,0:T(8,128)S(1)}, u32[]{:S(2)}, u32[]{:S(2)}) %collective-permute-start.7) | collective-permute-done | bytes 147488 | tf_op jit(solution)/shard_map/ppermute | solution.py:396
  29.4 0.4 %shard_map.64 = (f32[9,12,8,128]{3,2,1,0:T(8,128)S(1)}, f32[36,8,128]{2,1,0:T(8,128)S(1)}, f32[27,8,128]{2,1,0:T(8,128)S(1)}, f32[37,8,128]{2,1,0:T(8,128)S(1)}) custom-call(f32[9,12,8,128]{3,2,1,0:T(8,128)S(1)} %copy-done.1, f32[9,12,8,128]{3,2,1,0:T(8,128)S(1)} %get-tuple-element.44.s_ref, f32[9,12,8,128]{3,2,1,0:T(8,128)S(1)} %shard_map.62.part_ref, ...), custom_call_target="tpu_custom_call" | custom-call | tf_op jit(solution)/shard_map/pallas_call | solution.py:430
  29.8 1.5 %collective-permute-start.10 = (f32[37,8,128]{2,1,0:T(8,128)S(1)}, f32[37,8,128]{2,1,0:T(8,128)S(1)}, u32[]{:S(2)}, u32[]{:S(2)}) collective-permute-start(f32[37,8,128]{2,1,0:T(8,128)S(1)} %get-tuple-element.62), channel_id=1, source_target_pairs={{8,16},{24,0},{16,8},{0,24},{9,17},{25,1},{17,9},{1,25},{10,18},{2... | collective-permute-start | bytes 454664 | tf_op jit(solution)/shard_map/ppermute | solution.py:396
  31.4 2.4 %collective-permute-start.11 = (f32[36,8,128]{2,1,0:T(8,128)S(1)}, f32[36,8,128]{2,1,0:T(8,128)S(1)}, u32[]{:S(2)}, u32[]{:S(2)}) collective-permute-start(f32[36,8,128]{2,1,0:T(8,128)S(1)} %get-tuple-element.63), channel_id=1, source_target_pairs={{1,2},{3,4},{5,6},{2,1},{4,3},{6,5},{0,0},{7,7},{9,10},{11,12},{13... | collective-permute-start | bytes 442376 | tf_op jit(solution)/shard_map/ppermute | solution.py:396
  33.8 0.1 collective-permute-start.9
  33.9 0.0 collective-permute-done.8.ghosts_ref
  33.9 2.0 %shard_map.65 = (f32[9,12,8,128]{3,2,1,0:T(8,128)S(1)}, f32[9,12,8,128]{3,2,1,0:T(8,128)S(1)}) custom-call(f32[9,12,8,128]{3,2,1,0:T(8,128)S(1)} %get-tuple-element.58.s_ref, f32[7,128,128]{2,1,0:T(8,128)S(1)} %get-tuple-element.45.rest_0_, f32[8,128]{1,0:T(8,128)S(1)} %get-tuple-element.46.rest_1_.pk_ref), custom_call_target="tpu_custom_call" | custom-call | tf_op jit(solution)/shard_map/pallas_call | solution.py:430
  35.9 0.0 collective-permute-done.9.near_ref
  35.9 0.0 collective-permute-done.10.far_ref
  35.9 0.8 %shard_map.66.part_ref = f32[9,12,8,128]{3,2,1,0:T(8,128)S(1)} custom-call(f32[9,12,8,128]{3,2,1,0:T(8,128)S(1)} %get-tuple-element.58.s_ref, f32[9,12,8,128]{3,2,1,0:T(8,128)S(1)} %get-tuple-element.59.speed_ref, f32[9,12,8,128]{3,2,1,0:T(8,128)S(1)} %get-tuple-element.60.part_ref, f32[27,8,128]{2,1,0:T(8,128)S(1)} %collective-permute-done.9.near_ref, ...), custom_call_target="tpu_custom_call" | custom-call | flops 110592000 | bytes 110592000 | tf_op jit(solution)/shard_map/pallas_call | solution.py:430
  36.7 0.7 %shard_map.67.refs_0_ = f32[9,12,8,128]{3,2,1,0:T(8,128)S(1)} custom-call(f32[9,12,8,128]{3,2,1,0:T(8,128)S(1)} %copy-done.1, f32[9,12,8,128]{3,2,1,0:T(8,128)S(1)} %get-tuple-element.58.s_ref, f32[9,12,8,128]{3,2,1,0:T(8,128)S(1)} %shard_map.66.part_ref, f32[38,8,128]{2,1,0:T(8,128)S(1)} %collective-permute-done.8.ghosts_ref, f32[9,2,128]{2,1,0:T(2,128)S(1)} %bitcast.6, ...), custom_call_target="tpu_custom_call" | custom-call | tf_op jit(solution)/shard_map/pallas_call | solution.py:430
  37.4 2.4 %collective-permute-done.11.ghosts_ref = f32[36,8,128]{2,1,0:T(8,128)S(1)} collective-permute-done((f32[36,8,128]{2,1,0:T(8,128)S(1)}, f32[36,8,128]{2,1,0:T(8,128)S(1)}, u32[]{:S(2)}, u32[]{:S(2)}) %collective-permute-start.11) | collective-permute-done | bytes 147488 | tf_op jit(solution)/shard_map/ppermute | solution.py:396
  39.8 1.1 %shard_map.68 = f32[9,12,8,128]{3,2,1,0:T(8,128)} custom-call(f32[9,12,8,128]{3,2,1,0:T(8,128)S(1)} %copy-done.1, f32[9,12,8,128]{3,2,1,0:T(8,128)S(1)} %get-tuple-element.58.s_ref, f32[9,12,8,128]{3,2,1,0:T(8,128)S(1)} %shard_map.66.part_ref, f32[36,8,128]{2,1,0:T(8,128)S(1)} %collective-permute-done.11.ghosts_ref, f32[9,2,128]{2,1,0:T(2,128)S(1)} %bitcast.7, ...), custom_call_target="tpu_custom_call" | custom-call | tf_op jit(solution)/shard_map/pallas_call | solution.py:430
  (1 shorter events, 0.0 us)
Async XLA Ops:
  0.0 1.0 %copy-start = (f32[9,12,8,128]{3,2,1,0:T(8,128)S(1)}, f32[9,12,8,128]{3,2,1,0:T(8,128)}, u32[]{:S(2)}) copy-start(f32[9,12,8,128]{3,2,1,0:T(8,128)} %base_ref.7) | copy-start | bytes 1327108
  1.0 11.4 %copy-start.1 = (f32[9,12,8,128]{3,2,1,0:T(8,128)S(1)}, f32[9,12,8,128]{3,2,1,0:T(8,128)}, u32[]{:S(2)}) copy-start(f32[9,12,8,128]{3,2,1,0:T(8,128)} %base_ref.7) | copy-start | bytes 1327108
  1.1 6.0 %copy-start.3 = (f32[2,9,128]{2,0,1:T(2,128)S(1)}, f32[2,9,128]{2,0,1:T(2,128)}, u32[]{:S(2)}) copy-start(f32[2,9,128]{2,0,1:T(2,128)} %param.6) | copy-start | bytes 27652
  1.1 14.4 %collective-permute-start.2 = (f32[39,8,128]{2,1,0:T(8,128)S(1)}, f32[39,8,128]{2,1,0:T(8,128)S(1)}, u32[]{:S(2)}, u32[]{:S(2)}) collective-permute-start(f32[39,8,128]{2,1,0:T(8,128)S(1)} %get-tuple-element.39), channel_id=1, source_target_pairs={{0,1},{2,3},{4,5},{6,7},{1,0},{3,2},{5,4},{7,6},{8,9},{10,11},{12,... | collective-permute-start | bytes 479240 | tf_op jit(solution)/shard_map/ppermute | solution.py:396
  1.4 14.1 %collective-permute-start.3 = (f32[38,8,128]{2,1,0:T(8,128)S(1)}, f32[38,8,128]{2,1,0:T(8,128)S(1)}, u32[]{:S(2)}, u32[]{:S(2)}) collective-permute-start(f32[38,8,128]{2,1,0:T(8,128)S(1)} %get-tuple-element.40), channel_id=1, source_target_pairs={{1,2},{3,4},{5,6},{2,1},{4,3},{6,5},{0,0},{7,7},{9,10},{11,12},{13... | collective-permute-start | bytes 466952 | tf_op jit(solution)/shard_map/ppermute | solution.py:396
  5.5 9.1 %collective-permute-start = (f32[37,8,128]{2,1,0:T(8,128)S(1)}, f32[37,8,128]{2,1,0:T(8,128)S(1)}, u32[]{:S(2)}, u32[]{:S(2)}) collective-permute-start(f32[37,8,128]{2,1,0:T(8,128)S(1)} %get-tuple-element.37), channel_id=1, source_target_pairs={{0,8},{16,24},{8,0},{24,16},{1,9},{17,25},{9,1},{25,17},{2,10},{18... | collective-permute-start | bytes 454664 | tf_op jit(solution)/shard_map/ppermute | solution.py:396
  6.8 7.8 %collective-permute-start.1 = (f32[37,8,128]{2,1,0:T(8,128)S(1)}, f32[37,8,128]{2,1,0:T(8,128)S(1)}, u32[]{:S(2)}, u32[]{:S(2)}) collective-permute-start(f32[37,8,128]{2,1,0:T(8,128)S(1)} %get-tuple-element.38), channel_id=1, source_target_pairs={{8,16},{24,0},{16,8},{0,24},{9,17},{25,1},{17,9},{1,25},{10,18},{2... | collective-permute-start | bytes 454664 | tf_op jit(solution)/shard_map/ppermute | solution.py:396
  7.0 5.4 %copy-start.2 = (f32[2,48,128]{2,1,0:T(8,128)S(1)}, f32[2,48,128]{2,1,0:T(8,128)}, u32[]{:S(2)}) copy-start(f32[2,48,128]{2,1,0:T(8,128)} %constant.2.clone.rest_1_.waves_ref) | copy-start | bytes 147460
  7.7 9.0 %all-to-all-start = ((f32[8,8,128]{2,1,0:T(8,128)}), f32[8,8,128]{2,1,0:T(8,128)S(1)}, u32[]{:S(2)}, u32[]{:S(2)}) async-start(f32[8,8,128]{2,1,0:T(8,128)} %shard_map.59), calls=%async_computation | async-start | bytes 65536 | tf_op jit(solution)/shard_map/all_to_all | solution.py:453
  15.5 1.2 %copy-start.4 = (s32[9,128]{1,0:T(8,128)S(1)}, s32[9,128]{1,0:T(8,128)}, u32[]{:S(2)}) copy-start(s32[9,128]{1,0:T(8,128)} %mask_ref.9) | copy-start | bytes 13828
  15.5 1.2 %copy-start.5 = (f32[9,128]{1,0:T(8,128)S(1)}, f32[9,128]{1,0:T(8,128)}, u32[]{:S(2)}) copy-start(f32[9,128]{1,0:T(8,128)} %depth_ref.9) | copy-start | bytes 13828
  17.1 8.9 %collective-permute-start.4 = (f32[38,8,128]{2,1,0:T(8,128)S(1)}, f32[38,8,128]{2,1,0:T(8,128)S(1)}, u32[]{:S(2)}, u32[]{:S(2)}) collective-permute-start(f32[38,8,128]{2,1,0:T(8,128)S(1)} %get-tuple-element.49), channel_id=1, source_target_pairs={{0,1},{2,3},{4,5},{6,7},{1,0},{3,2},{5,4},{7,6},{8,9},{10,11},{12,... | collective-permute-start | bytes 466952 | tf_op jit(solution)/shard_map/ppermute | solution.py:396
  18.4 8.0 %collective-permute-start.6 = (f32[37,8,128]{2,1,0:T(8,128)S(1)}, f32[37,8,128]{2,1,0:T(8,128)S(1)}, u32[]{:S(2)}, u32[]{:S(2)}) collective-permute-start(f32[37,8,128]{2,1,0:T(8,128)S(1)} %get-tuple-element.52), channel_id=1, source_target_pairs={{8,16},{24,0},{16,8},{0,24},{9,17},{25,1},{17,9},{1,25},{10,18},{2... | collective-permute-start | bytes 454664 | tf_op jit(solution)/shard_map/ppermute | solution.py:396
  21.7 7.7 %collective-permute-start.7 = (f32[36,8,128]{2,1,0:T(8,128)S(1)}, f32[36,8,128]{2,1,0:T(8,128)S(1)}, u32[]{:S(2)}, u32[]{:S(2)}) collective-permute-start(f32[36,8,128]{2,1,0:T(8,128)S(1)} %get-tuple-element.53), channel_id=1, source_target_pairs={{1,2},{3,4},{5,6},{2,1},{4,3},{6,5},{0,0},{7,7},{9,10},{11,12},{13... | collective-permute-start | bytes 442376 | tf_op jit(solution)/shard_map/ppermute | solution.py:396
  23.9 2.1 %collective-permute-start.5 = (f32[27,8,128]{2,1,0:T(8,128)S(1)}, f32[27,8,128]{2,1,0:T(8,128)S(1)}, u32[]{:S(2)}, u32[]{:S(2)}) collective-permute-start(f32[27,8,128]{2,1,0:T(8,128)S(1)} %get-tuple-element.51), channel_id=1, source_target_pairs={{0,8},{16,24},{8,0},{24,16},{1,9},{17,25},{9,1},{25,17},{2,10},{18... | collective-permute-start | bytes 331784 | tf_op jit(solution)/shard_map/ppermute | solution.py:396
  27.9 6.0 %collective-permute-start.8 = (f32[38,8,128]{2,1,0:T(8,128)S(1)}, f32[38,8,128]{2,1,0:T(8,128)S(1)}, u32[]{:S(2)}, u32[]{:S(2)}) collective-permute-start(f32[38,8,128]{2,1,0:T(8,128)S(1)} %get-tuple-element.57), channel_id=1, source_target_pairs={{0,1},{2,3},{4,5},{6,7},{1,0},{3,2},{5,4},{7,6},{8,9},{10,11},{12,... | collective-permute-start | bytes 466952 | tf_op jit(solution)/shard_map/ppermute | solution.py:396
  29.8 6.1 %collective-permute-start.10 = (f32[37,8,128]{2,1,0:T(8,128)S(1)}, f32[37,8,128]{2,1,0:T(8,128)S(1)}, u32[]{:S(2)}, u32[]{:S(2)}) collective-permute-start(f32[37,8,128]{2,1,0:T(8,128)S(1)} %get-tuple-element.62), channel_id=1, source_target_pairs={{8,16},{24,0},{16,8},{0,24},{9,17},{25,1},{17,9},{1,25},{10,18},{2... | collective-permute-start | bytes 454664 | tf_op jit(solution)/shard_map/ppermute | solution.py:396
  31.4 8.4 %collective-permute-start.11 = (f32[36,8,128]{2,1,0:T(8,128)S(1)}, f32[36,8,128]{2,1,0:T(8,128)S(1)}, u32[]{:S(2)}, u32[]{:S(2)}) collective-permute-start(f32[36,8,128]{2,1,0:T(8,128)S(1)} %get-tuple-element.63), channel_id=1, source_target_pairs={{1,2},{3,4},{5,6},{2,1},{4,3},{6,5},{0,0},{7,7},{9,10},{11,12},{13... | collective-permute-start | bytes 442376 | tf_op jit(solution)/shard_map/ppermute | solution.py:396
  33.8 2.1 %collective-permute-start.9 = (f32[27,8,128]{2,1,0:T(8,128)S(1)}, f32[27,8,128]{2,1,0:T(8,128)S(1)}, u32[]{:S(2)}, u32[]{:S(2)}) collective-permute-start(f32[27,8,128]{2,1,0:T(8,128)S(1)} %get-tuple-element.61), channel_id=1, source_target_pairs={{0,8},{16,24},{8,0},{24,16},{1,9},{17,25},{9,1},{25,17},{2,10},{18... | collective-permute-start | bytes 331784 | tf_op jit(solution)/shard_map/ppermute | solution.py:396

commit v18 on v17

--- a/solution.py
+++ b/solution.py
@@ -107,14 +107,17 @@
 
 def extremes_kernel(wind_ref, most_ref):
     put_extremes(wind_ref, most_ref.at[0])
-    for g in range(1, most_ref.shape[0]):
-        most_ref[g] = most_ref[0]
 
 
 def opening_kernel(level_ref, x_near, x_far, t_near, t_far):
     cut_near(level_ref, x_near)
     cut_far(level_ref, x_far)
     cut_headings(level_ref, t_near, t_far)
+
+
+def meeting_kernel(own_ref, other_ref, most_ref):
+    for g in range(most_ref.shape[0]):
+        most_ref[g] = jnp.maximum(own_ref[0], other_ref[0])
 
 
 def flows_into(flow_ref, speed_step, wind_ref, waves_ref):
@@ -449,8 +452,14 @@
     ]
     wide_room = room + [pltpu.VMEM(turned, jnp.float32), pltpu.VMEM(level_set.shape, jnp.float32)]
     values = level_set
-    (most,) = call(extremes_kernel, [wind], [shape(lax.axis_size("gx"))])
-    most = lax.all_to_all(most, "gx", 0, 0)
+    size = lax.axis_size("gx")
+
+    pairs = [(i, i + 1) for i in range(0, size - 1, 2)]
+    pairs += [(j, i) for i, j in pairs]
+    pairs += [(i, i) for i in range(size) if i not in dict(pairs)]
+
+    (most,) = call(extremes_kernel, [wind], [shape(longest + 2)])
+    other = lax.ppermute(most, "gx", pairs)
     x_shapes = [shape(longest + 1), shape(longest)]
     x_out, x_last, t_out, t_last = call(opening_kernel, [values], x_shapes + [shape(middle)] * 2)
     far_shapes = [shape(short), shape(rim * planes), shape(middle)]
@@ -463,6 +472,11 @@
         free = functools.partial(free_kernel, opening, speed_step)
         turning = functools.partial(heading_kernel, heading_step)
         if opening:
+            step = 1 if size % 2 else 2
+            groups = [list(range(k, size, step)) for k in range(step)]
+            (most,) = call(meeting_kernel, [most, other], [shape(size // step)])
+            values, most = lax.optimization_barrier((values, most))
+            most = lax.all_to_all(most, "gx", 0, 0, axis_index_groups=groups)
             ins = [values, wind, waves]
             spun, part, extra, flow = call(
                 free, ins, [field] * 3 + [jax.ShapeDtypeStruct(turned, jnp.float32)], wide_room, work=300

time: 41.2 us -> 41.6 us (level)
  the two profiles are of different devices: /device:TPU:7 before, /device:TPU:8 now
where the time goes in v18:
time: 41.6 us; the launch traced here: 41.3 us
  starting transfers between devices  23.7 us (57%)
  Pallas kernels  13.4 us (32%)
  waiting for transfers between devices  2.26 us (5%)
  local copies, waits for them, and re-layouts  1.74 us (4%)
    ppermute x12, starting transfers between devices, trade(): return lax.ppermute(value, axis, pairs)  16.7 us
    pallas_call x15, Pallas kernels, call(): pl.pallas_call(kernel, out_shape=outs, in_specs=[vmem] * len(ins), out_sp...  13.4 us
    all_to_all x1, starting transfers between devices, local(): most = lax.all_to_all(most, 'gx', 0, 0, axis_index_groups=groups)  5.45 us
    ppermute x12, waiting for transfers between devices, trade(): return lax.ppermute(value, axis, pairs)  1.99 us
    unnamed x14, local copies, waits for them, and re-layouts  1.74 us
    ppermute x1, starting transfers between devices, local(): other = lax.ppermute(most, 'gx', pairs)  1.58 us
  transfers between devices with their start and end apart: 14, of which 2 were waited for; matrix products, arithmetic and copies ran while one was open for 0% of the time, Pallas kernels for 29%

profile of v18, /device:TPU:8, one launch (start us, length us, event | category | flops | bytes accessed | tf_op | source)
XLA Modules:
  0.0 41.3 jit_solution(1906007115800798921)
XLA Ops:
  0.0 0.0 copy-start.3
  0.0 0.7 %copy-done.3 = f32[2,9,128]{2,0,1:T(2,128)S(1)} copy-done((f32[2,9,128]{2,0,1:T(2,128)S(1)}, f32[2,9,128]{2,0,1:T(2,128)}, u32[]{:S(2)}) %copy-start.3) | copy-done | bytes 9240
  0.7 1.6 %collective-permute-start = (f32[40,8,128]{2,1,0:T(8,128)S(1)}, f32[40,8,128]{2,1,0:T(8,128)S(1)}, u32[]{:S(2)}, u32[]{:S(2)}) collective-permute-start(f32[40,8,128]{2,1,0:T(8,128)S(1)} %shard_map.55.own_ref), channel_id=1, source_target_pairs={{0,1},{2,3},{4,5},{6,7},{1,0},{3,2},{5,4},{7,6},{8,9},{10,11},{12,... | collective-permute-start | bytes 491528 | tf_op jit(solution)/shard_map/ppermute | solution.py:462
  2.3 0.0 copy-start
  2.3 1.0 %copy-done = f32[9,12,8,128]{3,2,1,0:T(8,128)S(1)} copy-done((f32[9,12,8,128]{3,2,1,0:T(8,128)S(1)}, f32[9,12,8,128]{3,2,1,0:T(8,128)}, u32[]{:S(2)}) %copy-start) | copy-done | bytes 442392
  3.3 0.0 copy-start.1
  3.3 0.6 %collective-permute-start.3 = (f32[39,8,128]{2,1,0:T(8,128)S(1)}, f32[39,8,128]{2,1,0:T(8,128)S(1)}, u32[]{:S(2)}, u32[]{:S(2)}) collective-permute-start(f32[39,8,128]{2,1,0:T(8,128)S(1)} %get-tuple-element.42), channel_id=1, source_target_pairs={{0,1},{2,3},{4,5},{6,7},{1,0},{3,2},{5,4},{7,6},{8,9},{10,11},{12,... | collective-permute-start | bytes 479240 | tf_op jit(solution)/shard_map/ppermute | solution.py:399
  3.9 3.3 %collective-permute-start.4 = (f32[38,8,128]{2,1,0:T(8,128)S(1)}, f32[38,8,128]{2,1,0:T(8,128)S(1)}, u32[]{:S(2)}, u32[]{:S(2)}) collective-permute-start(f32[38,8,128]{2,1,0:T(8,128)S(1)} %get-tuple-element.43), channel_id=1, source_target_pairs={{1,2},{3,4},{5,6},{2,1},{4,3},{6,5},{0,0},{7,7},{9,10},{11,12},{13... | collective-permute-start | bytes 466952 | tf_op jit(solution)/shard_map/ppermute | solution.py:399
  7.2 0.1 collective-permute-start.1
  7.3 1.6 %collective-permute-start.2 = (f32[37,8,128]{2,1,0:T(8,128)S(1)}, f32[37,8,128]{2,1,0:T(8,128)S(1)}, u32[]{:S(2)}, u32[]{:S(2)}) collective-permute-start(f32[37,8,128]{2,1,0:T(8,128)S(1)} %get-tuple-element.41), channel_id=1, source_target_pairs={{8,16},{24,0},{16,8},{0,24},{9,17},{25,1},{17,9},{1,25},{10,18},{2... | collective-permute-start | bytes 454664 | tf_op jit(solution)/shard_map/ppermute | solution.py:399
  8.9 0.0 collective-permute-done.other_ref
  8.9 0.0 copy-start.2
  8.9 0.6 %shard_map.56 = f32[4,8,128]{2,1,0:T(8,128)} custom-call(f32[40,8,128]{2,1,0:T(8,128)S(1)} %shard_map.55.own_ref, f32[40,8,128]{2,1,0:T(8,128)S(1)} %collective-permute-done.other_ref), custom_call_target="tpu_custom_call" | custom-call | tf_op jit(solution)/shard_map/pallas_call | solution.py:433
  9.5 0.0 copy-start.4
  9.5 5.4 %all-to-all-start = ((f32[4,8,128]{2,1,0:T(8,128)}), f32[4,8,128]{2,1,0:T(8,128)S(1)}, u32[]{:S(2)}, u32[]{:S(2)}) async-start(f32[4,8,128]{2,1,0:T(8,128)} %shard_map.56), calls=%async_computation | async-start | bytes 32768 | tf_op jit(solution)/shard_map/all_to_all | solution.py:479
  15.0 0.0 copy-done.1
  15.0 0.0 copy-done.2
  15.0 0.0 copy-done.4
  15.0 2.2 %shard_map.57 = (f32[9,12,8,128]{3,2,1,0:T(8,128)S(1)}, f32[9,12,8,128]{3,2,1,0:T(8,128)S(1)}, f32[9,12,8,128]{3,2,1,0:T(8,128)S(1)}, f32[7,128,128]{2,1,0:T(8,128)S(1)}) custom-call(f32[9,12,8,128]{3,2,1,0:T(8,128)S(1)} %copy-done.1, f32[9,2,128]{2,1,0:T(2,128)S(1)} %bitcast.2, f32[2,48,128]{2,1,0:T(8,128)S(1)} %copy-done.2), custom_call_target="tpu_custom_call" | custom-call | flops 33177600 | bytes 33177600 | tf_op jit(solution)/shard_map/pallas_call | solution.py:433
  17.2 0.0 collective-permute-done.1.near_ref
  17.2 0.0 collective-permute-done.2.far_ref
  17.2 0.8 %shard_map.59.part_ref = f32[9,12,8,128]{3,2,1,0:T(8,128)S(1)} custom-call(f32[9,12,8,128]{3,2,1,0:T(8,128)S(1)} %copy-done.1, f32[9,12,8,128]{3,2,1,0:T(8,128)S(1)} %get-tuple-element.38.speed_ref, f32[9,12,8,128]{3,2,1,0:T(8,128)S(1)} %get-tuple-element.39.part_ref, f32[37,8,128]{2,1,0:T(8,128)S(1)} %collective-permute-done.1.near_ref, ...), custom_call_target="tpu_custom_call" | custom-call | tf_op jit(solution)/shard_map/pallas_call | solution.py:433
  18.0 0.0 collective-permute-done.4.far_ref
  18.0 0.0 collective-permute-done.3.near_ref
  18.0 0.0 copy-start.5
  18.0 0.0 copy-start.6
  18.0 0.9 %shard_map.60 = (f32[9,12,8,128]{3,2,1,0:T(8,128)S(1)}, f32[9,12,8,128]{3,2,1,0:T(8,128)S(1)}) custom-call(f32[9,12,8,128]{3,2,1,0:T(8,128)S(1)} %copy-done.1, f32[9,12,8,128]{3,2,1,0:T(8,128)S(1)} %shard_map.59.part_ref, f32[39,8,128]{2,1,0:T(8,128)S(1)} %collective-permute-done.3.near_ref, f32[38,8,128]{2,1,0:T(8,128)S(1)} %collective-permute-done.4.far_ref, ...), custom_call_target="tpu_custom_call" | custom-call | tf_op jit(solution)/shard_map/pallas_call | solution.py:433
  18.9 0.3 all-to-all-done.most_ref
  19.2 0.0 copy-done.5
  19.2 0.0 copy-done.6
  19.2 0.4 shard_map.61
  19.6 0.7 %collective-permute-start.5 = (f32[38,8,128]{2,1,0:T(8,128)S(1)}, f32[38,8,128]{2,1,0:T(8,128)S(1)}, u32[]{:S(2)}, u32[]{:S(2)}) collective-permute-start(f32[38,8,128]{2,1,0:T(8,128)S(1)} %get-tuple-element.53), channel_id=1, source_target_pairs={{0,1},{2,3},{4,5},{6,7},{1,0},{3,2},{5,4},{7,6},{8,9},{10,11},{12,... | collective-permute-start | bytes 466952 | tf_op jit(solution)/shard_map/ppermute | solution.py:399
  20.3 0.0 collective-permute-start.7
  20.3 4.1 %collective-permute-start.8 = (f32[36,8,128]{2,1,0:T(8,128)S(1)}, f32[36,8,128]{2,1,0:T(8,128)S(1)}, u32[]{:S(2)}, u32[]{:S(2)}) collective-permute-start(f32[36,8,128]{2,1,0:T(8,128)S(1)} %get-tuple-element.57), channel_id=1, source_target_pairs={{1,2},{3,4},{5,6},{2,1},{4,3},{6,5},{0,0},{7,7},{9,10},{11,12},{13... | collective-permute-start | bytes 442376 | tf_op jit(solution)/shard_map/ppermute | solution.py:399
  24.4 0.4 %collective-permute-start.6 = (f32[27,8,128]{2,1,0:T(8,128)S(1)}, f32[27,8,128]{2,1,0:T(8,128)S(1)}, u32[]{:S(2)}, u32[]{:S(2)}) collective-permute-start(f32[27,8,128]{2,1,0:T(8,128)S(1)} %get-tuple-element.55), channel_id=1, source_target_pairs={{0,8},{16,24},{8,0},{24,16},{1,9},{17,25},{9,1},{25,17},{2,10},{18... | collective-permute-start | bytes 331784 | tf_op jit(solution)/shard_map/ppermute | solution.py:399
  24.9 2.0 %shard_map.62 = (f32[9,12,8,128]{3,2,1,0:T(8,128)S(1)}, f32[9,12,8,128]{3,2,1,0:T(8,128)S(1)}) custom-call(f32[9,12,8,128]{3,2,1,0:T(8,128)S(1)} %get-tuple-element.48.s_ref, f32[7,128,128]{2,1,0:T(8,128)S(1)} %get-tuple-element.49.rest_0_, f32[8,128]{1,0:T(8,128)S(1)} %get-tuple-element.50.rest_1_.pk_ref), custom_call_target="tpu_custom_call" | custom-call | tf_op jit(solution)/shard_map/pallas_call | solution.py:433
  26.8 0.0 collective-permute-done.5.ghosts_ref
  26.9 0.0 collective-permute-done.6.near_ref
  26.9 0.0 collective-permute-done.7.far_ref
  26.9 0.8 %shard_map.63.part_ref = f32[9,12,8,128]{3,2,1,0:T(8,128)S(1)} custom-call(f32[9,12,8,128]{3,2,1,0:T(8,128)S(1)} %get-tuple-element.48.s_ref, f32[9,12,8,128]{3,2,1,0:T(8,128)S(1)} %get-tuple-element.51.speed_ref, f32[9,12,8,128]{3,2,1,0:T(8,128)S(1)} %get-tuple-element.54.part_ref, f32[27,8,128]{2,1,0:T(8,128)S(1)} %collective-permute-done.6.near_ref, ...), custom_call_target="tpu_custom_call" | custom-call | flops 110592000 | bytes 110592000 | tf_op jit(solution)/shard_map/pallas_call | solution.py:433
  27.7 0.7 %shard_map.64 = (f32[9,12,8,128]{3,2,1,0:T(8,128)S(1)}, f32[38,8,128]{2,1,0:T(8,128)S(1)}) custom-call(f32[9,12,8,128]{3,2,1,0:T(8,128)S(1)} %copy-done.1, f32[9,12,8,128]{3,2,1,0:T(8,128)S(1)} %get-tuple-element.48.s_ref, f32[9,12,8,128]{3,2,1,0:T(8,128)S(1)} %shard_map.63.part_ref, f32[38,8,128]{2,1,0:T(8,128)S(1)} %collective-permute-done.5.ghosts_ref, ...), custom_call_target="tpu_custom_call" | custom-call | tf_op jit(solution)/shard_map/pallas_call | solution.py:433
  28.4 1.3 %collective-permute-start.9 = (f32[38,8,128]{2,1,0:T(8,128)S(1)}, f32[38,8,128]{2,1,0:T(8,128)S(1)}, u32[]{:S(2)}, u32[]{:S(2)}) collective-permute-start(f32[38,8,128]{2,1,0:T(8,128)S(1)} %get-tuple-element.61), channel_id=1, source_target_pairs={{0,1},{2,3},{4,5},{6,7},{1,0},{3,2},{5,4},{7,6},{8,9},{10,11},{12,... | collective-permute-start | bytes 466952 | tf_op jit(solution)/shard_map/ppermute | solution.py:399
  29.7 0.0 collective-permute-done.8.ghosts_ref
  29.7 0.4 %shard_map.65 = (f32[9,12,8,128]{3,2,1,0:T(8,128)S(1)}, f32[36,8,128]{2,1,0:T(8,128)S(1)}, f32[27,8,128]{2,1,0:T(8,128)S(1)}, f32[37,8,128]{2,1,0:T(8,128)S(1)}) custom-call(f32[9,12,8,128]{3,2,1,0:T(8,128)S(1)} %copy-done.1, f32[9,12,8,128]{3,2,1,0:T(8,128)S(1)} %get-tuple-element.48.s_ref, f32[9,12,8,128]{3,2,1,0:T(8,128)S(1)} %shard_map.63.part_ref, ...), custom_call_target="tpu_custom_call" | custom-call | tf_op jit(solution)/shard_map/pallas_call | solution.py:433
  30.1 0.9 %collective-permute-start.11 = (f32[37,8,128]{2,1,0:T(8,128)S(1)}, f32[37,8,128]{2,1,0:T(8,128)S(1)}, u32[]{:S(2)}, u32[]{:S(2)}) collective-permute-start(f32[37,8,128]{2,1,0:T(8,128)S(1)} %get-tuple-element.66), channel_id=1, source_target_pairs={{8,16},{24,0},{16,8},{0,24},{9,17},{25,1},{17,9},{1,25},{10,18},{2... | collective-permute-start | bytes 454664 | tf_op jit(solution)/shard_map/ppermute | solution.py:399
  31.0 3.6 %collective-permute-start.12 = (f32[36,8,128]{2,1,0:T(8,128)S(1)}, f32[36,8,128]{2,1,0:T(8,128)S(1)}, u32[]{:S(2)}, u32[]{:S(2)}) collective-permute-start(f32[36,8,128]{2,1,0:T(8,128)S(1)} %get-tuple-element.67), channel_id=1, source_target_pairs={{1,2},{3,4},{5,6},{2,1},{4,3},{6,5},{0,0},{7,7},{9,10},{11,12},{13... | collective-permute-start | bytes 442376 | tf_op jit(solution)/shard_map/ppermute | solution.py:399
  34.6 0.1 collective-permute-start.10
  34.7 0.0 collective-permute-done.9.ghosts_ref
  34.7 2.0 %shard_map.66 = (f32[9,12,8,128]{3,2,1,0:T(8,128)S(1)}, f32[9,12,8,128]{3,2,1,0:T(8,128)S(1)}) custom-call(f32[9,12,8,128]{3,2,1,0:T(8,128)S(1)} %get-tuple-element.62.s_ref, f32[7,128,128]{2,1,0:T(8,128)S(1)} %get-tuple-element.49.rest_0_, f32[8,128]{1,0:T(8,128)S(1)} %get-tuple-element.50.rest_1_.pk_ref), custom_call_target="tpu_custom_call" | custom-call | tf_op jit(solution)/shard_map/pallas_call | solution.py:433
  36.7 0.0 collective-permute-done.10.near_ref
  36.7 0.0 collective-permute-done.11.far_ref
  36.7 0.8 %shard_map.67.part_ref = f32[9,12,8,128]{3,2,1,0:T(8,128)S(1)} custom-call(f32[9,12,8,128]{3,2,1,0:T(8,128)S(1)} %get-tuple-element.62.s_ref, f32[9,12,8,128]{3,2,1,0:T(8,128)S(1)} %get-tuple-element.63.speed_ref, f32[9,12,8,128]{3,2,1,0:T(8,128)S(1)} %get-tuple-element.64.part_ref, f32[27,8,128]{2,1,0:T(8,128)S(1)} %collective-permute-done.10.near_ref, ...), custom_call_target="tpu_custom_call" | custom-call | flops 110592000 | bytes 110592000 | tf_op jit(solution)/shard_map/pallas_call | solution.py:433
  37.5 0.7 %shard_map.68.refs_0_ = f32[9,12,8,128]{3,2,1,0:T(8,128)S(1)} custom-call(f32[9,12,8,128]{3,2,1,0:T(8,128)S(1)} %copy-done.1, f32[9,12,8,128]{3,2,1,0:T(8,128)S(1)} %get-tuple-element.62.s_ref, f32[9,12,8,128]{3,2,1,0:T(8,128)S(1)} %shard_map.67.part_ref, f32[38,8,128]{2,1,0:T(8,128)S(1)} %collective-permute-done.9.ghosts_ref, f32[9,2,128]{2,1,0:T(2,128)S(1)} %bitcast.6, ...), custom_call_target="tpu_custom_call" | custom-call | tf_op jit(solution)/shard_map/pallas_call | solution.py:433
  38.2 2.0 %collective-permute-done.12.ghosts_ref = f32[36,8,128]{2,1,0:T(8,128)S(1)} collective-permute-done((f32[36,8,128]{2,1,0:T(8,128)S(1)}, f32[36,8,128]{2,1,0:T(8,128)S(1)}, u32[]{:S(2)}, u32[]{:S(2)}) %collective-permute-start.12) | collective-permute-done | bytes 147488 | tf_op jit(solution)/shard_map/ppermute | solution.py:399
  40.1 1.1 %shard_map.69 = f32[9,12,8,128]{3,2,1,0:T(8,128)} custom-call(f32[9,12,8,128]{3,2,1,0:T(8,128)S(1)} %copy-done.1, f32[9,12,8,128]{3,2,1,0:T(8,128)S(1)} %get-tuple-element.62.s_ref, f32[9,12,8,128]{3,2,1,0:T(8,128)S(1)} %shard_map.67.part_ref, f32[36,8,128]{2,1,0:T(8,128)S(1)} %collective-permute-done.12.ghosts_ref, f32[9,2,128]{2,1,0:T(2,128)S(1)} %bitcast.7, ...), custom_call_target="tpu_custom_call" | custom-call | tf_op jit(solution)/shard_map/pallas_call | solution.py:433
  (2 shorter events, 0.0 us)
Async XLA Ops:
  0.0 0.7 %copy-start.3 = (f32[2,9,128]{2,0,1:T(2,128)S(1)}, f32[2,9,128]{2,0,1:T(2,128)}, u32[]{:S(2)}) copy-start(f32[2,9,128]{2,0,1:T(2,128)} %param.6) | copy-start | bytes 27652
  0.7 8.2 %collective-permute-start = (f32[40,8,128]{2,1,0:T(8,128)S(1)}, f32[40,8,128]{2,1,0:T(8,128)S(1)}, u32[]{:S(2)}, u32[]{:S(2)}) collective-permute-start(f32[40,8,128]{2,1,0:T(8,128)S(1)} %shard_map.55.own_ref), channel_id=1, source_target_pairs={{0,1},{2,3},{4,5},{6,7},{1,0},{3,2},{5,4},{7,6},{8,9},{10,11},{12,... | collective-permute-start | bytes 491528 | tf_op jit(solution)/shard_map/ppermute | solution.py:462
  2.3 1.0 %copy-start = (f32[9,12,8,128]{3,2,1,0:T(8,128)S(1)}, f32[9,12,8,128]{3,2,1,0:T(8,128)}, u32[]{:S(2)}) copy-start(f32[9,12,8,128]{3,2,1,0:T(8,128)} %base_ref.7) | copy-start | bytes 1327108
  3.3 11.7 %copy-start.1 = (f32[9,12,8,128]{3,2,1,0:T(8,128)S(1)}, f32[9,12,8,128]{3,2,1,0:T(8,128)}, u32[]{:S(2)}) copy-start(f32[9,12,8,128]{3,2,1,0:T(8,128)} %base_ref.7) | copy-start | bytes 1327108
  3.3 14.7 %collective-permute-start.3 = (f32[39,8,128]{2,1,0:T(8,128)S(1)}, f32[39,8,128]{2,1,0:T(8,128)S(1)}, u32[]{:S(2)}, u32[]{:S(2)}) collective-permute-start(f32[39,8,128]{2,1,0:T(8,128)S(1)} %get-tuple-element.42), channel_id=1, source_target_pairs={{0,1},{2,3},{4,5},{6,7},{1,0},{3,2},{5,4},{7,6},{8,9},{10,11},{12,... | collective-permute-start | bytes 479240 | tf_op jit(solution)/shard_map/ppermute | solution.py:399
  3.9 14.1 %collective-permute-start.4 = (f32[38,8,128]{2,1,0:T(8,128)S(1)}, f32[38,8,128]{2,1,0:T(8,128)S(1)}, u32[]{:S(2)}, u32[]{:S(2)}) collective-permute-start(f32[38,8,128]{2,1,0:T(8,128)S(1)} %get-tuple-element.43), channel_id=1, source_target_pairs={{1,2},{3,4},{5,6},{2,1},{4,3},{6,5},{0,0},{7,7},{9,10},{11,12},{13... | collective-permute-start | bytes 466952 | tf_op jit(solution)/shard_map/ppermute | solution.py:399
  7.2 9.9 %collective-permute-start.1 = (f32[37,8,128]{2,1,0:T(8,128)S(1)}, f32[37,8,128]{2,1,0:T(8,128)S(1)}, u32[]{:S(2)}, u32[]{:S(2)}) collective-permute-start(f32[37,8,128]{2,1,0:T(8,128)S(1)} %get-tuple-element.40), channel_id=1, source_target_pairs={{0,8},{16,24},{8,0},{24,16},{1,9},{17,25},{9,1},{25,17},{2,10},{18... | collective-permute-start | bytes 454664 | tf_op jit(solution)/shard_map/ppermute | solution.py:399
  7.3 9.9 %collective-permute-start.2 = (f32[37,8,128]{2,1,0:T(8,128)S(1)}, f32[37,8,128]{2,1,0:T(8,128)S(1)}, u32[]{:S(2)}, u32[]{:S(2)}) collective-permute-start(f32[37,8,128]{2,1,0:T(8,128)S(1)} %get-tuple-element.41), channel_id=1, source_target_pairs={{8,16},{24,0},{16,8},{0,24},{9,17},{25,1},{17,9},{1,25},{10,18},{2... | collective-permute-start | bytes 454664 | tf_op jit(solution)/shard_map/ppermute | solution.py:399
  8.9 6.1 %copy-start.2 = (f32[2,48,128]{2,1,0:T(8,128)S(1)}, f32[2,48,128]{2,1,0:T(8,128)}, u32[]{:S(2)}) copy-start(f32[2,48,128]{2,1,0:T(8,128)} %constant.2.clone.rest_1_.waves_ref) | copy-start | bytes 147460
  9.5 5.5 %copy-start.4 = (f32[2,9,128]{2,0,1:T(2,128)S(1)}, f32[2,9,128]{2,0,1:T(2,128)}, u32[]{:S(2)}) copy-start(f32[2,9,128]{2,0,1:T(2,128)} %param.6) | copy-start | bytes 27652
  9.5 9.7 %all-to-all-start = ((f32[4,8,128]{2,1,0:T(8,128)}), f32[4,8,128]{2,1,0:T(8,128)S(1)}, u32[]{:S(2)}, u32[]{:S(2)}) async-start(f32[4,8,128]{2,1,0:T(8,128)} %shard_map.56), calls=%async_computation | async-start | bytes 32768 | tf_op jit(solution)/shard_map/all_to_all | solution.py:479
  18.0 1.2 %copy-start.5 = (s32[9,128]{1,0:T(8,128)S(1)}, s32[9,128]{1,0:T(8,128)}, u32[]{:S(2)}) copy-start(s32[9,128]{1,0:T(8,128)} %mask_ref.9) | copy-start | bytes 13828
  18.0 1.2 %copy-start.6 = (f32[9,128]{1,0:T(8,128)S(1)}, f32[9,128]{1,0:T(8,128)}, u32[]{:S(2)}) copy-start(f32[9,128]{1,0:T(8,128)} %depth_ref.9) | copy-start | bytes 13828
  19.6 7.2 %collective-permute-start.5 = (f32[38,8,128]{2,1,0:T(8,128)S(1)}, f32[38,8,128]{2,1,0:T(8,128)S(1)}, u32[]{:S(2)}, u32[]{:S(2)}) collective-permute-start(f32[38,8,128]{2,1,0:T(8,128)S(1)} %get-tuple-element.53), channel_id=1, source_target_pairs={{0,1},{2,3},{4,5},{6,7},{1,0},{3,2},{5,4},{7,6},{8,9},{10,11},{12,... | collective-permute-start | bytes 466952 | tf_op jit(solution)/shard_map/ppermute | solution.py:399
  20.3 6.6 %collective-permute-start.7 = (f32[37,8,128]{2,1,0:T(8,128)S(1)}, f32[37,8,128]{2,1,0:T(8,128)S(1)}, u32[]{:S(2)}, u32[]{:S(2)}) collective-permute-start(f32[37,8,128]{2,1,0:T(8,128)S(1)} %get-tuple-element.56), channel_id=1, source_target_pairs={{8,16},{24,0},{16,8},{0,24},{9,17},{25,1},{17,9},{1,25},{10,18},{2... | collective-permute-start | bytes 454664 | tf_op jit(solution)/shard_map/ppermute | solution.py:399
  20.3 9.4 %collective-permute-start.8 = (f32[36,8,128]{2,1,0:T(8,128)S(1)}, f32[36,8,128]{2,1,0:T(8,128)S(1)}, u32[]{:S(2)}, u32[]{:S(2)}) collective-permute-start(f32[36,8,128]{2,1,0:T(8,128)S(1)} %get-tuple-element.57), channel_id=1, source_target_pairs={{1,2},{3,4},{5,6},{2,1},{4,3},{6,5},{0,0},{7,7},{9,10},{11,12},{13... | collective-permute-start | bytes 442376 | tf_op jit(solution)/shard_map/ppermute | solution.py:399
  24.4 2.4 %collective-permute-start.6 = (f32[27,8,128]{2,1,0:T(8,128)S(1)}, f32[27,8,128]{2,1,0:T(8,128)S(1)}, u32[]{:S(2)}, u32[]{:S(2)}) collective-permute-start(f32[27,8,128]{2,1,0:T(8,128)S(1)} %get-tuple-element.55), channel_id=1, source_target_pairs={{0,8},{16,24},{8,0},{24,16},{1,9},{17,25},{9,1},{25,17},{2,10},{18... | collective-permute-start | bytes 331784 | tf_op jit(solution)/shard_map/ppermute | solution.py:399
  28.4 6.3 %collective-permute-start.9 = (f32[38,8,128]{2,1,0:T(8,128)S(1)}, f32[38,8,128]{2,1,0:T(8,128)S(1)}, u32[]{:S(2)}, u32[]{:S(2)}) collective-permute-start(f32[38,8,128]{2,1,0:T(8,128)S(1)} %get-tuple-element.61), channel_id=1, source_target_pairs={{0,1},{2,3},{4,5},{6,7},{1,0},{3,2},{5,4},{7,6},{8,9},{10,11},{12,... | collective-permute-start | bytes 466952 | tf_op jit(solution)/shard_map/ppermute | solution.py:399
  30.1 6.6 %collective-permute-start.11 = (f32[37,8,128]{2,1,0:T(8,128)S(1)}, f32[37,8,128]{2,1,0:T(8,128)S(1)}, u32[]{:S(2)}, u32[]{:S(2)}) collective-permute-start(f32[37,8,128]{2,1,0:T(8,128)S(1)} %get-tuple-element.66), channel_id=1, source_target_pairs={{8,16},{24,0},{16,8},{0,24},{9,17},{25,1},{17,9},{1,25},{10,18},{2... | collective-permute-start | bytes 454664 | tf_op jit(solution)/shard_map/ppermute | solution.py:399
  31.0 9.1 %collective-permute-start.12 = (f32[36,8,128]{2,1,0:T(8,128)S(1)}, f32[36,8,128]{2,1,0:T(8,128)S(1)}, u32[]{:S(2)}, u32[]{:S(2)}) collective-permute-start(f32[36,8,128]{2,1,0:T(8,128)S(1)} %get-tuple-element.67), channel_id=1, source_target_pairs={{1,2},{3,4},{5,6},{2,1},{4,3},{6,5},{0,0},{7,7},{9,10},{11,12},{13... | collective-permute-start | bytes 442376 | tf_op jit(solution)/shard_map/ppermute | solution.py:399
  34.6 2.1 %collective-permute-start.10 = (f32[27,8,128]{2,1,0:T(8,128)S(1)}, f32[27,8,128]{2,1,0:T(8,128)S(1)}, u32[]{:S(2)}, u32[]{:S(2)}) collective-permute-start(f32[27,8,128]{2,1,0:T(8,128)S(1)} %get-tuple-element.65), channel_id=1, source_target_pairs={{0,8},{16,24},{8,0},{24,16},{1,9},{17,25},{9,1},{25,17},{2,10},{18... | collective-permute-start | bytes 331784 | tf_op jit(solution)/shard_map/ppermute | solution.py:399

commit v19 on v16

--- a/solution.py
+++ b/solution.py
@@ -462,7 +462,7 @@
 
     (most,) = call(extremes_kernel, [wind], [shape(longest + 2)])
     other = spread(most, 1)
-    x_shapes = [shape(longest + 1), shape(longest)]
+    x_shapes = [shape(longest), shape(longest + 1)]
     x_out, x_last, t_out, t_last = call(opening_kernel, [values], x_shapes + [shape(middle)] * 2)
     far_shapes = [shape(short), shape(rim * planes), shape(middle)]
     for section in (1, 2, 3):
@@ -486,14 +486,14 @@
                 most, part = lax.optimization_barrier((most, part))
                 other = spread(most, reach)
                 reach *= 2
+            part, x_far = lax.optimization_barrier((part, x_far))
         else:
             if section == 3:
                 values, x_near = lax.optimization_barrier((values, x_near))
             spun, part = call(free, [values, flow, pk], [field] * 2, room)
             if section == 2:
                 part, x_near = lax.optimization_barrier((part, x_near))
-        weight = 0 if opening else 1000
-        (part,) = call(turning, [values, spun, part, t_near, t_far], [field], work=weight)
+        (part,) = call(turning, [values, spun, part, t_near, t_far], [field], work=1000)
         if opening:
             ins = [values, part, x_near, x_far, wind, waves]
             first = functools.partial(first_kernel, speed_step)

time: 40.2 us -> 39.9 us (level)
  waiting for transfers between devices: 4.91 us -> 4.18 us
    ppermute x12, waiting for transfers between devices: 3.36 us -> 2.14 us  [trade(): return lax.ppermute(value, axis, pairs)]
    ppermute x12, starting transfers between devices: 16.1 us -> 16.9 us  [trade(): return lax.ppermute(value, axis, pairs)]
    ppermute x3, waiting for transfers between devices: 1.55 us -> 2.04 us  [spread(): return lax.ppermute(most, 'gx', pairs)]
    ppermute x3, starting transfers between devices: 4.17 us -> 3.72 us  [spread(): return lax.ppermute(most, 'gx', pairs)]
  transfers between devices with their start and end apart: 15 -> 15, of which waited for: 7 -> 4; matrix products, arithmetic and copies ran while one was open for 0% -> 0% of each run, Pallas kernels for 28% -> 28%
where the time goes in v19:
time: 39.9 us; the launch traced here: 39.5 us
  starting transfers between devices  20.6 us (52%)
  Pallas kernels  12.8 us (32%)
  waiting for transfers between devices  4.18 us (10%)
  local copies, waits for them, and re-layouts  1.74 us (4%)
    ppermute x12, starting transfers between devices, trade(): return lax.ppermute(value, axis, pairs)  16.9 us
    pallas_call x15, Pallas kernels, call(): pl.pallas_call(kernel, out_shape=outs, in_specs=[vmem] * len(ins), out_sp...  12.8 us
    ppermute x3, starting transfers between devices, spread(): return lax.ppermute(most, 'gx', pairs)  3.72 us
    ppermute x12, waiting for transfers between devices, trade(): return lax.ppermute(value, axis, pairs)  2.14 us
    ppermute x3, waiting for transfers between devices, spread(): return lax.ppermute(most, 'gx', pairs)  2.04 us
    unnamed x14, local copies, waits for them, and re-layouts  1.74 us
  transfers between devices with their start and end apart: 15, of which 4 were waited for; matrix products, arithmetic and copies ran while one was open for 0% of the time, Pallas kernels for 28%

profile of v19, /device:TPU:8, one launch (start us, length us, event | category | flops | bytes accessed | tf_op | source)
XLA Modules:
  0.0 39.5 jit_solution(3902188521247073310)
XLA Ops:
  0.0 0.0 copy-start.3
  0.0 0.7 %copy-done.3 = f32[2,9,128]{2,0,1:T(2,128)S(1)} copy-done((f32[2,9,128]{2,0,1:T(2,128)S(1)}, f32[2,9,128]{2,0,1:T(2,128)}, u32[]{:S(2)}) %copy-start.3) | copy-done | bytes 9240
  0.7 1.6 %collective-permute-start = (f32[40,8,128]{2,1,0:T(8,128)S(1)}, f32[40,8,128]{2,1,0:T(8,128)S(1)}, u32[]{:S(2)}, u32[]{:S(2)}) collective-permute-start(f32[40,8,128]{2,1,0:T(8,128)S(1)} %shard_map.56.own_ref), channel_id=1, source_target_pairs={{0,1},{1,0},{2,3},{3,2},{4,5},{5,4},{6,7},{7,6},{8,9},{9,8},{10,11... | collective-permute-start | bytes 491528 | tf_op jit(solution)/shard_map/ppermute | solution.py:461
  2.3 0.0 copy-start
  2.3 1.0 %copy-done = f32[9,12,8,128]{3,2,1,0:T(8,128)S(1)} copy-done((f32[9,12,8,128]{3,2,1,0:T(8,128)S(1)}, f32[9,12,8,128]{3,2,1,0:T(8,128)}, u32[]{:S(2)}) %copy-start) | copy-done | bytes 442392
  3.3 0.0 copy-start.1
  3.3 2.1 %collective-permute-start.2 = (f32[39,8,128]{2,1,0:T(8,128)S(1)}, f32[39,8,128]{2,1,0:T(8,128)S(1)}, u32[]{:S(2)}, u32[]{:S(2)}) collective-permute-start(f32[39,8,128]{2,1,0:T(8,128)S(1)} %get-tuple-element.42), channel_id=1, source_target_pairs={{1,2},{3,4},{5,6},{2,1},{4,3},{6,5},{0,0},{7,7},{9,10},{11,12},{13... | collective-permute-start | bytes 479240 | tf_op jit(solution)/shard_map/ppermute | solution.py:398
  5.4 0.1 collective-permute-start.3
  5.5 2.0 %collective-permute-start.4 = (f32[37,8,128]{2,1,0:T(8,128)S(1)}, f32[37,8,128]{2,1,0:T(8,128)S(1)}, u32[]{:S(2)}, u32[]{:S(2)}) collective-permute-start(f32[37,8,128]{2,1,0:T(8,128)S(1)} %get-tuple-element.45), channel_id=1, source_target_pairs={{8,16},{24,0},{16,8},{0,24},{9,17},{25,1},{17,9},{1,25},{10,18},{2... | collective-permute-start | bytes 454664 | tf_op jit(solution)/shard_map/ppermute | solution.py:398
  7.5 0.0 copy-start.2
  7.5 0.0 copy-start.4
  7.5 2.6 %collective-permute-start.5 = (f32[38,8,128]{2,1,0:T(8,128)S(1)}, f32[38,8,128]{2,1,0:T(8,128)S(1)}, u32[]{:S(2)}, u32[]{:S(2)}) collective-permute-start(f32[38,8,128]{2,1,0:T(8,128)S(1)} %get-tuple-element.46), channel_id=1, source_target_pairs={{0,1},{2,3},{4,5},{6,7},{1,0},{3,2},{5,4},{7,6},{8,9},{10,11},{12,... | collective-permute-start | bytes 466952 | tf_op jit(solution)/shard_map/ppermute | solution.py:398
  10.1 0.0 collective-permute-done.other_ref
  10.1 0.5 %collective-permute-start.1 = (f32[8,128]{1,0:T(8,128)S(1)}, f32[8,128]{1,0:T(8,128)S(1)}, u32[]{:S(2)}, u32[]{:S(2)}) collective-permute-start(f32[8,128]{1,0:T(8,128)S(1)} %shard_map.57), channel_id=1, source_target_pairs={{0,2},{1,3},{2,0},{3,1},{4,6},{5,7},{6,4},{7,5},{8,10},{9,11},{10,... | collective-permute-start | bytes 12296 | tf_op jit(solution)/shard_map/ppermute | solution.py:461
  10.6 0.0 copy-done.1
  10.6 0.0 copy-done.2
  10.6 0.0 copy-done.4
  10.6 2.2 %shard_map.55 = (f32[9,12,8,128]{3,2,1,0:T(8,128)S(1)}, f32[9,12,8,128]{3,2,1,0:T(8,128)S(1)}, f32[9,12,8,128]{3,2,1,0:T(8,128)S(1)}, f32[7,128,128]{2,1,0:T(8,128)S(1)}) custom-call(f32[9,12,8,128]{3,2,1,0:T(8,128)S(1)} %copy-done.1, f32[9,2,128]{2,1,0:T(2,128)S(1)} %bitcast.2, f32[2,48,128]{2,1,0:T(8,128)S(1)} %copy-done.2), custom_call_target="tpu_custom_call" | custom-call | flops 33177600 | bytes 33177600 | tf_op jit(solution)/shard_map/pallas_call | solution.py:432
  12.8 1.0 %collective-permute-done.1 = f32[8,128]{1,0:T(8,128)S(1)} collective-permute-done((f32[8,128]{1,0:T(8,128)S(1)}, f32[8,128]{1,0:T(8,128)S(1)}, u32[]{:S(2)}, u32[]{:S(2)}) %collective-permute-start.1) | collective-permute-done | bytes 4128 | tf_op jit(solution)/shard_map/ppermute | solution.py:461
  13.7 0.0 collective-permute-done.2.far_ref
  13.7 1.7 %collective-permute-start.6 = (f32[8,128]{1,0:T(8,128)S(1)}, f32[8,128]{1,0:T(8,128)S(1)}, u32[]{:S(2)}, u32[]{:S(2)}) collective-permute-start(f32[8,128]{1,0:T(8,128)S(1)} %max.3.most_ref), channel_id=1, source_target_pairs={{0,4},{1,5},{2,6},{3,7},{4,0},{5,1},{6,2},{7,3},{8,12},{9,13},{10,... | collective-permute-start | bytes 12296 | tf_op jit(solution)/shard_map/ppermute | solution.py:461
  15.4 0.0 collective-permute-done.3.near_ref
  15.4 0.0 collective-permute-done.4.far_ref
  15.4 0.8 %shard_map.59.part_ref = f32[9,12,8,128]{3,2,1,0:T(8,128)S(1)} custom-call(f32[9,12,8,128]{3,2,1,0:T(8,128)S(1)} %copy-done.1, f32[9,12,8,128]{3,2,1,0:T(8,128)S(1)} %get-tuple-element.39.speed_ref, f32[9,12,8,128]{3,2,1,0:T(8,128)S(1)} %get-tuple-element.43.part_ref, f32[37,8,128]{2,1,0:T(8,128)S(1)} %collective-permute-done.3.near_ref, ...), custom_call_target="tpu_custom_call" | custom-call | flops 110592000 | bytes 110592000 | tf_op jit(solution)/shard_map/pallas_call | solution.py:432
  16.3 0.0 collective-permute-done.5.near_ref
  16.3 0.0 copy-start.5
  16.3 0.0 copy-start.6
  16.3 0.9 %shard_map.60 = (f32[9,12,8,128]{3,2,1,0:T(8,128)S(1)}, f32[9,12,8,128]{3,2,1,0:T(8,128)S(1)}) custom-call(f32[9,12,8,128]{3,2,1,0:T(8,128)S(1)} %copy-done.1, f32[9,12,8,128]{3,2,1,0:T(8,128)S(1)} %shard_map.59.part_ref, f32[38,8,128]{2,1,0:T(8,128)S(1)} %collective-permute-done.5.near_ref, f32[39,8,128]{2,1,0:T(8,128)S(1)} %collective-permute-done.2.far_ref, ...), custom_call_target="tpu_custom_call" | custom-call | tf_op jit(solution)/shard_map/pallas_call | solution.py:432
  17.2 1.0 %collective-permute-done.6.other_ref = f32[8,128]{1,0:T(8,128)S(1)} collective-permute-done((f32[8,128]{1,0:T(8,128)S(1)}, f32[8,128]{1,0:T(8,128)S(1)}, u32[]{:S(2)}, u32[]{:S(2)}) %collective-permute-start.6) | collective-permute-done | bytes 4128 | tf_op jit(solution)/shard_map/ppermute | solution.py:461
  18.3 0.0 copy-done.5
  18.3 0.0 copy-done.6
  18.3 0.4 shard_map.61
  18.7 0.1 collective-permute-start.7
  18.8 0.0 collective-permute-start.9
  18.8 4.0 %collective-permute-start.10 = (f32[36,8,128]{2,1,0:T(8,128)S(1)}, f32[36,8,128]{2,1,0:T(8,128)S(1)}, u32[]{:S(2)}, u32[]{:S(2)}) collective-permute-start(f32[36,8,128]{2,1,0:T(8,128)S(1)} %get-tuple-element.61), channel_id=1, source_target_pairs={{1,2},{3,4},{5,6},{2,1},{4,3},{6,5},{0,0},{7,7},{9,10},{11,12},{13... | collective-permute-start | bytes 442376 | tf_op jit(solution)/shard_map/ppermute | solution.py:398
  22.8 0.4 %collective-permute-start.8 = (f32[27,8,128]{2,1,0:T(8,128)S(1)}, f32[27,8,128]{2,1,0:T(8,128)S(1)}, u32[]{:S(2)}, u32[]{:S(2)}) collective-permute-start(f32[27,8,128]{2,1,0:T(8,128)S(1)} %get-tuple-element.59), channel_id=1, source_target_pairs={{0,8},{16,24},{8,0},{24,16},{1,9},{17,25},{9,1},{25,17},{2,10},{18... | collective-permute-start | bytes 331784 | tf_op jit(solution)/shard_map/ppermute | solution.py:398
  23.2 2.0 %shard_map.62 = (f32[9,12,8,128]{3,2,1,0:T(8,128)S(1)}, f32[9,12,8,128]{3,2,1,0:T(8,128)S(1)}) custom-call(f32[9,12,8,128]{3,2,1,0:T(8,128)S(1)} %get-tuple-element.52.s_ref, f32[7,128,128]{2,1,0:T(8,128)S(1)} %get-tuple-element.53.rest_0_, f32[8,128]{1,0:T(8,128)S(1)} %get-tuple-element.54.rest_1_.pk_ref), custom_call_target="tpu_custom_call" | custom-call | tf_op jit(solution)/shard_map/pallas_call | solution.py:432
  25.2 0.0 collective-permute-done.7.ghosts_ref
  25.2 0.0 collective-permute-done.8.near_ref
  25.2 0.0 collective-permute-done.9.far_ref
  25.2 0.8 %shard_map.63.part_ref = f32[9,12,8,128]{3,2,1,0:T(8,128)S(1)} custom-call(f32[9,12,8,128]{3,2,1,0:T(8,128)S(1)} %get-tuple-element.52.s_ref, f32[9,12,8,128]{3,2,1,0:T(8,128)S(1)} %get-tuple-element.55.speed_ref, f32[9,12,8,128]{3,2,1,0:T(8,128)S(1)} %get-tuple-element.58.part_ref, f32[27,8,128]{2,1,0:T(8,128)S(1)} %collective-permute-done.8.near_ref, ...), custom_call_target="tpu_custom_call" | custom-call | flops 110592000 | bytes 110592000 | tf_op jit(solution)/shard_map/pallas_call | solution.py:432
  26.0 0.7 %shard_map.64 = (f32[9,12,8,128]{3,2,1,0:T(8,128)S(1)}, f32[38,8,128]{2,1,0:T(8,128)S(1)}) custom-call(f32[9,12,8,128]{3,2,1,0:T(8,128)S(1)} %copy-done.1, f32[9,12,8,128]{3,2,1,0:T(8,128)S(1)} %get-tuple-element.52.s_ref, f32[9,12,8,128]{3,2,1,0:T(8,128)S(1)} %shard_map.63.part_ref, f32[38,8,128]{2,1,0:T(8,128)S(1)} %collective-permute-done.7.ghosts_ref, ...), custom_call_target="tpu_custom_call" | custom-call | tf_op jit(solution)/shard_map/pallas_call | solution.py:432
  26.7 1.0 %collective-permute-start.11 = (f32[38,8,128]{2,1,0:T(8,128)S(1)}, f32[38,8,128]{2,1,0:T(8,128)S(1)}, u32[]{:S(2)}, u32[]{:S(2)}) collective-permute-start(f32[38,8,128]{2,1,0:T(8,128)S(1)} %get-tuple-element.65), channel_id=1, source_target_pairs={{0,1},{2,3},{4,5},{6,7},{1,0},{3,2},{5,4},{7,6},{8,9},{10,11},{12,... | collective-permute-start | bytes 466952 | tf_op jit(solution)/shard_map/ppermute | solution.py:398
  27.7 0.2 collective-permute-done.10.ghosts_ref
  28.0 0.4 %shard_map.65 = (f32[9,12,8,128]{3,2,1,0:T(8,128)S(1)}, f32[36,8,128]{2,1,0:T(8,128)S(1)}, f32[27,8,128]{2,1,0:T(8,128)S(1)}, f32[37,8,128]{2,1,0:T(8,128)S(1)}) custom-call(f32[9,12,8,128]{3,2,1,0:T(8,128)S(1)} %copy-done.1, f32[9,12,8,128]{3,2,1,0:T(8,128)S(1)} %get-tuple-element.52.s_ref, f32[9,12,8,128]{3,2,1,0:T(8,128)S(1)} %shard_map.63.part_ref, ...), custom_call_target="tpu_custom_call" | custom-call | tf_op jit(solution)/shard_map/pallas_call | solution.py:432
  28.4 0.7 %collective-permute-start.13 = (f32[37,8,128]{2,1,0:T(8,128)S(1)}, f32[37,8,128]{2,1,0:T(8,128)S(1)}, u32[]{:S(2)}, u32[]{:S(2)}) collective-permute-start(f32[37,8,128]{2,1,0:T(8,128)S(1)} %get-tuple-element.70), channel_id=1, source_target_pairs={{8,16},{24,0},{16,8},{0,24},{9,17},{25,1},{17,9},{1,25},{10,18},{2... | collective-permute-start | bytes 454664 | tf_op jit(solution)/shard_map/ppermute | solution.py:398
  29.0 3.9 %collective-permute-start.14 = (f32[36,8,128]{2,1,0:T(8,128)S(1)}, f32[36,8,128]{2,1,0:T(8,128)S(1)}, u32[]{:S(2)}, u32[]{:S(2)}) collective-permute-start(f32[36,8,128]{2,1,0:T(8,128)S(1)} %get-tuple-element.71), channel_id=1, source_target_pairs={{1,2},{3,4},{5,6},{2,1},{4,3},{6,5},{0,0},{7,7},{9,10},{11,12},{13... | collective-permute-start | bytes 442376 | tf_op jit(solution)/shard_map/ppermute | solution.py:398
  32.9 0.1 collective-permute-start.12
  33.0 0.0 collective-permute-done.11.ghosts_ref
  33.0 2.0 %shard_map.66 = (f32[9,12,8,128]{3,2,1,0:T(8,128)S(1)}, f32[9,12,8,128]{3,2,1,0:T(8,128)S(1)}) custom-call(f32[9,12,8,128]{3,2,1,0:T(8,128)S(1)} %get-tuple-element.66.s_ref, f32[7,128,128]{2,1,0:T(8,128)S(1)} %get-tuple-element.53.rest_0_, f32[8,128]{1,0:T(8,128)S(1)} %get-tuple-element.54.rest_1_.pk_ref), custom_call_target="tpu_custom_call" | custom-call | tf_op jit(solution)/shard_map/pallas_call | solution.py:432
  35.0 0.0 collective-permute-done.12.near_ref
  35.0 0.0 collective-permute-done.13.far_ref
  35.0 0.8 %shard_map.67.part_ref = f32[9,12,8,128]{3,2,1,0:T(8,128)S(1)} custom-call(f32[9,12,8,128]{3,2,1,0:T(8,128)S(1)} %get-tuple-element.66.s_ref, f32[9,12,8,128]{3,2,1,0:T(8,128)S(1)} %get-tuple-element.67.speed_ref, f32[9,12,8,128]{3,2,1,0:T(8,128)S(1)} %get-tuple-element.68.part_ref, f32[27,8,128]{2,1,0:T(8,128)S(1)} %collective-permute-done.12.near_ref, ...), custom_call_target="tpu_custom_call" | custom-call | flops 110592000 | bytes 110592000 | tf_op jit(solution)/shard_map/pallas_call | solution.py:432
  35.8 0.7 %shard_map.68.refs_0_ = f32[9,12,8,128]{3,2,1,0:T(8,128)S(1)} custom-call(f32[9,12,8,128]{3,2,1,0:T(8,128)S(1)} %copy-done.1, f32[9,12,8,128]{3,2,1,0:T(8,128)S(1)} %get-tuple-element.66.s_ref, f32[9,12,8,128]{3,2,1,0:T(8,128)S(1)} %shard_map.67.part_ref, f32[38,8,128]{2,1,0:T(8,128)S(1)} %collective-permute-done.11.ghosts_ref, f32[9,2,128]{2,1,0:T(2,128)S(1)} %bitcast.6, ...), custom_call_target="tpu_custom_call" | custom-call | tf_op jit(solution)/shard_map/pallas_call | solution.py:432
  36.5 1.9 %collective-permute-done.14.ghosts_ref = f32[36,8,128]{2,1,0:T(8,128)S(1)} collective-permute-done((f32[36,8,128]{2,1,0:T(8,128)S(1)}, f32[36,8,128]{2,1,0:T(8,128)S(1)}, u32[]{:S(2)}, u32[]{:S(2)}) %collective-permute-start.14) | collective-permute-done | bytes 147488 | tf_op jit(solution)/shard_map/ppermute | solution.py:398
  38.4 1.1 %shard_map.69 = f32[9,12,8,128]{3,2,1,0:T(8,128)} custom-call(f32[9,12,8,128]{3,2,1,0:T(8,128)S(1)} %copy-done.1, f32[9,12,8,128]{3,2,1,0:T(8,128)S(1)} %get-tuple-element.66.s_ref, f32[9,12,8,128]{3,2,1,0:T(8,128)S(1)} %shard_map.67.part_ref, f32[36,8,128]{2,1,0:T(8,128)S(1)} %collective-permute-done.14.ghosts_ref, f32[9,2,128]{2,1,0:T(2,128)S(1)} %bitcast.7, ...), custom_call_target="tpu_custom_call" | custom-call | tf_op jit(solution)/shard_map/pallas_call | solution.py:432
  (4 shorter events, 0.1 us)
Async XLA Ops:
  0.0 0.7 %copy-start.3 = (f32[2,9,128]{2,0,1:T(2,128)S(1)}, f32[2,9,128]{2,0,1:T(2,128)}, u32[]{:S(2)}) copy-start(f32[2,9,128]{2,0,1:T(2,128)} %param.6) | copy-start | bytes 27652
  0.7 9.4 %collective-permute-start = (f32[40,8,128]{2,1,0:T(8,128)S(1)}, f32[40,8,128]{2,1,0:T(8,128)S(1)}, u32[]{:S(2)}, u32[]{:S(2)}) collective-permute-start(f32[40,8,128]{2,1,0:T(8,128)S(1)} %shard_map.56.own_ref), channel_id=1, source_target_pairs={{0,1},{1,0},{2,3},{3,2},{4,5},{5,4},{6,7},{7,6},{8,9},{9,8},{10,11... | collective-permute-start | bytes 491528 | tf_op jit(solution)/shard_map/ppermute | solution.py:461
  2.3 1.0 %copy-start = (f32[9,12,8,128]{3,2,1,0:T(8,128)S(1)}, f32[9,12,8,128]{3,2,1,0:T(8,128)}, u32[]{:S(2)}) copy-start(f32[9,12,8,128]{3,2,1,0:T(8,128)} %base_ref.7) | copy-start | bytes 1327108
  3.3 7.3 %copy-start.1 = (f32[9,12,8,128]{3,2,1,0:T(8,128)S(1)}, f32[9,12,8,128]{3,2,1,0:T(8,128)}, u32[]{:S(2)}) copy-start(f32[9,12,8,128]{3,2,1,0:T(8,128)} %base_ref.7) | copy-start | bytes 1327108
  3.3 10.4 %collective-permute-start.2 = (f32[39,8,128]{2,1,0:T(8,128)S(1)}, f32[39,8,128]{2,1,0:T(8,128)S(1)}, u32[]{:S(2)}, u32[]{:S(2)}) collective-permute-start(f32[39,8,128]{2,1,0:T(8,128)S(1)} %get-tuple-element.42), channel_id=1, source_target_pairs={{1,2},{3,4},{5,6},{2,1},{4,3},{6,5},{0,0},{7,7},{9,10},{11,12},{13... | collective-permute-start | bytes 479240 | tf_op jit(solution)/shard_map/ppermute | solution.py:398
  5.4 10.0 %collective-permute-start.3 = (f32[37,8,128]{2,1,0:T(8,128)S(1)}, f32[37,8,128]{2,1,0:T(8,128)S(1)}, u32[]{:S(2)}, u32[]{:S(2)}) collective-permute-start(f32[37,8,128]{2,1,0:T(8,128)S(1)} %get-tuple-element.44), channel_id=1, source_target_pairs={{0,8},{16,24},{8,0},{24,16},{1,9},{17,25},{9,1},{25,17},{2,10},{18... | collective-permute-start | bytes 454664 | tf_op jit(solution)/shard_map/ppermute | solution.py:398
  5.5 10.0 %collective-permute-start.4 = (f32[37,8,128]{2,1,0:T(8,128)S(1)}, f32[37,8,128]{2,1,0:T(8,128)S(1)}, u32[]{:S(2)}, u32[]{:S(2)}) collective-permute-start(f32[37,8,128]{2,1,0:T(8,128)S(1)} %get-tuple-element.45), channel_id=1, source_target_pairs={{8,16},{24,0},{16,8},{0,24},{9,17},{25,1},{17,9},{1,25},{10,18},{2... | collective-permute-start | bytes 454664 | tf_op jit(solution)/shard_map/ppermute | solution.py:398
  7.5 3.1 %copy-start.2 = (f32[2,48,128]{2,1,0:T(8,128)S(1)}, f32[2,48,128]{2,1,0:T(8,128)}, u32[]{:S(2)}) copy-start(f32[2,48,128]{2,1,0:T(8,128)} %constant.2.clone.rest_1_.waves_ref) | copy-start | bytes 147460
  7.5 3.1 %copy-start.4 = (f32[2,9,128]{2,0,1:T(2,128)S(1)}, f32[2,9,128]{2,0,1:T(2,128)}, u32[]{:S(2)}) copy-start(f32[2,9,128]{2,0,1:T(2,128)} %param.6) | copy-start | bytes 27652
  7.5 8.8 %collective-permute-start.5 = (f32[38,8,128]{2,1,0:T(8,128)S(1)}, f32[38,8,128]{2,1,0:T(8,128)S(1)}, u32[]{:S(2)}, u32[]{:S(2)}) collective-permute-start(f32[38,8,128]{2,1,0:T(8,128)S(1)} %get-tuple-element.46), channel_id=1, source_target_pairs={{0,1},{2,3},{4,5},{6,7},{1,0},{3,2},{5,4},{7,6},{8,9},{10,11},{12,... | collective-permute-start | bytes 466952 | tf_op jit(solution)/shard_map/ppermute | solution.py:398
  10.1 3.6 %collective-permute-start.1 = (f32[8,128]{1,0:T(8,128)S(1)}, f32[8,128]{1,0:T(8,128)S(1)}, u32[]{:S(2)}, u32[]{:S(2)}) collective-permute-start(f32[8,128]{1,0:T(8,128)S(1)} %shard_map.57), channel_id=1, source_target_pairs={{0,2},{1,3},{2,0},{3,1},{4,6},{5,7},{6,4},{7,5},{8,10},{9,11},{10,... | collective-permute-start | bytes 12296 | tf_op jit(solution)/shard_map/ppermute | solution.py:461
  13.7 4.5 %collective-permute-start.6 = (f32[8,128]{1,0:T(8,128)S(1)}, f32[8,128]{1,0:T(8,128)S(1)}, u32[]{:S(2)}, u32[]{:S(2)}) collective-permute-start(f32[8,128]{1,0:T(8,128)S(1)} %max.3.most_ref), channel_id=1, source_target_pairs={{0,4},{1,5},{2,6},{3,7},{4,0},{5,1},{6,2},{7,3},{8,12},{9,13},{10,... | collective-permute-start | bytes 12296 | tf_op jit(solution)/shard_map/ppermute | solution.py:461
  16.3 2.0 %copy-start.5 = (s32[9,128]{1,0:T(8,128)S(1)}, s32[9,128]{1,0:T(8,128)}, u32[]{:S(2)}) copy-start(s32[9,128]{1,0:T(8,128)} %mask_ref.9) | copy-start | bytes 13828
  16.3 2.0 %copy-start.6 = (f32[9,128]{1,0:T(8,128)S(1)}, f32[9,128]{1,0:T(8,128)}, u32[]{:S(2)}) copy-start(f32[9,128]{1,0:T(8,128)} %depth_ref.9) | copy-start | bytes 13828
  18.7 6.5 %collective-permute-start.7 = (f32[38,8,128]{2,1,0:T(8,128)S(1)}, f32[38,8,128]{2,1,0:T(8,128)S(1)}, u32[]{:S(2)}, u32[]{:S(2)}) collective-permute-start(f32[38,8,128]{2,1,0:T(8,128)S(1)} %get-tuple-element.57), channel_id=1, source_target_pairs={{0,1},{2,3},{4,5},{6,7},{1,0},{3,2},{5,4},{7,6},{8,9},{10,11},{12,... | collective-permute-start | bytes 466952 | tf_op jit(solution)/shard_map/ppermute | solution.py:398
  18.8 6.4 %collective-permute-start.9 = (f32[37,8,128]{2,1,0:T(8,128)S(1)}, f32[37,8,128]{2,1,0:T(8,128)S(1)}, u32[]{:S(2)}, u32[]{:S(2)}) collective-permute-start(f32[37,8,128]{2,1,0:T(8,128)S(1)} %get-tuple-element.60), channel_id=1, source_target_pairs={{8,16},{24,0},{16,8},{0,24},{9,17},{25,1},{17,9},{1,25},{10,18},{2... | collective-permute-start | bytes 454664 | tf_op jit(solution)/shard_map/ppermute | solution.py:398
  18.8 9.2 %collective-permute-start.10 = (f32[36,8,128]{2,1,0:T(8,128)S(1)}, f32[36,8,128]{2,1,0:T(8,128)S(1)}, u32[]{:S(2)}, u32[]{:S(2)}) collective-permute-start(f32[36,8,128]{2,1,0:T(8,128)S(1)} %get-tuple-element.61), channel_id=1, source_target_pairs={{1,2},{3,4},{5,6},{2,1},{4,3},{6,5},{0,0},{7,7},{9,10},{11,12},{13... | collective-permute-start | bytes 442376 | tf_op jit(solution)/shard_map/ppermute | solution.py:398
  22.8 2.4 %collective-permute-start.8 = (f32[27,8,128]{2,1,0:T(8,128)S(1)}, f32[27,8,128]{2,1,0:T(8,128)S(1)}, u32[]{:S(2)}, u32[]{:S(2)}) collective-permute-start(f32[27,8,128]{2,1,0:T(8,128)S(1)} %get-tuple-element.59), channel_id=1, source_target_pairs={{0,8},{16,24},{8,0},{24,16},{1,9},{17,25},{9,1},{25,17},{2,10},{18... | collective-permute-start | bytes 331784 | tf_op jit(solution)/shard_map/ppermute | solution.py:398
  26.7 6.3 %collective-permute-start.11 = (f32[38,8,128]{2,1,0:T(8,128)S(1)}, f32[38,8,128]{2,1,0:T(8,128)S(1)}, u32[]{:S(2)}, u32[]{:S(2)}) collective-permute-start(f32[38,8,128]{2,1,0:T(8,128)S(1)} %get-tuple-element.65), channel_id=1, source_target_pairs={{0,1},{2,3},{4,5},{6,7},{1,0},{3,2},{5,4},{7,6},{8,9},{10,11},{12,... | collective-permute-start | bytes 466952 | tf_op jit(solution)/shard_map/ppermute | solution.py:398
  28.4 6.6 %collective-permute-start.13 = (f32[37,8,128]{2,1,0:T(8,128)S(1)}, f32[37,8,128]{2,1,0:T(8,128)S(1)}, u32[]{:S(2)}, u32[]{:S(2)}) collective-permute-start(f32[37,8,128]{2,1,0:T(8,128)S(1)} %get-tuple-element.70), channel_id=1, source_target_pairs={{8,16},{24,0},{16,8},{0,24},{9,17},{25,1},{17,9},{1,25},{10,18},{2... | collective-permute-start | bytes 454664 | tf_op jit(solution)/shard_map/ppermute | solution.py:398
  29.0 9.3 %collective-permute-start.14 = (f32[36,8,128]{2,1,0:T(8,128)S(1)}, f32[36,8,128]{2,1,0:T(8,128)S(1)}, u32[]{:S(2)}, u32[]{:S(2)}) collective-permute-start(f32[36,8,128]{2,1,0:T(8,128)S(1)} %get-tuple-element.71), channel_id=1, source_target_pairs={{1,2},{3,4},{5,6},{2,1},{4,3},{6,5},{0,0},{7,7},{9,10},{11,12},{13... | collective-permute-start | bytes 442376 | tf_op jit(solution)/shard_map/ppermute | solution.py:398
  32.9 2.1 %collective-permute-start.12 = (f32[27,8,128]{2,1,0:T(8,128)S(1)}, f32[27,8,128]{2,1,0:T(8,128)S(1)}, u32[]{:S(2)}, u32[]{:S(2)}) collective-permute-start(f32[27,8,128]{2,1,0:T(8,128)S(1)} %get-tuple-element.69), channel_id=1, source_target_pairs={{0,8},{16,24},{8,0},{24,16},{1,9},{17,25},{9,1},{25,17},{2,10},{18... | collective-permute-start | bytes 331784 | tf_op jit(solution)/shard_map/ppermute | solution.py:398

commit v20 on v16

--- a/solution.py
+++ b/solution.py
@@ -462,7 +462,7 @@
 
     (most,) = call(extremes_kernel, [wind], [shape(longest + 2)])
     other = spread(most, 1)
-    x_shapes = [shape(longest + 1), shape(longest)]
+    x_shapes = [shape(longest), shape(longest + 1)]
     x_out, x_last, t_out, t_last = call(opening_kernel, [values], x_shapes + [shape(middle)] * 2)
     far_shapes = [shape(short), shape(rim * planes), shape(middle)]
     for section in (1, 2, 3):

time: 40.2 us -> 39.9 us (level)
  waiting for transfers between devices: 4.91 us -> 4.2 us
    ppermute x12, waiting for transfers between devices: 3.36 us -> 2.17 us  [trade(): return lax.ppermute(value, axis, pairs)]
    ppermute x12, starting transfers between devices: 16.1 us -> 16.9 us  [trade(): return lax.ppermute(value, axis, pairs)]
    ppermute x3, waiting for transfers between devices: 1.55 us -> 2.03 us  [spread(): return lax.ppermute(most, 'gx', pairs)]
    ppermute x3, starting transfers between devices: 4.17 us -> 3.71 us  [spread(): return lax.ppermute(most, 'gx', pairs)]
  transfers between devices with their start and end apart: 15 -> 15, of which waited for: 7 -> 4; matrix products, arithmetic and copies ran while one was open for 0% -> 0% of each run, Pallas kernels for 28% -> 28%
where the time goes in v20:
time: 39.9 us; the launch traced here: 39.5 us
  starting transfers between devices  20.6 us (52%)
  Pallas kernels  12.8 us (32%)
  waiting for transfers between devices  4.2 us (11%)
  local copies, waits for them, and re-layouts  1.74 us (4%)
    ppermute x12, starting transfers between devices, trade(): return lax.ppermute(value, axis, pairs)  16.9 us
    pallas_call x15, Pallas kernels, call(): pl.pallas_call(kernel, out_shape=outs, in_specs=[vmem] * len(ins), out_sp...  12.8 us
    ppermute x3, starting transfers between devices, spread(): return lax.ppermute(most, 'gx', pairs)  3.71 us
    ppermute x12, waiting for transfers between devices, trade(): return lax.ppermute(value, axis, pairs)  2.17 us
    ppermute x3, waiting for transfers between devices, spread(): return lax.ppermute(most, 'gx', pairs)  2.03 us
    unnamed x14, local copies, waits for them, and re-layouts  1.74 us
  transfers between devices with their start and end apart: 15, of which 4 were waited for; matrix products, arithmetic and copies ran while one was open for 0% of the time, Pallas kernels for 28%

profile of v20, /device:TPU:8, one launch (start us, length us, event | category | flops | bytes accessed | tf_op | source)
XLA Modules:
  0.0 39.5 jit_solution(11095881156243892565)
XLA Ops:
  0.0 0.0 copy-start.3
  0.0 0.7 %copy-done.3 = f32[2,9,128]{2,0,1:T(2,128)S(1)} copy-done((f32[2,9,128]{2,0,1:T(2,128)S(1)}, f32[2,9,128]{2,0,1:T(2,128)}, u32[]{:S(2)}) %copy-start.3) | copy-done | bytes 9240
  0.7 1.6 %collective-permute-start = (f32[40,8,128]{2,1,0:T(8,128)S(1)}, f32[40,8,128]{2,1,0:T(8,128)S(1)}, u32[]{:S(2)}, u32[]{:S(2)}) collective-permute-start(f32[40,8,128]{2,1,0:T(8,128)S(1)} %shard_map.56.own_ref), channel_id=1, source_target_pairs={{0,1},{1,0},{2,3},{3,2},{4,5},{5,4},{6,7},{7,6},{8,9},{9,8},{10,11... | collective-permute-start | bytes 491528 | tf_op jit(solution)/shard_map/ppermute | solution.py:461
  2.3 0.0 copy-start
  2.3 1.0 %copy-done = f32[9,12,8,128]{3,2,1,0:T(8,128)S(1)} copy-done((f32[9,12,8,128]{3,2,1,0:T(8,128)S(1)}, f32[9,12,8,128]{3,2,1,0:T(8,128)}, u32[]{:S(2)}) %copy-start) | copy-done | bytes 442392
  3.3 0.0 copy-start.1
  3.3 2.1 %collective-permute-start.5 = (f32[39,8,128]{2,1,0:T(8,128)S(1)}, f32[39,8,128]{2,1,0:T(8,128)S(1)}, u32[]{:S(2)}, u32[]{:S(2)}) collective-permute-start(f32[39,8,128]{2,1,0:T(8,128)S(1)} %get-tuple-element.43), channel_id=1, source_target_pairs={{1,2},{3,4},{5,6},{2,1},{4,3},{6,5},{0,0},{7,7},{9,10},{11,12},{13... | collective-permute-start | bytes 479240 | tf_op jit(solution)/shard_map/ppermute | solution.py:398
  5.4 3.1 %collective-permute-start.4 = (f32[38,8,128]{2,1,0:T(8,128)S(1)}, f32[38,8,128]{2,1,0:T(8,128)S(1)}, u32[]{:S(2)}, u32[]{:S(2)}) collective-permute-start(f32[38,8,128]{2,1,0:T(8,128)S(1)} %get-tuple-element.42), channel_id=1, source_target_pairs={{0,1},{2,3},{4,5},{6,7},{1,0},{3,2},{5,4},{7,6},{8,9},{10,11},{12,... | collective-permute-start | bytes 466952 | tf_op jit(solution)/shard_map/ppermute | solution.py:398
  8.5 0.0 collective-permute-start.2
  8.5 0.0 copy-start.2
  8.5 0.0 copy-start.4
  8.5 1.6 %collective-permute-start.3 = (f32[37,8,128]{2,1,0:T(8,128)S(1)}, f32[37,8,128]{2,1,0:T(8,128)S(1)}, u32[]{:S(2)}, u32[]{:S(2)}) collective-permute-start(f32[37,8,128]{2,1,0:T(8,128)S(1)} %get-tuple-element.41), channel_id=1, source_target_pairs={{8,16},{24,0},{16,8},{0,24},{9,17},{25,1},{17,9},{1,25},{10,18},{2... | collective-permute-start | bytes 454664 | tf_op jit(solution)/shard_map/ppermute | solution.py:398
  10.1 0.0 collective-permute-done.other_ref
  10.1 0.5 %collective-permute-start.1 = (f32[8,128]{1,0:T(8,128)S(1)}, f32[8,128]{1,0:T(8,128)S(1)}, u32[]{:S(2)}, u32[]{:S(2)}) collective-permute-start(f32[8,128]{1,0:T(8,128)S(1)} %shard_map.57), channel_id=1, source_target_pairs={{0,2},{1,3},{2,0},{3,1},{4,6},{5,7},{6,4},{7,5},{8,10},{9,11},{10,... | collective-permute-start | bytes 12296 | tf_op jit(solution)/shard_map/ppermute | solution.py:461
  10.6 0.0 copy-done.1
  10.6 0.0 copy-done.2
  10.6 0.0 copy-done.4
  10.6 2.2 %shard_map.55 = (f32[9,12,8,128]{3,2,1,0:T(8,128)S(1)}, f32[9,12,8,128]{3,2,1,0:T(8,128)S(1)}, f32[9,12,8,128]{3,2,1,0:T(8,128)S(1)}, f32[7,128,128]{2,1,0:T(8,128)S(1)}) custom-call(f32[9,12,8,128]{3,2,1,0:T(8,128)S(1)} %copy-done.1, f32[9,2,128]{2,1,0:T(2,128)S(1)} %bitcast.2, f32[2,48,128]{2,1,0:T(8,128)S(1)} %copy-done.2), custom_call_target="tpu_custom_call" | custom-call | flops 33177600 | bytes 33177600 | tf_op jit(solution)/shard_map/pallas_call | solution.py:432
  12.7 1.0 %collective-permute-done.1 = f32[8,128]{1,0:T(8,128)S(1)} collective-permute-done((f32[8,128]{1,0:T(8,128)S(1)}, f32[8,128]{1,0:T(8,128)S(1)}, u32[]{:S(2)}, u32[]{:S(2)}) %collective-permute-start.1) | collective-permute-done | bytes 4128 | tf_op jit(solution)/shard_map/ppermute | solution.py:461
  13.7 1.7 %collective-permute-start.6 = (f32[8,128]{1,0:T(8,128)S(1)}, f32[8,128]{1,0:T(8,128)S(1)}, u32[]{:S(2)}, u32[]{:S(2)}) collective-permute-start(f32[8,128]{1,0:T(8,128)S(1)} %max.3.most_ref), channel_id=1, source_target_pairs={{0,4},{1,5},{2,6},{3,7},{4,0},{5,1},{6,2},{7,3},{8,12},{9,13},{10,... | collective-permute-start | bytes 12296 | tf_op jit(solution)/shard_map/ppermute | solution.py:461
  15.4 0.0 collective-permute-done.2.near_ref
  15.4 0.0 collective-permute-done.3.far_ref
  15.4 0.8 %shard_map.59.part_ref = f32[9,12,8,128]{3,2,1,0:T(8,128)S(1)} custom-call(f32[9,12,8,128]{3,2,1,0:T(8,128)S(1)} %copy-done.1, f32[9,12,8,128]{3,2,1,0:T(8,128)S(1)} %get-tuple-element.37.speed_ref, f32[9,12,8,128]{3,2,1,0:T(8,128)S(1)} %get-tuple-element.39.part_ref, f32[37,8,128]{2,1,0:T(8,128)S(1)} %collective-permute-done.2.near_ref, ...), custom_call_target="tpu_custom_call" | custom-call | tf_op jit(solution)/shard_map/pallas_call | solution.py:432
  16.2 0.0 collective-permute-done.4.near_ref
  16.2 0.0 collective-permute-done.5.far_ref
  16.3 0.0 copy-start.5
  16.3 0.0 copy-start.6
  16.3 0.9 %shard_map.60 = (f32[9,12,8,128]{3,2,1,0:T(8,128)S(1)}, f32[9,12,8,128]{3,2,1,0:T(8,128)S(1)}) custom-call(f32[9,12,8,128]{3,2,1,0:T(8,128)S(1)} %copy-done.1, f32[9,12,8,128]{3,2,1,0:T(8,128)S(1)} %shard_map.59.part_ref, f32[38,8,128]{2,1,0:T(8,128)S(1)} %collective-permute-done.4.near_ref, f32[39,8,128]{2,1,0:T(8,128)S(1)} %collective-permute-done.5.far_ref, ...), custom_call_target="tpu_custom_call" | custom-call | tf_op jit(solution)/shard_map/pallas_call | solution.py:432
  17.2 1.0 %collective-permute-done.6.other_ref = f32[8,128]{1,0:T(8,128)S(1)} collective-permute-done((f32[8,128]{1,0:T(8,128)S(1)}, f32[8,128]{1,0:T(8,128)S(1)}, u32[]{:S(2)}, u32[]{:S(2)}) %collective-permute-start.6) | collective-permute-done | bytes 4128 | tf_op jit(solution)/shard_map/ppermute | solution.py:461
  18.2 0.0 copy-done.5
  18.2 0.0 copy-done.6
  18.2 0.4 shard_map.61
  18.6 0.2 collective-permute-start.7
  18.8 0.0 collective-permute-start.9
  18.8 3.9 %collective-permute-start.10 = (f32[36,8,128]{2,1,0:T(8,128)S(1)}, f32[36,8,128]{2,1,0:T(8,128)S(1)}, u32[]{:S(2)}, u32[]{:S(2)}) collective-permute-start(f32[36,8,128]{2,1,0:T(8,128)S(1)} %get-tuple-element.57), channel_id=1, source_target_pairs={{1,2},{3,4},{5,6},{2,1},{4,3},{6,5},{0,0},{7,7},{9,10},{11,12},{13... | collective-permute-start | bytes 442376 | tf_op jit(solution)/shard_map/ppermute | solution.py:398
  22.7 0.4 %collective-permute-start.8 = (f32[27,8,128]{2,1,0:T(8,128)S(1)}, f32[27,8,128]{2,1,0:T(8,128)S(1)}, u32[]{:S(2)}, u32[]{:S(2)}) collective-permute-start(f32[27,8,128]{2,1,0:T(8,128)S(1)} %get-tuple-element.55), channel_id=1, source_target_pairs={{0,8},{16,24},{8,0},{24,16},{1,9},{17,25},{9,1},{25,17},{2,10},{18... | collective-permute-start | bytes 331784 | tf_op jit(solution)/shard_map/ppermute | solution.py:398
  23.2 2.0 %shard_map.62 = (f32[9,12,8,128]{3,2,1,0:T(8,128)S(1)}, f32[9,12,8,128]{3,2,1,0:T(8,128)S(1)}) custom-call(f32[9,12,8,128]{3,2,1,0:T(8,128)S(1)} %get-tuple-element.48.s_ref, f32[7,128,128]{2,1,0:T(8,128)S(1)} %get-tuple-element.49.rest_0_, f32[8,128]{1,0:T(8,128)S(1)} %get-tuple-element.50.rest_1_.pk_ref), custom_call_target="tpu_custom_call" | custom-call | tf_op jit(solution)/shard_map/pallas_call | solution.py:432
  25.2 0.0 collective-permute-done.7.ghosts_ref
  25.2 0.0 collective-permute-done.8.near_ref
  25.2 0.0 collective-permute-done.9.far_ref
  25.2 0.8 %shard_map.63.part_ref = f32[9,12,8,128]{3,2,1,0:T(8,128)S(1)} custom-call(f32[9,12,8,128]{3,2,1,0:T(8,128)S(1)} %get-tuple-element.48.s_ref, f32[9,12,8,128]{3,2,1,0:T(8,128)S(1)} %get-tuple-element.51.speed_ref, f32[9,12,8,128]{3,2,1,0:T(8,128)S(1)} %get-tuple-element.54.part_ref, f32[27,8,128]{2,1,0:T(8,128)S(1)} %collective-permute-done.8.near_ref, ...), custom_call_target="tpu_custom_call" | custom-call | flops 110592000 | bytes 110592000 | tf_op jit(solution)/shard_map/pallas_call | solution.py:432
  26.0 0.7 %shard_map.64 = (f32[9,12,8,128]{3,2,1,0:T(8,128)S(1)}, f32[38,8,128]{2,1,0:T(8,128)S(1)}) custom-call(f32[9,12,8,128]{3,2,1,0:T(8,128)S(1)} %copy-done.1, f32[9,12,8,128]{3,2,1,0:T(8,128)S(1)} %get-tuple-element.48.s_ref, f32[9,12,8,128]{3,2,1,0:T(8,128)S(1)} %shard_map.63.part_ref, f32[38,8,128]{2,1,0:T(8,128)S(1)} %collective-permute-done.7.ghosts_ref, ...), custom_call_target="tpu_custom_call" | custom-call | tf_op jit(solution)/shard_map/pallas_call | solution.py:432
  26.7 1.1 %collective-permute-start.11 = (f32[38,8,128]{2,1,0:T(8,128)S(1)}, f32[38,8,128]{2,1,0:T(8,128)S(1)}, u32[]{:S(2)}, u32[]{:S(2)}) collective-permute-start(f32[38,8,128]{2,1,0:T(8,128)S(1)} %get-tuple-element.61), channel_id=1, source_target_pairs={{0,1},{2,3},{4,5},{6,7},{1,0},{3,2},{5,4},{7,6},{8,9},{10,11},{12,... | collective-permute-start | bytes 466952 | tf_op jit(solution)/shard_map/ppermute | solution.py:398
  27.7 0.2 collective-permute-done.10.ghosts_ref
  28.0 0.4 %shard_map.65 = (f32[9,12,8,128]{3,2,1,0:T(8,128)S(1)}, f32[36,8,128]{2,1,0:T(8,128)S(1)}, f32[27,8,128]{2,1,0:T(8,128)S(1)}, f32[37,8,128]{2,1,0:T(8,128)S(1)}) custom-call(f32[9,12,8,128]{3,2,1,0:T(8,128)S(1)} %copy-done.1, f32[9,12,8,128]{3,2,1,0:T(8,128)S(1)} %get-tuple-element.48.s_ref, f32[9,12,8,128]{3,2,1,0:T(8,128)S(1)} %shard_map.63.part_ref, ...), custom_call_target="tpu_custom_call" | custom-call | tf_op jit(solution)/shard_map/pallas_call | solution.py:432
  28.4 0.7 %collective-permute-start.13 = (f32[37,8,128]{2,1,0:T(8,128)S(1)}, f32[37,8,128]{2,1,0:T(8,128)S(1)}, u32[]{:S(2)}, u32[]{:S(2)}) collective-permute-start(f32[37,8,128]{2,1,0:T(8,128)S(1)} %get-tuple-element.66), channel_id=1, source_target_pairs={{8,16},{24,0},{16,8},{0,24},{9,17},{25,1},{17,9},{1,25},{10,18},{2... | collective-permute-start | bytes 454664 | tf_op jit(solution)/shard_map/ppermute | solution.py:398
  29.0 3.8 %collective-permute-start.14 = (f32[36,8,128]{2,1,0:T(8,128)S(1)}, f32[36,8,128]{2,1,0:T(8,128)S(1)}, u32[]{:S(2)}, u32[]{:S(2)}) collective-permute-start(f32[36,8,128]{2,1,0:T(8,128)S(1)} %get-tuple-element.67), channel_id=1, source_target_pairs={{1,2},{3,4},{5,6},{2,1},{4,3},{6,5},{0,0},{7,7},{9,10},{11,12},{13... | collective-permute-start | bytes 442376 | tf_op jit(solution)/shard_map/ppermute | solution.py:398
  32.9 0.1 collective-permute-start.12
  33.0 0.0 collective-permute-done.11.ghosts_ref
  33.0 2.0 %shard_map.66 = (f32[9,12,8,128]{3,2,1,0:T(8,128)S(1)}, f32[9,12,8,128]{3,2,1,0:T(8,128)S(1)}) custom-call(f32[9,12,8,128]{3,2,1,0:T(8,128)S(1)} %get-tuple-element.62.s_ref, f32[7,128,128]{2,1,0:T(8,128)S(1)} %get-tuple-element.49.rest_0_, f32[8,128]{1,0:T(8,128)S(1)} %get-tuple-element.50.rest_1_.pk_ref), custom_call_target="tpu_custom_call" | custom-call | tf_op jit(solution)/shard_map/pallas_call | solution.py:432
  35.0 0.0 collective-permute-done.12.near_ref
  35.0 0.0 collective-permute-done.13.far_ref
  35.0 0.8 %shard_map.67.part_ref = f32[9,12,8,128]{3,2,1,0:T(8,128)S(1)} custom-call(f32[9,12,8,128]{3,2,1,0:T(8,128)S(1)} %get-tuple-element.62.s_ref, f32[9,12,8,128]{3,2,1,0:T(8,128)S(1)} %get-tuple-element.63.speed_ref, f32[9,12,8,128]{3,2,1,0:T(8,128)S(1)} %get-tuple-element.64.part_ref, f32[27,8,128]{2,1,0:T(8,128)S(1)} %collective-permute-done.12.near_ref, ...), custom_call_target="tpu_custom_call" | custom-call | flops 110592000 | bytes 110592000 | tf_op jit(solution)/shard_map/pallas_call | solution.py:432
  35.8 0.7 %shard_map.68.refs_0_ = f32[9,12,8,128]{3,2,1,0:T(8,128)S(1)} custom-call(f32[9,12,8,128]{3,2,1,0:T(8,128)S(1)} %copy-done.1, f32[9,12,8,128]{3,2,1,0:T(8,128)S(1)} %get-tuple-element.62.s_ref, f32[9,12,8,128]{3,2,1,0:T(8,128)S(1)} %shard_map.67.part_ref, f32[38,8,128]{2,1,0:T(8,128)S(1)} %collective-permute-done.11.ghosts_ref, f32[9,2,128]{2,1,0:T(2,128)S(1)} %bitcast.6, ...), custom_call_target="tpu_custom_call" | custom-call | tf_op jit(solution)/shard_map/pallas_call | solution.py:432
  36.5 1.9 %collective-permute-done.14.ghosts_ref = f32[36,8,128]{2,1,0:T(8,128)S(1)} collective-permute-done((f32[36,8,128]{2,1,0:T(8,128)S(1)}, f32[36,8,128]{2,1,0:T(8,128)S(1)}, u32[]{:S(2)}, u32[]{:S(2)}) %collective-permute-start.14) | collective-permute-done | bytes 147488 | tf_op jit(solution)/shard_map/ppermute | solution.py:398
  38.4 1.1 %shard_map.69 = f32[9,12,8,128]{3,2,1,0:T(8,128)} custom-call(f32[9,12,8,128]{3,2,1,0:T(8,128)S(1)} %copy-done.1, f32[9,12,8,128]{3,2,1,0:T(8,128)S(1)} %get-tuple-element.62.s_ref, f32[9,12,8,128]{3,2,1,0:T(8,128)S(1)} %shard_map.67.part_ref, f32[36,8,128]{2,1,0:T(8,128)S(1)} %collective-permute-done.14.ghosts_ref, f32[9,2,128]{2,1,0:T(2,128)S(1)} %bitcast.7, ...), custom_call_target="tpu_custom_call" | custom-call | tf_op jit(solution)/shard_map/pallas_call | solution.py:432
  (4 shorter events, 0.1 us)
Async XLA Ops:
  0.0 0.7 %copy-start.3 = (f32[2,9,128]{2,0,1:T(2,128)S(1)}, f32[2,9,128]{2,0,1:T(2,128)}, u32[]{:S(2)}) copy-start(f32[2,9,128]{2,0,1:T(2,128)} %param.6) | copy-start | bytes 27652
  0.7 9.4 %collective-permute-start = (f32[40,8,128]{2,1,0:T(8,128)S(1)}, f32[40,8,128]{2,1,0:T(8,128)S(1)}, u32[]{:S(2)}, u32[]{:S(2)}) collective-permute-start(f32[40,8,128]{2,1,0:T(8,128)S(1)} %shard_map.56.own_ref), channel_id=1, source_target_pairs={{0,1},{1,0},{2,3},{3,2},{4,5},{5,4},{6,7},{7,6},{8,9},{9,8},{10,11... | collective-permute-start | bytes 491528 | tf_op jit(solution)/shard_map/ppermute | solution.py:461
  2.3 1.0 %copy-start = (f32[9,12,8,128]{3,2,1,0:T(8,128)S(1)}, f32[9,12,8,128]{3,2,1,0:T(8,128)}, u32[]{:S(2)}) copy-start(f32[9,12,8,128]{3,2,1,0:T(8,128)} %base_ref.7) | copy-start | bytes 1327108
  3.3 7.3 %copy-start.1 = (f32[9,12,8,128]{3,2,1,0:T(8,128)S(1)}, f32[9,12,8,128]{3,2,1,0:T(8,128)}, u32[]{:S(2)}) copy-start(f32[9,12,8,128]{3,2,1,0:T(8,128)} %base_ref.7) | copy-start | bytes 1327108
  3.3 12.9 %collective-permute-start.5 = (f32[39,8,128]{2,1,0:T(8,128)S(1)}, f32[39,8,128]{2,1,0:T(8,128)S(1)}, u32[]{:S(2)}, u32[]{:S(2)}) collective-permute-start(f32[39,8,128]{2,1,0:T(8,128)S(1)} %get-tuple-element.43), channel_id=1, source_target_pairs={{1,2},{3,4},{5,6},{2,1},{4,3},{6,5},{0,0},{7,7},{9,10},{11,12},{13... | collective-permute-start | bytes 479240 | tf_op jit(solution)/shard_map/ppermute | solution.py:398
  5.4 10.8 %collective-permute-start.4 = (f32[38,8,128]{2,1,0:T(8,128)S(1)}, f32[38,8,128]{2,1,0:T(8,128)S(1)}, u32[]{:S(2)}, u32[]{:S(2)}) collective-permute-start(f32[38,8,128]{2,1,0:T(8,128)S(1)} %get-tuple-element.42), channel_id=1, source_target_pairs={{0,1},{2,3},{4,5},{6,7},{1,0},{3,2},{5,4},{7,6},{8,9},{10,11},{12,... | collective-permute-start | bytes 466952 | tf_op jit(solution)/shard_map/ppermute | solution.py:398
  8.5 6.9 %collective-permute-start.2 = (f32[37,8,128]{2,1,0:T(8,128)S(1)}, f32[37,8,128]{2,1,0:T(8,128)S(1)}, u32[]{:S(2)}, u32[]{:S(2)}) collective-permute-start(f32[37,8,128]{2,1,0:T(8,128)S(1)} %get-tuple-element.40), channel_id=1, source_target_pairs={{0,8},{16,24},{8,0},{24,16},{1,9},{17,25},{9,1},{25,17},{2,10},{18... | collective-permute-start | bytes 454664 | tf_op jit(solution)/shard_map/ppermute | solution.py:398
  8.5 2.1 %copy-start.2 = (f32[2,48,128]{2,1,0:T(8,128)S(1)}, f32[2,48,128]{2,1,0:T(8,128)}, u32[]{:S(2)}) copy-start(f32[2,48,128]{2,1,0:T(8,128)} %constant.2.clone.rest_1_.waves_ref) | copy-start | bytes 147460
  8.5 2.1 %copy-start.4 = (f32[2,9,128]{2,0,1:T(2,128)S(1)}, f32[2,9,128]{2,0,1:T(2,128)}, u32[]{:S(2)}) copy-start(f32[2,9,128]{2,0,1:T(2,128)} %param.6) | copy-start | bytes 27652
  8.5 6.9 %collective-permute-start.3 = (f32[37,8,128]{2,1,0:T(8,128)S(1)}, f32[37,8,128]{2,1,0:T(8,128)S(1)}, u32[]{:S(2)}, u32[]{:S(2)}) collective-permute-start(f32[37,8,128]{2,1,0:T(8,128)S(1)} %get-tuple-element.41), channel_id=1, source_target_pairs={{8,16},{24,0},{16,8},{0,24},{9,17},{25,1},{17,9},{1,25},{10,18},{2... | collective-permute-start | bytes 454664 | tf_op jit(solution)/shard_map/ppermute | solution.py:398
  10.1 3.6 %collective-permute-start.1 = (f32[8,128]{1,0:T(8,128)S(1)}, f32[8,128]{1,0:T(8,128)S(1)}, u32[]{:S(2)}, u32[]{:S(2)}) collective-permute-start(f32[8,128]{1,0:T(8,128)S(1)} %shard_map.57), channel_id=1, source_target_pairs={{0,2},{1,3},{2,0},{3,1},{4,6},{5,7},{6,4},{7,5},{8,10},{9,11},{10,... | collective-permute-start | bytes 12296 | tf_op jit(solution)/shard_map/ppermute | solution.py:461
  13.7 4.5 %collective-permute-start.6 = (f32[8,128]{1,0:T(8,128)S(1)}, f32[8,128]{1,0:T(8,128)S(1)}, u32[]{:S(2)}, u32[]{:S(2)}) collective-permute-start(f32[8,128]{1,0:T(8,128)S(1)} %max.3.most_ref), channel_id=1, source_target_pairs={{0,4},{1,5},{2,6},{3,7},{4,0},{5,1},{6,2},{7,3},{8,12},{9,13},{10,... | collective-permute-start | bytes 12296 | tf_op jit(solution)/shard_map/ppermute | solution.py:461
  16.3 2.0 %copy-start.5 = (s32[9,128]{1,0:T(8,128)S(1)}, s32[9,128]{1,0:T(8,128)}, u32[]{:S(2)}) copy-start(s32[9,128]{1,0:T(8,128)} %mask_ref.9) | copy-start | bytes 13828
  16.3 2.0 %copy-start.6 = (f32[9,128]{1,0:T(8,128)S(1)}, f32[9,128]{1,0:T(8,128)}, u32[]{:S(2)}) copy-start(f32[9,128]{1,0:T(8,128)} %depth_ref.9) | copy-start | bytes 13828
  18.6 6.5 %collective-permute-start.7 = (f32[38,8,128]{2,1,0:T(8,128)S(1)}, f32[38,8,128]{2,1,0:T(8,128)S(1)}, u32[]{:S(2)}, u32[]{:S(2)}) collective-permute-start(f32[38,8,128]{2,1,0:T(8,128)S(1)} %get-tuple-element.53), channel_id=1, source_target_pairs={{0,1},{2,3},{4,5},{6,7},{1,0},{3,2},{5,4},{7,6},{8,9},{10,11},{12,... | collective-permute-start | bytes 466952 | tf_op jit(solution)/shard_map/ppermute | solution.py:398
  18.8 6.4 %collective-permute-start.9 = (f32[37,8,128]{2,1,0:T(8,128)S(1)}, f32[37,8,128]{2,1,0:T(8,128)S(1)}, u32[]{:S(2)}, u32[]{:S(2)}) collective-permute-start(f32[37,8,128]{2,1,0:T(8,128)S(1)} %get-tuple-element.56), channel_id=1, source_target_pairs={{8,16},{24,0},{16,8},{0,24},{9,17},{25,1},{17,9},{1,25},{10,18},{2... | collective-permute-start | bytes 454664 | tf_op jit(solution)/shard_map/ppermute | solution.py:398
  18.8 9.2 %collective-permute-start.10 = (f32[36,8,128]{2,1,0:T(8,128)S(1)}, f32[36,8,128]{2,1,0:T(8,128)S(1)}, u32[]{:S(2)}, u32[]{:S(2)}) collective-permute-start(f32[36,8,128]{2,1,0:T(8,128)S(1)} %get-tuple-element.57), channel_id=1, source_target_pairs={{1,2},{3,4},{5,6},{2,1},{4,3},{6,5},{0,0},{7,7},{9,10},{11,12},{13... | collective-permute-start | bytes 442376 | tf_op jit(solution)/shard_map/ppermute | solution.py:398
  22.7 2.4 %collective-permute-start.8 = (f32[27,8,128]{2,1,0:T(8,128)S(1)}, f32[27,8,128]{2,1,0:T(8,128)S(1)}, u32[]{:S(2)}, u32[]{:S(2)}) collective-permute-start(f32[27,8,128]{2,1,0:T(8,128)S(1)} %get-tuple-element.55), channel_id=1, source_target_pairs={{0,8},{16,24},{8,0},{24,16},{1,9},{17,25},{9,1},{25,17},{2,10},{18... | collective-permute-start | bytes 331784 | tf_op jit(solution)/shard_map/ppermute | solution.py:398
  26.7 6.3 %collective-permute-start.11 = (f32[38,8,128]{2,1,0:T(8,128)S(1)}, f32[38,8,128]{2,1,0:T(8,128)S(1)}, u32[]{:S(2)}, u32[]{:S(2)}) collective-permute-start(f32[38,8,128]{2,1,0:T(8,128)S(1)} %get-tuple-element.61), channel_id=1, source_target_pairs={{0,1},{2,3},{4,5},{6,7},{1,0},{3,2},{5,4},{7,6},{8,9},{10,11},{12,... | collective-permute-start | bytes 466952 | tf_op jit(solution)/shard_map/ppermute | solution.py:398
  28.4 6.6 %collective-permute-start.13 = (f32[37,8,128]{2,1,0:T(8,128)S(1)}, f32[37,8,128]{2,1,0:T(8,128)S(1)}, u32[]{:S(2)}, u32[]{:S(2)}) collective-permute-start(f32[37,8,128]{2,1,0:T(8,128)S(1)} %get-tuple-element.66), channel_id=1, source_target_pairs={{8,16},{24,0},{16,8},{0,24},{9,17},{25,1},{17,9},{1,25},{10,18},{2... | collective-permute-start | bytes 454664 | tf_op jit(solution)/shard_map/ppermute | solution.py:398
  29.0 9.3 %collective-permute-start.14 = (f32[36,8,128]{2,1,0:T(8,128)S(1)}, f32[36,8,128]{2,1,0:T(8,128)S(1)}, u32[]{:S(2)}, u32[]{:S(2)}) collective-permute-start(f32[36,8,128]{2,1,0:T(8,128)S(1)} %get-tuple-element.67), channel_id=1, source_target_pairs={{1,2},{3,4},{5,6},{2,1},{4,3},{6,5},{0,0},{7,7},{9,10},{11,12},{13... | collective-permute-start | bytes 442376 | tf_op jit(solution)/shard_map/ppermute | solution.py:398
  32.9 2.1 %collective-permute-start.12 = (f32[27,8,128]{2,1,0:T(8,128)S(1)}, f32[27,8,128]{2,1,0:T(8,128)S(1)}, u32[]{:S(2)}, u32[]{:S(2)}) collective-permute-start(f32[27,8,128]{2,1,0:T(8,128)S(1)} %get-tuple-element.65), channel_id=1, source_target_pairs={{0,8},{16,24},{8,0},{24,16},{1,9},{17,25},{9,1},{25,17},{2,10},{18... | collective-permute-start | bytes 331784 | tf_op jit(solution)/shard_map/ppermute | solution.py:398

commit v21 on v20

--- a/solution.py
+++ b/solution.py
@@ -295,7 +295,7 @@
     pace = speeds_of(tile, speed_step) * side
     first = lax.axis_index("head") * headings
     low, high = span
-    wide = batches(headings, max(1, 72 // (high - low)))
+    wide = batches(headings, max(1, 108 // (high - low)))
 
     def line(i, j):
         if i < 0:
@@ -342,13 +342,17 @@
     peak_y = splat(pk_ref[1:2, :] * gain, tile)
     time_step = splat(pk_ref[2:3, :], tile)
 
-    def plane(i, carry):
-        for j in range(headings):
-            rate = part_ref[i, j] + (gap_x_ref[i, j] * peak_x + gap_y_ref[i, j] * peak_y)
-            out_ref[i, j] = jnp.minimum(s_ref[i, j] + time_step * rate, target_ref[i])
+    wide = batches(planes, 3)
+
+    def step(n, carry):
+        for w in range(wide):
+            i = n * wide + w
+            for j in range(headings):
+                rate = part_ref[i, j] + (gap_x_ref[i, j] * peak_x + gap_y_ref[i, j] * peak_y)
+                out_ref[i, j] = jnp.minimum(s_ref[i, j] + time_step * rate, target_ref[i])
         return carry
 
-    lax.fori_loop(0, planes, plane, 0)
+    lax.fori_loop(0, planes // wide, step, 0)
     cut_near(out_ref, x_near)
     cut_far(out_ref, x_far)
     cut_headings(out_ref, t_near, t_far)

time: 39.9 us -> 39.8 us (level)
  no operation moved by 1% of the time
where the time goes in v21:
time: 39.8 us; the launch traced here: 39.5 us
  starting transfers between devices  20.6 us (52%)
  Pallas kernels  12.7 us (32%)
  waiting for transfers between devices  4.28 us (11%)
  local copies, waits for them, and re-layouts  1.74 us (4%)
    ppermute x12, starting transfers between devices, trade(): return lax.ppermute(value, axis, pairs)  16.9 us
    pallas_call x15, Pallas kernels, call(): pl.pallas_call(kernel, out_shape=outs, in_specs=[vmem] * len(ins), out_sp...  12.7 us
    ppermute x3, starting transfers between devices, spread(): return lax.ppermute(most, 'gx', pairs)  3.71 us
    ppermute x12, waiting for transfers between devices, trade(): return lax.ppermute(value, axis, pairs)  2.17 us
    ppermute x3, waiting for transfers between devices, spread(): return lax.ppermute(most, 'gx', pairs)  2.11 us
    unnamed x14, local copies, waits for them, and re-layouts  1.74 us
  transfers between devices with their start and end apart: 15, of which 4 were waited for; matrix products, arithmetic and copies ran while one was open for 0% of the time, Pallas kernels for 28%

profile of v21, /device:TPU:8, one launch (start us, length us, event | category | flops | bytes accessed | tf_op | source)
XLA Modules:
  0.0 39.5 jit_solution(4638321848284215902)
XLA Ops:
  0.0 0.0 copy-start.3
  0.0 0.7 %copy-done.3 = f32[2,9,128]{2,0,1:T(2,128)S(1)} copy-done((f32[2,9,128]{2,0,1:T(2,128)S(1)}, f32[2,9,128]{2,0,1:T(2,128)}, u32[]{:S(2)}) %copy-start.3) | copy-done | bytes 9240
  0.7 1.6 %collective-permute-start = (f32[40,8,128]{2,1,0:T(8,128)S(1)}, f32[40,8,128]{2,1,0:T(8,128)S(1)}, u32[]{:S(2)}, u32[]{:S(2)}) collective-permute-start(f32[40,8,128]{2,1,0:T(8,128)S(1)} %shard_map.56.own_ref), channel_id=1, source_target_pairs={{0,1},{1,0},{2,3},{3,2},{4,5},{5,4},{6,7},{7,6},{8,9},{9,8},{10,11... | collective-permute-start | bytes 491528 | tf_op jit(solution)/shard_map/ppermute | solution.py:465
  2.3 0.0 copy-start
  2.3 1.0 %copy-done = f32[9,12,8,128]{3,2,1,0:T(8,128)S(1)} copy-done((f32[9,12,8,128]{3,2,1,0:T(8,128)S(1)}, f32[9,12,8,128]{3,2,1,0:T(8,128)}, u32[]{:S(2)}) %copy-start) | copy-done | bytes 442392
  3.3 0.0 copy-start.1
  3.3 2.1 %collective-permute-start.5 = (f32[39,8,128]{2,1,0:T(8,128)S(1)}, f32[39,8,128]{2,1,0:T(8,128)S(1)}, u32[]{:S(2)}, u32[]{:S(2)}) collective-permute-start(f32[39,8,128]{2,1,0:T(8,128)S(1)} %get-tuple-element.43), channel_id=1, source_target_pairs={{1,2},{3,4},{5,6},{2,1},{4,3},{6,5},{0,0},{7,7},{9,10},{11,12},{13... | collective-permute-start | bytes 479240 | tf_op jit(solution)/shard_map/ppermute | solution.py:402
  5.4 3.1 %collective-permute-start.4 = (f32[38,8,128]{2,1,0:T(8,128)S(1)}, f32[38,8,128]{2,1,0:T(8,128)S(1)}, u32[]{:S(2)}, u32[]{:S(2)}) collective-permute-start(f32[38,8,128]{2,1,0:T(8,128)S(1)} %get-tuple-element.42), channel_id=1, source_target_pairs={{0,1},{2,3},{4,5},{6,7},{1,0},{3,2},{5,4},{7,6},{8,9},{10,11},{12,... | collective-permute-start | bytes 466952 | tf_op jit(solution)/shard_map/ppermute | solution.py:402
  8.5 0.0 collective-permute-start.2
  8.5 0.0 copy-start.2
  8.5 0.0 copy-start.4
  8.5 1.6 %collective-permute-start.3 = (f32[37,8,128]{2,1,0:T(8,128)S(1)}, f32[37,8,128]{2,1,0:T(8,128)S(1)}, u32[]{:S(2)}, u32[]{:S(2)}) collective-permute-start(f32[37,8,128]{2,1,0:T(8,128)S(1)} %get-tuple-element.41), channel_id=1, source_target_pairs={{8,16},{24,0},{16,8},{0,24},{9,17},{25,1},{17,9},{1,25},{10,18},{2... | collective-permute-start | bytes 454664 | tf_op jit(solution)/shard_map/ppermute | solution.py:402
  10.1 0.0 collective-permute-done.other_ref
  10.1 0.5 %collective-permute-start.1 = (f32[8,128]{1,0:T(8,128)S(1)}, f32[8,128]{1,0:T(8,128)S(1)}, u32[]{:S(2)}, u32[]{:S(2)}) collective-permute-start(f32[8,128]{1,0:T(8,128)S(1)} %shard_map.57), channel_id=1, source_target_pairs={{0,2},{1,3},{2,0},{3,1},{4,6},{5,7},{6,4},{7,5},{8,10},{9,11},{10,... | collective-permute-start | bytes 12296 | tf_op jit(solution)/shard_map/ppermute | solution.py:465
  10.6 0.0 copy-done.1
  10.6 0.0 copy-done.2
  10.6 0.0 copy-done.4
  10.6 2.2 %shard_map.55 = (f32[9,12,8,128]{3,2,1,0:T(8,128)S(1)}, f32[9,12,8,128]{3,2,1,0:T(8,128)S(1)}, f32[9,12,8,128]{3,2,1,0:T(8,128)S(1)}, f32[7,128,128]{2,1,0:T(8,128)S(1)}) custom-call(f32[9,12,8,128]{3,2,1,0:T(8,128)S(1)} %copy-done.1, f32[9,2,128]{2,1,0:T(2,128)S(1)} %bitcast.2, f32[2,48,128]{2,1,0:T(8,128)S(1)} %copy-done.2), custom_call_target="tpu_custom_call" | custom-call | flops 33177600 | bytes 33177600 | tf_op jit(solution)/shard_map/pallas_call | solution.py:436
  12.7 1.0 %collective-permute-done.1 = f32[8,128]{1,0:T(8,128)S(1)} collective-permute-done((f32[8,128]{1,0:T(8,128)S(1)}, f32[8,128]{1,0:T(8,128)S(1)}, u32[]{:S(2)}, u32[]{:S(2)}) %collective-permute-start.1) | collective-permute-done | bytes 4128 | tf_op jit(solution)/shard_map/ppermute | solution.py:465
  13.7 1.7 %collective-permute-start.6 = (f32[8,128]{1,0:T(8,128)S(1)}, f32[8,128]{1,0:T(8,128)S(1)}, u32[]{:S(2)}, u32[]{:S(2)}) collective-permute-start(f32[8,128]{1,0:T(8,128)S(1)} %max.3.most_ref), channel_id=1, source_target_pairs={{0,4},{1,5},{2,6},{3,7},{4,0},{5,1},{6,2},{7,3},{8,12},{9,13},{10,... | collective-permute-start | bytes 12296 | tf_op jit(solution)/shard_map/ppermute | solution.py:465
  15.4 0.0 collective-permute-done.2.near_ref
  15.4 0.0 collective-permute-done.3.far_ref
  15.4 0.8 %shard_map.59.part_ref = f32[9,12,8,128]{3,2,1,0:T(8,128)S(1)} custom-call(f32[9,12,8,128]{3,2,1,0:T(8,128)S(1)} %copy-done.1, f32[9,12,8,128]{3,2,1,0:T(8,128)S(1)} %get-tuple-element.37.speed_ref, f32[9,12,8,128]{3,2,1,0:T(8,128)S(1)} %get-tuple-element.39.part_ref, f32[37,8,128]{2,1,0:T(8,128)S(1)} %collective-permute-done.2.near_ref, ...), custom_call_target="tpu_custom_call" | custom-call | tf_op jit(solution)/shard_map/pallas_call | solution.py:436
  16.2 0.0 collective-permute-done.4.near_ref
  16.2 0.0 collective-permute-done.5.far_ref
  16.3 0.0 copy-start.5
  16.3 0.0 copy-start.6
  16.3 0.8 %shard_map.60 = (f32[9,12,8,128]{3,2,1,0:T(8,128)S(1)}, f32[9,12,8,128]{3,2,1,0:T(8,128)S(1)}) custom-call(f32[9,12,8,128]{3,2,1,0:T(8,128)S(1)} %copy-done.1, f32[9,12,8,128]{3,2,1,0:T(8,128)S(1)} %shard_map.59.part_ref, f32[38,8,128]{2,1,0:T(8,128)S(1)} %collective-permute-done.4.near_ref, f32[39,8,128]{2,1,0:T(8,128)S(1)} %collective-permute-done.5.far_ref, ...), custom_call_target="tpu_custom_call" | custom-call | tf_op jit(solution)/shard_map/pallas_call | solution.py:436
  17.1 1.1 %collective-permute-done.6.other_ref = f32[8,128]{1,0:T(8,128)S(1)} collective-permute-done((f32[8,128]{1,0:T(8,128)S(1)}, f32[8,128]{1,0:T(8,128)S(1)}, u32[]{:S(2)}, u32[]{:S(2)}) %collective-permute-start.6) | collective-permute-done | bytes 4128 | tf_op jit(solution)/shard_map/ppermute | solution.py:465
  18.2 0.0 copy-done.5
  18.2 0.0 copy-done.6
  18.2 0.3 shard_map.61
  18.6 0.2 collective-permute-start.7
  18.8 0.0 collective-permute-start.9
  18.8 3.9 %collective-permute-start.10 = (f32[36,8,128]{2,1,0:T(8,128)S(1)}, f32[36,8,128]{2,1,0:T(8,128)S(1)}, u32[]{:S(2)}, u32[]{:S(2)}) collective-permute-start(f32[36,8,128]{2,1,0:T(8,128)S(1)} %get-tuple-element.57), channel_id=1, source_target_pairs={{1,2},{3,4},{5,6},{2,1},{4,3},{6,5},{0,0},{7,7},{9,10},{11,12},{13... | collective-permute-start | bytes 442376 | tf_op jit(solution)/shard_map/ppermute | solution.py:402
  22.7 0.4 %collective-permute-start.8 = (f32[27,8,128]{2,1,0:T(8,128)S(1)}, f32[27,8,128]{2,1,0:T(8,128)S(1)}, u32[]{:S(2)}, u32[]{:S(2)}) collective-permute-start(f32[27,8,128]{2,1,0:T(8,128)S(1)} %get-tuple-element.55), channel_id=1, source_target_pairs={{0,8},{16,24},{8,0},{24,16},{1,9},{17,25},{9,1},{25,17},{2,10},{18... | collective-permute-start | bytes 331784 | tf_op jit(solution)/shard_map/ppermute | solution.py:402
  23.1 2.0 %shard_map.62 = (f32[9,12,8,128]{3,2,1,0:T(8,128)S(1)}, f32[9,12,8,128]{3,2,1,0:T(8,128)S(1)}) custom-call(f32[9,12,8,128]{3,2,1,0:T(8,128)S(1)} %get-tuple-element.48.s_ref, f32[7,128,128]{2,1,0:T(8,128)S(1)} %get-tuple-element.49.rest_0_, f32[8,128]{1,0:T(8,128)S(1)} %get-tuple-element.50.rest_1_.pk_ref), custom_call_target="tpu_custom_call" | custom-call | tf_op jit(solution)/shard_map/pallas_call | solution.py:436
  25.1 0.0 collective-permute-done.7.ghosts_ref
  25.1 0.0 collective-permute-done.8.near_ref
  25.1 0.0 collective-permute-done.9.far_ref
  25.1 0.8 %shard_map.63.part_ref = f32[9,12,8,128]{3,2,1,0:T(8,128)S(1)} custom-call(f32[9,12,8,128]{3,2,1,0:T(8,128)S(1)} %get-tuple-element.48.s_ref, f32[9,12,8,128]{3,2,1,0:T(8,128)S(1)} %get-tuple-element.51.speed_ref, f32[9,12,8,128]{3,2,1,0:T(8,128)S(1)} %get-tuple-element.54.part_ref, f32[27,8,128]{2,1,0:T(8,128)S(1)} %collective-permute-done.8.near_ref, ...), custom_call_target="tpu_custom_call" | custom-call | flops 110592000 | bytes 110592000 | tf_op jit(solution)/shard_map/pallas_call | solution.py:436
  26.0 0.7 %shard_map.64 = (f32[9,12,8,128]{3,2,1,0:T(8,128)S(1)}, f32[38,8,128]{2,1,0:T(8,128)S(1)}) custom-call(f32[9,12,8,128]{3,2,1,0:T(8,128)S(1)} %copy-done.1, f32[9,12,8,128]{3,2,1,0:T(8,128)S(1)} %get-tuple-element.48.s_ref, f32[9,12,8,128]{3,2,1,0:T(8,128)S(1)} %shard_map.63.part_ref, f32[38,8,128]{2,1,0:T(8,128)S(1)} %collective-permute-done.7.ghosts_ref, ...), custom_call_target="tpu_custom_call" | custom-call | tf_op jit(solution)/shard_map/pallas_call | solution.py:436
  26.6 1.1 %collective-permute-start.11 = (f32[38,8,128]{2,1,0:T(8,128)S(1)}, f32[38,8,128]{2,1,0:T(8,128)S(1)}, u32[]{:S(2)}, u32[]{:S(2)}) collective-permute-start(f32[38,8,128]{2,1,0:T(8,128)S(1)} %get-tuple-element.61), channel_id=1, source_target_pairs={{0,1},{2,3},{4,5},{6,7},{1,0},{3,2},{5,4},{7,6},{8,9},{10,11},{12,... | collective-permute-start | bytes 466952 | tf_op jit(solution)/shard_map/ppermute | solution.py:402
  27.7 0.2 collective-permute-done.10.ghosts_ref
  27.9 0.4 %shard_map.65 = (f32[9,12,8,128]{3,2,1,0:T(8,128)S(1)}, f32[36,8,128]{2,1,0:T(8,128)S(1)}, f32[27,8,128]{2,1,0:T(8,128)S(1)}, f32[37,8,128]{2,1,0:T(8,128)S(1)}) custom-call(f32[9,12,8,128]{3,2,1,0:T(8,128)S(1)} %copy-done.1, f32[9,12,8,128]{3,2,1,0:T(8,128)S(1)} %get-tuple-element.48.s_ref, f32[9,12,8,128]{3,2,1,0:T(8,128)S(1)} %shard_map.63.part_ref, ...), custom_call_target="tpu_custom_call" | custom-call | tf_op jit(solution)/shard_map/pallas_call | solution.py:436
  28.4 0.7 %collective-permute-start.13 = (f32[37,8,128]{2,1,0:T(8,128)S(1)}, f32[37,8,128]{2,1,0:T(8,128)S(1)}, u32[]{:S(2)}, u32[]{:S(2)}) collective-permute-start(f32[37,8,128]{2,1,0:T(8,128)S(1)} %get-tuple-element.66), channel_id=1, source_target_pairs={{8,16},{24,0},{16,8},{0,24},{9,17},{25,1},{17,9},{1,25},{10,18},{2... | collective-permute-start | bytes 454664 | tf_op jit(solution)/shard_map/ppermute | solution.py:402
  29.0 3.8 %collective-permute-start.14 = (f32[36,8,128]{2,1,0:T(8,128)S(1)}, f32[36,8,128]{2,1,0:T(8,128)S(1)}, u32[]{:S(2)}, u32[]{:S(2)}) collective-permute-start(f32[36,8,128]{2,1,0:T(8,128)S(1)} %get-tuple-element.67), channel_id=1, source_target_pairs={{1,2},{3,4},{5,6},{2,1},{4,3},{6,5},{0,0},{7,7},{9,10},{11,12},{13... | collective-permute-start | bytes 442376 | tf_op jit(solution)/shard_map/ppermute | solution.py:402
  32.8 0.1 collective-permute-start.12
  32.9 0.0 collective-permute-done.11.ghosts_ref
  32.9 2.0 %shard_map.66 = (f32[9,12,8,128]{3,2,1,0:T(8,128)S(1)}, f32[9,12,8,128]{3,2,1,0:T(8,128)S(1)}) custom-call(f32[9,12,8,128]{3,2,1,0:T(8,128)S(1)} %get-tuple-element.62.s_ref, f32[7,128,128]{2,1,0:T(8,128)S(1)} %get-tuple-element.49.rest_0_, f32[8,128]{1,0:T(8,128)S(1)} %get-tuple-element.50.rest_1_.pk_ref), custom_call_target="tpu_custom_call" | custom-call | tf_op jit(solution)/shard_map/pallas_call | solution.py:436
  34.9 0.0 collective-permute-done.12.near_ref
  34.9 0.0 collective-permute-done.13.far_ref
  34.9 0.8 %shard_map.67.part_ref = f32[9,12,8,128]{3,2,1,0:T(8,128)S(1)} custom-call(f32[9,12,8,128]{3,2,1,0:T(8,128)S(1)} %get-tuple-element.62.s_ref, f32[9,12,8,128]{3,2,1,0:T(8,128)S(1)} %get-tuple-element.63.speed_ref, f32[9,12,8,128]{3,2,1,0:T(8,128)S(1)} %get-tuple-element.64.part_ref, f32[27,8,128]{2,1,0:T(8,128)S(1)} %collective-permute-done.12.near_ref, ...), custom_call_target="tpu_custom_call" | custom-call | flops 110592000 | bytes 110592000 | tf_op jit(solution)/shard_map/pallas_call | solution.py:436
  35.8 0.7 %shard_map.68.refs_0_ = f32[9,12,8,128]{3,2,1,0:T(8,128)S(1)} custom-call(f32[9,12,8,128]{3,2,1,0:T(8,128)S(1)} %copy-done.1, f32[9,12,8,128]{3,2,1,0:T(8,128)S(1)} %get-tuple-element.62.s_ref, f32[9,12,8,128]{3,2,1,0:T(8,128)S(1)} %shard_map.67.part_ref, f32[38,8,128]{2,1,0:T(8,128)S(1)} %collective-permute-done.11.ghosts_ref, f32[9,2,128]{2,1,0:T(2,128)S(1)} %bitcast.6, ...), custom_call_target="tpu_custom_call" | custom-call | tf_op jit(solution)/shard_map/pallas_call | solution.py:436
  36.4 1.9 %collective-permute-done.14.ghosts_ref = f32[36,8,128]{2,1,0:T(8,128)S(1)} collective-permute-done((f32[36,8,128]{2,1,0:T(8,128)S(1)}, f32[36,8,128]{2,1,0:T(8,128)S(1)}, u32[]{:S(2)}, u32[]{:S(2)}) %collective-permute-start.14) | collective-permute-done | bytes 147488 | tf_op jit(solution)/shard_map/ppermute | solution.py:402
  38.3 1.1 %shard_map.69 = f32[9,12,8,128]{3,2,1,0:T(8,128)} custom-call(f32[9,12,8,128]{3,2,1,0:T(8,128)S(1)} %copy-done.1, f32[9,12,8,128]{3,2,1,0:T(8,128)S(1)} %get-tuple-element.62.s_ref, f32[9,12,8,128]{3,2,1,0:T(8,128)S(1)} %shard_map.67.part_ref, f32[36,8,128]{2,1,0:T(8,128)S(1)} %collective-permute-done.14.ghosts_ref, f32[9,2,128]{2,1,0:T(2,128)S(1)} %bitcast.7, ...), custom_call_target="tpu_custom_call" | custom-call | tf_op jit(solution)/shard_map/pallas_call | solution.py:436
  (4 shorter events, 0.1 us)
Async XLA Ops:
  0.0 0.7 %copy-start.3 = (f32[2,9,128]{2,0,1:T(2,128)S(1)}, f32[2,9,128]{2,0,1:T(2,128)}, u32[]{:S(2)}) copy-start(f32[2,9,128]{2,0,1:T(2,128)} %param.6) | copy-start | bytes 27652
  0.7 9.4 %collective-permute-start = (f32[40,8,128]{2,1,0:T(8,128)S(1)}, f32[40,8,128]{2,1,0:T(8,128)S(1)}, u32[]{:S(2)}, u32[]{:S(2)}) collective-permute-start(f32[40,8,128]{2,1,0:T(8,128)S(1)} %shard_map.56.own_ref), channel_id=1, source_target_pairs={{0,1},{1,0},{2,3},{3,2},{4,5},{5,4},{6,7},{7,6},{8,9},{9,8},{10,11... | collective-permute-start | bytes 491528 | tf_op jit(solution)/shard_map/ppermute | solution.py:465
  2.3 1.0 %copy-start = (f32[9,12,8,128]{3,2,1,0:T(8,128)S(1)}, f32[9,12,8,128]{3,2,1,0:T(8,128)}, u32[]{:S(2)}) copy-start(f32[9,12,8,128]{3,2,1,0:T(8,128)} %base_ref.7) | copy-start | bytes 1327108
  3.3 7.3 %copy-start.1 = (f32[9,12,8,128]{3,2,1,0:T(8,128)S(1)}, f32[9,12,8,128]{3,2,1,0:T(8,128)}, u32[]{:S(2)}) copy-start(f32[9,12,8,128]{3,2,1,0:T(8,128)} %base_ref.7) | copy-start | bytes 1327108
  3.3 12.9 %collective-permute-start.5 = (f32[39,8,128]{2,1,0:T(8,128)S(1)}, f32[39,8,128]{2,1,0:T(8,128)S(1)}, u32[]{:S(2)}, u32[]{:S(2)}) collective-permute-start(f32[39,8,128]{2,1,0:T(8,128)S(1)} %get-tuple-element.43), channel_id=1, source_target_pairs={{1,2},{3,4},{5,6},{2,1},{4,3},{6,5},{0,0},{7,7},{9,10},{11,12},{13... | collective-permute-start | bytes 479240 | tf_op jit(solution)/shard_map/ppermute | solution.py:402
  5.4 10.8 %collective-permute-start.4 = (f32[38,8,128]{2,1,0:T(8,128)S(1)}, f32[38,8,128]{2,1,0:T(8,128)S(1)}, u32[]{:S(2)}, u32[]{:S(2)}) collective-permute-start(f32[38,8,128]{2,1,0:T(8,128)S(1)} %get-tuple-element.42), channel_id=1, source_target_pairs={{0,1},{2,3},{4,5},{6,7},{1,0},{3,2},{5,4},{7,6},{8,9},{10,11},{12,... | collective-permute-start | bytes 466952 | tf_op jit(solution)/shard_map/ppermute | solution.py:402
  8.5 6.9 %collective-permute-start.2 = (f32[37,8,128]{2,1,0:T(8,128)S(1)}, f32[37,8,128]{2,1,0:T(8,128)S(1)}, u32[]{:S(2)}, u32[]{:S(2)}) collective-permute-start(f32[37,8,128]{2,1,0:T(8,128)S(1)} %get-tuple-element.40), channel_id=1, source_target_pairs={{0,8},{16,24},{8,0},{24,16},{1,9},{17,25},{9,1},{25,17},{2,10},{18... | collective-permute-start | bytes 454664 | tf_op jit(solution)/shard_map/ppermute | solution.py:402
  8.5 2.1 %copy-start.2 = (f32[2,48,128]{2,1,0:T(8,128)S(1)}, f32[2,48,128]{2,1,0:T(8,128)}, u32[]{:S(2)}) copy-start(f32[2,48,128]{2,1,0:T(8,128)} %constant.2.clone.rest_1_.waves_ref) | copy-start | bytes 147460
  8.5 2.1 %copy-start.4 = (f32[2,9,128]{2,0,1:T(2,128)S(1)}, f32[2,9,128]{2,0,1:T(2,128)}, u32[]{:S(2)}) copy-start(f32[2,9,128]{2,0,1:T(2,128)} %param.6) | copy-start | bytes 27652
  8.5 6.9 %collective-permute-start.3 = (f32[37,8,128]{2,1,0:T(8,128)S(1)}, f32[37,8,128]{2,1,0:T(8,128)S(1)}, u32[]{:S(2)}, u32[]{:S(2)}) collective-permute-start(f32[37,8,128]{2,1,0:T(8,128)S(1)} %get-tuple-element.41), channel_id=1, source_target_pairs={{8,16},{24,0},{16,8},{0,24},{9,17},{25,1},{17,9},{1,25},{10,18},{2... | collective-permute-start | bytes 454664 | tf_op jit(solution)/shard_map/ppermute | solution.py:402
  10.1 3.6 %collective-permute-start.1 = (f32[8,128]{1,0:T(8,128)S(1)}, f32[8,128]{1,0:T(8,128)S(1)}, u32[]{:S(2)}, u32[]{:S(2)}) collective-permute-start(f32[8,128]{1,0:T(8,128)S(1)} %shard_map.57), channel_id=1, source_target_pairs={{0,2},{1,3},{2,0},{3,1},{4,6},{5,7},{6,4},{7,5},{8,10},{9,11},{10,... | collective-permute-start | bytes 12296 | tf_op jit(solution)/shard_map/ppermute | solution.py:465
  13.7 4.5 %collective-permute-start.6 = (f32[8,128]{1,0:T(8,128)S(1)}, f32[8,128]{1,0:T(8,128)S(1)}, u32[]{:S(2)}, u32[]{:S(2)}) collective-permute-start(f32[8,128]{1,0:T(8,128)S(1)} %max.3.most_ref), channel_id=1, source_target_pairs={{0,4},{1,5},{2,6},{3,7},{4,0},{5,1},{6,2},{7,3},{8,12},{9,13},{10,... | collective-permute-start | bytes 12296 | tf_op jit(solution)/shard_map/ppermute | solution.py:465
  16.3 2.0 %copy-start.5 = (s32[9,128]{1,0:T(8,128)S(1)}, s32[9,128]{1,0:T(8,128)}, u32[]{:S(2)}) copy-start(s32[9,128]{1,0:T(8,128)} %mask_ref.9) | copy-start | bytes 13828
  16.3 2.0 %copy-start.6 = (f32[9,128]{1,0:T(8,128)S(1)}, f32[9,128]{1,0:T(8,128)}, u32[]{:S(2)}) copy-start(f32[9,128]{1,0:T(8,128)} %depth_ref.9) | copy-start | bytes 13828
  18.6 6.5 %collective-permute-start.7 = (f32[38,8,128]{2,1,0:T(8,128)S(1)}, f32[38,8,128]{2,1,0:T(8,128)S(1)}, u32[]{:S(2)}, u32[]{:S(2)}) collective-permute-start(f32[38,8,128]{2,1,0:T(8,128)S(1)} %get-tuple-element.53), channel_id=1, source_target_pairs={{0,1},{2,3},{4,5},{6,7},{1,0},{3,2},{5,4},{7,6},{8,9},{10,11},{12,... | collective-permute-start | bytes 466952 | tf_op jit(solution)/shard_map/ppermute | solution.py:402
  18.8 6.4 %collective-permute-start.9 = (f32[37,8,128]{2,1,0:T(8,128)S(1)}, f32[37,8,128]{2,1,0:T(8,128)S(1)}, u32[]{:S(2)}, u32[]{:S(2)}) collective-permute-start(f32[37,8,128]{2,1,0:T(8,128)S(1)} %get-tuple-element.56), channel_id=1, source_target_pairs={{8,16},{24,0},{16,8},{0,24},{9,17},{25,1},{17,9},{1,25},{10,18},{2... | collective-permute-start | bytes 454664 | tf_op jit(solution)/shard_map/ppermute | solution.py:402
  18.8 9.2 %collective-permute-start.10 = (f32[36,8,128]{2,1,0:T(8,128)S(1)}, f32[36,8,128]{2,1,0:T(8,128)S(1)}, u32[]{:S(2)}, u32[]{:S(2)}) collective-permute-start(f32[36,8,128]{2,1,0:T(8,128)S(1)} %get-tuple-element.57), channel_id=1, source_target_pairs={{1,2},{3,4},{5,6},{2,1},{4,3},{6,5},{0,0},{7,7},{9,10},{11,12},{13... | collective-permute-start | bytes 442376 | tf_op jit(solution)/shard_map/ppermute | solution.py:402
  22.7 2.4 %collective-permute-start.8 = (f32[27,8,128]{2,1,0:T(8,128)S(1)}, f32[27,8,128]{2,1,0:T(8,128)S(1)}, u32[]{:S(2)}, u32[]{:S(2)}) collective-permute-start(f32[27,8,128]{2,1,0:T(8,128)S(1)} %get-tuple-element.55), channel_id=1, source_target_pairs={{0,8},{16,24},{8,0},{24,16},{1,9},{17,25},{9,1},{25,17},{2,10},{18... | collective-permute-start | bytes 331784 | tf_op jit(solution)/shard_map/ppermute | solution.py:402
  26.6 6.3 %collective-permute-start.11 = (f32[38,8,128]{2,1,0:T(8,128)S(1)}, f32[38,8,128]{2,1,0:T(8,128)S(1)}, u32[]{:S(2)}, u32[]{:S(2)}) collective-permute-start(f32[38,8,128]{2,1,0:T(8,128)S(1)} %get-tuple-element.61), channel_id=1, source_target_pairs={{0,1},{2,3},{4,5},{6,7},{1,0},{3,2},{5,4},{7,6},{8,9},{10,11},{12,... | collective-permute-start | bytes 466952 | tf_op jit(solution)/shard_map/ppermute | solution.py:402
  28.4 6.6 %collective-permute-start.13 = (f32[37,8,128]{2,1,0:T(8,128)S(1)}, f32[37,8,128]{2,1,0:T(8,128)S(1)}, u32[]{:S(2)}, u32[]{:S(2)}) collective-permute-start(f32[37,8,128]{2,1,0:T(8,128)S(1)} %get-tuple-element.66), channel_id=1, source_target_pairs={{8,16},{24,0},{16,8},{0,24},{9,17},{25,1},{17,9},{1,25},{10,18},{2... | collective-permute-start | bytes 454664 | tf_op jit(solution)/shard_map/ppermute | solution.py:402
  29.0 9.3 %collective-permute-start.14 = (f32[36,8,128]{2,1,0:T(8,128)S(1)}, f32[36,8,128]{2,1,0:T(8,128)S(1)}, u32[]{:S(2)}, u32[]{:S(2)}) collective-permute-start(f32[36,8,128]{2,1,0:T(8,128)S(1)} %get-tuple-element.67), channel_id=1, source_target_pairs={{1,2},{3,4},{5,6},{2,1},{4,3},{6,5},{0,0},{7,7},{9,10},{11,12},{13... | collective-permute-start | bytes 442376 | tf_op jit(solution)/shard_map/ppermute | solution.py:402
  32.8 2.1 %collective-permute-start.12 = (f32[27,8,128]{2,1,0:T(8,128)S(1)}, f32[27,8,128]{2,1,0:T(8,128)S(1)}, u32[]{:S(2)}, u32[]{:S(2)}) collective-permute-start(f32[27,8,128]{2,1,0:T(8,128)S(1)} %get-tuple-element.65), channel_id=1, source_target_pairs={{0,8},{16,24},{8,0},{24,16},{1,9},{17,25},{9,1},{25,17},{2,10},{18... | collective-permute-start | bytes 331784 | tf_op jit(solution)/shard_map/ppermute | solution.py:402

commit v22 on v21

--- a/solution.py
+++ b/solution.py
@@ -85,6 +85,13 @@
     return max(k for k in range(1, most + 1) if total % k == 0)
 
 
+def repeat(count, step):
+    if count == 1:
+        step(0, 0)
+    else:
+        lax.fori_loop(0, count, step, 0)
+
+
 def splat(row, tile):
     return jnp.broadcast_to(row, tile)
 
@@ -222,7 +229,7 @@
                 out_ref[i, j] = own + gain_t * (gap - jnp.abs(mean))
         return carry
 
-    lax.fori_loop(0, planes // wide, step, 0)
+    repeat(planes // wide, step)
 
 
 def peaks_into(pk_ref, most, bounds, heading_step, speed_step):
@@ -314,7 +321,7 @@
                 use(spot, j, mean * (table + flow_ref[spot]), gap, cells[k + rim])
         return carry
 
-    lax.fori_loop(0, headings // wide, step, 0)
+    repeat(headings // wide, step)
 
 
 def first_kernel(
@@ -352,7 +359,7 @@
                 out_ref[i, j] = jnp.minimum(s_ref[i, j] + time_step * rate, target_ref[i])
         return carry
 
-    lax.fori_loop(0, planes // wide, step, 0)
+    repeat(planes // wide, step)
     cut_near(out_ref, x_near)
     cut_far(out_ref, x_far)
     cut_headings(out_ref, t_near, t_far)
@@ -378,13 +385,13 @@
         moved = base_share * base_ref[i, j] + own_share * (cell + time_step * rate)
         out_ref[i, j] = jnp.minimum(moved, target_ref[i])
 
+    for i in range(span[0]):
+        spot = plane_at(i, planes)
+        out_ref[spot] = early_ref[spot]
     near_ref, far_ref = (None, ghosts_ref) if span[0] > 0 else (ghosts_ref, None)
     across_planes(
         span, speed_step, s_ref, near_ref, far_ref, wind_ref, waves_ref, flow_ref, use
     )
-    for i in range(span[0]):
-        spot = plane_at(i, planes)
-        out_ref[spot] = early_ref[spot]
     if section == 2 and span[0] == 0:
         cut_near(out_ref, *refs)
     elif section == 2:

time: 39.8 us -> 39.9 us (level)
  no operation moved by 1% of the time
where the time goes in v22:
time: 39.9 us; the launch traced here: 39.5 us
  starting transfers between devices  20.6 us (52%)
  Pallas kernels  12.7 us (32%)
  waiting for transfers between devices  4.28 us (11%)
  local copies, waits for them, and re-layouts  1.74 us (4%)
    ppermute x12, starting transfers between devices, trade(): return lax.ppermute(value, axis, pairs)  16.9 us
    pallas_call x15, Pallas kernels, call(): pl.pallas_call(kernel, out_shape=outs, in_specs=[vmem] * len(ins), out_sp...  12.7 us
    ppermute x3, starting transfers between devices, spread(): return lax.ppermute(most, 'gx', pairs)  3.71 us
    ppermute x12, waiting for transfers between devices, trade(): return lax.ppermute(value, axis, pairs)  2.17 us
    ppermute x3, waiting for transfers between devices, spread(): return lax.ppermute(most, 'gx', pairs)  2.11 us
    unnamed x14, local copies, waits for them, and re-layouts  1.74 us
  transfers between devices with their start and end apart: 15, of which 4 were waited for; matrix products, arithmetic and copies ran while one was open for 0% of the time, Pallas kernels for 28%

profile of v22, /device:TPU:8, one launch (start us, length us, event | category | flops | bytes accessed | tf_op | source)
XLA Modules:
  0.0 39.5 jit_solution(18269329001722109937)
XLA Ops:
  0.0 0.0 copy-start.3
  0.0 0.7 %copy-done.3 = f32[2,9,128]{2,0,1:T(2,128)S(1)} copy-done((f32[2,9,128]{2,0,1:T(2,128)S(1)}, f32[2,9,128]{2,0,1:T(2,128)}, u32[]{:S(2)}) %copy-start.3) | copy-done | bytes 9240
  0.7 1.6 %collective-permute-start = (f32[40,8,128]{2,1,0:T(8,128)S(1)}, f32[40,8,128]{2,1,0:T(8,128)S(1)}, u32[]{:S(2)}, u32[]{:S(2)}) collective-permute-start(f32[40,8,128]{2,1,0:T(8,128)S(1)} %shard_map.56.own_ref), channel_id=1, source_target_pairs={{0,1},{1,0},{2,3},{3,2},{4,5},{5,4},{6,7},{7,6},{8,9},{9,8},{10,11... | collective-permute-start | bytes 491528 | tf_op jit(solution)/shard_map/ppermute | solution.py:472
  2.3 0.0 copy-start
  2.3 1.0 %copy-done = f32[9,12,8,128]{3,2,1,0:T(8,128)S(1)} copy-done((f32[9,12,8,128]{3,2,1,0:T(8,128)S(1)}, f32[9,12,8,128]{3,2,1,0:T(8,128)}, u32[]{:S(2)}) %copy-start) | copy-done | bytes 442392
  3.3 0.0 copy-start.1
  3.3 2.1 %collective-permute-start.5 = (f32[39,8,128]{2,1,0:T(8,128)S(1)}, f32[39,8,128]{2,1,0:T(8,128)S(1)}, u32[]{:S(2)}, u32[]{:S(2)}) collective-permute-start(f32[39,8,128]{2,1,0:T(8,128)S(1)} %get-tuple-element.43), channel_id=1, source_target_pairs={{1,2},{3,4},{5,6},{2,1},{4,3},{6,5},{0,0},{7,7},{9,10},{11,12},{13... | collective-permute-start | bytes 479240 | tf_op jit(solution)/shard_map/ppermute | solution.py:409
  5.4 3.1 %collective-permute-start.4 = (f32[38,8,128]{2,1,0:T(8,128)S(1)}, f32[38,8,128]{2,1,0:T(8,128)S(1)}, u32[]{:S(2)}, u32[]{:S(2)}) collective-permute-start(f32[38,8,128]{2,1,0:T(8,128)S(1)} %get-tuple-element.42), channel_id=1, source_target_pairs={{0,1},{2,3},{4,5},{6,7},{1,0},{3,2},{5,4},{7,6},{8,9},{10,11},{12,... | collective-permute-start | bytes 466952 | tf_op jit(solution)/shard_map/ppermute | solution.py:409
  8.5 0.0 collective-permute-start.2
  8.5 0.0 copy-start.2
  8.5 0.0 copy-start.4
  8.5 1.6 %collective-permute-start.3 = (f32[37,8,128]{2,1,0:T(8,128)S(1)}, f32[37,8,128]{2,1,0:T(8,128)S(1)}, u32[]{:S(2)}, u32[]{:S(2)}) collective-permute-start(f32[37,8,128]{2,1,0:T(8,128)S(1)} %get-tuple-element.41), channel_id=1, source_target_pairs={{8,16},{24,0},{16,8},{0,24},{9,17},{25,1},{17,9},{1,25},{10,18},{2... | collective-permute-start | bytes 454664 | tf_op jit(solution)/shard_map/ppermute | solution.py:409
  10.1 0.0 collective-permute-done.other_ref
  10.1 0.5 %collective-permute-start.1 = (f32[8,128]{1,0:T(8,128)S(1)}, f32[8,128]{1,0:T(8,128)S(1)}, u32[]{:S(2)}, u32[]{:S(2)}) collective-permute-start(f32[8,128]{1,0:T(8,128)S(1)} %shard_map.57), channel_id=1, source_target_pairs={{0,2},{1,3},{2,0},{3,1},{4,6},{5,7},{6,4},{7,5},{8,10},{9,11},{10,... | collective-permute-start | bytes 12296 | tf_op jit(solution)/shard_map/ppermute | solution.py:472
  10.6 0.0 copy-done.1
  10.6 0.0 copy-done.2
  10.6 0.0 copy-done.4
  10.6 2.2 %shard_map.55 = (f32[9,12,8,128]{3,2,1,0:T(8,128)S(1)}, f32[9,12,8,128]{3,2,1,0:T(8,128)S(1)}, f32[9,12,8,128]{3,2,1,0:T(8,128)S(1)}, f32[7,128,128]{2,1,0:T(8,128)S(1)}) custom-call(f32[9,12,8,128]{3,2,1,0:T(8,128)S(1)} %copy-done.1, f32[9,2,128]{2,1,0:T(2,128)S(1)} %bitcast.2, f32[2,48,128]{2,1,0:T(8,128)S(1)} %copy-done.2), custom_call_target="tpu_custom_call" | custom-call | flops 33177600 | bytes 33177600 | tf_op jit(solution)/shard_map/pallas_call | solution.py:443
  12.7 1.0 %collective-permute-done.1 = f32[8,128]{1,0:T(8,128)S(1)} collective-permute-done((f32[8,128]{1,0:T(8,128)S(1)}, f32[8,128]{1,0:T(8,128)S(1)}, u32[]{:S(2)}, u32[]{:S(2)}) %collective-permute-start.1) | collective-permute-done | bytes 4128 | tf_op jit(solution)/shard_map/ppermute | solution.py:472
  13.7 1.7 %collective-permute-start.6 = (f32[8,128]{1,0:T(8,128)S(1)}, f32[8,128]{1,0:T(8,128)S(1)}, u32[]{:S(2)}, u32[]{:S(2)}) collective-permute-start(f32[8,128]{1,0:T(8,128)S(1)} %max.3.most_ref), channel_id=1, source_target_pairs={{0,4},{1,5},{2,6},{3,7},{4,0},{5,1},{6,2},{7,3},{8,12},{9,13},{10,... | collective-permute-start | bytes 12296 | tf_op jit(solution)/shard_map/ppermute | solution.py:472
  15.4 0.0 collective-permute-done.2.near_ref
  15.4 0.0 collective-permute-done.3.far_ref
  15.4 0.8 %shard_map.59.part_ref = f32[9,12,8,128]{3,2,1,0:T(8,128)S(1)} custom-call(f32[9,12,8,128]{3,2,1,0:T(8,128)S(1)} %copy-done.1, f32[9,12,8,128]{3,2,1,0:T(8,128)S(1)} %get-tuple-element.37.speed_ref, f32[9,12,8,128]{3,2,1,0:T(8,128)S(1)} %get-tuple-element.39.part_ref, f32[37,8,128]{2,1,0:T(8,128)S(1)} %collective-permute-done.2.near_ref, ...), custom_call_target="tpu_custom_call" | custom-call | tf_op jit(solution)/shard_map/pallas_call | solution.py:443
  16.2 0.0 collective-permute-done.4.near_ref
  16.2 0.0 collective-permute-done.5.far_ref
  16.3 0.0 copy-start.5
  16.3 0.0 copy-start.6
  16.3 0.8 %shard_map.60 = (f32[9,12,8,128]{3,2,1,0:T(8,128)S(1)}, f32[9,12,8,128]{3,2,1,0:T(8,128)S(1)}) custom-call(f32[9,12,8,128]{3,2,1,0:T(8,128)S(1)} %copy-done.1, f32[9,12,8,128]{3,2,1,0:T(8,128)S(1)} %shard_map.59.part_ref, f32[38,8,128]{2,1,0:T(8,128)S(1)} %collective-permute-done.4.near_ref, f32[39,8,128]{2,1,0:T(8,128)S(1)} %collective-permute-done.5.far_ref, ...), custom_call_target="tpu_custom_call" | custom-call | tf_op jit(solution)/shard_map/pallas_call | solution.py:443
  17.1 1.1 %collective-permute-done.6.other_ref = f32[8,128]{1,0:T(8,128)S(1)} collective-permute-done((f32[8,128]{1,0:T(8,128)S(1)}, f32[8,128]{1,0:T(8,128)S(1)}, u32[]{:S(2)}, u32[]{:S(2)}) %collective-permute-start.6) | collective-permute-done | bytes 4128 | tf_op jit(solution)/shard_map/ppermute | solution.py:472
  18.2 0.0 copy-done.5
  18.2 0.0 copy-done.6
  18.2 0.3 shard_map.61
  18.6 0.2 collective-permute-start.7
  18.8 0.0 collective-permute-start.9
  18.8 3.9 %collective-permute-start.10 = (f32[36,8,128]{2,1,0:T(8,128)S(1)}, f32[36,8,128]{2,1,0:T(8,128)S(1)}, u32[]{:S(2)}, u32[]{:S(2)}) collective-permute-start(f32[36,8,128]{2,1,0:T(8,128)S(1)} %get-tuple-element.57), channel_id=1, source_target_pairs={{1,2},{3,4},{5,6},{2,1},{4,3},{6,5},{0,0},{7,7},{9,10},{11,12},{13... | collective-permute-start | bytes 442376 | tf_op jit(solution)/shard_map/ppermute | solution.py:409
  22.7 0.4 %collective-permute-start.8 = (f32[27,8,128]{2,1,0:T(8,128)S(1)}, f32[27,8,128]{2,1,0:T(8,128)S(1)}, u32[]{:S(2)}, u32[]{:S(2)}) collective-permute-start(f32[27,8,128]{2,1,0:T(8,128)S(1)} %get-tuple-element.55), channel_id=1, source_target_pairs={{0,8},{16,24},{8,0},{24,16},{1,9},{17,25},{9,1},{25,17},{2,10},{18... | collective-permute-start | bytes 331784 | tf_op jit(solution)/shard_map/ppermute | solution.py:409
  23.1 2.0 %shard_map.62 = (f32[9,12,8,128]{3,2,1,0:T(8,128)S(1)}, f32[9,12,8,128]{3,2,1,0:T(8,128)S(1)}) custom-call(f32[9,12,8,128]{3,2,1,0:T(8,128)S(1)} %get-tuple-element.48.s_ref, f32[7,128,128]{2,1,0:T(8,128)S(1)} %get-tuple-element.49.rest_0_, f32[8,128]{1,0:T(8,128)S(1)} %get-tuple-element.50.rest_1_.pk_ref), custom_call_target="tpu_custom_call" | custom-call | tf_op jit(solution)/shard_map/pallas_call | solution.py:443
  25.1 0.0 collective-permute-done.7.ghosts_ref
  25.1 0.0 collective-permute-done.8.near_ref
  25.1 0.0 collective-permute-done.9.far_ref
  25.1 0.8 %shard_map.63.part_ref = f32[9,12,8,128]{3,2,1,0:T(8,128)S(1)} custom-call(f32[9,12,8,128]{3,2,1,0:T(8,128)S(1)} %get-tuple-element.48.s_ref, f32[9,12,8,128]{3,2,1,0:T(8,128)S(1)} %get-tuple-element.51.speed_ref, f32[9,12,8,128]{3,2,1,0:T(8,128)S(1)} %get-tuple-element.54.part_ref, f32[27,8,128]{2,1,0:T(8,128)S(1)} %collective-permute-done.8.near_ref, ...), custom_call_target="tpu_custom_call" | custom-call | flops 110592000 | bytes 110592000 | tf_op jit(solution)/shard_map/pallas_call | solution.py:443
  26.0 0.7 %shard_map.64 = (f32[9,12,8,128]{3,2,1,0:T(8,128)S(1)}, f32[38,8,128]{2,1,0:T(8,128)S(1)}) custom-call(f32[9,12,8,128]{3,2,1,0:T(8,128)S(1)} %copy-done.1, f32[9,12,8,128]{3,2,1,0:T(8,128)S(1)} %get-tuple-element.48.s_ref, f32[9,12,8,128]{3,2,1,0:T(8,128)S(1)} %shard_map.63.part_ref, f32[38,8,128]{2,1,0:T(8,128)S(1)} %collective-permute-done.7.ghosts_ref, ...), custom_call_target="tpu_custom_call" | custom-call | tf_op jit(solution)/shard_map/pallas_call | solution.py:443
  26.6 1.1 %collective-permute-start.11 = (f32[38,8,128]{2,1,0:T(8,128)S(1)}, f32[38,8,128]{2,1,0:T(8,128)S(1)}, u32[]{:S(2)}, u32[]{:S(2)}) collective-permute-start(f32[38,8,128]{2,1,0:T(8,128)S(1)} %get-tuple-element.61), channel_id=1, source_target_pairs={{0,1},{2,3},{4,5},{6,7},{1,0},{3,2},{5,4},{7,6},{8,9},{10,11},{12,... | collective-permute-start | bytes 466952 | tf_op jit(solution)/shard_map/ppermute | solution.py:409
  27.7 0.2 collective-permute-done.10.ghosts_ref
  27.9 0.4 %shard_map.65 = (f32[9,12,8,128]{3,2,1,0:T(8,128)S(1)}, f32[36,8,128]{2,1,0:T(8,128)S(1)}, f32[27,8,128]{2,1,0:T(8,128)S(1)}, f32[37,8,128]{2,1,0:T(8,128)S(1)}) custom-call(f32[9,12,8,128]{3,2,1,0:T(8,128)S(1)} %copy-done.1, f32[9,12,8,128]{3,2,1,0:T(8,128)S(1)} %get-tuple-element.48.s_ref, f32[9,12,8,128]{3,2,1,0:T(8,128)S(1)} %shard_map.63.part_ref, ...), custom_call_target="tpu_custom_call" | custom-call | tf_op jit(solution)/shard_map/pallas_call | solution.py:443
  28.4 0.7 %collective-permute-start.13 = (f32[37,8,128]{2,1,0:T(8,128)S(1)}, f32[37,8,128]{2,1,0:T(8,128)S(1)}, u32[]{:S(2)}, u32[]{:S(2)}) collective-permute-start(f32[37,8,128]{2,1,0:T(8,128)S(1)} %get-tuple-element.66), channel_id=1, source_target_pairs={{8,16},{24,0},{16,8},{0,24},{9,17},{25,1},{17,9},{1,25},{10,18},{2... | collective-permute-start | bytes 454664 | tf_op jit(solution)/shard_map/ppermute | solution.py:409
  29.0 3.8 %collective-permute-start.14 = (f32[36,8,128]{2,1,0:T(8,128)S(1)}, f32[36,8,128]{2,1,0:T(8,128)S(1)}, u32[]{:S(2)}, u32[]{:S(2)}) collective-permute-start(f32[36,8,128]{2,1,0:T(8,128)S(1)} %get-tuple-element.67), channel_id=1, source_target_pairs={{1,2},{3,4},{5,6},{2,1},{4,3},{6,5},{0,0},{7,7},{9,10},{11,12},{13... | collective-permute-start | bytes 442376 | tf_op jit(solution)/shard_map/ppermute | solution.py:409
  32.8 0.1 collective-permute-start.12
  32.9 0.0 collective-permute-done.11.ghosts_ref
  32.9 2.0 %shard_map.66 = (f32[9,12,8,128]{3,2,1,0:T(8,128)S(1)}, f32[9,12,8,128]{3,2,1,0:T(8,128)S(1)}) custom-call(f32[9,12,8,128]{3,2,1,0:T(8,128)S(1)} %get-tuple-element.62.s_ref, f32[7,128,128]{2,1,0:T(8,128)S(1)} %get-tuple-element.49.rest_0_, f32[8,128]{1,0:T(8,128)S(1)} %get-tuple-element.50.rest_1_.pk_ref), custom_call_target="tpu_custom_call" | custom-call | tf_op jit(solution)/shard_map/pallas_call | solution.py:443
  34.9 0.0 collective-permute-done.12.near_ref
  34.9 0.0 collective-permute-done.13.far_ref
  34.9 0.8 %shard_map.67.part_ref = f32[9,12,8,128]{3,2,1,0:T(8,128)S(1)} custom-call(f32[9,12,8,128]{3,2,1,0:T(8,128)S(1)} %get-tuple-element.62.s_ref, f32[9,12,8,128]{3,2,1,0:T(8,128)S(1)} %get-tuple-element.63.speed_ref, f32[9,12,8,128]{3,2,1,0:T(8,128)S(1)} %get-tuple-element.64.part_ref, f32[27,8,128]{2,1,0:T(8,128)S(1)} %collective-permute-done.12.near_ref, ...), custom_call_target="tpu_custom_call" | custom-call | flops 110592000 | bytes 110592000 | tf_op jit(solution)/shard_map/pallas_call | solution.py:443
  35.8 0.7 %shard_map.68.refs_0_ = f32[9,12,8,128]{3,2,1,0:T(8,128)S(1)} custom-call(f32[9,12,8,128]{3,2,1,0:T(8,128)S(1)} %copy-done.1, f32[9,12,8,128]{3,2,1,0:T(8,128)S(1)} %get-tuple-element.62.s_ref, f32[9,12,8,128]{3,2,1,0:T(8,128)S(1)} %shard_map.67.part_ref, f32[38,8,128]{2,1,0:T(8,128)S(1)} %collective-permute-done.11.ghosts_ref, f32[9,2,128]{2,1,0:T(2,128)S(1)} %bitcast.6, ...), custom_call_target="tpu_custom_call" | custom-call | tf_op jit(solution)/shard_map/pallas_call | solution.py:443
  36.4 1.9 %collective-permute-done.14.ghosts_ref = f32[36,8,128]{2,1,0:T(8,128)S(1)} collective-permute-done((f32[36,8,128]{2,1,0:T(8,128)S(1)}, f32[36,8,128]{2,1,0:T(8,128)S(1)}, u32[]{:S(2)}, u32[]{:S(2)}) %collective-permute-start.14) | collective-permute-done | bytes 147488 | tf_op jit(solution)/shard_map/ppermute | solution.py:409
  38.3 1.2 %shard_map.69 = f32[9,12,8,128]{3,2,1,0:T(8,128)} custom-call(f32[9,12,8,128]{3,2,1,0:T(8,128)S(1)} %copy-done.1, f32[9,12,8,128]{3,2,1,0:T(8,128)S(1)} %get-tuple-element.62.s_ref, f32[9,12,8,128]{3,2,1,0:T(8,128)S(1)} %shard_map.67.part_ref, f32[36,8,128]{2,1,0:T(8,128)S(1)} %collective-permute-done.14.ghosts_ref, f32[9,2,128]{2,1,0:T(2,128)S(1)} %bitcast.7, ...), custom_call_target="tpu_custom_call" | custom-call | tf_op jit(solution)/shard_map/pallas_call | solution.py:443
  (4 shorter events, 0.1 us)
Async XLA Ops:
  0.0 0.7 %copy-start.3 = (f32[2,9,128]{2,0,1:T(2,128)S(1)}, f32[2,9,128]{2,0,1:T(2,128)}, u32[]{:S(2)}) copy-start(f32[2,9,128]{2,0,1:T(2,128)} %param.6) | copy-start | bytes 27652
  0.7 9.4 %collective-permute-start = (f32[40,8,128]{2,1,0:T(8,128)S(1)}, f32[40,8,128]{2,1,0:T(8,128)S(1)}, u32[]{:S(2)}, u32[]{:S(2)}) collective-permute-start(f32[40,8,128]{2,1,0:T(8,128)S(1)} %shard_map.56.own_ref), channel_id=1, source_target_pairs={{0,1},{1,0},{2,3},{3,2},{4,5},{5,4},{6,7},{7,6},{8,9},{9,8},{10,11... | collective-permute-start | bytes 491528 | tf_op jit(solution)/shard_map/ppermute | solution.py:472
  2.3 1.0 %copy-start = (f32[9,12,8,128]{3,2,1,0:T(8,128)S(1)}, f32[9,12,8,128]{3,2,1,0:T(8,128)}, u32[]{:S(2)}) copy-start(f32[9,12,8,128]{3,2,1,0:T(8,128)} %base_ref.7) | copy-start | bytes 1327108
  3.3 7.3 %copy-start.1 = (f32[9,12,8,128]{3,2,1,0:T(8,128)S(1)}, f32[9,12,8,128]{3,2,1,0:T(8,128)}, u32[]{:S(2)}) copy-start(f32[9,12,8,128]{3,2,1,0:T(8,128)} %base_ref.7) | copy-start | bytes 1327108
  3.3 12.9 %collective-permute-start.5 = (f32[39,8,128]{2,1,0:T(8,128)S(1)}, f32[39,8,128]{2,1,0:T(8,128)S(1)}, u32[]{:S(2)}, u32[]{:S(2)}) collective-permute-start(f32[39,8,128]{2,1,0:T(8,128)S(1)} %get-tuple-element.43), channel_id=1, source_target_pairs={{1,2},{3,4},{5,6},{2,1},{4,3},{6,5},{0,0},{7,7},{9,10},{11,12},{13... | collective-permute-start | bytes 479240 | tf_op jit(solution)/shard_map/ppermute | solution.py:409
  5.4 10.8 %collective-permute-start.4 = (f32[38,8,128]{2,1,0:T(8,128)S(1)}, f32[38,8,128]{2,1,0:T(8,128)S(1)}, u32[]{:S(2)}, u32[]{:S(2)}) collective-permute-start(f32[38,8,128]{2,1,0:T(8,128)S(1)} %get-tuple-element.42), channel_id=1, source_target_pairs={{0,1},{2,3},{4,5},{6,7},{1,0},{3,2},{5,4},{7,6},{8,9},{10,11},{12,... | collective-permute-start | bytes 466952 | tf_op jit(solution)/shard_map/ppermute | solution.py:409
  8.5 6.9 %collective-permute-start.2 = (f32[37,8,128]{2,1,0:T(8,128)S(1)}, f32[37,8,128]{2,1,0:T(8,128)S(1)}, u32[]{:S(2)}, u32[]{:S(2)}) collective-permute-start(f32[37,8,128]{2,1,0:T(8,128)S(1)} %get-tuple-element.40), channel_id=1, source_target_pairs={{0,8},{16,24},{8,0},{24,16},{1,9},{17,25},{9,1},{25,17},{2,10},{18... | collective-permute-start | bytes 454664 | tf_op jit(solution)/shard_map/ppermute | solution.py:409
  8.5 2.1 %copy-start.2 = (f32[2,48,128]{2,1,0:T(8,128)S(1)}, f32[2,48,128]{2,1,0:T(8,128)}, u32[]{:S(2)}) copy-start(f32[2,48,128]{2,1,0:T(8,128)} %constant.2.clone.rest_1_.waves_ref) | copy-start | bytes 147460
  8.5 2.1 %copy-start.4 = (f32[2,9,128]{2,0,1:T(2,128)S(1)}, f32[2,9,128]{2,0,1:T(2,128)}, u32[]{:S(2)}) copy-start(f32[2,9,128]{2,0,1:T(2,128)} %param.6) | copy-start | bytes 27652
  8.5 6.9 %collective-permute-start.3 = (f32[37,8,128]{2,1,0:T(8,128)S(1)}, f32[37,8,128]{2,1,0:T(8,128)S(1)}, u32[]{:S(2)}, u32[]{:S(2)}) collective-permute-start(f32[37,8,128]{2,1,0:T(8,128)S(1)} %get-tuple-element.41), channel_id=1, source_target_pairs={{8,16},{24,0},{16,8},{0,24},{9,17},{25,1},{17,9},{1,25},{10,18},{2... | collective-permute-start | bytes 454664 | tf_op jit(solution)/shard_map/ppermute | solution.py:409
  10.1 3.6 %collective-permute-start.1 = (f32[8,128]{1,0:T(8,128)S(1)}, f32[8,128]{1,0:T(8,128)S(1)}, u32[]{:S(2)}, u32[]{:S(2)}) collective-permute-start(f32[8,128]{1,0:T(8,128)S(1)} %shard_map.57), channel_id=1, source_target_pairs={{0,2},{1,3},{2,0},{3,1},{4,6},{5,7},{6,4},{7,5},{8,10},{9,11},{10,... | collective-permute-start | bytes 12296 | tf_op jit(solution)/shard_map/ppermute | solution.py:472
  13.7 4.5 %collective-permute-start.6 = (f32[8,128]{1,0:T(8,128)S(1)}, f32[8,128]{1,0:T(8,128)S(1)}, u32[]{:S(2)}, u32[]{:S(2)}) collective-permute-start(f32[8,128]{1,0:T(8,128)S(1)} %max.3.most_ref), channel_id=1, source_target_pairs={{0,4},{1,5},{2,6},{3,7},{4,0},{5,1},{6,2},{7,3},{8,12},{9,13},{10,... | collective-permute-start | bytes 12296 | tf_op jit(solution)/shard_map/ppermute | solution.py:472
  16.3 2.0 %copy-start.5 = (s32[9,128]{1,0:T(8,128)S(1)}, s32[9,128]{1,0:T(8,128)}, u32[]{:S(2)}) copy-start(s32[9,128]{1,0:T(8,128)} %mask_ref.9) | copy-start | bytes 13828
  16.3 2.0 %copy-start.6 = (f32[9,128]{1,0:T(8,128)S(1)}, f32[9,128]{1,0:T(8,128)}, u32[]{:S(2)}) copy-start(f32[9,128]{1,0:T(8,128)} %depth_ref.9) | copy-start | bytes 13828
  18.6 6.5 %collective-permute-start.7 = (f32[38,8,128]{2,1,0:T(8,128)S(1)}, f32[38,8,128]{2,1,0:T(8,128)S(1)}, u32[]{:S(2)}, u32[]{:S(2)}) collective-permute-start(f32[38,8,128]{2,1,0:T(8,128)S(1)} %get-tuple-element.53), channel_id=1, source_target_pairs={{0,1},{2,3},{4,5},{6,7},{1,0},{3,2},{5,4},{7,6},{8,9},{10,11},{12,... | collective-permute-start | bytes 466952 | tf_op jit(solution)/shard_map/ppermute | solution.py:409
  18.8 6.4 %collective-permute-start.9 = (f32[37,8,128]{2,1,0:T(8,128)S(1)}, f32[37,8,128]{2,1,0:T(8,128)S(1)}, u32[]{:S(2)}, u32[]{:S(2)}) collective-permute-start(f32[37,8,128]{2,1,0:T(8,128)S(1)} %get-tuple-element.56), channel_id=1, source_target_pairs={{8,16},{24,0},{16,8},{0,24},{9,17},{25,1},{17,9},{1,25},{10,18},{2... | collective-permute-start | bytes 454664 | tf_op jit(solution)/shard_map/ppermute | solution.py:409
  18.8 9.2 %collective-permute-start.10 = (f32[36,8,128]{2,1,0:T(8,128)S(1)}, f32[36,8,128]{2,1,0:T(8,128)S(1)}, u32[]{:S(2)}, u32[]{:S(2)}) collective-permute-start(f32[36,8,128]{2,1,0:T(8,128)S(1)} %get-tuple-element.57), channel_id=1, source_target_pairs={{1,2},{3,4},{5,6},{2,1},{4,3},{6,5},{0,0},{7,7},{9,10},{11,12},{13... | collective-permute-start | bytes 442376 | tf_op jit(solution)/shard_map/ppermute | solution.py:409
  22.7 2.4 %collective-permute-start.8 = (f32[27,8,128]{2,1,0:T(8,128)S(1)}, f32[27,8,128]{2,1,0:T(8,128)S(1)}, u32[]{:S(2)}, u32[]{:S(2)}) collective-permute-start(f32[27,8,128]{2,1,0:T(8,128)S(1)} %get-tuple-element.55), channel_id=1, source_target_pairs={{0,8},{16,24},{8,0},{24,16},{1,9},{17,25},{9,1},{25,17},{2,10},{18... | collective-permute-start | bytes 331784 | tf_op jit(solution)/shard_map/ppermute | solution.py:409
  26.6 6.3 %collective-permute-start.11 = (f32[38,8,128]{2,1,0:T(8,128)S(1)}, f32[38,8,128]{2,1,0:T(8,128)S(1)}, u32[]{:S(2)}, u32[]{:S(2)}) collective-permute-start(f32[38,8,128]{2,1,0:T(8,128)S(1)} %get-tuple-element.61), channel_id=1, source_target_pairs={{0,1},{2,3},{4,5},{6,7},{1,0},{3,2},{5,4},{7,6},{8,9},{10,11},{12,... | collective-permute-start | bytes 466952 | tf_op jit(solution)/shard_map/ppermute | solution.py:409
  28.4 6.6 %collective-permute-start.13 = (f32[37,8,128]{2,1,0:T(8,128)S(1)}, f32[37,8,128]{2,1,0:T(8,128)S(1)}, u32[]{:S(2)}, u32[]{:S(2)}) collective-permute-start(f32[37,8,128]{2,1,0:T(8,128)S(1)} %get-tuple-element.66), channel_id=1, source_target_pairs={{8,16},{24,0},{16,8},{0,24},{9,17},{25,1},{17,9},{1,25},{10,18},{2... | collective-permute-start | bytes 454664 | tf_op jit(solution)/shard_map/ppermute | solution.py:409
  29.0 9.3 %collective-permute-start.14 = (f32[36,8,128]{2,1,0:T(8,128)S(1)}, f32[36,8,128]{2,1,0:T(8,128)S(1)}, u32[]{:S(2)}, u32[]{:S(2)}) collective-permute-start(f32[36,8,128]{2,1,0:T(8,128)S(1)} %get-tuple-element.67), channel_id=1, source_target_pairs={{1,2},{3,4},{5,6},{2,1},{4,3},{6,5},{0,0},{7,7},{9,10},{11,12},{13... | collective-permute-start | bytes 442376 | tf_op jit(solution)/shard_map/ppermute | solution.py:409
  32.8 2.1 %collective-permute-start.12 = (f32[27,8,128]{2,1,0:T(8,128)S(1)}, f32[27,8,128]{2,1,0:T(8,128)S(1)}, u32[]{:S(2)}, u32[]{:S(2)}) collective-permute-start(f32[27,8,128]{2,1,0:T(8,128)S(1)} %get-tuple-element.65), channel_id=1, source_target_pairs={{0,8},{16,24},{8,0},{24,16},{1,9},{17,25},{9,1},{25,17},{2,10},{18... | collective-permute-start | bytes 331784 | tf_op jit(solution)/shard_map/ppermute | solution.py:409

commit v23 on v21

--- a/solution.py
+++ b/solution.py
@@ -363,9 +363,23 @@
     mask_ref, depth_ref, pk_ref, *refs
 ):
     planes = s_ref.shape[0]
-    refs, (flow_ref, target_ref) = list(refs[:-2]), refs[-2:]
+    final = section == 3 and span[0] > 0
+    refs = list(refs)
+    if final:
+        out_ref, sems = refs.pop(), refs.pop()
+    refs, (flow_ref, target_ref) = refs[:-2], refs[-2:]
     early_ref = refs.pop(0) if span[0] > 0 else None
-    out_ref = refs.pop(0)
+    if final:
+        result_ref = refs.pop(0)
+        early = pl.ds(jnp.where(odd_place("gx"), 0, planes - span[0]), span[0])
+        late = pl.ds(jnp.where(odd_place("gx"), span[0], 0), planes - span[0])
+        sends = [
+            pltpu.make_async_copy(early_ref.at[early], result_ref.at[early], sems.at[0]),
+            pltpu.make_async_copy(out_ref.at[late], result_ref.at[late], sems.at[1]),
+        ]
+        sends[0].start()
+    else:
+        out_ref = refs.pop(0)
     tile = s_ref.shape[2:]
     splat_targets(mask_ref, depth_ref, target_ref)
     peak_x = splat(pk_ref[0:1, :] * gain, tile)
@@ -382,6 +396,11 @@
     across_planes(
         span, speed_step, s_ref, near_ref, far_ref, wind_ref, waves_ref, flow_ref, use
     )
+    if final:
+        sends[1].start()
+        for send in sends:
+            send.wait()
+        return
     for i in range(span[0]):
         spot = plane_at(i, planes)
         out_ref[spot] = early_ref[spot]
@@ -432,12 +451,12 @@
     rows = pltpu.VMEM((planes,) + tile, jnp.float32)
     cells = math.prod(level_set.shape)
 
-    def call(kernel, ins, outs, scratch=(), work=0):
+    def call(kernel, ins, outs, scratch=(), work=0, place=vmem):
         return pl.pallas_call(
             kernel,
             out_shape=outs,
             in_specs=[vmem] * len(ins),
-            out_specs=[vmem] * len(outs),
+            out_specs=[place] * len(outs),
             scratch_shapes=list(scratch),
             compiler_params=pltpu.CompilerParams(vmem_limit_bytes=16 * 1024 * 1024),
             cost_estimate=pl.CostEstimate(
@@ -515,7 +534,11 @@
             ins = ins[:3] + [x_far] + ins[4:] + [early]
             outs = [field] + (far_shapes if more else [])
             last = functools.partial(section_kernel, section, (planes - rim, planes), speed_step)
-            values, *far_next = call(last, ins, outs, [rows, rows])
+            scratch, place = [rows, rows], vmem
+            if not more:
+                scratch += [pltpu.SemaphoreType.DMA((2,)), pltpu.VMEM(level_set.shape, jnp.float32)]
+                place = pl.BlockSpec(memory_space=pltpu.HBM)
+            values, *far_next = call(last, ins, outs, scratch, place=place)
             if more:
                 (x_out,), (x_last, t_out, t_last) = x_next, far_next
     return values

time: 39.8 us -> 39.9 us (level)
  no operation moved by 1% of the time
where the time goes in v23:
time: 39.9 us; the launch traced here: 39.5 us
  starting transfers between devices  20.6 us (52%)
  Pallas kernels  12.6 us (32%)
  waiting for transfers between devices  4.28 us (11%)
  local copies, waits for them, and re-layouts  1.74 us (4%)
    ppermute x12, starting transfers between devices, trade(): return lax.ppermute(value, axis, pairs)  16.9 us
    pallas_call x15, Pallas kernels, call(): pl.pallas_call(kernel, out_shape=outs, in_specs=[vmem] * len(ins), out_sp...  12.6 us
    ppermute x3, starting transfers between devices, spread(): return lax.ppermute(most, 'gx', pairs)  3.71 us
    ppermute x12, waiting for transfers between devices, trade(): return lax.ppermute(value, axis, pairs)  2.17 us
    ppermute x3, waiting for transfers between devices, spread(): return lax.ppermute(most, 'gx', pairs)  2.11 us
    unnamed x14, local copies, waits for them, and re-layouts  1.74 us
  transfers between devices with their start and end apart: 15, of which 4 were waited for; matrix products, arithmetic and copies ran while one was open for 0% of the time, Pallas kernels for 28%

profile of v23, /device:TPU:8, one launch (start us, length us, event | category | flops | bytes accessed | tf_op | source)
XLA Modules:
  0.0 39.5 jit_solution(11641860159340370092)
XLA Ops:
  0.0 0.0 copy-start.3
  0.0 0.7 %copy-done.3 = f32[2,9,128]{2,0,1:T(2,128)S(1)} copy-done((f32[2,9,128]{2,0,1:T(2,128)S(1)}, f32[2,9,128]{2,0,1:T(2,128)}, u32[]{:S(2)}) %copy-start.3) | copy-done | bytes 9240
  0.7 1.6 %collective-permute-start = (f32[40,8,128]{2,1,0:T(8,128)S(1)}, f32[40,8,128]{2,1,0:T(8,128)S(1)}, u32[]{:S(2)}, u32[]{:S(2)}) collective-permute-start(f32[40,8,128]{2,1,0:T(8,128)S(1)} %shard_map.56.own_ref), channel_id=1, source_target_pairs={{0,1},{1,0},{2,3},{3,2},{4,5},{5,4},{6,7},{7,6},{8,9},{9,8},{10,11... | collective-permute-start | bytes 491528 | tf_op jit(solution)/shard_map/ppermute | solution.py:484
  2.3 0.0 copy-start
  2.3 1.0 %copy-done = f32[9,12,8,128]{3,2,1,0:T(8,128)S(1)} copy-done((f32[9,12,8,128]{3,2,1,0:T(8,128)S(1)}, f32[9,12,8,128]{3,2,1,0:T(8,128)}, u32[]{:S(2)}) %copy-start) | copy-done | bytes 442392
  3.3 0.0 copy-start.1
  3.3 2.1 %collective-permute-start.5 = (f32[39,8,128]{2,1,0:T(8,128)S(1)}, f32[39,8,128]{2,1,0:T(8,128)S(1)}, u32[]{:S(2)}, u32[]{:S(2)}) collective-permute-start(f32[39,8,128]{2,1,0:T(8,128)S(1)} %get-tuple-element.43), channel_id=1, source_target_pairs={{1,2},{3,4},{5,6},{2,1},{4,3},{6,5},{0,0},{7,7},{9,10},{11,12},{13... | collective-permute-start | bytes 479240 | tf_op jit(solution)/shard_map/ppermute | solution.py:421
  5.4 3.1 %collective-permute-start.4 = (f32[38,8,128]{2,1,0:T(8,128)S(1)}, f32[38,8,128]{2,1,0:T(8,128)S(1)}, u32[]{:S(2)}, u32[]{:S(2)}) collective-permute-start(f32[38,8,128]{2,1,0:T(8,128)S(1)} %get-tuple-element.42), channel_id=1, source_target_pairs={{0,1},{2,3},{4,5},{6,7},{1,0},{3,2},{5,4},{7,6},{8,9},{10,11},{12,... | collective-permute-start | bytes 466952 | tf_op jit(solution)/shard_map/ppermute | solution.py:421
  8.5 0.0 collective-permute-start.2
  8.5 0.0 copy-start.2
  8.5 0.0 copy-start.4
  8.5 1.6 %collective-permute-start.3 = (f32[37,8,128]{2,1,0:T(8,128)S(1)}, f32[37,8,128]{2,1,0:T(8,128)S(1)}, u32[]{:S(2)}, u32[]{:S(2)}) collective-permute-start(f32[37,8,128]{2,1,0:T(8,128)S(1)} %get-tuple-element.41), channel_id=1, source_target_pairs={{8,16},{24,0},{16,8},{0,24},{9,17},{25,1},{17,9},{1,25},{10,18},{2... | collective-permute-start | bytes 454664 | tf_op jit(solution)/shard_map/ppermute | solution.py:421
  10.1 0.0 collective-permute-done.other_ref
  10.1 0.5 %collective-permute-start.1 = (f32[8,128]{1,0:T(8,128)S(1)}, f32[8,128]{1,0:T(8,128)S(1)}, u32[]{:S(2)}, u32[]{:S(2)}) collective-permute-start(f32[8,128]{1,0:T(8,128)S(1)} %shard_map.57), channel_id=1, source_target_pairs={{0,2},{1,3},{2,0},{3,1},{4,6},{5,7},{6,4},{7,5},{8,10},{9,11},{10,... | collective-permute-start | bytes 12296 | tf_op jit(solution)/shard_map/ppermute | solution.py:484
  10.6 0.0 copy-done.1
  10.6 0.0 copy-done.2
  10.6 0.0 copy-done.4
  10.6 2.2 %shard_map.55 = (f32[9,12,8,128]{3,2,1,0:T(8,128)S(1)}, f32[9,12,8,128]{3,2,1,0:T(8,128)S(1)}, f32[9,12,8,128]{3,2,1,0:T(8,128)S(1)}, f32[7,128,128]{2,1,0:T(8,128)S(1)}) custom-call(f32[9,12,8,128]{3,2,1,0:T(8,128)S(1)} %copy-done.1, f32[9,2,128]{2,1,0:T(2,128)S(1)} %bitcast.2, f32[2,48,128]{2,1,0:T(8,128)S(1)} %copy-done.2), custom_call_target="tpu_custom_call" | custom-call | flops 33177600 | bytes 33177600 | tf_op jit(solution)/shard_map/pallas_call | solution.py:455
  12.7 1.0 %collective-permute-done.1 = f32[8,128]{1,0:T(8,128)S(1)} collective-permute-done((f32[8,128]{1,0:T(8,128)S(1)}, f32[8,128]{1,0:T(8,128)S(1)}, u32[]{:S(2)}, u32[]{:S(2)}) %collective-permute-start.1) | collective-permute-done | bytes 4128 | tf_op jit(solution)/shard_map/ppermute | solution.py:484
  13.7 1.7 %collective-permute-start.6 = (f32[8,128]{1,0:T(8,128)S(1)}, f32[8,128]{1,0:T(8,128)S(1)}, u32[]{:S(2)}, u32[]{:S(2)}) collective-permute-start(f32[8,128]{1,0:T(8,128)S(1)} %max.3.most_ref), channel_id=1, source_target_pairs={{0,4},{1,5},{2,6},{3,7},{4,0},{5,1},{6,2},{7,3},{8,12},{9,13},{10,... | collective-permute-start | bytes 12296 | tf_op jit(solution)/shard_map/ppermute | solution.py:484
  15.4 0.0 collective-permute-done.2.near_ref
  15.4 0.0 collective-permute-done.3.far_ref
  15.4 0.8 %shard_map.59.part_ref = f32[9,12,8,128]{3,2,1,0:T(8,128)S(1)} custom-call(f32[9,12,8,128]{3,2,1,0:T(8,128)S(1)} %copy-done.1, f32[9,12,8,128]{3,2,1,0:T(8,128)S(1)} %get-tuple-element.37.speed_ref, f32[9,12,8,128]{3,2,1,0:T(8,128)S(1)} %get-tuple-element.39.part_ref, f32[37,8,128]{2,1,0:T(8,128)S(1)} %collective-permute-done.2.near_ref, ...), custom_call_target="tpu_custom_call" | custom-call | tf_op jit(solution)/shard_map/pallas_call | solution.py:455
  16.2 0.0 collective-permute-done.4.near_ref
  16.2 0.0 collective-permute-done.5.far_ref
  16.3 0.0 copy-start.5
  16.3 0.0 copy-start.6
  16.3 0.8 %shard_map.60 = (f32[9,12,8,128]{3,2,1,0:T(8,128)S(1)}, f32[9,12,8,128]{3,2,1,0:T(8,128)S(1)}) custom-call(f32[9,12,8,128]{3,2,1,0:T(8,128)S(1)} %copy-done.1, f32[9,12,8,128]{3,2,1,0:T(8,128)S(1)} %shard_map.59.part_ref, f32[38,8,128]{2,1,0:T(8,128)S(1)} %collective-permute-done.4.near_ref, f32[39,8,128]{2,1,0:T(8,128)S(1)} %collective-permute-done.5.far_ref, ...), custom_call_target="tpu_custom_call" | custom-call | tf_op jit(solution)/shard_map/pallas_call | solution.py:455
  17.1 1.1 %collective-permute-done.6.other_ref = f32[8,128]{1,0:T(8,128)S(1)} collective-permute-done((f32[8,128]{1,0:T(8,128)S(1)}, f32[8,128]{1,0:T(8,128)S(1)}, u32[]{:S(2)}, u32[]{:S(2)}) %collective-permute-start.6) | collective-permute-done | bytes 4128 | tf_op jit(solution)/shard_map/ppermute | solution.py:484
  18.2 0.0 copy-done.5
  18.2 0.0 copy-done.6
  18.2 0.3 shard_map.61
  18.6 0.2 collective-permute-start.7
  18.8 0.0 collective-permute-start.9
  18.8 3.9 %collective-permute-start.10 = (f32[36,8,128]{2,1,0:T(8,128)S(1)}, f32[36,8,128]{2,1,0:T(8,128)S(1)}, u32[]{:S(2)}, u32[]{:S(2)}) collective-permute-start(f32[36,8,128]{2,1,0:T(8,128)S(1)} %get-tuple-element.57), channel_id=1, source_target_pairs={{1,2},{3,4},{5,6},{2,1},{4,3},{6,5},{0,0},{7,7},{9,10},{11,12},{13... | collective-permute-start | bytes 442376 | tf_op jit(solution)/shard_map/ppermute | solution.py:421
  22.7 0.4 %collective-permute-start.8 = (f32[27,8,128]{2,1,0:T(8,128)S(1)}, f32[27,8,128]{2,1,0:T(8,128)S(1)}, u32[]{:S(2)}, u32[]{:S(2)}) collective-permute-start(f32[27,8,128]{2,1,0:T(8,128)S(1)} %get-tuple-element.55), channel_id=1, source_target_pairs={{0,8},{16,24},{8,0},{24,16},{1,9},{17,25},{9,1},{25,17},{2,10},{18... | collective-permute-start | bytes 331784 | tf_op jit(solution)/shard_map/ppermute | solution.py:421
  23.1 2.0 %shard_map.62 = (f32[9,12,8,128]{3,2,1,0:T(8,128)S(1)}, f32[9,12,8,128]{3,2,1,0:T(8,128)S(1)}) custom-call(f32[9,12,8,128]{3,2,1,0:T(8,128)S(1)} %get-tuple-element.48.s_ref, f32[7,128,128]{2,1,0:T(8,128)S(1)} %get-tuple-element.49.rest_0_, f32[8,128]{1,0:T(8,128)S(1)} %get-tuple-element.50.rest_1_.pk_ref), custom_call_target="tpu_custom_call" | custom-call | tf_op jit(solution)/shard_map/pallas_call | solution.py:455
  25.1 0.0 collective-permute-done.7.ghosts_ref
  25.1 0.0 collective-permute-done.8.near_ref
  25.1 0.0 collective-permute-done.9.far_ref
  25.1 0.8 %shard_map.63.part_ref = f32[9,12,8,128]{3,2,1,0:T(8,128)S(1)} custom-call(f32[9,12,8,128]{3,2,1,0:T(8,128)S(1)} %get-tuple-element.48.s_ref, f32[9,12,8,128]{3,2,1,0:T(8,128)S(1)} %get-tuple-element.51.speed_ref, f32[9,12,8,128]{3,2,1,0:T(8,128)S(1)} %get-tuple-element.54.part_ref, f32[27,8,128]{2,1,0:T(8,128)S(1)} %collective-permute-done.8.near_ref, ...), custom_call_target="tpu_custom_call" | custom-call | flops 110592000 | bytes 110592000 | tf_op jit(solution)/shard_map/pallas_call | solution.py:455
  26.0 0.7 %shard_map.64 = (f32[9,12,8,128]{3,2,1,0:T(8,128)S(1)}, f32[38,8,128]{2,1,0:T(8,128)S(1)}) custom-call(f32[9,12,8,128]{3,2,1,0:T(8,128)S(1)} %copy-done.1, f32[9,12,8,128]{3,2,1,0:T(8,128)S(1)} %get-tuple-element.48.s_ref, f32[9,12,8,128]{3,2,1,0:T(8,128)S(1)} %shard_map.63.part_ref, f32[38,8,128]{2,1,0:T(8,128)S(1)} %collective-permute-done.7.ghosts_ref, ...), custom_call_target="tpu_custom_call" | custom-call | tf_op jit(solution)/shard_map/pallas_call | solution.py:455
  26.6 1.1 %collective-permute-start.11 = (f32[38,8,128]{2,1,0:T(8,128)S(1)}, f32[38,8,128]{2,1,0:T(8,128)S(1)}, u32[]{:S(2)}, u32[]{:S(2)}) collective-permute-start(f32[38,8,128]{2,1,0:T(8,128)S(1)} %get-tuple-element.61), channel_id=1, source_target_pairs={{0,1},{2,3},{4,5},{6,7},{1,0},{3,2},{5,4},{7,6},{8,9},{10,11},{12,... | collective-permute-start | bytes 466952 | tf_op jit(solution)/shard_map/ppermute | solution.py:421
  27.7 0.2 collective-permute-done.10.ghosts_ref
  27.9 0.4 %shard_map.65 = (f32[9,12,8,128]{3,2,1,0:T(8,128)S(1)}, f32[36,8,128]{2,1,0:T(8,128)S(1)}, f32[27,8,128]{2,1,0:T(8,128)S(1)}, f32[37,8,128]{2,1,0:T(8,128)S(1)}) custom-call(f32[9,12,8,128]{3,2,1,0:T(8,128)S(1)} %copy-done.1, f32[9,12,8,128]{3,2,1,0:T(8,128)S(1)} %get-tuple-element.48.s_ref, f32[9,12,8,128]{3,2,1,0:T(8,128)S(1)} %shard_map.63.part_ref, ...), custom_call_target="tpu_custom_call" | custom-call | tf_op jit(solution)/shard_map/pallas_call | solution.py:455
  28.4 0.7 %collective-permute-start.13 = (f32[37,8,128]{2,1,0:T(8,128)S(1)}, f32[37,8,128]{2,1,0:T(8,128)S(1)}, u32[]{:S(2)}, u32[]{:S(2)}) collective-permute-start(f32[37,8,128]{2,1,0:T(8,128)S(1)} %get-tuple-element.66), channel_id=1, source_target_pairs={{8,16},{24,0},{16,8},{0,24},{9,17},{25,1},{17,9},{1,25},{10,18},{2... | collective-permute-start | bytes 454664 | tf_op jit(solution)/shard_map/ppermute | solution.py:421
  29.0 3.8 %collective-permute-start.14 = (f32[36,8,128]{2,1,0:T(8,128)S(1)}, f32[36,8,128]{2,1,0:T(8,128)S(1)}, u32[]{:S(2)}, u32[]{:S(2)}) collective-permute-start(f32[36,8,128]{2,1,0:T(8,128)S(1)} %get-tuple-element.67), channel_id=1, source_target_pairs={{1,2},{3,4},{5,6},{2,1},{4,3},{6,5},{0,0},{7,7},{9,10},{11,12},{13... | collective-permute-start | bytes 442376 | tf_op jit(solution)/shard_map/ppermute | solution.py:421
  32.8 0.1 collective-permute-start.12
  32.9 0.0 collective-permute-done.11.ghosts_ref
  32.9 2.0 %shard_map.66 = (f32[9,12,8,128]{3,2,1,0:T(8,128)S(1)}, f32[9,12,8,128]{3,2,1,0:T(8,128)S(1)}) custom-call(f32[9,12,8,128]{3,2,1,0:T(8,128)S(1)} %get-tuple-element.62.s_ref, f32[7,128,128]{2,1,0:T(8,128)S(1)} %get-tuple-element.49.rest_0_, f32[8,128]{1,0:T(8,128)S(1)} %get-tuple-element.50.rest_1_.pk_ref), custom_call_target="tpu_custom_call" | custom-call | tf_op jit(solution)/shard_map/pallas_call | solution.py:455
  34.9 0.0 collective-permute-done.12.near_ref
  34.9 0.0 collective-permute-done.13.far_ref
  34.9 0.8 %shard_map.67.part_ref = f32[9,12,8,128]{3,2,1,0:T(8,128)S(1)} custom-call(f32[9,12,8,128]{3,2,1,0:T(8,128)S(1)} %get-tuple-element.62.s_ref, f32[9,12,8,128]{3,2,1,0:T(8,128)S(1)} %get-tuple-element.63.speed_ref, f32[9,12,8,128]{3,2,1,0:T(8,128)S(1)} %get-tuple-element.64.part_ref, f32[27,8,128]{2,1,0:T(8,128)S(1)} %collective-permute-done.12.near_ref, ...), custom_call_target="tpu_custom_call" | custom-call | flops 110592000 | bytes 110592000 | tf_op jit(solution)/shard_map/pallas_call | solution.py:455
  35.8 0.7 %shard_map.68.refs_0_ = f32[9,12,8,128]{3,2,1,0:T(8,128)S(1)} custom-call(f32[9,12,8,128]{3,2,1,0:T(8,128)S(1)} %copy-done.1, f32[9,12,8,128]{3,2,1,0:T(8,128)S(1)} %get-tuple-element.62.s_ref, f32[9,12,8,128]{3,2,1,0:T(8,128)S(1)} %shard_map.67.part_ref, f32[38,8,128]{2,1,0:T(8,128)S(1)} %collective-permute-done.11.ghosts_ref, f32[9,2,128]{2,1,0:T(2,128)S(1)} %bitcast.6, ...), custom_call_target="tpu_custom_call" | custom-call | tf_op jit(solution)/shard_map/pallas_call | solution.py:455
  36.4 1.9 %collective-permute-done.14.ghosts_ref = f32[36,8,128]{2,1,0:T(8,128)S(1)} collective-permute-done((f32[36,8,128]{2,1,0:T(8,128)S(1)}, f32[36,8,128]{2,1,0:T(8,128)S(1)}, u32[]{:S(2)}, u32[]{:S(2)}) %collective-permute-start.14) | collective-permute-done | bytes 147488 | tf_op jit(solution)/shard_map/ppermute | solution.py:421
  38.3 1.1 %shard_map.69 = f32[9,12,8,128]{3,2,1,0:T(8,128)} custom-call(f32[9,12,8,128]{3,2,1,0:T(8,128)S(1)} %copy-done.1, f32[9,12,8,128]{3,2,1,0:T(8,128)S(1)} %get-tuple-element.62.s_ref, f32[9,12,8,128]{3,2,1,0:T(8,128)S(1)} %shard_map.67.part_ref, f32[36,8,128]{2,1,0:T(8,128)S(1)} %collective-permute-done.14.ghosts_ref, f32[9,2,128]{2,1,0:T(2,128)S(1)} %bitcast.7, ...), custom_call_target="tpu_custom_call" | custom-call | tf_op jit(solution)/shard_map/pallas_call | solution.py:455
  (4 shorter events, 0.1 us)
Async XLA Ops:
  0.0 0.7 %copy-start.3 = (f32[2,9,128]{2,0,1:T(2,128)S(1)}, f32[2,9,128]{2,0,1:T(2,128)}, u32[]{:S(2)}) copy-start(f32[2,9,128]{2,0,1:T(2,128)} %param.6) | copy-start | bytes 27652
  0.7 9.4 %collective-permute-start = (f32[40,8,128]{2,1,0:T(8,128)S(1)}, f32[40,8,128]{2,1,0:T(8,128)S(1)}, u32[]{:S(2)}, u32[]{:S(2)}) collective-permute-start(f32[40,8,128]{2,1,0:T(8,128)S(1)} %shard_map.56.own_ref), channel_id=1, source_target_pairs={{0,1},{1,0},{2,3},{3,2},{4,5},{5,4},{6,7},{7,6},{8,9},{9,8},{10,11... | collective-permute-start | bytes 491528 | tf_op jit(solution)/shard_map/ppermute | solution.py:484
  2.3 1.0 %copy-start = (f32[9,12,8,128]{3,2,1,0:T(8,128)S(1)}, f32[9,12,8,128]{3,2,1,0:T(8,128)}, u32[]{:S(2)}) copy-start(f32[9,12,8,128]{3,2,1,0:T(8,128)} %base_ref.7) | copy-start | bytes 1327108
  3.3 7.3 %copy-start.1 = (f32[9,12,8,128]{3,2,1,0:T(8,128)S(1)}, f32[9,12,8,128]{3,2,1,0:T(8,128)}, u32[]{:S(2)}) copy-start(f32[9,12,8,128]{3,2,1,0:T(8,128)} %base_ref.7) | copy-start | bytes 1327108
  3.3 12.9 %collective-permute-start.5 = (f32[39,8,128]{2,1,0:T(8,128)S(1)}, f32[39,8,128]{2,1,0:T(8,128)S(1)}, u32[]{:S(2)}, u32[]{:S(2)}) collective-permute-start(f32[39,8,128]{2,1,0:T(8,128)S(1)} %get-tuple-element.43), channel_id=1, source_target_pairs={{1,2},{3,4},{5,6},{2,1},{4,3},{6,5},{0,0},{7,7},{9,10},{11,12},{13... | collective-permute-start | bytes 479240 | tf_op jit(solution)/shard_map/ppermute | solution.py:421
  5.4 10.8 %collective-permute-start.4 = (f32[38,8,128]{2,1,0:T(8,128)S(1)}, f32[38,8,128]{2,1,0:T(8,128)S(1)}, u32[]{:S(2)}, u32[]{:S(2)}) collective-permute-start(f32[38,8,128]{2,1,0:T(8,128)S(1)} %get-tuple-element.42), channel_id=1, source_target_pairs={{0,1},{2,3},{4,5},{6,7},{1,0},{3,2},{5,4},{7,6},{8,9},{10,11},{12,... | collective-permute-start | bytes 466952 | tf_op jit(solution)/shard_map/ppermute | solution.py:421
  8.5 6.9 %collective-permute-start.2 = (f32[37,8,128]{2,1,0:T(8,128)S(1)}, f32[37,8,128]{2,1,0:T(8,128)S(1)}, u32[]{:S(2)}, u32[]{:S(2)}) collective-permute-start(f32[37,8,128]{2,1,0:T(8,128)S(1)} %get-tuple-element.40), channel_id=1, source_target_pairs={{0,8},{16,24},{8,0},{24,16},{1,9},{17,25},{9,1},{25,17},{2,10},{18... | collective-permute-start | bytes 454664 | tf_op jit(solution)/shard_map/ppermute | solution.py:421
  8.5 2.1 %copy-start.2 = (f32[2,48,128]{2,1,0:T(8,128)S(1)}, f32[2,48,128]{2,1,0:T(8,128)}, u32[]{:S(2)}) copy-start(f32[2,48,128]{2,1,0:T(8,128)} %constant.2.clone.rest_1_.waves_ref) | copy-start | bytes 147460
  8.5 2.1 %copy-start.4 = (f32[2,9,128]{2,0,1:T(2,128)S(1)}, f32[2,9,128]{2,0,1:T(2,128)}, u32[]{:S(2)}) copy-start(f32[2,9,128]{2,0,1:T(2,128)} %param.6) | copy-start | bytes 27652
  8.5 6.9 %collective-permute-start.3 = (f32[37,8,128]{2,1,0:T(8,128)S(1)}, f32[37,8,128]{2,1,0:T(8,128)S(1)}, u32[]{:S(2)}, u32[]{:S(2)}) collective-permute-start(f32[37,8,128]{2,1,0:T(8,128)S(1)} %get-tuple-element.41), channel_id=1, source_target_pairs={{8,16},{24,0},{16,8},{0,24},{9,17},{25,1},{17,9},{1,25},{10,18},{2... | collective-permute-start | bytes 454664 | tf_op jit(solution)/shard_map/ppermute | solution.py:421
  10.1 3.6 %collective-permute-start.1 = (f32[8,128]{1,0:T(8,128)S(1)}, f32[8,128]{1,0:T(8,128)S(1)}, u32[]{:S(2)}, u32[]{:S(2)}) collective-permute-start(f32[8,128]{1,0:T(8,128)S(1)} %shard_map.57), channel_id=1, source_target_pairs={{0,2},{1,3},{2,0},{3,1},{4,6},{5,7},{6,4},{7,5},{8,10},{9,11},{10,... | collective-permute-start | bytes 12296 | tf_op jit(solution)/shard_map/ppermute | solution.py:484
  13.7 4.5 %collective-permute-start.6 = (f32[8,128]{1,0:T(8,128)S(1)}, f32[8,128]{1,0:T(8,128)S(1)}, u32[]{:S(2)}, u32[]{:S(2)}) collective-permute-start(f32[8,128]{1,0:T(8,128)S(1)} %max.3.most_ref), channel_id=1, source_target_pairs={{0,4},{1,5},{2,6},{3,7},{4,0},{5,1},{6,2},{7,3},{8,12},{9,13},{10,... | collective-permute-start | bytes 12296 | tf_op jit(solution)/shard_map/ppermute | solution.py:484
  16.3 2.0 %copy-start.5 = (s32[9,128]{1,0:T(8,128)S(1)}, s32[9,128]{1,0:T(8,128)}, u32[]{:S(2)}) copy-start(s32[9,128]{1,0:T(8,128)} %mask_ref.9) | copy-start | bytes 13828
  16.3 2.0 %copy-start.6 = (f32[9,128]{1,0:T(8,128)S(1)}, f32[9,128]{1,0:T(8,128)}, u32[]{:S(2)}) copy-start(f32[9,128]{1,0:T(8,128)} %depth_ref.9) | copy-start | bytes 13828
  18.6 6.5 %collective-permute-start.7 = (f32[38,8,128]{2,1,0:T(8,128)S(1)}, f32[38,8,128]{2,1,0:T(8,128)S(1)}, u32[]{:S(2)}, u32[]{:S(2)}) collective-permute-start(f32[38,8,128]{2,1,0:T(8,128)S(1)} %get-tuple-element.53), channel_id=1, source_target_pairs={{0,1},{2,3},{4,5},{6,7},{1,0},{3,2},{5,4},{7,6},{8,9},{10,11},{12,... | collective-permute-start | bytes 466952 | tf_op jit(solution)/shard_map/ppermute | solution.py:421
  18.8 6.4 %collective-permute-start.9 = (f32[37,8,128]{2,1,0:T(8,128)S(1)}, f32[37,8,128]{2,1,0:T(8,128)S(1)}, u32[]{:S(2)}, u32[]{:S(2)}) collective-permute-start(f32[37,8,128]{2,1,0:T(8,128)S(1)} %get-tuple-element.56), channel_id=1, source_target_pairs={{8,16},{24,0},{16,8},{0,24},{9,17},{25,1},{17,9},{1,25},{10,18},{2... | collective-permute-start | bytes 454664 | tf_op jit(solution)/shard_map/ppermute | solution.py:421
  18.8 9.2 %collective-permute-start.10 = (f32[36,8,128]{2,1,0:T(8,128)S(1)}, f32[36,8,128]{2,1,0:T(8,128)S(1)}, u32[]{:S(2)}, u32[]{:S(2)}) collective-permute-start(f32[36,8,128]{2,1,0:T(8,128)S(1)} %get-tuple-element.57), channel_id=1, source_target_pairs={{1,2},{3,4},{5,6},{2,1},{4,3},{6,5},{0,0},{7,7},{9,10},{11,12},{13... | collective-permute-start | bytes 442376 | tf_op jit(solution)/shard_map/ppermute | solution.py:421
  22.7 2.4 %collective-permute-start.8 = (f32[27,8,128]{2,1,0:T(8,128)S(1)}, f32[27,8,128]{2,1,0:T(8,128)S(1)}, u32[]{:S(2)}, u32[]{:S(2)}) collective-permute-start(f32[27,8,128]{2,1,0:T(8,128)S(1)} %get-tuple-element.55), channel_id=1, source_target_pairs={{0,8},{16,24},{8,0},{24,16},{1,9},{17,25},{9,1},{25,17},{2,10},{18... | collective-permute-start | bytes 331784 | tf_op jit(solution)/shard_map/ppermute | solution.py:421
  26.6 6.3 %collective-permute-start.11 = (f32[38,8,128]{2,1,0:T(8,128)S(1)}, f32[38,8,128]{2,1,0:T(8,128)S(1)}, u32[]{:S(2)}, u32[]{:S(2)}) collective-permute-start(f32[38,8,128]{2,1,0:T(8,128)S(1)} %get-tuple-element.61), channel_id=1, source_target_pairs={{0,1},{2,3},{4,5},{6,7},{1,0},{3,2},{5,4},{7,6},{8,9},{10,11},{12,... | collective-permute-start | bytes 466952 | tf_op jit(solution)/shard_map/ppermute | solution.py:421
  28.4 6.6 %collective-permute-start.13 = (f32[37,8,128]{2,1,0:T(8,128)S(1)}, f32[37,8,128]{2,1,0:T(8,128)S(1)}, u32[]{:S(2)}, u32[]{:S(2)}) collective-permute-start(f32[37,8,128]{2,1,0:T(8,128)S(1)} %get-tuple-element.66), channel_id=1, source_target_pairs={{8,16},{24,0},{16,8},{0,24},{9,17},{25,1},{17,9},{1,25},{10,18},{2... | collective-permute-start | bytes 454664 | tf_op jit(solution)/shard_map/ppermute | solution.py:421
  29.0 9.3 %collective-permute-start.14 = (f32[36,8,128]{2,1,0:T(8,128)S(1)}, f32[36,8,128]{2,1,0:T(8,128)S(1)}, u32[]{:S(2)}, u32[]{:S(2)}) collective-permute-start(f32[36,8,128]{2,1,0:T(8,128)S(1)} %get-tuple-element.67), channel_id=1, source_target_pairs={{1,2},{3,4},{5,6},{2,1},{4,3},{6,5},{0,0},{7,7},{9,10},{11,12},{13... | collective-permute-start | bytes 442376 | tf_op jit(solution)/shard_map/ppermute | solution.py:421
  32.8 2.1 %collective-permute-start.12 = (f32[27,8,128]{2,1,0:T(8,128)S(1)}, f32[27,8,128]{2,1,0:T(8,128)S(1)}, u32[]{:S(2)}, u32[]{:S(2)}) collective-permute-start(f32[27,8,128]{2,1,0:T(8,128)S(1)} %get-tuple-element.65), channel_id=1, source_target_pairs={{0,8},{16,24},{8,0},{24,16},{1,9},{17,25},{9,1},{25,17},{2,10},{18... | collective-permute-start | bytes 331784 | tf_op jit(solution)/shard_map/ppermute | solution.py:421

commit v24 on v21

--- a/solution.py
+++ b/solution.py
@@ -513,7 +513,7 @@
             last = functools.partial(section_kernel, section, (0, planes - rim), speed_step)
             early, *x_next = call(last, ins, outs, [rows, rows])
             ins = ins[:3] + [x_far] + ins[4:] + [early]
-            outs = [field] + (far_shapes if more else [])
+            outs = [field] + ([shape(short)] + [shape(rim * planes)] * 2 if more else [])
             last = functools.partial(section_kernel, section, (planes - rim, planes), speed_step)
             values, *far_next = call(last, ins, outs, [rows, rows])
             if more:

time: 39.8 us -> 40.9 us (1.028)
  the two profiles are of different devices: /device:TPU:8 before, /device:TPU:9 now
where the time goes in v24:
time: 40.9 us; the launch traced here: 40.6 us
  starting transfers between devices  22.7 us (56%)
  Pallas kernels  12.7 us (31%)
  waiting for transfers between devices  3.3 us (8%)
  local copies, waits for them, and re-layouts  1.74 us (4%)
    ppermute x12, starting transfers between devices, trade(): return lax.ppermute(value, axis, pairs)  19.3 us
    pallas_call x15, Pallas kernels, call(): pl.pallas_call(kernel, out_shape=outs, in_specs=[vmem] * len(ins), out_sp...  12.7 us
    ppermute x3, starting transfers between devices, spread(): return lax.ppermute(most, 'gx', pairs)  3.45 us
    ppermute x12, waiting for transfers between devices, trade(): return lax.ppermute(value, axis, pairs)  2.89 us
    unnamed x14, local copies, waits for them, and re-layouts  1.74 us
  transfers between devices with their start and end apart: 15, of which 3 were waited for; matrix products, arithmetic and copies ran while one was open for 0% of the time, Pallas kernels for 28%

profile of v24, /device:TPU:9, one launch (start us, length us, event | category | flops | bytes accessed | tf_op | source)
XLA Modules:
  0.0 40.6 jit_solution(9752567470112436039)
XLA Ops:
  0.0 0.0 copy-start.3
  0.0 0.7 %copy-done.3 = f32[2,9,128]{2,0,1:T(2,128)S(1)} copy-done((f32[2,9,128]{2,0,1:T(2,128)S(1)}, f32[2,9,128]{2,0,1:T(2,128)}, u32[]{:S(2)}) %copy-start.3) | copy-done | bytes 9240
  0.7 1.3 %collective-permute-start = (f32[40,8,128]{2,1,0:T(8,128)S(1)}, f32[40,8,128]{2,1,0:T(8,128)S(1)}, u32[]{:S(2)}, u32[]{:S(2)}) collective-permute-start(f32[40,8,128]{2,1,0:T(8,128)S(1)} %shard_map.56.own_ref), channel_id=1, source_target_pairs={{0,1},{1,0},{2,3},{3,2},{4,5},{5,4},{6,7},{7,6},{8,9},{9,8},{10,11... | collective-permute-start | bytes 491528 | tf_op jit(solution)/shard_map/ppermute | solution.py:465
  2.0 0.0 copy-start
  2.0 1.0 %copy-done = f32[9,12,8,128]{3,2,1,0:T(8,128)S(1)} copy-done((f32[9,12,8,128]{3,2,1,0:T(8,128)S(1)}, f32[9,12,8,128]{3,2,1,0:T(8,128)}, u32[]{:S(2)}) %copy-start) | copy-done | bytes 442392
  3.0 0.0 copy-start.1
  3.1 2.1 %collective-permute-start.5 = (f32[39,8,128]{2,1,0:T(8,128)S(1)}, f32[39,8,128]{2,1,0:T(8,128)S(1)}, u32[]{:S(2)}, u32[]{:S(2)}) collective-permute-start(f32[39,8,128]{2,1,0:T(8,128)S(1)} %get-tuple-element.43), channel_id=1, source_target_pairs={{1,2},{3,4},{5,6},{2,1},{4,3},{6,5},{0,0},{7,7},{9,10},{11,12},{13... | collective-permute-start | bytes 479240 | tf_op jit(solution)/shard_map/ppermute | solution.py:402
  5.1 2.5 %collective-permute-start.4 = (f32[38,8,128]{2,1,0:T(8,128)S(1)}, f32[38,8,128]{2,1,0:T(8,128)S(1)}, u32[]{:S(2)}, u32[]{:S(2)}) collective-permute-start(f32[38,8,128]{2,1,0:T(8,128)S(1)} %get-tuple-element.42), channel_id=1, source_target_pairs={{0,1},{2,3},{4,5},{6,7},{1,0},{3,2},{5,4},{7,6},{8,9},{10,11},{12,... | collective-permute-start | bytes 466952 | tf_op jit(solution)/shard_map/ppermute | solution.py:402
  7.7 1.5 %collective-permute-start.2 = (f32[37,8,128]{2,1,0:T(8,128)S(1)}, f32[37,8,128]{2,1,0:T(8,128)S(1)}, u32[]{:S(2)}, u32[]{:S(2)}) collective-permute-start(f32[37,8,128]{2,1,0:T(8,128)S(1)} %get-tuple-element.40), channel_id=1, source_target_pairs={{0,8},{16,24},{8,0},{24,16},{1,9},{17,25},{9,1},{25,17},{2,10},{18... | collective-permute-start | bytes 454664 | tf_op jit(solution)/shard_map/ppermute | solution.py:402
  9.2 0.0 copy-start.2
  9.2 0.0 copy-start.4
  9.2 1.1 %collective-permute-start.3 = (f32[37,8,128]{2,1,0:T(8,128)S(1)}, f32[37,8,128]{2,1,0:T(8,128)S(1)}, u32[]{:S(2)}, u32[]{:S(2)}) collective-permute-start(f32[37,8,128]{2,1,0:T(8,128)S(1)} %get-tuple-element.41), channel_id=1, source_target_pairs={{8,16},{24,0},{16,8},{0,24},{9,17},{25,1},{17,9},{1,25},{10,18},{2... | collective-permute-start | bytes 454664 | tf_op jit(solution)/shard_map/ppermute | solution.py:402
  10.3 0.0 collective-permute-done.other_ref
  10.3 0.2 collective-permute-start.1
  10.5 0.0 copy-done.1
  10.5 0.0 copy-done.2
  10.5 0.0 copy-done.4
  10.5 2.2 %shard_map.55 = (f32[9,12,8,128]{3,2,1,0:T(8,128)S(1)}, f32[9,12,8,128]{3,2,1,0:T(8,128)S(1)}, f32[9,12,8,128]{3,2,1,0:T(8,128)S(1)}, f32[7,128,128]{2,1,0:T(8,128)S(1)}) custom-call(f32[9,12,8,128]{3,2,1,0:T(8,128)S(1)} %copy-done.1, f32[9,2,128]{2,1,0:T(2,128)S(1)} %bitcast.2, f32[2,48,128]{2,1,0:T(8,128)S(1)} %copy-done.2), custom_call_target="tpu_custom_call" | custom-call | flops 33177600 | bytes 33177600 | tf_op jit(solution)/shard_map/pallas_call | solution.py:436
  12.6 0.4 %collective-permute-done.1 = f32[8,128]{1,0:T(8,128)S(1)} collective-permute-done((f32[8,128]{1,0:T(8,128)S(1)}, f32[8,128]{1,0:T(8,128)S(1)}, u32[]{:S(2)}, u32[]{:S(2)}) %collective-permute-start.1) | collective-permute-done | bytes 4128 | tf_op jit(solution)/shard_map/ppermute | solution.py:465
  13.0 2.0 %collective-permute-start.6 = (f32[8,128]{1,0:T(8,128)S(1)}, f32[8,128]{1,0:T(8,128)S(1)}, u32[]{:S(2)}, u32[]{:S(2)}) collective-permute-start(f32[8,128]{1,0:T(8,128)S(1)} %max.3.most_ref), channel_id=1, source_target_pairs={{0,4},{1,5},{2,6},{3,7},{4,0},{5,1},{6,2},{7,3},{8,12},{9,13},{10,... | collective-permute-start | bytes 12296 | tf_op jit(solution)/shard_map/ppermute | solution.py:465
  15.0 0.0 collective-permute-done.2.near_ref
  15.0 0.0 collective-permute-done.3.far_ref
  15.0 0.8 %shard_map.59.part_ref = f32[9,12,8,128]{3,2,1,0:T(8,128)S(1)} custom-call(f32[9,12,8,128]{3,2,1,0:T(8,128)S(1)} %copy-done.1, f32[9,12,8,128]{3,2,1,0:T(8,128)S(1)} %get-tuple-element.37.speed_ref, f32[9,12,8,128]{3,2,1,0:T(8,128)S(1)} %get-tuple-element.39.part_ref, f32[37,8,128]{2,1,0:T(8,128)S(1)} %collective-permute-done.2.near_ref, ...), custom_call_target="tpu_custom_call" | custom-call | tf_op jit(solution)/shard_map/pallas_call | solution.py:436
  15.8 0.0 collective-permute-done.4.near_ref
  15.9 0.0 collective-permute-done.5.far_ref
  15.9 0.0 copy-start.5
  15.9 0.0 copy-start.6
  15.9 0.8 %shard_map.60 = (f32[9,12,8,128]{3,2,1,0:T(8,128)S(1)}, f32[9,12,8,128]{3,2,1,0:T(8,128)S(1)}) custom-call(f32[9,12,8,128]{3,2,1,0:T(8,128)S(1)} %copy-done.1, f32[9,12,8,128]{3,2,1,0:T(8,128)S(1)} %shard_map.59.part_ref, f32[38,8,128]{2,1,0:T(8,128)S(1)} %collective-permute-done.4.near_ref, f32[39,8,128]{2,1,0:T(8,128)S(1)} %collective-permute-done.5.far_ref, ...), custom_call_target="tpu_custom_call" | custom-call | tf_op jit(solution)/shard_map/pallas_call | solution.py:436
  16.7 0.0 collective-permute-done.6.other_ref
  16.7 0.0 copy-done.5
  16.7 0.0 copy-done.6
  16.8 0.4 shard_map.61
  17.1 0.1 collective-permute-start.7
  17.2 2.4 %collective-permute-start.9 = (f32[37,8,128]{2,1,0:T(8,128)S(1)}, f32[37,8,128]{2,1,0:T(8,128)S(1)}, u32[]{:S(2)}, u32[]{:S(2)}) collective-permute-start(f32[37,8,128]{2,1,0:T(8,128)S(1)} %get-tuple-element.56), channel_id=1, source_target_pairs={{8,16},{24,0},{16,8},{0,24},{9,17},{25,1},{17,9},{1,25},{10,18},{2... | collective-permute-start | bytes 454664 | tf_op jit(solution)/shard_map/ppermute | solution.py:402
  19.6 3.7 %collective-permute-start.10 = (f32[36,8,128]{2,1,0:T(8,128)S(1)}, f32[36,8,128]{2,1,0:T(8,128)S(1)}, u32[]{:S(2)}, u32[]{:S(2)}) collective-permute-start(f32[36,8,128]{2,1,0:T(8,128)S(1)} %get-tuple-element.57), channel_id=1, source_target_pairs={{1,2},{3,4},{5,6},{2,1},{4,3},{6,5},{0,0},{7,7},{9,10},{11,12},{13... | collective-permute-start | bytes 442376 | tf_op jit(solution)/shard_map/ppermute | solution.py:402
  23.3 0.2 collective-permute-start.8
  23.5 2.0 %shard_map.62 = (f32[9,12,8,128]{3,2,1,0:T(8,128)S(1)}, f32[9,12,8,128]{3,2,1,0:T(8,128)S(1)}) custom-call(f32[9,12,8,128]{3,2,1,0:T(8,128)S(1)} %get-tuple-element.48.s_ref, f32[7,128,128]{2,1,0:T(8,128)S(1)} %get-tuple-element.49.rest_0_, f32[8,128]{1,0:T(8,128)S(1)} %get-tuple-element.50.rest_1_.pk_ref), custom_call_target="tpu_custom_call" | custom-call | tf_op jit(solution)/shard_map/pallas_call | solution.py:436
  25.4 0.0 collective-permute-done.7.ghosts_ref
  25.5 0.0 collective-permute-done.8.near_ref
  25.5 0.0 collective-permute-done.9.far_ref
  25.5 0.8 %shard_map.63.part_ref = f32[9,12,8,128]{3,2,1,0:T(8,128)S(1)} custom-call(f32[9,12,8,128]{3,2,1,0:T(8,128)S(1)} %get-tuple-element.48.s_ref, f32[9,12,8,128]{3,2,1,0:T(8,128)S(1)} %get-tuple-element.51.speed_ref, f32[9,12,8,128]{3,2,1,0:T(8,128)S(1)} %get-tuple-element.54.part_ref, f32[27,8,128]{2,1,0:T(8,128)S(1)} %collective-permute-done.8.near_ref, ...), custom_call_target="tpu_custom_call" | custom-call | flops 110592000 | bytes 110592000 | tf_op jit(solution)/shard_map/pallas_call | solution.py:436
  26.3 0.7 %shard_map.64 = (f32[9,12,8,128]{3,2,1,0:T(8,128)S(1)}, f32[38,8,128]{2,1,0:T(8,128)S(1)}) custom-call(f32[9,12,8,128]{3,2,1,0:T(8,128)S(1)} %copy-done.1, f32[9,12,8,128]{3,2,1,0:T(8,128)S(1)} %get-tuple-element.48.s_ref, f32[9,12,8,128]{3,2,1,0:T(8,128)S(1)} %shard_map.63.part_ref, f32[38,8,128]{2,1,0:T(8,128)S(1)} %collective-permute-done.7.ghosts_ref, ...), custom_call_target="tpu_custom_call" | custom-call | tf_op jit(solution)/shard_map/pallas_call | solution.py:436
  27.0 0.8 %collective-permute-start.11 = (f32[38,8,128]{2,1,0:T(8,128)S(1)}, f32[38,8,128]{2,1,0:T(8,128)S(1)}, u32[]{:S(2)}, u32[]{:S(2)}) collective-permute-start(f32[38,8,128]{2,1,0:T(8,128)S(1)} %get-tuple-element.61), channel_id=1, source_target_pairs={{0,1},{2,3},{4,5},{6,7},{1,0},{3,2},{5,4},{7,6},{8,9},{10,11},{12,... | collective-permute-start | bytes 466952 | tf_op jit(solution)/shard_map/ppermute | solution.py:402
  27.7 0.2 collective-permute-done.10.ghosts_ref
  27.9 0.4 %shard_map.65 = (f32[9,12,8,128]{3,2,1,0:T(8,128)S(1)}, f32[36,8,128]{2,1,0:T(8,128)S(1)}, f32[27,8,128]{2,1,0:T(8,128)S(1)}, f32[27,8,128]{2,1,0:T(8,128)S(1)}) custom-call(f32[9,12,8,128]{3,2,1,0:T(8,128)S(1)} %copy-done.1, f32[9,12,8,128]{3,2,1,0:T(8,128)S(1)} %get-tuple-element.48.s_ref, f32[9,12,8,128]{3,2,1,0:T(8,128)S(1)} %shard_map.63.part_ref, ...), custom_call_target="tpu_custom_call" | custom-call | tf_op jit(solution)/shard_map/pallas_call | solution.py:436
  28.3 3.8 %collective-permute-start.14 = (f32[36,8,128]{2,1,0:T(8,128)S(1)}, f32[36,8,128]{2,1,0:T(8,128)S(1)}, u32[]{:S(2)}, u32[]{:S(2)}) collective-permute-start(f32[36,8,128]{2,1,0:T(8,128)S(1)} %get-tuple-element.67), channel_id=1, source_target_pairs={{1,2},{3,4},{5,6},{2,1},{4,3},{6,5},{0,0},{7,7},{9,10},{11,12},{13... | collective-permute-start | bytes 442376 | tf_op jit(solution)/shard_map/ppermute | solution.py:402
  32.2 1.1 %collective-permute-start.12 = (f32[27,8,128]{2,1,0:T(8,128)S(1)}, f32[27,8,128]{2,1,0:T(8,128)S(1)}, u32[]{:S(2)}, u32[]{:S(2)}) collective-permute-start(f32[27,8,128]{2,1,0:T(8,128)S(1)} %get-tuple-element.65), channel_id=1, source_target_pairs={{0,8},{16,24},{8,0},{24,16},{1,9},{17,25},{9,1},{25,17},{2,10},{18... | collective-permute-start | bytes 331784 | tf_op jit(solution)/shard_map/ppermute | solution.py:402
  33.2 0.0 collective-permute-start.13
  33.3 0.0 collective-permute-done.11.ghosts_ref
  33.3 2.0 %shard_map.66 = (f32[9,12,8,128]{3,2,1,0:T(8,128)S(1)}, f32[9,12,8,128]{3,2,1,0:T(8,128)S(1)}) custom-call(f32[9,12,8,128]{3,2,1,0:T(8,128)S(1)} %get-tuple-element.62.s_ref, f32[7,128,128]{2,1,0:T(8,128)S(1)} %get-tuple-element.49.rest_0_, f32[8,128]{1,0:T(8,128)S(1)} %get-tuple-element.50.rest_1_.pk_ref), custom_call_target="tpu_custom_call" | custom-call | tf_op jit(solution)/shard_map/pallas_call | solution.py:436
  35.3 0.0 collective-permute-done.12.near_ref
  35.3 2.7 %collective-permute-done.13.far_ref = f32[27,8,128]{2,1,0:T(8,128)S(1)} collective-permute-done((f32[27,8,128]{2,1,0:T(8,128)S(1)}, f32[27,8,128]{2,1,0:T(8,128)S(1)}, u32[]{:S(2)}, u32[]{:S(2)}) %collective-permute-start.13) | collective-permute-done | bytes 110624 | tf_op jit(solution)/shard_map/ppermute | solution.py:402
  38.0 0.8 %shard_map.67.part_ref = f32[9,12,8,128]{3,2,1,0:T(8,128)S(1)} custom-call(f32[9,12,8,128]{3,2,1,0:T(8,128)S(1)} %get-tuple-element.62.s_ref, f32[9,12,8,128]{3,2,1,0:T(8,128)S(1)} %get-tuple-element.63.speed_ref, f32[9,12,8,128]{3,2,1,0:T(8,128)S(1)} %get-tuple-element.64.part_ref, f32[27,8,128]{2,1,0:T(8,128)S(1)} %collective-permute-done.12.near_ref, ...), custom_call_target="tpu_custom_call" | custom-call | flops 110592000 | bytes 110592000 | tf_op jit(solution)/shard_map/pallas_call | solution.py:436
  38.8 0.7 %shard_map.68.refs_0_ = f32[9,12,8,128]{3,2,1,0:T(8,128)S(1)} custom-call(f32[9,12,8,128]{3,2,1,0:T(8,128)S(1)} %copy-done.1, f32[9,12,8,128]{3,2,1,0:T(8,128)S(1)} %get-tuple-element.62.s_ref, f32[9,12,8,128]{3,2,1,0:T(8,128)S(1)} %shard_map.67.part_ref, f32[38,8,128]{2,1,0:T(8,128)S(1)} %collective-permute-done.11.ghosts_ref, f32[9,2,128]{2,1,0:T(2,128)S(1)} %bitcast.6, ...), custom_call_target="tpu_custom_call" | custom-call | tf_op jit(solution)/shard_map/pallas_call | solution.py:436
  39.5 0.0 collective-permute-done.14.ghosts_ref
  39.5 1.2 %shard_map.69 = f32[9,12,8,128]{3,2,1,0:T(8,128)} custom-call(f32[9,12,8,128]{3,2,1,0:T(8,128)S(1)} %copy-done.1, f32[9,12,8,128]{3,2,1,0:T(8,128)S(1)} %get-tuple-element.62.s_ref, f32[9,12,8,128]{3,2,1,0:T(8,128)S(1)} %shard_map.67.part_ref, f32[36,8,128]{2,1,0:T(8,128)S(1)} %collective-permute-done.14.ghosts_ref, f32[9,2,128]{2,1,0:T(2,128)S(1)} %bitcast.7, ...), custom_call_target="tpu_custom_call" | custom-call | tf_op jit(solution)/shard_map/pallas_call | solution.py:436
  (4 shorter events, 0.1 us)
Async XLA Ops:
  0.0 0.7 %copy-start.3 = (f32[2,9,128]{2,0,1:T(2,128)S(1)}, f32[2,9,128]{2,0,1:T(2,128)}, u32[]{:S(2)}) copy-start(f32[2,9,128]{2,0,1:T(2,128)} %param.6) | copy-start | bytes 27652
  0.7 9.6 %collective-permute-start = (f32[40,8,128]{2,1,0:T(8,128)S(1)}, f32[40,8,128]{2,1,0:T(8,128)S(1)}, u32[]{:S(2)}, u32[]{:S(2)}) collective-permute-start(f32[40,8,128]{2,1,0:T(8,128)S(1)} %shard_map.56.own_ref), channel_id=1, source_target_pairs={{0,1},{1,0},{2,3},{3,2},{4,5},{5,4},{6,7},{7,6},{8,9},{9,8},{10,11... | collective-permute-start | bytes 491528 | tf_op jit(solution)/shard_map/ppermute | solution.py:465
  2.0 1.0 %copy-start = (f32[9,12,8,128]{3,2,1,0:T(8,128)S(1)}, f32[9,12,8,128]{3,2,1,0:T(8,128)}, u32[]{:S(2)}) copy-start(f32[9,12,8,128]{3,2,1,0:T(8,128)} %base_ref.7) | copy-start | bytes 1327108
  3.0 7.4 %copy-start.1 = (f32[9,12,8,128]{3,2,1,0:T(8,128)S(1)}, f32[9,12,8,128]{3,2,1,0:T(8,128)}, u32[]{:S(2)}) copy-start(f32[9,12,8,128]{3,2,1,0:T(8,128)} %base_ref.7) | copy-start | bytes 1327108
  3.1 12.8 %collective-permute-start.5 = (f32[39,8,128]{2,1,0:T(8,128)S(1)}, f32[39,8,128]{2,1,0:T(8,128)S(1)}, u32[]{:S(2)}, u32[]{:S(2)}) collective-permute-start(f32[39,8,128]{2,1,0:T(8,128)S(1)} %get-tuple-element.43), channel_id=1, source_target_pairs={{1,2},{3,4},{5,6},{2,1},{4,3},{6,5},{0,0},{7,7},{9,10},{11,12},{13... | collective-permute-start | bytes 479240 | tf_op jit(solution)/shard_map/ppermute | solution.py:402
  5.1 10.7 %collective-permute-start.4 = (f32[38,8,128]{2,1,0:T(8,128)S(1)}, f32[38,8,128]{2,1,0:T(8,128)S(1)}, u32[]{:S(2)}, u32[]{:S(2)}) collective-permute-start(f32[38,8,128]{2,1,0:T(8,128)S(1)} %get-tuple-element.42), channel_id=1, source_target_pairs={{0,1},{2,3},{4,5},{6,7},{1,0},{3,2},{5,4},{7,6},{8,9},{10,11},{12,... | collective-permute-start | bytes 466952 | tf_op jit(solution)/shard_map/ppermute | solution.py:402
  7.7 7.4 %collective-permute-start.2 = (f32[37,8,128]{2,1,0:T(8,128)S(1)}, f32[37,8,128]{2,1,0:T(8,128)S(1)}, u32[]{:S(2)}, u32[]{:S(2)}) collective-permute-start(f32[37,8,128]{2,1,0:T(8,128)S(1)} %get-tuple-element.40), channel_id=1, source_target_pairs={{0,8},{16,24},{8,0},{24,16},{1,9},{17,25},{9,1},{25,17},{2,10},{18... | collective-permute-start | bytes 454664 | tf_op jit(solution)/shard_map/ppermute | solution.py:402
  9.2 1.3 %copy-start.2 = (f32[2,48,128]{2,1,0:T(8,128)S(1)}, f32[2,48,128]{2,1,0:T(8,128)}, u32[]{:S(2)}) copy-start(f32[2,48,128]{2,1,0:T(8,128)} %constant.2.clone.rest_1_.waves_ref) | copy-start | bytes 147460
  9.2 1.3 %copy-start.4 = (f32[2,9,128]{2,0,1:T(2,128)S(1)}, f32[2,9,128]{2,0,1:T(2,128)}, u32[]{:S(2)}) copy-start(f32[2,9,128]{2,0,1:T(2,128)} %param.6) | copy-start | bytes 27652
  9.2 5.9 %collective-permute-start.3 = (f32[37,8,128]{2,1,0:T(8,128)S(1)}, f32[37,8,128]{2,1,0:T(8,128)S(1)}, u32[]{:S(2)}, u32[]{:S(2)}) collective-permute-start(f32[37,8,128]{2,1,0:T(8,128)S(1)} %get-tuple-element.41), channel_id=1, source_target_pairs={{8,16},{24,0},{16,8},{0,24},{9,17},{25,1},{17,9},{1,25},{10,18},{2... | collective-permute-start | bytes 454664 | tf_op jit(solution)/shard_map/ppermute | solution.py:402
  10.3 2.8 %collective-permute-start.1 = (f32[8,128]{1,0:T(8,128)S(1)}, f32[8,128]{1,0:T(8,128)S(1)}, u32[]{:S(2)}, u32[]{:S(2)}) collective-permute-start(f32[8,128]{1,0:T(8,128)S(1)} %shard_map.57), channel_id=1, source_target_pairs={{0,2},{1,3},{2,0},{3,1},{4,6},{5,7},{6,4},{7,5},{8,10},{9,11},{10,... | collective-permute-start | bytes 12296 | tf_op jit(solution)/shard_map/ppermute | solution.py:465
  13.0 3.7 %collective-permute-start.6 = (f32[8,128]{1,0:T(8,128)S(1)}, f32[8,128]{1,0:T(8,128)S(1)}, u32[]{:S(2)}, u32[]{:S(2)}) collective-permute-start(f32[8,128]{1,0:T(8,128)S(1)} %max.3.most_ref), channel_id=1, source_target_pairs={{0,4},{1,5},{2,6},{3,7},{4,0},{5,1},{6,2},{7,3},{8,12},{9,13},{10,... | collective-permute-start | bytes 12296 | tf_op jit(solution)/shard_map/ppermute | solution.py:465
  15.9 0.9 %copy-start.5 = (s32[9,128]{1,0:T(8,128)S(1)}, s32[9,128]{1,0:T(8,128)}, u32[]{:S(2)}) copy-start(s32[9,128]{1,0:T(8,128)} %mask_ref.9) | copy-start | bytes 13828
  15.9 0.9 %copy-start.6 = (f32[9,128]{1,0:T(8,128)S(1)}, f32[9,128]{1,0:T(8,128)}, u32[]{:S(2)}) copy-start(f32[9,128]{1,0:T(8,128)} %depth_ref.9) | copy-start | bytes 13828
  17.1 8.3 %collective-permute-start.7 = (f32[38,8,128]{2,1,0:T(8,128)S(1)}, f32[38,8,128]{2,1,0:T(8,128)S(1)}, u32[]{:S(2)}, u32[]{:S(2)}) collective-permute-start(f32[38,8,128]{2,1,0:T(8,128)S(1)} %get-tuple-element.53), channel_id=1, source_target_pairs={{0,1},{2,3},{4,5},{6,7},{1,0},{3,2},{5,4},{7,6},{8,9},{10,11},{12,... | collective-permute-start | bytes 466952 | tf_op jit(solution)/shard_map/ppermute | solution.py:402
  17.2 8.3 %collective-permute-start.9 = (f32[37,8,128]{2,1,0:T(8,128)S(1)}, f32[37,8,128]{2,1,0:T(8,128)S(1)}, u32[]{:S(2)}, u32[]{:S(2)}) collective-permute-start(f32[37,8,128]{2,1,0:T(8,128)S(1)} %get-tuple-element.56), channel_id=1, source_target_pairs={{8,16},{24,0},{16,8},{0,24},{9,17},{25,1},{17,9},{1,25},{10,18},{2... | collective-permute-start | bytes 454664 | tf_op jit(solution)/shard_map/ppermute | solution.py:402
  19.6 8.3 %collective-permute-start.10 = (f32[36,8,128]{2,1,0:T(8,128)S(1)}, f32[36,8,128]{2,1,0:T(8,128)S(1)}, u32[]{:S(2)}, u32[]{:S(2)}) collective-permute-start(f32[36,8,128]{2,1,0:T(8,128)S(1)} %get-tuple-element.57), channel_id=1, source_target_pairs={{1,2},{3,4},{5,6},{2,1},{4,3},{6,5},{0,0},{7,7},{9,10},{11,12},{13... | collective-permute-start | bytes 442376 | tf_op jit(solution)/shard_map/ppermute | solution.py:402
  23.3 2.2 %collective-permute-start.8 = (f32[27,8,128]{2,1,0:T(8,128)S(1)}, f32[27,8,128]{2,1,0:T(8,128)S(1)}, u32[]{:S(2)}, u32[]{:S(2)}) collective-permute-start(f32[27,8,128]{2,1,0:T(8,128)S(1)} %get-tuple-element.55), channel_id=1, source_target_pairs={{0,8},{16,24},{8,0},{24,16},{1,9},{17,25},{9,1},{25,17},{2,10},{18... | collective-permute-start | bytes 331784 | tf_op jit(solution)/shard_map/ppermute | solution.py:402
  27.0 6.3 %collective-permute-start.11 = (f32[38,8,128]{2,1,0:T(8,128)S(1)}, f32[38,8,128]{2,1,0:T(8,128)S(1)}, u32[]{:S(2)}, u32[]{:S(2)}) collective-permute-start(f32[38,8,128]{2,1,0:T(8,128)S(1)} %get-tuple-element.61), channel_id=1, source_target_pairs={{0,1},{2,3},{4,5},{6,7},{1,0},{3,2},{5,4},{7,6},{8,9},{10,11},{12,... | collective-permute-start | bytes 466952 | tf_op jit(solution)/shard_map/ppermute | solution.py:402
  28.3 11.2 %collective-permute-start.14 = (f32[36,8,128]{2,1,0:T(8,128)S(1)}, f32[36,8,128]{2,1,0:T(8,128)S(1)}, u32[]{:S(2)}, u32[]{:S(2)}) collective-permute-start(f32[36,8,128]{2,1,0:T(8,128)S(1)} %get-tuple-element.67), channel_id=1, source_target_pairs={{1,2},{3,4},{5,6},{2,1},{4,3},{6,5},{0,0},{7,7},{9,10},{11,12},{13... | collective-permute-start | bytes 442376 | tf_op jit(solution)/shard_map/ppermute | solution.py:402
  32.2 3.1 %collective-permute-start.12 = (f32[27,8,128]{2,1,0:T(8,128)S(1)}, f32[27,8,128]{2,1,0:T(8,128)S(1)}, u32[]{:S(2)}, u32[]{:S(2)}) collective-permute-start(f32[27,8,128]{2,1,0:T(8,128)S(1)} %get-tuple-element.65), channel_id=1, source_target_pairs={{0,8},{16,24},{8,0},{24,16},{1,9},{17,25},{9,1},{25,17},{2,10},{18... | collective-permute-start | bytes 331784 | tf_op jit(solution)/shard_map/ppermute | solution.py:402
  33.2 4.7 %collective-permute-start.13 = (f32[27,8,128]{2,1,0:T(8,128)S(1)}, f32[27,8,128]{2,1,0:T(8,128)S(1)}, u32[]{:S(2)}, u32[]{:S(2)}) collective-permute-start(f32[27,8,128]{2,1,0:T(8,128)S(1)} %get-tuple-element.66), channel_id=1, source_target_pairs={{8,16},{24,0},{16,8},{0,24},{9,17},{25,1},{17,9},{1,25},{10,18},{2... | collective-permute-start | bytes 331784 | tf_op jit(solution)/shard_map/ppermute | solution.py:402

commit v25 on v21

--- a/solution.py
+++ b/solution.py
@@ -490,14 +490,14 @@
                 most, part = lax.optimization_barrier((most, part))
                 other = spread(most, reach)
                 reach *= 2
+            part, x_far = lax.optimization_barrier((part, x_far))
         else:
             if section == 3:
                 values, x_near = lax.optimization_barrier((values, x_near))
             spun, part = call(free, [values, flow, pk], [field] * 2, room)
             if section == 2:
                 part, x_near = lax.optimization_barrier((part, x_near))
-        weight = 0 if opening else 1000
-        (part,) = call(turning, [values, spun, part, t_near, t_far], [field], work=weight)
+        (part,) = call(turning, [values, spun, part, t_near, t_far], [field], work=1000)
         if opening:
             ins = [values, part, x_near, x_far, wind, waves]
             first = functools.partial(first_kernel, speed_step)

time: 39.8 us -> 39.8 us (level)
  no operation moved by 1% of the time
where the time goes in v25:
time: 39.8 us; the launch traced here: 39.5 us
  starting transfers between devices  20.6 us (52%)
  Pallas kernels  12.7 us (32%)
  waiting for transfers between devices  4.26 us (11%)
  local copies, waits for them, and re-layouts  1.74 us (4%)
    ppermute x12, starting transfers between devices, trade(): return lax.ppermute(value, axis, pairs)  16.9 us
    pallas_call x15, Pallas kernels, call(): pl.pallas_call(kernel, out_shape=outs, in_specs=[vmem] * len(ins), out_sp...  12.7 us
    ppermute x3, starting transfers between devices, spread(): return lax.ppermute(most, 'gx', pairs)  3.72 us
    ppermute x12, waiting for transfers between devices, trade(): return lax.ppermute(value, axis, pairs)  2.14 us
    ppermute x3, waiting for transfers between devices, spread(): return lax.ppermute(most, 'gx', pairs)  2.11 us
    unnamed x14, local copies, waits for them, and re-layouts  1.74 us
  transfers between devices with their start and end apart: 15, of which 4 were waited for; matrix products, arithmetic and copies ran while one was open for 0% of the time, Pallas kernels for 28%

profile of v25, /device:TPU:8, one launch (start us, length us, event | category | flops | bytes accessed | tf_op | source)
XLA Modules:
  0.0 39.5 jit_solution(8444616680160645394)
XLA Ops:
  0.0 0.0 copy-start.3
  0.0 0.7 %copy-done.3 = f32[2,9,128]{2,0,1:T(2,128)S(1)} copy-done((f32[2,9,128]{2,0,1:T(2,128)S(1)}, f32[2,9,128]{2,0,1:T(2,128)}, u32[]{:S(2)}) %copy-start.3) | copy-done | bytes 9240
  0.7 1.6 %collective-permute-start = (f32[40,8,128]{2,1,0:T(8,128)S(1)}, f32[40,8,128]{2,1,0:T(8,128)S(1)}, u32[]{:S(2)}, u32[]{:S(2)}) collective-permute-start(f32[40,8,128]{2,1,0:T(8,128)S(1)} %shard_map.56.own_ref), channel_id=1, source_target_pairs={{0,1},{1,0},{2,3},{3,2},{4,5},{5,4},{6,7},{7,6},{8,9},{9,8},{10,11... | collective-permute-start | bytes 491528 | tf_op jit(solution)/shard_map/ppermute | solution.py:465
  2.3 0.0 copy-start
  2.3 1.0 %copy-done = f32[9,12,8,128]{3,2,1,0:T(8,128)S(1)} copy-done((f32[9,12,8,128]{3,2,1,0:T(8,128)S(1)}, f32[9,12,8,128]{3,2,1,0:T(8,128)}, u32[]{:S(2)}) %copy-start) | copy-done | bytes 442392
  3.3 0.0 copy-start.1
  3.3 2.1 %collective-permute-start.2 = (f32[39,8,128]{2,1,0:T(8,128)S(1)}, f32[39,8,128]{2,1,0:T(8,128)S(1)}, u32[]{:S(2)}, u32[]{:S(2)}) collective-permute-start(f32[39,8,128]{2,1,0:T(8,128)S(1)} %get-tuple-element.42), channel_id=1, source_target_pairs={{1,2},{3,4},{5,6},{2,1},{4,3},{6,5},{0,0},{7,7},{9,10},{11,12},{13... | collective-permute-start | bytes 479240 | tf_op jit(solution)/shard_map/ppermute | solution.py:402
  5.4 0.1 collective-permute-start.3
  5.5 2.0 %collective-permute-start.4 = (f32[37,8,128]{2,1,0:T(8,128)S(1)}, f32[37,8,128]{2,1,0:T(8,128)S(1)}, u32[]{:S(2)}, u32[]{:S(2)}) collective-permute-start(f32[37,8,128]{2,1,0:T(8,128)S(1)} %get-tuple-element.45), channel_id=1, source_target_pairs={{8,16},{24,0},{16,8},{0,24},{9,17},{25,1},{17,9},{1,25},{10,18},{2... | collective-permute-start | bytes 454664 | tf_op jit(solution)/shard_map/ppermute | solution.py:402
  7.5 0.0 copy-start.2
  7.5 0.0 copy-start.4
  7.5 2.6 %collective-permute-start.5 = (f32[38,8,128]{2,1,0:T(8,128)S(1)}, f32[38,8,128]{2,1,0:T(8,128)S(1)}, u32[]{:S(2)}, u32[]{:S(2)}) collective-permute-start(f32[38,8,128]{2,1,0:T(8,128)S(1)} %get-tuple-element.46), channel_id=1, source_target_pairs={{0,1},{2,3},{4,5},{6,7},{1,0},{3,2},{5,4},{7,6},{8,9},{10,11},{12,... | collective-permute-start | bytes 466952 | tf_op jit(solution)/shard_map/ppermute | solution.py:402
  10.1 0.0 collective-permute-done.other_ref
  10.1 0.5 %collective-permute-start.1 = (f32[8,128]{1,0:T(8,128)S(1)}, f32[8,128]{1,0:T(8,128)S(1)}, u32[]{:S(2)}, u32[]{:S(2)}) collective-permute-start(f32[8,128]{1,0:T(8,128)S(1)} %shard_map.57), channel_id=1, source_target_pairs={{0,2},{1,3},{2,0},{3,1},{4,6},{5,7},{6,4},{7,5},{8,10},{9,11},{10,... | collective-permute-start | bytes 12296 | tf_op jit(solution)/shard_map/ppermute | solution.py:465
  10.6 0.0 copy-done.1
  10.6 0.0 copy-done.2
  10.6 0.0 copy-done.4
  10.6 2.2 %shard_map.55 = (f32[9,12,8,128]{3,2,1,0:T(8,128)S(1)}, f32[9,12,8,128]{3,2,1,0:T(8,128)S(1)}, f32[9,12,8,128]{3,2,1,0:T(8,128)S(1)}, f32[7,128,128]{2,1,0:T(8,128)S(1)}) custom-call(f32[9,12,8,128]{3,2,1,0:T(8,128)S(1)} %copy-done.1, f32[9,2,128]{2,1,0:T(2,128)S(1)} %bitcast.2, f32[2,48,128]{2,1,0:T(8,128)S(1)} %copy-done.2), custom_call_target="tpu_custom_call" | custom-call | flops 33177600 | bytes 33177600 | tf_op jit(solution)/shard_map/pallas_call | solution.py:436
  12.8 1.0 %collective-permute-done.1 = f32[8,128]{1,0:T(8,128)S(1)} collective-permute-done((f32[8,128]{1,0:T(8,128)S(1)}, f32[8,128]{1,0:T(8,128)S(1)}, u32[]{:S(2)}, u32[]{:S(2)}) %collective-permute-start.1) | collective-permute-done | bytes 4128 | tf_op jit(solution)/shard_map/ppermute | solution.py:465
  13.7 0.0 collective-permute-done.2.far_ref
  13.7 1.7 %collective-permute-start.6 = (f32[8,128]{1,0:T(8,128)S(1)}, f32[8,128]{1,0:T(8,128)S(1)}, u32[]{:S(2)}, u32[]{:S(2)}) collective-permute-start(f32[8,128]{1,0:T(8,128)S(1)} %max.3.most_ref), channel_id=1, source_target_pairs={{0,4},{1,5},{2,6},{3,7},{4,0},{5,1},{6,2},{7,3},{8,12},{9,13},{10,... | collective-permute-start | bytes 12296 | tf_op jit(solution)/shard_map/ppermute | solution.py:465
  15.4 0.0 collective-permute-done.3.near_ref
  15.4 0.0 collective-permute-done.4.far_ref
  15.4 0.8 %shard_map.59.part_ref = f32[9,12,8,128]{3,2,1,0:T(8,128)S(1)} custom-call(f32[9,12,8,128]{3,2,1,0:T(8,128)S(1)} %copy-done.1, f32[9,12,8,128]{3,2,1,0:T(8,128)S(1)} %get-tuple-element.39.speed_ref, f32[9,12,8,128]{3,2,1,0:T(8,128)S(1)} %get-tuple-element.43.part_ref, f32[37,8,128]{2,1,0:T(8,128)S(1)} %collective-permute-done.3.near_ref, ...), custom_call_target="tpu_custom_call" | custom-call | flops 110592000 | bytes 110592000 | tf_op jit(solution)/shard_map/pallas_call | solution.py:436
  16.3 0.0 collective-permute-done.5.near_ref
  16.3 0.0 copy-start.5
  16.3 0.0 copy-start.6
  16.3 0.8 %shard_map.60 = (f32[9,12,8,128]{3,2,1,0:T(8,128)S(1)}, f32[9,12,8,128]{3,2,1,0:T(8,128)S(1)}) custom-call(f32[9,12,8,128]{3,2,1,0:T(8,128)S(1)} %copy-done.1, f32[9,12,8,128]{3,2,1,0:T(8,128)S(1)} %shard_map.59.part_ref, f32[38,8,128]{2,1,0:T(8,128)S(1)} %collective-permute-done.5.near_ref, f32[39,8,128]{2,1,0:T(8,128)S(1)} %collective-permute-done.2.far_ref, ...), custom_call_target="tpu_custom_call" | custom-call | tf_op jit(solution)/shard_map/pallas_call | solution.py:436
  17.1 1.1 %collective-permute-done.6.other_ref = f32[8,128]{1,0:T(8,128)S(1)} collective-permute-done((f32[8,128]{1,0:T(8,128)S(1)}, f32[8,128]{1,0:T(8,128)S(1)}, u32[]{:S(2)}, u32[]{:S(2)}) %collective-permute-start.6) | collective-permute-done | bytes 4128 | tf_op jit(solution)/shard_map/ppermute | solution.py:465
  18.3 0.0 copy-done.5
  18.3 0.0 copy-done.6
  18.3 0.3 shard_map.61
  18.6 0.1 collective-permute-start.7
  18.8 0.0 collective-permute-start.9
  18.8 4.0 %collective-permute-start.10 = (f32[36,8,128]{2,1,0:T(8,128)S(1)}, f32[36,8,128]{2,1,0:T(8,128)S(1)}, u32[]{:S(2)}, u32[]{:S(2)}) collective-permute-start(f32[36,8,128]{2,1,0:T(8,128)S(1)} %get-tuple-element.61), channel_id=1, source_target_pairs={{1,2},{3,4},{5,6},{2,1},{4,3},{6,5},{0,0},{7,7},{9,10},{11,12},{13... | collective-permute-start | bytes 442376 | tf_op jit(solution)/shard_map/ppermute | solution.py:402
  22.7 0.4 %collective-permute-start.8 = (f32[27,8,128]{2,1,0:T(8,128)S(1)}, f32[27,8,128]{2,1,0:T(8,128)S(1)}, u32[]{:S(2)}, u32[]{:S(2)}) collective-permute-start(f32[27,8,128]{2,1,0:T(8,128)S(1)} %get-tuple-element.59), channel_id=1, source_target_pairs={{0,8},{16,24},{8,0},{24,16},{1,9},{17,25},{9,1},{25,17},{2,10},{18... | collective-permute-start | bytes 331784 | tf_op jit(solution)/shard_map/ppermute | solution.py:402
  23.2 2.0 %shard_map.62 = (f32[9,12,8,128]{3,2,1,0:T(8,128)S(1)}, f32[9,12,8,128]{3,2,1,0:T(8,128)S(1)}) custom-call(f32[9,12,8,128]{3,2,1,0:T(8,128)S(1)} %get-tuple-element.52.s_ref, f32[7,128,128]{2,1,0:T(8,128)S(1)} %get-tuple-element.53.rest_0_, f32[8,128]{1,0:T(8,128)S(1)} %get-tuple-element.54.rest_1_.pk_ref), custom_call_target="tpu_custom_call" | custom-call | tf_op jit(solution)/shard_map/pallas_call | solution.py:436
  25.1 0.0 collective-permute-done.7.ghosts_ref
  25.1 0.0 collective-permute-done.8.near_ref
  25.2 0.0 collective-permute-done.9.far_ref
  25.2 0.8 %shard_map.63.part_ref = f32[9,12,8,128]{3,2,1,0:T(8,128)S(1)} custom-call(f32[9,12,8,128]{3,2,1,0:T(8,128)S(1)} %get-tuple-element.52.s_ref, f32[9,12,8,128]{3,2,1,0:T(8,128)S(1)} %get-tuple-element.55.speed_ref, f32[9,12,8,128]{3,2,1,0:T(8,128)S(1)} %get-tuple-element.58.part_ref, f32[27,8,128]{2,1,0:T(8,128)S(1)} %collective-permute-done.8.near_ref, ...), custom_call_target="tpu_custom_call" | custom-call | flops 110592000 | bytes 110592000 | tf_op jit(solution)/shard_map/pallas_call | solution.py:436
  26.0 0.7 %shard_map.64 = (f32[9,12,8,128]{3,2,1,0:T(8,128)S(1)}, f32[38,8,128]{2,1,0:T(8,128)S(1)}) custom-call(f32[9,12,8,128]{3,2,1,0:T(8,128)S(1)} %copy-done.1, f32[9,12,8,128]{3,2,1,0:T(8,128)S(1)} %get-tuple-element.52.s_ref, f32[9,12,8,128]{3,2,1,0:T(8,128)S(1)} %shard_map.63.part_ref, f32[38,8,128]{2,1,0:T(8,128)S(1)} %collective-permute-done.7.ghosts_ref, ...), custom_call_target="tpu_custom_call" | custom-call | tf_op jit(solution)/shard_map/pallas_call | solution.py:436
  26.6 1.0 %collective-permute-start.11 = (f32[38,8,128]{2,1,0:T(8,128)S(1)}, f32[38,8,128]{2,1,0:T(8,128)S(1)}, u32[]{:S(2)}, u32[]{:S(2)}) collective-permute-start(f32[38,8,128]{2,1,0:T(8,128)S(1)} %get-tuple-element.65), channel_id=1, source_target_pairs={{0,1},{2,3},{4,5},{6,7},{1,0},{3,2},{5,4},{7,6},{8,9},{10,11},{12,... | collective-permute-start | bytes 466952 | tf_op jit(solution)/shard_map/ppermute | solution.py:402
  27.7 0.2 collective-permute-done.10.ghosts_ref
  27.9 0.4 %shard_map.65 = (f32[9,12,8,128]{3,2,1,0:T(8,128)S(1)}, f32[36,8,128]{2,1,0:T(8,128)S(1)}, f32[27,8,128]{2,1,0:T(8,128)S(1)}, f32[37,8,128]{2,1,0:T(8,128)S(1)}) custom-call(f32[9,12,8,128]{3,2,1,0:T(8,128)S(1)} %copy-done.1, f32[9,12,8,128]{3,2,1,0:T(8,128)S(1)} %get-tuple-element.52.s_ref, f32[9,12,8,128]{3,2,1,0:T(8,128)S(1)} %shard_map.63.part_ref, ...), custom_call_target="tpu_custom_call" | custom-call | tf_op jit(solution)/shard_map/pallas_call | solution.py:436
  28.4 0.7 %collective-permute-start.13 = (f32[37,8,128]{2,1,0:T(8,128)S(1)}, f32[37,8,128]{2,1,0:T(8,128)S(1)}, u32[]{:S(2)}, u32[]{:S(2)}) collective-permute-start(f32[37,8,128]{2,1,0:T(8,128)S(1)} %get-tuple-element.70), channel_id=1, source_target_pairs={{8,16},{24,0},{16,8},{0,24},{9,17},{25,1},{17,9},{1,25},{10,18},{2... | collective-permute-start | bytes 454664 | tf_op jit(solution)/shard_map/ppermute | solution.py:402
  29.0 3.9 %collective-permute-start.14 = (f32[36,8,128]{2,1,0:T(8,128)S(1)}, f32[36,8,128]{2,1,0:T(8,128)S(1)}, u32[]{:S(2)}, u32[]{:S(2)}) collective-permute-start(f32[36,8,128]{2,1,0:T(8,128)S(1)} %get-tuple-element.71), channel_id=1, source_target_pairs={{1,2},{3,4},{5,6},{2,1},{4,3},{6,5},{0,0},{7,7},{9,10},{11,12},{13... | collective-permute-start | bytes 442376 | tf_op jit(solution)/shard_map/ppermute | solution.py:402
  32.9 0.1 collective-permute-start.12
  33.0 0.0 collective-permute-done.11.ghosts_ref
  33.0 2.0 %shard_map.66 = (f32[9,12,8,128]{3,2,1,0:T(8,128)S(1)}, f32[9,12,8,128]{3,2,1,0:T(8,128)S(1)}) custom-call(f32[9,12,8,128]{3,2,1,0:T(8,128)S(1)} %get-tuple-element.66.s_ref, f32[7,128,128]{2,1,0:T(8,128)S(1)} %get-tuple-element.53.rest_0_, f32[8,128]{1,0:T(8,128)S(1)} %get-tuple-element.54.rest_1_.pk_ref), custom_call_target="tpu_custom_call" | custom-call | tf_op jit(solution)/shard_map/pallas_call | solution.py:436
  34.9 0.0 collective-permute-done.12.near_ref
  35.0 0.0 collective-permute-done.13.far_ref
  35.0 0.8 %shard_map.67.part_ref = f32[9,12,8,128]{3,2,1,0:T(8,128)S(1)} custom-call(f32[9,12,8,128]{3,2,1,0:T(8,128)S(1)} %get-tuple-element.66.s_ref, f32[9,12,8,128]{3,2,1,0:T(8,128)S(1)} %get-tuple-element.67.speed_ref, f32[9,12,8,128]{3,2,1,0:T(8,128)S(1)} %get-tuple-element.68.part_ref, f32[27,8,128]{2,1,0:T(8,128)S(1)} %collective-permute-done.12.near_ref, ...), custom_call_target="tpu_custom_call" | custom-call | flops 110592000 | bytes 110592000 | tf_op jit(solution)/shard_map/pallas_call | solution.py:436
  35.8 0.7 %shard_map.68.refs_0_ = f32[9,12,8,128]{3,2,1,0:T(8,128)S(1)} custom-call(f32[9,12,8,128]{3,2,1,0:T(8,128)S(1)} %copy-done.1, f32[9,12,8,128]{3,2,1,0:T(8,128)S(1)} %get-tuple-element.66.s_ref, f32[9,12,8,128]{3,2,1,0:T(8,128)S(1)} %shard_map.67.part_ref, f32[38,8,128]{2,1,0:T(8,128)S(1)} %collective-permute-done.11.ghosts_ref, f32[9,2,128]{2,1,0:T(2,128)S(1)} %bitcast.6, ...), custom_call_target="tpu_custom_call" | custom-call | tf_op jit(solution)/shard_map/pallas_call | solution.py:436
  36.4 1.9 %collective-permute-done.14.ghosts_ref = f32[36,8,128]{2,1,0:T(8,128)S(1)} collective-permute-done((f32[36,8,128]{2,1,0:T(8,128)S(1)}, f32[36,8,128]{2,1,0:T(8,128)S(1)}, u32[]{:S(2)}, u32[]{:S(2)}) %collective-permute-start.14) | collective-permute-done | bytes 147488 | tf_op jit(solution)/shard_map/ppermute | solution.py:402
  38.3 1.1 %shard_map.69 = f32[9,12,8,128]{3,2,1,0:T(8,128)} custom-call(f32[9,12,8,128]{3,2,1,0:T(8,128)S(1)} %copy-done.1, f32[9,12,8,128]{3,2,1,0:T(8,128)S(1)} %get-tuple-element.66.s_ref, f32[9,12,8,128]{3,2,1,0:T(8,128)S(1)} %shard_map.67.part_ref, f32[36,8,128]{2,1,0:T(8,128)S(1)} %collective-permute-done.14.ghosts_ref, f32[9,2,128]{2,1,0:T(2,128)S(1)} %bitcast.7, ...), custom_call_target="tpu_custom_call" | custom-call | tf_op jit(solution)/shard_map/pallas_call | solution.py:436
  (4 shorter events, 0.1 us)
Async XLA Ops:
  0.0 0.7 %copy-start.3 = (f32[2,9,128]{2,0,1:T(2,128)S(1)}, f32[2,9,128]{2,0,1:T(2,128)}, u32[]{:S(2)}) copy-start(f32[2,9,128]{2,0,1:T(2,128)} %param.6) | copy-start | bytes 27652
  0.7 9.4 %collective-permute-start = (f32[40,8,128]{2,1,0:T(8,128)S(1)}, f32[40,8,128]{2,1,0:T(8,128)S(1)}, u32[]{:S(2)}, u32[]{:S(2)}) collective-permute-start(f32[40,8,128]{2,1,0:T(8,128)S(1)} %shard_map.56.own_ref), channel_id=1, source_target_pairs={{0,1},{1,0},{2,3},{3,2},{4,5},{5,4},{6,7},{7,6},{8,9},{9,8},{10,11... | collective-permute-start | bytes 491528 | tf_op jit(solution)/shard_map/ppermute | solution.py:465
  2.3 1.0 %copy-start = (f32[9,12,8,128]{3,2,1,0:T(8,128)S(1)}, f32[9,12,8,128]{3,2,1,0:T(8,128)}, u32[]{:S(2)}) copy-start(f32[9,12,8,128]{3,2,1,0:T(8,128)} %base_ref.7) | copy-start | bytes 1327108
  3.3 7.3 %copy-start.1 = (f32[9,12,8,128]{3,2,1,0:T(8,128)S(1)}, f32[9,12,8,128]{3,2,1,0:T(8,128)}, u32[]{:S(2)}) copy-start(f32[9,12,8,128]{3,2,1,0:T(8,128)} %base_ref.7) | copy-start | bytes 1327108
  3.3 10.4 %collective-permute-start.2 = (f32[39,8,128]{2,1,0:T(8,128)S(1)}, f32[39,8,128]{2,1,0:T(8,128)S(1)}, u32[]{:S(2)}, u32[]{:S(2)}) collective-permute-start(f32[39,8,128]{2,1,0:T(8,128)S(1)} %get-tuple-element.42), channel_id=1, source_target_pairs={{1,2},{3,4},{5,6},{2,1},{4,3},{6,5},{0,0},{7,7},{9,10},{11,12},{13... | collective-permute-start | bytes 479240 | tf_op jit(solution)/shard_map/ppermute | solution.py:402
  5.4 10.0 %collective-permute-start.3 = (f32[37,8,128]{2,1,0:T(8,128)S(1)}, f32[37,8,128]{2,1,0:T(8,128)S(1)}, u32[]{:S(2)}, u32[]{:S(2)}) collective-permute-start(f32[37,8,128]{2,1,0:T(8,128)S(1)} %get-tuple-element.44), channel_id=1, source_target_pairs={{0,8},{16,24},{8,0},{24,16},{1,9},{17,25},{9,1},{25,17},{2,10},{18... | collective-permute-start | bytes 454664 | tf_op jit(solution)/shard_map/ppermute | solution.py:402
  5.5 10.0 %collective-permute-start.4 = (f32[37,8,128]{2,1,0:T(8,128)S(1)}, f32[37,8,128]{2,1,0:T(8,128)S(1)}, u32[]{:S(2)}, u32[]{:S(2)}) collective-permute-start(f32[37,8,128]{2,1,0:T(8,128)S(1)} %get-tuple-element.45), channel_id=1, source_target_pairs={{8,16},{24,0},{16,8},{0,24},{9,17},{25,1},{17,9},{1,25},{10,18},{2... | collective-permute-start | bytes 454664 | tf_op jit(solution)/shard_map/ppermute | solution.py:402
  7.5 3.1 %copy-start.2 = (f32[2,48,128]{2,1,0:T(8,128)S(1)}, f32[2,48,128]{2,1,0:T(8,128)}, u32[]{:S(2)}) copy-start(f32[2,48,128]{2,1,0:T(8,128)} %constant.2.clone.rest_1_.waves_ref) | copy-start | bytes 147460
  7.5 3.1 %copy-start.4 = (f32[2,9,128]{2,0,1:T(2,128)S(1)}, f32[2,9,128]{2,0,1:T(2,128)}, u32[]{:S(2)}) copy-start(f32[2,9,128]{2,0,1:T(2,128)} %param.6) | copy-start | bytes 27652
  7.5 8.8 %collective-permute-start.5 = (f32[38,8,128]{2,1,0:T(8,128)S(1)}, f32[38,8,128]{2,1,0:T(8,128)S(1)}, u32[]{:S(2)}, u32[]{:S(2)}) collective-permute-start(f32[38,8,128]{2,1,0:T(8,128)S(1)} %get-tuple-element.46), channel_id=1, source_target_pairs={{0,1},{2,3},{4,5},{6,7},{1,0},{3,2},{5,4},{7,6},{8,9},{10,11},{12,... | collective-permute-start | bytes 466952 | tf_op jit(solution)/shard_map/ppermute | solution.py:402
  10.1 3.6 %collective-permute-start.1 = (f32[8,128]{1,0:T(8,128)S(1)}, f32[8,128]{1,0:T(8,128)S(1)}, u32[]{:S(2)}, u32[]{:S(2)}) collective-permute-start(f32[8,128]{1,0:T(8,128)S(1)} %shard_map.57), channel_id=1, source_target_pairs={{0,2},{1,3},{2,0},{3,1},{4,6},{5,7},{6,4},{7,5},{8,10},{9,11},{10,... | collective-permute-start | bytes 12296 | tf_op jit(solution)/shard_map/ppermute | solution.py:465
  13.7 4.5 %collective-permute-start.6 = (f32[8,128]{1,0:T(8,128)S(1)}, f32[8,128]{1,0:T(8,128)S(1)}, u32[]{:S(2)}, u32[]{:S(2)}) collective-permute-start(f32[8,128]{1,0:T(8,128)S(1)} %max.3.most_ref), channel_id=1, source_target_pairs={{0,4},{1,5},{2,6},{3,7},{4,0},{5,1},{6,2},{7,3},{8,12},{9,13},{10,... | collective-permute-start | bytes 12296 | tf_op jit(solution)/shard_map/ppermute | solution.py:465
  16.3 2.0 %copy-start.5 = (s32[9,128]{1,0:T(8,128)S(1)}, s32[9,128]{1,0:T(8,128)}, u32[]{:S(2)}) copy-start(s32[9,128]{1,0:T(8,128)} %mask_ref.9) | copy-start | bytes 13828
  16.3 2.0 %copy-start.6 = (f32[9,128]{1,0:T(8,128)S(1)}, f32[9,128]{1,0:T(8,128)}, u32[]{:S(2)}) copy-start(f32[9,128]{1,0:T(8,128)} %depth_ref.9) | copy-start | bytes 13828
  18.6 6.5 %collective-permute-start.7 = (f32[38,8,128]{2,1,0:T(8,128)S(1)}, f32[38,8,128]{2,1,0:T(8,128)S(1)}, u32[]{:S(2)}, u32[]{:S(2)}) collective-permute-start(f32[38,8,128]{2,1,0:T(8,128)S(1)} %get-tuple-element.57), channel_id=1, source_target_pairs={{0,1},{2,3},{4,5},{6,7},{1,0},{3,2},{5,4},{7,6},{8,9},{10,11},{12,... | collective-permute-start | bytes 466952 | tf_op jit(solution)/shard_map/ppermute | solution.py:402
  18.8 6.4 %collective-permute-start.9 = (f32[37,8,128]{2,1,0:T(8,128)S(1)}, f32[37,8,128]{2,1,0:T(8,128)S(1)}, u32[]{:S(2)}, u32[]{:S(2)}) collective-permute-start(f32[37,8,128]{2,1,0:T(8,128)S(1)} %get-tuple-element.60), channel_id=1, source_target_pairs={{8,16},{24,0},{16,8},{0,24},{9,17},{25,1},{17,9},{1,25},{10,18},{2... | collective-permute-start | bytes 454664 | tf_op jit(solution)/shard_map/ppermute | solution.py:402
  18.8 9.2 %collective-permute-start.10 = (f32[36,8,128]{2,1,0:T(8,128)S(1)}, f32[36,8,128]{2,1,0:T(8,128)S(1)}, u32[]{:S(2)}, u32[]{:S(2)}) collective-permute-start(f32[36,8,128]{2,1,0:T(8,128)S(1)} %get-tuple-element.61), channel_id=1, source_target_pairs={{1,2},{3,4},{5,6},{2,1},{4,3},{6,5},{0,0},{7,7},{9,10},{11,12},{13... | collective-permute-start | bytes 442376 | tf_op jit(solution)/shard_map/ppermute | solution.py:402
  22.7 2.4 %collective-permute-start.8 = (f32[27,8,128]{2,1,0:T(8,128)S(1)}, f32[27,8,128]{2,1,0:T(8,128)S(1)}, u32[]{:S(2)}, u32[]{:S(2)}) collective-permute-start(f32[27,8,128]{2,1,0:T(8,128)S(1)} %get-tuple-element.59), channel_id=1, source_target_pairs={{0,8},{16,24},{8,0},{24,16},{1,9},{17,25},{9,1},{25,17},{2,10},{18... | collective-permute-start | bytes 331784 | tf_op jit(solution)/shard_map/ppermute | solution.py:402
  26.6 6.3 %collective-permute-start.11 = (f32[38,8,128]{2,1,0:T(8,128)S(1)}, f32[38,8,128]{2,1,0:T(8,128)S(1)}, u32[]{:S(2)}, u32[]{:S(2)}) collective-permute-start(f32[38,8,128]{2,1,0:T(8,128)S(1)} %get-tuple-element.65), channel_id=1, source_target_pairs={{0,1},{2,3},{4,5},{6,7},{1,0},{3,2},{5,4},{7,6},{8,9},{10,11},{12,... | collective-permute-start | bytes 466952 | tf_op jit(solution)/shard_map/ppermute | solution.py:402
  28.4 6.6 %collective-permute-start.13 = (f32[37,8,128]{2,1,0:T(8,128)S(1)}, f32[37,8,128]{2,1,0:T(8,128)S(1)}, u32[]{:S(2)}, u32[]{:S(2)}) collective-permute-start(f32[37,8,128]{2,1,0:T(8,128)S(1)} %get-tuple-element.70), channel_id=1, source_target_pairs={{8,16},{24,0},{16,8},{0,24},{9,17},{25,1},{17,9},{1,25},{10,18},{2... | collective-permute-start | bytes 454664 | tf_op jit(solution)/shard_map/ppermute | solution.py:402
  29.0 9.3 %collective-permute-start.14 = (f32[36,8,128]{2,1,0:T(8,128)S(1)}, f32[36,8,128]{2,1,0:T(8,128)S(1)}, u32[]{:S(2)}, u32[]{:S(2)}) collective-permute-start(f32[36,8,128]{2,1,0:T(8,128)S(1)} %get-tuple-element.71), channel_id=1, source_target_pairs={{1,2},{3,4},{5,6},{2,1},{4,3},{6,5},{0,0},{7,7},{9,10},{11,12},{13... | collective-permute-start | bytes 442376 | tf_op jit(solution)/shard_map/ppermute | solution.py:402
  32.9 2.1 %collective-permute-start.12 = (f32[27,8,128]{2,1,0:T(8,128)S(1)}, f32[27,8,128]{2,1,0:T(8,128)S(1)}, u32[]{:S(2)}, u32[]{:S(2)}) collective-permute-start(f32[27,8,128]{2,1,0:T(8,128)S(1)} %get-tuple-element.69), channel_id=1, source_target_pairs={{0,8},{16,24},{8,0},{24,16},{1,9},{17,25},{9,1},{25,17},{2,10},{18... | collective-permute-start | bytes 331784 | tf_op jit(solution)/shard_map/ppermute | solution.py:402
